TPU v7x, 32 devices: a whole 2x2x4 slice. The times are simulated.
32 devices in a mesh: dp: 8 (over z, y), tensor: 4 (over x, core).
Axes of the slice: x: 2, y: 2, z: 4, core: 2. Of those that a mesh axis runs over, the one named last changes fastest.
Arguments:
- prompt_hidden_input: bfloat16 [10240, 5120], P('dp', 'tensor'), may hold values from -100 to 100
- input_norm_gain: float32 [5120], P('tensor'), may hold values from 0.5 to 1.5
- frozen_key_value: bfloat16 [5120, 2048], P(None, 'tensor'), may hold values from -0.078125 to 0.078125
- down_factor_matrix: float32 [5120, 2, 64], P('tensor'), may hold values from -6 to 6
- down_moment_first: float32 [5120, 2, 64], P('tensor'), may hold values from -6 to 6
- down_moment_second: float32 [5120, 2, 64], P('tensor'), may hold values from 0.5 to 4
- up_factor_matrix: float32 [64, 2048], P(None, 'tensor'), may hold values from -6 to 6
- up_moment_first: float32 [64, 2048], P(None, 'tensor'), may hold values from -6 to 6
- up_moment_second: float32 [64, 2048], P(None, 'tensor'), may hold values from 0.5 to 4
- down_gradient: float32 [8, 5120, 2, 64], P('dp', 'tensor'), may hold values from -20 to 20
- up_gradient: float32 [8, 64, 2048], P('dp', None, 'tensor'), may hold values from -20 to 20
Outputs:
- a_next: float32 [3, 5120, 2, 64], P(None, ('tensor', 'dp'))
- b_next: float32 [3, 64, 2048], P(None, 'dp', 'tensor')
- keys_values: bfloat16 [10240, 2048], P('dp', 'tensor')
All inputs are finite; a program needn't handle non-finite values.
Results may differ from a plain program's by a relative error of at most 0.0052.
The roundings to bfloat16 on the way count: a program that leaves them out, or rounds other values in their place, can miss the bound.
Values may be sent and summed in bfloat16 or wider, within the bound.
No kernel may reach another device: no remote copies, remote signals or barrier semaphores. Data moves between devices by JAX's collectives and lax.ppermute only.
A program may use at most 128 MiB of HBM per device.

v0:
```python
import math

import jax
import jax.numpy as jnp
from jax import lax
from jax.sharding import PartitionSpec as P

KEY_VALUE_WIDTH = 1024
STEP = 100


def adaptive_moment_update(param, first, second, grad_mean):
    first_new = 0.9 * first + 0.1 * grad_mean
    second_new = 0.999 * second + 0.001 * grad_mean * grad_mean
    step_size = first_new / (1.0 - 0.9**STEP) / (jnp.sqrt(second_new / (1.0 - 0.999**STEP)) + 1e-08)
    return (param - 0.1 * step_size, first_new, second_new)


def body(
    prompt_hidden_input,
    input_norm_gain,
    frozen_key_value,
    down_factor_matrix,
    down_moment_first,
    down_moment_second,
    up_factor_matrix,
    up_moment_first,
    up_moment_second,
    down_gradient,
    up_gradient,
):
    replica_total_count = lax.axis_size("dp")
    replica = lax.axis_index("dp")
    down_factor_rows = down_factor_matrix.shape[0] // replica_total_count
    up_factor_rows = up_factor_matrix.shape[0] // replica_total_count
    reduced_sum = (
        lax.psum(down_gradient[0].astype(jnp.bfloat16), "dp").astype(jnp.float32),
        lax.psum(up_gradient[0].astype(jnp.bfloat16), "dp").astype(jnp.float32),
    )
    down_parameter, down_first_moment, down_second_moment = adaptive_moment_update(
        down_factor_matrix,
        down_moment_first,
        down_moment_second,
        reduced_sum[0] / replica_total_count,
    )
    up_parameter, up_first_moment, up_second_moment = adaptive_moment_update(
        up_factor_matrix, up_moment_first, up_moment_second, reduced_sum[1] / replica_total_count
    )
    a_next = lax.dynamic_slice_in_dim(
        jnp.stack([down_parameter, down_first_moment, down_second_moment]),
        replica * down_factor_rows,
        down_factor_rows,
        1,
    )
    b_next = lax.dynamic_slice_in_dim(
        jnp.stack([up_parameter, up_first_moment, up_second_moment]),
        replica * up_factor_rows,
        up_factor_rows,
        1,
    )
    factor_a = down_parameter.astype(jnp.bfloat16)
    factor_b = up_parameter.astype(jnp.bfloat16)
    full_a = lax.all_gather(factor_a, "tensor", axis=0, tiled=True)
    column_width = full_a.shape[0]
    columns = factor_b.shape[1]
    which_part = lax.axis_index("tensor") * columns // KEY_VALUE_WIDTH
    chosen_a = lax.dynamic_index_in_dim(full_a, which_part, 1, keepdims=False)
    adapter_scale = 0.5 / math.sqrt(column_width * down_factor_matrix.shape[2])
    weight_change = jnp.dot(chosen_a, factor_b, preferred_element_type=jnp.float32)
    merged_weight = (frozen_key_value.astype(jnp.float32) + adapter_scale * weight_change).astype(
        jnp.bfloat16
    )
    widened = prompt_hidden_input.astype(jnp.float32)
    squares = lax.psum(jnp.sum(widened * widened, axis=1), "tensor")
    inv_rms = lax.rsqrt(squares / column_width + 1e-06)
    scaled = (widened * input_norm_gain[None, :]).astype(jnp.bfloat16)
    totals = jnp.dot(
        lax.all_gather(scaled, "tensor", axis=1, tiled=True),
        merged_weight,
        preferred_element_type=jnp.float32,
    )
    keys_values = (totals * inv_rms[:, None]).astype(jnp.bfloat16)
    return (a_next, b_next, keys_values)


def solution(mesh):
    placed = (
        P("dp", "tensor"),
        P("tensor"),
        P(None, "tensor"),
        P("tensor", None, None),
        P("tensor", None, None),
        P("tensor", None, None),
        P(None, "tensor"),
        P(None, "tensor"),
        P(None, "tensor"),
        P("dp", "tensor", None, None),
        P("dp", None, "tensor"),
    )
    return jax.shard_map(
        body,
        mesh=mesh,
        in_specs=placed,
        out_specs=(
            P(None, ("tensor", "dp"), None, None),
            P(None, "dp", "tensor"),
            P("dp", "tensor"),
        ),
        check_vma=False,
    )
```

profile of v0, /device:TPU:0, one launch (start us, length us, event | category | flops | bytes accessed | tf_op | source)
XLA Modules:
  0.0 216.2 jit_solution(3020143064288122978)
XLA Ops:
  7.2 0.0 copy-start
  7.2 0.0 copy-start.3
  7.2 0.0 all-reduce.3.cloned.1.call-start
  7.2 2.0 convert_bitcast_fusion
  9.2 1.5 convert_bitcast_fusion.1
  10.8 0.0 all-reduce.3.cloned.1.call-update
  10.8 0.0 all-gather.5.cloned.1.call-start
  10.8 75.3 %all-reduce.3.cloned.1.call-done = (bf16[1280,2,64]{0,2,1:T(8,128)(2,1)}, bf16[64,512]{1,0:T(8,128)(2,1)}) async-done(((bf16[1280,2,64]{0,2,1:T(8,128)(2,1)}, bf16[64,512]{1,0:T(8,128)(2,1)}), (bf16[1280,2,64]{0,2,1:T(8,128)(2,1)}, bf16[64,512]{1,0:T(8,128)(2,1)})) %all-reduce.3.cloned.1.call-update) | async-done | bytes 393232 | tf_op jit(solution)/shard_map/psum | solution.py:37
  86.2 3.5 %fusion.26 = (bf16[1280,2,64]{0,2,1:T(8,128)(2,1)}, f32[1280,2,64]{0,2,1:T(8,128)}, f32[1,1280,2,64]{1,3,2,0:T(8,128)}, f32[1,1280,2,64]{1,3,2,0:T(8,128)}) fusion(f32[1280,2,64]{0,2,1:T(8,128)} %param.14, f32[1280,2,64]{0,2,1:T(8,128)} %param.16, bf16[1280,2,64]{0,2,1:T(8,128)(2,1)} %get-tuple-element.3, f32[1280,2,64]{0,2,1:T(8,128)} %param.15), kind=kLoop, calls=%fused_computation.43 | loop fusion | flops 2621440 | bytes 4587520 | tf_op jit(solution)/shard_map/convert_element_type | solution.py:61
  89.6 0.0 copy-start.1
  89.6 0.0 copy-start.2
  89.6 0.0 all-gather.5.cloned.1.call-update
  89.7 0.0 all-gather.3.cloned.1.call-start
  89.7 0.0 copy-done
  89.7 0.0 copy-done.3
  89.7 2.6 %fusion.1 = (f32[1280]{0:T(1024)S(1)}, bf16[1280,1280]{1,0:T(8,128)(2,1)}) fusion(bf16[1280,1280]{1,0:T(8,128)(2,1)S(1)} %copy-done, f32[1280]{0:T(1024)S(1)} %copy-done.3), kind=kLoop, calls=%fused_computation.4 | loop fusion | flops 8190720 | bytes 6563840 | tf_op jit(solution)/shard_map/reduce_sum | solution.py:74
  92.4 0.0 all-gather.3.cloned.1.call-update
  92.4 5.8 %psum.23 = f32[1280]{0:T(1024)S(1)} all-reduce(f32[1280]{0:T(1024)S(1)} %get-tuple-element.7), channel_id=1, replica_groups=mesh['dp'=8,'tensor'=4] {'tensor'}, use_global_device_ids=true, to_apply=%region_3.4 | all-reduce | flops 1280 | bytes 10240 | tf_op jit(solution)/shard_map/psum | solution.py:74
  98.2 0.0 copy-done.1
  98.2 0.0 copy-done.2
  98.2 1.1 fusion.20
  99.3 0.6 fusion.22
  99.9 2.1 fusion.11
  102.0 5.1 %all-gather.5.cloned.1.call-done = bf16[5120,2,64]{0,2,1:T(8,128)(2,1)} async-done(((bf16[1280,2,64]{0,2,1:T(8,128)(2,1)}), bf16[5120,2,64]{0,2,1:T(8,128)(2,1)}) %all-gather.5.cloned.1.call-update) | async-done | bytes 1310736 | tf_op jit(solution)/shard_map/all_gather | solution.py:63
  107.1 86.8 %all-gather.3.cloned.1.call-done = bf16[1280,5120]{1,0:T(8,128)(2,1)} async-done(((bf16[1280,1280]{1,0:T(8,128)(2,1)}), bf16[1280,5120]{1,0:T(8,128)(2,1)}) %all-gather.3.cloned.1.call-update) | async-done | bytes 13107216 | tf_op jit(solution)/shard_map/all_gather | solution.py:78
  193.8 15.9 %fusion.2 = bf16[1280,512]{1,0:T(8,128)(2,1)} fusion(bf16[1280,5120]{1,0:T(8,128)(2,1)} %all-gather.3.cloned.1.call-done, bf16[5120,512]{1,0:T(8,128)(2,1)} %param.13, f32[1280]{0:T(1024)S(1)} %add_rsqrt_fusion, bf16[5120,2,64]{0,2,1:T(8,128)(2,1)} %all-gather.5.cloned.1.call-done, s32[]{:T(128)S(6)} %select_n.18, f32[64,512]{1,0:T(8,128)S(1)} %get-tuple-element.12), kind=kOutput, calls=%fused_computation.6 | convolution fusion | flops 7058259968 | bytes 20452356 | tf_op jit(solution)/shard_map/dot_general | solution.py:77
  (1 shorter events, 0.0 us)
Async XLA Ops:
  7.2 82.5 %copy-start = (bf16[1280,1280]{1,0:T(8,128)(2,1)S(1)}, bf16[1280,1280]{1,0:T(8,128)(2,1)}, u32[]{:S(2)}) copy-start(bf16[1280,1280]{1,0:T(8,128)(2,1)} %param.11) | copy-start | bytes 9830404
  7.2 82.5 %copy-start.3 = (f32[1280]{0:T(1024)S(1)}, f32[1280]{0:T(1024)}, u32[]{:S(2)}) copy-start(f32[1280]{0:T(1024)} %param.12) | copy-start | bytes 15364
  7.2 79.0 %all-reduce.3.cloned.1.call-start = ((), (), s32[]{:S(2)}) async-start(), calls=%async_computation.2 | async-start | bytes 786432 | tf_op jit(solution)/shard_map/psum | solution.py:37
  10.8 96.3 %all-gather.5.cloned.1.call-start = ((), (), s32[]{:S(2)}) async-start(), calls=%async_computation.1 | async-start | bytes 1638400 | tf_op jit(solution)/shard_map/all_gather | solution.py:63
  89.6 8.6 %copy-start.1 = (f32[64,512]{1,0:T(8,128)S(1)}, f32[64,512]{1,0:T(8,128)}, u32[]{:S(2)}) copy-start(f32[64,512]{1,0:T(8,128)} %param.19) | copy-start | bytes 393220
  89.6 8.6 %copy-start.2 = (f32[64,512]{1,0:T(8,128)S(1)}, f32[64,512]{1,0:T(8,128)}, u32[]{:S(2)}) copy-start(f32[64,512]{1,0:T(8,128)} %param.17) | copy-start | bytes 393220
  89.7 104.2 %all-gather.3.cloned.1.call-start = ((), (), s32[]{:S(2)}) async-start(), calls=%async_computation | async-start | bytes 16384000 | tf_op jit(solution)/shard_map/all_gather | solution.py:78
Sparse Core Ops, SparseCore 0:
  11.9 74.1 all-reduce.2
  89.8 17.2 all-gather.4
  108.7 85.0 all-gather.2
where the time goes:
time: 216 us
  waiting for transfers between devices  167 us (77%)
  matrix products  15.9 us (7%)
  between operations  13.8 us (6%)
  other arithmetic  13.4 us (6%)
  blocking collectives  5.77 us (3%)
    all_gather x1, waiting for transfers between devices, body(): lax.all_gather(scaled, 'tensor', axis=1, tiled=True)  86.8 us
    psum x1, waiting for transfers between devices, body(): lax.psum(down_gradient[0].astype(jnp.bfloat16), 'dp').astype(jnp.float32)  75.3 us
    dot_general x1, matrix products, body(): jnp.dot(lax.all_gather(scaled, 'tensor', axis=1, tiled=True), merged_weig...  15.9 us
    psum x1, blocking collectives, body(): squares = lax.psum(jnp.sum(widened * widened, axis=1), 'tensor')  5.77 us
    all_gather x1, waiting for transfers between devices, body(): full_a = lax.all_gather(factor_a, 'tensor', axis=0, tiled=True)  5.09 us
  transfers between devices with their start and end apart: 3, of which 3 were waited for; matrix products, arithmetic and copies ran while one was open for 3% of the time, Pallas kernels for 0%

commit v1 on v0

v1 whole, which is shorter than its diff:
```python
import functools
import math

import jax
import jax.numpy as jnp
from jax import lax
from jax.experimental import pallas as pl
from jax.experimental.pallas import tpu as pltpu
from jax.sharding import PartitionSpec as P

KEY_VALUE_WIDTH = 1024
STEP = 100
CORES = 2
CHUNKS = 4


def adaptive_moment_update(param, first, second, grad_mean):
    first_new = 0.9 * first + 0.1 * grad_mean
    second_new = 0.999 * second + 0.001 * grad_mean * grad_mean
    step_size = first_new / (1.0 - 0.9**STEP) / (jnp.sqrt(second_new / (1.0 - 0.999**STEP)) + 1e-08)
    return (param - 0.1 * step_size, first_new, second_new)


def pack_kernel(down_ref, up_ref, out_ref):
    shares, rows, lanes = out_ref.shape
    down = down_ref[...].T
    up = up_ref[...]
    down_rows = down.shape[0] // shares
    up_rows = up.shape[0] // shares
    for i in range(shares):
        pieces = [down[i * down_rows : (i + 1) * down_rows]]
        for k in range(up.shape[1] // lanes):
            pieces.append(up[i * up_rows : (i + 1) * up_rows, k * lanes : (k + 1) * lanes])
        out_ref[i] = jnp.concatenate(pieces, axis=0).astype(jnp.bfloat16)


def adam_kernel(
    replicas, grad_ref, dp_ref, dm_ref, dv_ref, up_ref, um_ref, uv_ref, a_ref, b_ref, fa_ref, fb_ref
):
    total = jnp.sum(grad_ref[...].astype(jnp.float32), axis=0) / replicas
    down_rows = dp_ref.shape[1]
    up_rows, columns = up_ref.shape
    lanes = total.shape[1]
    down = total[:down_rows].T
    up = jnp.concatenate(
        [
            total[down_rows + k * up_rows : down_rows + (k + 1) * up_rows]
            for k in range(columns // lanes)
        ],
        axis=1,
    )
    p, m, v = adaptive_moment_update(dp_ref[...], dm_ref[...], dv_ref[...], down)
    a_ref[0], a_ref[1], a_ref[2] = p, m, v
    fa_ref[...] = p.T.astype(jnp.bfloat16)
    p, m, v = adaptive_moment_update(up_ref[...], um_ref[...], uv_ref[...], up)
    b_ref[0], b_ref[1], b_ref[2] = p, m, v
    fb_ref[...] = p.astype(jnp.bfloat16)


def vmem(count):
    return [pl.BlockSpec(memory_space=pltpu.VMEM)] * count


def body(
    prompt_hidden_input,
    input_norm_gain,
    frozen_key_value,
    down_factor_matrix,
    down_moment_first,
    down_moment_second,
    up_factor_matrix,
    up_moment_first,
    up_moment_second,
    down_gradient,
    up_gradient,
):
    n_dp = lax.axis_size("dp")
    n_tensor = lax.axis_size("tensor")
    chips = n_tensor // CORES
    replica = lax.axis_index("dp")
    place = lax.axis_index("tensor")
    chip, core = place // CORES, place % CORES
    tokens, features = prompt_hidden_input.shape
    width, columns = frozen_key_value.shape
    rank = up_factor_matrix.shape[0]
    factors = down_factor_matrix.shape[1] * rank
    chip_features = CORES * features

    def to_sibling(value):
        return lax.ppermute(value, "tensor", [(t, t ^ 1) for t in range(n_tensor)])

    def to_chip(value, step):
        pairs = [
            (CORES * q + k, CORES * ((q + step) % chips) + k)
            for q in range(chips)
            for k in range(CORES)
        ]
        return lax.ppermute(value, "tensor", pairs)

    share = chip_features // n_dp
    pieces = []
    for step in range(1, chips):
        row = (chip + step) % chips * chip_features + replica * share
        pieces.append(to_chip(lax.dynamic_slice_in_dim(frozen_key_value, row, share, 0), step))
    gathered = [lax.all_gather(piece, "dp", axis=0, tiled=True) for piece in pieces]

    sibling_input = to_sibling(prompt_hidden_input)
    sibling_gain = to_sibling(input_norm_gain)

    down_rows = features // n_dp
    up_rows = rank // n_dp
    packed_rows = down_rows + up_rows * columns // 128

    def by_rank(value):
        return jnp.transpose(value, (1, 2, 0)).reshape(factors, features)

    packed = pl.pallas_call(
        pack_kernel,
        out_shape=jax.ShapeDtypeStruct((n_dp, packed_rows, 128), jnp.bfloat16),
        in_specs=vmem(2),
        out_specs=vmem(1)[0],
    )(by_rank(down_gradient[0]), up_gradient[0])
    exchanged = lax.all_to_all(packed, "dp", 0, 0, tiled=True)

    def own_down(value):
        return lax.dynamic_slice_in_dim(by_rank(value), replica * down_rows, down_rows, 1)

    def own_up(value):
        return lax.dynamic_slice_in_dim(value, replica * up_rows, up_rows, 0)

    a_next, b_next, share_a, share_b = pl.pallas_call(
        functools.partial(adam_kernel, n_dp),
        out_shape=(
            jax.ShapeDtypeStruct((3, factors, down_rows), jnp.float32),
            jax.ShapeDtypeStruct((3, up_rows, columns), jnp.float32),
            jax.ShapeDtypeStruct((down_rows, factors), jnp.bfloat16),
            jax.ShapeDtypeStruct((up_rows, columns), jnp.bfloat16),
        ),
        in_specs=vmem(7),
        out_specs=tuple(vmem(4)),
    )(
        exchanged,
        own_down(down_factor_matrix),
        own_down(down_moment_first),
        own_down(down_moment_second),
        own_up(up_factor_matrix),
        own_up(up_moment_first),
        own_up(up_moment_second),
    )
    a_next = jnp.transpose(
        a_next.reshape(3, factors // rank, rank, down_rows), (0, 3, 1, 2)
    )

    def over_replicas(value):
        copies = jnp.broadcast_to(value[None], (n_dp,) + value.shape)
        return lax.all_to_all(copies, "dp", 0, 0, tiled=True).reshape(
            (n_dp * value.shape[0],) + value.shape[1:]
        )

    factor_a = over_replicas(share_a)
    factor_b = over_replicas(share_b)
    sibling_a = to_sibling(factor_a)

    adapter_scale = 0.5 / math.sqrt(width * rank)

    def merged(weights, first_row, factor_b, owner):
        part = owner * columns // KEY_VALUE_WIDTH
        halves = []
        for factor, half in ((factor_a, core), (sibling_a, 1 - core)):
            chosen = lax.dynamic_slice_in_dim(factor, part * rank, rank, 1)
            change = jnp.dot(chosen, factor_b, preferred_element_type=jnp.float32)
            block = lax.dynamic_slice_in_dim(weights, first_row + half * features, features, 0)
            halves.append(
                (block.astype(jnp.float32) + adapter_scale * change).astype(jnp.bfloat16)
            )
        return jnp.concatenate(halves, axis=0)

    own_wide = prompt_hidden_input.astype(jnp.float32)
    sibling_wide = sibling_input.astype(jnp.float32)
    squares = jnp.sum(own_wide * own_wide, axis=1) + jnp.sum(sibling_wide * sibling_wide, axis=1)
    squares = squares + sum(to_chip(squares, step) for step in range(1, chips))
    inv_rms = lax.rsqrt(squares / width + 1e-06)
    scaled = jnp.concatenate(
        [
            (own_wide * input_norm_gain[None, :]).astype(jnp.bfloat16),
            (sibling_wide * sibling_gain[None, :]).astype(jnp.bfloat16),
        ],
        axis=1,
    )

    received = []
    for step in range(1, chips):
        owner = CORES * ((chip - step) % chips) + core
        weights = merged(gathered[step - 1], 0, to_chip(factor_b, step), owner)
        parts = []
        for rows in jnp.split(scaled, CHUNKS, axis=0):
            product = jnp.dot(rows, weights, preferred_element_type=jnp.float32)
            parts.append(to_chip(product.astype(jnp.bfloat16), chips - step))
        received.append(jnp.concatenate(parts, axis=0).astype(jnp.float32))
    own_weights = merged(frozen_key_value, chip * chip_features, factor_b, place)
    totals = jnp.dot(scaled, own_weights, preferred_element_type=jnp.float32)
    totals = totals + sum(received)
    keys_values = (totals * inv_rms[:, None]).astype(jnp.bfloat16)
    return (a_next, b_next, keys_values)


def solution(mesh):
    placed = (
        P("dp", "tensor"),
        P("tensor"),
        P(None, "tensor"),
        P("tensor", None, None),
        P("tensor", None, None),
        P("tensor", None, None),
        P(None, "tensor"),
        P(None, "tensor"),
        P(None, "tensor"),
        P("dp", "tensor", None, None),
        P("dp", None, "tensor"),
    )
    return jax.shard_map(
        body,
        mesh=mesh,
        in_specs=placed,
        out_specs=(
            P(None, ("tensor", "dp"), None, None),
            P(None, "dp", "tensor"),
            P("dp", "tensor"),
        ),
        check_vma=False,
    )
```

time: 216 us -> 147 us (0.68)
  waiting for transfers between devices: 167 us -> 59.2 us
  starting transfers between devices: 0.12 us -> 19.8 us
  local copies, waits for them, and re-layouts: 0.02 us -> 10.1 us
  blocking collectives: 5.77 us -> 11.6 us
  Pallas kernels: 0 us -> 4.17 us
  other arithmetic: 13.4 us -> 9.26 us
    all_gather x2 -> x1, waiting for transfers between devices: 91.9 us -> 0.01 us  [body(): lax.all_gather(piece, 'dp', axis=0, tiled=True)]
    psum x1 -> x0, waiting for transfers between devices: 75.3 us -> none  [body(): lax.psum(down_gradient[0].astype(jnp.bfloat16), 'dp').astype(jnp.float32)]
    ppermute x0 -> x10, waiting for transfers between devices: none -> 32.7 us  [the longest x7 32.7 us: to_chip(): return lax.ppermute(value, 'tensor', pairs)]
    all_to_all x0 -> x2, waiting for transfers between devices: none -> 26.5 us  [the longest x1 15.2 us: body(): exchanged = lax.all_to_all(packed, 'dp', 0, 0, tiled=True)]
    all_to_all x0 -> x1, blocking collectives: none -> 11.6 us  [over_replicas(): lax.all_to_all(copies, 'dp', 0, 0, tiled=True)]
    ppermute x0 -> x10, starting transfers between devices: none -> 10.3 us  [the longest x7 10.1 us: to_chip(): return lax.ppermute(value, 'tensor', pairs)]
    all_to_all x0 -> x2, starting transfers between devices: none -> 9.52 us  [the longest x1 6.08 us: body(): exchanged = lax.all_to_all(packed, 'dp', 0, 0, tiled=True)]
    convert_element_type x3 -> x0, other arithmetic: 7.01 us -> none  [the longest x1 3.47 us: body(): factor_a = down_parameter.astype(jnp.bfloat16)]
  transfers between devices with their start and end apart: 3 -> 13, of which waited for: 3 -> 7; matrix products, arithmetic and copies ran while one was open for 3% -> 20% of each run, Pallas kernels for 0% -> 3%
where the time goes in v1:
time: 147 us; the launch traced here: 146 us
  waiting for transfers between devices  59.2 us (40%)
  starting transfers between devices  19.8 us (13%)
  matrix products  17.6 us (12%)
  between operations  14.3 us (10%)
  blocking collectives  11.6 us (8%)
  local copies, waits for them, and re-layouts  10.1 us (7%)
  other arithmetic  9.26 us (6%)
  Pallas kernels  4.17 us (3%)
    ppermute x7, waiting for transfers between devices, to_chip(): return lax.ppermute(value, 'tensor', pairs)  32.7 us
    all_to_all x1, waiting for transfers between devices, body(): exchanged = lax.all_to_all(packed, 'dp', 0, 0, tiled=True)  15.2 us
    all_to_all x1, blocking collectives, over_replicas(): lax.all_to_all(copies, 'dp', 0, 0, tiled=True)  11.6 us
    all_to_all x1, waiting for transfers between devices, over_replicas(): lax.all_to_all(copies, 'dp', 0, 0, tiled=True)  11.3 us
    ppermute x7, starting transfers between devices, to_chip(): return lax.ppermute(value, 'tensor', pairs)  10.1 us
    dot_general x4, matrix products, merged(): change = jnp.dot(chosen, factor_b, preferred_element_type=jnp.float32)  7.63 us
    all_to_all x1, starting transfers between devices, body(): exchanged = lax.all_to_all(packed, 'dp', 0, 0, tiled=True)  6.08 us
    dot_general x4, matrix products, body(): product = jnp.dot(rows, weights, preferred_element_type=jnp.float32)  5.32 us
  transfers between devices with their start and end apart: 13, of which 7 were waited for; matrix products, arithmetic and copies ran while one was open for 20% of the time, Pallas kernels for 3%

profile of v1, /device:TPU:0, one launch (start us, length us, event | category | flops | bytes accessed | tf_op | source)
XLA Modules:
  0.0 146.1 jit_solution(5425291137807068939)
XLA Ops:
  7.2 0.0 copy-start
  7.2 0.0 all-gather.2.cloned.1.call-start
  7.3 1.1 constant_dynamic-slice_fusion
  8.3 3.0 %collective-permute-start.3 = (bf16[320,512]{1,0:T(8,128)(2,1)S(1)}, bf16[320,512]{1,0:T(8,128)(2,1)S(1)}, u32[]{:S(2)}, u32[]{:S(2)}) collective-permute-start(bf16[320,512]{1,0:T(8,128)(2,1)S(1)} %constant_dynamic-slice_fusion), channel_id=1, source_target_pairs={{0,2},{1,3},{2,0},{3,1},{4,6},{5,7},{6,4},{7,5},{8,10},{9,11},{10,... | collective-permute-start | bytes 983048 | tf_op jit(solution)/shard_map/ppermute | solution.py:98
  11.3 7.7 %collective-permute-done.3 = bf16[320,512]{1,0:T(8,128)(2,1)S(1)} collective-permute-done((bf16[320,512]{1,0:T(8,128)(2,1)S(1)}, bf16[320,512]{1,0:T(8,128)(2,1)S(1)}, u32[]{:S(2)}, u32[]{:S(2)}) %collective-permute-start.3) | collective-permute-done | bytes 327712 | tf_op jit(solution)/shard_map/ppermute | solution.py:98
  19.0 0.0 copy-start.4
  19.0 0.0 copy-start.5
  19.0 0.7 copy-done.4
  19.8 0.0 all-gather.2.cloned.1.call-update
  19.8 0.1 collective-permute-start
  19.9 2.0 %shard_map.130 = bf16[8,192,128]{2,1,0:T(8,128)(2,1)} custom-call(f32[128,1280]{1,0:T(8,128)} %bitcast.30, f32[64,512]{1,0:T(8,128)} %bitcast.32), custom_call_target="tpu_custom_call" | custom-call | tf_op jit(solution)/shard_map/pallas_call | solution.py:117
  21.9 6.1 %all-to-all-start = ((bf16[8,192,128]{2,1,0:T(8,128)(2,1)}), bf16[8,192,128]{2,1,0:T(8,128)(2,1)S(1)}, u32[]{:S(2)}, u32[]{:S(2)}) async-start(bf16[8,192,128]{2,1,0:T(8,128)(2,1)} %shard_map.130), calls=%async_computation | async-start | bytes 786432 | tf_op jit(solution)/shard_map/all_to_all | solution.py:123
  28.0 1.3 constant_dynamic-slice_fusion.3.up_ref
  29.3 1.3 constant_dynamic-slice_fusion.1
  30.7 0.0 copy-done
  30.7 0.7 constant_dynamic-slice_fusion.6.dp_ref
  31.4 1.9 %constant_dynamic-slice_fusion.4 = (f32[128,160]{1,0:T(8,128)}, f32[128,160]{1,0:T(8,128)}) fusion(f32[128,1280]{1,0:T(8,128)} %bitcast.33, s32[]{:T(128)S(6)} %select_n.58, f32[128,1280]{1,0:T(8,128)} %bitcast.34), kind=kLoop, calls=%fused_computation.60 | loop fusion | bytes 327684 | tf_op jit(solution)/shard_map/dynamic_slice | solution.py:126
  33.3 15.2 %all-to-all-done.grad_ref = bf16[8,192,128]{2,1,0:T(8,128)(2,1)S(1)} async-done(((bf16[8,192,128]{2,1,0:T(8,128)(2,1)}), bf16[8,192,128]{2,1,0:T(8,128)(2,1)S(1)}, u32[]{:S(2)}, u32[]{:S(2)}) %all-to-all-start) | async-done | bytes 393248 | tf_op jit(solution)/shard_map/all_to_all | solution.py:123
  48.5 0.0 copy-start.3
  48.5 0.7 copy-done.3
  49.3 2.1 %shard_map.131 = (f32[3,128,160]{2,1,0:T(8,128)}, f32[3,8,512]{2,1,0:T(8,128)}, bf16[160,128]{1,0:T(8,128)(2,1)}, bf16[8,512]{1,0:T(8,128)(2,1)}) custom-call(bf16[8,192,128]{2,1,0:T(8,128)(2,1)} %copy-done.3, f32[128,160]{1,0:T(8,128)} %constant_dynamic-slice_fusion.6.dp_ref, f32[128,160]{1,0:T(8,128)} %get-tuple-element.16.dm_ref, ...), custom_call_target="tpu_custom_call" | custom-call | tf_op jit(solution)/shard_map/pallas_call | solution.py:131
  51.4 0.7 broadcast_in_dim.5
  52.1 11.6 %all_to_all.15 = bf16[8,8,512]{2,1,0:T(8,128)(2,1)S(1)} all-to-all(bf16[8,8,512]{2,1,0:T(8,128)(2,1)S(1)} %broadcast_in_dim.5), channel_id=1, replica_groups=mesh['dp'=8,'tensor'=4] {'dp'}, dimensions={0} | all-to-all | bytes 131072 | tf_op jit(solution)/shard_map/all_to_all | solution.py:156
  63.7 1.5 %broadcast_in_dim.4 = bf16[8,160,128]{2,1,0:T(8,128)(2,1)} broadcast(bf16[160,128]{1,0:T(8,128)(2,1)} %get-tuple-element.9), dimensions={1,2} | broadcast | bytes 368640 | tf_op jit(solution)/shard_map/broadcast_in_dim | solution.py:155
  65.2 3.4 %all-to-all-start.1 = ((bf16[8,160,128]{2,1,0:T(8,128)(2,1)}), bf16[8,160,128]{2,1,0:T(8,128)(2,1)S(1)}, u32[]{:S(2)}, u32[]{:S(2)}) async-start(bf16[8,160,128]{2,1,0:T(8,128)(2,1)} %broadcast_in_dim.4), calls=%async_computation.1 | async-start | bytes 655360 | tf_op jit(solution)/shard_map/all_to_all | solution.py:156
  68.7 0.0 copy-done.5
  68.7 0.1 collective-permute-start.1
  68.9 4.6 %fusion.1 = (f32[1280]{0:T(1024)S(1)}, bf16[1280,1280]{1,0:T(8,128)(2,1)}) fusion(bf16[1280,1280]{1,0:T(8,128)(2,1)} %param.11, f32[1280]{0:T(1024)S(1)} %copy-done.5), kind=kLoop, calls=%fused_computation.14 | loop fusion | flops 8190720 | bytes 6563840 | tf_op jit(solution)/shard_map/reduce_sum | solution.py:180
  73.5 1.5 %collective-permute-start.4 = (bf16[64,512]{1,0:T(8,128)(2,1)S(1)}, bf16[64,512]{1,0:T(8,128)(2,1)S(1)}, u32[]{:S(2)}, u32[]{:S(2)}) collective-permute-start(bf16[64,512]{1,0:T(8,128)(2,1)S(1)} %bitcast.31), channel_id=1, source_target_pairs={{0,2},{1,3},{2,0},{3,1},{4,6},{5,7},{6,4},{7,5},{8,10},{9,11},{10,... | collective-permute-start | bytes 196616 | tf_op jit(solution)/shard_map/ppermute | solution.py:98
  75.0 11.3 %all-to-all-done.1 = bf16[8,160,128]{2,1,0:T(8,128)(2,1)S(1)} async-done(((bf16[8,160,128]{2,1,0:T(8,128)(2,1)}), bf16[8,160,128]{2,1,0:T(8,128)(2,1)S(1)}, u32[]{:S(2)}, u32[]{:S(2)}) %all-to-all-start.1) | async-done | bytes 327712 | tf_op jit(solution)/shard_map/all_to_all | solution.py:156
  86.4 0.0 collective-permute-start.2
  86.4 1.9 %fusion.10 = bf16[1280,512]{1,0:T(8,128)(2,1)S(1)} fusion(bf16[5120,512]{1,0:T(8,128)(2,1)} %param.13, s32[]{:T(128)S(6)} %select_n.62, bf16[1280,128]{1,0:T(8,128)(2,1)S(1)} %bitcast.28, s32[]{:T(128)S(6)} %select_n.64, bf16[8,8,512]{2,1,0:T(8,128)(2,1)S(1)} %all_to_all.15), kind=kOutput, calls=%fused_computation.27 | convolution fusion | flops 86507520 | bytes 3014664 | tf_op jit(solution)/shard_map/dot_general | solution.py:171
  88.2 0.0 collective-permute-done.1
  88.2 0.0 collective-permute-done
  88.3 4.6 %fusion.3 = (f32[1280]{0:T(1024)S(1)}, bf16[1280,1280]{1,0:T(8,128)(2,1)}) fusion(bf16[1280,1280]{1,0:T(8,128)(2,1)} %collective-permute-done, f32[1280]{0:T(1024)S(1)} %collective-permute-done.1), kind=kLoop, calls=%fused_computation.16 | loop fusion | flops 8190720 | bytes 6563840 | tf_op jit(solution)/shard_map/reduce_sum | solution.py:180
  92.9 1.5 %collective-permute-start.9 = (f32[1280]{0:T(1024)S(1)}, f32[1280]{0:T(1024)S(1)}, u32[]{:S(2)}, u32[]{:S(2)}) collective-permute-start(f32[1280]{0:T(1024)S(1)} %add.111), channel_id=1, source_target_pairs={{0,2},{1,3},{2,0},{3,1},{4,6},{5,7},{6,4},{7,5},{8,10},{9,11},{10,... | collective-permute-start | bytes 15368 | tf_op jit(solution)/shard_map/ppermute | solution.py:98
  94.4 0.0 collective-permute-done.4
  94.4 0.0 all-gather.2.cloned.1.call-done
  94.4 0.0 copy-start.1
  94.4 2.0 %add_convert_fusion.1 = bf16[1280,512]{1,0:T(8,128)(2,1)S(1)} fusion(bf16[2560,512]{1,0:T(8,128)(2,1)} %all-gather.2.cloned.1.call-done, s32[]{:T(128)S(6)} %select_n.68, bf16[64,512]{1,0:T(8,128)(2,1)S(1)} %collective-permute-done.4, bf16[1280,128]{1,0:T(8,128)(2,1)S(1)} %bitcast.29, s32[]{:T(128)S(6)} %select_n.71), kind=kOutput, calls=%fused_computation.34 | convolution fusion | flops 86507520 | bytes 3014664 | tf_op jit(solution)/shard_map/dot_general | solution.py:171
  96.4 0.0 collective-permute-done.2
  96.4 1.9 %add_convert_fusion = bf16[1280,512]{1,0:T(8,128)(2,1)S(1)} fusion(bf16[2560,512]{1,0:T(8,128)(2,1)} %all-gather.2.cloned.1.call-done, s32[]{:T(128)S(6)} %select_n.72, bf16[64,512]{1,0:T(8,128)(2,1)S(1)} %collective-permute-done.4, bf16[1280,128]{1,0:T(8,128)(2,1)S(1)} %collective-permute-done.2, s32[]{:T(128)S(6)} %select_n.71), kind=kOutput, calls=%fused_computation.33 | convolution fusion | flops 86507520 | bytes 3014664 | tf_op jit(solution)/shard_map/dot_general | solution.py:171
  98.3 0.0 copy-done.1
  98.3 0.0 copy-start.2
  98.3 2.3 %fusion.36 = bf16[320,512]{1,0:T(8,128)(2,1)S(1)} fusion(bf16[1280,1280]{1,0:T(8,128)(2,1)S(1)} %copy-done.1, bf16[1280,1280]{1,0:T(8,128)(2,1)} %get-tuple-element.12, bf16[1280,512]{1,0:T(8,128)(2,1)S(1)} %add_convert_fusion, bf16[1280,512]{1,0:T(8,128)(2,1)S(1)} %add_convert_fusion.1), kind=kOutput, calls=%fused_computation.46 | convolution fusion | flops 847544320 | bytes 9502720 | tf_op jit(solution)/shard_map/dot_general | solution.py:197
  100.6 0.0 copy-done.2
  100.6 1.0 fusion.33
  101.6 1.0 fusion.30
  102.6 1.0 fusion.27
  103.7 0.6 collective-permute-start.5
  104.3 1.5 %collective-permute-start.6 = (bf16[320,512]{1,0:T(8,128)(2,1)S(1)}, bf16[320,512]{1,0:T(8,128)(2,1)S(1)}, u32[]{:S(2)}, u32[]{:S(2)}) collective-permute-start(bf16[320,512]{1,0:T(8,128)(2,1)S(1)} %fusion.33), channel_id=1, source_target_pairs={{0,2},{1,3},{2,0},{3,1},{4,6},{5,7},{6,4},{7,5},{8,10},{9,11},{10,... | collective-permute-start | bytes 983048 | tf_op jit(solution)/shard_map/ppermute | solution.py:98
  105.7 0.5 collective-permute-start.7
  106.3 1.5 %collective-permute-start.8 = (bf16[320,512]{1,0:T(8,128)(2,1)S(1)}, bf16[320,512]{1,0:T(8,128)(2,1)S(1)}, u32[]{:S(2)}, u32[]{:S(2)}) collective-permute-start(bf16[320,512]{1,0:T(8,128)(2,1)S(1)} %fusion.27), channel_id=1, source_target_pairs={{0,2},{1,3},{2,0},{3,1},{4,6},{5,7},{6,4},{7,5},{8,10},{9,11},{10,... | collective-permute-start | bytes 983048 | tf_op jit(solution)/shard_map/ppermute | solution.py:98
  107.8 1.9 %fusion.11 = bf16[1280,512]{1,0:T(8,128)(2,1)S(1)} fusion(bf16[5120,512]{1,0:T(8,128)(2,1)} %param.13, s32[]{:T(128)S(6)} %select_n.65, bf16[1280,128]{1,0:T(8,128)(2,1)S(1)} %collective-permute-done.2, s32[]{:T(128)S(6)} %select_n.64, bf16[8,8,512]{2,1,0:T(8,128)(2,1)S(1)} %all_to_all.15), kind=kOutput, calls=%fused_computation.28 | convolution fusion | flops 86507520 | bytes 3014664 | tf_op jit(solution)/shard_map/dot_general | solution.py:171
  109.6 0.0 collective-permute-done.9
  109.7 4.6 %collective-permute-done.5 = bf16[320,512]{1,0:T(8,128)(2,1)S(1)} collective-permute-done((bf16[320,512]{1,0:T(8,128)(2,1)S(1)}, bf16[320,512]{1,0:T(8,128)(2,1)S(1)}, u32[]{:S(2)}, u32[]{:S(2)}) %collective-permute-start.5) | collective-permute-done | bytes 327712 | tf_op jit(solution)/shard_map/ppermute | solution.py:98
  114.3 7.0 %collective-permute-done.6 = bf16[320,512]{1,0:T(8,128)(2,1)S(1)} collective-permute-done((bf16[320,512]{1,0:T(8,128)(2,1)S(1)}, bf16[320,512]{1,0:T(8,128)(2,1)S(1)}, u32[]{:S(2)}, u32[]{:S(2)}) %collective-permute-start.6) | collective-permute-done | bytes 327712 | tf_op jit(solution)/shard_map/ppermute | solution.py:98
  121.3 7.0 %collective-permute-done.7 = bf16[320,512]{1,0:T(8,128)(2,1)S(1)} collective-permute-done((bf16[320,512]{1,0:T(8,128)(2,1)S(1)}, bf16[320,512]{1,0:T(8,128)(2,1)S(1)}, u32[]{:S(2)}, u32[]{:S(2)}) %collective-permute-start.7) | collective-permute-done | bytes 327712 | tf_op jit(solution)/shard_map/ppermute | solution.py:98
  128.3 6.3 %collective-permute-done.8 = bf16[320,512]{1,0:T(8,128)(2,1)S(1)} collective-permute-done((bf16[320,512]{1,0:T(8,128)(2,1)S(1)}, bf16[320,512]{1,0:T(8,128)(2,1)S(1)}, u32[]{:S(2)}, u32[]{:S(2)}) %collective-permute-start.8) | collective-permute-done | bytes 327712 | tf_op jit(solution)/shard_map/ppermute | solution.py:98
  134.6 4.7 %fusion.9 = bf16[1280,512]{1,0:T(8,128)(2,1)} fusion(bf16[1280,1280]{1,0:T(8,128)(2,1)S(1)} %copy-done.2, bf16[1280,1280]{1,0:T(8,128)(2,1)S(1)} %copy-done.1, bf16[1280,512]{1,0:T(8,128)(2,1)S(1)} %fusion.11, bf16[1280,512]{1,0:T(8,128)(2,1)S(1)} %fusion.10, bf16[320,512]{1,0:T(8,128)(2,1)S(1)} %collective-permute-done.8, ...), kind=kOutput, calls=%fused_computation.26 | convolution fusion | flops 3381002240 | bytes 11801600 | tf_op jit(solution)/shard_map/dot_general | solution.py:201
  (2 shorter events, 0.0 us)
Async XLA Ops:
  7.2 23.5 %copy-start = (f32[1280,2,64]{0,2,1:T(8,128)S(1)}, f32[1280,2,64]{0,2,1:T(8,128)}, u32[]{:S(2)}) copy-start(f32[1280,2,64]{0,2,1:T(8,128)} %param.14) | copy-start | bytes 1966084
  7.2 87.2 %all-gather.2.cloned.1.call-start = ((), (), s32[]{:S(2)}) async-start(), calls=%async_computation.3 | async-start | bytes 2949120 | tf_op jit(solution)/shard_map/all_gather | solution.py:105
  8.3 10.7 %collective-permute-start.3 = (bf16[320,512]{1,0:T(8,128)(2,1)S(1)}, bf16[320,512]{1,0:T(8,128)(2,1)S(1)}, u32[]{:S(2)}, u32[]{:S(2)}) collective-permute-start(bf16[320,512]{1,0:T(8,128)(2,1)S(1)} %constant_dynamic-slice_fusion), channel_id=1, source_target_pairs={{0,2},{1,3},{2,0},{3,1},{4,6},{5,7},{6,4},{7,5},{8,10},{9,11},{10,... | collective-permute-start | bytes 983048 | tf_op jit(solution)/shard_map/ppermute | solution.py:98
  19.0 0.7 copy-start.4
  19.0 49.7 %copy-start.5 = (f32[1280]{0:T(1024)S(1)}, f32[1280]{0:T(1024)}, u32[]{:S(2)}) copy-start(f32[1280]{0:T(1024)} %param.12) | copy-start | bytes 15364
  19.8 68.4 %collective-permute-start = (bf16[1280,1280]{1,0:T(8,128)(2,1)}, bf16[1280,1280]{1,0:T(8,128)(2,1)}, u32[]{:S(2)}, u32[]{:S(2)}) collective-permute-start(bf16[1280,1280]{1,0:T(8,128)(2,1)} %param.11), channel_id=1, source_target_pairs={{0,1},{1,0},{2,3},{3,2},{4,5},{5,4},{6,7},{7,6},{8,9},{9,8},{10,11... | collective-permute-start | bytes 9830408 | tf_op jit(solution)/shard_map/ppermute | solution.py:90
  21.9 26.6 %all-to-all-start = ((bf16[8,192,128]{2,1,0:T(8,128)(2,1)}), bf16[8,192,128]{2,1,0:T(8,128)(2,1)S(1)}, u32[]{:S(2)}, u32[]{:S(2)}) async-start(bf16[8,192,128]{2,1,0:T(8,128)(2,1)} %shard_map.130), calls=%async_computation | async-start | bytes 786432 | tf_op jit(solution)/shard_map/all_to_all | solution.py:123
  48.5 0.7 copy-start.3
  65.2 21.1 %all-to-all-start.1 = ((bf16[8,160,128]{2,1,0:T(8,128)(2,1)}), bf16[8,160,128]{2,1,0:T(8,128)(2,1)S(1)}, u32[]{:S(2)}, u32[]{:S(2)}) async-start(bf16[8,160,128]{2,1,0:T(8,128)(2,1)} %broadcast_in_dim.4), calls=%async_computation.1 | async-start | bytes 655360 | tf_op jit(solution)/shard_map/all_to_all | solution.py:156
  68.7 19.5 %collective-permute-start.1 = (f32[1280]{0:T(1024)S(1)}, f32[1280]{0:T(1024)S(1)}, u32[]{:S(2)}, u32[]{:S(2)}) collective-permute-start(f32[1280]{0:T(1024)S(1)} %copy-done.5), channel_id=1, source_target_pairs={{0,1},{1,0},{2,3},{3,2},{4,5},{5,4},{6,7},{7,6},{8,9},{9,8},{10,11... | collective-permute-start | bytes 15368 | tf_op jit(solution)/shard_map/ppermute | solution.py:90
  73.5 20.8 %collective-permute-start.4 = (bf16[64,512]{1,0:T(8,128)(2,1)S(1)}, bf16[64,512]{1,0:T(8,128)(2,1)S(1)}, u32[]{:S(2)}, u32[]{:S(2)}) collective-permute-start(bf16[64,512]{1,0:T(8,128)(2,1)S(1)} %bitcast.31), channel_id=1, source_target_pairs={{0,2},{1,3},{2,0},{3,1},{4,6},{5,7},{6,4},{7,5},{8,10},{9,11},{10,... | collective-permute-start | bytes 196616 | tf_op jit(solution)/shard_map/ppermute | solution.py:98
  86.4 10.0 %collective-permute-start.2 = (bf16[1280,128]{1,0:T(8,128)(2,1)S(1)}, bf16[1280,128]{1,0:T(8,128)(2,1)S(1)}, u32[]{:S(2)}, u32[]{:S(2)}) collective-permute-start(bf16[1280,128]{1,0:T(8,128)(2,1)S(1)} %bitcast.27), channel_id=1, source_target_pairs={{0,1},{1,0},{2,3},{3,2},{4,5},{5,4},{6,7},{7,6},{8,9},{9,8},{10,11... | collective-permute-start | bytes 983048 | tf_op jit(solution)/shard_map/ppermute | solution.py:90
  92.9 16.8 %collective-permute-start.9 = (f32[1280]{0:T(1024)S(1)}, f32[1280]{0:T(1024)S(1)}, u32[]{:S(2)}, u32[]{:S(2)}) collective-permute-start(f32[1280]{0:T(1024)S(1)} %add.111), channel_id=1, source_target_pairs={{0,2},{1,3},{2,0},{3,1},{4,6},{5,7},{6,4},{7,5},{8,10},{9,11},{10,... | collective-permute-start | bytes 15368 | tf_op jit(solution)/shard_map/ppermute | solution.py:98
  94.4 3.9 %copy-start.1 = (bf16[1280,1280]{1,0:T(8,128)(2,1)S(1)}, bf16[1280,1280]{1,0:T(8,128)(2,1)}, u32[]{:S(2)}) copy-start(bf16[1280,1280]{1,0:T(8,128)(2,1)} %get-tuple-element.14) | copy-start | bytes 9830404
  98.3 2.3 %copy-start.2 = (bf16[1280,1280]{1,0:T(8,128)(2,1)S(1)}, bf16[1280,1280]{1,0:T(8,128)(2,1)}, u32[]{:S(2)}) copy-start(bf16[1280,1280]{1,0:T(8,128)(2,1)} %get-tuple-element.12) | copy-start | bytes 9830404
  103.7 10.6 %collective-permute-start.5 = (bf16[320,512]{1,0:T(8,128)(2,1)S(1)}, bf16[320,512]{1,0:T(8,128)(2,1)S(1)}, u32[]{:S(2)}, u32[]{:S(2)}) collective-permute-start(bf16[320,512]{1,0:T(8,128)(2,1)S(1)} %fusion.36), channel_id=1, source_target_pairs={{0,2},{1,3},{2,0},{3,1},{4,6},{5,7},{6,4},{7,5},{8,10},{9,11},{10,... | collective-permute-start | bytes 983048 | tf_op jit(solution)/shard_map/ppermute | solution.py:98
  104.3 17.0 %collective-permute-start.6 = (bf16[320,512]{1,0:T(8,128)(2,1)S(1)}, bf16[320,512]{1,0:T(8,128)(2,1)S(1)}, u32[]{:S(2)}, u32[]{:S(2)}) collective-permute-start(bf16[320,512]{1,0:T(8,128)(2,1)S(1)} %fusion.33), channel_id=1, source_target_pairs={{0,2},{1,3},{2,0},{3,1},{4,6},{5,7},{6,4},{7,5},{8,10},{9,11},{10,... | collective-permute-start | bytes 983048 | tf_op jit(solution)/shard_map/ppermute | solution.py:98
  105.7 22.6 %collective-permute-start.7 = (bf16[320,512]{1,0:T(8,128)(2,1)S(1)}, bf16[320,512]{1,0:T(8,128)(2,1)S(1)}, u32[]{:S(2)}, u32[]{:S(2)}) collective-permute-start(bf16[320,512]{1,0:T(8,128)(2,1)S(1)} %fusion.30), channel_id=1, source_target_pairs={{0,2},{1,3},{2,0},{3,1},{4,6},{5,7},{6,4},{7,5},{8,10},{9,11},{10,... | collective-permute-start | bytes 983048 | tf_op jit(solution)/shard_map/ppermute | solution.py:98
  106.3 28.3 %collective-permute-start.8 = (bf16[320,512]{1,0:T(8,128)(2,1)S(1)}, bf16[320,512]{1,0:T(8,128)(2,1)S(1)}, u32[]{:S(2)}, u32[]{:S(2)}) collective-permute-start(bf16[320,512]{1,0:T(8,128)(2,1)S(1)} %fusion.27), channel_id=1, source_target_pairs={{0,2},{1,3},{2,0},{3,1},{4,6},{5,7},{6,4},{7,5},{8,10},{9,11},{10,... | collective-permute-start | bytes 983048 | tf_op jit(solution)/shard_map/ppermute | solution.py:98
Sparse Core Ops, SparseCore 0:
  19.9 68.5 all-gather.1

commit v2 on v1

v2 whole, which is shorter than its diff:
```python
import functools
import math

import jax
import jax.numpy as jnp
from jax import lax
from jax.experimental import pallas as pl
from jax.experimental.pallas import tpu as pltpu
from jax.sharding import PartitionSpec as P

KEY_VALUE_WIDTH = 1024
STEP = 100
CORES = 2
COLUMN_HALVES = 2
TOKEN_HALVES = 2


def adaptive_moment_update(param, first, second, grad_mean):
    first_new = 0.9 * first + 0.1 * grad_mean
    second_new = 0.999 * second + 0.001 * grad_mean * grad_mean
    step_size = first_new / (1.0 - 0.9**STEP) / (jnp.sqrt(second_new / (1.0 - 0.999**STEP)) + 1e-08)
    return (param - 0.1 * step_size, first_new, second_new)


def pack_kernel(down_ref, up_ref, out_ref):
    shares, rows, lanes = out_ref.shape
    down = down_ref[...].T
    up = up_ref[...]
    down_rows = down.shape[0] // shares
    up_rows = up.shape[0] // shares
    for i in range(shares):
        pieces = [down[i * down_rows : (i + 1) * down_rows]]
        for k in range(up.shape[1] // lanes):
            pieces.append(up[i * up_rows : (i + 1) * up_rows, k * lanes : (k + 1) * lanes])
        out_ref[i] = jnp.concatenate(pieces, axis=0).astype(jnp.bfloat16)


def adam_kernel(
    replicas, grad_ref, dp_ref, dm_ref, dv_ref, up_ref, um_ref, uv_ref, a_ref, b_ref, factor_ref
):
    total = jnp.sum(grad_ref[...].astype(jnp.float32), axis=0) / replicas
    down_rows = dp_ref.shape[1]
    up_rows, columns = up_ref.shape
    lanes = total.shape[1]
    strips = columns // lanes
    down = total[:down_rows].T
    up = jnp.concatenate(
        [total[down_rows + k * up_rows : down_rows + (k + 1) * up_rows] for k in range(strips)],
        axis=1,
    )
    p, m, v = adaptive_moment_update(dp_ref[...], dm_ref[...], dv_ref[...], down)
    a_ref[0], a_ref[1], a_ref[2] = p, m, v
    pieces = [p.T]
    p, m, v = adaptive_moment_update(up_ref[...], um_ref[...], uv_ref[...], up)
    b_ref[0], b_ref[1], b_ref[2] = p, m, v
    pieces += [p[:, k * lanes : (k + 1) * lanes] for k in range(strips)]
    rounded = jnp.concatenate(pieces, axis=0).astype(jnp.bfloat16)
    for i in range(replicas):
        factor_ref[i] = rounded


def finish_kernel(*refs):
    own_ref, received_ref, inv_ref, out_ref = refs[0], refs[1], refs[2], refs[-1]
    total = own_ref[...] + received_ref[...].astype(jnp.float32)
    out_ref[...] = (total * inv_ref[:, :1]).astype(out_ref.dtype)


def finish(own, received, inv_rms, at, before):
    rows, columns = received.shape
    block = pl.BlockSpec((rows, columns), lambda i: at)
    in_specs = [
        block,
        pl.BlockSpec((rows, columns), lambda i: (0, 0)),
        pl.BlockSpec((rows, 128), lambda i: (at[0], 0)),
    ]
    operands = [own, received, inv_rms]
    aliases = {}
    if before is not None:
        in_specs.append(pl.BlockSpec(memory_space=pl.ANY))
        operands.append(before)
        aliases = {3: 0}
    return pl.pallas_call(
        finish_kernel,
        grid=(1,),
        out_shape=jax.ShapeDtypeStruct(own.shape, jnp.bfloat16),
        in_specs=in_specs,
        out_specs=block,
        input_output_aliases=aliases,
    )(*operands)


def vmem(count):
    return [pl.BlockSpec(memory_space=pltpu.VMEM)] * count


def body(
    prompt_hidden_input,
    input_norm_gain,
    frozen_key_value,
    down_factor_matrix,
    down_moment_first,
    down_moment_second,
    up_factor_matrix,
    up_moment_first,
    up_moment_second,
    down_gradient,
    up_gradient,
):
    n_dp = lax.axis_size("dp")
    n_tensor = lax.axis_size("tensor")
    chips = n_tensor // CORES
    replica = lax.axis_index("dp")
    place = lax.axis_index("tensor")
    chip, core = place // CORES, place % CORES
    tokens, features = prompt_hidden_input.shape
    width, columns = frozen_key_value.shape
    rank = up_factor_matrix.shape[0]
    factors = down_factor_matrix.shape[1] * rank
    chip_features = CORES * features

    def to_sibling(value):
        return lax.ppermute(value, "tensor", [(t, t ^ 1) for t in range(n_tensor)])

    def to_chip(value, step):
        pairs = [
            (CORES * q + k, CORES * ((q + step) % chips) + k)
            for q in range(chips)
            for k in range(CORES)
        ]
        return lax.ppermute(value, "tensor", pairs)

    halves = min(COLUMN_HALVES, columns // 128)
    wide = columns // halves
    odd = replica % 2

    def swap(value):
        return lax.ppermute(value, "dp", [(k, k ^ 1) for k in range(n_dp)])

    def outside_weights(half, after):
        arrived = []
        for step in range(1, chips):
            row = (chip + step) % chips * chip_features + (core ^ odd) * features
            block = lax.dynamic_slice(
                frozen_key_value, (row, half * wide), (features, wide)
            )
            if after is not None:
                block, _ = lax.optimization_barrier((block, after))
            arrived.append(to_chip(block, step))
        return arrived

    first_half = outside_weights(0, None)

    down_rows = features // n_dp
    up_rows = rank // n_dp
    strips = columns // 128
    packed_rows = down_rows + up_rows * strips

    def by_rank(value):
        return jnp.transpose(value, (1, 2, 0)).reshape(factors, features)

    packed = pl.pallas_call(
        pack_kernel,
        out_shape=jax.ShapeDtypeStruct((n_dp, packed_rows, 128), jnp.bfloat16),
        in_specs=vmem(2),
        out_specs=vmem(1)[0],
    )(by_rank(down_gradient[0]), up_gradient[0])
    exchanged = lax.all_to_all(packed, "dp", 0, 0, tiled=True)

    def own_down(value):
        return lax.dynamic_slice_in_dim(by_rank(value), replica * down_rows, down_rows, 1)

    def own_up(value):
        return lax.dynamic_slice_in_dim(value, replica * up_rows, up_rows, 0)

    a_next, b_next, copies = pl.pallas_call(
        functools.partial(adam_kernel, n_dp),
        out_shape=(
            jax.ShapeDtypeStruct((3, factors, down_rows), jnp.float32),
            jax.ShapeDtypeStruct((3, up_rows, columns), jnp.float32),
            jax.ShapeDtypeStruct((n_dp, packed_rows, 128), jnp.bfloat16),
        ),
        in_specs=vmem(7),
        out_specs=tuple(vmem(3)),
    )(
        exchanged,
        own_down(down_factor_matrix),
        own_down(down_moment_first),
        own_down(down_moment_second),
        own_up(up_factor_matrix),
        own_up(up_moment_first),
        own_up(up_moment_second),
    )
    a_next = jnp.transpose(
        a_next.reshape(3, factors // rank, rank, down_rows), (0, 3, 1, 2)
    )
    own_factors = lax.all_to_all(copies, "dp", 0, 0, tiled=True)

    widened = prompt_hidden_input.astype(jnp.float32)
    squares = jnp.sum(widened * widened, axis=1)
    own_scaled = (widened * input_norm_gain[None, :]).astype(jnp.bfloat16)
    sibling_scaled = to_sibling(own_scaled)
    squares = squares + to_sibling(squares)
    squares = squares + sum(to_chip(squares, step) for step in range(1, chips))
    inv_rms = lax.rsqrt(squares / width + 1e-06)
    inv_rms = jnp.broadcast_to(inv_rms[:, None], (tokens, 128))

    outside = [first_half]
    for half in range(1, halves):
        outside.append(outside_weights(half, (outside[-1], copies)))
    outside = [[(mine, swap(mine)) for mine in arrived] for arrived in outside]

    sibling_factors = to_sibling(own_factors)
    adapter_scale = 0.5 / math.sqrt(width * rank)

    def factor_a(packed):
        return packed[:, :down_rows].reshape(features, factors)

    def factor_b(packed, owner):
        value = packed.reshape(n_dp, strips, up_rows, 128)
        value = jnp.transpose(value, (0, 2, 1, 3)).reshape(rank, columns)
        part = owner * columns // KEY_VALUE_WIDTH
        return jnp.concatenate(
            [jnp.where(part == j, value, jnp.zeros_like(value)) for j in range(factors // rank)],
            axis=0,
        )

    own_a, sibling_a = factor_a(own_factors), factor_a(sibling_factors)
    packed_b = own_factors[:, down_rows:]

    def merged(block, a, b):
        change = jnp.dot(a, b, preferred_element_type=jnp.float32)
        return (block.astype(jnp.float32) + adapter_scale * change).astype(jnp.bfloat16)

    def apply(rows, own_weights, sibling_weights):
        return jnp.dot(
            own_scaled[rows], own_weights, preferred_element_type=jnp.float32
        ) + jnp.dot(sibling_scaled[rows], sibling_weights, preferred_element_type=jnp.float32)

    token_slices = [
        slice(k * tokens // TOKEN_HALVES, (k + 1) * tokens // TOKEN_HALVES)
        for k in range(TOKEN_HALVES)
    ]
    other_b = [
        factor_b(to_chip(packed_b, step), CORES * ((chip - step) % chips) + core)
        for step in range(1, chips)
    ]
    received = {}
    for half in range(halves):
        for step in range(1, chips):
            mine, other = outside[half][step - 1]
            b = other_b[step - 1][:, half * wide : (half + 1) * wide]
            own_weights = merged(jnp.where(odd == 0, mine, other), own_a, b)
            sibling_weights = merged(jnp.where(odd == 0, other, mine), sibling_a, b)
            for k, rows in enumerate(token_slices):
                product = apply(rows, own_weights, sibling_weights).astype(jnp.bfloat16)
                received.setdefault((k, half), []).append(to_chip(product, chips - step))

    own_b = factor_b(packed_b, place)
    row = chip * chip_features
    own_weights = merged(
        lax.dynamic_slice_in_dim(frozen_key_value, row + core * features, features, 0),
        own_a,
        own_b,
    )
    sibling_weights = merged(
        lax.dynamic_slice_in_dim(frozen_key_value, row + (1 - core) * features, features, 0),
        sibling_a,
        own_b,
    )
    totals = apply(slice(None), own_weights, sibling_weights)
    keys_values = None
    for at, arrived in received.items():
        for value in arrived[1:]:
            arrived = [arrived[0].astype(jnp.float32) + value.astype(jnp.float32)]
        keys_values = finish(totals, arrived[0], inv_rms, at, keys_values)
    return (a_next, b_next, keys_values)


def solution(mesh):
    placed = (
        P("dp", "tensor"),
        P("tensor"),
        P(None, "tensor"),
        P("tensor", None, None),
        P("tensor", None, None),
        P("tensor", None, None),
        P(None, "tensor"),
        P(None, "tensor"),
        P(None, "tensor"),
        P("dp", "tensor", None, None),
        P("dp", None, "tensor"),
    )
    return jax.shard_map(
        body,
        mesh=mesh,
        in_specs=placed,
        out_specs=(
            P(None, ("tensor", "dp"), None, None),
            P(None, "dp", "tensor"),
            P("dp", "tensor"),
        ),
        check_vma=False,
    )
```

time: 147 us -> 124 us (0.84)
  waiting for transfers between devices: 59.2 us -> 34.3 us
  matrix products: 17.6 us -> 33.7 us
  between operations: 14.3 us -> 0.78 us
  blocking collectives: 11.6 us -> 0 us
  Pallas kernels: 4.17 us -> 13 us
  other arithmetic: 9.26 us -> 5.31 us
  starting transfers between devices: 19.8 us -> 23.4 us
  local copies, waits for them, and re-layouts: 10.1 us -> 12.6 us
    ppermute x0 -> x2, waiting for transfers between devices: none -> 19 us  [swap(): return lax.ppermute(value, 'dp', [(k, k ^ 1) for k in range(n_dp)])]
    ppermute x7 -> x8, waiting for transfers between devices: 32.7 us -> 14.1 us  [to_chip(): return lax.ppermute(value, 'tensor', pairs)]
    dot_general x9 -> x14, matrix products: 17.6 us -> 33.7 us  [the longest x5 16.3 us: apply(): jnp.dot(own_scaled[rows], own_weights, preferred_element_type=jnp.float32)]
    all_to_all x1, waiting for transfers between devices: 15.2 us -> 0.01 us  [body(): exchanged = lax.all_to_all(packed, 'dp', 0, 0, tiled=True)]
    all_to_all x1 -> x0, blocking collectives: 11.6 us -> none  [over_replicas(): lax.all_to_all(copies, 'dp', 0, 0, tiled=True)]
    all_to_all x1, waiting for transfers between devices: 11.3 us -> 0.01 us  [body(): own_factors = lax.all_to_all(copies, 'dp', 0, 0, tiled=True)]
    pallas_call x0 -> x4, Pallas kernels: none -> 8.58 us  [finish(): pl.pallas_call(finish_kernel, grid=(1,), out_shape=jax.ShapeDtypeStruct(o...]
    reduce_sum x2 -> x1, other arithmetic: 9.25 us -> 4.6 us  [body(): squares = jnp.sum(widened * widened, axis=1)]
  transfers between devices with their start and end apart: 13 -> 15, of which waited for: 7 -> 4; matrix products, arithmetic and copies ran while one was open for 20% -> 32% of each run, Pallas kernels for 3% -> 7%
where the time goes in v2:
time: 124 us; the launch traced here: 123 us
  waiting for transfers between devices  34.3 us (28%)
  matrix products  33.7 us (27%)
  starting transfers between devices  23.4 us (19%)
  Pallas kernels  13 us (10%)
  local copies, waits for them, and re-layouts  12.6 us (10%)
  other arithmetic  5.31 us (4%)
    ppermute x2, waiting for transfers between devices, swap(): return lax.ppermute(value, 'dp', [(k, k ^ 1) for k in range(n_dp)])  19 us
    dot_general x5, matrix products, apply(): jnp.dot(own_scaled[rows], own_weights, preferred_element_type=jnp.float32)  16.3 us
    dot_general x5, matrix products, apply(): jnp.dot(sibling_scaled[rows], sibling_weights, preferred_element_type=jnp...  15 us
    ppermute x8, waiting for transfers between devices, to_chip(): return lax.ppermute(value, 'tensor', pairs)  14.1 us
    pallas_call x4, Pallas kernels, finish(): pl.pallas_call(finish_kernel, grid=(1,), out_shape=jax.ShapeDtypeStruct(o...  8.58 us
    ppermute x8, starting transfers between devices, to_chip(): return lax.ppermute(value, 'tensor', pairs)  8.17 us
    all_to_all x1, starting transfers between devices, body(): exchanged = lax.all_to_all(packed, 'dp', 0, 0, tiled=True)  7.28 us
    all_to_all x1, starting transfers between devices, body(): own_factors = lax.all_to_all(copies, 'dp', 0, 0, tiled=True)  5.94 us
  transfers between devices with their start and end apart: 15, of which 4 were waited for; matrix products, arithmetic and copies ran while one was open for 32% of the time, Pallas kernels for 7%

profile of v2, /device:TPU:0, one launch (start us, length us, event | category | flops | bytes accessed | tf_op | source)
XLA Modules:
  0.0 123.1 jit_solution(5179644564106736721)
XLA Ops:
  0.6 0.0 copy-start
  0.7 2.1 %shard_map.130 = bf16[8,192,128]{2,1,0:T(8,128)(2,1)} custom-call(f32[128,1280]{1,0:T(8,128)} %bitcast.67, f32[64,512]{1,0:T(8,128)} %bitcast.68), custom_call_target="tpu_custom_call" | custom-call | tf_op jit(solution)/shard_map/pallas_call | solution.py:161
  2.7 7.3 %all-to-all-start = ((bf16[8,192,128]{2,1,0:T(8,128)(2,1)}), bf16[8,192,128]{2,1,0:T(8,128)(2,1)S(1)}, u32[]{:S(2)}, u32[]{:S(2)}) async-start(bf16[8,192,128]{2,1,0:T(8,128)(2,1)} %shard_map.130), calls=%async_computation | async-start | bytes 786432 | tf_op jit(solution)/shard_map/all_to_all | solution.py:167
  10.0 2.2 %constant_dynamic-slice_fusion = (bf16[1280,256]{1,0:T(8,128)(2,1)S(1)}, bf16[1280,256]{1,0:T(8,128)(2,1)}) fusion(bf16[5120,512]{1,0:T(8,128)(2,1)} %param.13, s32[]{:T(128)S(6)} %select_n.153), kind=kLoop, calls=%fused_computation.54 | loop fusion | bytes 2621444 | tf_op jit(solution)/shard_map/dynamic_slice | solution.py:143
  12.2 1.5 %collective-permute-start.2 = (bf16[1280,256]{1,0:T(8,128)(2,1)S(1)}, bf16[1280,256]{1,0:T(8,128)(2,1)S(1)}, u32[]{:S(2)}, u32[]{:S(2)}) collective-permute-start(bf16[1280,256]{1,0:T(8,128)(2,1)S(1)} %get-tuple-element.11), channel_id=1, source_target_pairs={{0,2},{1,3},{2,0},{3,1},{4,6},{5,7},{6,4},{7,5},{8,10},{9,11},{10,... | collective-permute-start | bytes 1966088 | tf_op jit(solution)/shard_map/ppermute | solution.py:130
  13.7 4.6 %fusion.1 = (f32[1280]{0:T(1024)S(1)}, bf16[1280,1280]{1,0:T(8,128)(2,1)}) fusion(bf16[1280,1280]{1,0:T(8,128)(2,1)} %param.11, f32[1280]{0:T(1024)S(1)} %copy-done.7), kind=kLoop, calls=%fused_computation.3 | loop fusion | flops 8190720 | bytes 6563840 | tf_op jit(solution)/shard_map/reduce_sum | solution.py:199
  18.3 0.0 collective-permute-start
  18.3 1.3 %constant_dynamic-slice_fusion.3.up_ref = f32[8,512]{1,0:T(8,128)} fusion(f32[64,512]{1,0:T(8,128)} %param.17, s32[]{:T(128)S(6)} %select_n.134), kind=kLoop, calls=%fused_computation.59 | loop fusion | bytes 32772 | tf_op jit(solution)/shard_map/dynamic_slice | solution.py:173
  19.6 1.4 %constant_dynamic-slice_fusion.1 = (f32[8,512]{1,0:T(8,128)}, f32[8,512]{1,0:T(8,128)}) fusion(f32[64,512]{1,0:T(8,128)} %param.19, s32[]{:T(128)S(6)} %select_n.134, f32[64,512]{1,0:T(8,128)} %param.18), kind=kLoop, calls=%fused_computation.57 | loop fusion | bytes 65540 | tf_op jit(solution)/shard_map/dynamic_slice | solution.py:173
  21.0 0.7 constant_dynamic-slice_fusion.6.dp_ref
  21.7 1.9 %constant_dynamic-slice_fusion.4 = (f32[128,160]{1,0:T(8,128)}, f32[128,160]{1,0:T(8,128)}) fusion(f32[128,1280]{1,0:T(8,128)} %bitcast.69, s32[]{:T(128)S(6)} %select_n.133, f32[128,1280]{1,0:T(8,128)} %bitcast.70), kind=kLoop, calls=%fused_computation.60 | loop fusion | bytes 327684 | tf_op jit(solution)/shard_map/dynamic_slice | solution.py:170
  23.6 0.0 all-to-all-done.grad_ref
  23.6 0.7 copy-done.2
  24.4 2.3 %shard_map.131 = (f32[3,128,160]{2,1,0:T(8,128)}, f32[3,8,512]{2,1,0:T(8,128)}, bf16[8,192,128]{2,1,0:T(8,128)(2,1)}) custom-call(bf16[8,192,128]{2,1,0:T(8,128)(2,1)} %copy-done.2, f32[128,160]{1,0:T(8,128)} %constant_dynamic-slice_fusion.6.dp_ref, f32[128,160]{1,0:T(8,128)} %get-tuple-element.21.dm_ref, f32[128,160]{1,0:T(8,128)} %get-tuple-element.20.dv_ref, ...), custom_call_target="tpu_custom_call" | custom-call | tf_op jit(solution)/shard_map/pallas_call | solution.py:175
  26.6 5.9 %all-to-all-start.1 = ((bf16[8,192,128]{2,1,0:T(8,128)(2,1)}), bf16[8,192,128]{2,1,0:T(8,128)(2,1)S(1)}, u32[]{:S(2)}, u32[]{:S(2)}) async-start(bf16[8,192,128]{2,1,0:T(8,128)(2,1)} %get-tuple-element.9), calls=%async_computation.1 | async-start | bytes 786432 | tf_op jit(solution)/shard_map/all_to_all | solution.py:196
  32.6 0.0 collective-permute-done.2
  32.6 0.6 collective-permute-start.3
  33.2 0.0 collective-permute-start.7
  33.2 1.2 collective-permute-done.7
  34.4 1.5 %collective-permute-start.8 = (f32[1280]{0:T(1024)S(1)}, f32[1280]{0:T(1024)S(1)}, u32[]{:S(2)}, u32[]{:S(2)}) collective-permute-start(f32[1280]{0:T(1024)S(1)} %add.120), channel_id=1, source_target_pairs={{0,2},{1,3},{2,0},{3,1},{4,6},{5,7},{6,4},{7,5},{8,10},{9,11},{10,... | collective-permute-start | bytes 15368 | tf_op jit(solution)/shard_map/ppermute | solution.py:130
  35.9 14.0 %collective-permute-done.8 = f32[1280]{0:T(1024)S(1)} collective-permute-done((f32[1280]{0:T(1024)S(1)}, f32[1280]{0:T(1024)S(1)}, u32[]{:S(2)}, u32[]{:S(2)}) %collective-permute-start.8) | collective-permute-done | bytes 5152 | tf_op jit(solution)/shard_map/ppermute | solution.py:130
  49.9 1.7 %collective-permute-start.10 = (bf16[1280,256]{1,0:T(8,128)(2,1)S(1)}, bf16[1280,256]{1,0:T(8,128)(2,1)S(1)}, u32[]{:S(2)}, u32[]{:S(2)}) collective-permute-start(bf16[1280,256]{1,0:T(8,128)(2,1)S(1)} %collective-permute-done.2), channel_id=1, source_target_pairs={{0,4},{4,0},{8,12},{12,8},{16,20},{20,16},{24,28},{28,24},{1,5},{5... | collective-permute-start | bytes 1966088 | tf_op jit(solution)/shard_map/ppermute | solution.py:137
  51.6 0.0 collective-permute-done.3
  51.6 0.4 collective-permute-start.4
  52.0 0.0 all-to-all-done.1
  52.0 0.7 fusion.60
  52.6 0.1 copy-done.1
  52.7 0.5 collective-permute-start.5
  53.3 1.0 slice.40
  54.3 6.1 %fusion.22 = f32[1280,512]{1,0:T(8,128)} fusion(bf16[1280,1280]{1,0:T(8,128)(2,1)} %get-tuple-element.14, bf16[1280,128]{1,0:T(8,128)(2,1)S(1)} %bitcast.64, bf16[5120,512]{1,0:T(8,128)(2,1)} %param.13, s32[]{:T(128)S(6)} %select_n.137, bf16[64,512]{1,0:T(8,128)(2,1)S(1)} %get-tuple-element.17, bf16[64,512]{1,0:T(8,128)(2,1)S(1)} %get-tuple-element.16), kind=kOutput, calls=%fused_computation.35 | convolution fusion | flops 1848377344 | bytes 7667716 | tf_op jit(solution)/shard_map/dot_general | solution.py:235
  60.3 0.0 collective-permute-start.1
  60.3 0.0 collective-permute-done.5
  60.4 7.2 %collective-permute-done.10 = bf16[1280,256]{1,0:T(8,128)(2,1)S(1)} collective-permute-done((bf16[1280,256]{1,0:T(8,128)(2,1)S(1)}, bf16[1280,256]{1,0:T(8,128)(2,1)S(1)}, u32[]{:S(2)}, u32[]{:S(2)}) %collective-permute-start.10) | collective-permute-done | bytes 655392 | tf_op jit(solution)/shard_map/ppermute | solution.py:137
  67.6 0.3 add_convert_fusion.1
  67.9 0.0 collective-permute-done.1
  68.0 0.3 add_convert_fusion
  68.3 11.8 %collective-permute-done.4 = bf16[1280,256]{1,0:T(8,128)(2,1)} collective-permute-done((bf16[1280,256]{1,0:T(8,128)(2,1)S(1)}, bf16[1280,256]{1,0:T(8,128)(2,1)}, u32[]{:S(2)}, u32[]{:S(2)}) %collective-permute-start.4) | collective-permute-done | bytes 655392 | tf_op jit(solution)/shard_map/ppermute | solution.py:137
  80.1 1.4 %add_convert_fusion.2 = bf16[1280,256]{1,0:T(8,128)(2,1)S(1)} fusion(bf16[1280,256]{1,0:T(8,128)(2,1)} %collective-permute-done.4, bf16[1280,256]{1,0:T(8,128)(2,1)S(1)} %collective-permute-done.3, bf16[1280,128]{1,0:T(8,128)(2,1)S(1)} %bitcast.62, pred[]{:T(512)S(6)} %eq.26, bf16[64,512]{1,0:T(8,128)(2,1)S(1)} %get-tuple-element.19, ...), kind=kOutput, calls=%fused_computation.33 | convolution fusion | flops 85655552 | bytes 2424833 | tf_op jit(solution)/shard_map/dot_general | solution.py:231
  81.5 0.3 add_convert_fusion.3
  81.9 0.0 collective-permute-done
  81.9 2.0 %fusion.14 = f32[640,256]{1,0:T(8,128)S(1)} fusion(bf16[1280,256]{1,0:T(8,128)(2,1)S(1)} %add_convert_fusion, bf16[1280,1280]{1,0:T(8,128)(2,1)} %collective-permute-done), kind=kOutput, calls=%fused_computation.23 | convolution fusion | flops 419430400 | bytes 2949120 | tf_op jit(solution)/shard_map/dot_general | solution.py:237
  83.9 2.0 %fusion.41 = bf16[640,256]{1,0:T(8,128)(2,1)S(1)} fusion(f32[640,256]{1,0:T(8,128)S(1)} %fusion.14, bf16[1280,256]{1,0:T(8,128)(2,1)S(1)} %add_convert_fusion.1, bf16[1280,1280]{1,0:T(8,128)(2,1)} %get-tuple-element.14), kind=kOutput, calls=%fused_computation.42 | convolution fusion | flops 419758080 | bytes 3276800 | tf_op jit(solution)/shard_map/dot_general | solution.py:235
  86.0 2.0 %fusion.6 = f32[640,256]{1,0:T(8,128)S(1)} fusion(bf16[1280,256]{1,0:T(8,128)(2,1)S(1)} %add_convert_fusion, bf16[1280,1280]{1,0:T(8,128)(2,1)} %collective-permute-done), kind=kOutput, calls=%fused_computation.15 | convolution fusion | flops 419430400 | bytes 2949120 | tf_op jit(solution)/shard_map/dot_general | solution.py:237
  88.0 2.8 %fusion.35 = bf16[640,256]{1,0:T(8,128)(2,1)} fusion(f32[640,256]{1,0:T(8,128)S(1)} %fusion.6, bf16[1280,256]{1,0:T(8,128)(2,1)S(1)} %add_convert_fusion.1, bf16[1280,1280]{1,0:T(8,128)(2,1)} %get-tuple-element.14), kind=kOutput, calls=%fused_computation.40 | convolution fusion | flops 419758080 | bytes 3276800 | tf_op jit(solution)/shard_map/dot_general | solution.py:235
  90.7 0.5 collective-permute-start.12
  91.3 1.5 %collective-permute-start.11 = (bf16[640,256]{1,0:T(8,128)(2,1)S(1)}, bf16[640,256]{1,0:T(8,128)(2,1)S(1)}, u32[]{:S(2)}, u32[]{:S(2)}) collective-permute-start(bf16[640,256]{1,0:T(8,128)(2,1)S(1)} %fusion.41), channel_id=1, source_target_pairs={{0,2},{1,3},{2,0},{3,1},{4,6},{5,7},{6,4},{7,5},{8,10},{9,11},{10,... | collective-permute-start | bytes 983048 | tf_op jit(solution)/shard_map/ppermute | solution.py:130
  92.8 2.0 %fusion.16 = f32[640,256]{1,0:T(8,128)S(1)} fusion(bf16[1280,256]{1,0:T(8,128)(2,1)S(1)} %add_convert_fusion.2, bf16[1280,1280]{1,0:T(8,128)(2,1)} %collective-permute-done), kind=kOutput, calls=%fused_computation.25 | convolution fusion | flops 419430400 | bytes 2949120 | tf_op jit(solution)/shard_map/dot_general | solution.py:237
  94.8 2.8 %fusion.44 = bf16[640,256]{1,0:T(8,128)(2,1)} fusion(f32[640,256]{1,0:T(8,128)S(1)} %fusion.16, bf16[1280,256]{1,0:T(8,128)(2,1)S(1)} %add_convert_fusion.3, bf16[1280,1280]{1,0:T(8,128)(2,1)} %get-tuple-element.14), kind=kOutput, calls=%fused_computation.43 | convolution fusion | flops 419758080 | bytes 3276800 | tf_op jit(solution)/shard_map/dot_general | solution.py:235
  97.6 2.0 %fusion.8 = f32[640,256]{1,0:T(8,128)S(1)} fusion(bf16[1280,256]{1,0:T(8,128)(2,1)S(1)} %add_convert_fusion.2, bf16[1280,1280]{1,0:T(8,128)(2,1)} %collective-permute-done), kind=kOutput, calls=%fused_computation.17 | convolution fusion | flops 419430400 | bytes 2949120 | tf_op jit(solution)/shard_map/dot_general | solution.py:237
  99.6 2.8 %fusion.38 = bf16[640,256]{1,0:T(8,128)(2,1)} fusion(f32[640,256]{1,0:T(8,128)S(1)} %fusion.8, bf16[1280,256]{1,0:T(8,128)(2,1)S(1)} %add_convert_fusion.3, bf16[1280,1280]{1,0:T(8,128)(2,1)} %get-tuple-element.14), kind=kOutput, calls=%fused_computation.41 | convolution fusion | flops 419758080 | bytes 3276800 | tf_op jit(solution)/shard_map/dot_general | solution.py:235
  102.3 0.5 collective-permute-start.9
  102.9 1.5 %collective-permute-start.6 = (bf16[640,256]{1,0:T(8,128)(2,1)}, bf16[640,256]{1,0:T(8,128)(2,1)S(1)}, u32[]{:S(2)}, u32[]{:S(2)}) collective-permute-start(bf16[640,256]{1,0:T(8,128)(2,1)} %fusion.44), channel_id=1, source_target_pairs={{0,2},{1,3},{2,0},{3,1},{4,6},{5,7},{6,4},{7,5},{8,10},{9,11},{10,... | collective-permute-start | bytes 983048 | tf_op jit(solution)/shard_map/ppermute | solution.py:130
  104.4 6.9 %convolution_add_fusion.refs_0_ = f32[1280,512]{1,0:T(8,128)} fusion(f32[1280,512]{1,0:T(8,128)} %fusion.22, bf16[1280,1280]{1,0:T(8,128)(2,1)} %collective-permute-done, bf16[1280,128]{1,0:T(8,128)(2,1)S(1)} %bitcast.63, bf16[5120,512]{1,0:T(8,128)(2,1)} %param.13, s32[]{:T(128)S(6)} %select_n.149, bf16[64,512]{1,0:T(8,128)(2,1)S(1)} %get-tuple-element.17, ...), kind=kOutput, calls=%fused_computation.8 | convolution fusion | flops 1849032704 | bytes 10289156 | tf_op jit(solution)/shard_map/dot_general | solution.py:237
  111.3 0.0 collective-permute-done.12.refs_1_
  111.3 1.1 broadcast_in_dim.2.refs_2_
  112.3 2.1 %shard_map.132.refs_3_ = bf16[1280,512]{1,0:T(8,128)(2,1)} custom-call(f32[1280,512]{1,0:T(8,128)} %convolution_add_fusion.refs_0_, bf16[640,256]{1,0:T(8,128)(2,1)} %copy-done.4, f32[1280,128]{1,0:T(8,128)} %broadcast_in_dim.2.refs_2_), custom_call_target="tpu_custom_call" | custom-call | tf_op jit(solution)/shard_map/pallas_call | solution.py:82
  114.5 0.0 collective-permute-done.11.refs_1_
  114.5 0.7 copy-done.3
  115.2 2.1 %shard_map.133.refs_3_ = bf16[1280,512]{1,0:T(8,128)(2,1)} custom-call(f32[1280,512]{1,0:T(8,128)} %convolution_add_fusion.refs_0_, bf16[640,256]{1,0:T(8,128)(2,1)} %copy-done.3, f32[1280,128]{1,0:T(8,128)} %broadcast_in_dim.2.refs_2_, bf16[1280,512]{1,0:T(8,128)(2,1)} %shard_map.132.refs_3_), custom_call_target="tpu_custom_call", output_to_operand_aliasing={{}: (3, {})} | custom-call | tf_op jit(solution)/shard_map/pallas_call | solution.py:82
  117.4 0.0 collective-permute-done.9.refs_1_
  117.4 0.7 copy-done.6
  118.1 2.1 %shard_map.134.refs_3_ = bf16[1280,512]{1,0:T(8,128)(2,1)} custom-call(f32[1280,512]{1,0:T(8,128)} %convolution_add_fusion.refs_0_, bf16[640,256]{1,0:T(8,128)(2,1)} %copy-done.6, f32[1280,128]{1,0:T(8,128)} %broadcast_in_dim.2.refs_2_, bf16[1280,512]{1,0:T(8,128)(2,1)} %shard_map.133.refs_3_), custom_call_target="tpu_custom_call", output_to_operand_aliasing={{}: (3, {})} | custom-call | tf_op jit(solution)/shard_map/pallas_call | solution.py:82
  120.2 0.7 copy-done.5
  121.0 2.1 %shard_map.135 = bf16[1280,512]{1,0:T(8,128)(2,1)} custom-call(f32[1280,512]{1,0:T(8,128)} %convolution_add_fusion.refs_0_, bf16[640,256]{1,0:T(8,128)(2,1)} %copy-done.5, f32[1280,128]{1,0:T(8,128)} %broadcast_in_dim.2.refs_2_, bf16[1280,512]{1,0:T(8,128)(2,1)} %shard_map.134.refs_3_), custom_call_target="tpu_custom_call", output_to_operand_aliasing={{}: (3, {})} | custom-call | tf_op jit(solution)/shard_map/pallas_call | solution.py:82
  (15 shorter events, 0.1 us)
Async XLA Ops:
  0.6 20.4 %copy-start = (f32[1280,2,64]{0,2,1:T(8,128)S(1)}, f32[1280,2,64]{0,2,1:T(8,128)}, u32[]{:S(2)}) copy-start(f32[1280,2,64]{0,2,1:T(8,128)} %param.14) | copy-start | bytes 1966084
  0.6 13.1 %copy-start.7 = (f32[1280]{0:T(1024)S(1)}, f32[1280]{0:T(1024)}, u32[]{:S(2)}) copy-start(f32[1280]{0:T(1024)} %param.12) | copy-start | bytes 15364
  2.7 20.9 %all-to-all-start = ((bf16[8,192,128]{2,1,0:T(8,128)(2,1)}), bf16[8,192,128]{2,1,0:T(8,128)(2,1)S(1)}, u32[]{:S(2)}, u32[]{:S(2)}) async-start(bf16[8,192,128]{2,1,0:T(8,128)(2,1)} %shard_map.130), calls=%async_computation | async-start | bytes 786432 | tf_op jit(solution)/shard_map/all_to_all | solution.py:167
  12.2 20.4 %collective-permute-start.2 = (bf16[1280,256]{1,0:T(8,128)(2,1)S(1)}, bf16[1280,256]{1,0:T(8,128)(2,1)S(1)}, u32[]{:S(2)}, u32[]{:S(2)}) collective-permute-start(bf16[1280,256]{1,0:T(8,128)(2,1)S(1)} %get-tuple-element.11), channel_id=1, source_target_pairs={{0,2},{1,3},{2,0},{3,1},{4,6},{5,7},{6,4},{7,5},{8,10},{9,11},{10,... | collective-permute-start | bytes 1966088 | tf_op jit(solution)/shard_map/ppermute | solution.py:130
  18.3 63.6 %collective-permute-start = (bf16[1280,1280]{1,0:T(8,128)(2,1)}, bf16[1280,1280]{1,0:T(8,128)(2,1)}, u32[]{:S(2)}, u32[]{:S(2)}) collective-permute-start(bf16[1280,1280]{1,0:T(8,128)(2,1)} %get-tuple-element.14), channel_id=1, source_target_pairs={{0,1},{1,0},{2,3},{3,2},{4,5},{5,4},{6,7},{7,6},{8,9},{9,8},{10,11... | collective-permute-start | bytes 9830408 | tf_op jit(solution)/shard_map/ppermute | solution.py:122
  23.6 0.7 copy-start.2
  26.6 25.3 %all-to-all-start.1 = ((bf16[8,192,128]{2,1,0:T(8,128)(2,1)}), bf16[8,192,128]{2,1,0:T(8,128)(2,1)S(1)}, u32[]{:S(2)}, u32[]{:S(2)}) async-start(bf16[8,192,128]{2,1,0:T(8,128)(2,1)} %get-tuple-element.9), calls=%async_computation.1 | async-start | bytes 786432 | tf_op jit(solution)/shard_map/all_to_all | solution.py:196
  32.6 19.0 %collective-permute-start.3 = (bf16[1280,256]{1,0:T(8,128)(2,1)}, bf16[1280,256]{1,0:T(8,128)(2,1)S(1)}, u32[]{:S(2)}, u32[]{:S(2)}) collective-permute-start(bf16[1280,256]{1,0:T(8,128)(2,1)} %get-tuple-element.10), channel_id=1, source_target_pairs={{0,2},{1,3},{2,0},{3,1},{4,6},{5,7},{6,4},{7,5},{8,10},{9,11},{10,... | collective-permute-start | bytes 1966088 | tf_op jit(solution)/shard_map/ppermute | solution.py:130
  33.2 1.2 collective-permute-start.7
  34.4 15.5 %collective-permute-start.8 = (f32[1280]{0:T(1024)S(1)}, f32[1280]{0:T(1024)S(1)}, u32[]{:S(2)}, u32[]{:S(2)}) collective-permute-start(f32[1280]{0:T(1024)S(1)} %add.120), channel_id=1, source_target_pairs={{0,2},{1,3},{2,0},{3,1},{4,6},{5,7},{6,4},{7,5},{8,10},{9,11},{10,... | collective-permute-start | bytes 15368 | tf_op jit(solution)/shard_map/ppermute | solution.py:130
  49.9 17.7 %collective-permute-start.10 = (bf16[1280,256]{1,0:T(8,128)(2,1)S(1)}, bf16[1280,256]{1,0:T(8,128)(2,1)S(1)}, u32[]{:S(2)}, u32[]{:S(2)}) collective-permute-start(bf16[1280,256]{1,0:T(8,128)(2,1)S(1)} %collective-permute-done.2), channel_id=1, source_target_pairs={{0,4},{4,0},{8,12},{12,8},{16,20},{20,16},{24,28},{28,24},{1,5},{5... | collective-permute-start | bytes 1966088 | tf_op jit(solution)/shard_map/ppermute | solution.py:137
  51.6 28.5 %collective-permute-start.4 = (bf16[1280,256]{1,0:T(8,128)(2,1)S(1)}, bf16[1280,256]{1,0:T(8,128)(2,1)}, u32[]{:S(2)}, u32[]{:S(2)}) collective-permute-start(bf16[1280,256]{1,0:T(8,128)(2,1)S(1)} %collective-permute-done.3), channel_id=1, source_target_pairs={{0,4},{4,0},{8,12},{12,8},{16,20},{20,16},{24,28},{28,24},{1,5},{5... | collective-permute-start | bytes 1966088 | tf_op jit(solution)/shard_map/ppermute | solution.py:137
  52.0 0.8 copy-start.1
  52.7 7.6 %collective-permute-start.5 = (bf16[8,32,128]{2,1,0:T(8,128)(2,1)}, bf16[8,32,128]{2,1,0:T(8,128)(2,1)S(1)}, u32[]{:S(2)}, u32[]{:S(2)}) collective-permute-start(bf16[8,32,128]{2,1,0:T(8,128)(2,1)} %get-tuple-element.15), channel_id=1, source_target_pairs={{0,2},{1,3},{2,0},{3,1},{4,6},{5,7},{6,4},{7,5},{8,10},{9,11},{10,... | collective-permute-start | bytes 196616 | tf_op jit(solution)/shard_map/ppermute | solution.py:130
  60.3 7.6 %collective-permute-start.1 = (bf16[8,192,128]{2,1,0:T(8,128)(2,1)}, bf16[8,192,128]{2,1,0:T(8,128)(2,1)S(1)}, u32[]{:S(2)}, u32[]{:S(2)}) collective-permute-start(bf16[8,192,128]{2,1,0:T(8,128)(2,1)} %copy-done.1), channel_id=1, source_target_pairs={{0,1},{1,0},{2,3},{3,2},{4,5},{5,4},{6,7},{7,6},{8,9},{9,8},{10,11... | collective-permute-start | bytes 1179656 | tf_op jit(solution)/shard_map/ppermute | solution.py:122
  90.7 20.5 %collective-permute-start.12 = (bf16[640,256]{1,0:T(8,128)(2,1)}, bf16[640,256]{1,0:T(8,128)(2,1)S(1)}, u32[]{:S(2)}, u32[]{:S(2)}) collective-permute-start(bf16[640,256]{1,0:T(8,128)(2,1)} %fusion.35), channel_id=1, source_target_pairs={{0,2},{1,3},{2,0},{3,1},{4,6},{5,7},{6,4},{7,5},{8,10},{9,11},{10,... | collective-permute-start | bytes 983048 | tf_op jit(solution)/shard_map/ppermute | solution.py:130
  91.3 23.2 %collective-permute-start.11 = (bf16[640,256]{1,0:T(8,128)(2,1)S(1)}, bf16[640,256]{1,0:T(8,128)(2,1)S(1)}, u32[]{:S(2)}, u32[]{:S(2)}) collective-permute-start(bf16[640,256]{1,0:T(8,128)(2,1)S(1)} %fusion.41), channel_id=1, source_target_pairs={{0,2},{1,3},{2,0},{3,1},{4,6},{5,7},{6,4},{7,5},{8,10},{9,11},{10,... | collective-permute-start | bytes 983048 | tf_op jit(solution)/shard_map/ppermute | solution.py:130
  102.3 15.0 %collective-permute-start.9 = (bf16[640,256]{1,0:T(8,128)(2,1)}, bf16[640,256]{1,0:T(8,128)(2,1)S(1)}, u32[]{:S(2)}, u32[]{:S(2)}) collective-permute-start(bf16[640,256]{1,0:T(8,128)(2,1)} %fusion.38), channel_id=1, source_target_pairs={{0,2},{1,3},{2,0},{3,1},{4,6},{5,7},{6,4},{7,5},{8,10},{9,11},{10,... | collective-permute-start | bytes 983048 | tf_op jit(solution)/shard_map/ppermute | solution.py:130
  102.9 17.4 %collective-permute-start.6 = (bf16[640,256]{1,0:T(8,128)(2,1)}, bf16[640,256]{1,0:T(8,128)(2,1)S(1)}, u32[]{:S(2)}, u32[]{:S(2)}) collective-permute-start(bf16[640,256]{1,0:T(8,128)(2,1)} %fusion.44), channel_id=1, source_target_pairs={{0,2},{1,3},{2,0},{3,1},{4,6},{5,7},{6,4},{7,5},{8,10},{9,11},{10,... | collective-permute-start | bytes 983048 | tf_op jit(solution)/shard_map/ppermute | solution.py:130
  111.3 1.1 copy-start.4
  114.5 0.7 copy-start.3
  117.4 0.7 copy-start.6
  120.2 0.7 copy-start.5

commit v3 on v0

v3 whole, which is shorter than its diff:
```python
import functools
import math

import jax
import jax.numpy as jnp
from jax import lax
from jax.experimental import pallas as pl
from jax.experimental.pallas import tpu as pltpu
from jax.sharding import PartitionSpec as P

KEY_VALUE_WIDTH = 1024
STEP = 100
CORES = 2
LANES = 128
VMEM_BYTES = 40 * 2**20


def adaptive_moment_update(param, first, second, grad_mean):
    first_new = 0.9 * first + 0.1 * grad_mean
    second_new = 0.999 * second + 0.001 * grad_mean * grad_mean
    step_size = first_new / (1.0 - 0.9**STEP) / (jnp.sqrt(second_new / (1.0 - 0.999**STEP)) + 1e-08)
    return (param - 0.1 * step_size, first_new, second_new)


def in_vmem(count):
    return [pl.BlockSpec(memory_space=pltpu.VMEM)] * count


def anywhere(count):
    return [pl.BlockSpec(memory_space=pl.ANY)] * count


SCALARS = pl.BlockSpec(memory_space=pltpu.SMEM)


def params(**more):
    return pltpu.CompilerParams(vmem_limit_bytes=VMEM_BYTES, **more)


def pack_kernel(down_ref, up_ref, out_ref):
    shares = out_ref.shape[0]
    down = down_ref[...].T
    up = up_ref[...]
    down_rows = down.shape[0] // shares
    up_rows = up.shape[0] // shares
    for i in range(shares):
        pieces = [down[i * down_rows : (i + 1) * down_rows]]
        for k in range(up.shape[1] // LANES):
            pieces.append(up[i * up_rows : (i + 1) * up_rows, k * LANES : (k + 1) * LANES])
        out_ref[i] = jnp.concatenate(pieces, axis=0).astype(jnp.bfloat16)


def update(grad_ref, down, up, a_ref, b_ref, factor_ref):
    replicas = grad_ref.shape[0]
    total = jnp.sum(grad_ref[...].astype(jnp.float32), axis=0) / replicas
    down_rows = a_ref.shape[2]
    up_rows, columns = b_ref.shape[1:]
    strips = columns // LANES
    down_mean = total[:down_rows].T
    up_mean = jnp.concatenate(
        [total[down_rows + k * up_rows : down_rows + (k + 1) * up_rows] for k in range(strips)],
        axis=1,
    )
    p, m, v = adaptive_moment_update(*down(), down_mean)
    a_ref[0], a_ref[1], a_ref[2] = p, m, v
    pieces = [p.T]
    p, m, v = adaptive_moment_update(*up(), up_mean)
    b_ref[0], b_ref[1], b_ref[2] = p, m, v
    pieces += [p[:, k * LANES : (k + 1) * LANES] for k in range(strips)]
    rounded = jnp.concatenate(pieces, axis=0).astype(jnp.bfloat16)
    for i in range(replicas):
        factor_ref[i] = rounded


def adam_sliced_kernel(grad_ref, dp, dm, dv, up, um, uv, a_ref, b_ref, factor_ref):
    update(
        grad_ref,
        lambda: [ref[...] for ref in (dp, dm, dv)],
        lambda: [ref[...] for ref in (up, um, uv)],
        a_ref,
        b_ref,
        factor_ref,
    )


def adam_kernel(
    replica_ref, grad_ref, dp, dm, dv, up, um, uv, a_ref, b_ref, factor_ref, down_buf, up_buf, sem
):
    down_rows, window = a_ref.shape[2], down_buf.shape[2]
    up_rows = b_ref.shape[1]
    first = replica_ref[0] * down_rows
    lane = jnp.minimum(first // LANES * LANES, dp.shape[1] - window)
    copies = []
    for i, ref in enumerate((dp, dm, dv)):
        source = ref.at[:, pl.ds(pl.multiple_of(lane, LANES), window)]
        copies.append(pltpu.make_async_copy(source, down_buf.at[i], sem.at[i]))
    for i, ref in enumerate((up, um, uv)):
        row = pl.multiple_of(replica_ref[0] * up_rows, up_rows)
        copies.append(
            pltpu.make_async_copy(ref.at[pl.ds(row, up_rows)], up_buf.at[i], sem.at[3 + i])
        )
    for copy in copies:
        copy.start()
    for copy in copies:
        copy.wait()
    shift = window - (first - lane)
    update(
        grad_ref,
        lambda: [pltpu.roll(down_buf[i], shift, 1)[:, :down_rows] for i in range(3)],
        lambda: [up_buf[i] for i in range(3)],
        a_ref,
        b_ref,
        factor_ref,
    )


def factor_a(packed_ref, down_rows):
    pieces = [packed_ref[i].astype(jnp.float32)[:down_rows] for i in range(packed_ref.shape[0])]
    return jnp.concatenate(pieces, axis=0).astype(jnp.bfloat16)


def factor_b(packed, part, parts, strip, up_rows):
    pieces = [
        packed[i].astype(jnp.float32)[strip * up_rows : (strip + 1) * up_rows]
        for i in range(packed.shape[0])
    ]
    value = jnp.concatenate(pieces, axis=0)
    rows = [jnp.where(part == j, value, jnp.zeros_like(value)) for j in range(parts)]
    return jnp.concatenate(rows, axis=0).astype(jnp.bfloat16)


def merge(scale, block, a, b):
    change = jnp.dot(a, b, preferred_element_type=jnp.float32)
    return (block.astype(jnp.float32) + scale * change).astype(jnp.bfloat16)


def tile_of(size):
    return 256 if size % 256 == 0 else size


def apply(own_x, sibling_x, own_w, sibling_w, store):
    tile = tile_of(own_x.shape[0])

    @pl.loop(0, own_x.shape[0] // tile)
    def _(i):
        rows = pl.ds(pl.multiple_of(i * tile, tile), tile)
        store(
            rows,
            jnp.dot(own_x[rows, :], own_w[...], preferred_element_type=jnp.float32)
            + jnp.dot(sibling_x[rows, :], sibling_w[...], preferred_element_type=jnp.float32),
        )


def outside_kernel(
    static, numbers, mine, other, own_f, sibling_f, b_ref, own_x, sibling_x, out, own_w, sibling_w
):
    scale, parts, strip, up_rows = static
    odd, part = numbers[0], numbers[1]
    down_rows = own_f.shape[1] - b_ref.shape[1]
    b = factor_b(b_ref[...], part, parts, strip, up_rows)
    for factors, first, second, target in (
        (own_f, mine, other, own_w),
        (sibling_f, other, mine, sibling_w),
    ):
        block = jnp.where(odd == 0, first[...], second[...])
        target[...] = merge(scale, block, factor_a(factors, down_rows), b)

    def store(rows, value):
        out[rows, :] = value.astype(jnp.bfloat16)

    apply(own_x, sibling_x, own_w, sibling_w, store)


def own_kernel(
    static, numbers, own_block, sibling_block, own_f, sibling_f, own_x, sibling_x, *refs
):
    scale, parts, up_rows = static
    outs, (own_w, sibling_w) = refs[:-2], refs[-2:]
    part = numbers[2]
    strips = len(outs)
    down_rows = own_f.shape[1] - strips * up_rows
    packed = own_f[:, down_rows:]
    b = jnp.concatenate(
        [factor_b(packed, part, parts, strip, up_rows) for strip in range(strips)], axis=1
    )
    for factors, block, target in (
        (own_f, own_block, own_w),
        (sibling_f, sibling_block, sibling_w),
    ):
        target[...] = merge(scale, block[...], factor_a(factors, down_rows), b)

    def store(rows, value):
        for k, out in enumerate(outs):
            out[rows, :] = value[:, k * LANES : (k + 1) * LANES]

    apply(own_x, sibling_x, own_w, sibling_w, store)


def finish_kernel(sources, own, inv, *refs):
    total = own[...]
    for value in refs[:sources]:
        total = total + value[...].astype(jnp.float32)
    refs[-1][...] = (total * inv[...]).astype(refs[-1].dtype)


def finish(own, inv_rms, received, strip, columns, before):
    rows = own.shape[0]
    operands = [own, inv_rms] + received
    in_specs = in_vmem(len(operands))
    aliases = {}
    if before is not None:
        aliases = {len(operands): 0}
        in_specs += anywhere(1)
        operands.append(before)
    return pl.pallas_call(
        functools.partial(finish_kernel, len(received)),
        grid=(1,),
        out_shape=jax.ShapeDtypeStruct((rows, columns), jnp.bfloat16),
        in_specs=in_specs,
        out_specs=pl.BlockSpec((rows, LANES), lambda i: (0, strip)),
        input_output_aliases=aliases,
        compiler_params=params(),
    )(*operands)


def body(
    prompt_hidden_input,
    input_norm_gain,
    frozen_key_value,
    down_factor_matrix,
    down_moment_first,
    down_moment_second,
    up_factor_matrix,
    up_moment_first,
    up_moment_second,
    down_gradient,
    up_gradient,
):
    n_dp = lax.axis_size("dp")
    n_tensor = lax.axis_size("tensor")
    chips = n_tensor // CORES
    replica = lax.axis_index("dp")
    place = lax.axis_index("tensor")
    chip, core = place // CORES, place % CORES
    odd = replica % 2
    tokens, features = prompt_hidden_input.shape
    width, columns = frozen_key_value.shape
    rank = up_factor_matrix.shape[0]
    parts = down_factor_matrix.shape[1]
    factors = parts * rank
    strips = columns // LANES
    down_rows = features // n_dp
    up_rows = rank // n_dp
    packed_rows = down_rows + up_rows * strips
    steps = range(1, chips)
    f32, bf16 = jnp.float32, jnp.bfloat16

    def to_sibling(value):
        return lax.ppermute(value, "tensor", [(t, t ^ 1) for t in range(n_tensor)])

    def to_chip(value, step):
        pairs = [
            (CORES * q + k, CORES * ((q + step) % chips) + k)
            for q in range(chips)
            for k in range(CORES)
        ]
        return lax.ppermute(value, "tensor", pairs)

    def swap(value):
        return lax.ppermute(value, "dp", [(k, k ^ 1) for k in range(n_dp)])

    def owner(step):
        return CORES * ((chip - step) % chips) + core

    def by_rank(value):
        return jnp.transpose(value, (1, 2, 0)).reshape(factors, features)

    packed = pl.pallas_call(
        pack_kernel,
        out_shape=jax.ShapeDtypeStruct((n_dp, packed_rows, LANES), bf16),
        in_specs=in_vmem(2),
        out_specs=in_vmem(1)[0],
        compiler_params=params(),
    )(by_rank(down_gradient[0]), up_gradient[0])
    exchanged = lax.all_to_all(packed, "dp", 0, 0, tiled=True)

    mine = []
    for step in steps:
        row = ((chip + step) % chips * CORES + (core ^ odd)) * features
        mine.append(
            to_chip(lax.dynamic_slice_in_dim(frozen_key_value, row, features, 0), step)
        )

    widened = prompt_hidden_input.astype(f32)
    squares = jnp.sum(widened * widened, axis=1)
    own_x = (widened * input_norm_gain[None, :]).astype(bf16)
    sibling_x = to_sibling(own_x)
    squares = squares + to_sibling(squares)

    down_state = [by_rank(v) for v in (down_factor_matrix, down_moment_first, down_moment_second)]
    up_state = [up_factor_matrix, up_moment_first, up_moment_second]
    out_shape = (
        jax.ShapeDtypeStruct((3, factors, down_rows), f32),
        jax.ShapeDtypeStruct((3, up_rows, columns), f32),
        jax.ShapeDtypeStruct((n_dp, packed_rows, LANES), bf16),
    )
    window = pl.cdiv(down_rows + LANES, LANES) * LANES
    if features % LANES == 0 and window <= features and up_rows % 8 == 0:
        a_next, b_next, copies = pl.pallas_call(
            adam_kernel,
            out_shape=out_shape,
            in_specs=[SCALARS] + in_vmem(1) + anywhere(6),
            out_specs=tuple(in_vmem(3)),
            scratch_shapes=[
                pltpu.VMEM((3, factors, window), f32),
                pltpu.VMEM((3, up_rows, columns), f32),
                pltpu.SemaphoreType.DMA((6,)),
            ],
            compiler_params=params(),
        )(replica[None].astype(jnp.int32), exchanged, *down_state, *up_state)
    else:
        down_state = [
            lax.dynamic_slice_in_dim(v, replica * down_rows, down_rows, 1) for v in down_state
        ]
        up_state = [lax.dynamic_slice_in_dim(v, replica * up_rows, up_rows, 0) for v in up_state]
        a_next, b_next, copies = pl.pallas_call(
            adam_sliced_kernel,
            out_shape=out_shape,
            in_specs=in_vmem(7),
            out_specs=tuple(in_vmem(3)),
            compiler_params=params(),
        )(exchanged, *down_state, *up_state)
    a_next = jnp.transpose(a_next.reshape(3, parts, rank, down_rows), (0, 3, 1, 2))

    own_f = lax.all_to_all(copies, "dp", 0, 0, tiled=True)
    sibling_f = to_sibling(own_f)
    packed_b = own_f[:, down_rows:]
    other_b = [to_chip(packed_b, step) for step in steps]

    held, other = [], []
    for strip in range(strips):
        for value in mine:
            value, _ = lax.optimization_barrier((value, copies))
            held.append(value[:, strip * LANES : (strip + 1) * LANES])
            other.append(swap(held[-1]))

    squares, _ = lax.optimization_barrier((squares, other_b))
    squares = squares + sum(to_chip(squares, step) for step in steps)
    inv_rms = jnp.broadcast_to(lax.rsqrt(squares / width + 1e-06)[:, None], (tokens, LANES))

    scale = 0.5 / math.sqrt(width * rank)
    weight_scratch = lambda n: [pltpu.VMEM((features, n), bf16)] * 2

    def part_of(who):
        return who * columns // KEY_VALUE_WIDTH

    received = [[] for _ in range(strips)]
    product = None
    for strip in range(strips):
        for step in steps:
            at = strip * len(steps) + step - 1
            numbers = jnp.stack([odd, part_of(owner(step))]).astype(jnp.int32)
            if product is not None:
                numbers, _ = lax.optimization_barrier((numbers, product))
            product = pl.pallas_call(
                functools.partial(outside_kernel, (scale, parts, strip, up_rows)),
                out_shape=jax.ShapeDtypeStruct((tokens, LANES), bf16),
                in_specs=[SCALARS] + in_vmem(7),
                out_specs=in_vmem(1)[0],
                scratch_shapes=weight_scratch(LANES),
                compiler_params=params(),
                cost_estimate=pl.CostEstimate(
                    flops=2 * tokens * CORES * features * LANES,
                    bytes_accessed=4 * tokens * features,
                    transcendentals=0,
                ),
            )(numbers, held[at], other[at], own_f, sibling_f, other_b[step - 1], own_x, sibling_x)
            received[strip].append(to_chip(product, chips - step))

    numbers = jnp.stack([place, place ^ 1, part_of(place)]).astype(jnp.int32)
    numbers, _ = lax.optimization_barrier((numbers, product))
    totals = pl.pallas_call(
        functools.partial(own_kernel, (scale, parts, up_rows)),
        out_shape=(jax.ShapeDtypeStruct((tokens, LANES), f32),) * strips,
        grid_spec=pltpu.PrefetchScalarGridSpec(
            num_scalar_prefetch=1,
            grid=(1,),
            in_specs=[
                pl.BlockSpec((features, columns), lambda i, numbers: (numbers[0], 0)),
                pl.BlockSpec((features, columns), lambda i, numbers: (numbers[1], 0)),
            ]
            + in_vmem(4),
            out_specs=tuple(in_vmem(strips)),
            scratch_shapes=weight_scratch(columns),
        ),
        compiler_params=params(),
        cost_estimate=pl.CostEstimate(
            flops=2 * tokens * CORES * features * columns,
            bytes_accessed=4 * tokens * features,
            transcendentals=0,
        ),
    )(numbers, frozen_key_value, frozen_key_value, own_f, sibling_f, own_x, sibling_x)

    keys_values = None
    for strip in range(strips):
        keys_values = finish(
            totals[strip], inv_rms, received[strip], strip, columns, keys_values
        )
    return (a_next, b_next, keys_values)


def solution(mesh):
    placed = (
        P("dp", "tensor"),
        P("tensor"),
        P(None, "tensor"),
        P("tensor", None, None),
        P("tensor", None, None),
        P("tensor", None, None),
        P(None, "tensor"),
        P(None, "tensor"),
        P(None, "tensor"),
        P("dp", "tensor", None, None),
        P("dp", None, "tensor"),
    )
    return jax.shard_map(
        body,
        mesh=mesh,
        in_specs=placed,
        out_specs=(
            P(None, ("tensor", "dp"), None, None),
            P(None, "dp", "tensor"),
            P("dp", "tensor"),
        ),
        check_vma=False,
    )
```

time: 216 us -> 102 us (0.47)
  waiting for transfers between devices: 167 us -> 19.9 us
  Pallas kernels: 0 us -> 33.6 us
  starting transfers between devices: 0.12 us -> 18.7 us
  matrix products: 15.9 us -> 0 us
  between operations: 13.8 us -> 0.82 us
  blocking collectives: 5.77 us -> 18 us
  other arithmetic: 13.4 us -> 3.15 us
  local copies, waits for them, and re-layouts: 0.02 us -> 7.94 us
    all_gather x2 -> x0, waiting for transfers between devices: 91.9 us -> none  [the longest x1 86.8 us: body(): lax.all_gather(scaled, 'tensor', axis=1, tiled=True)]
    psum x1 -> x0, waiting for transfers between devices: 75.3 us -> none  [body(): lax.psum(down_gradient[0].astype(jnp.bfloat16), 'dp').astype(jnp.float32)]
    pallas_call x0 -> x11, Pallas kernels: none -> 33.6 us  [the longest x4 20.2 us: body(): pl.pallas_call(functools.partial(outside_kernel, (scale, parts, strip, up...]
    all_to_all x0 -> x1, blocking collectives: none -> 18 us  [body(): exchanged = lax.all_to_all(packed, 'dp', 0, 0, tiled=True)]
    ppermute x0 -> x14, waiting for transfers between devices: none -> 17.4 us  [the longest x7 15.3 us: to_chip(): return lax.ppermute(value, 'tensor', pairs)]
    dot_general x1 -> x0, matrix products: 15.9 us -> none  [body(): jnp.dot(lax.all_gather(scaled, 'tensor', axis=1, tiled=True), merged_weig...]
    ppermute x0 -> x14, starting transfers between devices: none -> 14.6 us  [the longest x7 7.89 us: to_chip(): return lax.ppermute(value, 'tensor', pairs)]
    convert_element_type x3 -> x0, other arithmetic: 7.01 us -> none  [the longest x1 3.47 us: body(): factor_a = down_parameter.astype(jnp.bfloat16)]
  transfers between devices with their start and end apart: 3 -> 15, of which waited for: 3 -> 7; matrix products, arithmetic and copies ran while one was open for 3% -> 6% of each run, Pallas kernels for 0% -> 32%
where the time goes in v3:
time: 102 us
  Pallas kernels  33.6 us (33%)
  waiting for transfers between devices  19.9 us (20%)
  starting transfers between devices  18.7 us (18%)
  blocking collectives  18 us (18%)
  local copies, waits for them, and re-layouts  7.94 us (8%)
  other arithmetic  3.15 us (3%)
    pallas_call x4, Pallas kernels, body(): pl.pallas_call(functools.partial(outside_kernel, (scale, parts, strip, up...  20.2 us
    all_to_all x1, blocking collectives, body(): exchanged = lax.all_to_all(packed, 'dp', 0, 0, tiled=True)  18 us
    ppermute x7, waiting for transfers between devices, to_chip(): return lax.ppermute(value, 'tensor', pairs)  15.3 us
    pallas_call x1, Pallas kernels, body(): pl.pallas_call(functools.partial(own_kernel, (scale, parts, up_rows)), ou...  8.56 us
    ppermute x7, starting transfers between devices, to_chip(): return lax.ppermute(value, 'tensor', pairs)  7.89 us
    ppermute x4, starting transfers between devices, swap(): return lax.ppermute(value, 'dp', [(k, k ^ 1) for k in range(n_dp)])  5.95 us
    all_to_all x1, starting transfers between devices, body(): own_f = lax.all_to_all(copies, 'dp', 0, 0, tiled=True)  4.09 us
    pallas_call x4, Pallas kernels, finish(): pl.pallas_call(functools.partial(finish_kernel, len(received)), grid=(1,)...  3.31 us
  transfers between devices with their start and end apart: 15, of which 7 were waited for; matrix products, arithmetic and copies ran while one was open for 6% of the time, Pallas kernels for 32%

profile of v3, /device:TPU:0, one launch (start us, length us, event | category | flops | bytes accessed | tf_op | source)
XLA Modules:
  0.0 102.0 jit_solution(11764028532556181413)
XLA Ops:
  0.6 0.0 copy-start.8
  0.6 3.0 %fusion.1 = (f32[1280]{0:T(1024)S(1)}, bf16[1280,1280]{1,0:T(8,128)(2,1)S(1)}) fusion(bf16[1280,1280]{1,0:T(8,128)(2,1)} %param.11, f32[1280]{0:T(1024)} %param.12), kind=kLoop, calls=%fused_computation.3 | loop fusion | flops 8190720 | bytes 6563840 | tf_op jit(solution)/shard_map/reduce_sum | solution.py:295
  3.6 0.0 copy-start.9
  3.6 0.5 collective-permute-start.4
  4.2 0.0 copy-start.11
  4.2 2.6 %constant_dynamic-slice_fusion = bf16[1280,512]{1,0:T(8,128)(2,1)} fusion(bf16[5120,512]{1,0:T(8,128)(2,1)} %sibling_block.1, s32[]{:T(128)S(6)} %select_n.48), kind=kLoop, calls=%fused_computation.7 | loop fusion | bytes 2621444 | tf_op jit(solution)/shard_map/dynamic_slice | solution.py:291
  6.8 2.6 %collective-permute-start = (bf16[1280,512]{1,0:T(8,128)(2,1)}, bf16[1280,512]{1,0:T(8,128)(2,1)}, u32[]{:S(2)}, u32[]{:S(2)}) collective-permute-start(bf16[1280,512]{1,0:T(8,128)(2,1)} %constant_dynamic-slice_fusion), channel_id=1, source_target_pairs={{0,2},{1,3},{2,0},{3,1},{4,6},{5,7},{6,4},{7,5},{8,10},{9,11},{10,... | collective-permute-start | bytes 3932168 | tf_op jit(solution)/shard_map/ppermute | solution.py:267
  9.4 0.0 copy-done.8
  9.4 1.1 %copy-done.3 = f32[1,1280,2,64]{1,3,2,0:T(8,128)S(1)} copy-done((f32[1,1280,2,64]{1,3,2,0:T(8,128)S(1)}, f32[1,1280,2,64]{1,3,2,0:T(8,128)}, u32[]{:S(2)}) %copy-start.3) | copy-done | bytes 655384
  10.5 0.2 shard_map.130
  10.6 18.0 %all_to_all.10.grad_ref = bf16[8,192,128]{2,1,0:T(8,128)(2,1)S(1)} all-to-all(bf16[8,192,128]{2,1,0:T(8,128)(2,1)S(1)} %shard_map.130), channel_id=1, replica_groups=mesh['dp'=8,'tensor'=4] {'dp'}, dimensions={0} | all-to-all | bytes 786432 | tf_op jit(solution)/shard_map/all_to_all | solution.py:285
  28.6 0.0 copy-done.9
  28.6 0.0 copy-done.4
  28.6 0.0 copy-done.5
  28.6 0.0 copy-done.6
  28.7 0.0 copy-done.10
  28.7 0.0 copy-done.11
  28.7 1.3 %shard_map.131 = (f32[3,128,160]{2,1,0:T(8,128)}, f32[3,8,512]{2,1,0:T(8,128)}, bf16[8,192,128]{2,1,0:T(8,128)(2,1)S(1)}) custom-call(s32[1]{0:T(128)} %bitcast.replica_ref, bf16[8,192,128]{2,1,0:T(8,128)(2,1)S(1)} %all_to_all.10.grad_ref, f32[128,1280]{1,0:T(8,128)S(1)} %bitcast.25, f32[128,1280]{1,0:T(8,128)S(1)} %bitcast.26, f32[128,1280]{1,0:T(8,128)S(1)} %bitcast.27, ...), custom_call_target="tpu_custom_call" | custom-call | tf_op jit(solution)/shard_map/pallas_call | solution.py:309
  30.0 0.8 copy-done.7
  30.8 4.1 %all-to-all-start.1 = ((bf16[8,192,128]{2,1,0:T(8,128)(2,1)}), bf16[8,192,128]{2,1,0:T(8,128)(2,1)}, u32[]{:S(2)}, u32[]{:S(2)}) async-start(bf16[8,192,128]{2,1,0:T(8,128)(2,1)} %copy-done.7), calls=%async_computation.1 | async-start | bytes 786432 | tf_op jit(solution)/shard_map/all_to_all | solution.py:335
  34.9 4.2 %collective-permute-done = bf16[1280,512]{1,0:T(8,128)(2,1)} collective-permute-done((bf16[1280,512]{1,0:T(8,128)(2,1)}, bf16[1280,512]{1,0:T(8,128)(2,1)}, u32[]{:S(2)}, u32[]{:S(2)}) %collective-permute-start) | collective-permute-done | bytes 1310752 | tf_op jit(solution)/shard_map/ppermute | solution.py:267
  39.0 2.4 %fusion.2 = (bf16[1280,128]{1,0:T(8,128)(2,1)}, bf16[1280,128]{1,0:T(8,128)(2,1)}, bf16[1280,128]{1,0:T(8,128)(2,1)}, bf16[1280,128]{1,0:T(8,128)(2,1)}) fusion(bf16[1280,512]{1,0:T(8,128)(2,1)} %collective-permute-done), kind=kLoop, calls=%fused_computation.8 | loop fusion | bytes 2621440 | tf_op jit(solution)/shard_map/slice | solution.py:344
  41.4 1.8 %collective-permute-start.1 = (bf16[1280,128]{1,0:T(8,128)(2,1)}, bf16[1280,128]{1,0:T(8,128)(2,1)}, u32[]{:S(2)}, u32[]{:S(2)}) collective-permute-start(bf16[1280,128]{1,0:T(8,128)(2,1)} %get-tuple-element.34.mine), channel_id=1, source_target_pairs={{0,4},{4,0},{8,12},{12,8},{16,20},{20,16},{24,28},{28,24},{1,5},{5... | collective-permute-start | bytes 983048 | tf_op jit(solution)/shard_map/ppermute | solution.py:270
  43.2 2.4 %all-to-all-done.1.own_f = bf16[8,192,128]{2,1,0:T(8,128)(2,1)} async-done(((bf16[8,192,128]{2,1,0:T(8,128)(2,1)}), bf16[8,192,128]{2,1,0:T(8,128)(2,1)}, u32[]{:S(2)}, u32[]{:S(2)}) %all-to-all-start.1) | async-done | bytes 393248 | tf_op jit(solution)/shard_map/all_to_all | solution.py:335
  45.6 0.0 collective-permute-start.2
  45.6 0.8 slice.20
  46.5 0.5 collective-permute-start.3
  47.0 0.2 collective-permute-start.8
  47.2 0.9 collective-permute-done.8
  48.2 1.5 %collective-permute-start.5 = (bf16[1280,128]{1,0:T(8,128)(2,1)}, bf16[1280,128]{1,0:T(8,128)(2,1)}, u32[]{:S(2)}, u32[]{:S(2)}) collective-permute-start(bf16[1280,128]{1,0:T(8,128)(2,1)} %get-tuple-element.33.mine), channel_id=1, source_target_pairs={{0,4},{4,0},{8,12},{12,8},{16,20},{20,16},{24,28},{28,24},{1,5},{5... | collective-permute-start | bytes 983048 | tf_op jit(solution)/shard_map/ppermute | solution.py:270
  49.6 1.3 %collective-permute-done.3.b_ref = bf16[8,32,128]{2,1,0:T(8,128)(2,1)S(1)} collective-permute-done((bf16[8,32,128]{2,1,0:T(8,128)(2,1)S(1)}, bf16[8,32,128]{2,1,0:T(8,128)(2,1)S(1)}, u32[]{:S(2)}, u32[]{:S(2)}) %collective-permute-start.3) | collective-permute-done | bytes 65568 | tf_op jit(solution)/shard_map/ppermute | solution.py:267
  51.0 1.5 %collective-permute-start.6 = (bf16[1280,128]{1,0:T(8,128)(2,1)}, bf16[1280,128]{1,0:T(8,128)(2,1)S(1)}, u32[]{:S(2)}, u32[]{:S(2)}) collective-permute-start(bf16[1280,128]{1,0:T(8,128)(2,1)} %get-tuple-element.32.mine), channel_id=1, source_target_pairs={{0,4},{4,0},{8,12},{12,8},{16,20},{20,16},{24,28},{28,24},{1,5},{5... | collective-permute-start | bytes 983048 | tf_op jit(solution)/shard_map/ppermute | solution.py:270
  52.4 0.1 pad_add_fusion.1.numbers
  52.5 0.0 collective-permute-done.1.other
  52.5 1.2 %collective-permute-start.7 = (bf16[1280,128]{1,0:T(8,128)(2,1)}, bf16[1280,128]{1,0:T(8,128)(2,1)S(1)}, u32[]{:S(2)}, u32[]{:S(2)}) collective-permute-start(bf16[1280,128]{1,0:T(8,128)(2,1)} %get-tuple-element.31.mine), channel_id=1, source_target_pairs={{0,4},{4,0},{8,12},{12,8},{16,20},{20,16},{24,28},{28,24},{1,5},{5... | collective-permute-start | bytes 983048 | tf_op jit(solution)/shard_map/ppermute | solution.py:270
  53.8 0.1 pad_add_fusion.numbers
  53.8 0.0 collective-permute-done.2.sibling_f
  53.8 0.6 collective-permute-start.9
  54.4 0.0 collective-permute-done.4.sibling_x
  54.4 5.2 %shard_map.132 = bf16[1280,128]{1,0:T(8,128)(2,1)S(1)} custom-call(s32[2]{0:T(128)S(1)} %pad_add_fusion.1.numbers, bf16[1280,128]{1,0:T(8,128)(2,1)} %get-tuple-element.34.mine, bf16[1280,128]{1,0:T(8,128)(2,1)} %collective-permute-done.1.other, bf16[8,192,128]{2,1,0:T(8,128)(2,1)} %all-to-all-done.1.own_f, ...), custom_call_target="tpu_custom_call" | custom-call | flops 838860800 | bytes 6553600 | tf_op jit(solution)/shard_map/pallas_call | solution.py:365
  59.6 0.0 copy-start.1
  59.6 0.0 collective-permute-done.5.other
  59.6 5.1 %shard_map.133 = bf16[1280,128]{1,0:T(8,128)(2,1)S(1)} custom-call(s32[2]{0:T(128)S(1)} %pad_add_fusion.1.numbers, bf16[1280,128]{1,0:T(8,128)(2,1)S(1)} %copy-done.2, bf16[1280,128]{1,0:T(8,128)(2,1)} %collective-permute-done.5.other, bf16[8,192,128]{2,1,0:T(8,128)(2,1)} %all-to-all-done.1.own_f, bf16[8,192,128]{2,1,0:T(8,128)(2,1)} %collective-permute-done.2.sibling_f, ...), custom_call_target="tpu_custom_call" | custom-call | flops 838860800 | bytes 6553600 | tf_op jit(solution)/shard_map/pallas_call | solution.py:365
  64.7 0.0 copy-start
  64.7 1.2 %collective-permute-done.6.other = bf16[1280,128]{1,0:T(8,128)(2,1)S(1)} collective-permute-done((bf16[1280,128]{1,0:T(8,128)(2,1)}, bf16[1280,128]{1,0:T(8,128)(2,1)S(1)}, u32[]{:S(2)}, u32[]{:S(2)}) %collective-permute-start.6) | collective-permute-done | bytes 327712 | tf_op jit(solution)/shard_map/ppermute | solution.py:270
  66.0 0.0 copy-done.1
  66.0 5.0 %shard_map.134 = bf16[1280,128]{1,0:T(8,128)(2,1)S(1)} custom-call(s32[2]{0:T(128)S(1)} %pad_add_fusion.1.numbers, bf16[1280,128]{1,0:T(8,128)(2,1)S(1)} %copy-done.1, bf16[1280,128]{1,0:T(8,128)(2,1)S(1)} %collective-permute-done.6.other, bf16[8,192,128]{2,1,0:T(8,128)(2,1)} %all-to-all-done.1.own_f, bf16[8,192,128]{2,1,0:T(8,128)(2,1)} %collective-permute-done.2.sibling_f, ...), custom_call_target="tpu_custom_call" | custom-call | flops 838860800 | bytes 6553600 | tf_op jit(solution)/shard_map/pallas_call | solution.py:365
  71.0 1.5 %collective-permute-start.11 = (bf16[1280,128]{1,0:T(8,128)(2,1)S(1)}, bf16[1280,128]{1,0:T(8,128)(2,1)S(1)}, u32[]{:S(2)}, u32[]{:S(2)}) collective-permute-start(bf16[1280,128]{1,0:T(8,128)(2,1)S(1)} %shard_map.134), channel_id=1, source_target_pairs={{0,2},{1,3},{2,0},{3,1},{4,6},{5,7},{6,4},{7,5},{8,10},{9,11},{10,... | collective-permute-start | bytes 983048 | tf_op jit(solution)/shard_map/ppermute | solution.py:267
  72.5 0.5 collective-permute-start.12
  73.0 1.5 %collective-permute-start.13 = (bf16[1280,128]{1,0:T(8,128)(2,1)S(1)}, bf16[1280,128]{1,0:T(8,128)(2,1)S(1)}, u32[]{:S(2)}, u32[]{:S(2)}) collective-permute-start(bf16[1280,128]{1,0:T(8,128)(2,1)S(1)} %shard_map.132), channel_id=1, source_target_pairs={{0,2},{1,3},{2,0},{3,1},{4,6},{5,7},{6,4},{7,5},{8,10},{9,11},{10,... | collective-permute-start | bytes 983048 | tf_op jit(solution)/shard_map/ppermute | solution.py:267
  74.5 0.0 collective-permute-done.7.other
  74.5 5.0 %shard_map.135 = bf16[1280,128]{1,0:T(8,128)(2,1)S(1)} custom-call(s32[2]{0:T(128)S(1)} %pad_add_fusion.1.numbers, bf16[1280,128]{1,0:T(8,128)(2,1)S(1)} %copy-done, bf16[1280,128]{1,0:T(8,128)(2,1)S(1)} %collective-permute-done.7.other, bf16[8,192,128]{2,1,0:T(8,128)(2,1)} %all-to-all-done.1.own_f, bf16[8,192,128]{2,1,0:T(8,128)(2,1)} %collective-permute-done.2.sibling_f, ...), custom_call_target="tpu_custom_call" | custom-call | flops 838860800 | bytes 6553600 | tf_op jit(solution)/shard_map/pallas_call | solution.py:365
  79.5 0.6 collective-permute-start.10
  80.1 0.0 collective-permute-done.9
  80.2 8.6 %shard_map.136 = (f32[1280,128]{1,0:T(8,128)S(1)}, f32[1280,128]{1,0:T(8,128)S(1)}, f32[1280,128]{1,0:T(8,128)S(1)}, f32[1280,128]{1,0:T(8,128)S(1)}) custom-call(s32[3]{0:T(128)S(1)} %pad_add_fusion.numbers, bf16[5120,512]{1,0:T(8,128)(2,1)} %sibling_block.1, bf16[5120,512]{1,0:T(8,128)(2,1)} %sibling_block.1, bf16[8,192,128]{2,1,0:T(8,128)(2,1)} %all-to-all-done.1.own_f, ...), custom_call_target="tpu_custom_call" | custom-call | flops 3355443200 | bytes 6553600 | tf_op jit(solution)/shard_map/pallas_call | solution.py:382
  88.7 7.0 %collective-permute-done.13.refs_0_ = bf16[1280,128]{1,0:T(8,128)(2,1)S(1)} collective-permute-done((bf16[1280,128]{1,0:T(8,128)(2,1)S(1)}, bf16[1280,128]{1,0:T(8,128)(2,1)S(1)}, u32[]{:S(2)}, u32[]{:S(2)}) %collective-permute-start.13) | collective-permute-done | bytes 327712 | tf_op jit(solution)/shard_map/ppermute | solution.py:267
  95.7 0.2 broadcast_in_dim.5.inv
  95.9 0.8 shard_map.137.refs_1_
  96.8 0.0 collective-permute-done.12.refs_0_
  96.8 0.8 shard_map.138.refs_1_
  97.6 0.0 collective-permute-done.11.refs_0_
  97.6 0.8 shard_map.139.refs_1_
  98.4 2.7 %collective-permute-done.10.refs_0_ = bf16[1280,128]{1,0:T(8,128)(2,1)S(1)} collective-permute-done((bf16[1280,128]{1,0:T(8,128)(2,1)S(1)}, bf16[1280,128]{1,0:T(8,128)(2,1)S(1)}, u32[]{:S(2)}, u32[]{:S(2)}) %collective-permute-start.10) | collective-permute-done | bytes 327712 | tf_op jit(solution)/shard_map/ppermute | solution.py:267
  101.2 0.8 shard_map.140
  (11 shorter events, 0.0 us)
Async XLA Ops:
  0.6 8.8 %copy-start.8 = (f32[1,64,512]{2,1,0:T(8,128)S(1)}, f32[1,64,512]{2,1,0:T(8,128)}, u32[]{:S(2)}) copy-start(f32[1,64,512]{2,1,0:T(8,128)} %param.21) | copy-start | bytes 393220
  3.6 25.0 %copy-start.9 = (f32[64,512]{1,0:T(8,128)S(1)}, f32[64,512]{1,0:T(8,128)}, u32[]{:S(2)}) copy-start(f32[64,512]{1,0:T(8,128)} %up.1) | copy-start | bytes 393220
  3.6 50.8 %collective-permute-start.4 = (bf16[1280,1280]{1,0:T(8,128)(2,1)S(1)}, bf16[1280,1280]{1,0:T(8,128)(2,1)}, u32[]{:S(2)}, u32[]{:S(2)}) collective-permute-start(bf16[1280,1280]{1,0:T(8,128)(2,1)S(1)} %get-tuple-element.30.own_x), channel_id=1, source_target_pairs={{0,1},{1,0},{2,3},{3,2},{4,5},{5,4},{6,7},{7,6},{8,9},{9,8},{10,11... | collective-permute-start | bytes 9830408 | tf_op jit(solution)/shard_map/ppermute | solution.py:259
  4.2 24.5 %copy-start.4 = (f32[1280,2,64]{0,2,1:T(8,128)S(1)}, f32[1280,2,64]{0,2,1:T(8,128)}, u32[]{:S(2)}) copy-start(f32[1280,2,64]{0,2,1:T(8,128)} %param.14) | copy-start | bytes 1966084
  4.2 24.5 %copy-start.5 = (f32[1280,2,64]{0,2,1:T(8,128)S(1)}, f32[1280,2,64]{0,2,1:T(8,128)}, u32[]{:S(2)}) copy-start(f32[1280,2,64]{0,2,1:T(8,128)} %param.15) | copy-start | bytes 1966084
  4.2 24.5 %copy-start.6 = (f32[1280,2,64]{0,2,1:T(8,128)S(1)}, f32[1280,2,64]{0,2,1:T(8,128)}, u32[]{:S(2)}) copy-start(f32[1280,2,64]{0,2,1:T(8,128)} %param.16) | copy-start | bytes 1966084
  4.2 24.5 %copy-start.10 = (f32[64,512]{1,0:T(8,128)S(1)}, f32[64,512]{1,0:T(8,128)}, u32[]{:S(2)}) copy-start(f32[64,512]{1,0:T(8,128)} %um.1) | copy-start | bytes 393220
  4.2 24.5 %copy-start.11 = (f32[64,512]{1,0:T(8,128)S(1)}, f32[64,512]{1,0:T(8,128)}, u32[]{:S(2)}) copy-start(f32[64,512]{1,0:T(8,128)} %uv.1) | copy-start | bytes 393220
  6.8 32.3 %collective-permute-start = (bf16[1280,512]{1,0:T(8,128)(2,1)}, bf16[1280,512]{1,0:T(8,128)(2,1)}, u32[]{:S(2)}, u32[]{:S(2)}) collective-permute-start(bf16[1280,512]{1,0:T(8,128)(2,1)} %constant_dynamic-slice_fusion), channel_id=1, source_target_pairs={{0,2},{1,3},{2,0},{3,1},{4,6},{5,7},{6,4},{7,5},{8,10},{9,11},{10,... | collective-permute-start | bytes 3932168 | tf_op jit(solution)/shard_map/ppermute | solution.py:267
  9.4 1.1 %copy-start.3 = (f32[1,1280,2,64]{1,3,2,0:T(8,128)S(1)}, f32[1,1280,2,64]{1,3,2,0:T(8,128)}, u32[]{:S(2)}) copy-start(f32[1,1280,2,64]{1,3,2,0:T(8,128)} %param.20) | copy-start | bytes 1966084
  30.0 0.8 copy-start.7
  30.8 14.9 %all-to-all-start.1 = ((bf16[8,192,128]{2,1,0:T(8,128)(2,1)}), bf16[8,192,128]{2,1,0:T(8,128)(2,1)}, u32[]{:S(2)}, u32[]{:S(2)}) async-start(bf16[8,192,128]{2,1,0:T(8,128)(2,1)} %copy-done.7), calls=%async_computation.1 | async-start | bytes 786432 | tf_op jit(solution)/shard_map/all_to_all | solution.py:335
  41.4 11.1 %collective-permute-start.1 = (bf16[1280,128]{1,0:T(8,128)(2,1)}, bf16[1280,128]{1,0:T(8,128)(2,1)}, u32[]{:S(2)}, u32[]{:S(2)}) collective-permute-start(bf16[1280,128]{1,0:T(8,128)(2,1)} %get-tuple-element.34.mine), channel_id=1, source_target_pairs={{0,4},{4,0},{8,12},{12,8},{16,20},{20,16},{24,28},{28,24},{1,5},{5... | collective-permute-start | bytes 983048 | tf_op jit(solution)/shard_map/ppermute | solution.py:270
  45.6 8.2 %collective-permute-start.2 = (bf16[8,192,128]{2,1,0:T(8,128)(2,1)}, bf16[8,192,128]{2,1,0:T(8,128)(2,1)}, u32[]{:S(2)}, u32[]{:S(2)}) collective-permute-start(bf16[8,192,128]{2,1,0:T(8,128)(2,1)} %all-to-all-done.1.own_f), channel_id=1, source_target_pairs={{0,1},{1,0},{2,3},{3,2},{4,5},{5,4},{6,7},{7,6},{8,9},{9,8},{10,11... | collective-permute-start | bytes 1179656 | tf_op jit(solution)/shard_map/ppermute | solution.py:259
  46.5 4.5 %collective-permute-start.3 = (bf16[8,32,128]{2,1,0:T(8,128)(2,1)S(1)}, bf16[8,32,128]{2,1,0:T(8,128)(2,1)S(1)}, u32[]{:S(2)}, u32[]{:S(2)}) collective-permute-start(bf16[8,32,128]{2,1,0:T(8,128)(2,1)S(1)} %slice.20), channel_id=1, source_target_pairs={{0,2},{1,3},{2,0},{3,1},{4,6},{5,7},{6,4},{7,5},{8,10},{9,11},{10,... | collective-permute-start | bytes 196616 | tf_op jit(solution)/shard_map/ppermute | solution.py:267
  47.0 1.2 %collective-permute-start.8 = (f32[1280]{0:T(1024)S(1)}, f32[1280]{0:T(1024)S(1)}, u32[]{:S(2)}, u32[]{:S(2)}) collective-permute-start(f32[1280]{0:T(1024)S(1)} %get-tuple-element.29), channel_id=1, source_target_pairs={{0,1},{1,0},{2,3},{3,2},{4,5},{5,4},{6,7},{7,6},{8,9},{9,8},{10,11... | collective-permute-start | bytes 15368 | tf_op jit(solution)/shard_map/ppermute | solution.py:259
  48.2 11.4 %collective-permute-start.5 = (bf16[1280,128]{1,0:T(8,128)(2,1)}, bf16[1280,128]{1,0:T(8,128)(2,1)}, u32[]{:S(2)}, u32[]{:S(2)}) collective-permute-start(bf16[1280,128]{1,0:T(8,128)(2,1)} %get-tuple-element.33.mine), channel_id=1, source_target_pairs={{0,4},{4,0},{8,12},{12,8},{16,20},{20,16},{24,28},{28,24},{1,5},{5... | collective-permute-start | bytes 983048 | tf_op jit(solution)/shard_map/ppermute | solution.py:270
  51.0 15.0 %collective-permute-start.6 = (bf16[1280,128]{1,0:T(8,128)(2,1)}, bf16[1280,128]{1,0:T(8,128)(2,1)S(1)}, u32[]{:S(2)}, u32[]{:S(2)}) collective-permute-start(bf16[1280,128]{1,0:T(8,128)(2,1)} %get-tuple-element.32.mine), channel_id=1, source_target_pairs={{0,4},{4,0},{8,12},{12,8},{16,20},{20,16},{24,28},{28,24},{1,5},{5... | collective-permute-start | bytes 983048 | tf_op jit(solution)/shard_map/ppermute | solution.py:270
  52.5 22.0 %collective-permute-start.7 = (bf16[1280,128]{1,0:T(8,128)(2,1)}, bf16[1280,128]{1,0:T(8,128)(2,1)S(1)}, u32[]{:S(2)}, u32[]{:S(2)}) collective-permute-start(bf16[1280,128]{1,0:T(8,128)(2,1)} %get-tuple-element.31.mine), channel_id=1, source_target_pairs={{0,4},{4,0},{8,12},{12,8},{16,20},{20,16},{24,28},{28,24},{1,5},{5... | collective-permute-start | bytes 983048 | tf_op jit(solution)/shard_map/ppermute | solution.py:270
  53.8 5.8 %copy-start.2 = (bf16[1280,128]{1,0:T(8,128)(2,1)S(1)}, bf16[1280,128]{1,0:T(8,128)(2,1)}, u32[]{:S(2)}) copy-start(bf16[1280,128]{1,0:T(8,128)(2,1)} %get-tuple-element.33.mine) | copy-start | bytes 983044
  53.8 26.3 %collective-permute-start.9 = (f32[1280]{0:T(1024)S(1)}, f32[1280]{0:T(1024)S(1)}, u32[]{:S(2)}, u32[]{:S(2)}) collective-permute-start(f32[1280]{0:T(1024)S(1)} %add.55), channel_id=1, source_target_pairs={{0,2},{1,3},{2,0},{3,1},{4,6},{5,7},{6,4},{7,5},{8,10},{9,11},{10,... | collective-permute-start | bytes 15368 | tf_op jit(solution)/shard_map/ppermute | solution.py:267
  59.6 6.4 %copy-start.1 = (bf16[1280,128]{1,0:T(8,128)(2,1)S(1)}, bf16[1280,128]{1,0:T(8,128)(2,1)}, u32[]{:S(2)}) copy-start(bf16[1280,128]{1,0:T(8,128)(2,1)} %get-tuple-element.32.mine) | copy-start | bytes 983044
  64.7 9.8 %copy-start = (bf16[1280,128]{1,0:T(8,128)(2,1)S(1)}, bf16[1280,128]{1,0:T(8,128)(2,1)}, u32[]{:S(2)}) copy-start(bf16[1280,128]{1,0:T(8,128)(2,1)} %get-tuple-element.31.mine) | copy-start | bytes 983044
  71.0 26.7 %collective-permute-start.11 = (bf16[1280,128]{1,0:T(8,128)(2,1)S(1)}, bf16[1280,128]{1,0:T(8,128)(2,1)S(1)}, u32[]{:S(2)}, u32[]{:S(2)}) collective-permute-start(bf16[1280,128]{1,0:T(8,128)(2,1)S(1)} %shard_map.134), channel_id=1, source_target_pairs={{0,2},{1,3},{2,0},{3,1},{4,6},{5,7},{6,4},{7,5},{8,10},{9,11},{10,... | collective-permute-start | bytes 983048 | tf_op jit(solution)/shard_map/ppermute | solution.py:267
  72.5 24.3 %collective-permute-start.12 = (bf16[1280,128]{1,0:T(8,128)(2,1)S(1)}, bf16[1280,128]{1,0:T(8,128)(2,1)S(1)}, u32[]{:S(2)}, u32[]{:S(2)}) collective-permute-start(bf16[1280,128]{1,0:T(8,128)(2,1)S(1)} %shard_map.133), channel_id=1, source_target_pairs={{0,2},{1,3},{2,0},{3,1},{4,6},{5,7},{6,4},{7,5},{8,10},{9,11},{10,... | collective-permute-start | bytes 983048 | tf_op jit(solution)/shard_map/ppermute | solution.py:267
  73.0 22.7 %collective-permute-start.13 = (bf16[1280,128]{1,0:T(8,128)(2,1)S(1)}, bf16[1280,128]{1,0:T(8,128)(2,1)S(1)}, u32[]{:S(2)}, u32[]{:S(2)}) collective-permute-start(bf16[1280,128]{1,0:T(8,128)(2,1)S(1)} %shard_map.132), channel_id=1, source_target_pairs={{0,2},{1,3},{2,0},{3,1},{4,6},{5,7},{6,4},{7,5},{8,10},{9,11},{10,... | collective-permute-start | bytes 983048 | tf_op jit(solution)/shard_map/ppermute | solution.py:267
  79.5 21.7 %collective-permute-start.10 = (bf16[1280,128]{1,0:T(8,128)(2,1)S(1)}, bf16[1280,128]{1,0:T(8,128)(2,1)S(1)}, u32[]{:S(2)}, u32[]{:S(2)}) collective-permute-start(bf16[1280,128]{1,0:T(8,128)(2,1)S(1)} %shard_map.135), channel_id=1, source_target_pairs={{0,2},{1,3},{2,0},{3,1},{4,6},{5,7},{6,4},{7,5},{8,10},{9,11},{10,... | collective-permute-start | bytes 983048 | tf_op jit(solution)/shard_map/ppermute | solution.py:267

commit v4 on v3

--- a/solution.py
+++ b/solution.py
@@ -12,6 +12,8 @@
 STEP = 100
 CORES = 2
 LANES = 128
+COLUMN_HALVES = 2
+TOKEN_HALVES = 2
 VMEM_BYTES = 40 * 2**20
 
 
@@ -48,6 +50,21 @@
         for k in range(up.shape[1] // LANES):
             pieces.append(up[i * up_rows : (i + 1) * up_rows, k * LANES : (k + 1) * LANES])
         out_ref[i] = jnp.concatenate(pieces, axis=0).astype(jnp.bfloat16)
+
+
+def take_kernel(rows_ref, weights_ref, *refs):
+    outs, sem = refs[:-1], refs[-1]
+    features, wide = outs[0].shape
+    groups = weights_ref.shape[1] // wide
+    copies = []
+    for i, out in enumerate(outs):
+        row = pl.multiple_of(rows_ref[i // groups] * features, features)
+        source = weights_ref.at[pl.ds(row, features), pl.ds(i % groups * wide, wide)]
+        copies.append(pltpu.make_async_copy(source, out, sem.at[i]))
+    for copy in copies:
+        copy.start()
+    for copy in copies:
+        copy.wait()
 
 
 def update(grad_ref, down, up, a_ref, b_ref, factor_ref):
@@ -138,73 +155,54 @@
     return 256 if size % 256 == 0 else size
 
 
-def apply(own_x, sibling_x, own_w, sibling_w, store):
-    tile = tile_of(own_x.shape[0])
-
-    @pl.loop(0, own_x.shape[0] // tile)
+def up_factor(static, packed, part):
+    _, parts, up_rows, strips = static
+    return jnp.concatenate(
+        [factor_b(packed, part, parts, strip, up_rows) for strip in strips], axis=1
+    )
+
+
+def outside_kernel(static, numbers, mine, other, own_f, sibling_f, b_ref, out):
+    odd, part = numbers[0], numbers[1]
+    features = mine.shape[0]
+    down_rows = own_f.shape[1] - b_ref.shape[1]
+    b = up_factor(static, b_ref[...], part)
+    for at, factors, first, second in (
+        (0, own_f, mine, other),
+        (features, sibling_f, other, mine),
+    ):
+        block = jnp.where(odd == 0, first[...], second[...])
+        out[at : at + features] = merge(static[0], block, factor_a(factors, down_rows), b)
+
+
+def own_kernel(static, numbers, own_block, sibling_block, own_f, sibling_f, x, *refs):
+    outs, weights = refs[:-1], refs[-1]
+    features = own_block.shape[0]
+    wide = outs[0].shape[1]
+    down_rows = own_f.shape[1] - len(static[3]) * static[2]
+    b = up_factor(static, own_f[:, down_rows:], numbers[2])
+    for at, factors, block in ((0, own_f, own_block), (features, sibling_f, sibling_block)):
+        weights[at : at + features] = merge(static[0], block[...], factor_a(factors, down_rows), b)
+    tile = tile_of(x.shape[0])
+
+    @pl.loop(0, x.shape[0] // tile)
     def _(i):
         rows = pl.ds(pl.multiple_of(i * tile, tile), tile)
-        store(
-            rows,
-            jnp.dot(own_x[rows, :], own_w[...], preferred_element_type=jnp.float32)
-            + jnp.dot(sibling_x[rows, :], sibling_w[...], preferred_element_type=jnp.float32),
-        )
-
-
-def outside_kernel(
-    static, numbers, mine, other, own_f, sibling_f, b_ref, own_x, sibling_x, out, own_w, sibling_w
-):
-    scale, parts, strip, up_rows = static
-    odd, part = numbers[0], numbers[1]
-    down_rows = own_f.shape[1] - b_ref.shape[1]
-    b = factor_b(b_ref[...], part, parts, strip, up_rows)
-    for factors, first, second, target in (
-        (own_f, mine, other, own_w),
-        (sibling_f, other, mine, sibling_w),
-    ):
-        block = jnp.where(odd == 0, first[...], second[...])
-        target[...] = merge(scale, block, factor_a(factors, down_rows), b)
-
-    def store(rows, value):
-        out[rows, :] = value.astype(jnp.bfloat16)
-
-    apply(own_x, sibling_x, own_w, sibling_w, store)
-
-
-def own_kernel(
-    static, numbers, own_block, sibling_block, own_f, sibling_f, own_x, sibling_x, *refs
-):
-    scale, parts, up_rows = static
-    outs, (own_w, sibling_w) = refs[:-2], refs[-2:]
-    part = numbers[2]
-    strips = len(outs)
-    down_rows = own_f.shape[1] - strips * up_rows
-    packed = own_f[:, down_rows:]
-    b = jnp.concatenate(
-        [factor_b(packed, part, parts, strip, up_rows) for strip in range(strips)], axis=1
-    )
-    for factors, block, target in (
-        (own_f, own_block, own_w),
-        (sibling_f, sibling_block, sibling_w),
-    ):
-        target[...] = merge(scale, block[...], factor_a(factors, down_rows), b)
-
-    def store(rows, value):
+        value = jnp.dot(x[rows, :], weights[...], preferred_element_type=jnp.float32)
         for k, out in enumerate(outs):
-            out[rows, :] = value[:, k * LANES : (k + 1) * LANES]
-
-    apply(own_x, sibling_x, own_w, sibling_w, store)
-
-
-def finish_kernel(sources, own, inv, *refs):
-    total = own[...]
+            out[rows, :] = value[:, k * wide : (k + 1) * wide]
+
+
+def finish_kernel(sources, first, own, inv, *refs):
+    rows = pl.ds(first, refs[-1].shape[0])
+    total = own[rows, :]
     for value in refs[:sources]:
         total = total + value[...].astype(jnp.float32)
-    refs[-1][...] = (total * inv[...]).astype(refs[-1].dtype)
-
-
-def finish(own, inv_rms, received, strip, columns, before):
-    rows = own.shape[0]
+    refs[-1][...] = (total * inv[rows, :1]).astype(refs[-1].dtype)
+
+
+def finish(own, inv_rms, received, at, shape, before):
+    block = received[0].shape
     operands = [own, inv_rms] + received
     in_specs = in_vmem(len(operands))
     aliases = {}
@@ -213,11 +211,11 @@
         in_specs += anywhere(1)
         operands.append(before)
     return pl.pallas_call(
-        functools.partial(finish_kernel, len(received)),
+        functools.partial(finish_kernel, len(received), at[0] * block[0]),
         grid=(1,),
-        out_shape=jax.ShapeDtypeStruct((rows, columns), jnp.bfloat16),
+        out_shape=jax.ShapeDtypeStruct(shape, jnp.bfloat16),
         in_specs=in_specs,
-        out_specs=pl.BlockSpec((rows, LANES), lambda i: (0, strip)),
+        out_specs=pl.BlockSpec(block, lambda i: at),
         input_output_aliases=aliases,
         compiler_params=params(),
     )(*operands)
@@ -272,29 +270,47 @@
     def owner(step):
         return CORES * ((chip - step) % chips) + core
 
+    halves = min(COLUMN_HALVES, strips)
+    wide = columns // halves
+    blocks = jnp.stack(
+        [(chip + step) % chips * CORES + (core ^ odd) for step in steps]
+    ).astype(jnp.int32)
+    count = len(steps) * halves
+    pieces = pl.pallas_call(
+        take_kernel,
+        out_shape=(jax.ShapeDtypeStruct((features, wide), bf16),) * count,
+        in_specs=[SCALARS] + anywhere(1),
+        out_specs=tuple(anywhere(count)),
+        scratch_shapes=[pltpu.SemaphoreType.DMA((count,))],
+        compiler_params=params(),
+    )(blocks, frozen_key_value)
+
     def by_rank(value):
         return jnp.transpose(value, (1, 2, 0)).reshape(factors, features)
 
+    up_sent, _ = lax.optimization_barrier((up_gradient[0], pieces))
     packed = pl.pallas_call(
         pack_kernel,
         out_shape=jax.ShapeDtypeStruct((n_dp, packed_rows, LANES), bf16),
         in_specs=in_vmem(2),
         out_specs=in_vmem(1)[0],
         compiler_params=params(),
-    )(by_rank(down_gradient[0]), up_gradient[0])
+    )(by_rank(down_gradient[0]), up_sent)
     exchanged = lax.all_to_all(packed, "dp", 0, 0, tiled=True)
 
     mine = []
-    for step in steps:
-        row = ((chip + step) % chips * CORES + (core ^ odd)) * features
-        mine.append(
-            to_chip(lax.dynamic_slice_in_dim(frozen_key_value, row, features, 0), step)
-        )
-
-    widened = prompt_hidden_input.astype(f32)
+    for half in range(halves):
+        for step in steps:
+            piece = pieces[(step - 1) * halves + half]
+            if half > 0:
+                piece, _ = lax.optimization_barrier((piece, packed))
+            mine.append(to_chip(piece, step))
+
+    hidden, _ = lax.optimization_barrier((prompt_hidden_input, packed))
+    widened = hidden.astype(f32)
     squares = jnp.sum(widened * widened, axis=1)
     own_x = (widened * input_norm_gain[None, :]).astype(bf16)
-    sibling_x = to_sibling(own_x)
+    x = lax.optimization_barrier(jnp.concatenate([own_x, to_sibling(own_x)], axis=1))
     squares = squares + to_sibling(squares)
 
     down_state = [by_rank(v) for v in (down_factor_matrix, down_moment_first, down_moment_second)]
@@ -334,54 +350,52 @@
 
     own_f = lax.all_to_all(copies, "dp", 0, 0, tiled=True)
     sibling_f = to_sibling(own_f)
-    packed_b = own_f[:, down_rows:]
+    packed_b, _ = lax.optimization_barrier((own_f[:, down_rows:], x))
     other_b = [to_chip(packed_b, step) for step in steps]
 
-    held, other = [], []
-    for strip in range(strips):
-        for value in mine:
-            value, _ = lax.optimization_barrier((value, copies))
-            held.append(value[:, strip * LANES : (strip + 1) * LANES])
-            other.append(swap(held[-1]))
+    held = [lax.optimization_barrier((value, copies))[0] for value in mine]
+    other = [swap(value) for value in held]
 
     squares, _ = lax.optimization_barrier((squares, other_b))
     squares = squares + sum(to_chip(squares, step) for step in steps)
     inv_rms = jnp.broadcast_to(lax.rsqrt(squares / width + 1e-06)[:, None], (tokens, LANES))
 
     scale = 0.5 / math.sqrt(width * rank)
-    weight_scratch = lambda n: [pltpu.VMEM((features, n), bf16)] * 2
 
     def part_of(who):
         return who * columns // KEY_VALUE_WIDTH
 
-    received = [[] for _ in range(strips)]
+    token_slices = [
+        slice(k * tokens // TOKEN_HALVES, (k + 1) * tokens // TOKEN_HALVES)
+        for k in range(TOKEN_HALVES)
+    ]
+    received = {}
     product = None
-    for strip in range(strips):
+    for half in range(halves):
+        group = range(half * strips // halves, (half + 1) * strips // halves)
         for step in steps:
-            at = strip * len(steps) + step - 1
+            at = half * len(steps) + step - 1
             numbers = jnp.stack([odd, part_of(owner(step))]).astype(jnp.int32)
             if product is not None:
                 numbers, _ = lax.optimization_barrier((numbers, product))
-            product = pl.pallas_call(
-                functools.partial(outside_kernel, (scale, parts, strip, up_rows)),
-                out_shape=jax.ShapeDtypeStruct((tokens, LANES), bf16),
-                in_specs=[SCALARS] + in_vmem(7),
+            weights = pl.pallas_call(
+                functools.partial(outside_kernel, (scale, parts, up_rows, group)),
+                out_shape=jax.ShapeDtypeStruct((CORES * features, wide), bf16),
+                in_specs=[SCALARS] + in_vmem(5),
                 out_specs=in_vmem(1)[0],
-                scratch_shapes=weight_scratch(LANES),
                 compiler_params=params(),
-                cost_estimate=pl.CostEstimate(
-                    flops=2 * tokens * CORES * features * LANES,
-                    bytes_accessed=4 * tokens * features,
-                    transcendentals=0,
-                ),
-            )(numbers, held[at], other[at], own_f, sibling_f, other_b[step - 1], own_x, sibling_x)
-            received[strip].append(to_chip(product, chips - step))
+            )(numbers, held[at], other[at], own_f, sibling_f, other_b[step - 1])
+            for k, rows in enumerate(token_slices):
+                if k > 0:
+                    weights, _ = lax.optimization_barrier((weights, product))
+                product = jnp.dot(x[rows], weights, preferred_element_type=f32).astype(bf16)
+                received.setdefault((k, half), []).append(to_chip(product, chips - step))
 
     numbers = jnp.stack([place, place ^ 1, part_of(place)]).astype(jnp.int32)
-    numbers, _ = lax.optimization_barrier((numbers, product))
+    numbers, _ = lax.optimization_barrier((numbers, (product, received[0, 0])))
     totals = pl.pallas_call(
-        functools.partial(own_kernel, (scale, parts, up_rows)),
-        out_shape=(jax.ShapeDtypeStruct((tokens, LANES), f32),) * strips,
+        functools.partial(own_kernel, (scale, parts, up_rows, range(strips))),
+        out_shape=(jax.ShapeDtypeStruct((tokens, wide), f32),) * halves,
         grid_spec=pltpu.PrefetchScalarGridSpec(
             num_scalar_prefetch=1,
             grid=(1,),
@@ -389,9 +403,9 @@
                 pl.BlockSpec((features, columns), lambda i, numbers: (numbers[0], 0)),
                 pl.BlockSpec((features, columns), lambda i, numbers: (numbers[1], 0)),
             ]
-            + in_vmem(4),
-            out_specs=tuple(in_vmem(strips)),
-            scratch_shapes=weight_scratch(columns),
+            + in_vmem(3),
+            out_specs=tuple(in_vmem(halves)),
+            scratch_shapes=[pltpu.VMEM((CORES * features, columns), bf16)],
         ),
         compiler_params=params(),
         cost_estimate=pl.CostEstimate(
@@ -399,12 +413,12 @@
             bytes_accessed=4 * tokens * features,
             transcendentals=0,
         ),
-    )(numbers, frozen_key_value, frozen_key_value, own_f, sibling_f, own_x, sibling_x)
+    )(numbers, frozen_key_value, frozen_key_value, own_f, sibling_f, x)
 
     keys_values = None
-    for strip in range(strips):
+    for at, pieces in received.items():
         keys_values = finish(
-            totals[strip], inv_rms, received[strip], strip, columns, keys_values
+            totals[at[1]], inv_rms, pieces, at, (tokens, columns), keys_values
         )
     return (a_next, b_next, keys_values)
 

time: 102 us -> 106 us (1.039)
  Pallas kernels: 33.6 us -> 15.8 us
  matrix products: 0 us -> 10.1 us
  waiting for transfers between devices: 19.9 us -> 28.8 us
  other arithmetic: 3.15 us -> 9.01 us
  local copies, waits for them, and re-layouts: 7.94 us -> 4.63 us
  starting transfers between devices: 18.7 us -> 17.1 us
  blocking collectives: 18 us -> 19.3 us
    pallas_call x9 -> x8, Pallas kernels: 32.1 us -> 14.1 us  [the longest x1 8.44 us: body(): pl.pallas_call(functools.partial(own_kernel, (scale, parts, up_rows, rang...]
    dot_general x0 -> x4, matrix products: none -> 10.1 us  [body(): product = jnp.dot(x[rows], weights, preferred_element_type=f32).astype(bf16)]
    ppermute x7 -> x8, waiting for transfers between devices: 15.3 us -> 23.5 us  [to_chip(): return lax.ppermute(value, 'tensor', pairs)]
    concatenate x0 -> x1, other arithmetic: none -> 6.15 us  [body(): jnp.concatenate([own_x, to_sibling(own_x)], axis=1)]
    ppermute x4 -> x2, waiting for transfers between devices: 1.22 us -> 5.29 us  [swap(): return lax.ppermute(value, 'dp', [(k, k ^ 1) for k in range(n_dp)])]
    slice x2 -> x1, local copies, waits for them, and re-layouts: 3.22 us -> 0.01 us  [body(): packed_b, _ = lax.optimization_barrier((own_f[:, down_rows:], x))]
    dynamic_slice x1 -> x0, local copies, waits for them, and re-layouts: 2.61 us -> none  [body(): lax.dynamic_slice_in_dim(frozen_key_value, row, features, 0)]
    unnamed x24 -> x28, local copies, waits for them, and re-layouts: 1.89 us -> 4.4 us
  transfers between devices with their start and end apart: 15 -> 14, of which waited for: 7 -> 4; matrix products, arithmetic and copies ran while one was open for 6% -> 16% of each run, Pallas kernels for 32% -> 14%
where the time goes in v4:
time: 106 us
  waiting for transfers between devices  28.8 us (27%)
  blocking collectives  19.3 us (18%)
  starting transfers between devices  17.1 us (16%)
  Pallas kernels  15.8 us (15%)
  matrix products  10.1 us (10%)
  other arithmetic  9.01 us (8%)
  local copies, waits for them, and re-layouts  4.63 us (4%)
    ppermute x8, waiting for transfers between devices, to_chip(): return lax.ppermute(value, 'tensor', pairs)  23.5 us
    all_to_all x1, blocking collectives, body(): exchanged = lax.all_to_all(packed, 'dp', 0, 0, tiled=True)  19.3 us
    dot_general x4, matrix products, body(): product = jnp.dot(x[rows], weights, preferred_element_type=f32).astype(bf16)  10.1 us
    ppermute x8, starting transfers between devices, to_chip(): return lax.ppermute(value, 'tensor', pairs)  9.54 us
    pallas_call x1, Pallas kernels, body(): pl.pallas_call(functools.partial(own_kernel, (scale, parts, up_rows, rang...  8.44 us
    concatenate x1, other arithmetic, body(): jnp.concatenate([own_x, to_sibling(own_x)], axis=1)  6.15 us
    ppermute x2, waiting for transfers between devices, swap(): return lax.ppermute(value, 'dp', [(k, k ^ 1) for k in range(n_dp)])  5.29 us
    unnamed x28, local copies, waits for them, and re-layouts  4.4 us
  transfers between devices with their start and end apart: 14, of which 4 were waited for; matrix products, arithmetic and copies ran while one was open for 16% of the time, Pallas kernels for 14%

profile of v4, /device:TPU:0, one launch (start us, length us, event | category | flops | bytes accessed | tf_op | source)
XLA Modules:
  0.0 105.7 jit_solution(4191082764107077365)
XLA Ops:
  0.6 0.0 copy-start.11
  0.7 0.0 copy-start
  0.7 2.5 %copy-done = bf16[5120,512]{1,0:T(8,128)(2,1)S(1)} copy-done((bf16[5120,512]{1,0:T(8,128)(2,1)S(1)}, bf16[5120,512]{1,0:T(8,128)(2,1)}, u32[]{:S(2)}) %copy-start) | copy-done | bytes 5242904
  3.2 0.1 shard_map.130
  3.3 1.0 copy-done.1
  4.3 0.0 copy-done.5
  4.3 0.2 shard_map.131
  4.4 0.0 copy-done.11
  4.5 0.9 copy-done.10
  5.4 0.0 copy-start.7
  5.4 0.0 copy-start.8
  5.4 2.7 %fusion.1 = (f32[1280]{0:T(1024)S(1)}, bf16[1280,1280]{1,0:T(8,128)(2,1)}) fusion(bf16[1280,1280]{1,0:T(8,128)(2,1)S(1)} %copy-done.10, f32[1280]{0:T(1024)S(1)} %copy-done.11), kind=kLoop, calls=%fused_computation.3 | loop fusion | flops 8190720 | bytes 6563840 | tf_op jit(solution)/shard_map/reduce_sum | solution.py:311
  8.1 0.5 collective-permute-start
  8.5 19.3 %all_to_all.10.grad_ref = bf16[8,192,128]{2,1,0:T(8,128)(2,1)S(1)} all-to-all(bf16[8,192,128]{2,1,0:T(8,128)(2,1)S(1)} %shard_map.131), channel_id=1, replica_groups=mesh['dp'=8,'tensor'=4] {'dp'}, dimensions={0} | all-to-all | bytes 786432 | tf_op jit(solution)/shard_map/all_to_all | solution.py:299
  27.9 0.0 copy-done.2
  27.9 0.0 copy-done.3
  27.9 0.0 copy-done.4
  27.9 0.0 copy-done.6
  27.9 1.4 %shard_map.132 = (f32[3,128,160]{2,1,0:T(8,128)}, f32[3,8,512]{2,1,0:T(8,128)}, bf16[8,192,128]{2,1,0:T(8,128)(2,1)}) custom-call(s32[1]{0:T(128)} %bitcast.replica_ref, bf16[8,192,128]{2,1,0:T(8,128)(2,1)S(1)} %all_to_all.10.grad_ref, f32[128,1280]{1,0:T(8,128)S(1)} %bitcast.32, f32[128,1280]{1,0:T(8,128)S(1)} %bitcast.33, f32[128,1280]{1,0:T(8,128)S(1)} %bitcast.34, ...), custom_call_target="tpu_custom_call" | custom-call | tf_op jit(solution)/shard_map/pallas_call | solution.py:325
  29.4 3.5 %all-to-all-start.1 = ((bf16[8,192,128]{2,1,0:T(8,128)(2,1)}), bf16[8,192,128]{2,1,0:T(8,128)(2,1)S(1)}, u32[]{:S(2)}, u32[]{:S(2)}) async-start(bf16[8,192,128]{2,1,0:T(8,128)(2,1)} %get-tuple-element.27), calls=%async_computation.1 | async-start | bytes 786432 | tf_op jit(solution)/shard_map/all_to_all | solution.py:351
  32.8 1.6 %collective-permute-start.1 = (bf16[1280,256]{1,0:T(8,128)(2,1)S(1)}, bf16[1280,256]{1,0:T(8,128)(2,1)S(1)}, u32[]{:S(2)}, u32[]{:S(2)}) collective-permute-start(bf16[1280,256]{1,0:T(8,128)(2,1)S(1)} %get-tuple-element.21), channel_id=1, source_target_pairs={{0,2},{1,3},{2,0},{3,1},{4,6},{5,7},{6,4},{7,5},{8,10},{9,11},{10,... | collective-permute-start | bytes 1966088 | tf_op jit(solution)/shard_map/ppermute | solution.py:265
  34.4 0.0 collective-permute-start.8
  34.4 0.5 collective-permute-start.5
  34.9 0.1 pad_add_fusion.1.numbers
  35.0 15.6 %collective-permute-done.1.mine = bf16[1280,256]{1,0:T(8,128)(2,1)S(1)} collective-permute-done((bf16[1280,256]{1,0:T(8,128)(2,1)S(1)}, bf16[1280,256]{1,0:T(8,128)(2,1)S(1)}, u32[]{:S(2)}, u32[]{:S(2)}) %collective-permute-start.1) | collective-permute-done | bytes 655392 | tf_op jit(solution)/shard_map/ppermute | solution.py:265
  50.6 1.9 %collective-permute-start.2 = (bf16[1280,256]{1,0:T(8,128)(2,1)S(1)}, bf16[1280,256]{1,0:T(8,128)(2,1)S(1)}, u32[]{:S(2)}, u32[]{:S(2)}) collective-permute-start(bf16[1280,256]{1,0:T(8,128)(2,1)S(1)} %collective-permute-done.1.mine), channel_id=1, source_target_pairs={{0,4},{4,0},{8,12},{12,8},{16,20},{20,16},{24,28},{28,24},{1,5},{5... | collective-permute-start | bytes 1966088 | tf_op jit(solution)/shard_map/ppermute | solution.py:268
  52.4 0.0 all-to-all-done.1.own_f
  52.4 0.1 collective-permute-start.3
  52.5 0.0 collective-permute-done
  52.5 6.1 %pad_maximum_fusion.x = bf16[1280,2560]{1,0:T(8,128)(2,1)} fusion(bf16[1280,1280]{1,0:T(8,128)(2,1)} %collective-permute-done, bf16[1280,1280]{1,0:T(8,128)(2,1)} %get-tuple-element.40), kind=kLoop, calls=%fused_computation.4 | loop fusion | flops 13107200 | bytes 13107200 | tf_op jit(solution)/shard_map/concatenate | solution.py:313
  58.7 1.5 %collective-permute-start.4 = (bf16[8,32,128]{2,1,0:T(8,128)(2,1)S(1)}, bf16[8,32,128]{2,1,0:T(8,128)(2,1)S(1)}, u32[]{:S(2)}, u32[]{:S(2)}) collective-permute-start(bf16[8,32,128]{2,1,0:T(8,128)(2,1)S(1)} %slice.15), channel_id=1, source_target_pairs={{0,2},{1,3},{2,0},{3,1},{4,6},{5,7},{6,4},{7,5},{8,10},{9,11},{10,... | collective-permute-start | bytes 196616 | tf_op jit(solution)/shard_map/ppermute | solution.py:265
  60.2 0.1 pad_add_fusion.numbers
  60.2 0.0 collective-permute-done.8
  60.3 3.5 %collective-permute-done.5.mine = bf16[1280,256]{1,0:T(8,128)(2,1)S(1)} collective-permute-done((bf16[1280,256]{1,0:T(8,128)(2,1)S(1)}, bf16[1280,256]{1,0:T(8,128)(2,1)S(1)}, u32[]{:S(2)}, u32[]{:S(2)}) %collective-permute-start.5) | collective-permute-done | bytes 655392 | tf_op jit(solution)/shard_map/ppermute | solution.py:265
  63.8 1.7 %collective-permute-start.6 = (bf16[1280,256]{1,0:T(8,128)(2,1)S(1)}, bf16[1280,256]{1,0:T(8,128)(2,1)S(1)}, u32[]{:S(2)}, u32[]{:S(2)}) collective-permute-start(bf16[1280,256]{1,0:T(8,128)(2,1)S(1)} %collective-permute-done.5.mine), channel_id=1, source_target_pairs={{0,4},{4,0},{8,12},{12,8},{16,20},{20,16},{24,28},{28,24},{1,5},{5... | collective-permute-start | bytes 1966088 | tf_op jit(solution)/shard_map/ppermute | solution.py:268
  65.5 0.0 collective-permute-done.2.other
  65.5 0.0 collective-permute-done.3.sibling_f
  65.5 0.0 collective-permute-done.4.b_ref
  65.5 1.0 shard_map.133
  66.6 0.0 copy-start.9
  66.6 3.1 %fusion.16 = bf16[640,256]{1,0:T(8,128)(2,1)S(1)} fusion(bf16[2560,256]{1,0:T(8,128)(2,1)S(1)} %shard_map.133, bf16[1280,2560]{1,0:T(8,128)(2,1)} %pad_maximum_fusion.x), kind=kOutput, calls=%fused_computation.15 | convolution fusion | flops 839024640 | bytes 4915200 | tf_op jit(solution)/shard_map/dot_general | solution.py:391
  69.7 1.6 %collective-permute-start.7 = (bf16[640,256]{1,0:T(8,128)(2,1)S(1)}, bf16[640,256]{1,0:T(8,128)(2,1)S(1)}, u32[]{:S(2)}, u32[]{:S(2)}) collective-permute-start(bf16[640,256]{1,0:T(8,128)(2,1)S(1)} %fusion.16), channel_id=1, source_target_pairs={{0,2},{1,3},{2,0},{3,1},{4,6},{5,7},{6,4},{7,5},{8,10},{9,11},{10,... | collective-permute-start | bytes 983048 | tf_op jit(solution)/shard_map/ppermute | solution.py:265
  71.3 1.0 fusion.10
  72.3 0.7 collective-permute-start.12
  73.0 5.3 %collective-permute-done.6.other = bf16[1280,256]{1,0:T(8,128)(2,1)S(1)} collective-permute-done((bf16[1280,256]{1,0:T(8,128)(2,1)S(1)}, bf16[1280,256]{1,0:T(8,128)(2,1)S(1)}, u32[]{:S(2)}, u32[]{:S(2)}) %collective-permute-start.6) | collective-permute-done | bytes 655392 | tf_op jit(solution)/shard_map/ppermute | solution.py:268
  78.3 1.0 shard_map.134
  79.3 0.0 slice-start
  79.4 3.1 %fusion.19 = bf16[640,256]{1,0:T(8,128)(2,1)S(1)} fusion(bf16[2560,256]{1,0:T(8,128)(2,1)S(1)} %shard_map.134, bf16[1280,2560]{1,0:T(8,128)(2,1)} %pad_maximum_fusion.x), kind=kOutput, calls=%fused_computation.16 | convolution fusion | flops 839024640 | bytes 4915200 | tf_op jit(solution)/shard_map/dot_general | solution.py:391
  82.5 0.0 slice-start.1
  82.5 1.6 %collective-permute-start.11 = (bf16[640,256]{1,0:T(8,128)(2,1)S(1)}, bf16[640,256]{1,0:T(8,128)(2,1)S(1)}, u32[]{:S(2)}, u32[]{:S(2)}) collective-permute-start(bf16[640,256]{1,0:T(8,128)(2,1)S(1)} %fusion.19), channel_id=1, source_target_pairs={{0,2},{1,3},{2,0},{3,1},{4,6},{5,7},{6,4},{7,5},{8,10},{9,11},{10,... | collective-permute-start | bytes 983048 | tf_op jit(solution)/shard_map/ppermute | solution.py:265
  84.0 0.5 collective-permute-start.9
  84.6 2.9 %fusion.13 = bf16[640,256]{1,0:T(8,128)(2,1)S(1)} fusion(bf16[2560,256]{1,0:T(8,128)(2,1)S(1)} %shard_map.134, bf16[1280,2560]{1,0:T(8,128)(2,1)} %pad_maximum_fusion.x), kind=kOutput, calls=%fused_computation.14 | convolution fusion | flops 839024640 | bytes 4915200 | tf_op jit(solution)/shard_map/dot_general | solution.py:391
  87.5 1.6 %collective-permute-start.10 = (bf16[640,256]{1,0:T(8,128)(2,1)S(1)}, bf16[640,256]{1,0:T(8,128)(2,1)S(1)}, u32[]{:S(2)}, u32[]{:S(2)}) collective-permute-start(bf16[640,256]{1,0:T(8,128)(2,1)S(1)} %fusion.13), channel_id=1, source_target_pairs={{0,2},{1,3},{2,0},{3,1},{4,6},{5,7},{6,4},{7,5},{8,10},{9,11},{10,... | collective-permute-start | bytes 983048 | tf_op jit(solution)/shard_map/ppermute | solution.py:265
  89.1 4.4 %collective-permute-done.9 = f32[1280]{0:T(1024)S(1)} collective-permute-done((f32[1280]{0:T(1024)S(1)}, f32[1280]{0:T(1024)S(1)}, u32[]{:S(2)}, u32[]{:S(2)}) %collective-permute-start.9) | collective-permute-done | bytes 5152 | tf_op jit(solution)/shard_map/ppermute | solution.py:265
  93.5 0.0 collective-permute-done.7.refs_0_
  93.5 8.4 %shard_map.135 = (f32[1280,256]{1,0:T(8,128)S(1)}, f32[1280,256]{1,0:T(8,128)S(1)}) custom-call(s32[3]{0:T(128)S(1)} %pad_add_fusion.numbers, bf16[5120,512]{1,0:T(8,128)(2,1)S(1)} %bitcast.30, bf16[5120,512]{1,0:T(8,128)(2,1)S(1)} %bitcast.30, bf16[8,192,128]{2,1,0:T(8,128)(2,1)S(1)} %all-to-all-done.1.own_f, ...), custom_call_target="tpu_custom_call" | custom-call | flops 3355443200 | bytes 6553600 | tf_op jit(solution)/shard_map/pallas_call | solution.py:396
  101.9 0.2 broadcast_in_dim.5.inv
  102.2 0.9 shard_map.136.refs_1_
  103.1 0.0 collective-permute-done.12.refs_0_
  103.1 0.9 shard_map.137.refs_1_
  103.9 0.0 collective-permute-done.11.refs_0_
  103.9 0.9 shard_map.138.refs_1_
  104.8 0.0 collective-permute-done.10.refs_0_
  104.8 0.9 shard_map.139
  (16 shorter events, 0.0 us)
Async XLA Ops:
  0.6 3.8 %copy-start.11 = (f32[1280]{0:T(1024)S(1)}, f32[1280]{0:T(1024)}, u32[]{:S(2)}) copy-start(f32[1280]{0:T(1024)} %param.12) | copy-start | bytes 15364
  0.7 2.5 %copy-start = (bf16[5120,512]{1,0:T(8,128)(2,1)S(1)}, bf16[5120,512]{1,0:T(8,128)(2,1)}, u32[]{:S(2)}) copy-start(bf16[5120,512]{1,0:T(8,128)(2,1)} %sibling_block.1) | copy-start | bytes 15728644
  3.2 1.1 %copy-start.1 = (f32[1,1280,2,64]{1,3,2,0:T(8,128)S(1)}, f32[1,1280,2,64]{1,3,2,0:T(8,128)}, u32[]{:S(2)}) copy-start(f32[1,1280,2,64]{1,3,2,0:T(8,128)} %param.20) | copy-start | bytes 1966084
  3.2 1.1 %copy-start.5 = (f32[1,64,512]{2,1,0:T(8,128)S(1)}, f32[1,64,512]{2,1,0:T(8,128)}, u32[]{:S(2)}) copy-start(f32[1,64,512]{2,1,0:T(8,128)} %param.21) | copy-start | bytes 393220
  3.2 2.2 %copy-start.10 = (bf16[1280,1280]{1,0:T(8,128)(2,1)S(1)}, bf16[1280,1280]{1,0:T(8,128)(2,1)}, u32[]{:S(2)}) copy-start(bf16[1280,1280]{1,0:T(8,128)(2,1)} %param.11) | copy-start | bytes 9830404
  5.3 22.5 %copy-start.2 = (f32[1280,2,64]{0,2,1:T(8,128)S(1)}, f32[1280,2,64]{0,2,1:T(8,128)}, u32[]{:S(2)}) copy-start(f32[1280,2,64]{0,2,1:T(8,128)} %param.14) | copy-start | bytes 1966084
  5.3 22.5 %copy-start.3 = (f32[1280,2,64]{0,2,1:T(8,128)S(1)}, f32[1280,2,64]{0,2,1:T(8,128)}, u32[]{:S(2)}) copy-start(f32[1280,2,64]{0,2,1:T(8,128)} %param.15) | copy-start | bytes 1966084
  5.3 22.5 %copy-start.4 = (f32[1280,2,64]{0,2,1:T(8,128)S(1)}, f32[1280,2,64]{0,2,1:T(8,128)}, u32[]{:S(2)}) copy-start(f32[1280,2,64]{0,2,1:T(8,128)} %param.16) | copy-start | bytes 1966084
  5.3 22.5 %copy-start.6 = (f32[64,512]{1,0:T(8,128)S(1)}, f32[64,512]{1,0:T(8,128)}, u32[]{:S(2)}) copy-start(f32[64,512]{1,0:T(8,128)} %up.1) | copy-start | bytes 393220
  5.4 22.5 %copy-start.7 = (f32[64,512]{1,0:T(8,128)S(1)}, f32[64,512]{1,0:T(8,128)}, u32[]{:S(2)}) copy-start(f32[64,512]{1,0:T(8,128)} %um.1) | copy-start | bytes 393220
  5.4 22.5 %copy-start.8 = (f32[64,512]{1,0:T(8,128)S(1)}, f32[64,512]{1,0:T(8,128)}, u32[]{:S(2)}) copy-start(f32[64,512]{1,0:T(8,128)} %uv.1) | copy-start | bytes 393220
  8.1 44.4 %collective-permute-start = (bf16[1280,1280]{1,0:T(8,128)(2,1)}, bf16[1280,1280]{1,0:T(8,128)(2,1)}, u32[]{:S(2)}, u32[]{:S(2)}) collective-permute-start(bf16[1280,1280]{1,0:T(8,128)(2,1)} %get-tuple-element.40), channel_id=1, source_target_pairs={{0,1},{1,0},{2,3},{3,2},{4,5},{5,4},{6,7},{7,6},{8,9},{9,8},{10,11... | collective-permute-start | bytes 9830408 | tf_op jit(solution)/shard_map/ppermute | solution.py:257
  29.4 23.1 %all-to-all-start.1 = ((bf16[8,192,128]{2,1,0:T(8,128)(2,1)}), bf16[8,192,128]{2,1,0:T(8,128)(2,1)S(1)}, u32[]{:S(2)}, u32[]{:S(2)}) async-start(bf16[8,192,128]{2,1,0:T(8,128)(2,1)} %get-tuple-element.27), calls=%async_computation.1 | async-start | bytes 786432 | tf_op jit(solution)/shard_map/all_to_all | solution.py:351
  32.8 17.7 %collective-permute-start.1 = (bf16[1280,256]{1,0:T(8,128)(2,1)S(1)}, bf16[1280,256]{1,0:T(8,128)(2,1)S(1)}, u32[]{:S(2)}, u32[]{:S(2)}) collective-permute-start(bf16[1280,256]{1,0:T(8,128)(2,1)S(1)} %get-tuple-element.21), channel_id=1, source_target_pairs={{0,2},{1,3},{2,0},{3,1},{4,6},{5,7},{6,4},{7,5},{8,10},{9,11},{10,... | collective-permute-start | bytes 1966088 | tf_op jit(solution)/shard_map/ppermute | solution.py:265
  34.4 25.9 %collective-permute-start.8 = (f32[1280]{0:T(1024)S(1)}, f32[1280]{0:T(1024)S(1)}, u32[]{:S(2)}, u32[]{:S(2)}) collective-permute-start(f32[1280]{0:T(1024)S(1)} %get-tuple-element.39), channel_id=1, source_target_pairs={{0,1},{1,0},{2,3},{3,2},{4,5},{5,4},{6,7},{7,6},{8,9},{9,8},{10,11... | collective-permute-start | bytes 15368 | tf_op jit(solution)/shard_map/ppermute | solution.py:257
  34.4 29.4 %collective-permute-start.5 = (bf16[1280,256]{1,0:T(8,128)(2,1)S(1)}, bf16[1280,256]{1,0:T(8,128)(2,1)S(1)}, u32[]{:S(2)}, u32[]{:S(2)}) collective-permute-start(bf16[1280,256]{1,0:T(8,128)(2,1)S(1)} %get-tuple-element.32), channel_id=1, source_target_pairs={{0,2},{1,3},{2,0},{3,1},{4,6},{5,7},{6,4},{7,5},{8,10},{9,11},{10,... | collective-permute-start | bytes 1966088 | tf_op jit(solution)/shard_map/ppermute | solution.py:265
  50.6 15.0 %collective-permute-start.2 = (bf16[1280,256]{1,0:T(8,128)(2,1)S(1)}, bf16[1280,256]{1,0:T(8,128)(2,1)S(1)}, u32[]{:S(2)}, u32[]{:S(2)}) collective-permute-start(bf16[1280,256]{1,0:T(8,128)(2,1)S(1)} %collective-permute-done.1.mine), channel_id=1, source_target_pairs={{0,4},{4,0},{8,12},{12,8},{16,20},{20,16},{24,28},{28,24},{1,5},{5... | collective-permute-start | bytes 1966088 | tf_op jit(solution)/shard_map/ppermute | solution.py:268
  52.4 13.1 %collective-permute-start.3 = (bf16[8,192,128]{2,1,0:T(8,128)(2,1)S(1)}, bf16[8,192,128]{2,1,0:T(8,128)(2,1)S(1)}, u32[]{:S(2)}, u32[]{:S(2)}) collective-permute-start(bf16[8,192,128]{2,1,0:T(8,128)(2,1)S(1)} %all-to-all-done.1.own_f), channel_id=1, source_target_pairs={{0,1},{1,0},{2,3},{3,2},{4,5},{5,4},{6,7},{7,6},{8,9},{9,8},{10,11... | collective-permute-start | bytes 1179656 | tf_op jit(solution)/shard_map/ppermute | solution.py:257
  58.7 6.9 %collective-permute-start.4 = (bf16[8,32,128]{2,1,0:T(8,128)(2,1)S(1)}, bf16[8,32,128]{2,1,0:T(8,128)(2,1)S(1)}, u32[]{:S(2)}, u32[]{:S(2)}) collective-permute-start(bf16[8,32,128]{2,1,0:T(8,128)(2,1)S(1)} %slice.15), channel_id=1, source_target_pairs={{0,2},{1,3},{2,0},{3,1},{4,6},{5,7},{6,4},{7,5},{8,10},{9,11},{10,... | collective-permute-start | bytes 196616 | tf_op jit(solution)/shard_map/ppermute | solution.py:265
  63.8 14.5 %collective-permute-start.6 = (bf16[1280,256]{1,0:T(8,128)(2,1)S(1)}, bf16[1280,256]{1,0:T(8,128)(2,1)S(1)}, u32[]{:S(2)}, u32[]{:S(2)}) collective-permute-start(bf16[1280,256]{1,0:T(8,128)(2,1)S(1)} %collective-permute-done.5.mine), channel_id=1, source_target_pairs={{0,4},{4,0},{8,12},{12,8},{16,20},{20,16},{24,28},{28,24},{1,5},{5... | collective-permute-start | bytes 1966088 | tf_op jit(solution)/shard_map/ppermute | solution.py:268
  66.6 4.7 %copy-start.9 = (bf16[1280,2560]{1,0:T(8,128)(2,1)S(1)}, bf16[1280,2560]{1,0:T(8,128)(2,1)}, u32[]{:S(2)}) copy-start(bf16[1280,2560]{1,0:T(8,128)(2,1)} %pad_maximum_fusion.x) | copy-start | bytes 19660804
  69.7 23.8 %collective-permute-start.7 = (bf16[640,256]{1,0:T(8,128)(2,1)S(1)}, bf16[640,256]{1,0:T(8,128)(2,1)S(1)}, u32[]{:S(2)}, u32[]{:S(2)}) collective-permute-start(bf16[640,256]{1,0:T(8,128)(2,1)S(1)} %fusion.16), channel_id=1, source_target_pairs={{0,2},{1,3},{2,0},{3,1},{4,6},{5,7},{6,4},{7,5},{8,10},{9,11},{10,... | collective-permute-start | bytes 983048 | tf_op jit(solution)/shard_map/ppermute | solution.py:265
  72.3 30.8 %collective-permute-start.12 = (bf16[640,256]{1,0:T(8,128)(2,1)S(1)}, bf16[640,256]{1,0:T(8,128)(2,1)S(1)}, u32[]{:S(2)}, u32[]{:S(2)}) collective-permute-start(bf16[640,256]{1,0:T(8,128)(2,1)S(1)} %fusion.10), channel_id=1, source_target_pairs={{0,2},{1,3},{2,0},{3,1},{4,6},{5,7},{6,4},{7,5},{8,10},{9,11},{10,... | collective-permute-start | bytes 983048 | tf_op jit(solution)/shard_map/ppermute | solution.py:265
  79.3 14.1 %slice-start = ((s8[5242880]{0:T(1024)(128)(4,1)}), s8[4194304]{0:T(1024)(128)(4,1)S(1)}, s32[]{:S(2)}) async-start(s8[5242880]{0:T(1024)(128)(4,1)} %bitcast.29), calls=%async_computation.2 | async-start | bytes 8388608
  82.5 11.0 %slice-start.1 = ((s8[5242880]{0:T(1024)(128)(4,1)}), s8[1048576]{0:T(1024)(128)(4,1)S(1)}, s32[]{:S(2)}) async-start(s8[5242880]{0:T(1024)(128)(4,1)} %bitcast.29), calls=%async_computation.3 | async-start | bytes 2097152
  82.5 21.5 %collective-permute-start.11 = (bf16[640,256]{1,0:T(8,128)(2,1)S(1)}, bf16[640,256]{1,0:T(8,128)(2,1)S(1)}, u32[]{:S(2)}, u32[]{:S(2)}) collective-permute-start(bf16[640,256]{1,0:T(8,128)(2,1)S(1)} %fusion.19), channel_id=1, source_target_pairs={{0,2},{1,3},{2,0},{3,1},{4,6},{5,7},{6,4},{7,5},{8,10},{9,11},{10,... | collective-permute-start | bytes 983048 | tf_op jit(solution)/shard_map/ppermute | solution.py:265
  84.0 9.4 %collective-permute-start.9 = (f32[1280]{0:T(1024)S(1)}, f32[1280]{0:T(1024)S(1)}, u32[]{:S(2)}, u32[]{:S(2)}) collective-permute-start(f32[1280]{0:T(1024)S(1)} %add.47), channel_id=1, source_target_pairs={{0,2},{1,3},{2,0},{3,1},{4,6},{5,7},{6,4},{7,5},{8,10},{9,11},{10,... | collective-permute-start | bytes 15368 | tf_op jit(solution)/shard_map/ppermute | solution.py:265
  87.5 17.3 %collective-permute-start.10 = (bf16[640,256]{1,0:T(8,128)(2,1)S(1)}, bf16[640,256]{1,0:T(8,128)(2,1)S(1)}, u32[]{:S(2)}, u32[]{:S(2)}) collective-permute-start(bf16[640,256]{1,0:T(8,128)(2,1)S(1)} %fusion.13), channel_id=1, source_target_pairs={{0,2},{1,3},{2,0},{3,1},{4,6},{5,7},{6,4},{7,5},{8,10},{9,11},{10,... | collective-permute-start | bytes 983048 | tf_op jit(solution)/shard_map/ppermute | solution.py:265

commit v5 on v4

--- a/solution.py
+++ b/solution.py
@@ -39,27 +39,43 @@
     return pltpu.CompilerParams(vmem_limit_bytes=VMEM_BYTES, **more)
 
 
+def share_of(down, up, down_at, up_at, down_rows, up_rows):
+    pieces = [down[down_at : down_at + down_rows]] if isinstance(down_at, int) else [
+        down[pl.ds(down_at, down_rows)]
+    ]
+    rows = up[up_at : up_at + up_rows] if isinstance(up_at, int) else up[pl.ds(up_at, up_rows)]
+    for k in range(rows.shape[1] // LANES):
+        pieces.append(rows[:, k * LANES : (k + 1) * LANES])
+    return jnp.concatenate(pieces, axis=0).astype(jnp.bfloat16)
+
+
 def pack_kernel(down_ref, up_ref, out_ref):
     shares = out_ref.shape[0]
-    down = down_ref[...].T
-    up = up_ref[...]
-    down_rows = down.shape[0] // shares
-    up_rows = up.shape[0] // shares
+    down, up = down_ref[...].T, up_ref[...]
+    down_rows, up_rows = down.shape[0] // shares, up.shape[0] // shares
     for i in range(shares):
-        pieces = [down[i * down_rows : (i + 1) * down_rows]]
-        for k in range(up.shape[1] // LANES):
-            pieces.append(up[i * up_rows : (i + 1) * up_rows, k * LANES : (k + 1) * LANES])
-        out_ref[i] = jnp.concatenate(pieces, axis=0).astype(jnp.bfloat16)
+        out_ref[i] = share_of(down, up, i * down_rows, i * up_rows, down_rows, up_rows)
+
+
+def pack_direct_kernel(replica, down_ref, up_ref, *refs):
+    outs, down = refs[:-1], refs[-1]
+    down[...] = down_ref[...].T
+    down_rows, up_rows = down.shape[0] // len(outs), up_ref.shape[0] // len(outs)
+    for k, out in enumerate(outs):
+        i = replica[0] ^ k
+        down_at = pl.multiple_of(i * down_rows, down_rows)
+        up_at = pl.multiple_of(i * up_rows, up_rows)
+        out[...] = share_of(down, up_ref, down_at, up_at, down_rows, up_rows)
 
 
 def take_kernel(rows_ref, weights_ref, *refs):
     outs, sem = refs[:-1], refs[-1]
-    features, wide = outs[0].shape
-    groups = weights_ref.shape[1] // wide
+    features = outs[0].shape[0]
+    strips = weights_ref.shape[1] // LANES
     copies = []
     for i, out in enumerate(outs):
-        row = pl.multiple_of(rows_ref[i // groups] * features, features)
-        source = weights_ref.at[pl.ds(row, features), pl.ds(i % groups * wide, wide)]
+        row = pl.multiple_of(rows_ref[i] * features, features)
+        source = weights_ref.at[pl.ds(row, features), pl.ds(i % strips * LANES, LANES)]
         copies.append(pltpu.make_async_copy(source, out, sem.at[i]))
     for copy in copies:
         copy.start()
@@ -67,9 +83,18 @@
         copy.wait()
 
 
-def update(grad_ref, down, up, a_ref, b_ref, factor_ref):
-    replicas = grad_ref.shape[0]
-    total = jnp.sum(grad_ref[...].astype(jnp.float32), axis=0) / replicas
+def join_kernel(own_ref, sibling_ref, out_ref):
+    rows, features = own_ref.shape
+    tile = tile_of(rows)
+
+    @pl.loop(0, rows // tile)
+    def _(i):
+        at = pl.ds(pl.multiple_of(i * tile, tile), tile)
+        out_ref[at, :features] = own_ref[at, :]
+        out_ref[at, features:] = sibling_ref[at, :]
+
+
+def update(total, down, up, a_ref, b_ref):
     down_rows = a_ref.shape[2]
     up_rows, columns = b_ref.shape[1:]
     strips = columns // LANES
@@ -84,51 +109,62 @@
     p, m, v = adaptive_moment_update(*up(), up_mean)
     b_ref[0], b_ref[1], b_ref[2] = p, m, v
     pieces += [p[:, k * LANES : (k + 1) * LANES] for k in range(strips)]
-    rounded = jnp.concatenate(pieces, axis=0).astype(jnp.bfloat16)
-    for i in range(replicas):
-        factor_ref[i] = rounded
-
-
-def adam_sliced_kernel(grad_ref, dp, dm, dv, up, um, uv, a_ref, b_ref, factor_ref):
-    update(
-        grad_ref,
+    return jnp.concatenate(pieces, axis=0).astype(jnp.bfloat16)
+
+
+def adam_kernel(grad_ref, dp, dm, dv, up, um, uv, a_ref, b_ref, factor_ref):
+    replicas = grad_ref.shape[0]
+    rounded = update(
+        jnp.sum(grad_ref[...].astype(jnp.float32), axis=0) / replicas,
         lambda: [ref[...] for ref in (dp, dm, dv)],
         lambda: [ref[...] for ref in (up, um, uv)],
         a_ref,
         b_ref,
-        factor_ref,
-    )
-
-
-def adam_kernel(
-    replica_ref, grad_ref, dp, dm, dv, up, um, uv, a_ref, b_ref, factor_ref, down_buf, up_buf, sem
-):
+    )
+    for i in range(replicas):
+        factor_ref[i] = rounded
+
+
+def adam_direct_kernel(replicas, replica, *refs):
+    grads, refs = refs[:replicas], refs[replicas:]
+    down_state, up_state, refs = refs[:3], refs[3:6], refs[6:]
+    a_ref, b_ref, factor_ref, down_buf, up_buf, sem = refs
     down_rows, window = a_ref.shape[2], down_buf.shape[2]
     up_rows = b_ref.shape[1]
-    first = replica_ref[0] * down_rows
-    lane = jnp.minimum(first // LANES * LANES, dp.shape[1] - window)
+    first = replica[0] * down_rows
+    lane = jnp.minimum(first // LANES * LANES, down_state[0].shape[1] - window)
+    row = pl.multiple_of(replica[0] * up_rows, up_rows)
     copies = []
-    for i, ref in enumerate((dp, dm, dv)):
+    for i, ref in enumerate(down_state):
         source = ref.at[:, pl.ds(pl.multiple_of(lane, LANES), window)]
         copies.append(pltpu.make_async_copy(source, down_buf.at[i], sem.at[i]))
-    for i, ref in enumerate((up, um, uv)):
-        row = pl.multiple_of(replica_ref[0] * up_rows, up_rows)
-        copies.append(
-            pltpu.make_async_copy(ref.at[pl.ds(row, up_rows)], up_buf.at[i], sem.at[3 + i])
-        )
+    for i, ref in enumerate(up_state):
+        source = ref.at[pl.ds(row, up_rows)]
+        copies.append(pltpu.make_async_copy(source, up_buf.at[i], sem.at[3 + i]))
     for copy in copies:
         copy.start()
+    total = grads[0][...].astype(jnp.float32)
+    for grad in grads[1:]:
+        total = total + grad[...].astype(jnp.float32)
     for copy in copies:
         copy.wait()
     shift = window - (first - lane)
-    update(
-        grad_ref,
+    factor_ref[...] = update(
+        total / replicas,
         lambda: [pltpu.roll(down_buf[i], shift, 1)[:, :down_rows] for i in range(3)],
         lambda: [up_buf[i] for i in range(3)],
         a_ref,
         b_ref,
-        factor_ref,
-    )
+    )
+
+
+def assemble_kernel(replica, *refs):
+    shares, (factor_ref, b_ref) = refs[:-2], refs[-2:]
+    down_rows = factor_ref.shape[1] - b_ref.shape[1]
+    for k, share in enumerate(shares):
+        i = replica[0] ^ k
+        factor_ref[i] = share[...]
+        b_ref[i] = share[down_rows:]
 
 
 def factor_a(packed_ref, down_rows):
@@ -162,17 +198,21 @@
     )
 
 
-def outside_kernel(static, numbers, mine, other, own_f, sibling_f, b_ref, out):
-    odd, part = numbers[0], numbers[1]
-    features = mine.shape[0]
+def outside_kernel(static, numbers, own_f, sibling_f, b_ref, *refs):
+    out = refs[-1]
+    strips = static[3]
+    features = refs[0].shape[0]
     down_rows = own_f.shape[1] - b_ref.shape[1]
-    b = up_factor(static, b_ref[...], part)
-    for at, factors, first, second in (
-        (0, own_f, mine, other),
-        (features, sibling_f, other, mine),
-    ):
-        block = jnp.where(odd == 0, first[...], second[...])
-        out[at : at + features] = merge(static[0], block, factor_a(factors, down_rows), b)
+    b = up_factor(static, b_ref[...], numbers[0])
+    own_a, sibling_a = factor_a(own_f, down_rows), factor_a(sibling_f, down_rows)
+    for k in range(len(strips)):
+        mine, other = refs[2 * k : 2 * k + 2]
+        odd = numbers[1 + k]
+        lanes = slice(k * LANES, (k + 1) * LANES)
+        block = jnp.where(odd == 0, mine[...], other[...])
+        out[:features, lanes] = merge(static[0], block, own_a, b[:, lanes])
+        block = jnp.where(odd == 0, other[...], mine[...])
+        out[features:, lanes] = merge(static[0], block, sibling_a, b[:, lanes])
 
 
 def own_kernel(static, numbers, own_block, sibling_block, own_f, sibling_f, x, *refs):
@@ -240,7 +280,6 @@
     replica = lax.axis_index("dp")
     place = lax.axis_index("tensor")
     chip, core = place // CORES, place % CORES
-    odd = replica % 2
     tokens, features = prompt_hidden_input.shape
     width, columns = frozen_key_value.shape
     rank = up_factor_matrix.shape[0]
@@ -264,68 +303,80 @@
         ]
         return lax.ppermute(value, "tensor", pairs)
 
-    def swap(value):
-        return lax.ppermute(value, "dp", [(k, k ^ 1) for k in range(n_dp)])
-
     def owner(step):
         return CORES * ((chip - step) % chips) + core
 
-    halves = min(COLUMN_HALVES, strips)
-    wide = columns // halves
+    turns = [1, 2] if n_dp % 4 == 0 else [1, 1]
+    turn = [turns[strip % 2] for strip in range(strips)]
+    odds = [replica // k % 2 for k in turn]
     blocks = jnp.stack(
-        [(chip + step) % chips * CORES + (core ^ odd) for step in steps]
+        [(chip + step) % chips * CORES + (core ^ odd) for step in steps for odd in odds]
     ).astype(jnp.int32)
-    count = len(steps) * halves
+    count = len(steps) * strips
     pieces = pl.pallas_call(
         take_kernel,
-        out_shape=(jax.ShapeDtypeStruct((features, wide), bf16),) * count,
-        in_specs=[SCALARS] + anywhere(1),
+        out_shape=(jax.ShapeDtypeStruct((features, LANES), bf16),) * count,
+        in_specs=[SCALARS, pl.BlockSpec(memory_space=pltpu.HBM)],
         out_specs=tuple(anywhere(count)),
         scratch_shapes=[pltpu.SemaphoreType.DMA((count,))],
         compiler_params=params(),
     )(blocks, frozen_key_value)
-
-    def by_rank(value):
-        return jnp.transpose(value, (1, 2, 0)).reshape(factors, features)
+    mine = [
+        [to_chip(pieces[(step - 1) * strips + strip], step) for step in steps]
+        for strip in range(strips)
+    ]
+    halves = min(COLUMN_HALVES, strips)
+    wide = columns // halves
+    groups = [range(k * strips // halves, (k + 1) * strips // halves) for k in range(halves)]
 
     up_sent, _ = lax.optimization_barrier((up_gradient[0], pieces))
-    packed = pl.pallas_call(
-        pack_kernel,
-        out_shape=jax.ShapeDtypeStruct((n_dp, packed_rows, LANES), bf16),
+    widened = prompt_hidden_input.astype(f32)
+    squares = jnp.sum(widened * widened, axis=1)
+    own_x = (widened * input_norm_gain[None, :]).astype(bf16)
+    x = pl.pallas_call(
+        join_kernel,
+        out_shape=jax.ShapeDtypeStruct((tokens, CORES * features), bf16),
         in_specs=in_vmem(2),
         out_specs=in_vmem(1)[0],
         compiler_params=params(),
-    )(by_rank(down_gradient[0]), up_sent)
-    exchanged = lax.all_to_all(packed, "dp", 0, 0, tiled=True)
-
-    mine = []
-    for half in range(halves):
-        for step in steps:
-            piece = pieces[(step - 1) * halves + half]
-            if half > 0:
-                piece, _ = lax.optimization_barrier((piece, packed))
-            mine.append(to_chip(piece, step))
-
-    hidden, _ = lax.optimization_barrier((prompt_hidden_input, packed))
-    widened = hidden.astype(f32)
-    squares = jnp.sum(widened * widened, axis=1)
-    own_x = (widened * input_norm_gain[None, :]).astype(bf16)
-    x = lax.optimization_barrier(jnp.concatenate([own_x, to_sibling(own_x)], axis=1))
+    )(own_x, to_sibling(own_x))
     squares = squares + to_sibling(squares)
 
+    def by_rank(value):
+        return jnp.transpose(value, (1, 2, 0)).reshape(factors, features)
+
+    down_sent = by_rank(down_gradient[0])
     down_state = [by_rank(v) for v in (down_factor_matrix, down_moment_first, down_moment_second)]
     up_state = [up_factor_matrix, up_moment_first, up_moment_second]
-    out_shape = (
+    share = jax.ShapeDtypeStruct((packed_rows, LANES), bf16)
+    shares = jax.ShapeDtypeStruct((n_dp, packed_rows, LANES), bf16)
+    updated = (
         jax.ShapeDtypeStruct((3, factors, down_rows), f32),
         jax.ShapeDtypeStruct((3, up_rows, columns), f32),
-        jax.ShapeDtypeStruct((n_dp, packed_rows, LANES), bf16),
     )
     window = pl.cdiv(down_rows + LANES, LANES) * LANES
-    if features % LANES == 0 and window <= features and up_rows % 8 == 0:
-        a_next, b_next, copies = pl.pallas_call(
-            adam_kernel,
-            out_shape=out_shape,
-            in_specs=[SCALARS] + in_vmem(1) + anywhere(6),
+    aligned = features % LANES == 0 and window <= features
+    aligned = aligned and up_rows % 8 == 0 and down_rows % 16 == 0
+    if aligned and n_dp in (2, 4, 8):
+        number = replica[None].astype(jnp.int32)
+
+        def to_partner(value, k):
+            return lax.ppermute(value, "dp", [(i, i ^ k) for i in range(n_dp)])
+
+        packed = pl.pallas_call(
+            pack_direct_kernel,
+            out_shape=(share,) * n_dp,
+            in_specs=[SCALARS] + in_vmem(2),
+            out_specs=tuple(in_vmem(n_dp)),
+            scratch_shapes=[pltpu.VMEM((features, factors), f32)],
+            compiler_params=params(),
+        )(number, down_sent, up_sent)
+        grads = [packed[0]] + [to_partner(packed[k], k) for k in range(1, n_dp)]
+        grads, first = lax.optimization_barrier((grads, [mine[i] for i in groups[0]]))
+        a_next, b_next, rounded = pl.pallas_call(
+            functools.partial(adam_direct_kernel, n_dp),
+            out_shape=updated + (share,),
+            in_specs=[SCALARS] + in_vmem(n_dp) + anywhere(6),
             out_specs=tuple(in_vmem(3)),
             scratch_shapes=[
                 pltpu.VMEM((3, factors, window), f32),
@@ -333,30 +384,51 @@
                 pltpu.SemaphoreType.DMA((6,)),
             ],
             compiler_params=params(),
-        )(replica[None].astype(jnp.int32), exchanged, *down_state, *up_state)
+        )(number, *grads, *down_state, *up_state)
+        sent = rounded
+        gathered = [rounded] + [to_partner(rounded, k) for k in range(1, n_dp)]
+        gathered, _ = lax.optimization_barrier((gathered, (x, mine)))
+        own_f, packed_b = pl.pallas_call(
+            assemble_kernel,
+            out_shape=(shares, jax.ShapeDtypeStruct((n_dp, packed_rows - down_rows, LANES), bf16)),
+            in_specs=[SCALARS] + in_vmem(n_dp),
+            out_specs=tuple(in_vmem(2)),
+            compiler_params=params(),
+        )(number, *gathered)
     else:
+        packed = pl.pallas_call(
+            pack_kernel,
+            out_shape=shares,
+            in_specs=in_vmem(2),
+            out_specs=in_vmem(1)[0],
+            compiler_params=params(),
+        )(down_sent, up_sent)
+        exchanged = lax.all_to_all(packed, "dp", 0, 0, tiled=True)
         down_state = [
             lax.dynamic_slice_in_dim(v, replica * down_rows, down_rows, 1) for v in down_state
         ]
         up_state = [lax.dynamic_slice_in_dim(v, replica * up_rows, up_rows, 0) for v in up_state]
-        a_next, b_next, copies = pl.pallas_call(
-            adam_sliced_kernel,
-            out_shape=out_shape,
+        a_next, b_next, sent = pl.pallas_call(
+            adam_kernel,
+            out_shape=updated + (shares,),
             in_specs=in_vmem(7),
             out_specs=tuple(in_vmem(3)),
             compiler_params=params(),
         )(exchanged, *down_state, *up_state)
+        own_f = lax.all_to_all(sent, "dp", 0, 0, tiled=True)
+        packed_b = own_f[:, down_rows:]
     a_next = jnp.transpose(a_next.reshape(3, parts, rank, down_rows), (0, 3, 1, 2))
 
-    own_f = lax.all_to_all(copies, "dp", 0, 0, tiled=True)
     sibling_f = to_sibling(own_f)
-    packed_b, _ = lax.optimization_barrier((own_f[:, down_rows:], x))
     other_b = [to_chip(packed_b, step) for step in steps]
 
-    held = [lax.optimization_barrier((value, copies))[0] for value in mine]
-    other = [swap(value) for value in held]
-
-    squares, _ = lax.optimization_barrier((squares, other_b))
+    def swap(value, k):
+        value, _ = lax.optimization_barrier((value, sent))
+        return value, lax.ppermute(value, "dp", [(i, i ^ k) for i in range(n_dp)])
+
+    outside = [[swap(value, turn[strip]) for value in mine[strip]] for strip in range(strips)]
+
+    squares, _ = lax.optimization_barrier((squares, packed_b))
     squares = squares + sum(to_chip(squares, step) for step in steps)
     inv_rms = jnp.broadcast_to(lax.rsqrt(squares / width + 1e-06)[:, None], (tokens, LANES))
 
@@ -372,19 +444,20 @@
     received = {}
     product = None
     for half in range(halves):
-        group = range(half * strips // halves, (half + 1) * strips // halves)
+        group = groups[half]
         for step in steps:
-            at = half * len(steps) + step - 1
-            numbers = jnp.stack([odd, part_of(owner(step))]).astype(jnp.int32)
-            if product is not None:
-                numbers, _ = lax.optimization_barrier((numbers, product))
+            numbers = [part_of(owner(step))] + [odds[strip] for strip in group]
+            numbers = jnp.stack(numbers).astype(jnp.int32)
+            after = squares if product is None else product
+            numbers, _ = lax.optimization_barrier((numbers, after))
+            blocks = [value for strip in group for value in outside[strip][step - 1]]
             weights = pl.pallas_call(
                 functools.partial(outside_kernel, (scale, parts, up_rows, group)),
                 out_shape=jax.ShapeDtypeStruct((CORES * features, wide), bf16),
-                in_specs=[SCALARS] + in_vmem(5),
+                in_specs=[SCALARS] + in_vmem(3 + len(blocks)),
                 out_specs=in_vmem(1)[0],
                 compiler_params=params(),
-            )(numbers, held[at], other[at], own_f, sibling_f, other_b[step - 1])
+            )(numbers, own_f, sibling_f, other_b[step - 1], *blocks)
             for k, rows in enumerate(token_slices):
                 if k > 0:
                     weights, _ = lax.optimization_barrier((weights, product))

time: 106 us -> 110 us (1.038)
  starting transfers between devices: 17.1 us -> 41.5 us
  blocking collectives: 19.3 us -> 0 us
  other arithmetic: 9.01 us -> 3.22 us
  matrix products: 10.1 us -> 6.11 us
  Pallas kernels: 15.8 us -> 19.7 us
  local copies, waits for them, and re-layouts: 4.63 us -> 7.46 us
  waiting for transfers between devices: 28.8 us -> 31.1 us
    ppermute x2 -> x18, starting transfers between devices: 3.6 us -> 27.8 us  [the longest x14 25.7 us: to_partner(): return lax.ppermute(value, 'dp', [(i, i ^ k) for i in range(n_dp)])]
    all_to_all x1 -> x0, blocking collectives: 19.3 us -> none  [body(): exchanged = lax.all_to_all(packed, 'dp', 0, 0, tiled=True)]
    concatenate x1 -> x0, other arithmetic: 6.15 us -> none  [body(): jnp.concatenate([own_x, to_sibling(own_x)], axis=1)]
    dot_general x4, matrix products: 10.1 us -> 6.11 us  [body(): product = jnp.dot(x[rows], weights, preferred_element_type=f32).astype(bf16)]
    all_to_all x1 -> x0, starting transfers between devices: 3.47 us -> none  [body(): own_f = lax.all_to_all(copies, 'dp', 0, 0, tiled=True)]
    ppermute x2 -> x18, waiting for transfers between devices: 5.29 us -> 8.43 us  [the longest x4 4.53 us: swap(): return (value, lax.ppermute(value, 'dp', [(i, i ^ k) for i in range(n_dp)]))]
    pallas_call x3 -> x5, Pallas kernels: 1.72 us -> 4.84 us  [the longest x1 2.36 us: body(): pl.pallas_call(join_kernel, out_shape=jax.ShapeDtypeStruct((tokens, CORES...]
    ppermute x8 -> x10, starting transfers between devices: 9.54 us -> 12.7 us  [to_chip(): return lax.ppermute(value, 'tensor', pairs)]
  transfers between devices with their start and end apart: 14 -> 31, of which waited for: 4 -> 13; matrix products, arithmetic and copies ran while one was open for 16% -> 6% of each run, Pallas kernels for 14% -> 17%
where the time goes in v5:
time: 110 us
  starting transfers between devices  41.5 us (38%)
  waiting for transfers between devices  31.1 us (28%)
  Pallas kernels  19.7 us (18%)
  local copies, waits for them, and re-layouts  7.46 us (7%)
  matrix products  6.11 us (6%)
  other arithmetic  3.22 us (3%)
    ppermute x14, starting transfers between devices, to_partner(): return lax.ppermute(value, 'dp', [(i, i ^ k) for i in range(n_dp)])  25.7 us
    ppermute x10, waiting for transfers between devices, to_chip(): return lax.ppermute(value, 'tensor', pairs)  21.4 us
    ppermute x10, starting transfers between devices, to_chip(): return lax.ppermute(value, 'tensor', pairs)  12.7 us
    pallas_call x1, Pallas kernels, body(): pl.pallas_call(functools.partial(own_kernel, (scale, parts, up_rows, rang...  8.42 us
    unnamed x40, local copies, waits for them, and re-layouts  7.24 us
    dot_general x4, matrix products, body(): product = jnp.dot(x[rows], weights, preferred_element_type=f32).astype(bf16)  6.11 us
    ppermute x4, waiting for transfers between devices, swap(): return (value, lax.ppermute(value, 'dp', [(i, i ^ k) for i in range(n_dp)]))  4.53 us
    ppermute x14, waiting for transfers between devices, to_partner(): return lax.ppermute(value, 'dp', [(i, i ^ k) for i in range(n_dp)])  3.9 us
  transfers between devices with their start and end apart: 31, of which 13 were waited for; matrix products, arithmetic and copies ran while one was open for 6% of the time, Pallas kernels for 17%

profile of v5, /device:TPU:0, one launch (start us, length us, event | category | flops | bytes accessed | tf_op | source)
XLA Modules:
  0.0 110.1 jit_solution(14135187000154343018)
XLA Ops:
  0.6 3.0 %fusion = (bf16[1280,1280]{1,0:T(8,128)(2,1)S(1)}, f32[1280]{0:T(1024)S(1)}) fusion(bf16[1280,1280]{1,0:T(8,128)(2,1)} %param.11, f32[1280]{0:T(1024)} %param.12), kind=kLoop, calls=%fused_computation.2 | loop fusion | flops 8190720 | bytes 6563840 | tf_op jit(solution)/shard_map/convert_element_type | solution.py:335
  3.6 0.5 collective-permute-start.9
  4.2 0.1 pad_add_fusion.rows_ref
  4.2 2.5 %copy-done = bf16[5120,512]{1,0:T(8,128)(2,1)S(1)} copy-done((bf16[5120,512]{1,0:T(8,128)(2,1)S(1)}, bf16[5120,512]{1,0:T(8,128)(2,1)}, u32[]{:S(2)}) %copy-start) | copy-done | bytes 5242904
  6.8 0.8 shard_map.130
  7.6 0.2 copy-done.2
  7.8 0.3 shard_map.131
  8.1 2.7 %collective-permute-start = (bf16[192,128]{1,0:T(8,128)(2,1)S(1)}, bf16[192,128]{1,0:T(8,128)(2,1)S(1)}, u32[]{:S(2)}, u32[]{:S(2)}) collective-permute-start(bf16[192,128]{1,0:T(8,128)(2,1)S(1)} %get-tuple-element.55), channel_id=1, source_target_pairs={{0,4},{4,0},{8,12},{12,8},{16,20},{20,16},{24,28},{28,24},{1,5},{5... | collective-permute-start | bytes 147464 | tf_op jit(solution)/shard_map/ppermute | solution.py:364
  10.8 1.6 %collective-permute-start.1 = (bf16[192,128]{1,0:T(8,128)(2,1)S(1)}, bf16[192,128]{1,0:T(8,128)(2,1)S(1)}, u32[]{:S(2)}, u32[]{:S(2)}) collective-permute-start(bf16[192,128]{1,0:T(8,128)(2,1)S(1)} %get-tuple-element.56), channel_id=1, source_target_pairs={{0,8},{4,12},{8,0},{12,4},{16,24},{20,28},{24,16},{28,20},{1,9},{5... | collective-permute-start | bytes 147464 | tf_op jit(solution)/shard_map/ppermute | solution.py:364
  12.3 3.0 %collective-permute-start.3 = (bf16[192,128]{1,0:T(8,128)(2,1)S(1)}, bf16[192,128]{1,0:T(8,128)(2,1)S(1)}, u32[]{:S(2)}, u32[]{:S(2)}) collective-permute-start(bf16[192,128]{1,0:T(8,128)(2,1)S(1)} %get-tuple-element.58), channel_id=1, source_target_pairs={{0,16},{4,20},{8,24},{12,28},{16,0},{20,4},{24,8},{28,12},{1,17},{... | collective-permute-start | bytes 147464 | tf_op jit(solution)/shard_map/ppermute | solution.py:364
  15.3 1.6 %collective-permute-start.4 = (bf16[192,128]{1,0:T(8,128)(2,1)S(1)}, bf16[192,128]{1,0:T(8,128)(2,1)S(1)}, u32[]{:S(2)}, u32[]{:S(2)}) collective-permute-start(bf16[192,128]{1,0:T(8,128)(2,1)S(1)} %get-tuple-element.59), channel_id=1, source_target_pairs={{0,20},{4,16},{8,28},{12,24},{16,4},{20,0},{24,12},{28,8},{1,21},{... | collective-permute-start | bytes 147464 | tf_op jit(solution)/shard_map/ppermute | solution.py:364
  16.9 1.5 %collective-permute-start.7 = (bf16[1280,128]{1,0:T(8,128)(2,1)S(1)}, bf16[1280,128]{1,0:T(8,128)(2,1)}, u32[]{:S(2)}, u32[]{:S(2)}) collective-permute-start(bf16[1280,128]{1,0:T(8,128)(2,1)S(1)} %get-tuple-element.49), channel_id=1, source_target_pairs={{0,2},{1,3},{2,0},{3,1},{4,6},{5,7},{6,4},{7,5},{8,10},{9,11},{10,... | collective-permute-start | bytes 983048 | tf_op jit(solution)/shard_map/ppermute | solution.py:304
  18.4 0.9 collective-permute-start.8
  19.3 3.9 %collective-permute-start.5 = (bf16[192,128]{1,0:T(8,128)(2,1)S(1)}, bf16[192,128]{1,0:T(8,128)(2,1)S(1)}, u32[]{:S(2)}, u32[]{:S(2)}) collective-permute-start(bf16[192,128]{1,0:T(8,128)(2,1)S(1)} %get-tuple-element.60), channel_id=1, source_target_pairs={{0,24},{4,28},{8,16},{12,20},{16,8},{20,12},{24,0},{28,4},{1,25},{... | collective-permute-start | bytes 147464 | tf_op jit(solution)/shard_map/ppermute | solution.py:364
  23.2 1.7 %collective-permute-start.6 = (bf16[192,128]{1,0:T(8,128)(2,1)S(1)}, bf16[192,128]{1,0:T(8,128)(2,1)S(1)}, u32[]{:S(2)}, u32[]{:S(2)}) collective-permute-start(bf16[192,128]{1,0:T(8,128)(2,1)S(1)} %get-tuple-element.61), channel_id=1, source_target_pairs={{0,28},{4,24},{8,20},{12,16},{16,12},{20,8},{24,4},{28,0},{1,29},{... | collective-permute-start | bytes 147464 | tf_op jit(solution)/shard_map/ppermute | solution.py:364
  24.9 0.4 collective-permute-done.5.refs_6_
  25.3 1.5 %collective-permute-start.18 = (bf16[1280,128]{1,0:T(8,128)(2,1)S(1)}, bf16[1280,128]{1,0:T(8,128)(2,1)S(1)}, u32[]{:S(2)}, u32[]{:S(2)}) collective-permute-start(bf16[1280,128]{1,0:T(8,128)(2,1)S(1)} %get-tuple-element.51), channel_id=1, source_target_pairs={{0,2},{1,3},{2,0},{3,1},{4,6},{5,7},{6,4},{7,5},{8,10},{9,11},{10,... | collective-permute-start | bytes 983048 | tf_op jit(solution)/shard_map/ppermute | solution.py:304
  26.8 3.2 %collective-permute-done.6.refs_7_ = bf16[192,128]{1,0:T(8,128)(2,1)S(1)} collective-permute-done((bf16[192,128]{1,0:T(8,128)(2,1)S(1)}, bf16[192,128]{1,0:T(8,128)(2,1)S(1)}, u32[]{:S(2)}, u32[]{:S(2)}) %collective-permute-start.6) | collective-permute-done | bytes 49184 | tf_op jit(solution)/shard_map/ppermute | solution.py:364
  30.0 1.5 %collective-permute-start.19 = (bf16[1280,128]{1,0:T(8,128)(2,1)S(1)}, bf16[1280,128]{1,0:T(8,128)(2,1)S(1)}, u32[]{:S(2)}, u32[]{:S(2)}) collective-permute-start(bf16[1280,128]{1,0:T(8,128)(2,1)S(1)} %get-tuple-element.52), channel_id=1, source_target_pairs={{0,2},{1,3},{2,0},{3,1},{4,6},{5,7},{6,4},{7,5},{8,10},{9,11},{10,... | collective-permute-start | bytes 983048 | tf_op jit(solution)/shard_map/ppermute | solution.py:304
  31.5 3.2 %collective-permute-done.8.refs_2_ = bf16[1280,128]{1,0:T(8,128)(2,1)} collective-permute-done((bf16[1280,128]{1,0:T(8,128)(2,1)S(1)}, bf16[1280,128]{1,0:T(8,128)(2,1)}, u32[]{:S(2)}, u32[]{:S(2)}) %collective-permute-start.8) | collective-permute-done | bytes 327712 | tf_op jit(solution)/shard_map/ppermute | solution.py:304
  34.7 1.4 %shard_map.132 = (f32[3,128,160]{2,1,0:T(8,128)}, f32[3,8,512]{2,1,0:T(8,128)}, bf16[192,128]{1,0:T(8,128)(2,1)S(1)}) custom-call(s32[1]{0:T(128)} %bitcast.replica, bf16[192,128]{1,0:T(8,128)(2,1)S(1)} %get-tuple-element.62.refs_0_, bf16[192,128]{1,0:T(8,128)(2,1)S(1)} %collective-permute-done.refs_1_, bf16[192,128]{1,0:T(8,128)(2,1)S(1)} %collective-permute-done.1.refs_2_, ...), custom_call_target="tpu_custom_call" | custom-call | tf_op jit(solution)/shard_map/pallas_call | solution.py:376
  36.1 0.6 collective-permute-start.11
  36.6 1.6 %collective-permute-start.12 = (bf16[192,128]{1,0:T(8,128)(2,1)S(1)}, bf16[192,128]{1,0:T(8,128)(2,1)S(1)}, u32[]{:S(2)}, u32[]{:S(2)}) collective-permute-start(bf16[192,128]{1,0:T(8,128)(2,1)S(1)} %get-tuple-element.73.refs_0_), channel_id=1, source_target_pairs={{0,8},{4,12},{8,0},{12,4},{16,24},{20,28},{24,16},{28,20},{1,9},{5... | collective-permute-start | bytes 147464 | tf_op jit(solution)/shard_map/ppermute | solution.py:364
  38.2 3.4 %collective-permute-done.18.refs_0_ = bf16[1280,128]{1,0:T(8,128)(2,1)S(1)} collective-permute-done((bf16[1280,128]{1,0:T(8,128)(2,1)S(1)}, bf16[1280,128]{1,0:T(8,128)(2,1)S(1)}, u32[]{:S(2)}, u32[]{:S(2)}) %collective-permute-start.18) | collective-permute-done | bytes 327712 | tf_op jit(solution)/shard_map/ppermute | solution.py:304
  41.6 1.5 %collective-permute-start.13 = (bf16[192,128]{1,0:T(8,128)(2,1)S(1)}, bf16[192,128]{1,0:T(8,128)(2,1)S(1)}, u32[]{:S(2)}, u32[]{:S(2)}) collective-permute-start(bf16[192,128]{1,0:T(8,128)(2,1)S(1)} %get-tuple-element.73.refs_0_), channel_id=1, source_target_pairs={{0,12},{4,8},{8,4},{12,0},{16,28},{20,24},{24,20},{28,16},{1,13},{... | collective-permute-start | bytes 147464 | tf_op jit(solution)/shard_map/ppermute | solution.py:364
  43.1 3.5 %collective-permute-done.19.refs_2_ = bf16[1280,128]{1,0:T(8,128)(2,1)S(1)} collective-permute-done((bf16[1280,128]{1,0:T(8,128)(2,1)S(1)}, bf16[1280,128]{1,0:T(8,128)(2,1)S(1)}, u32[]{:S(2)}, u32[]{:S(2)}) %collective-permute-start.19) | collective-permute-done | bytes 327712 | tf_op jit(solution)/shard_map/ppermute | solution.py:304
  46.6 2.4 %collective-permute-start.14 = (bf16[192,128]{1,0:T(8,128)(2,1)S(1)}, bf16[192,128]{1,0:T(8,128)(2,1)S(1)}, u32[]{:S(2)}, u32[]{:S(2)}) collective-permute-start(bf16[192,128]{1,0:T(8,128)(2,1)S(1)} %get-tuple-element.73.refs_0_), channel_id=1, source_target_pairs={{0,16},{4,20},{8,24},{12,28},{16,0},{20,4},{24,8},{28,12},{1,17},{... | collective-permute-start | bytes 147464 | tf_op jit(solution)/shard_map/ppermute | solution.py:364
  48.9 0.5 collective-permute-start.15
  49.5 3.4 %collective-permute-start.16 = (bf16[192,128]{1,0:T(8,128)(2,1)S(1)}, bf16[192,128]{1,0:T(8,128)(2,1)S(1)}, u32[]{:S(2)}, u32[]{:S(2)}) collective-permute-start(bf16[192,128]{1,0:T(8,128)(2,1)S(1)} %get-tuple-element.73.refs_0_), channel_id=1, source_target_pairs={{0,24},{4,28},{8,16},{12,20},{16,8},{20,12},{24,0},{28,4},{1,25},{... | collective-permute-start | bytes 147464 | tf_op jit(solution)/shard_map/ppermute | solution.py:364
  52.8 1.5 %collective-permute-start.17 = (bf16[192,128]{1,0:T(8,128)(2,1)S(1)}, bf16[192,128]{1,0:T(8,128)(2,1)S(1)}, u32[]{:S(2)}, u32[]{:S(2)}) collective-permute-start(bf16[192,128]{1,0:T(8,128)(2,1)S(1)} %get-tuple-element.73.refs_0_), channel_id=1, source_target_pairs={{0,28},{4,24},{8,20},{12,16},{16,12},{20,8},{24,4},{28,0},{1,29},{... | collective-permute-start | bytes 147464 | tf_op jit(solution)/shard_map/ppermute | solution.py:364
  54.3 2.4 %shard_map.133.x = bf16[1280,2560]{1,0:T(8,128)(2,1)S(1)} custom-call(bf16[1280,1280]{1,0:T(8,128)(2,1)S(1)} %get-tuple-element.97.own_ref, bf16[1280,1280]{1,0:T(8,128)(2,1)} %collective-permute-done.9.sibling_ref), custom_call_target="tpu_custom_call" | custom-call | tf_op jit(solution)/shard_map/pallas_call | solution.py:336
  56.7 2.7 %copy-done.1 = bf16[1280,2560]{1,0:T(8,128)(2,1)} copy-done((bf16[1280,2560]{1,0:T(8,128)(2,1)}, bf16[1280,2560]{1,0:T(8,128)(2,1)S(1)}, u32[]{:S(2)}) %copy-start.1) | copy-done | bytes 6553624
  59.4 0.3 collective-permute-done.17.refs_7_
  59.8 0.5 collective-permute-start.10
  60.3 1.2 %collective-permute-done.10 = f32[1280]{0:T(1024)S(1)} collective-permute-done((f32[1280]{0:T(1024)S(1)}, f32[1280]{0:T(1024)S(1)}, u32[]{:S(2)}, u32[]{:S(2)}) %collective-permute-start.10) | collective-permute-done | bytes 5152 | tf_op jit(solution)/shard_map/ppermute | solution.py:296
  61.5 1.5 %collective-permute-start.23 = (bf16[1280,128]{1,0:T(8,128)(2,1)}, bf16[1280,128]{1,0:T(8,128)(2,1)S(1)}, u32[]{:S(2)}, u32[]{:S(2)}) collective-permute-start(bf16[1280,128]{1,0:T(8,128)(2,1)} %collective-permute-done.7.refs_0_), channel_id=1, source_target_pairs={{0,4},{4,0},{8,12},{12,8},{16,20},{20,16},{24,28},{28,24},{1,5},{5... | collective-permute-start | bytes 983048 | tf_op jit(solution)/shard_map/ppermute | solution.py:427
  63.1 1.5 %collective-permute-start.20 = (f32[1280]{0:T(1024)S(1)}, f32[1280]{0:T(1024)S(1)}, u32[]{:S(2)}, u32[]{:S(2)}) collective-permute-start(f32[1280]{0:T(1024)S(1)} %add.67), channel_id=1, source_target_pairs={{0,2},{1,3},{2,0},{3,1},{4,6},{5,7},{6,4},{7,5},{8,10},{9,11},{10,... | collective-permute-start | bytes 15368 | tf_op jit(solution)/shard_map/ppermute | solution.py:304
  64.6 0.5 collective-permute-start.25
  65.2 1.6 %collective-permute-done.20 = f32[1280]{0:T(1024)S(1)} collective-permute-done((f32[1280]{0:T(1024)S(1)}, f32[1280]{0:T(1024)S(1)}, u32[]{:S(2)}, u32[]{:S(2)}) %collective-permute-start.20) | collective-permute-done | bytes 5152 | tf_op jit(solution)/shard_map/ppermute | solution.py:304
  66.7 1.5 %collective-permute-start.22 = (bf16[8,32,128]{2,1,0:T(8,128)(2,1)S(1)}, bf16[8,32,128]{2,1,0:T(8,128)(2,1)S(1)}, u32[]{:S(2)}, u32[]{:S(2)}) collective-permute-start(bf16[8,32,128]{2,1,0:T(8,128)(2,1)S(1)} %get-tuple-element.81), channel_id=1, source_target_pairs={{0,2},{1,3},{2,0},{3,1},{4,6},{5,7},{6,4},{7,5},{8,10},{9,11},{10,... | collective-permute-start | bytes 196616 | tf_op jit(solution)/shard_map/ppermute | solution.py:304
  68.2 4.1 %collective-permute-done.23.refs_1_ = bf16[1280,128]{1,0:T(8,128)(2,1)S(1)} collective-permute-done((bf16[1280,128]{1,0:T(8,128)(2,1)}, bf16[1280,128]{1,0:T(8,128)(2,1)S(1)}, u32[]{:S(2)}, u32[]{:S(2)}) %collective-permute-start.23) | collective-permute-done | bytes 327712 | tf_op jit(solution)/shard_map/ppermute | solution.py:427
  72.3 0.4 collective-permute-done.24.refs_3_
  72.7 0.8 copy-done.10
  73.5 1.0 copy-done.11
  74.5 1.8 %shard_map.135 = bf16[2560,256]{1,0:T(8,128)(2,1)S(1)} custom-call(s32[3]{0:T(128)S(1)} %pad_add_fusion.2.numbers, bf16[8,192,128]{2,1,0:T(8,128)(2,1)S(1)} %get-tuple-element.84.own_f, bf16[8,192,128]{2,1,0:T(8,128)(2,1)S(1)} %collective-permute-done.21.sibling_f, bf16[8,32,128]{2,1,0:T(8,128)(2,1)S(1)} %collective-permute-done.22.b_ref, ...), custom_call_target="tpu_custom_call" | custom-call | tf_op jit(solution)/shard_map/pallas_call | solution.py:454
  76.3 3.1 %fusion.16 = bf16[640,256]{1,0:T(8,128)(2,1)S(1)} fusion(bf16[2560,256]{1,0:T(8,128)(2,1)S(1)} %shard_map.135, bf16[1280,2560]{1,0:T(8,128)(2,1)} %copy-done.1), kind=kOutput, calls=%fused_computation.14 | convolution fusion | flops 839024640 | bytes 4915200 | tf_op jit(solution)/shard_map/dot_general | solution.py:464
  79.4 1.6 %collective-permute-start.27 = (bf16[640,256]{1,0:T(8,128)(2,1)S(1)}, bf16[640,256]{1,0:T(8,128)(2,1)S(1)}, u32[]{:S(2)}, u32[]{:S(2)}) collective-permute-start(bf16[640,256]{1,0:T(8,128)(2,1)S(1)} %fusion.16), channel_id=1, source_target_pairs={{0,2},{1,3},{2,0},{3,1},{4,6},{5,7},{6,4},{7,5},{8,10},{9,11},{10,... | collective-permute-start | bytes 983048 | tf_op jit(solution)/shard_map/ppermute | solution.py:304
  81.0 1.0 fusion.10
  82.1 1.1 %shard_map.136 = bf16[2560,256]{1,0:T(8,128)(2,1)S(1)} custom-call(s32[3]{0:T(128)S(1)} %pad_add_fusion.2.numbers, bf16[8,192,128]{2,1,0:T(8,128)(2,1)S(1)} %get-tuple-element.84.own_f, bf16[8,192,128]{2,1,0:T(8,128)(2,1)S(1)} %collective-permute-done.21.sibling_f, bf16[8,32,128]{2,1,0:T(8,128)(2,1)S(1)} %collective-permute-done.22.b_ref, ...), custom_call_target="tpu_custom_call" | custom-call | tf_op jit(solution)/shard_map/pallas_call | solution.py:454
  83.2 1.0 fusion.19
  84.2 0.6 collective-permute-start.29
  84.8 1.5 %collective-permute-start.30 = (bf16[640,256]{1,0:T(8,128)(2,1)S(1)}, bf16[640,256]{1,0:T(8,128)(2,1)S(1)}, u32[]{:S(2)}, u32[]{:S(2)}) collective-permute-start(bf16[640,256]{1,0:T(8,128)(2,1)S(1)} %fusion.10), channel_id=1, source_target_pairs={{0,2},{1,3},{2,0},{3,1},{4,6},{5,7},{6,4},{7,5},{8,10},{9,11},{10,... | collective-permute-start | bytes 983048 | tf_op jit(solution)/shard_map/ppermute | solution.py:304
  86.3 1.0 fusion.13
  87.3 0.6 collective-permute-start.28
  87.9 0.1 pad_add_fusion.1.numbers
  88.0 2.1 %collective-permute-done.27.refs_0_ = bf16[640,256]{1,0:T(8,128)(2,1)S(1)} collective-permute-done((bf16[640,256]{1,0:T(8,128)(2,1)S(1)}, bf16[640,256]{1,0:T(8,128)(2,1)S(1)}, u32[]{:S(2)}, u32[]{:S(2)}) %collective-permute-start.27) | collective-permute-done | bytes 327712 | tf_op jit(solution)/shard_map/ppermute | solution.py:304
  90.2 8.4 %shard_map.137 = (f32[1280,256]{1,0:T(8,128)S(1)}, f32[1280,256]{1,0:T(8,128)S(1)}) custom-call(s32[3]{0:T(128)S(1)} %pad_add_fusion.1.numbers, bf16[5120,512]{1,0:T(8,128)(2,1)S(1)} %bitcast.32, bf16[5120,512]{1,0:T(8,128)(2,1)S(1)} %bitcast.32, bf16[8,192,128]{2,1,0:T(8,128)(2,1)S(1)} %get-tuple-element.84.own_f, ...), custom_call_target="tpu_custom_call" | custom-call | flops 3355443200 | bytes 6553600 | tf_op jit(solution)/shard_map/pallas_call | solution.py:469
  98.6 0.2 broadcast_in_dim.5.inv
  98.8 0.9 shard_map.138.refs_1_
  99.7 4.5 %collective-permute-done.30.refs_0_ = bf16[640,256]{1,0:T(8,128)(2,1)S(1)} collective-permute-done((bf16[640,256]{1,0:T(8,128)(2,1)S(1)}, bf16[640,256]{1,0:T(8,128)(2,1)S(1)}, u32[]{:S(2)}, u32[]{:S(2)}) %collective-permute-start.30) | collective-permute-done | bytes 327712 | tf_op jit(solution)/shard_map/ppermute | solution.py:304
  104.2 0.9 shard_map.139.refs_1_
  105.1 0.9 shard_map.140.refs_1_
  106.0 3.2 %collective-permute-done.28.refs_0_ = bf16[640,256]{1,0:T(8,128)(2,1)S(1)} collective-permute-done((bf16[640,256]{1,0:T(8,128)(2,1)S(1)}, bf16[640,256]{1,0:T(8,128)(2,1)S(1)}, u32[]{:S(2)}, u32[]{:S(2)}) %collective-permute-start.28) | collective-permute-done | bytes 327712 | tf_op jit(solution)/shard_map/ppermute | solution.py:304
  109.2 0.9 shard_map.141
  (63 shorter events, 0.4 us)
Async XLA Ops:
  0.6 34.0 %copy-start.13 = (f32[64,512]{1,0:T(8,128)S(1)}, f32[64,512]{1,0:T(8,128)}, u32[]{:S(2)}) copy-start(f32[64,512]{1,0:T(8,128)} %refs_12_.1) | copy-start | bytes 393220
  3.6 31.0 %copy-start.12 = (f32[64,512]{1,0:T(8,128)S(1)}, f32[64,512]{1,0:T(8,128)}, u32[]{:S(2)}) copy-start(f32[64,512]{1,0:T(8,128)} %refs_11_.1) | copy-start | bytes 393220
  3.6 49.2 %collective-permute-start.9 = (bf16[1280,1280]{1,0:T(8,128)(2,1)S(1)}, bf16[1280,1280]{1,0:T(8,128)(2,1)}, u32[]{:S(2)}, u32[]{:S(2)}) collective-permute-start(bf16[1280,1280]{1,0:T(8,128)(2,1)S(1)} %get-tuple-element.97.own_ref), channel_id=1, source_target_pairs={{0,1},{1,0},{2,3},{3,2},{4,5},{5,4},{6,7},{7,6},{8,9},{9,8},{10,11... | collective-permute-start | bytes 9830408 | tf_op jit(solution)/shard_map/ppermute | solution.py:296
  4.2 2.5 %copy-start = (bf16[5120,512]{1,0:T(8,128)(2,1)S(1)}, bf16[5120,512]{1,0:T(8,128)(2,1)}, u32[]{:S(2)}) copy-start(bf16[5120,512]{1,0:T(8,128)(2,1)} %sibling_block.1) | copy-start | bytes 15728644
  6.7 1.1 copy-start.2
  6.7 1.1 copy-start.15
  6.7 27.9 %copy-start.3 = (f32[1280,2,64]{0,2,1:T(8,128)S(1)}, f32[1280,2,64]{0,2,1:T(8,128)}, u32[]{:S(2)}) copy-start(f32[1280,2,64]{0,2,1:T(8,128)} %param.14) | copy-start | bytes 1966084
  6.7 27.9 %copy-start.4 = (f32[1280,2,64]{0,2,1:T(8,128)S(1)}, f32[1280,2,64]{0,2,1:T(8,128)}, u32[]{:S(2)}) copy-start(f32[1280,2,64]{0,2,1:T(8,128)} %param.15) | copy-start | bytes 1966084
  6.7 27.9 %copy-start.5 = (f32[1280,2,64]{0,2,1:T(8,128)S(1)}, f32[1280,2,64]{0,2,1:T(8,128)}, u32[]{:S(2)}) copy-start(f32[1280,2,64]{0,2,1:T(8,128)} %param.16) | copy-start | bytes 1966084
  6.7 27.9 %copy-start.14 = (f32[64,512]{1,0:T(8,128)S(1)}, f32[64,512]{1,0:T(8,128)}, u32[]{:S(2)}) copy-start(f32[64,512]{1,0:T(8,128)} %refs_13_.1) | copy-start | bytes 393220
  8.1 7.2 %collective-permute-start = (bf16[192,128]{1,0:T(8,128)(2,1)S(1)}, bf16[192,128]{1,0:T(8,128)(2,1)S(1)}, u32[]{:S(2)}, u32[]{:S(2)}) collective-permute-start(bf16[192,128]{1,0:T(8,128)(2,1)S(1)} %get-tuple-element.55), channel_id=1, source_target_pairs={{0,4},{4,0},{8,12},{12,8},{16,20},{20,16},{24,28},{28,24},{1,5},{5... | collective-permute-start | bytes 147464 | tf_op jit(solution)/shard_map/ppermute | solution.py:364
  10.8 6.1 %collective-permute-start.1 = (bf16[192,128]{1,0:T(8,128)(2,1)S(1)}, bf16[192,128]{1,0:T(8,128)(2,1)S(1)}, u32[]{:S(2)}, u32[]{:S(2)}) collective-permute-start(bf16[192,128]{1,0:T(8,128)(2,1)S(1)} %get-tuple-element.56), channel_id=1, source_target_pairs={{0,8},{4,12},{8,0},{12,4},{16,24},{20,28},{24,16},{28,20},{1,9},{5... | collective-permute-start | bytes 147464 | tf_op jit(solution)/shard_map/ppermute | solution.py:364
  12.3 6.0 %collective-permute-start.2 = (bf16[192,128]{1,0:T(8,128)(2,1)S(1)}, bf16[192,128]{1,0:T(8,128)(2,1)S(1)}, u32[]{:S(2)}, u32[]{:S(2)}) collective-permute-start(bf16[192,128]{1,0:T(8,128)(2,1)S(1)} %get-tuple-element.57), channel_id=1, source_target_pairs={{0,12},{4,8},{8,4},{12,0},{16,28},{20,24},{24,20},{28,16},{1,13},{... | collective-permute-start | bytes 147464 | tf_op jit(solution)/shard_map/ppermute | solution.py:364
  12.3 7.0 %collective-permute-start.3 = (bf16[192,128]{1,0:T(8,128)(2,1)S(1)}, bf16[192,128]{1,0:T(8,128)(2,1)S(1)}, u32[]{:S(2)}, u32[]{:S(2)}) collective-permute-start(bf16[192,128]{1,0:T(8,128)(2,1)S(1)} %get-tuple-element.58), channel_id=1, source_target_pairs={{0,16},{4,20},{8,24},{12,28},{16,0},{20,4},{24,8},{28,12},{1,17},{... | collective-permute-start | bytes 147464 | tf_op jit(solution)/shard_map/ppermute | solution.py:364
  15.3 7.9 %collective-permute-start.4 = (bf16[192,128]{1,0:T(8,128)(2,1)S(1)}, bf16[192,128]{1,0:T(8,128)(2,1)S(1)}, u32[]{:S(2)}, u32[]{:S(2)}) collective-permute-start(bf16[192,128]{1,0:T(8,128)(2,1)S(1)} %get-tuple-element.59), channel_id=1, source_target_pairs={{0,20},{4,16},{8,28},{12,24},{16,4},{20,0},{24,12},{28,8},{1,21},{... | collective-permute-start | bytes 147464 | tf_op jit(solution)/shard_map/ppermute | solution.py:364
  16.9 14.6 %collective-permute-start.7 = (bf16[1280,128]{1,0:T(8,128)(2,1)S(1)}, bf16[1280,128]{1,0:T(8,128)(2,1)}, u32[]{:S(2)}, u32[]{:S(2)}) collective-permute-start(bf16[1280,128]{1,0:T(8,128)(2,1)S(1)} %get-tuple-element.49), channel_id=1, source_target_pairs={{0,2},{1,3},{2,0},{3,1},{4,6},{5,7},{6,4},{7,5},{8,10},{9,11},{10,... | collective-permute-start | bytes 983048 | tf_op jit(solution)/shard_map/ppermute | solution.py:304
  18.4 16.3 %collective-permute-start.8 = (bf16[1280,128]{1,0:T(8,128)(2,1)S(1)}, bf16[1280,128]{1,0:T(8,128)(2,1)}, u32[]{:S(2)}, u32[]{:S(2)}) collective-permute-start(bf16[1280,128]{1,0:T(8,128)(2,1)S(1)} %get-tuple-element.50), channel_id=1, source_target_pairs={{0,2},{1,3},{2,0},{3,1},{4,6},{5,7},{6,4},{7,5},{8,10},{9,11},{10,... | collective-permute-start | bytes 983048 | tf_op jit(solution)/shard_map/ppermute | solution.py:304
  19.3 5.9 %collective-permute-start.5 = (bf16[192,128]{1,0:T(8,128)(2,1)S(1)}, bf16[192,128]{1,0:T(8,128)(2,1)S(1)}, u32[]{:S(2)}, u32[]{:S(2)}) collective-permute-start(bf16[192,128]{1,0:T(8,128)(2,1)S(1)} %get-tuple-element.60), channel_id=1, source_target_pairs={{0,24},{4,28},{8,16},{12,20},{16,8},{20,12},{24,0},{28,4},{1,25},{... | collective-permute-start | bytes 147464 | tf_op jit(solution)/shard_map/ppermute | solution.py:364
  23.2 6.8 %collective-permute-start.6 = (bf16[192,128]{1,0:T(8,128)(2,1)S(1)}, bf16[192,128]{1,0:T(8,128)(2,1)S(1)}, u32[]{:S(2)}, u32[]{:S(2)}) collective-permute-start(bf16[192,128]{1,0:T(8,128)(2,1)S(1)} %get-tuple-element.61), channel_id=1, source_target_pairs={{0,28},{4,24},{8,20},{12,16},{16,12},{20,8},{24,4},{28,0},{1,29},{... | collective-permute-start | bytes 147464 | tf_op jit(solution)/shard_map/ppermute | solution.py:364
  25.3 16.3 %collective-permute-start.18 = (bf16[1280,128]{1,0:T(8,128)(2,1)S(1)}, bf16[1280,128]{1,0:T(8,128)(2,1)S(1)}, u32[]{:S(2)}, u32[]{:S(2)}) collective-permute-start(bf16[1280,128]{1,0:T(8,128)(2,1)S(1)} %get-tuple-element.51), channel_id=1, source_target_pairs={{0,2},{1,3},{2,0},{3,1},{4,6},{5,7},{6,4},{7,5},{8,10},{9,11},{10,... | collective-permute-start | bytes 983048 | tf_op jit(solution)/shard_map/ppermute | solution.py:304
  30.0 16.6 %collective-permute-start.19 = (bf16[1280,128]{1,0:T(8,128)(2,1)S(1)}, bf16[1280,128]{1,0:T(8,128)(2,1)S(1)}, u32[]{:S(2)}, u32[]{:S(2)}) collective-permute-start(bf16[1280,128]{1,0:T(8,128)(2,1)S(1)} %get-tuple-element.52), channel_id=1, source_target_pairs={{0,2},{1,3},{2,0},{3,1},{4,6},{5,7},{6,4},{7,5},{8,10},{9,11},{10,... | collective-permute-start | bytes 983048 | tf_op jit(solution)/shard_map/ppermute | solution.py:304
  36.1 12.9 %collective-permute-start.11 = (bf16[192,128]{1,0:T(8,128)(2,1)S(1)}, bf16[192,128]{1,0:T(8,128)(2,1)S(1)}, u32[]{:S(2)}, u32[]{:S(2)}) collective-permute-start(bf16[192,128]{1,0:T(8,128)(2,1)S(1)} %get-tuple-element.73.refs_0_), channel_id=1, source_target_pairs={{0,4},{4,0},{8,12},{12,8},{16,20},{20,16},{24,28},{28,24},{1,5},{5... | collective-permute-start | bytes 147464 | tf_op jit(solution)/shard_map/ppermute | solution.py:364
  36.6 12.8 %collective-permute-start.12 = (bf16[192,128]{1,0:T(8,128)(2,1)S(1)}, bf16[192,128]{1,0:T(8,128)(2,1)S(1)}, u32[]{:S(2)}, u32[]{:S(2)}) collective-permute-start(bf16[192,128]{1,0:T(8,128)(2,1)S(1)} %get-tuple-element.73.refs_0_), channel_id=1, source_target_pairs={{0,8},{4,12},{8,0},{12,4},{16,24},{20,28},{24,16},{28,20},{1,9},{5... | collective-permute-start | bytes 147464 | tf_op jit(solution)/shard_map/ppermute | solution.py:364
  41.6 11.3 %copy-start.6 = (bf16[1280,128]{1,0:T(8,128)(2,1)}, bf16[1280,128]{1,0:T(8,128)(2,1)S(1)}, u32[]{:S(2)}) copy-start(bf16[1280,128]{1,0:T(8,128)(2,1)S(1)} %collective-permute-done.18.refs_0_) | copy-start | bytes 983044
  41.6 17.8 %collective-permute-start.13 = (bf16[192,128]{1,0:T(8,128)(2,1)S(1)}, bf16[192,128]{1,0:T(8,128)(2,1)S(1)}, u32[]{:S(2)}, u32[]{:S(2)}) collective-permute-start(bf16[192,128]{1,0:T(8,128)(2,1)S(1)} %get-tuple-element.73.refs_0_), channel_id=1, source_target_pairs={{0,12},{4,8},{8,4},{12,0},{16,28},{20,24},{24,20},{28,16},{1,13},{... | collective-permute-start | bytes 147464 | tf_op jit(solution)/shard_map/ppermute | solution.py:364
  46.6 6.3 %copy-start.8 = (bf16[1280,128]{1,0:T(8,128)(2,1)}, bf16[1280,128]{1,0:T(8,128)(2,1)S(1)}, u32[]{:S(2)}) copy-start(bf16[1280,128]{1,0:T(8,128)(2,1)S(1)} %collective-permute-done.19.refs_2_) | copy-start | bytes 983044
  46.6 12.8 %collective-permute-start.14 = (bf16[192,128]{1,0:T(8,128)(2,1)S(1)}, bf16[192,128]{1,0:T(8,128)(2,1)S(1)}, u32[]{:S(2)}, u32[]{:S(2)}) collective-permute-start(bf16[192,128]{1,0:T(8,128)(2,1)S(1)} %get-tuple-element.73.refs_0_), channel_id=1, source_target_pairs={{0,16},{4,20},{8,24},{12,28},{16,0},{20,4},{24,8},{28,12},{1,17},{... | collective-permute-start | bytes 147464 | tf_op jit(solution)/shard_map/ppermute | solution.py:364
  48.9 10.4 %collective-permute-start.15 = (bf16[192,128]{1,0:T(8,128)(2,1)S(1)}, bf16[192,128]{1,0:T(8,128)(2,1)S(1)}, u32[]{:S(2)}, u32[]{:S(2)}) collective-permute-start(bf16[192,128]{1,0:T(8,128)(2,1)S(1)} %get-tuple-element.73.refs_0_), channel_id=1, source_target_pairs={{0,20},{4,16},{8,28},{12,24},{16,4},{20,0},{24,12},{28,8},{1,21},{... | collective-permute-start | bytes 147464 | tf_op jit(solution)/shard_map/ppermute | solution.py:364
  49.5 9.9 %collective-permute-start.16 = (bf16[192,128]{1,0:T(8,128)(2,1)S(1)}, bf16[192,128]{1,0:T(8,128)(2,1)S(1)}, u32[]{:S(2)}, u32[]{:S(2)}) collective-permute-start(bf16[192,128]{1,0:T(8,128)(2,1)S(1)} %get-tuple-element.73.refs_0_), channel_id=1, source_target_pairs={{0,24},{4,28},{8,16},{12,20},{16,8},{20,12},{24,0},{28,4},{1,25},{... | collective-permute-start | bytes 147464 | tf_op jit(solution)/shard_map/ppermute | solution.py:364
  52.8 6.9 %collective-permute-start.17 = (bf16[192,128]{1,0:T(8,128)(2,1)S(1)}, bf16[192,128]{1,0:T(8,128)(2,1)S(1)}, u32[]{:S(2)}, u32[]{:S(2)}) collective-permute-start(bf16[192,128]{1,0:T(8,128)(2,1)S(1)} %get-tuple-element.73.refs_0_), channel_id=1, source_target_pairs={{0,28},{4,24},{8,20},{12,16},{16,12},{20,8},{24,4},{28,0},{1,29},{... | collective-permute-start | bytes 147464 | tf_op jit(solution)/shard_map/ppermute | solution.py:364
  56.7 2.7 %copy-start.1 = (bf16[1280,2560]{1,0:T(8,128)(2,1)}, bf16[1280,2560]{1,0:T(8,128)(2,1)S(1)}, u32[]{:S(2)}) copy-start(bf16[1280,2560]{1,0:T(8,128)(2,1)S(1)} %shard_map.133.x) | copy-start | bytes 19660804
  59.7 13.8 %collective-permute-start.21 = (bf16[8,192,128]{2,1,0:T(8,128)(2,1)S(1)}, bf16[8,192,128]{2,1,0:T(8,128)(2,1)S(1)}, u32[]{:S(2)}, u32[]{:S(2)}) collective-permute-start(bf16[8,192,128]{2,1,0:T(8,128)(2,1)S(1)} %get-tuple-element.84.own_f), channel_id=1, source_target_pairs={{0,1},{1,0},{2,3},{3,2},{4,5},{5,4},{6,7},{7,6},{8,9},{9,8},{10,11... | collective-permute-start | bytes 1179656 | tf_op jit(solution)/shard_map/ppermute | solution.py:296
  59.8 1.7 %collective-permute-start.10 = (f32[1280]{0:T(1024)S(1)}, f32[1280]{0:T(1024)S(1)}, u32[]{:S(2)}, u32[]{:S(2)}) collective-permute-start(f32[1280]{0:T(1024)S(1)} %get-tuple-element.98), channel_id=1, source_target_pairs={{0,1},{1,0},{2,3},{3,2},{4,5},{5,4},{6,7},{7,6},{8,9},{9,8},{10,11... | collective-permute-start | bytes 15368 | tf_op jit(solution)/shard_map/ppermute | solution.py:296
  61.5 10.8 %collective-permute-start.23 = (bf16[1280,128]{1,0:T(8,128)(2,1)}, bf16[1280,128]{1,0:T(8,128)(2,1)S(1)}, u32[]{:S(2)}, u32[]{:S(2)}) collective-permute-start(bf16[1280,128]{1,0:T(8,128)(2,1)} %collective-permute-done.7.refs_0_), channel_id=1, source_target_pairs={{0,4},{4,0},{8,12},{12,8},{16,20},{20,16},{24,28},{28,24},{1,5},{5... | collective-permute-start | bytes 983048 | tf_op jit(solution)/shard_map/ppermute | solution.py:427
  63.1 9.7 %collective-permute-start.24 = (bf16[1280,128]{1,0:T(8,128)(2,1)}, bf16[1280,128]{1,0:T(8,128)(2,1)S(1)}, u32[]{:S(2)}, u32[]{:S(2)}) collective-permute-start(bf16[1280,128]{1,0:T(8,128)(2,1)} %collective-permute-done.8.refs_2_), channel_id=1, source_target_pairs={{0,8},{4,12},{8,0},{12,4},{16,24},{20,28},{24,16},{28,20},{1,9},{5... | collective-permute-start | bytes 983048 | tf_op jit(solution)/shard_map/ppermute | solution.py:427
  63.1 3.7 %collective-permute-start.20 = (f32[1280]{0:T(1024)S(1)}, f32[1280]{0:T(1024)S(1)}, u32[]{:S(2)}, u32[]{:S(2)}) collective-permute-start(f32[1280]{0:T(1024)S(1)} %add.67), channel_id=1, source_target_pairs={{0,2},{1,3},{2,0},{3,1},{4,6},{5,7},{6,4},{7,5},{8,10},{9,11},{10,... | collective-permute-start | bytes 15368 | tf_op jit(solution)/shard_map/ppermute | solution.py:304
  64.6 17.4 %collective-permute-start.25 = (bf16[1280,128]{1,0:T(8,128)(2,1)}, bf16[1280,128]{1,0:T(8,128)(2,1)S(1)}, u32[]{:S(2)}, u32[]{:S(2)}) collective-permute-start(bf16[1280,128]{1,0:T(8,128)(2,1)} %copy-done.6), channel_id=1, source_target_pairs={{0,4},{4,0},{8,12},{12,8},{16,20},{20,16},{24,28},{28,24},{1,5},{5... | collective-permute-start | bytes 983048 | tf_op jit(solution)/shard_map/ppermute | solution.py:427
  66.7 6.8 %collective-permute-start.22 = (bf16[8,32,128]{2,1,0:T(8,128)(2,1)S(1)}, bf16[8,32,128]{2,1,0:T(8,128)(2,1)S(1)}, u32[]{:S(2)}, u32[]{:S(2)}) collective-permute-start(bf16[8,32,128]{2,1,0:T(8,128)(2,1)S(1)} %get-tuple-element.81), channel_id=1, source_target_pairs={{0,2},{1,3},{2,0},{3,1},{4,6},{5,7},{6,4},{7,5},{8,10},{9,11},{10,... | collective-permute-start | bytes 196616 | tf_op jit(solution)/shard_map/ppermute | solution.py:304
  72.3 9.7 %collective-permute-start.26 = (bf16[1280,128]{1,0:T(8,128)(2,1)}, bf16[1280,128]{1,0:T(8,128)(2,1)S(1)}, u32[]{:S(2)}, u32[]{:S(2)}) collective-permute-start(bf16[1280,128]{1,0:T(8,128)(2,1)} %copy-done.8), channel_id=1, source_target_pairs={{0,8},{4,12},{8,0},{12,4},{16,24},{20,28},{24,16},{28,20},{1,9},{5... | collective-permute-start | bytes 983048 | tf_op jit(solution)/shard_map/ppermute | solution.py:427
  72.7 0.8 copy-start.10
  73.5 1.0 copy-start.11
  74.5 6.5 %slice-start.2 = ((s8[6553600]{0:T(1024)(128)(4,1)}), s8[4194304]{0:T(1024)(128)(4,1)S(1)}, s32[]{:S(2)}) async-start(s8[6553600]{0:T(1024)(128)(4,1)} %bitcast.33), calls=%async_computation.2 | async-start | bytes 8388608
  76.3 4.7 %slice-start.3 = ((s8[6553600]{0:T(1024)(128)(4,1)}), s8[2359296]{0:T(1024)(128)(4,1)S(1)}, s32[]{:S(2)}) async-start(s8[6553600]{0:T(1024)(128)(4,1)} %bitcast.33), calls=%async_computation.3 | async-start | bytes 4718592
  79.4 2.6 %copy-start.7 = (bf16[1280,128]{1,0:T(8,128)(2,1)S(1)}, bf16[1280,128]{1,0:T(8,128)(2,1)}, u32[]{:S(2)}) copy-start(bf16[1280,128]{1,0:T(8,128)(2,1)} %copy-done.6) | copy-start | bytes 983044
  79.4 2.6 %copy-start.9 = (bf16[1280,128]{1,0:T(8,128)(2,1)S(1)}, bf16[1280,128]{1,0:T(8,128)(2,1)}, u32[]{:S(2)}) copy-start(bf16[1280,128]{1,0:T(8,128)(2,1)} %copy-done.8) | copy-start | bytes 983044
  79.4 10.7 %collective-permute-start.27 = (bf16[640,256]{1,0:T(8,128)(2,1)S(1)}, bf16[640,256]{1,0:T(8,128)(2,1)S(1)}, u32[]{:S(2)}, u32[]{:S(2)}) collective-permute-start(bf16[640,256]{1,0:T(8,128)(2,1)S(1)} %fusion.16), channel_id=1, source_target_pairs={{0,2},{1,3},{2,0},{3,1},{4,6},{5,7},{6,4},{7,5},{8,10},{9,11},{10,... | collective-permute-start | bytes 983048 | tf_op jit(solution)/shard_map/ppermute | solution.py:304
  83.2 7.0 %slice-start = ((s8[5242880]{0:T(1024)(128)(4,1)}), s8[4194304]{0:T(1024)(128)(4,1)S(1)}, s32[]{:S(2)}) async-start(s8[5242880]{0:T(1024)(128)(4,1)} %bitcast.31), calls=%async_computation | async-start | bytes 8388608
  84.2 5.9 %slice-start.1 = ((s8[5242880]{0:T(1024)(128)(4,1)}), s8[1048576]{0:T(1024)(128)(4,1)S(1)}, s32[]{:S(2)}) async-start(s8[5242880]{0:T(1024)(128)(4,1)} %bitcast.31), calls=%async_computation.1 | async-start | bytes 2097152
  84.2 20.9 %collective-permute-start.29 = (bf16[640,256]{1,0:T(8,128)(2,1)S(1)}, bf16[640,256]{1,0:T(8,128)(2,1)S(1)}, u32[]{:S(2)}, u32[]{:S(2)}) collective-permute-start(bf16[640,256]{1,0:T(8,128)(2,1)S(1)} %fusion.19), channel_id=1, source_target_pairs={{0,2},{1,3},{2,0},{3,1},{4,6},{5,7},{6,4},{7,5},{8,10},{9,11},{10,... | collective-permute-start | bytes 983048 | tf_op jit(solution)/shard_map/ppermute | solution.py:304
  84.8 19.4 %collective-permute-start.30 = (bf16[640,256]{1,0:T(8,128)(2,1)S(1)}, bf16[640,256]{1,0:T(8,128)(2,1)S(1)}, u32[]{:S(2)}, u32[]{:S(2)}) collective-permute-start(bf16[640,256]{1,0:T(8,128)(2,1)S(1)} %fusion.10), channel_id=1, source_target_pairs={{0,2},{1,3},{2,0},{3,1},{4,6},{5,7},{6,4},{7,5},{8,10},{9,11},{10,... | collective-permute-start | bytes 983048 | tf_op jit(solution)/shard_map/ppermute | solution.py:304
  87.3 21.8 %collective-permute-start.28 = (bf16[640,256]{1,0:T(8,128)(2,1)S(1)}, bf16[640,256]{1,0:T(8,128)(2,1)S(1)}, u32[]{:S(2)}, u32[]{:S(2)}) collective-permute-start(bf16[640,256]{1,0:T(8,128)(2,1)S(1)} %fusion.13), channel_id=1, source_target_pairs={{0,2},{1,3},{2,0},{3,1},{4,6},{5,7},{6,4},{7,5},{8,10},{9,11},{10,... | collective-permute-start | bytes 983048 | tf_op jit(solution)/shard_map/ppermute | solution.py:304

commit v6 on v5

--- a/solution.py
+++ b/solution.py
@@ -14,7 +14,8 @@
 LANES = 128
 COLUMN_HALVES = 2
 TOKEN_HALVES = 2
-VMEM_BYTES = 40 * 2**20
+VMEM_BYTES = 32 * 2**20
+TAKE_VMEM_BYTES = 60 * 2**20
 
 
 def adaptive_moment_update(param, first, second, grad_mean):
@@ -39,59 +40,55 @@
     return pltpu.CompilerParams(vmem_limit_bytes=VMEM_BYTES, **more)
 
 
-def share_of(down, up, down_at, up_at, down_rows, up_rows):
-    pieces = [down[down_at : down_at + down_rows]] if isinstance(down_at, int) else [
-        down[pl.ds(down_at, down_rows)]
-    ]
-    rows = up[up_at : up_at + up_rows] if isinstance(up_at, int) else up[pl.ds(up_at, up_rows)]
-    for k in range(rows.shape[1] // LANES):
-        pieces.append(rows[:, k * LANES : (k + 1) * LANES])
-    return jnp.concatenate(pieces, axis=0).astype(jnp.bfloat16)
-
-
 def pack_kernel(down_ref, up_ref, out_ref):
     shares = out_ref.shape[0]
     down, up = down_ref[...].T, up_ref[...]
     down_rows, up_rows = down.shape[0] // shares, up.shape[0] // shares
     for i in range(shares):
-        out_ref[i] = share_of(down, up, i * down_rows, i * up_rows, down_rows, up_rows)
-
-
-def pack_direct_kernel(replica, down_ref, up_ref, *refs):
-    outs, down = refs[:-1], refs[-1]
-    down[...] = down_ref[...].T
-    down_rows, up_rows = down.shape[0] // len(outs), up_ref.shape[0] // len(outs)
-    for k, out in enumerate(outs):
-        i = replica[0] ^ k
-        down_at = pl.multiple_of(i * down_rows, down_rows)
-        up_at = pl.multiple_of(i * up_rows, up_rows)
-        out[...] = share_of(down, up_ref, down_at, up_at, down_rows, up_rows)
+        pieces = [down[i * down_rows : (i + 1) * down_rows]]
+        for k in range(up.shape[1] // LANES):
+            pieces.append(up[i * up_rows : (i + 1) * up_rows, k * LANES : (k + 1) * LANES])
+        out_ref[i] = jnp.concatenate(pieces, axis=0).astype(jnp.bfloat16)
 
 
 def take_kernel(rows_ref, weights_ref, *refs):
     outs, sem = refs[:-1], refs[-1]
-    features = outs[0].shape[0]
-    strips = weights_ref.shape[1] // LANES
+    strips, features, _ = outs[0].shape
     copies = []
-    for i, out in enumerate(outs):
+    for i in range(len(outs) * strips):
         row = pl.multiple_of(rows_ref[i] * features, features)
         source = weights_ref.at[pl.ds(row, features), pl.ds(i % strips * LANES, LANES)]
-        copies.append(pltpu.make_async_copy(source, out, sem.at[i]))
+        copies.append(
+            pltpu.make_async_copy(source, outs[i // strips].at[i % strips], sem.at[i])
+        )
     for copy in copies:
         copy.start()
     for copy in copies:
         copy.wait()
 
 
-def join_kernel(own_ref, sibling_ref, out_ref):
+def split_kernel(in_ref, *outs):
+    for k, out in enumerate(outs):
+        out[...] = in_ref[k]
+
+
+def prepare_kernel(own_ref, sibling_ref, own_gain, sibling_gain, x_ref, squares_ref):
     rows, features = own_ref.shape
-    tile = tile_of(rows)
+    tile = 64 if rows % 64 == 0 else rows
 
     @pl.loop(0, rows // tile)
     def _(i):
         at = pl.ds(pl.multiple_of(i * tile, tile), tile)
-        out_ref[at, :features] = own_ref[at, :]
-        out_ref[at, features:] = sibling_ref[at, :]
+        total = jnp.zeros((tile, 1), jnp.float32)
+        for k, (ref, gain) in enumerate(((own_ref, own_gain), (sibling_ref, sibling_gain))):
+            wide = ref[at, :].astype(jnp.float32)
+            total += jnp.sum(wide * wide, axis=1, keepdims=True)
+            x_ref[at, k * features : (k + 1) * features] = (wide * gain[...]).astype(x_ref.dtype)
+        squares_ref[at, :] = jnp.broadcast_to(total, (tile, LANES))
+
+
+def tail_kernel(in_ref, out_ref):
+    out_ref[...] = in_ref[:, in_ref.shape[1] - out_ref.shape[1] :]
 
 
 def update(total, down, up, a_ref, b_ref):
@@ -125,10 +122,10 @@
         factor_ref[i] = rounded
 
 
-def adam_direct_kernel(replicas, replica, *refs):
-    grads, refs = refs[:replicas], refs[replicas:]
+def adam_copy_kernel(replica, grad_ref, *refs):
     down_state, up_state, refs = refs[:3], refs[3:6], refs[6:]
     a_ref, b_ref, factor_ref, down_buf, up_buf, sem = refs
+    replicas = grad_ref.shape[0]
     down_rows, window = a_ref.shape[2], down_buf.shape[2]
     up_rows = b_ref.shape[1]
     first = replica[0] * down_rows
@@ -143,28 +140,19 @@
         copies.append(pltpu.make_async_copy(source, up_buf.at[i], sem.at[3 + i]))
     for copy in copies:
         copy.start()
-    total = grads[0][...].astype(jnp.float32)
-    for grad in grads[1:]:
-        total = total + grad[...].astype(jnp.float32)
+    total = jnp.sum(grad_ref[...].astype(jnp.float32), axis=0) / replicas
     for copy in copies:
         copy.wait()
     shift = window - (first - lane)
-    factor_ref[...] = update(
-        total / replicas,
+    rounded = update(
+        total,
         lambda: [pltpu.roll(down_buf[i], shift, 1)[:, :down_rows] for i in range(3)],
         lambda: [up_buf[i] for i in range(3)],
         a_ref,
         b_ref,
     )
-
-
-def assemble_kernel(replica, *refs):
-    shares, (factor_ref, b_ref) = refs[:-2], refs[-2:]
-    down_rows = factor_ref.shape[1] - b_ref.shape[1]
-    for k, share in enumerate(shares):
-        i = replica[0] ^ k
-        factor_ref[i] = share[...]
-        b_ref[i] = share[down_rows:]
+    for i in range(replicas):
+        factor_ref[i] = rounded
 
 
 def factor_a(packed_ref, down_rows):
@@ -312,35 +300,34 @@
     blocks = jnp.stack(
         [(chip + step) % chips * CORES + (core ^ odd) for step in steps for odd in odds]
     ).astype(jnp.int32)
-    count = len(steps) * strips
-    pieces = pl.pallas_call(
+    taken = pl.pallas_call(
         take_kernel,
-        out_shape=(jax.ShapeDtypeStruct((features, LANES), bf16),) * count,
-        in_specs=[SCALARS, pl.BlockSpec(memory_space=pltpu.HBM)],
-        out_specs=tuple(anywhere(count)),
-        scratch_shapes=[pltpu.SemaphoreType.DMA((count,))],
-        compiler_params=params(),
+        out_shape=(jax.ShapeDtypeStruct((strips, features, LANES), bf16),) * len(steps),
+        in_specs=[SCALARS] + anywhere(1),
+        out_specs=tuple(anywhere(len(steps))),
+        scratch_shapes=[pltpu.SemaphoreType.DMA((len(steps) * strips,))],
+        compiler_params=pltpu.CompilerParams(vmem_limit_bytes=TAKE_VMEM_BYTES),
     )(blocks, frozen_key_value)
-    mine = [
-        [to_chip(pieces[(step - 1) * strips + strip], step) for step in steps]
-        for strip in range(strips)
-    ]
+    mine = [to_chip(value, step) for value, step in zip(taken, steps)]
     halves = min(COLUMN_HALVES, strips)
     wide = columns // halves
     groups = [range(k * strips // halves, (k + 1) * strips // halves) for k in range(halves)]
 
-    up_sent, _ = lax.optimization_barrier((up_gradient[0], pieces))
-    widened = prompt_hidden_input.astype(f32)
-    squares = jnp.sum(widened * widened, axis=1)
-    own_x = (widened * input_norm_gain[None, :]).astype(bf16)
-    x = pl.pallas_call(
-        join_kernel,
-        out_shape=jax.ShapeDtypeStruct((tokens, CORES * features), bf16),
-        in_specs=in_vmem(2),
-        out_specs=in_vmem(1)[0],
+    hidden, up_sent, _ = lax.optimization_barrier(
+        (prompt_hidden_input, up_gradient[0], taken)
+    )
+    gain = input_norm_gain[None, :]
+    x, squares = pl.pallas_call(
+        prepare_kernel,
+        out_shape=(
+            jax.ShapeDtypeStruct((tokens, CORES * features), bf16),
+            jax.ShapeDtypeStruct((tokens, LANES), f32),
+        ),
+        in_specs=in_vmem(4),
+        out_specs=tuple(in_vmem(2)),
         compiler_params=params(),
-    )(own_x, to_sibling(own_x))
-    squares = squares + to_sibling(squares)
+    )(hidden, to_sibling(hidden), gain, to_sibling(gain))
+    squares = squares[:, 0]
 
     def by_rank(value):
         return jnp.transpose(value, (1, 2, 0)).reshape(factors, features)
@@ -348,7 +335,6 @@
     down_sent = by_rank(down_gradient[0])
     down_state = [by_rank(v) for v in (down_factor_matrix, down_moment_first, down_moment_second)]
     up_state = [up_factor_matrix, up_moment_first, up_moment_second]
-    share = jax.ShapeDtypeStruct((packed_rows, LANES), bf16)
     shares = jax.ShapeDtypeStruct((n_dp, packed_rows, LANES), bf16)
     updated = (
         jax.ShapeDtypeStruct((3, factors, down_rows), f32),
@@ -357,26 +343,19 @@
     window = pl.cdiv(down_rows + LANES, LANES) * LANES
     aligned = features % LANES == 0 and window <= features
     aligned = aligned and up_rows % 8 == 0 and down_rows % 16 == 0
-    if aligned and n_dp in (2, 4, 8):
-        number = replica[None].astype(jnp.int32)
-
-        def to_partner(value, k):
-            return lax.ppermute(value, "dp", [(i, i ^ k) for i in range(n_dp)])
-
-        packed = pl.pallas_call(
-            pack_direct_kernel,
-            out_shape=(share,) * n_dp,
-            in_specs=[SCALARS] + in_vmem(2),
-            out_specs=tuple(in_vmem(n_dp)),
-            scratch_shapes=[pltpu.VMEM((features, factors), f32)],
-            compiler_params=params(),
-        )(number, down_sent, up_sent)
-        grads = [packed[0]] + [to_partner(packed[k], k) for k in range(1, n_dp)]
-        grads, first = lax.optimization_barrier((grads, [mine[i] for i in groups[0]]))
-        a_next, b_next, rounded = pl.pallas_call(
-            functools.partial(adam_direct_kernel, n_dp),
-            out_shape=updated + (share,),
-            in_specs=[SCALARS] + in_vmem(n_dp) + anywhere(6),
+    packed = pl.pallas_call(
+        pack_kernel,
+        out_shape=shares,
+        in_specs=in_vmem(2),
+        out_specs=in_vmem(1)[0],
+        compiler_params=params(),
+    )(down_sent, up_sent)
+    exchanged = lax.all_to_all(packed, "dp", 0, 0, tiled=True)
+    if aligned:
+        a_next, b_next, sent = pl.pallas_call(
+            adam_copy_kernel,
+            out_shape=updated + (shares,),
+            in_specs=[SCALARS] + in_vmem(1) + anywhere(6),
             out_specs=tuple(in_vmem(3)),
             scratch_shapes=[
                 pltpu.VMEM((3, factors, window), f32),
@@ -384,26 +363,8 @@
                 pltpu.SemaphoreType.DMA((6,)),
             ],
             compiler_params=params(),
-        )(number, *grads, *down_state, *up_state)
-        sent = rounded
-        gathered = [rounded] + [to_partner(rounded, k) for k in range(1, n_dp)]
-        gathered, _ = lax.optimization_barrier((gathered, (x, mine)))
-        own_f, packed_b = pl.pallas_call(
-            assemble_kernel,
-            out_shape=(shares, jax.ShapeDtypeStruct((n_dp, packed_rows - down_rows, LANES), bf16)),
-            in_specs=[SCALARS] + in_vmem(n_dp),
-            out_specs=tuple(in_vmem(2)),
-            compiler_params=params(),
-        )(number, *gathered)
+        )(replica[None].astype(jnp.int32), exchanged, *down_state, *up_state)
     else:
-        packed = pl.pallas_call(
-            pack_kernel,
-            out_shape=shares,
-            in_specs=in_vmem(2),
-            out_specs=in_vmem(1)[0],
-            compiler_params=params(),
-        )(down_sent, up_sent)
-        exchanged = lax.all_to_all(packed, "dp", 0, 0, tiled=True)
         down_state = [
             lax.dynamic_slice_in_dim(v, replica * down_rows, down_rows, 1) for v in down_state
         ]
@@ -415,20 +376,34 @@
             out_specs=tuple(in_vmem(3)),
             compiler_params=params(),
         )(exchanged, *down_state, *up_state)
-        own_f = lax.all_to_all(sent, "dp", 0, 0, tiled=True)
-        packed_b = own_f[:, down_rows:]
+    own_f = lax.all_to_all(sent, "dp", 0, 0, tiled=True)
     a_next = jnp.transpose(a_next.reshape(3, parts, rank, down_rows), (0, 3, 1, 2))
 
+    own_f, x, squares = lax.optimization_barrier((own_f, x, squares))
     sibling_f = to_sibling(own_f)
+    packed_b = pl.pallas_call(
+        tail_kernel,
+        out_shape=jax.ShapeDtypeStruct((n_dp, packed_rows - down_rows, LANES), bf16),
+        in_specs=in_vmem(1),
+        out_specs=in_vmem(1)[0],
+        compiler_params=params(),
+    )(own_f)
     other_b = [to_chip(packed_b, step) for step in steps]
 
-    def swap(value, k):
+    outside = [[] for _ in range(strips)]
+    for value in mine:
         value, _ = lax.optimization_barrier((value, sent))
-        return value, lax.ppermute(value, "dp", [(i, i ^ k) for i in range(n_dp)])
-
-    outside = [[swap(value, turn[strip]) for value in mine[strip]] for strip in range(strips)]
-
-    squares, _ = lax.optimization_barrier((squares, packed_b))
+        split = pl.pallas_call(
+            split_kernel,
+            out_shape=(jax.ShapeDtypeStruct((features, LANES), bf16),) * strips,
+            in_specs=in_vmem(1),
+            out_specs=tuple(in_vmem(strips)),
+            compiler_params=params(),
+        )(value)
+        for strip in range(strips):
+            pairs = [(i, i ^ turn[strip]) for i in range(n_dp)]
+            outside[strip].append((split[strip], lax.ppermute(split[strip], "dp", pairs)))
+
     squares = squares + sum(to_chip(squares, step) for step in steps)
     inv_rms = jnp.broadcast_to(lax.rsqrt(squares / width + 1e-06)[:, None], (tokens, LANES))
 
@@ -448,8 +423,8 @@
         for step in steps:
             numbers = [part_of(owner(step))] + [odds[strip] for strip in group]
             numbers = jnp.stack(numbers).astype(jnp.int32)
-            after = squares if product is None else product
-            numbers, _ = lax.optimization_barrier((numbers, after))
+            if product is not None:
+                numbers, _ = lax.optimization_barrier((numbers, product))
             blocks = [value for strip in group for value in outside[strip][step - 1]]
             weights = pl.pallas_call(
                 functools.partial(outside_kernel, (scale, parts, up_rows, group)),
@@ -460,7 +435,7 @@
             )(numbers, own_f, sibling_f, other_b[step - 1], *blocks)
             for k, rows in enumerate(token_slices):
                 if k > 0:
-                    weights, _ = lax.optimization_barrier((weights, product))
+                    weights, _ = lax.optimization_barrier((weights, (product, squares)))
                 product = jnp.dot(x[rows], weights, preferred_element_type=f32).astype(bf16)
                 received.setdefault((k, half), []).append(to_chip(product, chips - step))
 

time: 110 us -> 128 us (1.16)
  Pallas kernels: 19.7 us -> 61.9 us
  starting transfers between devices: 41.5 us -> 25.5 us
  waiting for transfers between devices: 31.1 us -> 27.9 us
  local copies, waits for them, and re-layouts: 7.46 us -> 4.39 us
  other arithmetic: 3.22 us -> 0.81 us
    pallas_call x5 -> x6, Pallas kernels: 4.84 us -> 50.6 us  [the longest x1 41.6 us: body(): pl.pallas_call(take_kernel, out_shape=(jax.ShapeDtypeStruct((strips, feat...]
    ppermute x18 -> x4, starting transfers between devices: 27.8 us -> 5.64 us  [body(): lax.ppermute(split[strip], 'dp', pairs)]
    all_to_all x0 -> x2, waiting for transfers between devices: none -> 12 us  [the longest x1 10.8 us: body(): exchanged = lax.all_to_all(packed, 'dp', 0, 0, tiled=True)]
    all_to_all x0 -> x2, starting transfers between devices: none -> 10.5 us  [the longest x1 6.86 us: body(): exchanged = lax.all_to_all(packed, 'dp', 0, 0, tiled=True)]
    ppermute x10 -> x7, waiting for transfers between devices: 21.4 us -> 12.5 us  [to_chip(): return lax.ppermute(value, 'tensor', pairs)]
    ppermute x18 -> x4, waiting for transfers between devices: 8.43 us -> 2.25 us  [body(): lax.ppermute(split[strip], 'dp', pairs)]
    ppermute x10 -> x7, starting transfers between devices: 12.7 us -> 8.79 us  [to_chip(): return lax.ppermute(value, 'tensor', pairs)]
    unnamed x40 -> x28, local copies, waits for them, and re-layouts: 7.24 us -> 3.93 us
  transfers between devices with their start and end apart: 31 -> 16, of which waited for: 13 -> 10; matrix products, arithmetic and copies ran while one was open for 6% -> 5% of each run, Pallas kernels for 17% -> 15%
where the time goes in v6:
time: 128 us
  Pallas kernels  61.9 us (48%)
  waiting for transfers between devices  27.9 us (22%)
  starting transfers between devices  25.5 us (20%)
  matrix products  6.11 us (5%)
  local copies, waits for them, and re-layouts  4.39 us (3%)
    pallas_call x1, Pallas kernels, body(): pl.pallas_call(take_kernel, out_shape=(jax.ShapeDtypeStruct((strips, feat...  41.6 us
    ppermute x7, waiting for transfers between devices, to_chip(): return lax.ppermute(value, 'tensor', pairs)  12.5 us
    all_to_all x1, waiting for transfers between devices, body(): exchanged = lax.all_to_all(packed, 'dp', 0, 0, tiled=True)  10.8 us
    ppermute x7, starting transfers between devices, to_chip(): return lax.ppermute(value, 'tensor', pairs)  8.79 us
    all_to_all x1, starting transfers between devices, body(): exchanged = lax.all_to_all(packed, 'dp', 0, 0, tiled=True)  6.86 us
    pallas_call x1, Pallas kernels, body(): pl.pallas_call(prepare_kernel, out_shape=(jax.ShapeDtypeStruct((tokens, C...  6.46 us
    dot_general x4, matrix products, body(): product = jnp.dot(x[rows], weights, preferred_element_type=f32).astype(bf16)  6.11 us
    ppermute x4, starting transfers between devices, body(): lax.ppermute(split[strip], 'dp', pairs)  5.64 us
  transfers between devices with their start and end apart: 16, of which 10 were waited for; matrix products, arithmetic and copies ran while one was open for 5% of the time, Pallas kernels for 15%

profile of v6, /device:TPU:0, one launch (start us, length us, event | category | flops | bytes accessed | tf_op | source)
XLA Modules:
  0.0 127.6 jit_solution(8472550738139898428)
XLA Ops:
  0.7 0.7 pad_add_fusion.rows_ref
  1.4 41.6 %shard_map.130 = bf16[4,1280,128]{2,1,0:T(8,128)(2,1)} custom-call(s32[4]{0:T(128)} %pad_add_fusion.rows_ref, bf16[5120,512]{1,0:T(8,128)(2,1)} %sibling_block.1), custom_call_target="tpu_custom_call" | custom-call | tf_op jit(solution)/shard_map/pallas_call | solution.py:303
  43.0 0.0 copy-start.2
  43.0 0.0 copy-start.3
  43.0 0.0 copy-start.6
  43.0 0.0 copy-start.7
  43.1 0.0 copy-start.8
  43.1 0.5 collective-permute-start
  43.6 0.9 shard_map.131
  44.5 6.9 %all-to-all-start = ((bf16[8,192,128]{2,1,0:T(8,128)(2,1)}), bf16[8,192,128]{2,1,0:T(8,128)(2,1)S(1)}, u32[]{:S(2)}, u32[]{:S(2)}) async-start(bf16[8,192,128]{2,1,0:T(8,128)(2,1)} %shard_map.131), calls=%async_computation | async-start | bytes 786432 | tf_op jit(solution)/shard_map/all_to_all | solution.py:353
  51.4 1.5 %collective-permute-start.4 = (bf16[4,1280,128]{2,1,0:T(8,128)(2,1)}, bf16[4,1280,128]{2,1,0:T(8,128)(2,1)S(1)}, u32[]{:S(2)}, u32[]{:S(2)}) collective-permute-start(bf16[4,1280,128]{2,1,0:T(8,128)(2,1)} %shard_map.130), channel_id=1, source_target_pairs={{0,2},{1,3},{2,0},{3,1},{4,6},{5,7},{6,4},{7,5},{8,10},{9,11},{10,... | collective-permute-start | bytes 3932168 | tf_op jit(solution)/shard_map/ppermute | solution.py:292
  52.9 10.8 %all-to-all-done.grad_ref = bf16[8,192,128]{2,1,0:T(8,128)(2,1)S(1)} async-done(((bf16[8,192,128]{2,1,0:T(8,128)(2,1)}), bf16[8,192,128]{2,1,0:T(8,128)(2,1)S(1)}, u32[]{:S(2)}, u32[]{:S(2)}) %all-to-all-start) | async-done | bytes 393248 | tf_op jit(solution)/shard_map/all_to_all | solution.py:353
  63.7 0.0 copy-start.4
  63.7 1.1 copy-done.4
  64.8 1.5 %shard_map.132 = (f32[3,128,160]{2,1,0:T(8,128)}, f32[3,8,512]{2,1,0:T(8,128)}, bf16[8,192,128]{2,1,0:T(8,128)(2,1)}) custom-call(s32[1]{0:T(128)} %bitcast.replica, bf16[8,192,128]{2,1,0:T(8,128)(2,1)S(1)} %all-to-all-done.grad_ref, f32[128,1280]{1,0:T(8,128)S(1)} %bitcast.36, f32[128,1280]{1,0:T(8,128)S(1)} %bitcast.37, f32[128,1280]{1,0:T(8,128)S(1)} %bitcast.38, ...), custom_call_target="tpu_custom_call" | custom-call | tf_op jit(solution)/shard_map/pallas_call | solution.py:355
  66.3 3.6 %all-to-all-start.1 = ((bf16[8,192,128]{2,1,0:T(8,128)(2,1)}), bf16[8,192,128]{2,1,0:T(8,128)(2,1)S(1)}, u32[]{:S(2)}, u32[]{:S(2)}) async-start(bf16[8,192,128]{2,1,0:T(8,128)(2,1)} %get-tuple-element.27), calls=%async_computation.1 | async-start | bytes 786432 | tf_op jit(solution)/shard_map/all_to_all | solution.py:379
  70.0 0.1 collective-permute-start.1
  70.0 1.2 collective-permute-done.1.sibling_gain
  71.2 0.0 collective-permute-done.sibling_ref
  71.2 6.5 %shard_map.133 = (bf16[1280,2560]{1,0:T(8,128)(2,1)S(1)}, f32[1280,128]{1,0:T(8,128)S(1)}) custom-call(bf16[1280,1280]{1,0:T(8,128)(2,1)} %own_ref, bf16[1280,1280]{1,0:T(8,128)(2,1)} %collective-permute-done.sibling_ref, f32[1,1280]{1,0:T(1,128)S(1)} %broadcast_in_dim.13.own_gain, f32[1,1280]{1,0:T(1,128)S(1)} %collective-permute-done.1.sibling_gain), custom_call_target="tpu_custom_call" | custom-call | tf_op jit(solution)/shard_map/pallas_call | solution.py:320
  77.7 2.8 %copy-done = bf16[1280,2560]{1,0:T(8,128)(2,1)} copy-done((bf16[1280,2560]{1,0:T(8,128)(2,1)}, bf16[1280,2560]{1,0:T(8,128)(2,1)S(1)}, u32[]{:S(2)}) %copy-start) | copy-done | bytes 6553624
  80.4 0.2 slice_reduce_fusion
  80.7 1.1 all-to-all-done.1.in_ref.own_f
  81.8 0.0 collective-permute-start.2
  81.8 0.6 collective-permute-done.4.in_ref
  82.5 0.1 shard_map.135
  82.5 1.8 %collective-permute-start.5 = (bf16[1280,128]{1,0:T(8,128)(2,1)S(1)}, bf16[1280,128]{1,0:T(8,128)(2,1)S(1)}, u32[]{:S(2)}, u32[]{:S(2)}) collective-permute-start(bf16[1280,128]{1,0:T(8,128)(2,1)S(1)} %get-tuple-element.34.refs_0_), channel_id=1, source_target_pairs={{0,4},{4,0},{8,12},{12,8},{16,20},{20,16},{24,28},{28,24},{1,5},{5... | collective-permute-start | bytes 983048 | tf_op jit(solution)/shard_map/ppermute | solution.py:405
  84.4 1.5 %collective-permute-start.6 = (bf16[1280,128]{1,0:T(8,128)(2,1)S(1)}, bf16[1280,128]{1,0:T(8,128)(2,1)S(1)}, u32[]{:S(2)}, u32[]{:S(2)}) collective-permute-start(bf16[1280,128]{1,0:T(8,128)(2,1)S(1)} %get-tuple-element.35.refs_2_), channel_id=1, source_target_pairs={{0,8},{4,12},{8,0},{12,4},{16,24},{20,28},{24,16},{28,20},{1,9},{5... | collective-permute-start | bytes 983048 | tf_op jit(solution)/shard_map/ppermute | solution.py:405
  85.8 1.5 %collective-permute-start.7 = (f32[1280]{0:T(1024)S(1)}, f32[1280]{0:T(1024)S(1)}, u32[]{:S(2)}, u32[]{:S(2)}) collective-permute-start(f32[1280]{0:T(1024)S(1)} %slice_reduce_fusion), channel_id=1, source_target_pairs={{0,2},{1,3},{2,0},{3,1},{4,6},{5,7},{6,4},{7,5},{8,10},{9,11},{10,... | collective-permute-start | bytes 15368 | tf_op jit(solution)/shard_map/ppermute | solution.py:292
  87.3 0.1 pad_add_fusion.2.numbers
  87.4 0.6 collective-permute-start.8
  88.0 1.5 %collective-permute-done.7 = f32[1280]{0:T(1024)S(1)} collective-permute-done((f32[1280]{0:T(1024)S(1)}, f32[1280]{0:T(1024)S(1)}, u32[]{:S(2)}, u32[]{:S(2)}) %collective-permute-start.7) | collective-permute-done | bytes 5152 | tf_op jit(solution)/shard_map/ppermute | solution.py:292
  89.5 1.5 %collective-permute-start.3 = (bf16[8,32,128]{2,1,0:T(8,128)(2,1)S(1)}, bf16[8,32,128]{2,1,0:T(8,128)(2,1)S(1)}, u32[]{:S(2)}, u32[]{:S(2)}) collective-permute-start(bf16[8,32,128]{2,1,0:T(8,128)(2,1)S(1)} %shard_map.134), channel_id=1, source_target_pairs={{0,2},{1,3},{2,0},{3,1},{4,6},{5,7},{6,4},{7,5},{8,10},{9,11},{10,... | collective-permute-start | bytes 196616 | tf_op jit(solution)/shard_map/ppermute | solution.py:292
  91.0 2.2 %collective-permute-done.5.refs_1_ = bf16[1280,128]{1,0:T(8,128)(2,1)S(1)} collective-permute-done((bf16[1280,128]{1,0:T(8,128)(2,1)S(1)}, bf16[1280,128]{1,0:T(8,128)(2,1)S(1)}, u32[]{:S(2)}, u32[]{:S(2)}) %collective-permute-start.5) | collective-permute-done | bytes 327712 | tf_op jit(solution)/shard_map/ppermute | solution.py:405
  93.2 1.8 %collective-permute-start.9 = (bf16[1280,128]{1,0:T(8,128)(2,1)S(1)}, bf16[1280,128]{1,0:T(8,128)(2,1)S(1)}, u32[]{:S(2)}, u32[]{:S(2)}) collective-permute-start(bf16[1280,128]{1,0:T(8,128)(2,1)S(1)} %get-tuple-element.40.refs_2_), channel_id=1, source_target_pairs={{0,8},{4,12},{8,0},{12,4},{16,24},{20,28},{24,16},{28,20},{1,9},{5... | collective-permute-start | bytes 983048 | tf_op jit(solution)/shard_map/ppermute | solution.py:405
  95.0 0.0 collective-permute-done.6.refs_3_
  95.0 0.0 collective-permute-done.3.b_ref
  95.0 0.0 collective-permute-done.2.sibling_f
  95.0 0.0 slice-start.2
  95.0 1.1 shard_map.136
  96.2 3.1 %fusion.14 = bf16[640,256]{1,0:T(8,128)(2,1)S(1)} fusion(bf16[2560,256]{1,0:T(8,128)(2,1)S(1)} %shard_map.136, bf16[1280,2560]{1,0:T(8,128)(2,1)} %copy-done), kind=kOutput, calls=%fused_computation.10 | convolution fusion | flops 839024640 | bytes 4915200 | tf_op jit(solution)/shard_map/dot_general | solution.py:439
  99.3 1.6 %collective-permute-start.10 = (bf16[640,256]{1,0:T(8,128)(2,1)S(1)}, bf16[640,256]{1,0:T(8,128)(2,1)S(1)}, u32[]{:S(2)}, u32[]{:S(2)}) collective-permute-start(bf16[640,256]{1,0:T(8,128)(2,1)S(1)} %fusion.14), channel_id=1, source_target_pairs={{0,2},{1,3},{2,0},{3,1},{4,6},{5,7},{6,4},{7,5},{8,10},{9,11},{10,... | collective-permute-start | bytes 983048 | tf_op jit(solution)/shard_map/ppermute | solution.py:292
  100.8 1.0 fusion.8
  101.8 0.6 collective-permute-start.13
  102.4 0.0 collective-permute-done.8.refs_1_
  102.4 0.0 collective-permute-done.9.refs_3_
  102.4 1.1 shard_map.137
  103.6 0.0 slice-start
  103.6 1.0 fusion.17
  104.6 0.0 slice-start.1
  104.6 1.6 %collective-permute-start.12 = (bf16[640,256]{1,0:T(8,128)(2,1)S(1)}, bf16[640,256]{1,0:T(8,128)(2,1)S(1)}, u32[]{:S(2)}, u32[]{:S(2)}) collective-permute-start(bf16[640,256]{1,0:T(8,128)(2,1)S(1)} %fusion.17), channel_id=1, source_target_pairs={{0,2},{1,3},{2,0},{3,1},{4,6},{5,7},{6,4},{7,5},{8,10},{9,11},{10,... | collective-permute-start | bytes 983048 | tf_op jit(solution)/shard_map/ppermute | solution.py:292
  106.2 1.0 fusion.11
  107.2 0.6 collective-permute-start.11
  107.8 0.1 pad_add_fusion.1.numbers
  107.9 2.1 %collective-permute-done.10.refs_0_ = bf16[640,256]{1,0:T(8,128)(2,1)S(1)} collective-permute-done((bf16[640,256]{1,0:T(8,128)(2,1)S(1)}, bf16[640,256]{1,0:T(8,128)(2,1)S(1)}, u32[]{:S(2)}, u32[]{:S(2)}) %collective-permute-start.10) | collective-permute-done | bytes 327712 | tf_op jit(solution)/shard_map/ppermute | solution.py:292
  110.0 5.6 %shard_map.138 = (f32[1280,256]{1,0:T(8,128)S(1)}, f32[1280,256]{1,0:T(8,128)S(1)}) custom-call(s32[3]{0:T(128)S(1)} %pad_add_fusion.1.numbers, bf16[5120,512]{1,0:T(8,128)(2,1)S(1)} %bitcast.32, bf16[5120,512]{1,0:T(8,128)(2,1)S(1)} %bitcast.32, bf16[8,192,128]{2,1,0:T(8,128)(2,1)S(1)} %all-to-all-done.1.in_ref.own_f, ...), custom_call_target="tpu_custom_call" | custom-call | flops 3355443200 | bytes 6553600 | tf_op jit(solution)/shard_map/pallas_call | solution.py:444
  115.6 0.2 broadcast_in_dim.14.inv
  115.8 0.9 shard_map.139.refs_1_
  116.7 0.3 collective-permute-done.13.refs_0_
  117.0 0.9 shard_map.140.refs_1_
  117.9 5.3 %collective-permute-done.12.refs_0_ = bf16[640,256]{1,0:T(8,128)(2,1)S(1)} collective-permute-done((bf16[640,256]{1,0:T(8,128)(2,1)S(1)}, bf16[640,256]{1,0:T(8,128)(2,1)S(1)}, u32[]{:S(2)}, u32[]{:S(2)}) %collective-permute-start.12) | collective-permute-done | bytes 327712 | tf_op jit(solution)/shard_map/ppermute | solution.py:292
  123.2 0.9 shard_map.141.refs_1_
  124.1 2.6 %collective-permute-done.11.refs_0_ = bf16[640,256]{1,0:T(8,128)(2,1)S(1)} collective-permute-done((bf16[640,256]{1,0:T(8,128)(2,1)S(1)}, bf16[640,256]{1,0:T(8,128)(2,1)S(1)}, u32[]{:S(2)}, u32[]{:S(2)}) %collective-permute-start.11) | collective-permute-done | bytes 327712 | tf_op jit(solution)/shard_map/ppermute | solution.py:292
  126.7 0.9 shard_map.142
  (22 shorter events, 0.1 us)
Async XLA Ops:
  1.4 42.2 %copy-start.1 = (f32[1,1280,2,64]{1,3,2,0:T(8,128)S(1)}, f32[1,1280,2,64]{1,3,2,0:T(8,128)}, u32[]{:S(2)}) copy-start(f32[1,1280,2,64]{1,3,2,0:T(8,128)} %param.20) | copy-start | bytes 1966084
  1.4 42.2 %copy-start.5 = (f32[1,64,512]{2,1,0:T(8,128)S(1)}, f32[1,64,512]{2,1,0:T(8,128)}, u32[]{:S(2)}) copy-start(f32[1,64,512]{2,1,0:T(8,128)} %param.21) | copy-start | bytes 393220
  43.0 20.7 %copy-start.2 = (f32[1280,2,64]{0,2,1:T(8,128)S(1)}, f32[1280,2,64]{0,2,1:T(8,128)}, u32[]{:S(2)}) copy-start(f32[1280,2,64]{0,2,1:T(8,128)} %param.14) | copy-start | bytes 1966084
  43.0 20.7 %copy-start.3 = (f32[1280,2,64]{0,2,1:T(8,128)S(1)}, f32[1280,2,64]{0,2,1:T(8,128)}, u32[]{:S(2)}) copy-start(f32[1280,2,64]{0,2,1:T(8,128)} %param.15) | copy-start | bytes 1966084
  43.0 20.7 %copy-start.6 = (f32[64,512]{1,0:T(8,128)S(1)}, f32[64,512]{1,0:T(8,128)}, u32[]{:S(2)}) copy-start(f32[64,512]{1,0:T(8,128)} %refs_3_.1) | copy-start | bytes 393220
  43.0 20.7 %copy-start.7 = (f32[64,512]{1,0:T(8,128)S(1)}, f32[64,512]{1,0:T(8,128)}, u32[]{:S(2)}) copy-start(f32[64,512]{1,0:T(8,128)} %refs_4_.1) | copy-start | bytes 393220
  43.1 20.7 %copy-start.8 = (f32[64,512]{1,0:T(8,128)S(1)}, f32[64,512]{1,0:T(8,128)}, u32[]{:S(2)}) copy-start(f32[64,512]{1,0:T(8,128)} %refs_5_.1) | copy-start | bytes 393220
  43.1 28.1 %collective-permute-start = (bf16[1280,1280]{1,0:T(8,128)(2,1)}, bf16[1280,1280]{1,0:T(8,128)(2,1)}, u32[]{:S(2)}, u32[]{:S(2)}) collective-permute-start(bf16[1280,1280]{1,0:T(8,128)(2,1)} %own_ref), channel_id=1, source_target_pairs={{0,1},{1,0},{2,3},{3,2},{4,5},{5,4},{6,7},{7,6},{8,9},{9,8},{10,11... | collective-permute-start | bytes 9830408 | tf_op jit(solution)/shard_map/ppermute | solution.py:284
  44.5 19.2 %all-to-all-start = ((bf16[8,192,128]{2,1,0:T(8,128)(2,1)}), bf16[8,192,128]{2,1,0:T(8,128)(2,1)S(1)}, u32[]{:S(2)}, u32[]{:S(2)}) async-start(bf16[8,192,128]{2,1,0:T(8,128)(2,1)} %shard_map.131), calls=%async_computation | async-start | bytes 786432 | tf_op jit(solution)/shard_map/all_to_all | solution.py:353
  51.4 31.1 %collective-permute-start.4 = (bf16[4,1280,128]{2,1,0:T(8,128)(2,1)}, bf16[4,1280,128]{2,1,0:T(8,128)(2,1)S(1)}, u32[]{:S(2)}, u32[]{:S(2)}) collective-permute-start(bf16[4,1280,128]{2,1,0:T(8,128)(2,1)} %shard_map.130), channel_id=1, source_target_pairs={{0,2},{1,3},{2,0},{3,1},{4,6},{5,7},{6,4},{7,5},{8,10},{9,11},{10,... | collective-permute-start | bytes 3932168 | tf_op jit(solution)/shard_map/ppermute | solution.py:292
  63.7 1.1 copy-start.4
  64.8 5.1 %copy-start.9 = (f32[1280]{0:T(1024)S(1)}, f32[1280]{0:T(1024)}, u32[]{:S(2)}) copy-start(f32[1280]{0:T(1024)} %param.12) | copy-start | bytes 15364
  66.3 15.5 %all-to-all-start.1 = ((bf16[8,192,128]{2,1,0:T(8,128)(2,1)}), bf16[8,192,128]{2,1,0:T(8,128)(2,1)S(1)}, u32[]{:S(2)}, u32[]{:S(2)}) async-start(bf16[8,192,128]{2,1,0:T(8,128)(2,1)} %get-tuple-element.27), calls=%async_computation.1 | async-start | bytes 786432 | tf_op jit(solution)/shard_map/all_to_all | solution.py:379
  70.0 1.2 collective-permute-start.1
  77.7 2.8 %copy-start = (bf16[1280,2560]{1,0:T(8,128)(2,1)}, bf16[1280,2560]{1,0:T(8,128)(2,1)S(1)}, u32[]{:S(2)}) copy-start(bf16[1280,2560]{1,0:T(8,128)(2,1)S(1)} %get-tuple-element.31.x) | copy-start | bytes 19660804
  81.8 13.2 %collective-permute-start.2 = (bf16[8,192,128]{2,1,0:T(8,128)(2,1)S(1)}, bf16[8,192,128]{2,1,0:T(8,128)(2,1)S(1)}, u32[]{:S(2)}, u32[]{:S(2)}) collective-permute-start(bf16[8,192,128]{2,1,0:T(8,128)(2,1)S(1)} %all-to-all-done.1.in_ref.own_f), channel_id=1, source_target_pairs={{0,1},{1,0},{2,3},{3,2},{4,5},{5,4},{6,7},{7,6},{8,9},{9,8},{10,11... | collective-permute-start | bytes 1179656 | tf_op jit(solution)/shard_map/ppermute | solution.py:284
  82.5 10.7 %collective-permute-start.5 = (bf16[1280,128]{1,0:T(8,128)(2,1)S(1)}, bf16[1280,128]{1,0:T(8,128)(2,1)S(1)}, u32[]{:S(2)}, u32[]{:S(2)}) collective-permute-start(bf16[1280,128]{1,0:T(8,128)(2,1)S(1)} %get-tuple-element.34.refs_0_), channel_id=1, source_target_pairs={{0,4},{4,0},{8,12},{12,8},{16,20},{20,16},{24,28},{28,24},{1,5},{5... | collective-permute-start | bytes 983048 | tf_op jit(solution)/shard_map/ppermute | solution.py:405
  84.4 10.7 %collective-permute-start.6 = (bf16[1280,128]{1,0:T(8,128)(2,1)S(1)}, bf16[1280,128]{1,0:T(8,128)(2,1)S(1)}, u32[]{:S(2)}, u32[]{:S(2)}) collective-permute-start(bf16[1280,128]{1,0:T(8,128)(2,1)S(1)} %get-tuple-element.35.refs_2_), channel_id=1, source_target_pairs={{0,8},{4,12},{8,0},{12,4},{16,24},{20,28},{24,16},{28,20},{1,9},{5... | collective-permute-start | bytes 983048 | tf_op jit(solution)/shard_map/ppermute | solution.py:405
  85.8 3.7 %collective-permute-start.7 = (f32[1280]{0:T(1024)S(1)}, f32[1280]{0:T(1024)S(1)}, u32[]{:S(2)}, u32[]{:S(2)}) collective-permute-start(f32[1280]{0:T(1024)S(1)} %slice_reduce_fusion), channel_id=1, source_target_pairs={{0,2},{1,3},{2,0},{3,1},{4,6},{5,7},{6,4},{7,5},{8,10},{9,11},{10,... | collective-permute-start | bytes 15368 | tf_op jit(solution)/shard_map/ppermute | solution.py:292
  87.4 15.1 %collective-permute-start.8 = (bf16[1280,128]{1,0:T(8,128)(2,1)S(1)}, bf16[1280,128]{1,0:T(8,128)(2,1)S(1)}, u32[]{:S(2)}, u32[]{:S(2)}) collective-permute-start(bf16[1280,128]{1,0:T(8,128)(2,1)S(1)} %get-tuple-element.39.refs_0_), channel_id=1, source_target_pairs={{0,4},{4,0},{8,12},{12,8},{16,20},{20,16},{24,28},{28,24},{1,5},{5... | collective-permute-start | bytes 983048 | tf_op jit(solution)/shard_map/ppermute | solution.py:405
  89.5 5.5 %collective-permute-start.3 = (bf16[8,32,128]{2,1,0:T(8,128)(2,1)S(1)}, bf16[8,32,128]{2,1,0:T(8,128)(2,1)S(1)}, u32[]{:S(2)}, u32[]{:S(2)}) collective-permute-start(bf16[8,32,128]{2,1,0:T(8,128)(2,1)S(1)} %shard_map.134), channel_id=1, source_target_pairs={{0,2},{1,3},{2,0},{3,1},{4,6},{5,7},{6,4},{7,5},{8,10},{9,11},{10,... | collective-permute-start | bytes 196616 | tf_op jit(solution)/shard_map/ppermute | solution.py:292
  93.2 9.2 %collective-permute-start.9 = (bf16[1280,128]{1,0:T(8,128)(2,1)S(1)}, bf16[1280,128]{1,0:T(8,128)(2,1)S(1)}, u32[]{:S(2)}, u32[]{:S(2)}) collective-permute-start(bf16[1280,128]{1,0:T(8,128)(2,1)S(1)} %get-tuple-element.40.refs_2_), channel_id=1, source_target_pairs={{0,8},{4,12},{8,0},{12,4},{16,24},{20,28},{24,16},{28,20},{1,9},{5... | collective-permute-start | bytes 983048 | tf_op jit(solution)/shard_map/ppermute | solution.py:405
  95.0 5.8 %slice-start.2 = ((s8[6553600]{0:T(1024)(128)(4,1)}), s8[4194304]{0:T(1024)(128)(4,1)S(1)}, s32[]{:S(2)}) async-start(s8[6553600]{0:T(1024)(128)(4,1)} %bitcast.33), calls=%async_computation.4 | async-start | bytes 8388608
  96.2 4.7 %slice-start.3 = ((s8[6553600]{0:T(1024)(128)(4,1)}), s8[2359296]{0:T(1024)(128)(4,1)S(1)}, s32[]{:S(2)}) async-start(s8[6553600]{0:T(1024)(128)(4,1)} %bitcast.33), calls=%async_computation.5 | async-start | bytes 4718592
  99.3 10.7 %collective-permute-start.10 = (bf16[640,256]{1,0:T(8,128)(2,1)S(1)}, bf16[640,256]{1,0:T(8,128)(2,1)S(1)}, u32[]{:S(2)}, u32[]{:S(2)}) collective-permute-start(bf16[640,256]{1,0:T(8,128)(2,1)S(1)} %fusion.14), channel_id=1, source_target_pairs={{0,2},{1,3},{2,0},{3,1},{4,6},{5,7},{6,4},{7,5},{8,10},{9,11},{10,... | collective-permute-start | bytes 983048 | tf_op jit(solution)/shard_map/ppermute | solution.py:292
  101.8 15.2 %collective-permute-start.13 = (bf16[640,256]{1,0:T(8,128)(2,1)S(1)}, bf16[640,256]{1,0:T(8,128)(2,1)S(1)}, u32[]{:S(2)}, u32[]{:S(2)}) collective-permute-start(bf16[640,256]{1,0:T(8,128)(2,1)S(1)} %fusion.8), channel_id=1, source_target_pairs={{0,2},{1,3},{2,0},{3,1},{4,6},{5,7},{6,4},{7,5},{8,10},{9,11},{10,... | collective-permute-start | bytes 983048 | tf_op jit(solution)/shard_map/ppermute | solution.py:292
  103.6 6.4 %slice-start = ((s8[5242880]{0:T(1024)(128)(4,1)}), s8[4194304]{0:T(1024)(128)(4,1)S(1)}, s32[]{:S(2)}) async-start(s8[5242880]{0:T(1024)(128)(4,1)} %bitcast.31), calls=%async_computation.2 | async-start | bytes 8388608
  104.6 5.4 %slice-start.1 = ((s8[5242880]{0:T(1024)(128)(4,1)}), s8[1048576]{0:T(1024)(128)(4,1)S(1)}, s32[]{:S(2)}) async-start(s8[5242880]{0:T(1024)(128)(4,1)} %bitcast.31), calls=%async_computation.3 | async-start | bytes 2097152
  104.6 18.6 %collective-permute-start.12 = (bf16[640,256]{1,0:T(8,128)(2,1)S(1)}, bf16[640,256]{1,0:T(8,128)(2,1)S(1)}, u32[]{:S(2)}, u32[]{:S(2)}) collective-permute-start(bf16[640,256]{1,0:T(8,128)(2,1)S(1)} %fusion.17), channel_id=1, source_target_pairs={{0,2},{1,3},{2,0},{3,1},{4,6},{5,7},{6,4},{7,5},{8,10},{9,11},{10,... | collective-permute-start | bytes 983048 | tf_op jit(solution)/shard_map/ppermute | solution.py:292
  107.2 19.5 %collective-permute-start.11 = (bf16[640,256]{1,0:T(8,128)(2,1)S(1)}, bf16[640,256]{1,0:T(8,128)(2,1)S(1)}, u32[]{:S(2)}, u32[]{:S(2)}) collective-permute-start(bf16[640,256]{1,0:T(8,128)(2,1)S(1)} %fusion.11), channel_id=1, source_target_pairs={{0,2},{1,3},{2,0},{3,1},{4,6},{5,7},{6,4},{7,5},{8,10},{9,11},{10,... | collective-permute-start | bytes 983048 | tf_op jit(solution)/shard_map/ppermute | solution.py:292

commit v7 on v6

--- a/solution.py
+++ b/solution.py
@@ -14,8 +14,8 @@
 LANES = 128
 COLUMN_HALVES = 2
 TOKEN_HALVES = 2
-VMEM_BYTES = 32 * 2**20
-TAKE_VMEM_BYTES = 60 * 2**20
+VMEM_BYTES = 16 * 2**20
+TAKE_VMEM_BYTES = 58 * 2**20
 
 
 def adaptive_moment_update(param, first, second, grad_mean):
@@ -51,16 +51,22 @@
         out_ref[i] = jnp.concatenate(pieces, axis=0).astype(jnp.bfloat16)
 
 
-def take_kernel(rows_ref, weights_ref, *refs):
+def take_kernel(chips, turn, weights_ref, *refs):
     outs, sem = refs[:-1], refs[-1]
-    strips, features, _ = outs[0].shape
+    features = outs[0].shape[1]
+    place, replica = lax.axis_index("tensor"), lax.axis_index("dp")
+    chip, core = place // CORES, place % CORES
     copies = []
-    for i in range(len(outs) * strips):
-        row = pl.multiple_of(rows_ref[i] * features, features)
-        source = weights_ref.at[pl.ds(row, features), pl.ds(i % strips * LANES, LANES)]
-        copies.append(
-            pltpu.make_async_copy(source, outs[i // strips].at[i % strips], sem.at[i])
-        )
+    for i, out in enumerate(outs):
+        step, first = 1 + i % (chips - 1), i // (chips - 1) * out.shape[0]
+        for k in range(out.shape[0]):
+            half = (core + replica // turn[first + k]) % 2
+            row = ((chip + step) % chips * CORES + half) * features
+            source = weights_ref.at[
+                pl.ds(pl.multiple_of(row, features), features),
+                pl.ds((first + k) * LANES, LANES),
+            ]
+            copies.append(pltpu.make_async_copy(source, out.at[k], sem.at[len(copies)]))
     for copy in copies:
         copy.start()
     for copy in copies:
@@ -297,21 +303,27 @@
     turns = [1, 2] if n_dp % 4 == 0 else [1, 1]
     turn = [turns[strip % 2] for strip in range(strips)]
     odds = [replica // k % 2 for k in turn]
-    blocks = jnp.stack(
-        [(chip + step) % chips * CORES + (core ^ odd) for step in steps for odd in odds]
-    ).astype(jnp.int32)
-    taken = pl.pallas_call(
-        take_kernel,
-        out_shape=(jax.ShapeDtypeStruct((strips, features, LANES), bf16),) * len(steps),
-        in_specs=[SCALARS] + anywhere(1),
-        out_specs=tuple(anywhere(len(steps))),
-        scratch_shapes=[pltpu.SemaphoreType.DMA((len(steps) * strips,))],
-        compiler_params=pltpu.CompilerParams(vmem_limit_bytes=TAKE_VMEM_BYTES),
-    )(blocks, frozen_key_value)
-    mine = [to_chip(value, step) for value, step in zip(taken, steps)]
     halves = min(COLUMN_HALVES, strips)
     wide = columns // halves
     groups = [range(k * strips // halves, (k + 1) * strips // halves) for k in range(halves)]
+    taken = pl.pallas_call(
+        functools.partial(take_kernel, chips, turn),
+        out_shape=tuple(
+            jax.ShapeDtypeStruct((len(group), features, LANES), bf16)
+            for group in groups
+            for _ in steps
+        ),
+        in_specs=anywhere(1),
+        out_specs=tuple(in_vmem(halves * len(steps))),
+        scratch_shapes=[pltpu.SemaphoreType.DMA((len(steps) * strips,))],
+        compiler_params=pltpu.CompilerParams(vmem_limit_bytes=TAKE_VMEM_BYTES),
+    )(frozen_key_value)
+    mine = []
+    for half in range(halves):
+        sent_half = taken[half * len(steps) : (half + 1) * len(steps)]
+        if half > 0:
+            sent_half, _ = lax.optimization_barrier((sent_half, mine[-1]))
+        mine.append([to_chip(value, step) for value, step in zip(sent_half, steps)])
 
     hidden, up_sent, _ = lax.optimization_barrier(
         (prompt_hidden_input, up_gradient[0], taken)
@@ -391,19 +403,21 @@
     other_b = [to_chip(packed_b, step) for step in steps]
 
     outside = [[] for _ in range(strips)]
-    for value in mine:
-        value, _ = lax.optimization_barrier((value, sent))
-        split = pl.pallas_call(
-            split_kernel,
-            out_shape=(jax.ShapeDtypeStruct((features, LANES), bf16),) * strips,
-            in_specs=in_vmem(1),
-            out_specs=tuple(in_vmem(strips)),
-            compiler_params=params(),
-        )(value)
-        for strip in range(strips):
-            pairs = [(i, i ^ turn[strip]) for i in range(n_dp)]
-            outside[strip].append((split[strip], lax.ppermute(split[strip], "dp", pairs)))
-
+    for half, group in enumerate(groups):
+        for value in mine[half]:
+            value, _ = lax.optimization_barrier((value, sent if half == 0 else other_b))
+            split = pl.pallas_call(
+                split_kernel,
+                out_shape=(jax.ShapeDtypeStruct((features, LANES), bf16),) * len(group),
+                in_specs=in_vmem(1),
+                out_specs=tuple(in_vmem(len(group))),
+                compiler_params=params(),
+            )(value)
+            for piece, strip in zip(split, group):
+                pairs = [(i, i ^ turn[strip]) for i in range(n_dp)]
+                outside[strip].append((piece, lax.ppermute(piece, "dp", pairs)))
+
+    squares, _ = lax.optimization_barrier((squares, other_b))
     squares = squares + sum(to_chip(squares, step) for step in steps)
     inv_rms = jnp.broadcast_to(lax.rsqrt(squares / width + 1e-06)[:, None], (tokens, LANES))
 
@@ -435,7 +449,7 @@
             )(numbers, own_f, sibling_f, other_b[step - 1], *blocks)
             for k, rows in enumerate(token_slices):
                 if k > 0:
-                    weights, _ = lax.optimization_barrier((weights, (product, squares)))
+                    weights, _ = lax.optimization_barrier((weights, product))
                 product = jnp.dot(x[rows], weights, preferred_element_type=f32).astype(bf16)
                 received.setdefault((k, half), []).append(to_chip(product, chips - step))
 

time: 128 us -> 88.8 us (0.69)
  Pallas kernels: 61.9 us -> 23 us
  waiting for transfers between devices: 27.9 us -> 30.5 us
    pallas_call x1, Pallas kernels: 41.6 us -> 2.56 us  [body(): pl.pallas_call(functools.partial(take_kernel, chips, turn), out_shape=tup...]
    ppermute x7 -> x8, waiting for transfers between devices: 12.5 us -> 15.7 us  [to_chip(): return lax.ppermute(value, 'tensor', pairs)]
    ppermute x7 -> x8, starting transfers between devices: 8.79 us -> 8.84 us  [to_chip(): return lax.ppermute(value, 'tensor', pairs)]
  transfers between devices with their start and end apart: 16 -> 17, of which waited for: 10 -> 9; matrix products, arithmetic and copies ran while one was open for 5% -> 8% of each run, Pallas kernels for 15% -> 22%
where the time goes in v7:
time: 88.8 us; the launch traced here: 88.5 us
  waiting for transfers between devices  30.5 us (34%)
  starting transfers between devices  24.5 us (28%)
  Pallas kernels  23 us (26%)
  matrix products  6.11 us (7%)
  local copies, waits for them, and re-layouts  3.31 us (4%)
  between operations  0.9 us (1%)
    ppermute x8, waiting for transfers between devices, to_chip(): return lax.ppermute(value, 'tensor', pairs)  15.7 us
    all_to_all x1, waiting for transfers between devices, body(): exchanged = lax.all_to_all(packed, 'dp', 0, 0, tiled=True)  10.8 us
    ppermute x8, starting transfers between devices, to_chip(): return lax.ppermute(value, 'tensor', pairs)  8.84 us
    all_to_all x1, starting transfers between devices, body(): exchanged = lax.all_to_all(packed, 'dp', 0, 0, tiled=True)  6.86 us
    pallas_call x1, Pallas kernels, body(): pl.pallas_call(prepare_kernel, out_shape=(jax.ShapeDtypeStruct((tokens, C...  6.46 us
    dot_general x4, matrix products, body(): product = jnp.dot(x[rows], weights, preferred_element_type=f32).astype(bf16)  6.11 us
    pallas_call x1, Pallas kernels, body(): pl.pallas_call(functools.partial(own_kernel, (scale, parts, up_rows, rang...  5.61 us
    ppermute x4, starting transfers between devices, body(): outside[strip].append((piece, lax.ppermute(piece, 'dp', pairs)))  4.38 us
  transfers between devices with their start and end apart: 17, of which 9 were waited for; matrix products, arithmetic and copies ran while one was open for 8% of the time, Pallas kernels for 22%

profile of v7, /device:TPU:0, one launch (start us, length us, event | category | flops | bytes accessed | tf_op | source)
XLA Modules:
  0.0 88.5 jit_solution(12682067384676622259)
XLA Ops:
  0.6 0.0 copy-start.5
  0.6 0.0 copy-start.1
  0.7 0.0 copy-start.4
  0.7 0.0 copy-start.2
  0.7 0.0 copy-start.3
  0.7 0.0 copy-start.6
  0.7 2.6 %shard_map.130 = (bf16[2,1280,128]{2,1,0:T(8,128)(2,1)}, bf16[2,1280,128]{2,1,0:T(8,128)(2,1)}) custom-call(bf16[5120,512]{1,0:T(8,128)(2,1)} %sibling_block.1), custom_call_target="tpu_custom_call" | custom-call | tf_op jit(solution)/shard_map/pallas_call | solution.py:309
  3.3 0.0 copy-start.9
  3.3 0.5 collective-permute-start
  3.8 0.9 %shard_map.131 = bf16[8,192,128]{2,1,0:T(8,128)(2,1)} custom-call(f32[128,1280]{1,0:T(8,128)S(1)} %bitcast.33, f32[64,512]{1,0:T(8,128)S(1)} %bitcast.37), custom_call_target="tpu_custom_call" | custom-call | tf_op jit(solution)/shard_map/pallas_call | solution.py:358
  4.7 6.9 %all-to-all-start = ((bf16[8,192,128]{2,1,0:T(8,128)(2,1)}), bf16[8,192,128]{2,1,0:T(8,128)(2,1)S(1)}, u32[]{:S(2)}, u32[]{:S(2)}) async-start(bf16[8,192,128]{2,1,0:T(8,128)(2,1)} %shard_map.131), calls=%async_computation | async-start | bytes 786432 | tf_op jit(solution)/shard_map/all_to_all | solution.py:365
  11.6 1.5 %collective-permute-start.4 = (bf16[2,1280,128]{2,1,0:T(8,128)(2,1)}, bf16[2,1280,128]{2,1,0:T(8,128)(2,1)S(1)}, u32[]{:S(2)}, u32[]{:S(2)}) collective-permute-start(bf16[2,1280,128]{2,1,0:T(8,128)(2,1)} %get-tuple-element.29), channel_id=1, source_target_pairs={{0,2},{1,3},{2,0},{3,1},{4,6},{5,7},{6,4},{7,5},{8,10},{9,11},{10,... | collective-permute-start | bytes 1966088 | tf_op jit(solution)/shard_map/ppermute | solution.py:298
  13.1 10.8 %all-to-all-done.grad_ref = bf16[8,192,128]{2,1,0:T(8,128)(2,1)S(1)} async-done(((bf16[8,192,128]{2,1,0:T(8,128)(2,1)}), bf16[8,192,128]{2,1,0:T(8,128)(2,1)S(1)}, u32[]{:S(2)}, u32[]{:S(2)}) %all-to-all-start) | async-done | bytes 393248 | tf_op jit(solution)/shard_map/all_to_all | solution.py:365
  24.0 1.5 %shard_map.132 = (f32[3,128,160]{2,1,0:T(8,128)}, f32[3,8,512]{2,1,0:T(8,128)}, bf16[8,192,128]{2,1,0:T(8,128)(2,1)}) custom-call(s32[1]{0:T(128)} %bitcast.replica, bf16[8,192,128]{2,1,0:T(8,128)(2,1)S(1)} %all-to-all-done.grad_ref, f32[128,1280]{1,0:T(8,128)S(1)} %bitcast.34, f32[128,1280]{1,0:T(8,128)S(1)} %bitcast.35, f32[128,1280]{1,0:T(8,128)S(1)} %bitcast.36, ...), custom_call_target="tpu_custom_call" | custom-call | tf_op jit(solution)/shard_map/pallas_call | solution.py:367
  25.5 3.6 %all-to-all-start.1 = ((bf16[8,192,128]{2,1,0:T(8,128)(2,1)}), bf16[8,192,128]{2,1,0:T(8,128)(2,1)S(1)}, u32[]{:S(2)}, u32[]{:S(2)}) async-start(bf16[8,192,128]{2,1,0:T(8,128)(2,1)} %get-tuple-element.34), calls=%async_computation.1 | async-start | bytes 786432 | tf_op jit(solution)/shard_map/all_to_all | solution.py:391
  29.1 0.0 collective-permute-done.4.in_ref
  29.1 1.6 %collective-permute-start.7 = (bf16[2,1280,128]{2,1,0:T(8,128)(2,1)}, bf16[2,1280,128]{2,1,0:T(8,128)(2,1)S(1)}, u32[]{:S(2)}, u32[]{:S(2)}) collective-permute-start(bf16[2,1280,128]{2,1,0:T(8,128)(2,1)} %get-tuple-element.45), channel_id=1, source_target_pairs={{0,2},{1,3},{2,0},{3,1},{4,6},{5,7},{6,4},{7,5},{8,10},{9,11},{10,... | collective-permute-start | bytes 1966088 | tf_op jit(solution)/shard_map/ppermute | solution.py:298
  30.7 0.0 collective-permute-start.1
  30.7 1.2 %collective-permute-done.1.sibling_gain = f32[1,1280]{1,0:T(1,128)S(1)} collective-permute-done((f32[1,1280]{1,0:T(1,128)S(1)}, f32[1,1280]{1,0:T(1,128)S(1)}, u32[]{:S(2)}, u32[]{:S(2)}) %collective-permute-start.1) | collective-permute-done | bytes 5152 | tf_op jit(solution)/shard_map/ppermute | solution.py:290
  31.9 0.0 collective-permute-done.sibling_ref
  31.9 6.5 %shard_map.133 = (bf16[1280,2560]{1,0:T(8,128)(2,1)S(1)}, f32[1280,128]{1,0:T(8,128)S(1)}) custom-call(bf16[1280,1280]{1,0:T(8,128)(2,1)} %own_ref, bf16[1280,1280]{1,0:T(8,128)(2,1)} %collective-permute-done.sibling_ref, f32[1,1280]{1,0:T(1,128)S(1)} %broadcast_in_dim.13.own_gain, f32[1,1280]{1,0:T(1,128)S(1)} %collective-permute-done.1.sibling_gain), custom_call_target="tpu_custom_call" | custom-call | tf_op jit(solution)/shard_map/pallas_call | solution.py:332
  38.3 2.8 %copy-done = bf16[1280,2560]{1,0:T(8,128)(2,1)} copy-done((bf16[1280,2560]{1,0:T(8,128)(2,1)}, bf16[1280,2560]{1,0:T(8,128)(2,1)S(1)}, u32[]{:S(2)}) %copy-start) | copy-done | bytes 6553624
  41.1 0.2 slice_reduce_fusion
  41.4 0.0 all-to-all-done.1.in_ref.own_f
  41.4 0.2 collective-permute-start.2
  41.6 2.0 %collective-permute-start.5 = (bf16[1280,128]{1,0:T(8,128)(2,1)S(1)}, bf16[1280,128]{1,0:T(8,128)(2,1)S(1)}, u32[]{:S(2)}, u32[]{:S(2)}) collective-permute-start(bf16[1280,128]{1,0:T(8,128)(2,1)S(1)} %get-tuple-element.41.refs_0_), channel_id=1, source_target_pairs={{0,4},{4,0},{8,12},{12,8},{16,20},{20,16},{24,28},{28,24},{1,5},{5... | collective-permute-start | bytes 983048 | tf_op jit(solution)/shard_map/ppermute | solution.py:418
  43.7 1.5 %collective-permute-start.6 = (bf16[1280,128]{1,0:T(8,128)(2,1)S(1)}, bf16[1280,128]{1,0:T(8,128)(2,1)S(1)}, u32[]{:S(2)}, u32[]{:S(2)}) collective-permute-start(bf16[1280,128]{1,0:T(8,128)(2,1)S(1)} %get-tuple-element.42.refs_2_), channel_id=1, source_target_pairs={{0,8},{4,12},{8,0},{12,4},{16,24},{20,28},{24,16},{28,20},{1,9},{5... | collective-permute-start | bytes 983048 | tf_op jit(solution)/shard_map/ppermute | solution.py:418
  45.1 0.1 pad_add_fusion.1.numbers
  45.2 0.6 collective-permute-start.3
  45.8 0.1 pad_add_fusion.numbers
  45.9 0.0 collective-permute-done.7.in_ref
  45.9 3.7 %collective-permute-done.3.b_ref = bf16[8,32,128]{2,1,0:T(8,128)(2,1)S(1)} collective-permute-done((bf16[8,32,128]{2,1,0:T(8,128)(2,1)S(1)}, bf16[8,32,128]{2,1,0:T(8,128)(2,1)S(1)}, u32[]{:S(2)}, u32[]{:S(2)}) %collective-permute-start.3) | collective-permute-done | bytes 65568 | tf_op jit(solution)/shard_map/ppermute | solution.py:298
  49.6 0.6 collective-permute-start.8
  50.2 0.3 collective-permute-start.9
  50.5 1.8 %collective-permute-done.5.refs_1_ = bf16[1280,128]{1,0:T(8,128)(2,1)S(1)} collective-permute-done((bf16[1280,128]{1,0:T(8,128)(2,1)S(1)}, bf16[1280,128]{1,0:T(8,128)(2,1)S(1)}, u32[]{:S(2)}, u32[]{:S(2)}) %collective-permute-start.5) | collective-permute-done | bytes 327712 | tf_op jit(solution)/shard_map/ppermute | solution.py:418
  52.2 0.9 %collective-permute-start.11 = (f32[1280]{0:T(1024)S(1)}, f32[1280]{0:T(1024)S(1)}, u32[]{:S(2)}, u32[]{:S(2)}) collective-permute-start(f32[1280]{0:T(1024)S(1)} %slice_reduce_fusion), channel_id=1, source_target_pairs={{0,2},{1,3},{2,0},{3,1},{4,6},{5,7},{6,4},{7,5},{8,10},{9,11},{10,... | collective-permute-start | bytes 15368 | tf_op jit(solution)/shard_map/ppermute | solution.py:298
  53.1 1.1 %collective-permute-done.6.refs_3_ = bf16[1280,128]{1,0:T(8,128)(2,1)S(1)} collective-permute-done((bf16[1280,128]{1,0:T(8,128)(2,1)S(1)}, bf16[1280,128]{1,0:T(8,128)(2,1)S(1)}, u32[]{:S(2)}, u32[]{:S(2)}) %collective-permute-start.6) | collective-permute-done | bytes 327712 | tf_op jit(solution)/shard_map/ppermute | solution.py:418
  54.2 0.0 collective-permute-done.2.sibling_f
  54.2 1.1 %shard_map.136 = bf16[2560,256]{1,0:T(8,128)(2,1)S(1)} custom-call(s32[3]{0:T(128)S(1)} %pad_add_fusion.1.numbers, bf16[8,192,128]{2,1,0:T(8,128)(2,1)S(1)} %all-to-all-done.1.in_ref.own_f, bf16[8,192,128]{2,1,0:T(8,128)(2,1)S(1)} %collective-permute-done.2.sibling_f, bf16[8,32,128]{2,1,0:T(8,128)(2,1)S(1)} %collective-permute-done.3.b_ref, ...), custom_call_target="tpu_custom_call" | custom-call | tf_op jit(solution)/shard_map/pallas_call | solution.py:443
  55.4 0.0 slice-start.3
  55.4 3.1 %fusion.14 = bf16[640,256]{1,0:T(8,128)(2,1)S(1)} fusion(bf16[2560,256]{1,0:T(8,128)(2,1)S(1)} %shard_map.136, bf16[1280,2560]{1,0:T(8,128)(2,1)} %copy-done), kind=kOutput, calls=%fused_computation.10 | convolution fusion | flops 839024640 | bytes 4915200 | tf_op jit(solution)/shard_map/dot_general | solution.py:453
  58.5 0.6 collective-permute-start.10
  59.1 1.0 %fusion.8 = bf16[640,256]{1,0:T(8,128)(2,1)S(1)} fusion(bf16[2560,256]{1,0:T(8,128)(2,1)S(1)} %shard_map.136, bf16[1280,2560]{1,0:T(8,128)(2,1)S(1)} %bitcast.32), kind=kOutput, calls=%fused_computation.8 | convolution fusion | flops 839024640 | bytes 4915200 | tf_op jit(solution)/shard_map/dot_general | solution.py:453
  60.1 1.5 %collective-permute-start.14 = (bf16[640,256]{1,0:T(8,128)(2,1)S(1)}, bf16[640,256]{1,0:T(8,128)(2,1)S(1)}, u32[]{:S(2)}, u32[]{:S(2)}) collective-permute-start(bf16[640,256]{1,0:T(8,128)(2,1)S(1)} %fusion.8), channel_id=1, source_target_pairs={{0,2},{1,3},{2,0},{3,1},{4,6},{5,7},{6,4},{7,5},{8,10},{9,11},{10,... | collective-permute-start | bytes 983048 | tf_op jit(solution)/shard_map/ppermute | solution.py:298
  61.7 0.0 collective-permute-done.8.refs_1_
  61.7 0.0 collective-permute-done.9.refs_3_
  61.7 1.2 %shard_map.138 = bf16[2560,256]{1,0:T(8,128)(2,1)S(1)} custom-call(s32[3]{0:T(128)S(1)} %pad_add_fusion.1.numbers, bf16[8,192,128]{2,1,0:T(8,128)(2,1)S(1)} %all-to-all-done.1.in_ref.own_f, bf16[8,192,128]{2,1,0:T(8,128)(2,1)S(1)} %collective-permute-done.2.sibling_f, bf16[8,32,128]{2,1,0:T(8,128)(2,1)S(1)} %collective-permute-done.3.b_ref, ...), custom_call_target="tpu_custom_call" | custom-call | tf_op jit(solution)/shard_map/pallas_call | solution.py:443
  62.8 0.0 slice-start
  62.9 1.0 %fusion.17 = bf16[640,256]{1,0:T(8,128)(2,1)S(1)} fusion(bf16[2560,256]{1,0:T(8,128)(2,1)S(1)} %shard_map.138, bf16[1280,2560]{1,0:T(8,128)(2,1)S(1)} %bitcast.32), kind=kOutput, calls=%fused_computation.11 | convolution fusion | flops 839024640 | bytes 4915200 | tf_op jit(solution)/shard_map/dot_general | solution.py:453
  63.9 0.0 slice-start.1
  63.9 0.6 collective-permute-start.13
  64.5 1.0 %fusion.11 = bf16[640,256]{1,0:T(8,128)(2,1)S(1)} fusion(bf16[2560,256]{1,0:T(8,128)(2,1)S(1)} %shard_map.138, bf16[1280,2560]{1,0:T(8,128)(2,1)S(1)} %bitcast.32), kind=kOutput, calls=%fused_computation.9 | convolution fusion | flops 839024640 | bytes 4915200 | tf_op jit(solution)/shard_map/dot_general | solution.py:453
  65.5 1.5 %collective-permute-start.12 = (bf16[640,256]{1,0:T(8,128)(2,1)S(1)}, bf16[640,256]{1,0:T(8,128)(2,1)S(1)}, u32[]{:S(2)}, u32[]{:S(2)}) collective-permute-start(bf16[640,256]{1,0:T(8,128)(2,1)S(1)} %fusion.11), channel_id=1, source_target_pairs={{0,2},{1,3},{2,0},{3,1},{4,6},{5,7},{6,4},{7,5},{8,10},{9,11},{10,... | collective-permute-start | bytes 983048 | tf_op jit(solution)/shard_map/ppermute | solution.py:298
  67.1 0.0 collective-permute-done.11
  67.1 2.1 %collective-permute-done.10.refs_0_ = bf16[640,256]{1,0:T(8,128)(2,1)S(1)} collective-permute-done((bf16[640,256]{1,0:T(8,128)(2,1)S(1)}, bf16[640,256]{1,0:T(8,128)(2,1)S(1)}, u32[]{:S(2)}, u32[]{:S(2)}) %collective-permute-start.10) | collective-permute-done | bytes 327712 | tf_op jit(solution)/shard_map/ppermute | solution.py:298
  69.2 5.6 %shard_map.139 = (f32[1280,256]{1,0:T(8,128)S(1)}, f32[1280,256]{1,0:T(8,128)S(1)}) custom-call(s32[3]{0:T(128)S(1)} %pad_add_fusion.numbers, bf16[5120,512]{1,0:T(8,128)(2,1)S(1)} %bitcast.30, bf16[5120,512]{1,0:T(8,128)(2,1)S(1)} %bitcast.30, bf16[8,192,128]{2,1,0:T(8,128)(2,1)S(1)} %all-to-all-done.1.in_ref.own_f, ...), custom_call_target="tpu_custom_call" | custom-call | flops 3355443200 | bytes 6553600 | tf_op jit(solution)/shard_map/pallas_call | solution.py:458
  74.8 0.2 broadcast_in_dim.14.inv
  75.1 0.9 %shard_map.140.refs_1_ = bf16[1280,512]{1,0:T(8,128)(2,1)} custom-call(f32[1280,256]{1,0:T(8,128)S(1)} %get-tuple-element.54.own, f32[1280,128]{1,0:T(8,128)S(1)} %broadcast_in_dim.14.inv, bf16[640,256]{1,0:T(8,128)(2,1)S(1)} %collective-permute-done.10.refs_0_), custom_call_target="tpu_custom_call" | custom-call | tf_op jit(solution)/shard_map/pallas_call | solution.py:247
  76.0 0.3 collective-permute-done.14.refs_0_
  76.2 0.9 shard_map.141.refs_1_
  77.1 6.1 %collective-permute-done.13.refs_0_ = bf16[640,256]{1,0:T(8,128)(2,1)S(1)} collective-permute-done((bf16[640,256]{1,0:T(8,128)(2,1)S(1)}, bf16[640,256]{1,0:T(8,128)(2,1)S(1)}, u32[]{:S(2)}, u32[]{:S(2)}) %collective-permute-start.13) | collective-permute-done | bytes 327712 | tf_op jit(solution)/shard_map/ppermute | solution.py:298
  83.3 0.9 shard_map.142.refs_1_
  84.1 3.4 %collective-permute-done.12.refs_0_ = bf16[640,256]{1,0:T(8,128)(2,1)S(1)} collective-permute-done((bf16[640,256]{1,0:T(8,128)(2,1)S(1)}, bf16[640,256]{1,0:T(8,128)(2,1)S(1)}, u32[]{:S(2)}, u32[]{:S(2)}) %collective-permute-start.12) | collective-permute-done | bytes 327712 | tf_op jit(solution)/shard_map/ppermute | solution.py:298
  87.6 0.9 shard_map.143
  (24 shorter events, 0.1 us)
Async XLA Ops:
  0.6 3.2 %copy-start.5 = (f32[1,64,512]{2,1,0:T(8,128)S(1)}, f32[1,64,512]{2,1,0:T(8,128)}, u32[]{:S(2)}) copy-start(f32[1,64,512]{2,1,0:T(8,128)} %param.21) | copy-start | bytes 393220
  0.6 3.2 %copy-start.1 = (f32[1,1280,2,64]{1,3,2,0:T(8,128)S(1)}, f32[1,1280,2,64]{1,3,2,0:T(8,128)}, u32[]{:S(2)}) copy-start(f32[1,1280,2,64]{1,3,2,0:T(8,128)} %param.20) | copy-start | bytes 1966084
  0.7 23.3 %copy-start.4 = (f32[1280,2,64]{0,2,1:T(8,128)S(1)}, f32[1280,2,64]{0,2,1:T(8,128)}, u32[]{:S(2)}) copy-start(f32[1280,2,64]{0,2,1:T(8,128)} %param.16) | copy-start | bytes 1966084
  0.7 23.3 %copy-start.2 = (f32[1280,2,64]{0,2,1:T(8,128)S(1)}, f32[1280,2,64]{0,2,1:T(8,128)}, u32[]{:S(2)}) copy-start(f32[1280,2,64]{0,2,1:T(8,128)} %param.14) | copy-start | bytes 1966084
  0.7 23.3 %copy-start.3 = (f32[1280,2,64]{0,2,1:T(8,128)S(1)}, f32[1280,2,64]{0,2,1:T(8,128)}, u32[]{:S(2)}) copy-start(f32[1280,2,64]{0,2,1:T(8,128)} %param.15) | copy-start | bytes 1966084
  0.7 23.3 %copy-start.6 = (f32[64,512]{1,0:T(8,128)S(1)}, f32[64,512]{1,0:T(8,128)}, u32[]{:S(2)}) copy-start(f32[64,512]{1,0:T(8,128)} %refs_3_.1) | copy-start | bytes 393220
  0.7 23.3 %copy-start.7 = (f32[64,512]{1,0:T(8,128)S(1)}, f32[64,512]{1,0:T(8,128)}, u32[]{:S(2)}) copy-start(f32[64,512]{1,0:T(8,128)} %refs_4_.1) | copy-start | bytes 393220
  0.7 23.3 %copy-start.8 = (f32[64,512]{1,0:T(8,128)S(1)}, f32[64,512]{1,0:T(8,128)}, u32[]{:S(2)}) copy-start(f32[64,512]{1,0:T(8,128)} %refs_5_.1) | copy-start | bytes 393220
  3.3 27.4 %copy-start.9 = (f32[1280]{0:T(1024)S(1)}, f32[1280]{0:T(1024)}, u32[]{:S(2)}) copy-start(f32[1280]{0:T(1024)} %param.12) | copy-start | bytes 15364
  3.3 28.6 %collective-permute-start = (bf16[1280,1280]{1,0:T(8,128)(2,1)}, bf16[1280,1280]{1,0:T(8,128)(2,1)}, u32[]{:S(2)}, u32[]{:S(2)}) collective-permute-start(bf16[1280,1280]{1,0:T(8,128)(2,1)} %own_ref), channel_id=1, source_target_pairs={{0,1},{1,0},{2,3},{3,2},{4,5},{5,4},{6,7},{7,6},{8,9},{9,8},{10,11... | collective-permute-start | bytes 9830408 | tf_op jit(solution)/shard_map/ppermute | solution.py:290
  4.7 19.2 %all-to-all-start = ((bf16[8,192,128]{2,1,0:T(8,128)(2,1)}), bf16[8,192,128]{2,1,0:T(8,128)(2,1)S(1)}, u32[]{:S(2)}, u32[]{:S(2)}) async-start(bf16[8,192,128]{2,1,0:T(8,128)(2,1)} %shard_map.131), calls=%async_computation | async-start | bytes 786432 | tf_op jit(solution)/shard_map/all_to_all | solution.py:365
  11.6 17.5 %collective-permute-start.4 = (bf16[2,1280,128]{2,1,0:T(8,128)(2,1)}, bf16[2,1280,128]{2,1,0:T(8,128)(2,1)S(1)}, u32[]{:S(2)}, u32[]{:S(2)}) collective-permute-start(bf16[2,1280,128]{2,1,0:T(8,128)(2,1)} %get-tuple-element.29), channel_id=1, source_target_pairs={{0,2},{1,3},{2,0},{3,1},{4,6},{5,7},{6,4},{7,5},{8,10},{9,11},{10,... | collective-permute-start | bytes 1966088 | tf_op jit(solution)/shard_map/ppermute | solution.py:298
  25.5 15.9 %all-to-all-start.1 = ((bf16[8,192,128]{2,1,0:T(8,128)(2,1)}), bf16[8,192,128]{2,1,0:T(8,128)(2,1)S(1)}, u32[]{:S(2)}, u32[]{:S(2)}) async-start(bf16[8,192,128]{2,1,0:T(8,128)(2,1)} %get-tuple-element.34), calls=%async_computation.1 | async-start | bytes 786432 | tf_op jit(solution)/shard_map/all_to_all | solution.py:391
  29.1 16.7 %collective-permute-start.7 = (bf16[2,1280,128]{2,1,0:T(8,128)(2,1)}, bf16[2,1280,128]{2,1,0:T(8,128)(2,1)S(1)}, u32[]{:S(2)}, u32[]{:S(2)}) collective-permute-start(bf16[2,1280,128]{2,1,0:T(8,128)(2,1)} %get-tuple-element.45), channel_id=1, source_target_pairs={{0,2},{1,3},{2,0},{3,1},{4,6},{5,7},{6,4},{7,5},{8,10},{9,11},{10,... | collective-permute-start | bytes 1966088 | tf_op jit(solution)/shard_map/ppermute | solution.py:298
  30.7 1.2 %collective-permute-start.1 = (f32[1,1280]{1,0:T(1,128)S(1)}, f32[1,1280]{1,0:T(1,128)S(1)}, u32[]{:S(2)}, u32[]{:S(2)}) collective-permute-start(f32[1,1280]{1,0:T(1,128)S(1)} %broadcast_in_dim.13.own_gain), channel_id=1, source_target_pairs={{0,1},{1,0},{2,3},{3,2},{4,5},{5,4},{6,7},{7,6},{8,9},{9,8},{10,11... | collective-permute-start | bytes 15368 | tf_op jit(solution)/shard_map/ppermute | solution.py:290
  38.3 2.8 %copy-start = (bf16[1280,2560]{1,0:T(8,128)(2,1)}, bf16[1280,2560]{1,0:T(8,128)(2,1)S(1)}, u32[]{:S(2)}) copy-start(bf16[1280,2560]{1,0:T(8,128)(2,1)S(1)} %get-tuple-element.38.x) | copy-start | bytes 19660804
  41.4 12.9 %collective-permute-start.2 = (bf16[8,192,128]{2,1,0:T(8,128)(2,1)S(1)}, bf16[8,192,128]{2,1,0:T(8,128)(2,1)S(1)}, u32[]{:S(2)}, u32[]{:S(2)}) collective-permute-start(bf16[8,192,128]{2,1,0:T(8,128)(2,1)S(1)} %all-to-all-done.1.in_ref.own_f), channel_id=1, source_target_pairs={{0,1},{1,0},{2,3},{3,2},{4,5},{5,4},{6,7},{7,6},{8,9},{9,8},{10,11... | collective-permute-start | bytes 1179656 | tf_op jit(solution)/shard_map/ppermute | solution.py:290
  41.6 10.6 %collective-permute-start.5 = (bf16[1280,128]{1,0:T(8,128)(2,1)S(1)}, bf16[1280,128]{1,0:T(8,128)(2,1)S(1)}, u32[]{:S(2)}, u32[]{:S(2)}) collective-permute-start(bf16[1280,128]{1,0:T(8,128)(2,1)S(1)} %get-tuple-element.41.refs_0_), channel_id=1, source_target_pairs={{0,4},{4,0},{8,12},{12,8},{16,20},{20,16},{24,28},{28,24},{1,5},{5... | collective-permute-start | bytes 983048 | tf_op jit(solution)/shard_map/ppermute | solution.py:418
  43.7 10.6 %collective-permute-start.6 = (bf16[1280,128]{1,0:T(8,128)(2,1)S(1)}, bf16[1280,128]{1,0:T(8,128)(2,1)S(1)}, u32[]{:S(2)}, u32[]{:S(2)}) collective-permute-start(bf16[1280,128]{1,0:T(8,128)(2,1)S(1)} %get-tuple-element.42.refs_2_), channel_id=1, source_target_pairs={{0,8},{4,12},{8,0},{12,4},{16,24},{20,28},{24,16},{28,20},{1,9},{5... | collective-permute-start | bytes 983048 | tf_op jit(solution)/shard_map/ppermute | solution.py:418
  45.2 4.3 %collective-permute-start.3 = (bf16[8,32,128]{2,1,0:T(8,128)(2,1)S(1)}, bf16[8,32,128]{2,1,0:T(8,128)(2,1)S(1)}, u32[]{:S(2)}, u32[]{:S(2)}) collective-permute-start(bf16[8,32,128]{2,1,0:T(8,128)(2,1)S(1)} %shard_map.134), channel_id=1, source_target_pairs={{0,2},{1,3},{2,0},{3,1},{4,6},{5,7},{6,4},{7,5},{8,10},{9,11},{10,... | collective-permute-start | bytes 196616 | tf_op jit(solution)/shard_map/ppermute | solution.py:298
  49.6 12.1 %collective-permute-start.8 = (bf16[1280,128]{1,0:T(8,128)(2,1)S(1)}, bf16[1280,128]{1,0:T(8,128)(2,1)S(1)}, u32[]{:S(2)}, u32[]{:S(2)}) collective-permute-start(bf16[1280,128]{1,0:T(8,128)(2,1)S(1)} %get-tuple-element.47.refs_0_), channel_id=1, source_target_pairs={{0,4},{4,0},{8,12},{12,8},{16,20},{20,16},{24,28},{28,24},{1,5},{5... | collective-permute-start | bytes 983048 | tf_op jit(solution)/shard_map/ppermute | solution.py:418
  50.2 11.5 %collective-permute-start.9 = (bf16[1280,128]{1,0:T(8,128)(2,1)S(1)}, bf16[1280,128]{1,0:T(8,128)(2,1)S(1)}, u32[]{:S(2)}, u32[]{:S(2)}) collective-permute-start(bf16[1280,128]{1,0:T(8,128)(2,1)S(1)} %get-tuple-element.48.refs_2_), channel_id=1, source_target_pairs={{0,8},{4,12},{8,0},{12,4},{16,24},{20,28},{24,16},{28,20},{1,9},{5... | collective-permute-start | bytes 983048 | tf_op jit(solution)/shard_map/ppermute | solution.py:418
  52.2 14.8 %collective-permute-start.11 = (f32[1280]{0:T(1024)S(1)}, f32[1280]{0:T(1024)S(1)}, u32[]{:S(2)}, u32[]{:S(2)}) collective-permute-start(f32[1280]{0:T(1024)S(1)} %slice_reduce_fusion), channel_id=1, source_target_pairs={{0,2},{1,3},{2,0},{3,1},{4,6},{5,7},{6,4},{7,5},{8,10},{9,11},{10,... | collective-permute-start | bytes 15368 | tf_op jit(solution)/shard_map/ppermute | solution.py:298
  54.2 4.9 %slice-start.2 = ((s8[6553600]{0:T(1024)(128)(4,1)}), s8[4194304]{0:T(1024)(128)(4,1)S(1)}, s32[]{:S(2)}) async-start(s8[6553600]{0:T(1024)(128)(4,1)} %bitcast.31), calls=%async_computation.4 | async-start | bytes 8388608
  55.4 3.7 %slice-start.3 = ((s8[6553600]{0:T(1024)(128)(4,1)}), s8[2359296]{0:T(1024)(128)(4,1)S(1)}, s32[]{:S(2)}) async-start(s8[6553600]{0:T(1024)(128)(4,1)} %bitcast.31), calls=%async_computation.5 | async-start | bytes 4718592
  58.5 10.7 %collective-permute-start.10 = (bf16[640,256]{1,0:T(8,128)(2,1)S(1)}, bf16[640,256]{1,0:T(8,128)(2,1)S(1)}, u32[]{:S(2)}, u32[]{:S(2)}) collective-permute-start(bf16[640,256]{1,0:T(8,128)(2,1)S(1)} %fusion.14), channel_id=1, source_target_pairs={{0,2},{1,3},{2,0},{3,1},{4,6},{5,7},{6,4},{7,5},{8,10},{9,11},{10,... | collective-permute-start | bytes 983048 | tf_op jit(solution)/shard_map/ppermute | solution.py:298
  60.1 16.1 %collective-permute-start.14 = (bf16[640,256]{1,0:T(8,128)(2,1)S(1)}, bf16[640,256]{1,0:T(8,128)(2,1)S(1)}, u32[]{:S(2)}, u32[]{:S(2)}) collective-permute-start(bf16[640,256]{1,0:T(8,128)(2,1)S(1)} %fusion.8), channel_id=1, source_target_pairs={{0,2},{1,3},{2,0},{3,1},{4,6},{5,7},{6,4},{7,5},{8,10},{9,11},{10,... | collective-permute-start | bytes 983048 | tf_op jit(solution)/shard_map/ppermute | solution.py:298
  62.8 6.4 %slice-start = ((s8[5242880]{0:T(1024)(128)(4,1)}), s8[4194304]{0:T(1024)(128)(4,1)S(1)}, s32[]{:S(2)}) async-start(s8[5242880]{0:T(1024)(128)(4,1)} %bitcast.29), calls=%async_computation.2 | async-start | bytes 8388608
  63.9 5.3 %slice-start.1 = ((s8[5242880]{0:T(1024)(128)(4,1)}), s8[1048576]{0:T(1024)(128)(4,1)S(1)}, s32[]{:S(2)}) async-start(s8[5242880]{0:T(1024)(128)(4,1)} %bitcast.29), calls=%async_computation.3 | async-start | bytes 2097152
  63.9 19.4 %collective-permute-start.13 = (bf16[640,256]{1,0:T(8,128)(2,1)S(1)}, bf16[640,256]{1,0:T(8,128)(2,1)S(1)}, u32[]{:S(2)}, u32[]{:S(2)}) collective-permute-start(bf16[640,256]{1,0:T(8,128)(2,1)S(1)} %fusion.17), channel_id=1, source_target_pairs={{0,2},{1,3},{2,0},{3,1},{4,6},{5,7},{6,4},{7,5},{8,10},{9,11},{10,... | collective-permute-start | bytes 983048 | tf_op jit(solution)/shard_map/ppermute | solution.py:298
  65.5 22.1 %collective-permute-start.12 = (bf16[640,256]{1,0:T(8,128)(2,1)S(1)}, bf16[640,256]{1,0:T(8,128)(2,1)S(1)}, u32[]{:S(2)}, u32[]{:S(2)}) collective-permute-start(bf16[640,256]{1,0:T(8,128)(2,1)S(1)} %fusion.11), channel_id=1, source_target_pairs={{0,2},{1,3},{2,0},{3,1},{4,6},{5,7},{6,4},{7,5},{8,10},{9,11},{10,... | collective-permute-start | bytes 983048 | tf_op jit(solution)/shard_map/ppermute | solution.py:298

commit v8 on v7

--- a/solution.py
+++ b/solution.py
@@ -40,7 +40,8 @@
     return pltpu.CompilerParams(vmem_limit_bytes=VMEM_BYTES, **more)
 
 
-def pack_kernel(down_ref, up_ref, out_ref):
+def pack_kernel(down_ref, up_ref, out_ref, mark_ref):
+    mark_ref[...] = jnp.zeros_like(mark_ref)
     shares = out_ref.shape[0]
     down, up = down_ref[...].T, up_ref[...]
     down_rows, up_rows = down.shape[0] // shares, up.shape[0] // shares
@@ -51,7 +52,7 @@
         out_ref[i] = jnp.concatenate(pieces, axis=0).astype(jnp.bfloat16)
 
 
-def take_kernel(chips, turn, weights_ref, *refs):
+def take_kernel(chips, turn, weights_ref, _, *refs):
     outs, sem = refs[:-1], refs[-1]
     features = outs[0].shape[1]
     place, replica = lax.axis_index("tensor"), lax.axis_index("dp")
@@ -78,19 +79,24 @@
         out[...] = in_ref[k]
 
 
-def prepare_kernel(own_ref, sibling_ref, own_gain, sibling_gain, x_ref, squares_ref):
-    rows, features = own_ref.shape
-    tile = 64 if rows % 64 == 0 else rows
-
-    @pl.loop(0, rows // tile)
-    def _(i):
-        at = pl.ds(pl.multiple_of(i * tile, tile), tile)
-        total = jnp.zeros((tile, 1), jnp.float32)
-        for k, (ref, gain) in enumerate(((own_ref, own_gain), (sibling_ref, sibling_gain))):
-            wide = ref[at, :].astype(jnp.float32)
-            total += jnp.sum(wide * wide, axis=1, keepdims=True)
-            x_ref[at, k * features : (k + 1) * features] = (wide * gain[...]).astype(x_ref.dtype)
-        squares_ref[at, :] = jnp.broadcast_to(total, (tile, LANES))
+def prepare_kernel(own_ref, sibling_ref, own_gain, sibling_gain, squares_ref, *x_refs):
+    features = own_ref.shape[1]
+    rows = x_refs[0].shape[0]
+    tile = 16 if rows % 16 == 0 else rows
+    for k, x_ref in enumerate(x_refs):
+
+        @pl.loop(0, rows // tile, unroll=2)
+        def _(i):
+            to = pl.ds(pl.multiple_of(i * tile, tile), tile)
+            at = pl.ds(pl.multiple_of(k * rows + i * tile, tile), tile)
+            own = own_ref[at, :].astype(jnp.float32)
+            x_ref[to, :features] = (own * own_gain[...]).astype(x_ref.dtype)
+            total = own * own
+            sibling = sibling_ref[at, :].astype(jnp.float32)
+            x_ref[to, features:] = (sibling * sibling_gain[...]).astype(x_ref.dtype)
+            total += sibling * sibling
+            total = jnp.sum(total, axis=1, keepdims=True)
+            squares_ref[at, :] = jnp.broadcast_to(total, (tile, LANES))
 
 
 def tail_kernel(in_ref, out_ref):
@@ -209,22 +215,25 @@
         out[features:, lanes] = merge(static[0], block, sibling_a, b[:, lanes])
 
 
-def own_kernel(static, numbers, own_block, sibling_block, own_f, sibling_f, x, *refs):
-    outs, weights = refs[:-1], refs[-1]
+def own_kernel(static, numbers, own_block, sibling_block, own_f, sibling_f, *refs):
+    xs, outs, weights = refs[: static[4]], refs[static[4] : -1], refs[-1]
     features = own_block.shape[0]
     wide = outs[0].shape[1]
     down_rows = own_f.shape[1] - len(static[3]) * static[2]
-    b = up_factor(static, own_f[:, down_rows:], numbers[2])
+    b = up_factor(static[:4], own_f[:, down_rows:], numbers[2])
     for at, factors, block in ((0, own_f, own_block), (features, sibling_f, sibling_block)):
         weights[at : at + features] = merge(static[0], block[...], factor_a(factors, down_rows), b)
-    tile = tile_of(x.shape[0])
-
-    @pl.loop(0, x.shape[0] // tile)
-    def _(i):
-        rows = pl.ds(pl.multiple_of(i * tile, tile), tile)
-        value = jnp.dot(x[rows, :], weights[...], preferred_element_type=jnp.float32)
-        for k, out in enumerate(outs):
-            out[rows, :] = value[:, k * wide : (k + 1) * wide]
+    for h, x in enumerate(xs):
+        rows = x.shape[0]
+        tile = 128 if rows % 128 == 0 else rows
+
+        @pl.loop(0, rows // tile)
+        def _(i):
+            at = pl.ds(pl.multiple_of(i * tile, tile), tile)
+            to = pl.ds(pl.multiple_of(h * rows + i * tile, tile), tile)
+            value = jnp.dot(x[at, :], weights[...], preferred_element_type=jnp.float32)
+            for k, out in enumerate(outs):
+                out[to, :] = value[:, k * wide : (k + 1) * wide]
 
 
 def finish_kernel(sources, first, own, inv, *refs):
@@ -300,6 +309,28 @@
     def owner(step):
         return CORES * ((chip - step) % chips) + core
 
+    def by_rank(value):
+        return jnp.transpose(value, (1, 2, 0)).reshape(factors, features)
+
+    down_sent = by_rank(down_gradient[0])
+    down_state = [by_rank(v) for v in (down_factor_matrix, down_moment_first, down_moment_second)]
+    up_state = [up_factor_matrix, up_moment_first, up_moment_second]
+    shares = jax.ShapeDtypeStruct((n_dp, packed_rows, LANES), bf16)
+    updated = (
+        jax.ShapeDtypeStruct((3, factors, down_rows), f32),
+        jax.ShapeDtypeStruct((3, up_rows, columns), f32),
+    )
+    window = pl.cdiv(down_rows + LANES, LANES) * LANES
+    aligned = features % LANES == 0 and window <= features
+    aligned = aligned and up_rows % 8 == 0 and down_rows % 16 == 0
+    packed, mark = pl.pallas_call(
+        pack_kernel,
+        out_shape=(shares, jax.ShapeDtypeStruct((8, LANES), f32)),
+        in_specs=in_vmem(2),
+        out_specs=tuple(in_vmem(2)),
+        compiler_params=params(),
+    )(down_sent, up_gradient[0])
+
     turns = [1, 2] if n_dp % 4 == 0 else [1, 1]
     turn = [turns[strip % 2] for strip in range(strips)]
     odds = [replica // k % 2 for k in turn]
@@ -313,55 +344,27 @@
             for group in groups
             for _ in steps
         ),
-        in_specs=anywhere(1),
+        in_specs=anywhere(1) + in_vmem(1),
         out_specs=tuple(in_vmem(halves * len(steps))),
         scratch_shapes=[pltpu.SemaphoreType.DMA((len(steps) * strips,))],
         compiler_params=pltpu.CompilerParams(vmem_limit_bytes=TAKE_VMEM_BYTES),
-    )(frozen_key_value)
-    mine = []
-    for half in range(halves):
-        sent_half = taken[half * len(steps) : (half + 1) * len(steps)]
-        if half > 0:
-            sent_half, _ = lax.optimization_barrier((sent_half, mine[-1]))
-        mine.append([to_chip(value, step) for value, step in zip(sent_half, steps)])
-
-    hidden, up_sent, _ = lax.optimization_barrier(
-        (prompt_hidden_input, up_gradient[0], taken)
-    )
+    )(frozen_key_value, mark)
+    mine = [
+        [to_chip(taken[half * len(steps) + step - 1], step) for step in steps]
+        for half in range(halves)
+    ]
+
     gain = input_norm_gain[None, :]
-    x, squares = pl.pallas_call(
+    squares, *x = pl.pallas_call(
         prepare_kernel,
-        out_shape=(
-            jax.ShapeDtypeStruct((tokens, CORES * features), bf16),
-            jax.ShapeDtypeStruct((tokens, LANES), f32),
-        ),
+        out_shape=(jax.ShapeDtypeStruct((tokens, LANES), f32),)
+        + (jax.ShapeDtypeStruct((tokens // TOKEN_HALVES, CORES * features), bf16),) * TOKEN_HALVES,
         in_specs=in_vmem(4),
-        out_specs=tuple(in_vmem(2)),
+        out_specs=tuple(in_vmem(1 + TOKEN_HALVES)),
         compiler_params=params(),
-    )(hidden, to_sibling(hidden), gain, to_sibling(gain))
+    )(prompt_hidden_input, to_sibling(prompt_hidden_input), gain, to_sibling(gain))
     squares = squares[:, 0]
 
-    def by_rank(value):
-        return jnp.transpose(value, (1, 2, 0)).reshape(factors, features)
-
-    down_sent = by_rank(down_gradient[0])
-    down_state = [by_rank(v) for v in (down_factor_matrix, down_moment_first, down_moment_second)]
-    up_state = [up_factor_matrix, up_moment_first, up_moment_second]
-    shares = jax.ShapeDtypeStruct((n_dp, packed_rows, LANES), bf16)
-    updated = (
-        jax.ShapeDtypeStruct((3, factors, down_rows), f32),
-        jax.ShapeDtypeStruct((3, up_rows, columns), f32),
-    )
-    window = pl.cdiv(down_rows + LANES, LANES) * LANES
-    aligned = features % LANES == 0 and window <= features
-    aligned = aligned and up_rows % 8 == 0 and down_rows % 16 == 0
-    packed = pl.pallas_call(
-        pack_kernel,
-        out_shape=shares,
-        in_specs=in_vmem(2),
-        out_specs=in_vmem(1)[0],
-        compiler_params=params(),
-    )(down_sent, up_sent)
     exchanged = lax.all_to_all(packed, "dp", 0, 0, tiled=True)
     if aligned:
         a_next, b_next, sent = pl.pallas_call(
@@ -391,7 +394,24 @@
     own_f = lax.all_to_all(sent, "dp", 0, 0, tiled=True)
     a_next = jnp.transpose(a_next.reshape(3, parts, rank, down_rows), (0, 3, 1, 2))
 
-    own_f, x, squares = lax.optimization_barrier((own_f, x, squares))
+    outside = [[] for _ in range(strips)]
+
+    def swap_half(half, after):
+        for value in mine[half]:
+            value, _ = lax.optimization_barrier((value, after))
+            split = pl.pallas_call(
+                split_kernel,
+                out_shape=(jax.ShapeDtypeStruct((features, LANES), bf16),) * len(groups[half]),
+                in_specs=in_vmem(1),
+                out_specs=tuple(in_vmem(len(groups[half]))),
+                compiler_params=params(),
+            )(value)
+            for piece, strip in zip(split, groups[half]):
+                pairs = [(i, i ^ turn[strip]) for i in range(n_dp)]
+                outside[strip].append((piece, lax.ppermute(piece, "dp", pairs)))
+
+    swap_half(0, sent)
+    own_f, squares, _ = lax.optimization_barrier((own_f, squares, outside))
     sibling_f = to_sibling(own_f)
     packed_b = pl.pallas_call(
         tail_kernel,
@@ -402,20 +422,8 @@
     )(own_f)
     other_b = [to_chip(packed_b, step) for step in steps]
 
-    outside = [[] for _ in range(strips)]
-    for half, group in enumerate(groups):
-        for value in mine[half]:
-            value, _ = lax.optimization_barrier((value, sent if half == 0 else other_b))
-            split = pl.pallas_call(
-                split_kernel,
-                out_shape=(jax.ShapeDtypeStruct((features, LANES), bf16),) * len(group),
-                in_specs=in_vmem(1),
-                out_specs=tuple(in_vmem(len(group))),
-                compiler_params=params(),
-            )(value)
-            for piece, strip in zip(split, group):
-                pairs = [(i, i ^ turn[strip]) for i in range(n_dp)]
-                outside[strip].append((piece, lax.ppermute(piece, "dp", pairs)))
+    for half in range(1, halves):
+        swap_half(half, other_b)
 
     squares, _ = lax.optimization_barrier((squares, other_b))
     squares = squares + sum(to_chip(squares, step) for step in steps)
@@ -426,19 +434,15 @@
     def part_of(who):
         return who * columns // KEY_VALUE_WIDTH
 
-    token_slices = [
-        slice(k * tokens // TOKEN_HALVES, (k + 1) * tokens // TOKEN_HALVES)
-        for k in range(TOKEN_HALVES)
-    ]
     received = {}
-    product = None
+    products = None
     for half in range(halves):
         group = groups[half]
         for step in steps:
             numbers = [part_of(owner(step))] + [odds[strip] for strip in group]
             numbers = jnp.stack(numbers).astype(jnp.int32)
-            if product is not None:
-                numbers, _ = lax.optimization_barrier((numbers, product))
+            if products is not None:
+                numbers, _ = lax.optimization_barrier((numbers, products))
             blocks = [value for strip in group for value in outside[strip][step - 1]]
             weights = pl.pallas_call(
                 functools.partial(outside_kernel, (scale, parts, up_rows, group)),
@@ -447,16 +451,16 @@
                 out_specs=in_vmem(1)[0],
                 compiler_params=params(),
             )(numbers, own_f, sibling_f, other_b[step - 1], *blocks)
-            for k, rows in enumerate(token_slices):
-                if k > 0:
-                    weights, _ = lax.optimization_barrier((weights, product))
-                product = jnp.dot(x[rows], weights, preferred_element_type=f32).astype(bf16)
+            products = [
+                jnp.dot(rows, weights, preferred_element_type=f32).astype(bf16) for rows in x
+            ]
+            for k, product in enumerate(products):
                 received.setdefault((k, half), []).append(to_chip(product, chips - step))
 
     numbers = jnp.stack([place, place ^ 1, part_of(place)]).astype(jnp.int32)
-    numbers, _ = lax.optimization_barrier((numbers, (product, received[0, 0])))
+    numbers, _ = lax.optimization_barrier((numbers, (products, received[0, 0])))
     totals = pl.pallas_call(
-        functools.partial(own_kernel, (scale, parts, up_rows, range(strips))),
+        functools.partial(own_kernel, (scale, parts, up_rows, range(strips), TOKEN_HALVES)),
         out_shape=(jax.ShapeDtypeStruct((tokens, wide), f32),) * halves,
         grid_spec=pltpu.PrefetchScalarGridSpec(
             num_scalar_prefetch=1,
@@ -465,7 +469,7 @@
                 pl.BlockSpec((features, columns), lambda i, numbers: (numbers[0], 0)),
                 pl.BlockSpec((features, columns), lambda i, numbers: (numbers[1], 0)),
             ]
-            + in_vmem(3),
+            + in_vmem(2 + TOKEN_HALVES),
             out_specs=tuple(in_vmem(halves)),
             scratch_shapes=[pltpu.VMEM((CORES * features, columns), bf16)],
         ),
@@ -475,7 +479,7 @@
             bytes_accessed=4 * tokens * features,
             transcendentals=0,
         ),
-    )(numbers, frozen_key_value, frozen_key_value, own_f, sibling_f, x)
+    )(numbers, frozen_key_value, frozen_key_value, own_f, sibling_f, *x)
 
     keys_values = None
     for at, pieces in received.items():

time: 88.8 us -> 91.7 us (1.033)
  local copies, waits for them, and re-layouts: 3.31 us -> 8.4 us
  matrix products: 6.11 us -> 4.04 us
  Pallas kernels: 23 us -> 24.5 us
  waiting for transfers between devices: 30.5 us -> 29.3 us
    unnamed x28 -> x36, local copies, waits for them, and re-layouts: 2.84 us -> 7.94 us
    all_to_all x1, waiting for transfers between devices: 10.8 us -> 7.49 us  [body(): exchanged = lax.all_to_all(packed, 'dp', 0, 0, tiled=True)]
    dot_general x4, matrix products: 6.11 us -> 4.04 us  [body(): jnp.dot(rows, weights, preferred_element_type=f32).astype(bf16)]
    ppermute x8, waiting for transfers between devices: 15.7 us -> 17.3 us  [to_chip(): return lax.ppermute(value, 'tensor', pairs)]
    pallas_call x1, Pallas kernels: 5.61 us -> 6.54 us  [body(): pl.pallas_call(functools.partial(own_kernel, (scale, parts, up_rows, rang...]
  transfers between devices with their start and end apart: 17 -> 17, of which waited for: 9 -> 8; matrix products, arithmetic and copies ran while one was open for 8% -> 5% of each run, Pallas kernels for 22% -> 26%
where the time goes in v8:
time: 91.7 us; the launch traced here: 91.2 us
  waiting for transfers between devices  29.3 us (32%)
  Pallas kernels  24.5 us (27%)
  starting transfers between devices  23.9 us (26%)
  local copies, waits for them, and re-layouts  8.4 us (9%)
  matrix products  4.04 us (4%)
  between operations  0.92 us (1%)
    ppermute x8, waiting for transfers between devices, to_chip(): return lax.ppermute(value, 'tensor', pairs)  17.3 us
    ppermute x8, starting transfers between devices, to_chip(): return lax.ppermute(value, 'tensor', pairs)  8.33 us
    unnamed x36, local copies, waits for them, and re-layouts  7.94 us
    all_to_all x1, waiting for transfers between devices, body(): exchanged = lax.all_to_all(packed, 'dp', 0, 0, tiled=True)  7.49 us
    all_to_all x1, starting transfers between devices, body(): exchanged = lax.all_to_all(packed, 'dp', 0, 0, tiled=True)  6.85 us
    pallas_call x1, Pallas kernels, body(): pl.pallas_call(functools.partial(own_kernel, (scale, parts, up_rows, rang...  6.54 us
    pallas_call x1, Pallas kernels, body(): pl.pallas_call(prepare_kernel, out_shape=(jax.ShapeDtypeStruct((tokens, L...  6.43 us
    ppermute x4, starting transfers between devices, swap_half(): outside[strip].append((piece, lax.ppermute(piece, 'dp', pairs)))  4.18 us
  transfers between devices with their start and end apart: 17, of which 8 were waited for; matrix products, arithmetic and copies ran while one was open for 5% of the time, Pallas kernels for 26%

profile of v8, /device:TPU:0, one launch (start us, length us, event | category | flops | bytes accessed | tf_op | source)
XLA Modules:
  0.0 91.2 jit_solution(4926185365575831092)
XLA Ops:
  0.6 0.5 collective-permute-start
  1.2 1.1 %copy-done.5 = f32[1,1280,2,64]{1,3,2,0:T(8,128)S(1)} copy-done((f32[1,1280,2,64]{1,3,2,0:T(8,128)S(1)}, f32[1,1280,2,64]{1,3,2,0:T(8,128)}, u32[]{:S(2)}) %copy-start.5) | copy-done | bytes 655384
  2.2 0.9 copy-done.12
  3.1 0.9 %shard_map.130 = (bf16[8,192,128]{2,1,0:T(8,128)(2,1)}, f32[8,128]{1,0:T(8,128)S(1)}) custom-call(f32[128,1280]{1,0:T(8,128)S(1)} %bitcast.35, f32[64,512]{1,0:T(8,128)S(1)} %bitcast.39), custom_call_target="tpu_custom_call" | custom-call | tf_op jit(solution)/shard_map/pallas_call | solution.py:326
  4.1 0.6 copy-done.13
  4.7 6.8 %all-to-all-start = ((bf16[8,192,128]{2,1,0:T(8,128)(2,1)}), bf16[8,192,128]{2,1,0:T(8,128)(2,1)S(1)}, u32[]{:S(2)}, u32[]{:S(2)}) async-start(bf16[8,192,128]{2,1,0:T(8,128)(2,1)} %get-tuple-element.26), calls=%async_computation | async-start | bytes 786432 | tf_op jit(solution)/shard_map/all_to_all | solution.py:368
  11.5 0.0 copy-start.7
  11.5 0.0 copy-start.8
  11.5 0.0 copy-start.9
  11.5 0.0 copy-start.10
  11.5 0.0 copy-start.11
  11.6 3.2 %shard_map.133 = (bf16[2,1280,128]{2,1,0:T(8,128)(2,1)}, bf16[2,1280,128]{2,1,0:T(8,128)(2,1)}) custom-call(bf16[5120,512]{1,0:T(8,128)(2,1)} %sibling_block.1, f32[8,128]{1,0:T(8,128)} %copy-done.13), custom_call_target="tpu_custom_call" | custom-call | tf_op jit(solution)/shard_map/pallas_call | solution.py:340
  14.8 1.6 %collective-permute-start.2 = (bf16[2,1280,128]{2,1,0:T(8,128)(2,1)}, bf16[2,1280,128]{2,1,0:T(8,128)(2,1)S(1)}, u32[]{:S(2)}, u32[]{:S(2)}) collective-permute-start(bf16[2,1280,128]{2,1,0:T(8,128)(2,1)} %get-tuple-element.33), channel_id=1, source_target_pairs={{0,2},{1,3},{2,0},{3,1},{4,6},{5,7},{6,4},{7,5},{8,10},{9,11},{10,... | collective-permute-start | bytes 1966088 | tf_op jit(solution)/shard_map/ppermute | solution.py:307
  16.3 7.5 %all-to-all-done.grad_ref = bf16[8,192,128]{2,1,0:T(8,128)(2,1)S(1)} async-done(((bf16[8,192,128]{2,1,0:T(8,128)(2,1)}), bf16[8,192,128]{2,1,0:T(8,128)(2,1)S(1)}, u32[]{:S(2)}, u32[]{:S(2)}) %all-to-all-start) | async-done | bytes 393248 | tf_op jit(solution)/shard_map/all_to_all | solution.py:368
  23.9 1.5 %shard_map.131 = (f32[3,128,160]{2,1,0:T(8,128)}, f32[3,8,512]{2,1,0:T(8,128)}, bf16[8,192,128]{2,1,0:T(8,128)(2,1)}) custom-call(s32[1]{0:T(128)} %bitcast.replica, bf16[8,192,128]{2,1,0:T(8,128)(2,1)S(1)} %all-to-all-done.grad_ref, f32[128,1280]{1,0:T(8,128)S(1)} %bitcast.36, f32[128,1280]{1,0:T(8,128)S(1)} %bitcast.37, f32[128,1280]{1,0:T(8,128)S(1)} %bitcast.38, ...), custom_call_target="tpu_custom_call" | custom-call | tf_op jit(solution)/shard_map/pallas_call | solution.py:370
  25.4 0.0 copy-start.14
  25.4 3.8 %all-to-all-start.1 = ((bf16[8,192,128]{2,1,0:T(8,128)(2,1)}), bf16[8,192,128]{2,1,0:T(8,128)(2,1)S(1)}, u32[]{:S(2)}, u32[]{:S(2)}) async-start(bf16[8,192,128]{2,1,0:T(8,128)(2,1)} %get-tuple-element.30), calls=%async_computation.1 | async-start | bytes 786432 | tf_op jit(solution)/shard_map/all_to_all | solution.py:394
  29.2 2.7 %collective-permute-done.2.in_ref = bf16[2,1280,128]{2,1,0:T(8,128)(2,1)S(1)} collective-permute-done((bf16[2,1280,128]{2,1,0:T(8,128)(2,1)}, bf16[2,1280,128]{2,1,0:T(8,128)(2,1)S(1)}, u32[]{:S(2)}, u32[]{:S(2)}) %collective-permute-start.2) | collective-permute-done | bytes 655392 | tf_op jit(solution)/shard_map/ppermute | solution.py:307
  32.0 1.8 %collective-permute-start.3 = (bf16[1280,128]{1,0:T(8,128)(2,1)S(1)}, bf16[1280,128]{1,0:T(8,128)(2,1)S(1)}, u32[]{:S(2)}, u32[]{:S(2)}) collective-permute-start(bf16[1280,128]{1,0:T(8,128)(2,1)S(1)} %get-tuple-element.35.refs_0_), channel_id=1, source_target_pairs={{0,4},{4,0},{8,12},{12,8},{16,20},{20,16},{24,28},{28,24},{1,5},{5... | collective-permute-start | bytes 983048 | tf_op jit(solution)/shard_map/ppermute | solution.py:411
  33.8 1.5 %collective-permute-start.4 = (bf16[1280,128]{1,0:T(8,128)(2,1)S(1)}, bf16[1280,128]{1,0:T(8,128)(2,1)S(1)}, u32[]{:S(2)}, u32[]{:S(2)}) collective-permute-start(bf16[1280,128]{1,0:T(8,128)(2,1)S(1)} %get-tuple-element.36.refs_2_), channel_id=1, source_target_pairs={{0,8},{4,12},{8,0},{12,4},{16,24},{20,28},{24,16},{28,20},{1,9},{5... | collective-permute-start | bytes 983048 | tf_op jit(solution)/shard_map/ppermute | solution.py:411
  35.2 1.5 %collective-permute-start.7 = (bf16[2,1280,128]{2,1,0:T(8,128)(2,1)S(1)}, bf16[2,1280,128]{2,1,0:T(8,128)(2,1)S(1)}, u32[]{:S(2)}, u32[]{:S(2)}) collective-permute-start(bf16[2,1280,128]{2,1,0:T(8,128)(2,1)S(1)} %copy-done.15), channel_id=1, source_target_pairs={{0,2},{1,3},{2,0},{3,1},{4,6},{5,7},{6,4},{7,5},{8,10},{9,11},{10,... | collective-permute-start | bytes 1966088 | tf_op jit(solution)/shard_map/ppermute | solution.py:307
  36.7 0.0 collective-permute-start.1
  36.7 1.2 %collective-permute-done.1.sibling_gain = f32[1,1280]{1,0:T(1,128)S(1)} collective-permute-done((f32[1,1280]{1,0:T(1,128)S(1)}, f32[1,1280]{1,0:T(1,128)S(1)}, u32[]{:S(2)}, u32[]{:S(2)}) %collective-permute-start.1) | collective-permute-done | bytes 5152 | tf_op jit(solution)/shard_map/ppermute | solution.py:299
  37.9 0.0 collective-permute-done.sibling_ref
  37.9 1.9 %copy-done.4 = bf16[1280,1280]{1,0:T(8,128)(2,1)S(1)} copy-done((bf16[1280,1280]{1,0:T(8,128)(2,1)S(1)}, bf16[1280,1280]{1,0:T(8,128)(2,1)}, u32[]{:S(2)}) %copy-start.4) | copy-done | bytes 3276824
  39.8 6.4 %shard_map.132 = (f32[1280,128]{1,0:T(8,128)S(1)}, bf16[640,2560]{1,0:T(8,128)(2,1)S(1)}, bf16[640,2560]{1,0:T(8,128)(2,1)S(1)}) custom-call(bf16[1280,1280]{1,0:T(8,128)(2,1)S(1)} %copy-done.4, bf16[1280,1280]{1,0:T(8,128)(2,1)} %collective-permute-done.sibling_ref, f32[1,1280]{1,0:T(1,128)S(1)} %broadcast_in_dim.13.own_gain, ...), custom_call_target="tpu_custom_call" | custom-call | tf_op jit(solution)/shard_map/pallas_call | solution.py:358
  46.3 1.7 %copy-done = bf16[640,2560]{1,0:T(8,128)(2,1)} copy-done((bf16[640,2560]{1,0:T(8,128)(2,1)}, bf16[640,2560]{1,0:T(8,128)(2,1)S(1)}, u32[]{:S(2)}) %copy-start) | copy-done | bytes 3276824
  47.9 1.7 %copy-done.2 = bf16[640,2560]{1,0:T(8,128)(2,1)} copy-done((bf16[640,2560]{1,0:T(8,128)(2,1)}, bf16[640,2560]{1,0:T(8,128)(2,1)S(1)}, u32[]{:S(2)}) %copy-start.2) | copy-done | bytes 3276824
  49.6 0.2 slice_reduce_fusion
  49.9 0.0 collective-permute-done.3.refs_1_
  49.9 0.0 collective-permute-done.4.refs_3_
  49.9 0.0 all-to-all-done.1.in_ref.own_f
  49.9 0.2 collective-permute-start.5
  50.1 0.1 pad_add_fusion.numbers
  50.2 0.6 collective-permute-start.6
  50.8 0.1 pad_add_fusion.1.numbers
  50.8 0.0 collective-permute-done.7.in_ref
  50.8 3.7 %collective-permute-done.6.b_ref = bf16[8,32,128]{2,1,0:T(8,128)(2,1)S(1)} collective-permute-done((bf16[8,32,128]{2,1,0:T(8,128)(2,1)S(1)}, bf16[8,32,128]{2,1,0:T(8,128)(2,1)S(1)}, u32[]{:S(2)}, u32[]{:S(2)}) %collective-permute-start.6) | collective-permute-done | bytes 65568 | tf_op jit(solution)/shard_map/ppermute | solution.py:307
  54.6 0.6 collective-permute-start.8
  55.3 0.3 collective-permute-start.9
  55.6 0.5 collective-permute-start.11
  56.1 0.0 collective-permute-done.5.sibling_f
  56.1 1.1 %shard_map.136 = bf16[2560,256]{1,0:T(8,128)(2,1)S(1)} custom-call(s32[3]{0:T(128)S(1)} %pad_add_fusion.1.numbers, bf16[8,192,128]{2,1,0:T(8,128)(2,1)S(1)} %all-to-all-done.1.in_ref.own_f, bf16[8,192,128]{2,1,0:T(8,128)(2,1)S(1)} %collective-permute-done.5.sibling_f, bf16[8,32,128]{2,1,0:T(8,128)(2,1)S(1)} %collective-permute-done.6.b_ref, ...), custom_call_target="tpu_custom_call" | custom-call | tf_op jit(solution)/shard_map/pallas_call | solution.py:447
  57.2 1.0 %convolution_convert_fusion.3 = bf16[640,256]{1,0:T(8,128)(2,1)S(1)} fusion(bf16[640,2560]{1,0:T(8,128)(2,1)S(1)} %copy-done.1, bf16[2560,256]{1,0:T(8,128)(2,1)S(1)} %shard_map.136), kind=kOutput, calls=%fused_computation.3 | convolution fusion | flops 839024640 | bytes 4915200 | tf_op jit(solution)/shard_map/dot_general | solution.py:455
  58.2 1.6 %collective-permute-start.10 = (bf16[640,256]{1,0:T(8,128)(2,1)S(1)}, bf16[640,256]{1,0:T(8,128)(2,1)S(1)}, u32[]{:S(2)}, u32[]{:S(2)}) collective-permute-start(bf16[640,256]{1,0:T(8,128)(2,1)S(1)} %convolution_convert_fusion.3), channel_id=1, source_target_pairs={{0,2},{1,3},{2,0},{3,1},{4,6},{5,7},{6,4},{7,5},{8,10},{9,11},{10,... | collective-permute-start | bytes 983048 | tf_op jit(solution)/shard_map/ppermute | solution.py:307
  59.8 1.0 %convolution_convert_fusion.2 = bf16[640,256]{1,0:T(8,128)(2,1)S(1)} fusion(bf16[640,2560]{1,0:T(8,128)(2,1)S(1)} %copy-done.3, bf16[2560,256]{1,0:T(8,128)(2,1)S(1)} %shard_map.136), kind=kOutput, calls=%fused_computation.2 | convolution fusion | flops 839024640 | bytes 4915200 | tf_op jit(solution)/shard_map/dot_general | solution.py:455
  60.8 3.0 %collective-permute-done.8.refs_1_ = bf16[1280,128]{1,0:T(8,128)(2,1)S(1)} collective-permute-done((bf16[1280,128]{1,0:T(8,128)(2,1)S(1)}, bf16[1280,128]{1,0:T(8,128)(2,1)S(1)}, u32[]{:S(2)}, u32[]{:S(2)}) %collective-permute-start.8) | collective-permute-done | bytes 327712 | tf_op jit(solution)/shard_map/ppermute | solution.py:411
  63.8 0.3 collective-permute-done.9.refs_3_
  64.1 1.1 %shard_map.138 = bf16[2560,256]{1,0:T(8,128)(2,1)S(1)} custom-call(s32[3]{0:T(128)S(1)} %pad_add_fusion.1.numbers, bf16[8,192,128]{2,1,0:T(8,128)(2,1)S(1)} %all-to-all-done.1.in_ref.own_f, bf16[8,192,128]{2,1,0:T(8,128)(2,1)S(1)} %collective-permute-done.5.sibling_f, bf16[8,32,128]{2,1,0:T(8,128)(2,1)S(1)} %collective-permute-done.6.b_ref, ...), custom_call_target="tpu_custom_call" | custom-call | tf_op jit(solution)/shard_map/pallas_call | solution.py:447
  65.3 0.0 slice-start.1
  65.3 1.0 %convolution_convert_fusion.1 = bf16[640,256]{1,0:T(8,128)(2,1)S(1)} fusion(bf16[640,2560]{1,0:T(8,128)(2,1)S(1)} %copy-done.1, bf16[2560,256]{1,0:T(8,128)(2,1)S(1)} %shard_map.138), kind=kOutput, calls=%fused_computation.1 | convolution fusion | flops 839024640 | bytes 4915200 | tf_op jit(solution)/shard_map/dot_general | solution.py:455
  66.3 1.0 %convolution_convert_fusion = bf16[640,256]{1,0:T(8,128)(2,1)S(1)} fusion(bf16[640,2560]{1,0:T(8,128)(2,1)S(1)} %copy-done.3, bf16[2560,256]{1,0:T(8,128)(2,1)S(1)} %shard_map.138), kind=kOutput, calls=%fused_computation | convolution fusion | flops 839024640 | bytes 4915200 | tf_op jit(solution)/shard_map/dot_general | solution.py:455
  67.3 0.6 collective-permute-start.14
  67.9 1.5 %collective-permute-start.12 = (bf16[640,256]{1,0:T(8,128)(2,1)S(1)}, bf16[640,256]{1,0:T(8,128)(2,1)S(1)}, u32[]{:S(2)}, u32[]{:S(2)}) collective-permute-start(bf16[640,256]{1,0:T(8,128)(2,1)S(1)} %convolution_convert_fusion), channel_id=1, source_target_pairs={{0,2},{1,3},{2,0},{3,1},{4,6},{5,7},{6,4},{7,5},{8,10},{9,11},{10,... | collective-permute-start | bytes 983048 | tf_op jit(solution)/shard_map/ppermute | solution.py:307
  69.4 0.5 collective-permute-start.13
  70.0 0.0 collective-permute-done.11
  70.0 6.5 %shard_map.139 = (f32[1280,256]{1,0:T(8,128)S(1)}, f32[1280,256]{1,0:T(8,128)S(1)}) custom-call(s32[3]{0:T(128)S(1)} %pad_add_fusion.numbers, bf16[5120,512]{1,0:T(8,128)(2,1)S(1)} %bitcast.34, bf16[5120,512]{1,0:T(8,128)(2,1)S(1)} %bitcast.34, bf16[8,192,128]{2,1,0:T(8,128)(2,1)S(1)} %all-to-all-done.1.in_ref.own_f, ...), custom_call_target="tpu_custom_call" | custom-call | flops 3355443200 | bytes 6553600 | tf_op jit(solution)/shard_map/pallas_call | solution.py:462
  76.6 0.2 broadcast_in_dim.14.inv
  76.8 0.9 shard_map.140.refs_1_
  77.7 0.4 collective-permute-done.14.refs_0_
  78.0 0.9 shard_map.141.refs_1_
  78.9 10.5 %collective-permute-done.13.refs_0_ = bf16[640,256]{1,0:T(8,128)(2,1)S(1)} collective-permute-done((bf16[640,256]{1,0:T(8,128)(2,1)S(1)}, bf16[640,256]{1,0:T(8,128)(2,1)S(1)}, u32[]{:S(2)}, u32[]{:S(2)}) %collective-permute-start.13) | collective-permute-done | bytes 327712 | tf_op jit(solution)/shard_map/ppermute | solution.py:307
  89.4 0.9 shard_map.142.refs_1_
  90.3 0.9 shard_map.143
  (31 shorter events, 0.2 us)
Async XLA Ops:
  0.6 37.3 %collective-permute-start = (bf16[1280,1280]{1,0:T(8,128)(2,1)}, bf16[1280,1280]{1,0:T(8,128)(2,1)}, u32[]{:S(2)}, u32[]{:S(2)}) collective-permute-start(bf16[1280,1280]{1,0:T(8,128)(2,1)} %own_ref.1), channel_id=1, source_target_pairs={{0,1},{1,0},{2,3},{3,2},{4,5},{5,4},{6,7},{7,6},{8,9},{9,8},{10,11... | collective-permute-start | bytes 9830408 | tf_op jit(solution)/shard_map/ppermute | solution.py:299
  1.1 1.1 %copy-start.5 = (f32[1,1280,2,64]{1,3,2,0:T(8,128)S(1)}, f32[1,1280,2,64]{1,3,2,0:T(8,128)}, u32[]{:S(2)}) copy-start(f32[1,1280,2,64]{1,3,2,0:T(8,128)} %param.20) | copy-start | bytes 1966084
  2.2 0.9 copy-start.12
  4.1 0.6 copy-start.13
  4.7 19.2 %all-to-all-start = ((bf16[8,192,128]{2,1,0:T(8,128)(2,1)}), bf16[8,192,128]{2,1,0:T(8,128)(2,1)S(1)}, u32[]{:S(2)}, u32[]{:S(2)}) async-start(bf16[8,192,128]{2,1,0:T(8,128)(2,1)} %get-tuple-element.26), calls=%async_computation | async-start | bytes 786432 | tf_op jit(solution)/shard_map/all_to_all | solution.py:368
  11.5 12.3 %copy-start.6 = (f32[1280,2,64]{0,2,1:T(8,128)S(1)}, f32[1280,2,64]{0,2,1:T(8,128)}, u32[]{:S(2)}) copy-start(f32[1280,2,64]{0,2,1:T(8,128)} %param.14) | copy-start | bytes 1966084
  11.5 12.3 %copy-start.7 = (f32[1280,2,64]{0,2,1:T(8,128)S(1)}, f32[1280,2,64]{0,2,1:T(8,128)}, u32[]{:S(2)}) copy-start(f32[1280,2,64]{0,2,1:T(8,128)} %param.15) | copy-start | bytes 1966084
  11.5 12.3 %copy-start.8 = (f32[1280,2,64]{0,2,1:T(8,128)S(1)}, f32[1280,2,64]{0,2,1:T(8,128)}, u32[]{:S(2)}) copy-start(f32[1280,2,64]{0,2,1:T(8,128)} %param.16) | copy-start | bytes 1966084
  11.5 12.3 %copy-start.9 = (f32[64,512]{1,0:T(8,128)S(1)}, f32[64,512]{1,0:T(8,128)}, u32[]{:S(2)}) copy-start(f32[64,512]{1,0:T(8,128)} %refs_3_.1) | copy-start | bytes 393220
  11.5 12.3 %copy-start.10 = (f32[64,512]{1,0:T(8,128)S(1)}, f32[64,512]{1,0:T(8,128)}, u32[]{:S(2)}) copy-start(f32[64,512]{1,0:T(8,128)} %refs_4_.1) | copy-start | bytes 393220
  11.5 12.3 %copy-start.11 = (f32[64,512]{1,0:T(8,128)S(1)}, f32[64,512]{1,0:T(8,128)}, u32[]{:S(2)}) copy-start(f32[64,512]{1,0:T(8,128)} %refs_5_.1) | copy-start | bytes 393220
  14.8 17.1 %collective-permute-start.2 = (bf16[2,1280,128]{2,1,0:T(8,128)(2,1)}, bf16[2,1280,128]{2,1,0:T(8,128)(2,1)S(1)}, u32[]{:S(2)}, u32[]{:S(2)}) collective-permute-start(bf16[2,1280,128]{2,1,0:T(8,128)(2,1)} %get-tuple-element.33), channel_id=1, source_target_pairs={{0,2},{1,3},{2,0},{3,1},{4,6},{5,7},{6,4},{7,5},{8,10},{9,11},{10,... | collective-permute-start | bytes 1966088 | tf_op jit(solution)/shard_map/ppermute | solution.py:307
  25.4 9.8 %copy-start.15 = (bf16[2,1280,128]{2,1,0:T(8,128)(2,1)S(1)}, bf16[2,1280,128]{2,1,0:T(8,128)(2,1)}, u32[]{:S(2)}) copy-start(bf16[2,1280,128]{2,1,0:T(8,128)(2,1)} %get-tuple-element.40) | copy-start | bytes 1966084
  25.4 11.3 %copy-start.14 = (f32[1280]{0:T(1024)S(1)}, f32[1280]{0:T(1024)}, u32[]{:S(2)}) copy-start(f32[1280]{0:T(1024)} %param.12) | copy-start | bytes 15364
  25.4 24.5 %all-to-all-start.1 = ((bf16[8,192,128]{2,1,0:T(8,128)(2,1)}), bf16[8,192,128]{2,1,0:T(8,128)(2,1)S(1)}, u32[]{:S(2)}, u32[]{:S(2)}) async-start(bf16[8,192,128]{2,1,0:T(8,128)(2,1)} %get-tuple-element.30), calls=%async_computation.1 | async-start | bytes 786432 | tf_op jit(solution)/shard_map/all_to_all | solution.py:394
  32.0 17.9 %collective-permute-start.3 = (bf16[1280,128]{1,0:T(8,128)(2,1)S(1)}, bf16[1280,128]{1,0:T(8,128)(2,1)S(1)}, u32[]{:S(2)}, u32[]{:S(2)}) collective-permute-start(bf16[1280,128]{1,0:T(8,128)(2,1)S(1)} %get-tuple-element.35.refs_0_), channel_id=1, source_target_pairs={{0,4},{4,0},{8,12},{12,8},{16,20},{20,16},{24,28},{28,24},{1,5},{5... | collective-permute-start | bytes 983048 | tf_op jit(solution)/shard_map/ppermute | solution.py:411
  33.8 16.1 %collective-permute-start.4 = (bf16[1280,128]{1,0:T(8,128)(2,1)S(1)}, bf16[1280,128]{1,0:T(8,128)(2,1)S(1)}, u32[]{:S(2)}, u32[]{:S(2)}) collective-permute-start(bf16[1280,128]{1,0:T(8,128)(2,1)S(1)} %get-tuple-element.36.refs_2_), channel_id=1, source_target_pairs={{0,8},{4,12},{8,0},{12,4},{16,24},{20,28},{24,16},{28,20},{1,9},{5... | collective-permute-start | bytes 983048 | tf_op jit(solution)/shard_map/ppermute | solution.py:411
  35.2 15.6 %collective-permute-start.7 = (bf16[2,1280,128]{2,1,0:T(8,128)(2,1)S(1)}, bf16[2,1280,128]{2,1,0:T(8,128)(2,1)S(1)}, u32[]{:S(2)}, u32[]{:S(2)}) collective-permute-start(bf16[2,1280,128]{2,1,0:T(8,128)(2,1)S(1)} %copy-done.15), channel_id=1, source_target_pairs={{0,2},{1,3},{2,0},{3,1},{4,6},{5,7},{6,4},{7,5},{8,10},{9,11},{10,... | collective-permute-start | bytes 1966088 | tf_op jit(solution)/shard_map/ppermute | solution.py:307
  36.7 1.2 %collective-permute-start.1 = (f32[1,1280]{1,0:T(1,128)S(1)}, f32[1,1280]{1,0:T(1,128)S(1)}, u32[]{:S(2)}, u32[]{:S(2)}) collective-permute-start(f32[1,1280]{1,0:T(1,128)S(1)} %broadcast_in_dim.13.own_gain), channel_id=1, source_target_pairs={{0,1},{1,0},{2,3},{3,2},{4,5},{5,4},{6,7},{7,6},{8,9},{9,8},{10,11... | collective-permute-start | bytes 15368 | tf_op jit(solution)/shard_map/ppermute | solution.py:299
  37.9 1.9 %copy-start.4 = (bf16[1280,1280]{1,0:T(8,128)(2,1)S(1)}, bf16[1280,1280]{1,0:T(8,128)(2,1)}, u32[]{:S(2)}) copy-start(bf16[1280,1280]{1,0:T(8,128)(2,1)} %own_ref.1) | copy-start | bytes 9830404
  46.2 1.7 %copy-start = (bf16[640,2560]{1,0:T(8,128)(2,1)}, bf16[640,2560]{1,0:T(8,128)(2,1)S(1)}, u32[]{:S(2)}) copy-start(bf16[640,2560]{1,0:T(8,128)(2,1)S(1)} %get-tuple-element.29.refs_0_) | copy-start | bytes 9830404
  47.9 1.7 %copy-start.2 = (bf16[640,2560]{1,0:T(8,128)(2,1)}, bf16[640,2560]{1,0:T(8,128)(2,1)S(1)}, u32[]{:S(2)}) copy-start(bf16[640,2560]{1,0:T(8,128)(2,1)S(1)} %get-tuple-element.38.refs_1_) | copy-start | bytes 9830404
  49.9 6.2 %collective-permute-start.5 = (bf16[8,192,128]{2,1,0:T(8,128)(2,1)S(1)}, bf16[8,192,128]{2,1,0:T(8,128)(2,1)S(1)}, u32[]{:S(2)}, u32[]{:S(2)}) collective-permute-start(bf16[8,192,128]{2,1,0:T(8,128)(2,1)S(1)} %all-to-all-done.1.in_ref.own_f), channel_id=1, source_target_pairs={{0,1},{1,0},{2,3},{3,2},{4,5},{5,4},{6,7},{7,6},{8,9},{9,8},{10,11... | collective-permute-start | bytes 1179656 | tf_op jit(solution)/shard_map/ppermute | solution.py:299
  50.2 4.4 %collective-permute-start.6 = (bf16[8,32,128]{2,1,0:T(8,128)(2,1)S(1)}, bf16[8,32,128]{2,1,0:T(8,128)(2,1)S(1)}, u32[]{:S(2)}, u32[]{:S(2)}) collective-permute-start(bf16[8,32,128]{2,1,0:T(8,128)(2,1)S(1)} %shard_map.135), channel_id=1, source_target_pairs={{0,2},{1,3},{2,0},{3,1},{4,6},{5,7},{6,4},{7,5},{8,10},{9,11},{10,... | collective-permute-start | bytes 196616 | tf_op jit(solution)/shard_map/ppermute | solution.py:307
  54.6 9.2 %collective-permute-start.8 = (bf16[1280,128]{1,0:T(8,128)(2,1)S(1)}, bf16[1280,128]{1,0:T(8,128)(2,1)S(1)}, u32[]{:S(2)}, u32[]{:S(2)}) collective-permute-start(bf16[1280,128]{1,0:T(8,128)(2,1)S(1)} %get-tuple-element.42.refs_0_), channel_id=1, source_target_pairs={{0,4},{4,0},{8,12},{12,8},{16,20},{20,16},{24,28},{28,24},{1,5},{5... | collective-permute-start | bytes 983048 | tf_op jit(solution)/shard_map/ppermute | solution.py:411
  55.2 2.0 %copy-start.1 = (bf16[640,2560]{1,0:T(8,128)(2,1)S(1)}, bf16[640,2560]{1,0:T(8,128)(2,1)}, u32[]{:S(2)}) copy-start(bf16[640,2560]{1,0:T(8,128)(2,1)} %copy-done) | copy-start | bytes 9830404
  55.3 8.9 %collective-permute-start.9 = (bf16[1280,128]{1,0:T(8,128)(2,1)S(1)}, bf16[1280,128]{1,0:T(8,128)(2,1)S(1)}, u32[]{:S(2)}, u32[]{:S(2)}) collective-permute-start(bf16[1280,128]{1,0:T(8,128)(2,1)S(1)} %get-tuple-element.43.refs_2_), channel_id=1, source_target_pairs={{0,8},{4,12},{8,0},{12,4},{16,24},{20,28},{24,16},{28,20},{1,9},{5... | collective-permute-start | bytes 983048 | tf_op jit(solution)/shard_map/ppermute | solution.py:411
  55.6 14.4 %collective-permute-start.11 = (f32[1280]{0:T(1024)S(1)}, f32[1280]{0:T(1024)S(1)}, u32[]{:S(2)}, u32[]{:S(2)}) collective-permute-start(f32[1280]{0:T(1024)S(1)} %slice_reduce_fusion), channel_id=1, source_target_pairs={{0,2},{1,3},{2,0},{3,1},{4,6},{5,7},{6,4},{7,5},{8,10},{9,11},{10,... | collective-permute-start | bytes 15368 | tf_op jit(solution)/shard_map/ppermute | solution.py:307
  57.2 2.6 %copy-start.3 = (bf16[640,2560]{1,0:T(8,128)(2,1)S(1)}, bf16[640,2560]{1,0:T(8,128)(2,1)}, u32[]{:S(2)}) copy-start(bf16[640,2560]{1,0:T(8,128)(2,1)} %copy-done.2) | copy-start | bytes 9830404
  58.2 11.7 %collective-permute-start.10 = (bf16[640,256]{1,0:T(8,128)(2,1)S(1)}, bf16[640,256]{1,0:T(8,128)(2,1)S(1)}, u32[]{:S(2)}, u32[]{:S(2)}) collective-permute-start(bf16[640,256]{1,0:T(8,128)(2,1)S(1)} %convolution_convert_fusion.3), channel_id=1, source_target_pairs={{0,2},{1,3},{2,0},{3,1},{4,6},{5,7},{6,4},{7,5},{8,10},{9,11},{10,... | collective-permute-start | bytes 983048 | tf_op jit(solution)/shard_map/ppermute | solution.py:307
  64.1 5.9 %slice-start = ((s8[5242880]{0:T(1024)(128)(4,1)}), s8[4194304]{0:T(1024)(128)(4,1)S(1)}, s32[]{:S(2)}) async-start(s8[5242880]{0:T(1024)(128)(4,1)} %bitcast.33), calls=%async_computation.2 | async-start | bytes 8388608
  65.3 4.7 %slice-start.1 = ((s8[5242880]{0:T(1024)(128)(4,1)}), s8[1048576]{0:T(1024)(128)(4,1)S(1)}, s32[]{:S(2)}) async-start(s8[5242880]{0:T(1024)(128)(4,1)} %bitcast.33), calls=%async_computation.3 | async-start | bytes 2097152
  67.3 10.7 %collective-permute-start.14 = (bf16[640,256]{1,0:T(8,128)(2,1)S(1)}, bf16[640,256]{1,0:T(8,128)(2,1)S(1)}, u32[]{:S(2)}, u32[]{:S(2)}) collective-permute-start(bf16[640,256]{1,0:T(8,128)(2,1)S(1)} %convolution_convert_fusion.2), channel_id=1, source_target_pairs={{0,2},{1,3},{2,0},{3,1},{4,6},{5,7},{6,4},{7,5},{8,10},{9,11},{10,... | collective-permute-start | bytes 983048 | tf_op jit(solution)/shard_map/ppermute | solution.py:307
  67.9 22.4 %collective-permute-start.12 = (bf16[640,256]{1,0:T(8,128)(2,1)S(1)}, bf16[640,256]{1,0:T(8,128)(2,1)S(1)}, u32[]{:S(2)}, u32[]{:S(2)}) collective-permute-start(bf16[640,256]{1,0:T(8,128)(2,1)S(1)} %convolution_convert_fusion), channel_id=1, source_target_pairs={{0,2},{1,3},{2,0},{3,1},{4,6},{5,7},{6,4},{7,5},{8,10},{9,11},{10,... | collective-permute-start | bytes 983048 | tf_op jit(solution)/shard_map/ppermute | solution.py:307
  69.4 20.0 %collective-permute-start.13 = (bf16[640,256]{1,0:T(8,128)(2,1)S(1)}, bf16[640,256]{1,0:T(8,128)(2,1)S(1)}, u32[]{:S(2)}, u32[]{:S(2)}) collective-permute-start(bf16[640,256]{1,0:T(8,128)(2,1)S(1)} %convolution_convert_fusion.1), channel_id=1, source_target_pairs={{0,2},{1,3},{2,0},{3,1},{4,6},{5,7},{6,4},{7,5},{8,10},{9,11},{10,... | collective-permute-start | bytes 983048 | tf_op jit(solution)/shard_map/ppermute | solution.py:307

commit v9 on v8

--- a/solution.py
+++ b/solution.py
@@ -15,7 +15,6 @@
 COLUMN_HALVES = 2
 TOKEN_HALVES = 2
 VMEM_BYTES = 16 * 2**20
-TAKE_VMEM_BYTES = 58 * 2**20
 
 
 def adaptive_moment_update(param, first, second, grad_mean):
@@ -347,12 +346,17 @@
         in_specs=anywhere(1) + in_vmem(1),
         out_specs=tuple(in_vmem(halves * len(steps))),
         scratch_shapes=[pltpu.SemaphoreType.DMA((len(steps) * strips,))],
-        compiler_params=pltpu.CompilerParams(vmem_limit_bytes=TAKE_VMEM_BYTES),
+        compiler_params=params(),
     )(frozen_key_value, mark)
-    mine = [
-        [to_chip(taken[half * len(steps) + step - 1], step) for step in steps]
-        for half in range(halves)
-    ]
+    mine = []
+
+    def send_half(half, after):
+        blocks = taken[half * len(steps) : (half + 1) * len(steps)]
+        if after is not None:
+            blocks, _ = lax.optimization_barrier((blocks, after))
+        mine.append([to_chip(value, step) for value, step in zip(blocks, steps)])
+
+    send_half(0, None)
 
     gain = input_norm_gain[None, :]
     squares, *x = pl.pallas_call(
@@ -366,6 +370,7 @@
     squares = squares[:, 0]
 
     exchanged = lax.all_to_all(packed, "dp", 0, 0, tiled=True)
+    exchanged, squares = lax.optimization_barrier((exchanged, squares))
     if aligned:
         a_next, b_next, sent = pl.pallas_call(
             adam_copy_kernel,
@@ -392,6 +397,8 @@
             compiler_params=params(),
         )(exchanged, *down_state, *up_state)
     own_f = lax.all_to_all(sent, "dp", 0, 0, tiled=True)
+    for half in range(1, halves):
+        send_half(half, (mine[-1], sent))
     a_next = jnp.transpose(a_next.reshape(3, parts, rank, down_rows), (0, 3, 1, 2))
 
     outside = [[] for _ in range(strips)]
@@ -411,7 +418,7 @@
                 outside[strip].append((piece, lax.ppermute(piece, "dp", pairs)))
 
     swap_half(0, sent)
-    own_f, squares, _ = lax.optimization_barrier((own_f, squares, outside))
+    own_f, _ = lax.optimization_barrier((own_f, outside))
     sibling_f = to_sibling(own_f)
     packed_b = pl.pallas_call(
         tail_kernel,

time: 91.7 us -> 101 us (1.10)
  local copies, waits for them, and re-layouts: 8.4 us -> 13.3 us
  waiting for transfers between devices: 29.3 us -> 31.6 us
  starting transfers between devices: 23.9 us -> 25.4 us
    ppermute x4, waiting for transfers between devices: 3.31 us -> 14.4 us  [swap_half(): outside[strip].append((piece, lax.ppermute(piece, 'dp', pairs)))]
    all_to_all x1, waiting for transfers between devices: 7.49 us -> 0.01 us  [body(): exchanged = lax.all_to_all(packed, 'dp', 0, 0, tiled=True)]
    unnamed x36 -> x38, local copies, waits for them, and re-layouts: 7.94 us -> 12.9 us
    all_to_all x1, starting transfers between devices: 3.78 us -> 6.14 us  [body(): own_f = lax.all_to_all(sent, 'dp', 0, 0, tiled=True)]
    pallas_call x1, Pallas kernels: 3.22 us -> 1.11 us  [body(): pl.pallas_call(functools.partial(take_kernel, chips, turn), out_shape=tup...]
    ppermute x8, waiting for transfers between devices: 17.3 us -> 16.1 us  [to_chip(): return lax.ppermute(value, 'tensor', pairs)]
    pallas_call x2, Pallas kernels: 0.09 us -> 1.17 us  [swap_half(): pl.pallas_call(split_kernel, out_shape=(jax.ShapeDtypeStruct((features, L...]
    ppermute x8, starting transfers between devices: 8.33 us -> 7.32 us  [to_chip(): return lax.ppermute(value, 'tensor', pairs)]
  transfers between devices with their start and end apart: 17 -> 17, of which waited for: 8 -> 9; matrix products, arithmetic and copies ran while one was open for 5% -> 5% of each run, Pallas kernels for 26% -> 24%
where the time goes in v9:
time: 101 us; the launch traced here: 99.9 us
  waiting for transfers between devices  31.6 us (31%)
  starting transfers between devices  25.4 us (25%)
  Pallas kernels  24.5 us (24%)
  local copies, waits for them, and re-layouts  13.3 us (13%)
  matrix products  4.04 us (4%)
    ppermute x8, waiting for transfers between devices, to_chip(): return lax.ppermute(value, 'tensor', pairs)  16.1 us
    ppermute x4, waiting for transfers between devices, swap_half(): outside[strip].append((piece, lax.ppermute(piece, 'dp', pairs)))  14.4 us
    unnamed x38, local copies, waits for them, and re-layouts  12.9 us
    ppermute x8, starting transfers between devices, to_chip(): return lax.ppermute(value, 'tensor', pairs)  7.32 us
    all_to_all x1, starting transfers between devices, body(): exchanged = lax.all_to_all(packed, 'dp', 0, 0, tiled=True)  6.85 us
    pallas_call x1, Pallas kernels, body(): pl.pallas_call(functools.partial(own_kernel, (scale, parts, up_rows, rang...  6.54 us
    pallas_call x1, Pallas kernels, body(): pl.pallas_call(prepare_kernel, out_shape=(jax.ShapeDtypeStruct((tokens, L...  6.43 us
    all_to_all x1, starting transfers between devices, body(): own_f = lax.all_to_all(sent, 'dp', 0, 0, tiled=True)  6.14 us
  transfers between devices with their start and end apart: 17, of which 9 were waited for; matrix products, arithmetic and copies ran while one was open for 5% of the time, Pallas kernels for 24%

profile of v9, /device:TPU:0, one launch (start us, length us, event | category | flops | bytes accessed | tf_op | source)
XLA Modules:
  0.0 99.9 jit_solution(7707406599117775981)
XLA Ops:
  0.6 0.5 collective-permute-start
  1.2 1.1 %copy-done.6 = f32[1,1280,2,64]{1,3,2,0:T(8,128)S(1)} copy-done((f32[1,1280,2,64]{1,3,2,0:T(8,128)S(1)}, f32[1,1280,2,64]{1,3,2,0:T(8,128)}, u32[]{:S(2)}) %copy-start.6) | copy-done | bytes 655384
  2.2 0.9 copy-done.13
  3.1 0.9 shard_map.130
  4.1 6.8 %all-to-all-start = ((bf16[8,192,128]{2,1,0:T(8,128)(2,1)}), bf16[8,192,128]{2,1,0:T(8,128)(2,1)}, u32[]{:S(2)}, u32[]{:S(2)}) async-start(bf16[8,192,128]{2,1,0:T(8,128)(2,1)} %get-tuple-element.28), calls=%async_computation | async-start | bytes 786432 | tf_op jit(solution)/shard_map/all_to_all | solution.py:372
  10.9 2.5 %copy-done = bf16[5120,512]{1,0:T(8,128)(2,1)S(1)} copy-done((bf16[5120,512]{1,0:T(8,128)(2,1)S(1)}, bf16[5120,512]{1,0:T(8,128)(2,1)}, u32[]{:S(2)}) %copy-start) | copy-done | bytes 5242904
  13.4 1.1 %shard_map.133 = (bf16[2,1280,128]{2,1,0:T(8,128)(2,1)}, bf16[2,1280,128]{2,1,0:T(8,128)(2,1)S(1)}) custom-call(bf16[5120,512]{1,0:T(8,128)(2,1)S(1)} %copy-done, f32[8,128]{1,0:T(8,128)S(1)} %get-tuple-element.35._), custom_call_target="tpu_custom_call" | custom-call | tf_op jit(solution)/shard_map/pallas_call | solution.py:339
  14.5 0.8 copy-done.14
  15.3 1.5 %collective-permute-start.2 = (bf16[2,1280,128]{2,1,0:T(8,128)(2,1)}, bf16[2,1280,128]{2,1,0:T(8,128)(2,1)}, u32[]{:S(2)}, u32[]{:S(2)}) collective-permute-start(bf16[2,1280,128]{2,1,0:T(8,128)(2,1)} %get-tuple-element.36), channel_id=1, source_target_pairs={{0,2},{1,3},{2,0},{3,1},{4,6},{5,7},{6,4},{7,5},{8,10},{9,11},{10,... | collective-permute-start | bytes 1966088 | tf_op jit(solution)/shard_map/ppermute | solution.py:306
  16.8 0.0 copy-start.10
  16.9 0.0 copy-start.11
  16.9 1.1 %collective-permute-done.1.sibling_gain = f32[1,1280]{1,0:T(1,128)S(1)} collective-permute-done((f32[1,1280]{1,0:T(1,128)S(1)}, f32[1,1280]{1,0:T(1,128)S(1)}, u32[]{:S(2)}, u32[]{:S(2)}) %collective-permute-start.1) | collective-permute-done | bytes 5152 | tf_op jit(solution)/shard_map/ppermute | solution.py:298
  18.0 6.4 %shard_map.131 = (f32[1280,128]{1,0:T(8,128)S(1)}, bf16[640,2560]{1,0:T(8,128)(2,1)S(1)}, bf16[640,2560]{1,0:T(8,128)(2,1)S(1)}) custom-call(bf16[1280,1280]{1,0:T(8,128)(2,1)S(1)} %copy-done.5, bf16[1280,1280]{1,0:T(8,128)(2,1)} %collective-permute-done.sibling_ref, f32[1,1280]{1,0:T(1,128)S(1)} %broadcast_in_dim.13.own_gain, ...), custom_call_target="tpu_custom_call" | custom-call | tf_op jit(solution)/shard_map/pallas_call | solution.py:362
  24.4 1.7 %copy-done.1 = bf16[640,2560]{1,0:T(8,128)(2,1)} copy-done((bf16[640,2560]{1,0:T(8,128)(2,1)}, bf16[640,2560]{1,0:T(8,128)(2,1)S(1)}, u32[]{:S(2)}) %copy-start.1) | copy-done | bytes 3276824
  26.1 1.7 %copy-done.3 = bf16[640,2560]{1,0:T(8,128)(2,1)} copy-done((bf16[640,2560]{1,0:T(8,128)(2,1)}, bf16[640,2560]{1,0:T(8,128)(2,1)S(1)}, u32[]{:S(2)}) %copy-start.3) | copy-done | bytes 3276824
  27.8 0.2 slice_reduce_fusion
  28.1 0.0 copy-start.7
  28.1 1.1 %copy-done.7 = f32[1280,2,64]{0,2,1:T(8,128)S(1)} copy-done((f32[1280,2,64]{0,2,1:T(8,128)S(1)}, f32[1280,2,64]{0,2,1:T(8,128)}, u32[]{:S(2)}) %copy-start.7) | copy-done | bytes 655384
  29.2 1.1 %copy-done.8 = f32[1280,2,64]{0,2,1:T(8,128)S(1)} copy-done((f32[1280,2,64]{0,2,1:T(8,128)S(1)}, f32[1280,2,64]{0,2,1:T(8,128)}, u32[]{:S(2)}) %copy-start.8) | copy-done | bytes 655384
  30.3 1.1 %copy-done.9 = f32[1280,2,64]{0,2,1:T(8,128)S(1)} copy-done((f32[1280,2,64]{0,2,1:T(8,128)S(1)}, f32[1280,2,64]{0,2,1:T(8,128)}, u32[]{:S(2)}) %copy-start.9) | copy-done | bytes 655384
  31.3 0.9 copy-done.12
  32.3 2.5 %shard_map.132 = (f32[3,128,160]{2,1,0:T(8,128)}, f32[3,8,512]{2,1,0:T(8,128)}, bf16[8,192,128]{2,1,0:T(8,128)(2,1)}) custom-call(s32[1]{0:T(128)} %bitcast.replica, bf16[8,192,128]{2,1,0:T(8,128)(2,1)} %all-to-all-done.grad_ref, f32[128,1280]{1,0:T(8,128)S(1)} %bitcast.36, f32[128,1280]{1,0:T(8,128)S(1)} %bitcast.37, f32[128,1280]{1,0:T(8,128)S(1)} %bitcast.38, ...), custom_call_target="tpu_custom_call" | custom-call | tf_op jit(solution)/shard_map/pallas_call | solution.py:375
  34.8 6.1 %all-to-all-start.1 = ((bf16[8,192,128]{2,1,0:T(8,128)(2,1)}), bf16[8,192,128]{2,1,0:T(8,128)(2,1)S(1)}, u32[]{:S(2)}, u32[]{:S(2)}) async-start(bf16[8,192,128]{2,1,0:T(8,128)(2,1)} %get-tuple-element.34), calls=%async_computation.1 | async-start | bytes 786432 | tf_op jit(solution)/shard_map/all_to_all | solution.py:399
  40.9 0.0 collective-permute-done.2.in_ref
  40.9 1.1 %shard_map.134 = (bf16[1280,128]{1,0:T(8,128)(2,1)S(1)}, bf16[1280,128]{1,0:T(8,128)(2,1)S(1)}) custom-call(bf16[2,1280,128]{2,1,0:T(8,128)(2,1)} %collective-permute-done.2.in_ref), custom_call_target="tpu_custom_call" | custom-call | tf_op jit(solution)/shard_map/pallas_call | solution.py:409
  42.1 2.1 %collective-permute-start.3 = (bf16[1280,128]{1,0:T(8,128)(2,1)S(1)}, bf16[1280,128]{1,0:T(8,128)(2,1)S(1)}, u32[]{:S(2)}, u32[]{:S(2)}) collective-permute-start(bf16[1280,128]{1,0:T(8,128)(2,1)S(1)} %get-tuple-element.38.refs_0_), channel_id=1, source_target_pairs={{0,4},{4,0},{8,12},{12,8},{16,20},{20,16},{24,28},{28,24},{1,5},{5... | collective-permute-start | bytes 983048 | tf_op jit(solution)/shard_map/ppermute | solution.py:418
  44.1 1.5 %collective-permute-start.4 = (bf16[1280,128]{1,0:T(8,128)(2,1)S(1)}, bf16[1280,128]{1,0:T(8,128)(2,1)S(1)}, u32[]{:S(2)}, u32[]{:S(2)}) collective-permute-start(bf16[1280,128]{1,0:T(8,128)(2,1)S(1)} %get-tuple-element.39.refs_2_), channel_id=1, source_target_pairs={{0,8},{4,12},{8,0},{12,4},{16,24},{20,28},{24,16},{28,20},{1,9},{5... | collective-permute-start | bytes 983048 | tf_op jit(solution)/shard_map/ppermute | solution.py:418
  45.6 0.5 collective-permute-start.7
  46.1 9.2 %collective-permute-done.3.refs_1_ = bf16[1280,128]{1,0:T(8,128)(2,1)S(1)} collective-permute-done((bf16[1280,128]{1,0:T(8,128)(2,1)S(1)}, bf16[1280,128]{1,0:T(8,128)(2,1)S(1)}, u32[]{:S(2)}, u32[]{:S(2)}) %collective-permute-start.3) | collective-permute-done | bytes 327712 | tf_op jit(solution)/shard_map/ppermute | solution.py:418
  55.3 1.7 %collective-permute-done.4.refs_3_ = bf16[1280,128]{1,0:T(8,128)(2,1)S(1)} collective-permute-done((bf16[1280,128]{1,0:T(8,128)(2,1)S(1)}, bf16[1280,128]{1,0:T(8,128)(2,1)S(1)}, u32[]{:S(2)}, u32[]{:S(2)}) %collective-permute-start.4) | collective-permute-done | bytes 327712 | tf_op jit(solution)/shard_map/ppermute | solution.py:418
  57.0 0.0 all-to-all-done.1.in_ref.own_f
  57.0 0.0 collective-permute-start.5
  57.0 0.1 pad_add_fusion.numbers
  57.1 0.6 collective-permute-start.6
  57.7 0.1 pad_add_fusion.1.numbers
  57.7 4.3 %collective-permute-done.7.in_ref = bf16[2,1280,128]{2,1,0:T(8,128)(2,1)S(1)} collective-permute-done((bf16[2,1280,128]{2,1,0:T(8,128)(2,1)S(1)}, bf16[2,1280,128]{2,1,0:T(8,128)(2,1)S(1)}, u32[]{:S(2)}, u32[]{:S(2)}) %collective-permute-start.7) | collective-permute-done | bytes 655392 | tf_op jit(solution)/shard_map/ppermute | solution.py:306
  62.0 0.7 collective-permute-done.6.b_ref
  62.7 0.6 collective-permute-start.8
  63.4 0.4 collective-permute-start.9
  63.8 0.5 collective-permute-start.11
  64.3 0.0 collective-permute-done.5.sibling_f
  64.3 1.1 %shard_map.136 = bf16[2560,256]{1,0:T(8,128)(2,1)S(1)} custom-call(s32[3]{0:T(128)S(1)} %pad_add_fusion.1.numbers, bf16[8,192,128]{2,1,0:T(8,128)(2,1)S(1)} %all-to-all-done.1.in_ref.own_f, bf16[8,192,128]{2,1,0:T(8,128)(2,1)S(1)} %collective-permute-done.5.sibling_f, bf16[8,32,128]{2,1,0:T(8,128)(2,1)S(1)} %collective-permute-done.6.b_ref, ...), custom_call_target="tpu_custom_call" | custom-call | tf_op jit(solution)/shard_map/pallas_call | solution.py:454
  65.4 1.0 %convolution_convert_fusion.3 = bf16[640,256]{1,0:T(8,128)(2,1)S(1)} fusion(bf16[640,2560]{1,0:T(8,128)(2,1)S(1)} %copy-done.2, bf16[2560,256]{1,0:T(8,128)(2,1)S(1)} %shard_map.136), kind=kOutput, calls=%fused_computation.3 | convolution fusion | flops 839024640 | bytes 4915200 | tf_op jit(solution)/shard_map/dot_general | solution.py:462
  66.4 1.6 %collective-permute-start.10 = (bf16[640,256]{1,0:T(8,128)(2,1)S(1)}, bf16[640,256]{1,0:T(8,128)(2,1)S(1)}, u32[]{:S(2)}, u32[]{:S(2)}) collective-permute-start(bf16[640,256]{1,0:T(8,128)(2,1)S(1)} %convolution_convert_fusion.3), channel_id=1, source_target_pairs={{0,2},{1,3},{2,0},{3,1},{4,6},{5,7},{6,4},{7,5},{8,10},{9,11},{10,... | collective-permute-start | bytes 983048 | tf_op jit(solution)/shard_map/ppermute | solution.py:306
  68.0 1.0 %convolution_convert_fusion.2 = bf16[640,256]{1,0:T(8,128)(2,1)S(1)} fusion(bf16[640,2560]{1,0:T(8,128)(2,1)S(1)} %copy-done.4, bf16[2560,256]{1,0:T(8,128)(2,1)S(1)} %shard_map.136), kind=kOutput, calls=%fused_computation.2 | convolution fusion | flops 839024640 | bytes 4915200 | tf_op jit(solution)/shard_map/dot_general | solution.py:462
  69.0 2.5 %collective-permute-done.8.refs_1_ = bf16[1280,128]{1,0:T(8,128)(2,1)S(1)} collective-permute-done((bf16[1280,128]{1,0:T(8,128)(2,1)S(1)}, bf16[1280,128]{1,0:T(8,128)(2,1)S(1)}, u32[]{:S(2)}, u32[]{:S(2)}) %collective-permute-start.8) | collective-permute-done | bytes 327712 | tf_op jit(solution)/shard_map/ppermute | solution.py:418
  71.5 1.0 collective-permute-done.9.refs_3_
  72.5 1.1 %shard_map.138 = bf16[2560,256]{1,0:T(8,128)(2,1)S(1)} custom-call(s32[3]{0:T(128)S(1)} %pad_add_fusion.1.numbers, bf16[8,192,128]{2,1,0:T(8,128)(2,1)S(1)} %all-to-all-done.1.in_ref.own_f, bf16[8,192,128]{2,1,0:T(8,128)(2,1)S(1)} %collective-permute-done.5.sibling_f, bf16[8,32,128]{2,1,0:T(8,128)(2,1)S(1)} %collective-permute-done.6.b_ref, ...), custom_call_target="tpu_custom_call" | custom-call | tf_op jit(solution)/shard_map/pallas_call | solution.py:454
  73.7 0.0 slice-start.1
  73.7 1.0 %convolution_convert_fusion.1 = bf16[640,256]{1,0:T(8,128)(2,1)S(1)} fusion(bf16[640,2560]{1,0:T(8,128)(2,1)S(1)} %copy-done.2, bf16[2560,256]{1,0:T(8,128)(2,1)S(1)} %shard_map.138), kind=kOutput, calls=%fused_computation.1 | convolution fusion | flops 839024640 | bytes 4915200 | tf_op jit(solution)/shard_map/dot_general | solution.py:462
  74.7 1.0 %convolution_convert_fusion = bf16[640,256]{1,0:T(8,128)(2,1)S(1)} fusion(bf16[640,2560]{1,0:T(8,128)(2,1)S(1)} %copy-done.4, bf16[2560,256]{1,0:T(8,128)(2,1)S(1)} %shard_map.138), kind=kOutput, calls=%fused_computation | convolution fusion | flops 839024640 | bytes 4915200 | tf_op jit(solution)/shard_map/dot_general | solution.py:462
  75.7 0.6 collective-permute-start.14
  76.3 1.5 %collective-permute-start.12 = (bf16[640,256]{1,0:T(8,128)(2,1)S(1)}, bf16[640,256]{1,0:T(8,128)(2,1)S(1)}, u32[]{:S(2)}, u32[]{:S(2)}) collective-permute-start(bf16[640,256]{1,0:T(8,128)(2,1)S(1)} %convolution_convert_fusion), channel_id=1, source_target_pairs={{0,2},{1,3},{2,0},{3,1},{4,6},{5,7},{6,4},{7,5},{8,10},{9,11},{10,... | collective-permute-start | bytes 983048 | tf_op jit(solution)/shard_map/ppermute | solution.py:306
  77.8 0.5 collective-permute-start.13
  78.4 0.0 collective-permute-done.11
  78.4 0.0 collective-permute-done.10.refs_0_
  78.4 6.5 %shard_map.139 = (f32[1280,256]{1,0:T(8,128)S(1)}, f32[1280,256]{1,0:T(8,128)S(1)}) custom-call(s32[3]{0:T(128)S(1)} %pad_add_fusion.numbers, bf16[5120,512]{1,0:T(8,128)(2,1)S(1)} %bitcast.34, bf16[5120,512]{1,0:T(8,128)(2,1)S(1)} %bitcast.34, bf16[8,192,128]{2,1,0:T(8,128)(2,1)S(1)} %all-to-all-done.1.in_ref.own_f, ...), custom_call_target="tpu_custom_call" | custom-call | flops 3355443200 | bytes 6553600 | tf_op jit(solution)/shard_map/pallas_call | solution.py:469
  85.0 0.2 broadcast_in_dim.14.inv
  85.2 0.9 shard_map.140.refs_1_
  86.1 0.4 collective-permute-done.14.refs_0_
  86.5 0.9 shard_map.141.refs_1_
  87.3 10.7 %collective-permute-done.13.refs_0_ = bf16[640,256]{1,0:T(8,128)(2,1)S(1)} collective-permute-done((bf16[640,256]{1,0:T(8,128)(2,1)S(1)}, bf16[640,256]{1,0:T(8,128)(2,1)S(1)}, u32[]{:S(2)}, u32[]{:S(2)}) %collective-permute-start.13) | collective-permute-done | bytes 327712 | tf_op jit(solution)/shard_map/ppermute | solution.py:306
  98.1 0.9 shard_map.142.refs_1_
  99.0 0.9 shard_map.143
  (33 shorter events, 0.1 us)
Async XLA Ops:
  0.6 17.4 %collective-permute-start = (bf16[1280,1280]{1,0:T(8,128)(2,1)}, bf16[1280,1280]{1,0:T(8,128)(2,1)}, u32[]{:S(2)}, u32[]{:S(2)}) collective-permute-start(bf16[1280,1280]{1,0:T(8,128)(2,1)} %own_ref.1), channel_id=1, source_target_pairs={{0,1},{1,0},{2,3},{3,2},{4,5},{5,4},{6,7},{7,6},{8,9},{9,8},{10,11... | collective-permute-start | bytes 9830408 | tf_op jit(solution)/shard_map/ppermute | solution.py:298
  1.1 1.1 %copy-start.6 = (f32[1,1280,2,64]{1,3,2,0:T(8,128)S(1)}, f32[1,1280,2,64]{1,3,2,0:T(8,128)}, u32[]{:S(2)}) copy-start(f32[1,1280,2,64]{1,3,2,0:T(8,128)} %param.20) | copy-start | bytes 1966084
  2.2 0.9 copy-start.13
  4.1 24.0 %all-to-all-start = ((bf16[8,192,128]{2,1,0:T(8,128)(2,1)}), bf16[8,192,128]{2,1,0:T(8,128)(2,1)}, u32[]{:S(2)}, u32[]{:S(2)}) async-start(bf16[8,192,128]{2,1,0:T(8,128)(2,1)} %get-tuple-element.28), calls=%async_computation | async-start | bytes 786432 | tf_op jit(solution)/shard_map/all_to_all | solution.py:372
  10.9 2.5 %copy-start = (bf16[5120,512]{1,0:T(8,128)(2,1)S(1)}, bf16[5120,512]{1,0:T(8,128)(2,1)}, u32[]{:S(2)}) copy-start(bf16[5120,512]{1,0:T(8,128)(2,1)} %sibling_block.1) | copy-start | bytes 15728644
  13.4 3.4 %copy-start.16 = (f32[1280]{0:T(1024)S(1)}, f32[1280]{0:T(1024)}, u32[]{:S(2)}) copy-start(f32[1280]{0:T(1024)} %param.12) | copy-start | bytes 15364
  13.4 4.6 %copy-start.5 = (bf16[1280,1280]{1,0:T(8,128)(2,1)S(1)}, bf16[1280,1280]{1,0:T(8,128)(2,1)}, u32[]{:S(2)}) copy-start(bf16[1280,1280]{1,0:T(8,128)(2,1)} %own_ref.1) | copy-start | bytes 9830404
  14.5 0.8 copy-start.14
  15.3 25.6 %collective-permute-start.2 = (bf16[2,1280,128]{2,1,0:T(8,128)(2,1)}, bf16[2,1280,128]{2,1,0:T(8,128)(2,1)}, u32[]{:S(2)}, u32[]{:S(2)}) collective-permute-start(bf16[2,1280,128]{2,1,0:T(8,128)(2,1)} %get-tuple-element.36), channel_id=1, source_target_pairs={{0,2},{1,3},{2,0},{3,1},{4,6},{5,7},{6,4},{7,5},{8,10},{9,11},{10,... | collective-permute-start | bytes 1966088 | tf_op jit(solution)/shard_map/ppermute | solution.py:306
  16.8 1.2 %collective-permute-start.1 = (f32[1,1280]{1,0:T(1,128)S(1)}, f32[1,1280]{1,0:T(1,128)S(1)}, u32[]{:S(2)}, u32[]{:S(2)}) collective-permute-start(f32[1,1280]{1,0:T(1,128)S(1)} %broadcast_in_dim.13.own_gain), channel_id=1, source_target_pairs={{0,1},{1,0},{2,3},{3,2},{4,5},{5,4},{6,7},{7,6},{8,9},{9,8},{10,11... | collective-permute-start | bytes 15368 | tf_op jit(solution)/shard_map/ppermute | solution.py:298
  16.8 11.2 %copy-start.10 = (f32[64,512]{1,0:T(8,128)S(1)}, f32[64,512]{1,0:T(8,128)}, u32[]{:S(2)}) copy-start(f32[64,512]{1,0:T(8,128)} %refs_3_.1) | copy-start | bytes 393220
  16.9 11.2 %copy-start.11 = (f32[64,512]{1,0:T(8,128)S(1)}, f32[64,512]{1,0:T(8,128)}, u32[]{:S(2)}) copy-start(f32[64,512]{1,0:T(8,128)} %refs_4_.1) | copy-start | bytes 393220
  24.4 1.7 %copy-start.1 = (bf16[640,2560]{1,0:T(8,128)(2,1)}, bf16[640,2560]{1,0:T(8,128)(2,1)S(1)}, u32[]{:S(2)}) copy-start(bf16[640,2560]{1,0:T(8,128)(2,1)S(1)} %get-tuple-element.33.refs_0_) | copy-start | bytes 9830404
  26.1 1.7 %copy-start.3 = (bf16[640,2560]{1,0:T(8,128)(2,1)}, bf16[640,2560]{1,0:T(8,128)(2,1)S(1)}, u32[]{:S(2)}) copy-start(bf16[640,2560]{1,0:T(8,128)(2,1)S(1)} %get-tuple-element.41.refs_1_) | copy-start | bytes 9830404
  28.1 1.1 %copy-start.7 = (f32[1280,2,64]{0,2,1:T(8,128)S(1)}, f32[1280,2,64]{0,2,1:T(8,128)}, u32[]{:S(2)}) copy-start(f32[1280,2,64]{0,2,1:T(8,128)} %param.14) | copy-start | bytes 1966084
  29.2 1.1 %copy-start.8 = (f32[1280,2,64]{0,2,1:T(8,128)S(1)}, f32[1280,2,64]{0,2,1:T(8,128)}, u32[]{:S(2)}) copy-start(f32[1280,2,64]{0,2,1:T(8,128)} %param.15) | copy-start | bytes 1966084
  30.3 1.1 %copy-start.9 = (f32[1280,2,64]{0,2,1:T(8,128)S(1)}, f32[1280,2,64]{0,2,1:T(8,128)}, u32[]{:S(2)}) copy-start(f32[1280,2,64]{0,2,1:T(8,128)} %param.16) | copy-start | bytes 1966084
  31.3 0.9 copy-start.12
  34.8 10.8 %copy-start.15 = (bf16[2,1280,128]{2,1,0:T(8,128)(2,1)S(1)}, bf16[2,1280,128]{2,1,0:T(8,128)(2,1)}, u32[]{:S(2)}) copy-start(bf16[2,1280,128]{2,1,0:T(8,128)(2,1)} %copy-done.14) | copy-start | bytes 1966084
  34.8 22.2 %all-to-all-start.1 = ((bf16[8,192,128]{2,1,0:T(8,128)(2,1)}), bf16[8,192,128]{2,1,0:T(8,128)(2,1)S(1)}, u32[]{:S(2)}, u32[]{:S(2)}) async-start(bf16[8,192,128]{2,1,0:T(8,128)(2,1)} %get-tuple-element.34), calls=%async_computation.1 | async-start | bytes 786432 | tf_op jit(solution)/shard_map/all_to_all | solution.py:399
  42.1 13.3 %collective-permute-start.3 = (bf16[1280,128]{1,0:T(8,128)(2,1)S(1)}, bf16[1280,128]{1,0:T(8,128)(2,1)S(1)}, u32[]{:S(2)}, u32[]{:S(2)}) collective-permute-start(bf16[1280,128]{1,0:T(8,128)(2,1)S(1)} %get-tuple-element.38.refs_0_), channel_id=1, source_target_pairs={{0,4},{4,0},{8,12},{12,8},{16,20},{20,16},{24,28},{28,24},{1,5},{5... | collective-permute-start | bytes 983048 | tf_op jit(solution)/shard_map/ppermute | solution.py:418
  44.1 12.9 %collective-permute-start.4 = (bf16[1280,128]{1,0:T(8,128)(2,1)S(1)}, bf16[1280,128]{1,0:T(8,128)(2,1)S(1)}, u32[]{:S(2)}, u32[]{:S(2)}) collective-permute-start(bf16[1280,128]{1,0:T(8,128)(2,1)S(1)} %get-tuple-element.39.refs_2_), channel_id=1, source_target_pairs={{0,8},{4,12},{8,0},{12,4},{16,24},{20,28},{24,16},{28,20},{1,9},{5... | collective-permute-start | bytes 983048 | tf_op jit(solution)/shard_map/ppermute | solution.py:418
  45.6 16.4 %collective-permute-start.7 = (bf16[2,1280,128]{2,1,0:T(8,128)(2,1)S(1)}, bf16[2,1280,128]{2,1,0:T(8,128)(2,1)S(1)}, u32[]{:S(2)}, u32[]{:S(2)}) collective-permute-start(bf16[2,1280,128]{2,1,0:T(8,128)(2,1)S(1)} %copy-done.15), channel_id=1, source_target_pairs={{0,2},{1,3},{2,0},{3,1},{4,6},{5,7},{6,4},{7,5},{8,10},{9,11},{10,... | collective-permute-start | bytes 1966088 | tf_op jit(solution)/shard_map/ppermute | solution.py:306
  57.0 7.3 %collective-permute-start.5 = (bf16[8,192,128]{2,1,0:T(8,128)(2,1)S(1)}, bf16[8,192,128]{2,1,0:T(8,128)(2,1)S(1)}, u32[]{:S(2)}, u32[]{:S(2)}) collective-permute-start(bf16[8,192,128]{2,1,0:T(8,128)(2,1)S(1)} %all-to-all-done.1.in_ref.own_f), channel_id=1, source_target_pairs={{0,1},{1,0},{2,3},{3,2},{4,5},{5,4},{6,7},{7,6},{8,9},{9,8},{10,11... | collective-permute-start | bytes 1179656 | tf_op jit(solution)/shard_map/ppermute | solution.py:298
  57.1 5.6 %collective-permute-start.6 = (bf16[8,32,128]{2,1,0:T(8,128)(2,1)S(1)}, bf16[8,32,128]{2,1,0:T(8,128)(2,1)S(1)}, u32[]{:S(2)}, u32[]{:S(2)}) collective-permute-start(bf16[8,32,128]{2,1,0:T(8,128)(2,1)S(1)} %shard_map.135), channel_id=1, source_target_pairs={{0,2},{1,3},{2,0},{3,1},{4,6},{5,7},{6,4},{7,5},{8,10},{9,11},{10,... | collective-permute-start | bytes 196616 | tf_op jit(solution)/shard_map/ppermute | solution.py:306
  62.7 8.8 %collective-permute-start.8 = (bf16[1280,128]{1,0:T(8,128)(2,1)S(1)}, bf16[1280,128]{1,0:T(8,128)(2,1)S(1)}, u32[]{:S(2)}, u32[]{:S(2)}) collective-permute-start(bf16[1280,128]{1,0:T(8,128)(2,1)S(1)} %get-tuple-element.46.refs_0_), channel_id=1, source_target_pairs={{0,4},{4,0},{8,12},{12,8},{16,20},{20,16},{24,28},{28,24},{1,5},{5... | collective-permute-start | bytes 983048 | tf_op jit(solution)/shard_map/ppermute | solution.py:418
  63.4 2.0 %copy-start.2 = (bf16[640,2560]{1,0:T(8,128)(2,1)S(1)}, bf16[640,2560]{1,0:T(8,128)(2,1)}, u32[]{:S(2)}) copy-start(bf16[640,2560]{1,0:T(8,128)(2,1)} %copy-done.1) | copy-start | bytes 9830404
  63.4 9.2 %collective-permute-start.9 = (bf16[1280,128]{1,0:T(8,128)(2,1)S(1)}, bf16[1280,128]{1,0:T(8,128)(2,1)S(1)}, u32[]{:S(2)}, u32[]{:S(2)}) collective-permute-start(bf16[1280,128]{1,0:T(8,128)(2,1)S(1)} %get-tuple-element.47.refs_2_), channel_id=1, source_target_pairs={{0,8},{4,12},{8,0},{12,4},{16,24},{20,28},{24,16},{28,20},{1,9},{5... | collective-permute-start | bytes 983048 | tf_op jit(solution)/shard_map/ppermute | solution.py:418
  63.8 14.6 %collective-permute-start.11 = (f32[1280]{0:T(1024)S(1)}, f32[1280]{0:T(1024)S(1)}, u32[]{:S(2)}, u32[]{:S(2)}) collective-permute-start(f32[1280]{0:T(1024)S(1)} %slice_reduce_fusion), channel_id=1, source_target_pairs={{0,2},{1,3},{2,0},{3,1},{4,6},{5,7},{6,4},{7,5},{8,10},{9,11},{10,... | collective-permute-start | bytes 15368 | tf_op jit(solution)/shard_map/ppermute | solution.py:306
  65.4 2.6 %copy-start.4 = (bf16[640,2560]{1,0:T(8,128)(2,1)S(1)}, bf16[640,2560]{1,0:T(8,128)(2,1)}, u32[]{:S(2)}) copy-start(bf16[640,2560]{1,0:T(8,128)(2,1)} %copy-done.3) | copy-start | bytes 9830404
  66.4 11.9 %collective-permute-start.10 = (bf16[640,256]{1,0:T(8,128)(2,1)S(1)}, bf16[640,256]{1,0:T(8,128)(2,1)S(1)}, u32[]{:S(2)}, u32[]{:S(2)}) collective-permute-start(bf16[640,256]{1,0:T(8,128)(2,1)S(1)} %convolution_convert_fusion.3), channel_id=1, source_target_pairs={{0,2},{1,3},{2,0},{3,1},{4,6},{5,7},{6,4},{7,5},{8,10},{9,11},{10,... | collective-permute-start | bytes 983048 | tf_op jit(solution)/shard_map/ppermute | solution.py:306
  72.5 5.9 %slice-start = ((s8[5242880]{0:T(1024)(128)(4,1)}), s8[4194304]{0:T(1024)(128)(4,1)S(1)}, s32[]{:S(2)}) async-start(s8[5242880]{0:T(1024)(128)(4,1)} %bitcast.33), calls=%async_computation.2 | async-start | bytes 8388608
  73.7 4.7 %slice-start.1 = ((s8[5242880]{0:T(1024)(128)(4,1)}), s8[1048576]{0:T(1024)(128)(4,1)S(1)}, s32[]{:S(2)}) async-start(s8[5242880]{0:T(1024)(128)(4,1)} %bitcast.33), calls=%async_computation.3 | async-start | bytes 2097152
  75.7 10.7 %collective-permute-start.14 = (bf16[640,256]{1,0:T(8,128)(2,1)S(1)}, bf16[640,256]{1,0:T(8,128)(2,1)S(1)}, u32[]{:S(2)}, u32[]{:S(2)}) collective-permute-start(bf16[640,256]{1,0:T(8,128)(2,1)S(1)} %convolution_convert_fusion.2), channel_id=1, source_target_pairs={{0,2},{1,3},{2,0},{3,1},{4,6},{5,7},{6,4},{7,5},{8,10},{9,11},{10,... | collective-permute-start | bytes 983048 | tf_op jit(solution)/shard_map/ppermute | solution.py:306
  76.3 22.6 %collective-permute-start.12 = (bf16[640,256]{1,0:T(8,128)(2,1)S(1)}, bf16[640,256]{1,0:T(8,128)(2,1)S(1)}, u32[]{:S(2)}, u32[]{:S(2)}) collective-permute-start(bf16[640,256]{1,0:T(8,128)(2,1)S(1)} %convolution_convert_fusion), channel_id=1, source_target_pairs={{0,2},{1,3},{2,0},{3,1},{4,6},{5,7},{6,4},{7,5},{8,10},{9,11},{10,... | collective-permute-start | bytes 983048 | tf_op jit(solution)/shard_map/ppermute | solution.py:306
  77.8 20.3 %collective-permute-start.13 = (bf16[640,256]{1,0:T(8,128)(2,1)S(1)}, bf16[640,256]{1,0:T(8,128)(2,1)S(1)}, u32[]{:S(2)}, u32[]{:S(2)}) collective-permute-start(bf16[640,256]{1,0:T(8,128)(2,1)S(1)} %convolution_convert_fusion.1), channel_id=1, source_target_pairs={{0,2},{1,3},{2,0},{3,1},{4,6},{5,7},{6,4},{7,5},{8,10},{9,11},{10,... | collective-permute-start | bytes 983048 | tf_op jit(solution)/shard_map/ppermute | solution.py:306

commit v10 on v9

v10 whole, which is shorter than its diff:
```python
import functools
import math

import jax
import jax.numpy as jnp
from jax import lax
from jax.experimental import pallas as pl
from jax.experimental.pallas import tpu as pltpu
from jax.sharding import PartitionSpec as P

KEY_VALUE_WIDTH = 1024
STEP = 100
CORES = 2
LANES = 128
COLUMN_HALVES = 2
TOKEN_HALVES = 2
VMEM_BYTES = 16 * 2**20
BEGIN_VMEM_BYTES = 58 * 2**20


def adaptive_moment_update(param, first, second, grad_mean):
    first_new = 0.9 * first + 0.1 * grad_mean
    second_new = 0.999 * second + 0.001 * grad_mean * grad_mean
    step_size = first_new / (1.0 - 0.9**STEP) / (jnp.sqrt(second_new / (1.0 - 0.999**STEP)) + 1e-08)
    return (param - 0.1 * step_size, first_new, second_new)


def in_vmem(count):
    return [pl.BlockSpec(memory_space=pltpu.VMEM)] * count


def anywhere(count):
    return [pl.BlockSpec(memory_space=pl.ANY)] * count


SCALARS = pl.BlockSpec(memory_space=pltpu.SMEM)


def params(**more):
    return pltpu.CompilerParams(vmem_limit_bytes=VMEM_BYTES, **more)


def pack(down, up, out_ref):
    shares = out_ref.shape[0]
    down = down.T
    down_rows, up_rows = down.shape[0] // shares, up.shape[0] // shares
    for i in range(shares):
        pieces = [down[i * down_rows : (i + 1) * down_rows]]
        for k in range(up.shape[1] // LANES):
            pieces.append(up[i * up_rows : (i + 1) * up_rows, k * LANES : (k + 1) * LANES])
        out_ref[i] = jnp.concatenate(pieces, axis=0).astype(jnp.bfloat16)


def first_lane(share, window, size):
    return jnp.minimum(share // LANES * LANES, size - window)


def begin_kernel(chips, turn, aligned, *refs):
    down_ref, up_ref, weights_ref = refs[:3]
    state, refs = refs[3 : 3 + 6 * aligned], refs[3 + 6 * aligned :]
    packed, refs = refs[0], refs[1:]
    windows, refs = refs[: 2 * aligned], refs[2 * aligned :]
    outs, (down, up, sem) = refs[:-3], refs[-3:]
    features = outs[0].shape[1]
    place, replica = lax.axis_index("tensor"), lax.axis_index("dp")
    chip, core = place // CORES, place % CORES
    copies = []

    def add(source, target):
        copies.append(pltpu.make_async_copy(source, target, sem.at[len(copies)]))
        copies[-1].start()

    add(down_ref, down)
    add(up_ref, up)
    for i, out in enumerate(outs):
        step, first = 1 + i % (chips - 1), i // (chips - 1) * out.shape[0]
        for k in range(out.shape[0]):
            half = (core + replica // turn[first + k]) % 2
            row = ((chip + step) % chips * CORES + half) * features
            add(
                weights_ref.at[
                    pl.ds(pl.multiple_of(row, features), features),
                    pl.ds((first + k) * LANES, LANES),
                ],
                out.at[k],
            )
    if aligned:
        down_win, up_win = windows
        window, up_rows = down_win.shape[2], up_win.shape[1]
        share = replica * (features // packed.shape[0])
        lane = pl.multiple_of(first_lane(share, window, features), LANES)
        row = pl.multiple_of(replica * up_rows, up_rows)
        for i in range(3):
            add(state[i].at[:, pl.ds(lane, window)], down_win.at[i])
            add(state[3 + i].at[pl.ds(row, up_rows)], up_win.at[i])
    copies[0].wait()
    copies[1].wait()
    pack(down[...], up[...], packed)
    for copy in copies[2:]:
        copy.wait()


def split_kernel(in_ref, *outs):
    for k, out in enumerate(outs):
        out[...] = in_ref[k]


def prepare_kernel(first, own_ref, sibling_ref, own_gain, sibling_gain, *refs):
    x_ref, sums_ref, squares = refs[-3:]
    features = own_ref.shape[1]
    rows = x_ref.shape[0]
    tile = 16 if rows % 16 == 0 else rows

    @pl.loop(0, rows // tile, unroll=2)
    def _(i):
        to = pl.ds(pl.multiple_of(i * tile, tile), tile)
        at = pl.ds(pl.multiple_of(first + i * tile, tile), tile)
        own = own_ref[at, :].astype(jnp.float32)
        x_ref[to, :features] = (own * own_gain[...]).astype(x_ref.dtype)
        total = own * own
        sibling = sibling_ref[at, :].astype(jnp.float32)
        x_ref[to, features:] = (sibling * sibling_gain[...]).astype(x_ref.dtype)
        total += sibling * sibling
        total = jnp.sum(total, axis=1, keepdims=True)
        squares[to, :] = jnp.broadcast_to(total, (tile, LANES))

    for ref in refs[:-3]:
        sums_ref[: ref.shape[0]] = ref[...]
    for i in range(rows // LANES):
        at = first // LANES + i
        sums_ref[at : at + 1] = squares[i * LANES : (i + 1) * LANES, :].T[:1]


def inverse_kernel(width, *refs):
    out = refs[-1]
    total = refs[0][...]
    for ref in refs[1:-1]:
        total = total + ref[...]
    inverse = lax.rsqrt(total / width + 1e-06)
    for i in range(inverse.shape[0]):
        out[i * LANES : (i + 1) * LANES, :] = jnp.broadcast_to(
            inverse[i : i + 1], (LANES, LANES)
        ).T


def tail_kernel(in_ref, out_ref):
    out_ref[...] = in_ref[:, in_ref.shape[1] - out_ref.shape[1] :]


def update(total, down, up, a_ref, b_ref):
    down_rows = a_ref.shape[2]
    up_rows, columns = b_ref.shape[1:]
    strips = columns // LANES
    down_mean = total[:down_rows].T
    up_mean = jnp.concatenate(
        [total[down_rows + k * up_rows : down_rows + (k + 1) * up_rows] for k in range(strips)],
        axis=1,
    )
    p, m, v = adaptive_moment_update(*down(), down_mean)
    a_ref[0], a_ref[1], a_ref[2] = p, m, v
    pieces = [p.T]
    p, m, v = adaptive_moment_update(*up(), up_mean)
    b_ref[0], b_ref[1], b_ref[2] = p, m, v
    pieces += [p[:, k * LANES : (k + 1) * LANES] for k in range(strips)]
    return jnp.concatenate(pieces, axis=0).astype(jnp.bfloat16)


def adam_kernel(grad_ref, down_win, up_win, a_ref, b_ref, factor_ref):
    replicas = grad_ref.shape[0]
    down_rows, window = a_ref.shape[2], down_win.shape[2]
    total = jnp.sum(grad_ref[...].astype(jnp.float32), axis=0) / replicas

    def down():
        if window == down_rows:
            return [down_win[i] for i in range(3)]
        share = lax.axis_index("dp") * down_rows
        shift = window - (share - first_lane(share, window, down_rows * replicas))
        return [pltpu.roll(down_win[i], shift, 1)[:, :down_rows] for i in range(3)]

    rounded = update(total, down, lambda: [up_win[i] for i in range(3)], a_ref, b_ref)
    for i in range(replicas):
        factor_ref[i] = rounded


def factor_a(packed_ref, down_rows):
    pieces = [packed_ref[i].astype(jnp.float32)[:down_rows] for i in range(packed_ref.shape[0])]
    return jnp.concatenate(pieces, axis=0).astype(jnp.bfloat16)


def factor_b(packed, part, parts, strip, up_rows):
    pieces = [
        packed[i].astype(jnp.float32)[strip * up_rows : (strip + 1) * up_rows]
        for i in range(packed.shape[0])
    ]
    value = jnp.concatenate(pieces, axis=0)
    rows = [jnp.where(part == j, value, jnp.zeros_like(value)) for j in range(parts)]
    return jnp.concatenate(rows, axis=0).astype(jnp.bfloat16)


def merge(scale, block, a, b):
    change = jnp.dot(a, b, preferred_element_type=jnp.float32)
    return (block.astype(jnp.float32) + scale * change).astype(jnp.bfloat16)


def multiply(x, weights, store):
    rows = x.shape[0]
    tile = rows // 2 if rows % 32 == 0 else rows

    @pl.loop(0, rows // tile)
    def _(i):
        at = pl.ds(pl.multiple_of(i * tile, tile), tile)
        store(i * tile, tile, jnp.dot(x[at, :], weights[...], preferred_element_type=jnp.float32))


def up_factor(static, packed, owner):
    _, parts, up_rows, strips, columns = static
    part = owner * columns // KEY_VALUE_WIDTH
    return jnp.concatenate(
        [factor_b(packed, part, parts, strip, up_rows) for strip in strips], axis=1
    )


def outside_kernel(static, chips, step, turn, own_f, sibling_f, b_ref, x, *refs):
    weights, product = refs[-2:]
    strips = static[3]
    features = refs[0].shape[0]
    down_rows = own_f.shape[1] - b_ref.shape[1]
    place, replica = lax.axis_index("tensor"), lax.axis_index("dp")
    owner = (place // CORES - step + chips) % chips * CORES + place % CORES
    b = up_factor(static, b_ref[...], owner)
    own_a, sibling_a = factor_a(own_f, down_rows), factor_a(sibling_f, down_rows)
    for k, strip in enumerate(strips):
        mine, other = refs[2 * k : 2 * k + 2]
        even = replica // turn[strip] % 2 == 0
        lanes = slice(k * LANES, (k + 1) * LANES)
        block = jnp.where(even, mine[...], other[...])
        weights[:features, lanes] = merge(static[0], block, own_a, b[:, lanes])
        block = jnp.where(even, other[...], mine[...])
        weights[features:, lanes] = merge(static[0], block, sibling_a, b[:, lanes])
    more_kernel(x, weights, product)


def more_kernel(x, weights, product):
    def store(first, size, value):
        product[pl.ds(first, size), :] = value.astype(product.dtype)

    multiply(x, weights, store)


def own_kernel(static, own_f, sibling_f, own_block, sibling_block, *refs):
    xs, weights = refs[: static[5]], refs[-1]
    outs = refs[len(refs) - 1 - static[6] : -1]
    features = own_block.shape[0]
    wide = outs[0].shape[1]
    down_rows = own_f.shape[1] - len(static[3]) * static[2]
    b = up_factor(static[:5], own_f[:, down_rows:], lax.axis_index("tensor"))
    for at, factors, block in ((0, own_f, own_block), (features, sibling_f, sibling_block)):
        weights[at : at + features] = merge(static[0], block[...], factor_a(factors, down_rows), b)
    for h, x in enumerate(xs):

        def store(first, size, value):
            to = pl.ds(pl.multiple_of(h * x.shape[0] + first, 16), size)
            for k, out in enumerate(outs):
                out[to, :] = value[:, k * wide : (k + 1) * wide]

        multiply(x, weights, store)


def finish_kernel(sources, first, own, inv, *refs):
    rows = pl.ds(first, refs[-1].shape[0])
    total = own[rows, :]
    for value in refs[:sources]:
        total = total + value[...].astype(jnp.float32)
    refs[-1][...] = (total * inv[rows, :1]).astype(refs[-1].dtype)


def finish(own, inv_rms, received, at, shape, before):
    block = received[0].shape
    operands = [own, inv_rms] + received
    in_specs = in_vmem(len(operands))
    aliases = {}
    if before is not None:
        aliases = {len(operands): 0}
        in_specs += anywhere(1)
        operands.append(before)
    return pl.pallas_call(
        functools.partial(finish_kernel, len(received), at[0] * block[0]),
        grid=(1,),
        out_shape=jax.ShapeDtypeStruct(shape, jnp.bfloat16),
        in_specs=in_specs,
        out_specs=pl.BlockSpec(block, lambda i: at),
        input_output_aliases=aliases,
        compiler_params=params(),
    )(*operands)


def body(
    prompt_hidden_input,
    input_norm_gain,
    frozen_key_value,
    down_factor_matrix,
    down_moment_first,
    down_moment_second,
    up_factor_matrix,
    up_moment_first,
    up_moment_second,
    down_gradient,
    up_gradient,
):
    n_dp = lax.axis_size("dp")
    n_tensor = lax.axis_size("tensor")
    chips = n_tensor // CORES
    replica = lax.axis_index("dp")
    tokens, features = prompt_hidden_input.shape
    width, columns = frozen_key_value.shape
    rank = up_factor_matrix.shape[0]
    parts = down_factor_matrix.shape[1]
    factors = parts * rank
    strips = columns // LANES
    down_rows = features // n_dp
    up_rows = rank // n_dp
    packed_rows = down_rows + up_rows * strips
    steps = range(1, chips)
    f32, bf16 = jnp.float32, jnp.bfloat16

    def to_sibling(value):
        return lax.ppermute(value, "tensor", [(t, t ^ 1) for t in range(n_tensor)])

    def to_chip(value, step):
        pairs = [
            (CORES * q + k, CORES * ((q + step) % chips) + k)
            for q in range(chips)
            for k in range(CORES)
        ]
        return lax.ppermute(value, "tensor", pairs)

    def by_rank(value):
        return jnp.transpose(value, (1, 2, 0)).reshape(factors, features)

    down_sent = by_rank(down_gradient[0])
    down_state = [by_rank(v) for v in (down_factor_matrix, down_moment_first, down_moment_second)]
    up_state = [up_factor_matrix, up_moment_first, up_moment_second]
    shares = jax.ShapeDtypeStruct((n_dp, packed_rows, LANES), bf16)
    window = pl.cdiv(down_rows + LANES, LANES) * LANES
    aligned = features % LANES == 0 and window <= features
    aligned = aligned and up_rows % 8 == 0 and down_rows % 16 == 0
    window = window if aligned else down_rows
    windows = (
        jax.ShapeDtypeStruct((3, factors, window), f32),
        jax.ShapeDtypeStruct((3, up_rows, columns), f32),
    )

    turns = [1, 2] if n_dp % 4 == 0 else [1, 1]
    turn = [turns[strip % 2] for strip in range(strips)]
    halves = min(COLUMN_HALVES, strips)
    wide = columns // halves
    groups = [range(k * strips // halves, (k + 1) * strips // halves) for k in range(halves)]
    out_shape = (shares,) + windows * aligned
    out_shape += tuple(
        jax.ShapeDtypeStruct((len(group), features, LANES), bf16)
        for group in groups
        for _ in steps
    )
    state = (down_state + up_state) * aligned
    packed, *rest = pl.pallas_call(
        functools.partial(begin_kernel, chips, turn, aligned),
        out_shape=out_shape,
        in_specs=anywhere(3 + len(state)),
        out_specs=tuple(in_vmem(len(out_shape))),
        scratch_shapes=[
            pltpu.VMEM((factors, features), f32),
            pltpu.VMEM((rank, columns), f32),
            pltpu.SemaphoreType.DMA((2 + len(steps) * strips + len(state),)),
        ],
        compiler_params=pltpu.CompilerParams(vmem_limit_bytes=BEGIN_VMEM_BYTES),
    )(down_sent, up_gradient[0], frozen_key_value, *state)
    exchanged = lax.all_to_all(packed, "dp", 0, 0, tiled=True)
    if aligned:
        down_win, up_win, *taken = rest
    else:
        taken = rest
        down_win = jnp.stack(
            [lax.dynamic_slice_in_dim(v, replica * down_rows, down_rows, 1) for v in down_state]
        )
        up_win = jnp.stack(
            [lax.dynamic_slice_in_dim(v, replica * up_rows, up_rows, 0) for v in up_state]
        )
    mine = []

    def send_half(half, after):
        blocks = taken[half * len(steps) : (half + 1) * len(steps)]
        if after is not None:
            blocks, _ = lax.optimization_barrier((blocks, after))
        mine.append([to_chip(value, step) for value, step in zip(blocks, steps)])

    send_half(0, None)

    gain = input_norm_gain[None, :]
    operands = [prompt_hidden_input, to_sibling(prompt_hidden_input), gain, to_sibling(gain)]
    x, squares = [], None
    some = tokens // TOKEN_HALVES
    for h in range(TOKEN_HALVES):
        before = [] if squares is None else [squares]
        value, squares = pl.pallas_call(
            functools.partial(prepare_kernel, h * some),
            out_shape=(
                jax.ShapeDtypeStruct((some, CORES * features), bf16),
                jax.ShapeDtypeStruct(((h + 1) * some // LANES, LANES), f32),
            ),
            in_specs=in_vmem(4 + len(before)),
            out_specs=tuple(in_vmem(2)),
            scratch_shapes=[pltpu.VMEM((some, LANES), f32)],
            compiler_params=params(),
        )(*operands, *before)
        x.append(value)
        if h == 0:
            exchanged, squares = lax.optimization_barrier((exchanged, squares))

    a_next, b_next, sent = pl.pallas_call(
        adam_kernel,
        out_shape=(
            jax.ShapeDtypeStruct((3, factors, down_rows), f32),
            jax.ShapeDtypeStruct((3, up_rows, columns), f32),
            shares,
        ),
        in_specs=in_vmem(3),
        out_specs=tuple(in_vmem(3)),
        compiler_params=params(),
    )(exchanged, down_win, up_win)
    own_f = lax.all_to_all(sent, "dp", 0, 0, tiled=True)
    for half in range(1, halves):
        send_half(half, (mine[-1], sent))
    a_next = jnp.transpose(a_next.reshape(3, parts, rank, down_rows), (0, 3, 1, 2))

    outside = [[] for _ in range(strips)]

    def swap_half(half, after):
        for value in mine[half]:
            value, _ = lax.optimization_barrier((value, after))
            split = pl.pallas_call(
                split_kernel,
                out_shape=(jax.ShapeDtypeStruct((features, LANES), bf16),) * len(groups[half]),
                in_specs=in_vmem(1),
                out_specs=tuple(in_vmem(len(groups[half]))),
                compiler_params=params(),
            )(value)
            for piece, strip in zip(split, groups[half]):
                pairs = [(i, i ^ turn[strip]) for i in range(n_dp)]
                outside[strip].append((piece, lax.ppermute(piece, "dp", pairs)))

    swap_half(0, sent)
    own_f, squares, _ = lax.optimization_barrier((own_f, squares, outside))
    sibling_f = to_sibling(own_f)
    packed_b = pl.pallas_call(
        tail_kernel,
        out_shape=jax.ShapeDtypeStruct((n_dp, packed_rows - down_rows, LANES), bf16),
        in_specs=in_vmem(1),
        out_specs=in_vmem(1)[0],
        compiler_params=params(),
    )(own_f)
    other_b = [to_chip(packed_b, step) for step in steps]

    for half in range(1, halves):
        swap_half(half, other_b)

    squares, _ = lax.optimization_barrier((squares, other_b))
    inv_rms = pl.pallas_call(
        functools.partial(inverse_kernel, width),
        out_shape=jax.ShapeDtypeStruct((tokens, LANES), f32),
        in_specs=in_vmem(chips),
        out_specs=in_vmem(1)[0],
        compiler_params=params(),
    )(squares, *[to_chip(squares, step) for step in steps])

    scale = 0.5 / math.sqrt(width * rank)

    received = {}
    after = [inv_rms]
    weights_shape = jax.ShapeDtypeStruct((CORES * features, wide), bf16)
    product_shape = jax.ShapeDtypeStruct((some, wide), bf16)
    for half, group in enumerate(groups):
        static = (scale, parts, up_rows, group, columns)
        for step in steps:
            blocks = [value for strip in group for value in outside[strip][step - 1]]
            weights, product = pl.pallas_call(
                functools.partial(outside_kernel, static, chips, step, turn),
                out_shape=(weights_shape, product_shape),
                in_specs=in_vmem(4 + len(blocks) + len(after)),
                out_specs=tuple(in_vmem(2)),
                compiler_params=params(),
            )(own_f, sibling_f, other_b[step - 1], x[0], *blocks, *after)
            after = [product]
            received.setdefault((0, half), []).append(to_chip(product, chips - step))
            for k in range(1, TOKEN_HALVES):
                product = pl.pallas_call(
                    more_kernel,
                    out_shape=product_shape,
                    in_specs=in_vmem(2),
                    out_specs=in_vmem(1)[0],
                    compiler_params=params(),
                )(x[k], weights)
                after.append(product)
                received.setdefault((k, half), []).append(to_chip(product, chips - step))

    after.append(received[0, 0][0])
    static = (scale, parts, up_rows, range(strips), columns, TOKEN_HALVES, halves)
    totals = pl.pallas_call(
        functools.partial(own_kernel, static),
        out_shape=(jax.ShapeDtypeStruct((tokens, wide), f32),) * halves,
        grid=(1,),
        in_specs=in_vmem(2)
        + [
            pl.BlockSpec((features, columns), lambda i: (lax.axis_index("tensor"), 0)),
            pl.BlockSpec((features, columns), lambda i: (lax.axis_index("tensor") ^ 1, 0)),
        ]
        + in_vmem(TOKEN_HALVES + len(after)),
        out_specs=tuple(in_vmem(halves)),
        scratch_shapes=[pltpu.VMEM((CORES * features, columns), bf16)],
        compiler_params=params(),
        cost_estimate=pl.CostEstimate(
            flops=2 * tokens * CORES * features * columns,
            bytes_accessed=4 * tokens * features,
            transcendentals=0,
        ),
    )(own_f, sibling_f, frozen_key_value, frozen_key_value, *x, *after)

    keys_values = None
    for at, pieces in received.items():
        keys_values = finish(
            totals[at[1]], inv_rms, pieces, at, (tokens, columns), keys_values
        )
    return (a_next, b_next, keys_values)


def solution(mesh):
    placed = (
        P("dp", "tensor"),
        P("tensor"),
        P(None, "tensor"),
        P("tensor", None, None),
        P("tensor", None, None),
        P("tensor", None, None),
        P(None, "tensor"),
        P(None, "tensor"),
        P(None, "tensor"),
        P("dp", "tensor", None, None),
        P("dp", None, "tensor"),
    )
    return jax.shard_map(
        body,
        mesh=mesh,
        in_specs=placed,
        out_specs=(
            P(None, ("tensor", "dp"), None, None),
            P(None, "dp", "tensor"),
            P("dp", "tensor"),
        ),
        check_vma=False,
    )
```

time: 101 us -> 94.9 us (0.940)
  waiting for transfers between devices: 31.6 us -> 21.4 us
  Pallas kernels: 24.5 us -> 31.1 us
  matrix products: 4.04 us -> 0 us
  local copies, waits for them, and re-layouts: 13.3 us -> 14.4 us
    ppermute x4, waiting for transfers between devices: 14.4 us -> 1.42 us  [swap_half(): outside[strip].append((piece, lax.ppermute(piece, 'dp', pairs)))]
    pallas_call x7 -> x10, Pallas kernels: 19.8 us -> 24.2 us  [the longest x1 5.86 us: body(): pl.pallas_call(functools.partial(own_kernel, static), out_shape=(jax.Shap...]
    dot_general x4 -> x0, matrix products: 4.04 us -> none  [body(): jnp.dot(rows, weights, preferred_element_type=f32).astype(bf16)]
    all_to_all x1, starting transfers between devices: 6.14 us -> 4.17 us  [body(): own_f = lax.all_to_all(sent, 'dp', 0, 0, tiled=True)]
    ppermute x8, starting transfers between devices: 7.32 us -> 9.18 us  [to_chip(): return lax.ppermute(value, 'tensor', pairs)]
    all_to_all x1, waiting for transfers between devices: 0.01 us -> 1.86 us  [body(): exchanged = lax.all_to_all(packed, 'dp', 0, 0, tiled=True)]
    unnamed x38 -> x42, local copies, waits for them, and re-layouts: 12.9 us -> 14.4 us
    pallas_call x2, Pallas kernels: 1.17 us -> 2.26 us  [swap_half(): pl.pallas_call(split_kernel, out_shape=(jax.ShapeDtypeStruct((features, L...]
  transfers between devices with their start and end apart: 17 -> 17, of which waited for: 9 -> 11; matrix products, arithmetic and copies ran while one was open for 5% -> 0% of each run, Pallas kernels for 24% -> 32%
where the time goes in v10:
time: 94.9 us; the launch traced here: 94.2 us
  Pallas kernels  31.1 us (33%)
  starting transfers between devices  26.4 us (28%)
  waiting for transfers between devices  21.4 us (23%)
  local copies, waits for them, and re-layouts  14.4 us (15%)
    ppermute x8, waiting for transfers between devices, to_chip(): return lax.ppermute(value, 'tensor', pairs)  17 us
    unnamed x42, local copies, waits for them, and re-layouts  14.4 us
    ppermute x8, starting transfers between devices, to_chip(): return lax.ppermute(value, 'tensor', pairs)  9.18 us
    all_to_all x1, starting transfers between devices, body(): exchanged = lax.all_to_all(packed, 'dp', 0, 0, tiled=True)  6.88 us
    pallas_call x1, Pallas kernels, body(): pl.pallas_call(functools.partial(own_kernel, static), out_shape=(jax.Shap...  5.86 us
    pallas_call x2, Pallas kernels, body(): pl.pallas_call(functools.partial(outside_kernel, static, chips, step, tur...  5.68 us
    ppermute x4, starting transfers between devices, swap_half(): outside[strip].append((piece, lax.ppermute(piece, 'dp', pairs)))  5.61 us
    pallas_call x2, Pallas kernels, body(): pl.pallas_call(functools.partial(prepare_kernel, h * some), out_shape=(ja...  4.72 us
  transfers between devices with their start and end apart: 17, of which 11 were waited for; matrix products, arithmetic and copies ran while one was open for 0% of the time, Pallas kernels for 32%

profile of v10, /device:TPU:0, one launch (start us, length us, event | category | flops | bytes accessed | tf_op | source)
XLA Modules:
  0.0 94.2 jit_solution(11247164794805840045)
XLA Ops:
  0.6 0.5 collective-permute-start
  1.2 3.2 %shard_map.130 = (bf16[8,192,128]{2,1,0:T(8,128)(2,1)}, f32[3,128,384]{2,1,0:T(8,128)}, f32[3,8,512]{2,1,0:T(8,128)}, bf16[2,1280,128]{2,1,0:T(8,128)(2,1)}, bf16[2,1280,128]{2,1,0:T(8,128)(2,1)}) custom-call(f32[128,1280]{1,0:T(8,128)} %bitcast.20, f32[64,512]{1,0:T(8,128)} %bitcast.24, bf16[5120,512]{1,0:T(8,128)(2,1)} %sibling_block.1, ...), custom_call_target="tpu_custom_call" | custom-call | tf_op jit(solution)/shard_map/pallas_call | solution.py:365
  4.4 6.9 %all-to-all-start = ((bf16[8,192,128]{2,1,0:T(8,128)(2,1)}), bf16[8,192,128]{2,1,0:T(8,128)(2,1)}, u32[]{:S(2)}, u32[]{:S(2)}) async-start(bf16[8,192,128]{2,1,0:T(8,128)(2,1)} %get-tuple-element.33), calls=%async_computation | async-start | bytes 786432 | tf_op jit(solution)/shard_map/all_to_all | solution.py:377
  11.3 1.5 %collective-permute-start.2 = (bf16[2,1280,128]{2,1,0:T(8,128)(2,1)}, bf16[2,1280,128]{2,1,0:T(8,128)(2,1)}, u32[]{:S(2)}, u32[]{:S(2)}) collective-permute-start(bf16[2,1280,128]{2,1,0:T(8,128)(2,1)} %get-tuple-element.43), channel_id=1, source_target_pairs={{0,2},{1,3},{2,0},{3,1},{4,6},{5,7},{6,4},{7,5},{8,10},{9,11},{10,... | collective-permute-start | bytes 1966088 | tf_op jit(solution)/shard_map/ppermute | solution.py:335
  12.8 0.0 collective-permute-start.1
  12.8 1.2 %collective-permute-done.1.sibling_gain = f32[1,1280]{1,0:T(1,128)S(1)} collective-permute-done((f32[1,1280]{1,0:T(1,128)S(1)}, f32[1,1280]{1,0:T(1,128)S(1)}, u32[]{:S(2)}, u32[]{:S(2)}) %collective-permute-start.1) | collective-permute-done | bytes 5152 | tf_op jit(solution)/shard_map/ppermute | solution.py:327
  13.9 0.0 collective-permute-done.sibling_ref
  13.9 1.7 %copy-done.4 = bf16[1280,1280]{1,0:T(8,128)(2,1)} copy-done((bf16[1280,1280]{1,0:T(8,128)(2,1)}, bf16[1280,1280]{1,0:T(8,128)(2,1)S(1)}, u32[]{:S(2)}) %copy-start.4) | copy-done | bytes 3276824
  15.6 1.9 %copy-done.2 = bf16[1280,1280]{1,0:T(8,128)(2,1)S(1)} copy-done((bf16[1280,1280]{1,0:T(8,128)(2,1)S(1)}, bf16[1280,1280]{1,0:T(8,128)(2,1)}, u32[]{:S(2)}) %copy-start.2) | copy-done | bytes 3276824
  17.6 1.9 %copy-done.5 = bf16[1280,1280]{1,0:T(8,128)(2,1)S(1)} copy-done((bf16[1280,1280]{1,0:T(8,128)(2,1)S(1)}, bf16[1280,1280]{1,0:T(8,128)(2,1)}, u32[]{:S(2)}) %copy-start.5) | copy-done | bytes 3276824
  19.5 2.4 %shard_map.131 = (bf16[640,2560]{1,0:T(8,128)(2,1)S(1)}, f32[5,128]{1,0:T(8,128)S(1)}) custom-call(bf16[1280,1280]{1,0:T(8,128)(2,1)S(1)} %copy-done.2, bf16[1280,1280]{1,0:T(8,128)(2,1)S(1)} %copy-done.5, f32[1,1280]{1,0:T(1,128)S(1)} %broadcast_in_dim.3.own_gain, f32[1,1280]{1,0:T(1,128)S(1)} %collective-permute-done.1.sibling_gain), custom_call_target="tpu_custom_call" | custom-call | tf_op jit(solution)/shard_map/pallas_call | solution.py:404
  21.8 1.9 %all-to-all-done.grad_ref = bf16[8,192,128]{2,1,0:T(8,128)(2,1)} async-done(((bf16[8,192,128]{2,1,0:T(8,128)(2,1)}), bf16[8,192,128]{2,1,0:T(8,128)(2,1)}, u32[]{:S(2)}, u32[]{:S(2)}) %all-to-all-start) | async-done | bytes 393248 | tf_op jit(solution)/shard_map/all_to_all | solution.py:377
  23.7 1.1 %copy-done.7 = f32[3,128,384]{2,1,0:T(8,128)S(1)} copy-done((f32[3,128,384]{2,1,0:T(8,128)S(1)}, f32[3,128,384]{2,1,0:T(8,128)}, u32[]{:S(2)}) %copy-start.7) | copy-done | bytes 589848
  24.8 2.1 %shard_map.132 = (f32[3,128,160]{2,1,0:T(8,128)}, f32[3,8,512]{2,1,0:T(8,128)}, bf16[8,192,128]{2,1,0:T(8,128)(2,1)S(1)}) custom-call(bf16[8,192,128]{2,1,0:T(8,128)(2,1)} %all-to-all-done.grad_ref, f32[3,128,384]{2,1,0:T(8,128)S(1)} %copy-done.7, f32[3,8,512]{2,1,0:T(8,128)S(1)} %copy-done.17), custom_call_target="tpu_custom_call" | custom-call | tf_op jit(solution)/shard_map/pallas_call | solution.py:419
  26.9 0.8 copy-done.8
  27.6 4.2 %all-to-all-start.1 = ((bf16[8,192,128]{2,1,0:T(8,128)(2,1)}), bf16[8,192,128]{2,1,0:T(8,128)(2,1)}, u32[]{:S(2)}, u32[]{:S(2)}) async-start(bf16[8,192,128]{2,1,0:T(8,128)(2,1)} %copy-done.8), calls=%async_computation.1 | async-start | bytes 786432 | tf_op jit(solution)/shard_map/all_to_all | solution.py:430
  31.8 0.0 collective-permute-done.2.in_ref
  31.8 1.1 %shard_map.134 = (bf16[1280,128]{1,0:T(8,128)(2,1)S(1)}, bf16[1280,128]{1,0:T(8,128)(2,1)S(1)}) custom-call(bf16[2,1280,128]{2,1,0:T(8,128)(2,1)} %collective-permute-done.2.in_ref), custom_call_target="tpu_custom_call" | custom-call | tf_op jit(solution)/shard_map/pallas_call | solution.py:440
  32.9 0.0 copy-start.9
  32.9 0.0 copy-start.11
  33.0 2.1 %collective-permute-start.3 = (bf16[1280,128]{1,0:T(8,128)(2,1)S(1)}, bf16[1280,128]{1,0:T(8,128)(2,1)S(1)}, u32[]{:S(2)}, u32[]{:S(2)}) collective-permute-start(bf16[1280,128]{1,0:T(8,128)(2,1)S(1)} %get-tuple-element.45.refs_0_), channel_id=1, source_target_pairs={{0,4},{4,0},{8,12},{12,8},{16,20},{20,16},{24,28},{28,24},{1,5},{5... | collective-permute-start | bytes 983048 | tf_op jit(solution)/shard_map/ppermute | solution.py:449
  35.0 1.5 %collective-permute-start.4 = (bf16[1280,128]{1,0:T(8,128)(2,1)S(1)}, bf16[1280,128]{1,0:T(8,128)(2,1)S(1)}, u32[]{:S(2)}, u32[]{:S(2)}) collective-permute-start(bf16[1280,128]{1,0:T(8,128)(2,1)S(1)} %get-tuple-element.46.refs_2_), channel_id=1, source_target_pairs={{0,8},{4,12},{8,0},{12,4},{16,24},{20,28},{24,16},{28,20},{1,9},{5... | collective-permute-start | bytes 983048 | tf_op jit(solution)/shard_map/ppermute | solution.py:449
  36.5 1.3 %collective-permute-start.7 = (bf16[2,1280,128]{2,1,0:T(8,128)(2,1)}, bf16[2,1280,128]{2,1,0:T(8,128)(2,1)}, u32[]{:S(2)}, u32[]{:S(2)}) collective-permute-start(bf16[2,1280,128]{2,1,0:T(8,128)(2,1)} %get-tuple-element.51), channel_id=1, source_target_pairs={{0,2},{1,3},{2,0},{3,1},{4,6},{5,7},{6,4},{7,5},{8,10},{9,11},{10,... | collective-permute-start | bytes 1966088 | tf_op jit(solution)/shard_map/ppermute | solution.py:335
  37.8 1.9 %copy-done.3 = bf16[1280,1280]{1,0:T(8,128)(2,1)S(1)} copy-done((bf16[1280,1280]{1,0:T(8,128)(2,1)S(1)}, bf16[1280,1280]{1,0:T(8,128)(2,1)}, u32[]{:S(2)}) %copy-start.3) | copy-done | bytes 3276824
  39.7 1.9 %copy-done.6 = bf16[1280,1280]{1,0:T(8,128)(2,1)S(1)} copy-done((bf16[1280,1280]{1,0:T(8,128)(2,1)S(1)}, bf16[1280,1280]{1,0:T(8,128)(2,1)}, u32[]{:S(2)}) %copy-start.6) | copy-done | bytes 3276824
  41.7 2.4 %shard_map.133 = (bf16[640,2560]{1,0:T(8,128)(2,1)S(1)}, f32[10,128]{1,0:T(8,128)S(1)}) custom-call(bf16[1280,1280]{1,0:T(8,128)(2,1)S(1)} %copy-done.3, bf16[1280,1280]{1,0:T(8,128)(2,1)S(1)} %copy-done.6, f32[1,1280]{1,0:T(1,128)S(1)} %broadcast_in_dim.3.own_gain, f32[1,1280]{1,0:T(1,128)S(1)} %collective-permute-done.1.sibling_gain, ...), custom_call_target="tpu_custom_call" | custom-call | tf_op jit(solution)/shard_map/pallas_call | solution.py:404
  44.0 1.7 %copy-done = bf16[640,2560]{1,0:T(8,128)(2,1)} copy-done((bf16[640,2560]{1,0:T(8,128)(2,1)}, bf16[640,2560]{1,0:T(8,128)(2,1)S(1)}, u32[]{:S(2)}) %copy-start) | copy-done | bytes 3276824
  45.7 0.5 collective-permute-done.3.refs_1_
  46.2 0.7 copy-done.13
  46.9 0.9 collective-permute-done.4.refs_3_
  47.9 0.7 copy-done.15
  48.6 0.0 all-to-all-done.1.in_ref.own_f
  48.6 0.1 collective-permute-start.5
  48.7 1.1 %shard_map.135 = bf16[8,32,128]{2,1,0:T(8,128)(2,1)S(1)} custom-call(bf16[8,192,128]{2,1,0:T(8,128)(2,1)} %all-to-all-done.1.in_ref.own_f), custom_call_target="tpu_custom_call" | custom-call | tf_op jit(solution)/shard_map/pallas_call | solution.py:454
  49.8 1.3 %collective-permute-start.6 = (bf16[8,32,128]{2,1,0:T(8,128)(2,1)S(1)}, bf16[8,32,128]{2,1,0:T(8,128)(2,1)S(1)}, u32[]{:S(2)}, u32[]{:S(2)}) collective-permute-start(bf16[8,32,128]{2,1,0:T(8,128)(2,1)S(1)} %shard_map.135), channel_id=1, source_target_pairs={{0,2},{1,3},{2,0},{3,1},{4,6},{5,7},{6,4},{7,5},{8,10},{9,11},{10,... | collective-permute-start | bytes 196616 | tf_op jit(solution)/shard_map/ppermute | solution.py:335
  51.1 1.4 %collective-permute-done.7.in_ref = bf16[2,1280,128]{2,1,0:T(8,128)(2,1)} collective-permute-done((bf16[2,1280,128]{2,1,0:T(8,128)(2,1)}, bf16[2,1280,128]{2,1,0:T(8,128)(2,1)}, u32[]{:S(2)}, u32[]{:S(2)}) %collective-permute-start.7) | collective-permute-done | bytes 655392 | tf_op jit(solution)/shard_map/ppermute | solution.py:335
  52.5 1.7 %collective-permute-done.6.b_ref = bf16[8,32,128]{2,1,0:T(8,128)(2,1)S(1)} collective-permute-done((bf16[8,32,128]{2,1,0:T(8,128)(2,1)S(1)}, bf16[8,32,128]{2,1,0:T(8,128)(2,1)S(1)}, u32[]{:S(2)}, u32[]{:S(2)}) %collective-permute-start.6) | collective-permute-done | bytes 65568 | tf_op jit(solution)/shard_map/ppermute | solution.py:335
  54.2 1.1 %shard_map.136 = (bf16[1280,128]{1,0:T(8,128)(2,1)S(1)}, bf16[1280,128]{1,0:T(8,128)(2,1)S(1)}) custom-call(bf16[2,1280,128]{2,1,0:T(8,128)(2,1)} %collective-permute-done.7.in_ref), custom_call_target="tpu_custom_call" | custom-call | tf_op jit(solution)/shard_map/pallas_call | solution.py:440
  55.4 1.5 %collective-permute-start.8 = (bf16[1280,128]{1,0:T(8,128)(2,1)S(1)}, bf16[1280,128]{1,0:T(8,128)(2,1)S(1)}, u32[]{:S(2)}, u32[]{:S(2)}) collective-permute-start(bf16[1280,128]{1,0:T(8,128)(2,1)S(1)} %get-tuple-element.53.refs_0_), channel_id=1, source_target_pairs={{0,4},{4,0},{8,12},{12,8},{16,20},{20,16},{24,28},{28,24},{1,5},{5... | collective-permute-start | bytes 983048 | tf_op jit(solution)/shard_map/ppermute | solution.py:449
  56.9 0.6 collective-permute-start.9
  57.4 0.8 collective-permute-start.10
  58.2 2.9 %collective-permute-done.10.refs_1_ = f32[10,128]{1,0:T(8,128)S(1)} collective-permute-done((f32[10,128]{1,0:T(8,128)S(1)}, f32[10,128]{1,0:T(8,128)S(1)}, u32[]{:S(2)}, u32[]{:S(2)}) %collective-permute-start.10) | collective-permute-done | bytes 5152 | tf_op jit(solution)/shard_map/ppermute | solution.py:335
  61.1 0.2 shard_map.137.refs_4_.inv
  61.3 0.0 collective-permute-done.5.sibling_f
  61.4 2.9 %shard_map.138 = (bf16[2560,256]{1,0:T(8,128)(2,1)S(1)}, bf16[640,256]{1,0:T(8,128)(2,1)S(1)}) custom-call(bf16[8,192,128]{2,1,0:T(8,128)(2,1)} %all-to-all-done.1.in_ref.own_f, bf16[8,192,128]{2,1,0:T(8,128)(2,1)S(1)} %collective-permute-done.5.sibling_f, bf16[8,32,128]{2,1,0:T(8,128)(2,1)S(1)} %collective-permute-done.6.b_ref, ...), custom_call_target="tpu_custom_call" | custom-call | tf_op jit(solution)/shard_map/pallas_call | solution.py:485
  64.3 0.9 collective-permute-start.11
  65.2 1.2 %shard_map.139.refs_5_ = bf16[640,256]{1,0:T(8,128)(2,1)S(1)} custom-call(bf16[640,2560]{1,0:T(8,128)(2,1)S(1)} %copy-done.1, bf16[2560,256]{1,0:T(8,128)(2,1)S(1)} %get-tuple-element.58.weights), custom_call_target="tpu_custom_call" | custom-call | tf_op jit(solution)/shard_map/pallas_call | solution.py:495
  66.4 0.0 slice-start.1
  66.4 1.3 %collective-permute-start.14 = (bf16[640,256]{1,0:T(8,128)(2,1)S(1)}, bf16[640,256]{1,0:T(8,128)(2,1)S(1)}, u32[]{:S(2)}, u32[]{:S(2)}) collective-permute-start(bf16[640,256]{1,0:T(8,128)(2,1)S(1)} %shard_map.139.refs_5_), channel_id=1, source_target_pairs={{0,2},{1,3},{2,0},{3,1},{4,6},{5,7},{6,4},{7,5},{8,10},{9,11},{10,... | collective-permute-start | bytes 983048 | tf_op jit(solution)/shard_map/ppermute | solution.py:335
  67.7 0.0 collective-permute-done.8.refs_1_
  67.7 0.0 collective-permute-done.9.refs_3_
  67.7 2.8 %shard_map.140 = (bf16[2560,256]{1,0:T(8,128)(2,1)S(1)}, bf16[640,256]{1,0:T(8,128)(2,1)S(1)}) custom-call(bf16[8,192,128]{2,1,0:T(8,128)(2,1)} %all-to-all-done.1.in_ref.own_f, bf16[8,192,128]{2,1,0:T(8,128)(2,1)S(1)} %collective-permute-done.5.sibling_f, bf16[8,32,128]{2,1,0:T(8,128)(2,1)S(1)} %collective-permute-done.6.b_ref, ...), custom_call_target="tpu_custom_call" | custom-call | tf_op jit(solution)/shard_map/pallas_call | solution.py:485
  70.4 0.9 collective-permute-start.13
  71.3 1.2 %shard_map.141.refs_3_ = bf16[640,256]{1,0:T(8,128)(2,1)S(1)} custom-call(bf16[640,2560]{1,0:T(8,128)(2,1)S(1)} %copy-done.1, bf16[2560,256]{1,0:T(8,128)(2,1)S(1)} %get-tuple-element.60.weights), custom_call_target="tpu_custom_call" | custom-call | tf_op jit(solution)/shard_map/pallas_call | solution.py:495
  72.5 1.3 %collective-permute-start.12 = (bf16[640,256]{1,0:T(8,128)(2,1)S(1)}, bf16[640,256]{1,0:T(8,128)(2,1)S(1)}, u32[]{:S(2)}, u32[]{:S(2)}) collective-permute-start(bf16[640,256]{1,0:T(8,128)(2,1)S(1)} %shard_map.141.refs_3_), channel_id=1, source_target_pairs={{0,2},{1,3},{2,0},{3,1},{4,6},{5,7},{6,4},{7,5},{8,10},{9,11},{10,... | collective-permute-start | bytes 983048 | tf_op jit(solution)/shard_map/ppermute | solution.py:335
  73.8 1.2 %collective-permute-done.11.refs_4_.refs_0_ = bf16[640,256]{1,0:T(8,128)(2,1)S(1)} collective-permute-done((bf16[640,256]{1,0:T(8,128)(2,1)S(1)}, bf16[640,256]{1,0:T(8,128)(2,1)S(1)}, u32[]{:S(2)}, u32[]{:S(2)}) %collective-permute-start.11) | collective-permute-done | bytes 327712 | tf_op jit(solution)/shard_map/ppermute | solution.py:335
  75.0 5.9 %shard_map.142 = (f32[1280,256]{1,0:T(8,128)S(1)}, f32[1280,256]{1,0:T(8,128)S(1)}) custom-call(bf16[8,192,128]{2,1,0:T(8,128)(2,1)} %all-to-all-done.1.in_ref.own_f, bf16[8,192,128]{2,1,0:T(8,128)(2,1)S(1)} %collective-permute-done.5.sibling_f, bf16[5120,512]{1,0:T(8,128)(2,1)S(1)} %bitcast.19, bf16[5120,512]{1,0:T(8,128)(2,1)S(1)} %bitcast.19, ...), custom_call_target="tpu_custom_call" | custom-call | flops 3355443200 | bytes 6553600 | tf_op jit(solution)/shard_map/pallas_call | solution.py:507
  80.9 0.9 shard_map.143.refs_1_
  81.8 0.3 collective-permute-done.14.refs_0_
  82.0 0.9 shard_map.144.refs_1_
  82.9 6.1 %collective-permute-done.13.refs_0_ = bf16[640,256]{1,0:T(8,128)(2,1)S(1)} collective-permute-done((bf16[640,256]{1,0:T(8,128)(2,1)S(1)}, bf16[640,256]{1,0:T(8,128)(2,1)S(1)}, u32[]{:S(2)}, u32[]{:S(2)}) %collective-permute-start.13) | collective-permute-done | bytes 327712 | tf_op jit(solution)/shard_map/ppermute | solution.py:335
  89.1 0.9 shard_map.145.refs_1_
  89.9 3.3 %collective-permute-done.12.refs_0_ = bf16[640,256]{1,0:T(8,128)(2,1)S(1)} collective-permute-done((bf16[640,256]{1,0:T(8,128)(2,1)S(1)}, bf16[640,256]{1,0:T(8,128)(2,1)S(1)}, u32[]{:S(2)}, u32[]{:S(2)}) %collective-permute-start.12) | collective-permute-done | bytes 327712 | tf_op jit(solution)/shard_map/ppermute | solution.py:335
  93.3 0.9 shard_map.146
  (31 shorter events, 0.1 us)
Async XLA Ops:
  0.6 13.3 %collective-permute-start = (bf16[1280,1280]{1,0:T(8,128)(2,1)}, bf16[1280,1280]{1,0:T(8,128)(2,1)S(1)}, u32[]{:S(2)}, u32[]{:S(2)}) collective-permute-start(bf16[1280,1280]{1,0:T(8,128)(2,1)} %own_ref.3), channel_id=1, source_target_pairs={{0,1},{1,0},{2,3},{3,2},{4,5},{5,4},{6,7},{7,6},{8,9},{9,8},{10,11... | collective-permute-start | bytes 9830408 | tf_op jit(solution)/shard_map/ppermute | solution.py:327
  1.2 11.6 %copy-start.18 = (f32[1280]{0:T(1024)S(1)}, f32[1280]{0:T(1024)}, u32[]{:S(2)}) copy-start(f32[1280]{0:T(1024)} %param.12) | copy-start | bytes 15364
  4.4 19.3 %all-to-all-start = ((bf16[8,192,128]{2,1,0:T(8,128)(2,1)}), bf16[8,192,128]{2,1,0:T(8,128)(2,1)}, u32[]{:S(2)}, u32[]{:S(2)}) async-start(bf16[8,192,128]{2,1,0:T(8,128)(2,1)} %get-tuple-element.33), calls=%async_computation | async-start | bytes 786432 | tf_op jit(solution)/shard_map/all_to_all | solution.py:377
  11.3 20.5 %collective-permute-start.2 = (bf16[2,1280,128]{2,1,0:T(8,128)(2,1)}, bf16[2,1280,128]{2,1,0:T(8,128)(2,1)}, u32[]{:S(2)}, u32[]{:S(2)}) collective-permute-start(bf16[2,1280,128]{2,1,0:T(8,128)(2,1)} %get-tuple-element.43), channel_id=1, source_target_pairs={{0,2},{1,3},{2,0},{3,1},{4,6},{5,7},{6,4},{7,5},{8,10},{9,11},{10,... | collective-permute-start | bytes 1966088 | tf_op jit(solution)/shard_map/ppermute | solution.py:335
  12.8 1.2 %collective-permute-start.1 = (f32[1,1280]{1,0:T(1,128)S(1)}, f32[1,1280]{1,0:T(1,128)S(1)}, u32[]{:S(2)}, u32[]{:S(2)}) collective-permute-start(f32[1,1280]{1,0:T(1,128)S(1)} %broadcast_in_dim.3.own_gain), channel_id=1, source_target_pairs={{0,1},{1,0},{2,3},{3,2},{4,5},{5,4},{6,7},{7,6},{8,9},{9,8},{10,11... | collective-permute-start | bytes 15368 | tf_op jit(solution)/shard_map/ppermute | solution.py:327
  13.9 1.7 %copy-start.4 = (bf16[1280,1280]{1,0:T(8,128)(2,1)}, bf16[1280,1280]{1,0:T(8,128)(2,1)S(1)}, u32[]{:S(2)}) copy-start(bf16[1280,1280]{1,0:T(8,128)(2,1)S(1)} %collective-permute-done.sibling_ref) | copy-start | bytes 9830404
  15.6 1.9 %copy-start.2 = (bf16[1280,1280]{1,0:T(8,128)(2,1)S(1)}, bf16[1280,1280]{1,0:T(8,128)(2,1)}, u32[]{:S(2)}) copy-start(bf16[1280,1280]{1,0:T(8,128)(2,1)} %own_ref.3) | copy-start | bytes 9830404
  17.5 1.9 %copy-start.5 = (bf16[1280,1280]{1,0:T(8,128)(2,1)S(1)}, bf16[1280,1280]{1,0:T(8,128)(2,1)}, u32[]{:S(2)}) copy-start(bf16[1280,1280]{1,0:T(8,128)(2,1)} %copy-done.4) | copy-start | bytes 9830404
  19.5 4.2 %copy-start.17 = (f32[3,8,512]{2,1,0:T(8,128)S(1)}, f32[3,8,512]{2,1,0:T(8,128)}, u32[]{:S(2)}) copy-start(f32[3,8,512]{2,1,0:T(8,128)} %get-tuple-element.37.up_win) | copy-start | bytes 147460
  23.7 1.1 %copy-start.7 = (f32[3,128,384]{2,1,0:T(8,128)S(1)}, f32[3,128,384]{2,1,0:T(8,128)}, u32[]{:S(2)}) copy-start(f32[3,128,384]{2,1,0:T(8,128)} %get-tuple-element.36.down_win) | copy-start | bytes 1769476
  26.9 0.8 copy-start.8
  27.6 21.0 %all-to-all-start.1 = ((bf16[8,192,128]{2,1,0:T(8,128)(2,1)}), bf16[8,192,128]{2,1,0:T(8,128)(2,1)}, u32[]{:S(2)}, u32[]{:S(2)}) async-start(bf16[8,192,128]{2,1,0:T(8,128)(2,1)} %copy-done.8), calls=%async_computation.1 | async-start | bytes 786432 | tf_op jit(solution)/shard_map/all_to_all | solution.py:430
  32.9 11.1 %copy-start.9 = (bf16[1280,128]{1,0:T(8,128)(2,1)}, bf16[1280,128]{1,0:T(8,128)(2,1)S(1)}, u32[]{:S(2)}) copy-start(bf16[1280,128]{1,0:T(8,128)(2,1)S(1)} %get-tuple-element.45.refs_0_) | copy-start | bytes 983044
  32.9 11.1 %copy-start.11 = (bf16[1280,128]{1,0:T(8,128)(2,1)}, bf16[1280,128]{1,0:T(8,128)(2,1)S(1)}, u32[]{:S(2)}) copy-start(bf16[1280,128]{1,0:T(8,128)(2,1)S(1)} %get-tuple-element.46.refs_2_) | copy-start | bytes 983044
  33.0 13.3 %collective-permute-start.3 = (bf16[1280,128]{1,0:T(8,128)(2,1)S(1)}, bf16[1280,128]{1,0:T(8,128)(2,1)S(1)}, u32[]{:S(2)}, u32[]{:S(2)}) collective-permute-start(bf16[1280,128]{1,0:T(8,128)(2,1)S(1)} %get-tuple-element.45.refs_0_), channel_id=1, source_target_pairs={{0,4},{4,0},{8,12},{12,8},{16,20},{20,16},{24,28},{28,24},{1,5},{5... | collective-permute-start | bytes 983048 | tf_op jit(solution)/shard_map/ppermute | solution.py:449
  35.0 12.8 %collective-permute-start.4 = (bf16[1280,128]{1,0:T(8,128)(2,1)S(1)}, bf16[1280,128]{1,0:T(8,128)(2,1)S(1)}, u32[]{:S(2)}, u32[]{:S(2)}) collective-permute-start(bf16[1280,128]{1,0:T(8,128)(2,1)S(1)} %get-tuple-element.46.refs_2_), channel_id=1, source_target_pairs={{0,8},{4,12},{8,0},{12,4},{16,24},{20,28},{24,16},{28,20},{1,9},{5... | collective-permute-start | bytes 983048 | tf_op jit(solution)/shard_map/ppermute | solution.py:449
  36.5 16.0 %collective-permute-start.7 = (bf16[2,1280,128]{2,1,0:T(8,128)(2,1)}, bf16[2,1280,128]{2,1,0:T(8,128)(2,1)}, u32[]{:S(2)}, u32[]{:S(2)}) collective-permute-start(bf16[2,1280,128]{2,1,0:T(8,128)(2,1)} %get-tuple-element.51), channel_id=1, source_target_pairs={{0,2},{1,3},{2,0},{3,1},{4,6},{5,7},{6,4},{7,5},{8,10},{9,11},{10,... | collective-permute-start | bytes 1966088 | tf_op jit(solution)/shard_map/ppermute | solution.py:335
  37.8 1.9 %copy-start.3 = (bf16[1280,1280]{1,0:T(8,128)(2,1)S(1)}, bf16[1280,1280]{1,0:T(8,128)(2,1)}, u32[]{:S(2)}) copy-start(bf16[1280,1280]{1,0:T(8,128)(2,1)} %own_ref.3) | copy-start | bytes 9830404
  39.7 1.9 %copy-start.6 = (bf16[1280,1280]{1,0:T(8,128)(2,1)S(1)}, bf16[1280,1280]{1,0:T(8,128)(2,1)}, u32[]{:S(2)}) copy-start(bf16[1280,1280]{1,0:T(8,128)(2,1)} %copy-done.4) | copy-start | bytes 9830404
  44.0 1.7 %copy-start = (bf16[640,2560]{1,0:T(8,128)(2,1)}, bf16[640,2560]{1,0:T(8,128)(2,1)S(1)}, u32[]{:S(2)}) copy-start(bf16[640,2560]{1,0:T(8,128)(2,1)S(1)} %get-tuple-element.49.x.refs_1_) | copy-start | bytes 9830404
  46.2 0.7 copy-start.13
  47.9 0.7 copy-start.15
  48.6 12.7 %copy-start.10 = (bf16[1280,128]{1,0:T(8,128)(2,1)S(1)}, bf16[1280,128]{1,0:T(8,128)(2,1)}, u32[]{:S(2)}) copy-start(bf16[1280,128]{1,0:T(8,128)(2,1)} %copy-done.9) | copy-start | bytes 983044
  48.6 12.7 %copy-start.12 = (bf16[1280,128]{1,0:T(8,128)(2,1)S(1)}, bf16[1280,128]{1,0:T(8,128)(2,1)}, u32[]{:S(2)}) copy-start(bf16[1280,128]{1,0:T(8,128)(2,1)} %copy-done.11) | copy-start | bytes 983044
  48.6 12.7 %copy-start.14 = (bf16[1280,128]{1,0:T(8,128)(2,1)S(1)}, bf16[1280,128]{1,0:T(8,128)(2,1)}, u32[]{:S(2)}) copy-start(bf16[1280,128]{1,0:T(8,128)(2,1)} %copy-done.13) | copy-start | bytes 983044
  48.6 12.7 %copy-start.16 = (bf16[1280,128]{1,0:T(8,128)(2,1)S(1)}, bf16[1280,128]{1,0:T(8,128)(2,1)}, u32[]{:S(2)}) copy-start(bf16[1280,128]{1,0:T(8,128)(2,1)} %copy-done.15) | copy-start | bytes 983044
  48.6 12.7 %collective-permute-start.5 = (bf16[8,192,128]{2,1,0:T(8,128)(2,1)}, bf16[8,192,128]{2,1,0:T(8,128)(2,1)S(1)}, u32[]{:S(2)}, u32[]{:S(2)}) collective-permute-start(bf16[8,192,128]{2,1,0:T(8,128)(2,1)} %all-to-all-done.1.in_ref.own_f), channel_id=1, source_target_pairs={{0,1},{1,0},{2,3},{3,2},{4,5},{5,4},{6,7},{7,6},{8,9},{9,8},{10,11... | collective-permute-start | bytes 1179656 | tf_op jit(solution)/shard_map/ppermute | solution.py:327
  49.8 4.4 %collective-permute-start.6 = (bf16[8,32,128]{2,1,0:T(8,128)(2,1)S(1)}, bf16[8,32,128]{2,1,0:T(8,128)(2,1)S(1)}, u32[]{:S(2)}, u32[]{:S(2)}) collective-permute-start(bf16[8,32,128]{2,1,0:T(8,128)(2,1)S(1)} %shard_map.135), channel_id=1, source_target_pairs={{0,2},{1,3},{2,0},{3,1},{4,6},{5,7},{6,4},{7,5},{8,10},{9,11},{10,... | collective-permute-start | bytes 196616 | tf_op jit(solution)/shard_map/ppermute | solution.py:335
  55.4 12.3 %collective-permute-start.8 = (bf16[1280,128]{1,0:T(8,128)(2,1)S(1)}, bf16[1280,128]{1,0:T(8,128)(2,1)S(1)}, u32[]{:S(2)}, u32[]{:S(2)}) collective-permute-start(bf16[1280,128]{1,0:T(8,128)(2,1)S(1)} %get-tuple-element.53.refs_0_), channel_id=1, source_target_pairs={{0,4},{4,0},{8,12},{12,8},{16,20},{20,16},{24,28},{28,24},{1,5},{5... | collective-permute-start | bytes 983048 | tf_op jit(solution)/shard_map/ppermute | solution.py:449
  56.9 10.8 %collective-permute-start.9 = (bf16[1280,128]{1,0:T(8,128)(2,1)S(1)}, bf16[1280,128]{1,0:T(8,128)(2,1)S(1)}, u32[]{:S(2)}, u32[]{:S(2)}) collective-permute-start(bf16[1280,128]{1,0:T(8,128)(2,1)S(1)} %get-tuple-element.54.refs_2_), channel_id=1, source_target_pairs={{0,8},{4,12},{8,0},{12,4},{16,24},{20,28},{24,16},{28,20},{1,9},{5... | collective-permute-start | bytes 983048 | tf_op jit(solution)/shard_map/ppermute | solution.py:449
  57.4 3.7 %collective-permute-start.10 = (f32[10,128]{1,0:T(8,128)S(1)}, f32[10,128]{1,0:T(8,128)S(1)}, u32[]{:S(2)}, u32[]{:S(2)}) collective-permute-start(f32[10,128]{1,0:T(8,128)S(1)} %get-tuple-element.56.refs_0_), channel_id=1, source_target_pairs={{0,2},{1,3},{2,0},{3,1},{4,6},{5,7},{6,4},{7,5},{8,10},{9,11},{10,... | collective-permute-start | bytes 15368 | tf_op jit(solution)/shard_map/ppermute | solution.py:335
  61.4 3.8 %copy-start.1 = (bf16[640,2560]{1,0:T(8,128)(2,1)S(1)}, bf16[640,2560]{1,0:T(8,128)(2,1)}, u32[]{:S(2)}) copy-start(bf16[640,2560]{1,0:T(8,128)(2,1)} %copy-done) | copy-start | bytes 9830404
  64.3 10.7 %collective-permute-start.11 = (bf16[640,256]{1,0:T(8,128)(2,1)S(1)}, bf16[640,256]{1,0:T(8,128)(2,1)S(1)}, u32[]{:S(2)}, u32[]{:S(2)}) collective-permute-start(bf16[640,256]{1,0:T(8,128)(2,1)S(1)} %get-tuple-element.57.refs_4_), channel_id=1, source_target_pairs={{0,2},{1,3},{2,0},{3,1},{4,6},{5,7},{6,4},{7,5},{8,10},{9,11},{10,... | collective-permute-start | bytes 983048 | tf_op jit(solution)/shard_map/ppermute | solution.py:335
  65.2 9.9 %slice-start = ((s8[5242880]{0:T(1024)(128)(4,1)}), s8[4194304]{0:T(1024)(128)(4,1)S(1)}, s32[]{:S(2)}) async-start(s8[5242880]{0:T(1024)(128)(4,1)} %bitcast.18), calls=%async_computation.2 | async-start | bytes 8388608
  66.4 8.7 %slice-start.1 = ((s8[5242880]{0:T(1024)(128)(4,1)}), s8[1048576]{0:T(1024)(128)(4,1)S(1)}, s32[]{:S(2)}) async-start(s8[5242880]{0:T(1024)(128)(4,1)} %bitcast.18), calls=%async_computation.3 | async-start | bytes 2097152
  66.4 15.7 %collective-permute-start.14 = (bf16[640,256]{1,0:T(8,128)(2,1)S(1)}, bf16[640,256]{1,0:T(8,128)(2,1)S(1)}, u32[]{:S(2)}, u32[]{:S(2)}) collective-permute-start(bf16[640,256]{1,0:T(8,128)(2,1)S(1)} %shard_map.139.refs_5_), channel_id=1, source_target_pairs={{0,2},{1,3},{2,0},{3,1},{4,6},{5,7},{6,4},{7,5},{8,10},{9,11},{10,... | collective-permute-start | bytes 983048 | tf_op jit(solution)/shard_map/ppermute | solution.py:335
  70.4 18.6 %collective-permute-start.13 = (bf16[640,256]{1,0:T(8,128)(2,1)S(1)}, bf16[640,256]{1,0:T(8,128)(2,1)S(1)}, u32[]{:S(2)}, u32[]{:S(2)}) collective-permute-start(bf16[640,256]{1,0:T(8,128)(2,1)S(1)} %get-tuple-element.59.refs_2_), channel_id=1, source_target_pairs={{0,2},{1,3},{2,0},{3,1},{4,6},{5,7},{6,4},{7,5},{8,10},{9,11},{10,... | collective-permute-start | bytes 983048 | tf_op jit(solution)/shard_map/ppermute | solution.py:335
  72.5 20.8 %collective-permute-start.12 = (bf16[640,256]{1,0:T(8,128)(2,1)S(1)}, bf16[640,256]{1,0:T(8,128)(2,1)S(1)}, u32[]{:S(2)}, u32[]{:S(2)}) collective-permute-start(bf16[640,256]{1,0:T(8,128)(2,1)S(1)} %shard_map.141.refs_3_), channel_id=1, source_target_pairs={{0,2},{1,3},{2,0},{3,1},{4,6},{5,7},{6,4},{7,5},{8,10},{9,11},{10,... | collective-permute-start | bytes 983048 | tf_op jit(solution)/shard_map/ppermute | solution.py:335

commit v11 on v10

--- a/solution.py
+++ b/solution.py
@@ -15,7 +15,7 @@
 COLUMN_HALVES = 2
 TOKEN_HALVES = 2
 VMEM_BYTES = 16 * 2**20
-BEGIN_VMEM_BYTES = 58 * 2**20
+LARGE_VMEM_BYTES = 58 * 2**20
 
 
 def adaptive_moment_update(param, first, second, grad_mean):
@@ -105,46 +105,69 @@
         out[...] = in_ref[k]
 
 
-def prepare_kernel(first, own_ref, sibling_ref, own_gain, sibling_gain, *refs):
-    x_ref, sums_ref, squares = refs[-3:]
-    features = own_ref.shape[1]
-    rows = x_ref.shape[0]
-    tile = 16 if rows % 16 == 0 else rows
-
-    @pl.loop(0, rows // tile, unroll=2)
-    def _(i):
-        to = pl.ds(pl.multiple_of(i * tile, tile), tile)
-        at = pl.ds(pl.multiple_of(first + i * tile, tile), tile)
-        own = own_ref[at, :].astype(jnp.float32)
-        x_ref[to, :features] = (own * own_gain[...]).astype(x_ref.dtype)
-        total = own * own
-        sibling = sibling_ref[at, :].astype(jnp.float32)
-        x_ref[to, features:] = (sibling * sibling_gain[...]).astype(x_ref.dtype)
-        total += sibling * sibling
-        total = jnp.sum(total, axis=1, keepdims=True)
-        squares[to, :] = jnp.broadcast_to(total, (tile, LANES))
-
-    for ref in refs[:-3]:
-        sums_ref[: ref.shape[0]] = ref[...]
-    for i in range(rows // LANES):
-        at = first // LANES + i
-        sums_ref[at : at + 1] = squares[i * LANES : (i + 1) * LANES, :].T[:1]
-
-
-def inverse_kernel(width, *refs):
-    out = refs[-1]
-    total = refs[0][...]
-    for ref in refs[1:-1]:
-        total = total + ref[...]
+def prepare_kernel(own_ref, sibling_ref, own_gain, sibling_gain, *refs):
+    xs, (sums_ref, squares) = refs[:-2], refs[-2:]
+    block, features = own_ref.shape
+    step, steps = pl.program_id(0), pl.num_programs(0)
+    tile = 16 if block % 16 == 0 else block
+    for k, x_ref in enumerate(xs):
+
+        @pl.when(step // (steps // len(xs)) == k)
+        def _():
+            @pl.loop(0, block // tile, unroll=2)
+            def _(i):
+                at = pl.ds(pl.multiple_of(i * tile, tile), tile)
+                own = own_ref[at, :].astype(jnp.float32)
+                x_ref[at, :features] = (own * own_gain[...]).astype(x_ref.dtype)
+                total = own * own
+                sibling = sibling_ref[at, :].astype(jnp.float32)
+                x_ref[at, features:] = (sibling * sibling_gain[...]).astype(x_ref.dtype)
+                total += sibling * sibling
+                total = jnp.sum(total, axis=1, keepdims=True)
+                to = pl.ds(pl.multiple_of(step * block + i * tile, tile), tile)
+                squares[to, :] = jnp.broadcast_to(total, (tile, LANES))
+
+    @pl.when(step == steps - 1)
+    def _():
+        for i in range(sums_ref.shape[0]):
+            sums_ref[i : i + 1] = squares[i * LANES : (i + 1) * LANES, :].T[:1]
+
+
+def message_kernel(factor_ref, sums_ref, out_ref, sem):
+    shares, up_rows = factor_ref.shape[0], out_ref.shape[1]
+    copy = pltpu.make_async_copy(
+        factor_ref.at[:, pl.ds(factor_ref.shape[1] - up_rows, up_rows)],
+        out_ref.at[pl.ds(0, shares)],
+        sem,
+    )
+    copy.start()
+    left = sums_ref[...]
+    terms = []
+    for _ in range(3):
+        terms.append(left.astype(jnp.bfloat16).astype(jnp.float32))
+        left = left - terms[-1]
+    rest = (out_ref.shape[0] - shares) * up_rows - 3 * left.shape[0]
+    if rest > 0:
+        terms.append(jnp.zeros((rest, LANES), jnp.float32))
+    rows = jnp.concatenate(terms, axis=0)
+    for i in range(out_ref.shape[0] - shares):
+        out_ref[shares + i] = rows[i * up_rows : (i + 1) * up_rows].astype(jnp.bfloat16)
+    copy.wait()
+
+
+def inverse_kernel(width, shares, sums_ref, *refs):
+    messages, out = refs[:-1], refs[-1]
+    total = sums_ref[...]
+    count = total.shape[0]
+    for ref in messages:
+        rows = [ref[i].astype(jnp.float32) for i in range(shares, ref.shape[0])]
+        rows = jnp.concatenate(rows, axis=0)
+        total += rows[:count] + rows[count : 2 * count] + rows[2 * count : 3 * count]
     inverse = lax.rsqrt(total / width + 1e-06)
-    for i in range(inverse.shape[0]):
+    for i in range(count):
         out[i * LANES : (i + 1) * LANES, :] = jnp.broadcast_to(
             inverse[i : i + 1], (LANES, LANES)
         ).T
-
-
-def tail_kernel(in_ref, out_ref):
-    out_ref[...] = in_ref[:, in_ref.shape[1] - out_ref.shape[1] :]
 
 
 def update(total, down, up, a_ref, b_ref):
@@ -165,7 +188,17 @@
     return jnp.concatenate(pieces, axis=0).astype(jnp.bfloat16)
 
 
-def adam_kernel(grad_ref, down_win, up_win, a_ref, b_ref, factor_ref):
+def adam_kernel(grad_in, down_in, up_in, a_ref, b_ref, factor_ref, grad_ref, down_win, up_win, sem):
+    copies = [
+        pltpu.make_async_copy(source, target, sem.at[i])
+        for i, (source, target) in enumerate(
+            ((grad_in, grad_ref), (down_in, down_win), (up_in, up_win))
+        )
+    ]
+    for copy in copies:
+        copy.start()
+    for copy in copies:
+        copy.wait()
     replicas = grad_ref.shape[0]
     down_rows, window = a_ref.shape[2], down_win.shape[2]
     total = jnp.sum(grad_ref[...].astype(jnp.float32), axis=0) / replicas
@@ -220,14 +253,16 @@
     )
 
 
-def outside_kernel(static, chips, step, turn, own_f, sibling_f, b_ref, x, *refs):
-    weights, product = refs[-2:]
+def outside_kernel(static, chips, step, turn, own_f, sibling_f, b_ref, x_in, *refs):
+    weights, product, x, sem = refs[-4:]
+    copy = pltpu.make_async_copy(x_in, x, sem)
+    copy.start()
     strips = static[3]
     features = refs[0].shape[0]
     down_rows = own_f.shape[1] - b_ref.shape[1]
     place, replica = lax.axis_index("tensor"), lax.axis_index("dp")
     owner = (place // CORES - step + chips) % chips * CORES + place % CORES
-    b = up_factor(static, b_ref[...], owner)
+    b = up_factor(static, b_ref[: own_f.shape[0]], owner)
     own_a, sibling_a = factor_a(own_f, down_rows), factor_a(sibling_f, down_rows)
     for k, strip in enumerate(strips):
         mine, other = refs[2 * k : 2 * k + 2]
@@ -237,6 +272,7 @@
         weights[:features, lanes] = merge(static[0], block, own_a, b[:, lanes])
         block = jnp.where(even, other[...], mine[...])
         weights[features:, lanes] = merge(static[0], block, sibling_a, b[:, lanes])
+    copy.wait()
     more_kernel(x, weights, product)
 
 
@@ -372,7 +408,7 @@
             pltpu.VMEM((rank, columns), f32),
             pltpu.SemaphoreType.DMA((2 + len(steps) * strips + len(state),)),
         ],
-        compiler_params=pltpu.CompilerParams(vmem_limit_bytes=BEGIN_VMEM_BYTES),
+        compiler_params=pltpu.CompilerParams(vmem_limit_bytes=LARGE_VMEM_BYTES),
     )(down_sent, up_gradient[0], frozen_key_value, *state)
     exchanged = lax.all_to_all(packed, "dp", 0, 0, tiled=True)
     if aligned:
@@ -396,26 +432,29 @@
     send_half(0, None)
 
     gain = input_norm_gain[None, :]
-    operands = [prompt_hidden_input, to_sibling(prompt_hidden_input), gain, to_sibling(gain)]
-    x, squares = [], None
     some = tokens // TOKEN_HALVES
-    for h in range(TOKEN_HALVES):
-        before = [] if squares is None else [squares]
-        value, squares = pl.pallas_call(
-            functools.partial(prepare_kernel, h * some),
-            out_shape=(
-                jax.ShapeDtypeStruct((some, CORES * features), bf16),
-                jax.ShapeDtypeStruct(((h + 1) * some // LANES, LANES), f32),
-            ),
-            in_specs=in_vmem(4 + len(before)),
-            out_specs=tuple(in_vmem(2)),
-            scratch_shapes=[pltpu.VMEM((some, LANES), f32)],
-            compiler_params=params(),
-        )(*operands, *before)
-        x.append(value)
-        if h == 0:
-            exchanged, squares = lax.optimization_barrier((exchanged, squares))
-
+    rows = LANES if some % LANES == 0 else some
+    groups_of = some // rows
+    token_block = pl.BlockSpec((rows, features), lambda i: (i, 0))
+    gain_block = pl.BlockSpec((1, features), lambda i: (0, 0))
+    *x, squares = pl.pallas_call(
+        prepare_kernel,
+        grid=(TOKEN_HALVES * groups_of,),
+        out_shape=(jax.ShapeDtypeStruct((some, CORES * features), bf16),) * TOKEN_HALVES
+        + (jax.ShapeDtypeStruct((tokens // LANES, LANES), f32),),
+        in_specs=[token_block, token_block, gain_block, gain_block],
+        out_specs=tuple(
+            pl.BlockSpec(
+                (rows, CORES * features),
+                lambda i, k=k: (jnp.clip(i - k * groups_of, 0, groups_of - 1), 0),
+            )
+            for k in range(TOKEN_HALVES)
+        )
+        + (pl.BlockSpec((tokens // LANES, LANES), lambda i: (0, 0)),),
+        scratch_shapes=[pltpu.VMEM((tokens, LANES), f32)],
+        compiler_params=pltpu.CompilerParams(vmem_limit_bytes=LARGE_VMEM_BYTES),
+    )(prompt_hidden_input, to_sibling(prompt_hidden_input), gain, to_sibling(gain))
+    exchanged, squares = lax.optimization_barrier((exchanged, squares))
     a_next, b_next, sent = pl.pallas_call(
         adam_kernel,
         out_shape=(
@@ -423,9 +462,15 @@
             jax.ShapeDtypeStruct((3, up_rows, columns), f32),
             shares,
         ),
-        in_specs=in_vmem(3),
+        in_specs=anywhere(3),
         out_specs=tuple(in_vmem(3)),
-        compiler_params=params(),
+        scratch_shapes=[
+            pltpu.VMEM((n_dp, packed_rows, LANES), bf16),
+            pltpu.VMEM((3, factors, window), f32),
+            pltpu.VMEM((3, up_rows, columns), f32),
+            pltpu.SemaphoreType.DMA((3,)),
+        ],
+        compiler_params=pltpu.CompilerParams(vmem_limit_bytes=LARGE_VMEM_BYTES),
     )(exchanged, down_win, up_win)
     own_f = lax.all_to_all(sent, "dp", 0, 0, tiled=True)
     for half in range(1, halves):
@@ -449,46 +494,50 @@
                 outside[strip].append((piece, lax.ppermute(piece, "dp", pairs)))
 
     swap_half(0, sent)
-    own_f, squares, _ = lax.optimization_barrier((own_f, squares, outside))
+    own_f, _ = lax.optimization_barrier((own_f, outside))
     sibling_f = to_sibling(own_f)
-    packed_b = pl.pallas_call(
-        tail_kernel,
-        out_shape=jax.ShapeDtypeStruct((n_dp, packed_rows - down_rows, LANES), bf16),
-        in_specs=in_vmem(1),
+    up_packed = packed_rows - down_rows
+    more = pl.cdiv(3 * (tokens // LANES), up_packed)
+    message = pl.pallas_call(
+        message_kernel,
+        out_shape=jax.ShapeDtypeStruct((n_dp + more, up_packed, LANES), bf16),
+        in_specs=anywhere(1) + in_vmem(1),
         out_specs=in_vmem(1)[0],
+        scratch_shapes=[pltpu.SemaphoreType.DMA],
         compiler_params=params(),
-    )(own_f)
-    other_b = [to_chip(packed_b, step) for step in steps]
-
-    for half in range(1, halves):
-        swap_half(half, other_b)
-
-    squares, _ = lax.optimization_barrier((squares, other_b))
+    )(own_f, squares)
+    messages = [to_chip(message, step) for step in steps]
     inv_rms = pl.pallas_call(
-        functools.partial(inverse_kernel, width),
+        functools.partial(inverse_kernel, width, n_dp),
         out_shape=jax.ShapeDtypeStruct((tokens, LANES), f32),
         in_specs=in_vmem(chips),
         out_specs=in_vmem(1)[0],
         compiler_params=params(),
-    )(squares, *[to_chip(squares, step) for step in steps])
+    )(squares, *messages)
 
     scale = 0.5 / math.sqrt(width * rank)
 
     received = {}
-    after = [inv_rms]
+    after = []
     weights_shape = jax.ShapeDtypeStruct((CORES * features, wide), bf16)
     product_shape = jax.ShapeDtypeStruct((some, wide), bf16)
     for half, group in enumerate(groups):
         static = (scale, parts, up_rows, group, columns)
+        if half > 0:
+            swap_half(half, after)
         for step in steps:
             blocks = [value for strip in group for value in outside[strip][step - 1]]
             weights, product = pl.pallas_call(
                 functools.partial(outside_kernel, static, chips, step, turn),
                 out_shape=(weights_shape, product_shape),
-                in_specs=in_vmem(4 + len(blocks) + len(after)),
+                in_specs=in_vmem(3) + anywhere(1) + in_vmem(len(blocks) + len(after)),
                 out_specs=tuple(in_vmem(2)),
+                scratch_shapes=[
+                    pltpu.VMEM((some, CORES * features), bf16),
+                    pltpu.SemaphoreType.DMA,
+                ],
                 compiler_params=params(),
-            )(own_f, sibling_f, other_b[step - 1], x[0], *blocks, *after)
+            )(own_f, sibling_f, messages[step - 1], x[0], *blocks, *after)
             after = [product]
             received.setdefault((0, half), []).append(to_chip(product, chips - step))
             for k in range(1, TOKEN_HALVES):

time: 94.9 us -> 94.2 us (level)
  local copies, waits for them, and re-layouts: 14.4 us -> 3.28 us
  waiting for transfers between devices: 21.4 us -> 31.7 us
    ppermute x4, waiting for transfers between devices: 1.42 us -> 18.4 us  [swap_half(): outside[strip].append((piece, lax.ppermute(piece, 'dp', pairs)))]
    unnamed x42 -> x22, local copies, waits for them, and re-layouts: 14.4 us -> 3.28 us
    pallas_call x4 -> x3, Pallas kernels: 6.04 us -> 10.9 us  [the longest x1 10.6 us: body(): pl.pallas_call(prepare_kernel, grid=(TOKEN_HALVES * groups_of,), out_shap...]
    ppermute x8 -> x7, waiting for transfers between devices: 17 us -> 12.2 us  [to_chip(): return lax.ppermute(value, 'tensor', pairs)]
    ppermute x8 -> x7, starting transfers between devices: 9.18 us -> 6.81 us  [to_chip(): return lax.ppermute(value, 'tensor', pairs)]
    pallas_call x2, Pallas kernels: 2.26 us -> 0.09 us  [swap_half(): pl.pallas_call(split_kernel, out_shape=(jax.ShapeDtypeStruct((features, L...]
    all_to_all x1, waiting for transfers between devices: 1.86 us -> 0.01 us  [body(): exchanged = lax.all_to_all(packed, 'dp', 0, 0, tiled=True)]
    all_to_all x1, starting transfers between devices: 4.17 us -> 6.01 us  [body(): own_f = lax.all_to_all(sent, 'dp', 0, 0, tiled=True)]
  transfers between devices with their start and end apart: 17 -> 16, of which waited for: 11 -> 8; matrix products, arithmetic and copies ran while one was open for 0% -> 0% of each run, Pallas kernels for 32% -> 33%
where the time goes in v11:
time: 94.2 us; the launch traced here: 93.6 us
  Pallas kernels  31.9 us (34%)
  waiting for transfers between devices  31.7 us (34%)
  starting transfers between devices  25.9 us (27%)
  local copies, waits for them, and re-layouts  3.28 us (3%)
    ppermute x4, waiting for transfers between devices, swap_half(): outside[strip].append((piece, lax.ppermute(piece, 'dp', pairs)))  18.4 us
    ppermute x7, waiting for transfers between devices, to_chip(): return lax.ppermute(value, 'tensor', pairs)  12.2 us
    pallas_call x1, Pallas kernels, body(): pl.pallas_call(prepare_kernel, grid=(TOKEN_HALVES * groups_of,), out_shap...  10.6 us
    all_to_all x1, starting transfers between devices, body(): exchanged = lax.all_to_all(packed, 'dp', 0, 0, tiled=True)  6.88 us
    ppermute x7, starting transfers between devices, to_chip(): return lax.ppermute(value, 'tensor', pairs)  6.81 us
    all_to_all x1, starting transfers between devices, body(): own_f = lax.all_to_all(sent, 'dp', 0, 0, tiled=True)  6.01 us
    ppermute x4, starting transfers between devices, swap_half(): outside[strip].append((piece, lax.ppermute(piece, 'dp', pairs)))  5.63 us
    pallas_call x1, Pallas kernels, body(): pl.pallas_call(functools.partial(own_kernel, static), out_shape=(jax.Shap...  4.88 us
  transfers between devices with their start and end apart: 16, of which 8 were waited for; matrix products, arithmetic and copies ran while one was open for 0% of the time, Pallas kernels for 33%

profile of v11, /device:TPU:0, one launch (start us, length us, event | category | flops | bytes accessed | tf_op | source)
XLA Modules:
  0.0 93.6 jit_solution(13227153297757060844)
XLA Ops:
  0.6 0.5 collective-permute-start
  1.2 0.0 copy-start.6
  1.2 3.3 %shard_map.130 = (bf16[8,192,128]{2,1,0:T(8,128)(2,1)}, f32[3,128,384]{2,1,0:T(8,128)}, f32[3,8,512]{2,1,0:T(8,128)}, bf16[2,1280,128]{2,1,0:T(8,128)(2,1)}, bf16[2,1280,128]{2,1,0:T(8,128)(2,1)}) custom-call(f32[128,1280]{1,0:T(8,128)} %bitcast.20, f32[64,512]{1,0:T(8,128)} %bitcast.24, bf16[5120,512]{1,0:T(8,128)(2,1)} %sibling_block.1, ...), custom_call_target="tpu_custom_call" | custom-call | tf_op jit(solution)/shard_map/pallas_call | solution.py:401
  4.4 6.9 %all-to-all-start = ((bf16[8,192,128]{2,1,0:T(8,128)(2,1)}), bf16[8,192,128]{2,1,0:T(8,128)(2,1)S(1)}, u32[]{:S(2)}, u32[]{:S(2)}) async-start(bf16[8,192,128]{2,1,0:T(8,128)(2,1)} %get-tuple-element.30), calls=%async_computation | async-start | bytes 786432 | tf_op jit(solution)/shard_map/all_to_all | solution.py:413
  11.3 1.5 %collective-permute-start.2 = (bf16[2,1280,128]{2,1,0:T(8,128)(2,1)}, bf16[2,1280,128]{2,1,0:T(8,128)(2,1)S(1)}, u32[]{:S(2)}, u32[]{:S(2)}) collective-permute-start(bf16[2,1280,128]{2,1,0:T(8,128)(2,1)} %get-tuple-element.38), channel_id=1, source_target_pairs={{0,2},{1,3},{2,0},{3,1},{4,6},{5,7},{6,4},{7,5},{8,10},{9,11},{10,... | collective-permute-start | bytes 1966088 | tf_op jit(solution)/shard_map/ppermute | solution.py:371
  12.8 0.0 copy-done.6
  12.8 0.0 copy-start.5
  12.8 0.1 collective-permute-start.1
  12.9 1.2 %collective-permute-done.1.sibling_gain = f32[1,1280]{1,0:T(1,128)S(1)} collective-permute-done((f32[1,1280]{1,0:T(1,128)S(1)}, f32[1,1280]{1,0:T(1,128)S(1)}, u32[]{:S(2)}, u32[]{:S(2)}) %collective-permute-start.1) | collective-permute-done | bytes 5152 | tf_op jit(solution)/shard_map/ppermute | solution.py:363
  14.1 0.0 copy-start.7
  14.1 0.0 collective-permute-done.sibling_ref
  14.1 0.0 copy-done.5
  14.1 0.6 copy-done.7
  14.6 10.6 %shard_map.131 = (bf16[640,2560]{1,0:T(8,128)(2,1)}, bf16[640,2560]{1,0:T(8,128)(2,1)}, f32[10,128]{1,0:T(8,128)}) custom-call(bf16[1280,1280]{1,0:T(8,128)(2,1)} %own_ref.1, bf16[1280,1280]{1,0:T(8,128)(2,1)} %collective-permute-done.sibling_ref, f32[1,1280]{1,0:T(1,128)} %copy-done.5, f32[1,1280]{1,0:T(1,128)} %copy-done.7), custom_call_target="tpu_custom_call" | custom-call | tf_op jit(solution)/shard_map/pallas_call | solution.py:440
  25.3 0.0 copy-start.8
  25.3 0.0 copy-start.3
  25.3 0.0 all-to-all-done.grad_in
  25.3 0.0 copy-start.4
  25.3 0.7 copy-done.4
  26.0 2.5 %shard_map.132 = (f32[3,128,160]{2,1,0:T(8,128)}, f32[3,8,512]{2,1,0:T(8,128)}, bf16[8,192,128]{2,1,0:T(8,128)(2,1)}) custom-call(bf16[8,192,128]{2,1,0:T(8,128)(2,1)} %copy-done.4, f32[3,128,384]{2,1,0:T(8,128)} %get-tuple-element.33.down_in, f32[3,8,512]{2,1,0:T(8,128)} %get-tuple-element.34.up_in), custom_call_target="tpu_custom_call" | custom-call | tf_op jit(solution)/shard_map/pallas_call | solution.py:458
  28.5 6.0 %all-to-all-start.1 = ((bf16[8,192,128]{2,1,0:T(8,128)(2,1)}), bf16[8,192,128]{2,1,0:T(8,128)(2,1)S(1)}, u32[]{:S(2)}, u32[]{:S(2)}) async-start(bf16[8,192,128]{2,1,0:T(8,128)(2,1)} %get-tuple-element.37), calls=%async_computation.1 | async-start | bytes 786432 | tf_op jit(solution)/shard_map/all_to_all | solution.py:475
  34.5 0.0 collective-permute-done.2.in_ref
  34.6 2.1 %collective-permute-start.3 = (bf16[1280,128]{1,0:T(8,128)(2,1)S(1)}, bf16[1280,128]{1,0:T(8,128)(2,1)S(1)}, u32[]{:S(2)}, u32[]{:S(2)}) collective-permute-start(bf16[1280,128]{1,0:T(8,128)(2,1)S(1)} %get-tuple-element.40.refs_0_), channel_id=1, source_target_pairs={{0,4},{4,0},{8,12},{12,8},{16,20},{20,16},{24,28},{28,24},{1,5},{5... | collective-permute-start | bytes 983048 | tf_op jit(solution)/shard_map/ppermute | solution.py:494
  36.7 1.5 %collective-permute-start.4 = (bf16[1280,128]{1,0:T(8,128)(2,1)S(1)}, bf16[1280,128]{1,0:T(8,128)(2,1)S(1)}, u32[]{:S(2)}, u32[]{:S(2)}) collective-permute-start(bf16[1280,128]{1,0:T(8,128)(2,1)S(1)} %get-tuple-element.41.refs_2_), channel_id=1, source_target_pairs={{0,8},{4,12},{8,0},{12,4},{16,24},{20,28},{24,16},{28,20},{1,9},{5... | collective-permute-start | bytes 983048 | tf_op jit(solution)/shard_map/ppermute | solution.py:494
  38.1 0.0 copy-done.8
  38.1 0.5 collective-permute-start.7
  38.7 9.8 %collective-permute-done.3.refs_1_ = bf16[1280,128]{1,0:T(8,128)(2,1)S(1)} collective-permute-done((bf16[1280,128]{1,0:T(8,128)(2,1)S(1)}, bf16[1280,128]{1,0:T(8,128)(2,1)S(1)}, u32[]{:S(2)}, u32[]{:S(2)}) %collective-permute-start.3) | collective-permute-done | bytes 327712 | tf_op jit(solution)/shard_map/ppermute | solution.py:494
  48.5 2.1 %collective-permute-done.4.refs_3_ = bf16[1280,128]{1,0:T(8,128)(2,1)S(1)} collective-permute-done((bf16[1280,128]{1,0:T(8,128)(2,1)S(1)}, bf16[1280,128]{1,0:T(8,128)(2,1)S(1)}, u32[]{:S(2)}, u32[]{:S(2)}) %collective-permute-start.4) | collective-permute-done | bytes 327712 | tf_op jit(solution)/shard_map/ppermute | solution.py:494
  50.6 0.0 all-to-all-done.1.factor_ref.own_f
  50.6 0.0 collective-permute-start.5
  50.6 0.0 copy-done.3
  50.6 0.6 collective-permute-start.6
  51.2 4.2 %collective-permute-done.6.b_ref.refs_0_ = bf16[9,32,128]{2,1,0:T(8,128)(2,1)S(1)} collective-permute-done((bf16[9,32,128]{2,1,0:T(8,128)(2,1)S(1)}, bf16[9,32,128]{2,1,0:T(8,128)(2,1)S(1)}, u32[]{:S(2)}, u32[]{:S(2)}) %collective-permute-start.6) | collective-permute-done | bytes 73760 | tf_op jit(solution)/shard_map/ppermute | solution.py:371
  55.4 0.0 collective-permute-done.5.sibling_f
  55.4 1.9 %copy-done.1 = bf16[640,2560]{1,0:T(8,128)(2,1)S(1)} copy-done((bf16[640,2560]{1,0:T(8,128)(2,1)S(1)}, bf16[640,2560]{1,0:T(8,128)(2,1)}, u32[]{:S(2)}) %copy-start.1) | copy-done | bytes 3276824
  57.3 2.2 %shard_map.135 = (bf16[2560,256]{1,0:T(8,128)(2,1)S(1)}, bf16[640,256]{1,0:T(8,128)(2,1)S(1)}) custom-call(bf16[8,192,128]{2,1,0:T(8,128)(2,1)S(1)} %all-to-all-done.1.factor_ref.own_f, bf16[8,192,128]{2,1,0:T(8,128)(2,1)S(1)} %collective-permute-done.5.sibling_f, bf16[9,32,128]{2,1,0:T(8,128)(2,1)S(1)} %collective-permute-done.6.b_ref.refs_0_, ...), custom_call_target="tpu_custom_call" | custom-call | tf_op jit(solution)/shard_map/pallas_call | solution.py:530
  59.5 0.0 copy-done
  59.5 0.0 copy-start.2
  59.6 1.2 %shard_map.136.refs_5_ = bf16[640,256]{1,0:T(8,128)(2,1)S(1)} custom-call(bf16[640,2560]{1,0:T(8,128)(2,1)S(1)} %copy-done, bf16[2560,256]{1,0:T(8,128)(2,1)S(1)} %get-tuple-element.49.weights), custom_call_target="tpu_custom_call" | custom-call | tf_op jit(solution)/shard_map/pallas_call | solution.py:544
  60.7 0.0 collective-permute-done.7.in_ref
  60.8 0.0 slice-start
  60.8 1.5 %collective-permute-start.8 = (bf16[1280,128]{1,0:T(8,128)(2,1)S(1)}, bf16[1280,128]{1,0:T(8,128)(2,1)S(1)}, u32[]{:S(2)}, u32[]{:S(2)}) collective-permute-start(bf16[1280,128]{1,0:T(8,128)(2,1)S(1)} %get-tuple-element.51.refs_0_), channel_id=1, source_target_pairs={{0,4},{4,0},{8,12},{12,8},{16,20},{20,16},{24,28},{28,24},{1,5},{5... | collective-permute-start | bytes 983048 | tf_op jit(solution)/shard_map/ppermute | solution.py:494
  62.4 0.6 collective-permute-start.9
  62.9 0.6 collective-permute-start.10
  63.5 1.5 %collective-permute-start.13 = (bf16[640,256]{1,0:T(8,128)(2,1)S(1)}, bf16[640,256]{1,0:T(8,128)(2,1)S(1)}, u32[]{:S(2)}, u32[]{:S(2)}) collective-permute-start(bf16[640,256]{1,0:T(8,128)(2,1)S(1)} %shard_map.136.refs_5_), channel_id=1, source_target_pairs={{0,2},{1,3},{2,0},{3,1},{4,6},{5,7},{6,4},{7,5},{8,10},{9,11},{10,... | collective-permute-start | bytes 983048 | tf_op jit(solution)/shard_map/ppermute | solution.py:371
  64.9 5.3 %collective-permute-done.8.refs_1_ = bf16[1280,128]{1,0:T(8,128)(2,1)S(1)} collective-permute-done((bf16[1280,128]{1,0:T(8,128)(2,1)S(1)}, bf16[1280,128]{1,0:T(8,128)(2,1)S(1)}, u32[]{:S(2)}, u32[]{:S(2)}) %collective-permute-start.8) | collective-permute-done | bytes 327712 | tf_op jit(solution)/shard_map/ppermute | solution.py:494
  70.2 1.2 %collective-permute-done.9.refs_3_ = bf16[1280,128]{1,0:T(8,128)(2,1)S(1)} collective-permute-done((bf16[1280,128]{1,0:T(8,128)(2,1)S(1)}, bf16[1280,128]{1,0:T(8,128)(2,1)S(1)}, u32[]{:S(2)}, u32[]{:S(2)}) %collective-permute-start.9) | collective-permute-done | bytes 327712 | tf_op jit(solution)/shard_map/ppermute | solution.py:494
  71.4 0.0 copy-done.2
  71.4 2.2 %shard_map.138 = (bf16[2560,256]{1,0:T(8,128)(2,1)S(1)}, bf16[640,256]{1,0:T(8,128)(2,1)S(1)}) custom-call(bf16[8,192,128]{2,1,0:T(8,128)(2,1)S(1)} %all-to-all-done.1.factor_ref.own_f, bf16[8,192,128]{2,1,0:T(8,128)(2,1)S(1)} %collective-permute-done.5.sibling_f, bf16[9,32,128]{2,1,0:T(8,128)(2,1)S(1)} %collective-permute-done.6.b_ref.refs_0_, ...), custom_call_target="tpu_custom_call" | custom-call | tf_op jit(solution)/shard_map/pallas_call | solution.py:530
  73.6 0.6 collective-permute-start.12
  74.2 1.2 %shard_map.139.refs_3_ = bf16[640,256]{1,0:T(8,128)(2,1)S(1)} custom-call(bf16[640,2560]{1,0:T(8,128)(2,1)S(1)} %copy-done, bf16[2560,256]{1,0:T(8,128)(2,1)S(1)} %get-tuple-element.54.weights), custom_call_target="tpu_custom_call" | custom-call | tf_op jit(solution)/shard_map/pallas_call | solution.py:544
  75.4 1.6 %collective-permute-start.11 = (bf16[640,256]{1,0:T(8,128)(2,1)S(1)}, bf16[640,256]{1,0:T(8,128)(2,1)S(1)}, u32[]{:S(2)}, u32[]{:S(2)}) collective-permute-start(bf16[640,256]{1,0:T(8,128)(2,1)S(1)} %shard_map.139.refs_3_), channel_id=1, source_target_pairs={{0,2},{1,3},{2,0},{3,1},{4,6},{5,7},{6,4},{7,5},{8,10},{9,11},{10,... | collective-permute-start | bytes 983048 | tf_op jit(solution)/shard_map/ppermute | solution.py:371
  77.0 0.2 shard_map.141.inv
  77.2 0.0 collective-permute-done.10.refs_4_.refs_0_
  77.2 0.0 slice-done
  77.2 0.0 slice-done.1
  77.2 4.9 %shard_map.140 = (f32[1280,256]{1,0:T(8,128)S(1)}, f32[1280,256]{1,0:T(8,128)S(1)}) custom-call(bf16[8,192,128]{2,1,0:T(8,128)(2,1)S(1)} %all-to-all-done.1.factor_ref.own_f, bf16[8,192,128]{2,1,0:T(8,128)(2,1)S(1)} %collective-permute-done.5.sibling_f, bf16[5120,512]{1,0:T(8,128)(2,1)S(1)} %bitcast.19, bf16[5120,512]{1,0:T(8,128)(2,1)S(1)} %bitcast.19, ...), custom_call_target="tpu_custom_call" | custom-call | flops 3355443200 | bytes 6553600 | tf_op jit(solution)/shard_map/pallas_call | solution.py:556
  82.1 0.9 shard_map.142.refs_1_
  83.0 0.0 collective-permute-done.13.refs_0_
  83.0 0.9 shard_map.143.refs_1_
  83.9 3.7 %collective-permute-done.12.refs_0_ = bf16[640,256]{1,0:T(8,128)(2,1)S(1)} collective-permute-done((bf16[640,256]{1,0:T(8,128)(2,1)S(1)}, bf16[640,256]{1,0:T(8,128)(2,1)S(1)}, u32[]{:S(2)}, u32[]{:S(2)}) %collective-permute-start.12) | collective-permute-done | bytes 327712 | tf_op jit(solution)/shard_map/ppermute | solution.py:371
  87.6 0.9 shard_map.144.refs_1_
  88.5 4.3 %collective-permute-done.11.refs_0_ = bf16[640,256]{1,0:T(8,128)(2,1)S(1)} collective-permute-done((bf16[640,256]{1,0:T(8,128)(2,1)S(1)}, bf16[640,256]{1,0:T(8,128)(2,1)S(1)}, u32[]{:S(2)}, u32[]{:S(2)}) %collective-permute-start.11) | collective-permute-done | bytes 327712 | tf_op jit(solution)/shard_map/ppermute | solution.py:371
  92.8 0.9 shard_map.145
  (8 shorter events, 0.1 us)
Async XLA Ops:
  0.6 13.4 %collective-permute-start = (bf16[1280,1280]{1,0:T(8,128)(2,1)}, bf16[1280,1280]{1,0:T(8,128)(2,1)}, u32[]{:S(2)}, u32[]{:S(2)}) collective-permute-start(bf16[1280,1280]{1,0:T(8,128)(2,1)} %own_ref.1), channel_id=1, source_target_pairs={{0,1},{1,0},{2,3},{3,2},{4,5},{5,4},{6,7},{7,6},{8,9},{9,8},{10,11... | collective-permute-start | bytes 9830408 | tf_op jit(solution)/shard_map/ppermute | solution.py:363
  1.2 11.7 %copy-start.6 = (f32[1280]{0:T(1024)S(1)}, f32[1280]{0:T(1024)}, u32[]{:S(2)}) copy-start(f32[1280]{0:T(1024)} %param.12) | copy-start | bytes 15364
  4.4 20.9 %all-to-all-start = ((bf16[8,192,128]{2,1,0:T(8,128)(2,1)}), bf16[8,192,128]{2,1,0:T(8,128)(2,1)S(1)}, u32[]{:S(2)}, u32[]{:S(2)}) async-start(bf16[8,192,128]{2,1,0:T(8,128)(2,1)} %get-tuple-element.30), calls=%async_computation | async-start | bytes 786432 | tf_op jit(solution)/shard_map/all_to_all | solution.py:413
  11.3 23.2 %collective-permute-start.2 = (bf16[2,1280,128]{2,1,0:T(8,128)(2,1)}, bf16[2,1280,128]{2,1,0:T(8,128)(2,1)S(1)}, u32[]{:S(2)}, u32[]{:S(2)}) collective-permute-start(bf16[2,1280,128]{2,1,0:T(8,128)(2,1)} %get-tuple-element.38), channel_id=1, source_target_pairs={{0,2},{1,3},{2,0},{3,1},{4,6},{5,7},{6,4},{7,5},{8,10},{9,11},{10,... | collective-permute-start | bytes 1966088 | tf_op jit(solution)/shard_map/ppermute | solution.py:371
  12.8 1.2 %copy-start.5 = (f32[1,1280]{1,0:T(1,128)}, f32[1,1280]{1,0:T(1,128)S(1)}, u32[]{:S(2)}) copy-start(f32[1,1280]{1,0:T(1,128)S(1)} %broadcast_in_dim.3.own_gain) | copy-start | bytes 15364
  12.8 1.2 %collective-permute-start.1 = (f32[1,1280]{1,0:T(1,128)S(1)}, f32[1,1280]{1,0:T(1,128)S(1)}, u32[]{:S(2)}, u32[]{:S(2)}) collective-permute-start(f32[1,1280]{1,0:T(1,128)S(1)} %broadcast_in_dim.3.own_gain), channel_id=1, source_target_pairs={{0,1},{1,0},{2,3},{3,2},{4,5},{5,4},{6,7},{7,6},{8,9},{9,8},{10,11... | collective-permute-start | bytes 15368 | tf_op jit(solution)/shard_map/ppermute | solution.py:363
  14.1 0.6 copy-start.7
  25.3 12.9 %copy-start.8 = (bf16[2,1280,128]{2,1,0:T(8,128)(2,1)S(1)}, bf16[2,1280,128]{2,1,0:T(8,128)(2,1)}, u32[]{:S(2)}) copy-start(bf16[2,1280,128]{2,1,0:T(8,128)(2,1)} %get-tuple-element.47) | copy-start | bytes 1966084
  25.3 25.3 %copy-start.3 = (f32[10,128]{1,0:T(8,128)S(1)}, f32[10,128]{1,0:T(8,128)}, u32[]{:S(2)}) copy-start(f32[10,128]{1,0:T(8,128)} %get-tuple-element.45.sums_ref) | copy-start | bytes 15364
  25.3 0.7 copy-start.4
  28.5 22.1 %all-to-all-start.1 = ((bf16[8,192,128]{2,1,0:T(8,128)(2,1)}), bf16[8,192,128]{2,1,0:T(8,128)(2,1)S(1)}, u32[]{:S(2)}, u32[]{:S(2)}) async-start(bf16[8,192,128]{2,1,0:T(8,128)(2,1)} %get-tuple-element.37), calls=%async_computation.1 | async-start | bytes 786432 | tf_op jit(solution)/shard_map/all_to_all | solution.py:475
  34.6 13.9 %collective-permute-start.3 = (bf16[1280,128]{1,0:T(8,128)(2,1)S(1)}, bf16[1280,128]{1,0:T(8,128)(2,1)S(1)}, u32[]{:S(2)}, u32[]{:S(2)}) collective-permute-start(bf16[1280,128]{1,0:T(8,128)(2,1)S(1)} %get-tuple-element.40.refs_0_), channel_id=1, source_target_pairs={{0,4},{4,0},{8,12},{12,8},{16,20},{20,16},{24,28},{28,24},{1,5},{5... | collective-permute-start | bytes 983048 | tf_op jit(solution)/shard_map/ppermute | solution.py:494
  36.7 13.9 %collective-permute-start.4 = (bf16[1280,128]{1,0:T(8,128)(2,1)S(1)}, bf16[1280,128]{1,0:T(8,128)(2,1)S(1)}, u32[]{:S(2)}, u32[]{:S(2)}) collective-permute-start(bf16[1280,128]{1,0:T(8,128)(2,1)S(1)} %get-tuple-element.41.refs_2_), channel_id=1, source_target_pairs={{0,8},{4,12},{8,0},{12,4},{16,24},{20,28},{24,16},{28,20},{1,9},{5... | collective-permute-start | bytes 983048 | tf_op jit(solution)/shard_map/ppermute | solution.py:494
  38.1 22.6 %collective-permute-start.7 = (bf16[2,1280,128]{2,1,0:T(8,128)(2,1)S(1)}, bf16[2,1280,128]{2,1,0:T(8,128)(2,1)S(1)}, u32[]{:S(2)}, u32[]{:S(2)}) collective-permute-start(bf16[2,1280,128]{2,1,0:T(8,128)(2,1)S(1)} %copy-done.8), channel_id=1, source_target_pairs={{0,2},{1,3},{2,0},{3,1},{4,6},{5,7},{6,4},{7,5},{8,10},{9,11},{10,... | collective-permute-start | bytes 1966088 | tf_op jit(solution)/shard_map/ppermute | solution.py:371
  50.6 4.8 %collective-permute-start.5 = (bf16[8,192,128]{2,1,0:T(8,128)(2,1)S(1)}, bf16[8,192,128]{2,1,0:T(8,128)(2,1)S(1)}, u32[]{:S(2)}, u32[]{:S(2)}) collective-permute-start(bf16[8,192,128]{2,1,0:T(8,128)(2,1)S(1)} %all-to-all-done.1.factor_ref.own_f), channel_id=1, source_target_pairs={{0,1},{1,0},{2,3},{3,2},{4,5},{5,4},{6,7},{7,6},{8,9},{9,8},{10,11... | collective-permute-start | bytes 1179656 | tf_op jit(solution)/shard_map/ppermute | solution.py:363
  50.6 4.8 %collective-permute-start.6 = (bf16[9,32,128]{2,1,0:T(8,128)(2,1)S(1)}, bf16[9,32,128]{2,1,0:T(8,128)(2,1)S(1)}, u32[]{:S(2)}, u32[]{:S(2)}) collective-permute-start(bf16[9,32,128]{2,1,0:T(8,128)(2,1)S(1)} %shard_map.134), channel_id=1, source_target_pairs={{0,2},{1,3},{2,0},{3,1},{4,6},{5,7},{6,4},{7,5},{8,10},{9,11},{10,... | collective-permute-start | bytes 221192 | tf_op jit(solution)/shard_map/ppermute | solution.py:371
  55.4 1.9 %copy-start.1 = (bf16[640,2560]{1,0:T(8,128)(2,1)S(1)}, bf16[640,2560]{1,0:T(8,128)(2,1)}, u32[]{:S(2)}) copy-start(bf16[640,2560]{1,0:T(8,128)(2,1)} %get-tuple-element.43.x_in.refs_0_) | copy-start | bytes 9830404
  57.3 2.2 %copy-start = (bf16[640,2560]{1,0:T(8,128)(2,1)S(1)}, bf16[640,2560]{1,0:T(8,128)(2,1)}, u32[]{:S(2)}) copy-start(bf16[640,2560]{1,0:T(8,128)(2,1)} %get-tuple-element.44.x.refs_1_) | copy-start | bytes 9830404
  59.5 11.9 %copy-start.2 = (bf16[640,2560]{1,0:T(8,128)(2,1)S(1)}, bf16[640,2560]{1,0:T(8,128)(2,1)}, u32[]{:S(2)}) copy-start(bf16[640,2560]{1,0:T(8,128)(2,1)} %get-tuple-element.43.x_in.refs_0_) | copy-start | bytes 9830404
  60.8 16.5 %slice-start = ((s8[5242880]{0:T(1024)(128)(4,1)}), s8[4194304]{0:T(1024)(128)(4,1)S(1)}, s32[]{:S(2)}) async-start(s8[5242880]{0:T(1024)(128)(4,1)} %bitcast.18), calls=%async_computation.2 | async-start | bytes 8388608
  60.8 9.4 %collective-permute-start.8 = (bf16[1280,128]{1,0:T(8,128)(2,1)S(1)}, bf16[1280,128]{1,0:T(8,128)(2,1)S(1)}, u32[]{:S(2)}, u32[]{:S(2)}) collective-permute-start(bf16[1280,128]{1,0:T(8,128)(2,1)S(1)} %get-tuple-element.51.refs_0_), channel_id=1, source_target_pairs={{0,4},{4,0},{8,12},{12,8},{16,20},{20,16},{24,28},{28,24},{1,5},{5... | collective-permute-start | bytes 983048 | tf_op jit(solution)/shard_map/ppermute | solution.py:494
  62.4 14.9 %slice-start.1 = ((s8[5242880]{0:T(1024)(128)(4,1)}), s8[1048576]{0:T(1024)(128)(4,1)S(1)}, s32[]{:S(2)}) async-start(s8[5242880]{0:T(1024)(128)(4,1)} %bitcast.18), calls=%async_computation.3 | async-start | bytes 2097152
  62.4 9.1 %collective-permute-start.9 = (bf16[1280,128]{1,0:T(8,128)(2,1)S(1)}, bf16[1280,128]{1,0:T(8,128)(2,1)S(1)}, u32[]{:S(2)}, u32[]{:S(2)}) collective-permute-start(bf16[1280,128]{1,0:T(8,128)(2,1)S(1)} %get-tuple-element.52.refs_2_), channel_id=1, source_target_pairs={{0,8},{4,12},{8,0},{12,4},{16,24},{20,28},{24,16},{28,20},{1,9},{5... | collective-permute-start | bytes 983048 | tf_op jit(solution)/shard_map/ppermute | solution.py:494
  62.9 14.3 %collective-permute-start.10 = (bf16[640,256]{1,0:T(8,128)(2,1)S(1)}, bf16[640,256]{1,0:T(8,128)(2,1)S(1)}, u32[]{:S(2)}, u32[]{:S(2)}) collective-permute-start(bf16[640,256]{1,0:T(8,128)(2,1)S(1)} %get-tuple-element.48.refs_4_), channel_id=1, source_target_pairs={{0,2},{1,3},{2,0},{3,1},{4,6},{5,7},{6,4},{7,5},{8,10},{9,11},{10,... | collective-permute-start | bytes 983048 | tf_op jit(solution)/shard_map/ppermute | solution.py:371
  63.5 19.5 %collective-permute-start.13 = (bf16[640,256]{1,0:T(8,128)(2,1)S(1)}, bf16[640,256]{1,0:T(8,128)(2,1)S(1)}, u32[]{:S(2)}, u32[]{:S(2)}) collective-permute-start(bf16[640,256]{1,0:T(8,128)(2,1)S(1)} %shard_map.136.refs_5_), channel_id=1, source_target_pairs={{0,2},{1,3},{2,0},{3,1},{4,6},{5,7},{6,4},{7,5},{8,10},{9,11},{10,... | collective-permute-start | bytes 983048 | tf_op jit(solution)/shard_map/ppermute | solution.py:371
  73.6 14.0 %collective-permute-start.12 = (bf16[640,256]{1,0:T(8,128)(2,1)S(1)}, bf16[640,256]{1,0:T(8,128)(2,1)S(1)}, u32[]{:S(2)}, u32[]{:S(2)}) collective-permute-start(bf16[640,256]{1,0:T(8,128)(2,1)S(1)} %get-tuple-element.53.refs_2_), channel_id=1, source_target_pairs={{0,2},{1,3},{2,0},{3,1},{4,6},{5,7},{6,4},{7,5},{8,10},{9,11},{10,... | collective-permute-start | bytes 983048 | tf_op jit(solution)/shard_map/ppermute | solution.py:371
  75.4 17.4 %collective-permute-start.11 = (bf16[640,256]{1,0:T(8,128)(2,1)S(1)}, bf16[640,256]{1,0:T(8,128)(2,1)S(1)}, u32[]{:S(2)}, u32[]{:S(2)}) collective-permute-start(bf16[640,256]{1,0:T(8,128)(2,1)S(1)} %shard_map.139.refs_3_), channel_id=1, source_target_pairs={{0,2},{1,3},{2,0},{3,1},{4,6},{5,7},{6,4},{7,5},{8,10},{9,11},{10,... | collective-permute-start | bytes 983048 | tf_op jit(solution)/shard_map/ppermute | solution.py:371

commit v12 on v11

--- a/solution.py
+++ b/solution.py
@@ -14,8 +14,10 @@
 LANES = 128
 COLUMN_HALVES = 2
 TOKEN_HALVES = 2
+FACTOR_PIECES = 2
 VMEM_BYTES = 16 * 2**20
 LARGE_VMEM_BYTES = 58 * 2**20
+PREPARE_VMEM_BYTES = 40 * 2**20
 
 
 def adaptive_moment_update(param, first, second, grad_mean):
@@ -105,42 +107,60 @@
         out[...] = in_ref[k]
 
 
-def prepare_kernel(own_ref, sibling_ref, own_gain, sibling_gain, *refs):
-    xs, (sums_ref, squares) = refs[:-2], refs[-2:]
+def prepare(own_ref, sibling_ref, own_gain, sibling_gain, x_ref, sums_ref, squares):
     block, features = own_ref.shape
-    step, steps = pl.program_id(0), pl.num_programs(0)
+    step = pl.program_id(0)
     tile = 16 if block % 16 == 0 else block
-    for k, x_ref in enumerate(xs):
-
-        @pl.when(step // (steps // len(xs)) == k)
-        def _():
-            @pl.loop(0, block // tile, unroll=2)
-            def _(i):
-                at = pl.ds(pl.multiple_of(i * tile, tile), tile)
-                own = own_ref[at, :].astype(jnp.float32)
-                x_ref[at, :features] = (own * own_gain[...]).astype(x_ref.dtype)
-                total = own * own
-                sibling = sibling_ref[at, :].astype(jnp.float32)
-                x_ref[at, features:] = (sibling * sibling_gain[...]).astype(x_ref.dtype)
-                total += sibling * sibling
-                total = jnp.sum(total, axis=1, keepdims=True)
-                to = pl.ds(pl.multiple_of(step * block + i * tile, tile), tile)
-                squares[to, :] = jnp.broadcast_to(total, (tile, LANES))
-
-    @pl.when(step == steps - 1)
+
+    @pl.loop(0, block // tile, unroll=2)
+    def _(i):
+        at = pl.ds(pl.multiple_of(i * tile, tile), tile)
+        to = pl.ds(pl.multiple_of(step * block + i * tile, tile), tile)
+        own = own_ref[at, :].astype(jnp.float32)
+        x_ref[to, :features] = (own * own_gain[...]).astype(x_ref.dtype)
+        total = own * own
+        sibling = sibling_ref[at, :].astype(jnp.float32)
+        x_ref[to, features:] = (sibling * sibling_gain[...]).astype(x_ref.dtype)
+        total += sibling * sibling
+        total = jnp.sum(total, axis=1, keepdims=True)
+        squares[to, :] = jnp.broadcast_to(total, (tile, LANES))
+
+    @pl.when(step == pl.num_programs(0) - 1)
     def _():
         for i in range(sums_ref.shape[0]):
             sums_ref[i : i + 1] = squares[i * LANES : (i + 1) * LANES, :].T[:1]
 
-
-def message_kernel(factor_ref, sums_ref, out_ref, sem):
+    return pl.ds(pl.multiple_of(step * block, block), block)
+
+
+def prepare_kernel(*refs):
+    prepare(*refs)
+
+
+def prepare_multiply_kernel(own_ref, sibling_ref, own_gain, sibling_gain, weights, *refs):
+    x_ref, sums_ref, product, squares = refs
+    rows = prepare(own_ref, sibling_ref, own_gain, sibling_gain, x_ref, sums_ref, squares)
+    value = jnp.dot(x_ref[rows, :], weights[...], preferred_element_type=jnp.float32)
+    product[rows, :] = value.astype(product.dtype)
+
+
+def message_kernel(factor_ref, sums_ref, out_ref, *refs):
+    pieces, sem = refs[:-1], refs[-1]
     shares, up_rows = factor_ref.shape[0], out_ref.shape[1]
-    copy = pltpu.make_async_copy(
-        factor_ref.at[:, pl.ds(factor_ref.shape[1] - up_rows, up_rows)],
-        out_ref.at[pl.ds(0, shares)],
-        sem,
-    )
-    copy.start()
+    copies = [
+        pltpu.make_async_copy(
+            factor_ref.at[:, pl.ds(factor_ref.shape[1] - up_rows, up_rows)],
+            out_ref.at[pl.ds(0, shares)],
+            sem.at[0],
+        )
+    ]
+    for k, piece in enumerate(pieces):
+        size = piece.shape[0]
+        copies.append(
+            pltpu.make_async_copy(factor_ref.at[pl.ds(k * size, size)], piece, sem.at[1 + k])
+        )
+    for copy in copies:
+        copy.start()
     left = sums_ref[...]
     terms = []
     for _ in range(3):
@@ -152,7 +172,8 @@
     rows = jnp.concatenate(terms, axis=0)
     for i in range(out_ref.shape[0] - shares):
         out_ref[shares + i] = rows[i * up_rows : (i + 1) * up_rows].astype(jnp.bfloat16)
-    copy.wait()
+    for copy in copies:
+        copy.wait()
 
 
 def inverse_kernel(width, shares, sums_ref, *refs):
@@ -160,6 +181,9 @@
     total = sums_ref[...]
     count = total.shape[0]
     for ref in messages:
+        if shares == 0:
+            total += ref[...]
+            continue
         rows = [ref[i].astype(jnp.float32) for i in range(shares, ref.shape[0])]
         rows = jnp.concatenate(rows, axis=0)
         total += rows[:count] + rows[count : 2 * count] + rows[2 * count : 3 * count]
@@ -215,8 +239,10 @@
         factor_ref[i] = rounded
 
 
-def factor_a(packed_ref, down_rows):
-    pieces = [packed_ref[i].astype(jnp.float32)[:down_rows] for i in range(packed_ref.shape[0])]
+def factor_a(refs, down_rows):
+    pieces = []
+    for ref in refs:
+        pieces += [ref[i].astype(jnp.float32)[:down_rows] for i in range(ref.shape[0])]
     return jnp.concatenate(pieces, axis=0).astype(jnp.bfloat16)
 
 
@@ -253,26 +279,24 @@
     )
 
 
-def outside_kernel(static, chips, step, turn, own_f, sibling_f, b_ref, x_in, *refs):
-    weights, product, x, sem = refs[-4:]
-    copy = pltpu.make_async_copy(x_in, x, sem)
-    copy.start()
+def outside_kernel(static, chips, step, turn, own_f, b_ref, x, *refs):
+    sibling_f, blocks = refs[:FACTOR_PIECES], refs[FACTOR_PIECES:]
+    weights, product = refs[-2:]
     strips = static[3]
-    features = refs[0].shape[0]
+    features = blocks[0].shape[0]
     down_rows = own_f.shape[1] - b_ref.shape[1]
     place, replica = lax.axis_index("tensor"), lax.axis_index("dp")
     owner = (place // CORES - step + chips) % chips * CORES + place % CORES
     b = up_factor(static, b_ref[: own_f.shape[0]], owner)
-    own_a, sibling_a = factor_a(own_f, down_rows), factor_a(sibling_f, down_rows)
+    own_a, sibling_a = factor_a([own_f], down_rows), factor_a(sibling_f, down_rows)
     for k, strip in enumerate(strips):
-        mine, other = refs[2 * k : 2 * k + 2]
+        mine, other = blocks[2 * k : 2 * k + 2]
         even = replica // turn[strip] % 2 == 0
         lanes = slice(k * LANES, (k + 1) * LANES)
         block = jnp.where(even, mine[...], other[...])
         weights[:features, lanes] = merge(static[0], block, own_a, b[:, lanes])
         block = jnp.where(even, other[...], mine[...])
         weights[features:, lanes] = merge(static[0], block, sibling_a, b[:, lanes])
-    copy.wait()
     more_kernel(x, weights, product)
 
 
@@ -283,14 +307,15 @@
     multiply(x, weights, store)
 
 
-def own_kernel(static, own_f, sibling_f, own_block, sibling_block, *refs):
+def own_kernel(static, own_block, sibling_block, own_f, *refs):
+    sibling_f, refs = refs[:FACTOR_PIECES], refs[FACTOR_PIECES:]
     xs, weights = refs[: static[5]], refs[-1]
     outs = refs[len(refs) - 1 - static[6] : -1]
     features = own_block.shape[0]
     wide = outs[0].shape[1]
     down_rows = own_f.shape[1] - len(static[3]) * static[2]
     b = up_factor(static[:5], own_f[:, down_rows:], lax.axis_index("tensor"))
-    for at, factors, block in ((0, own_f, own_block), (features, sibling_f, sibling_block)):
+    for at, factors, block in ((0, [own_f], own_block), (features, sibling_f, sibling_block)):
         weights[at : at + features] = merge(static[0], block[...], factor_a(factors, down_rows), b)
     for h, x in enumerate(xs):
 
@@ -303,11 +328,10 @@
 
 
 def finish_kernel(sources, first, own, inv, *refs):
-    rows = pl.ds(first, refs[-1].shape[0])
-    total = own[rows, :]
+    total = own[pl.ds(first, refs[-1].shape[0]), :]
     for value in refs[:sources]:
         total = total + value[...].astype(jnp.float32)
-    refs[-1][...] = (total * inv[rows, :1]).astype(refs[-1].dtype)
+    refs[-1][...] = (total * inv[:, :1]).astype(refs[-1].dtype)
 
 
 def finish(own, inv_rms, received, at, shape, before):
@@ -434,26 +458,27 @@
     gain = input_norm_gain[None, :]
     some = tokens // TOKEN_HALVES
     rows = LANES if some % LANES == 0 else some
-    groups_of = some // rows
-    token_block = pl.BlockSpec((rows, features), lambda i: (i, 0))
-    gain_block = pl.BlockSpec((1, features), lambda i: (0, 0))
-    *x, squares = pl.pallas_call(
-        prepare_kernel,
-        grid=(TOKEN_HALVES * groups_of,),
-        out_shape=(jax.ShapeDtypeStruct((some, CORES * features), bf16),) * TOKEN_HALVES
-        + (jax.ShapeDtypeStruct((tokens // LANES, LANES), f32),),
-        in_specs=[token_block, token_block, gain_block, gain_block],
-        out_specs=tuple(
-            pl.BlockSpec(
-                (rows, CORES * features),
-                lambda i, k=k: (jnp.clip(i - k * groups_of, 0, groups_of - 1), 0),
-            )
-            for k in range(TOKEN_HALVES)
+    operands = [prompt_hidden_input, to_sibling(prompt_hidden_input), gain, to_sibling(gain)]
+
+    def prepared(half, kernel, more, limit):
+        token_block = pl.BlockSpec((rows, features), lambda i: (half * (some // rows) + i, 0))
+        gain_block = pl.BlockSpec((1, features), lambda i: (0, 0))
+        out_shape = (
+            jax.ShapeDtypeStruct((some, CORES * features), bf16),
+            jax.ShapeDtypeStruct((some // LANES, LANES), f32),
         )
-        + (pl.BlockSpec((tokens // LANES, LANES), lambda i: (0, 0)),),
-        scratch_shapes=[pltpu.VMEM((tokens, LANES), f32)],
-        compiler_params=pltpu.CompilerParams(vmem_limit_bytes=LARGE_VMEM_BYTES),
-    )(prompt_hidden_input, to_sibling(prompt_hidden_input), gain, to_sibling(gain))
+        out_shape += (jax.ShapeDtypeStruct((some, wide), bf16),) * len(more)
+        return pl.pallas_call(
+            kernel,
+            grid=(some // rows,),
+            out_shape=out_shape,
+            in_specs=[token_block, token_block, gain_block, gain_block] + in_vmem(len(more)),
+            out_specs=tuple(in_vmem(len(out_shape))),
+            scratch_shapes=[pltpu.VMEM((some, LANES), f32)],
+            compiler_params=pltpu.CompilerParams(vmem_limit_bytes=limit),
+        )(*operands, *more)
+
+    x0, squares = prepared(0, prepare_kernel, [], PREPARE_VMEM_BYTES)
     exchanged, squares = lax.optimization_barrier((exchanged, squares))
     a_next, b_next, sent = pl.pallas_call(
         adam_kernel,
@@ -494,75 +519,83 @@
                 outside[strip].append((piece, lax.ppermute(piece, "dp", pairs)))
 
     swap_half(0, sent)
-    own_f, _ = lax.optimization_barrier((own_f, outside))
-    sibling_f = to_sibling(own_f)
     up_packed = packed_rows - down_rows
-    more = pl.cdiv(3 * (tokens // LANES), up_packed)
-    message = pl.pallas_call(
+    more = pl.cdiv(3 * (tokens // TOKEN_HALVES // LANES), up_packed)
+    piece = jax.ShapeDtypeStruct((n_dp // FACTOR_PIECES, packed_rows, LANES), bf16)
+    message, *pieces = pl.pallas_call(
         message_kernel,
-        out_shape=jax.ShapeDtypeStruct((n_dp + more, up_packed, LANES), bf16),
+        out_shape=(jax.ShapeDtypeStruct((n_dp + more, up_packed, LANES), bf16),)
+        + (piece,) * FACTOR_PIECES,
         in_specs=anywhere(1) + in_vmem(1),
-        out_specs=in_vmem(1)[0],
-        scratch_shapes=[pltpu.SemaphoreType.DMA],
+        out_specs=tuple(in_vmem(1 + FACTOR_PIECES)),
+        scratch_shapes=[pltpu.SemaphoreType.DMA((1 + FACTOR_PIECES,))],
         compiler_params=params(),
     )(own_f, squares)
     messages = [to_chip(message, step) for step in steps]
-    inv_rms = pl.pallas_call(
-        functools.partial(inverse_kernel, width, n_dp),
-        out_shape=jax.ShapeDtypeStruct((tokens, LANES), f32),
-        in_specs=in_vmem(chips),
-        out_specs=in_vmem(1)[0],
-        compiler_params=params(),
-    )(squares, *messages)
+    sibling_f = [to_sibling(piece) for piece in pieces]
+
+    def inverse(shares, *sums):
+        return pl.pallas_call(
+            functools.partial(inverse_kernel, width, shares),
+            out_shape=jax.ShapeDtypeStruct((some, LANES), f32),
+            in_specs=in_vmem(chips),
+            out_specs=in_vmem(1)[0],
+            compiler_params=params(),
+        )(*sums)
+
+    inv_rms = [inverse(n_dp, squares, *messages)]
 
     scale = 0.5 / math.sqrt(width * rank)
 
     received = {}
     after = []
+    x1 = None
     weights_shape = jax.ShapeDtypeStruct((CORES * features, wide), bf16)
     product_shape = jax.ShapeDtypeStruct((some, wide), bf16)
     for half, group in enumerate(groups):
         static = (scale, parts, up_rows, group, columns)
         if half > 0:
-            swap_half(half, after)
+            swap_half(half, products[0])
         for step in steps:
             blocks = [value for strip in group for value in outside[strip][step - 1]]
             weights, product = pl.pallas_call(
                 functools.partial(outside_kernel, static, chips, step, turn),
                 out_shape=(weights_shape, product_shape),
-                in_specs=in_vmem(3) + anywhere(1) + in_vmem(len(blocks) + len(after)),
+                in_specs=in_vmem(3 + FACTOR_PIECES + len(blocks)) + anywhere(len(after)),
                 out_specs=tuple(in_vmem(2)),
-                scratch_shapes=[
-                    pltpu.VMEM((some, CORES * features), bf16),
-                    pltpu.SemaphoreType.DMA,
-                ],
                 compiler_params=params(),
-            )(own_f, sibling_f, messages[step - 1], x[0], *blocks, *after)
-            after = [product]
+            )(own_f, messages[step - 1], x0, *sibling_f, *blocks, *after)
             received.setdefault((0, half), []).append(to_chip(product, chips - step))
-            for k in range(1, TOKEN_HALVES):
-                product = pl.pallas_call(
+            if x1 is None:
+                x1, sums, second = prepared(1, prepare_multiply_kernel, [weights], VMEM_BYTES)
+            else:
+                second = pl.pallas_call(
                     more_kernel,
                     out_shape=product_shape,
                     in_specs=in_vmem(2),
                     out_specs=in_vmem(1)[0],
                     compiler_params=params(),
-                )(x[k], weights)
-                after.append(product)
-                received.setdefault((k, half), []).append(to_chip(product, chips - step))
-
-    after.append(received[0, 0][0])
+                )(x1, weights)
+            products = [product, second]
+            after = [second]
+            received.setdefault((1, half), []).append(to_chip(second, chips - step))
+        if half == 0:
+            after = [received[0, 0][0]]
+            sent_sums, _ = lax.optimization_barrier((sums, products))
+            inv_rms.append(inverse(0, sums, *[to_chip(sent_sums, step) for step in steps]))
+
+    after.append(received[1, 0][0])
     static = (scale, parts, up_rows, range(strips), columns, TOKEN_HALVES, halves)
     totals = pl.pallas_call(
         functools.partial(own_kernel, static),
         out_shape=(jax.ShapeDtypeStruct((tokens, wide), f32),) * halves,
         grid=(1,),
-        in_specs=in_vmem(2)
-        + [
+        in_specs=[
             pl.BlockSpec((features, columns), lambda i: (lax.axis_index("tensor"), 0)),
             pl.BlockSpec((features, columns), lambda i: (lax.axis_index("tensor") ^ 1, 0)),
         ]
-        + in_vmem(TOKEN_HALVES + len(after)),
+        + in_vmem(1 + FACTOR_PIECES + TOKEN_HALVES)
+        + anywhere(len(after)),
         out_specs=tuple(in_vmem(halves)),
         scratch_shapes=[pltpu.VMEM((CORES * features, columns), bf16)],
         compiler_params=params(),
@@ -571,12 +604,12 @@
             bytes_accessed=4 * tokens * features,
             transcendentals=0,
         ),
-    )(own_f, sibling_f, frozen_key_value, frozen_key_value, *x, *after)
+    )(frozen_key_value, frozen_key_value, own_f, *sibling_f, x0, x1, *after)
 
     keys_values = None
     for at, pieces in received.items():
         keys_values = finish(
-            totals[at[1]], inv_rms, pieces, at, (tokens, columns), keys_values
+            totals[at[1]], inv_rms[at[0]], pieces, at, (tokens, columns), keys_values
         )
     return (a_next, b_next, keys_values)
 

time: 94.2 us -> 96 us (1.019)
  waiting for transfers between devices: 31.7 us -> 26.2 us
  local copies, waits for them, and re-layouts: 3.28 us -> 7.48 us
  Pallas kernels: 31.9 us -> 33.5 us
  starting transfers between devices: 25.9 us -> 27.4 us
    ppermute x4, waiting for transfers between devices: 18.4 us -> 1.72 us  [swap_half(): outside[strip].append((piece, lax.ppermute(piece, 'dp', pairs)))]
    all_to_all x1, waiting for transfers between devices: 0.01 us -> 5.38 us  [body(): own_f = lax.all_to_all(sent, 'dp', 0, 0, tiled=True)]
    unnamed x22 -> x16, local copies, waits for them, and re-layouts: 3.28 us -> 7.48 us
    ppermute x7 -> x8, waiting for transfers between devices: 12.2 us -> 16.1 us  [to_chip(): return lax.ppermute(value, 'tensor', pairs)]
    pallas_call x2, Pallas kernels: 0.09 us -> 3.07 us  [swap_half(): pl.pallas_call(split_kernel, out_shape=(jax.ShapeDtypeStruct((features, L...]
    pallas_call x3 -> x5, Pallas kernels: 10.9 us -> 7.94 us  [the longest x2 6.52 us: prepared(): pl.pallas_call(kernel, grid=(some // rows,), out_shape=out_shape, in_spec...]
    ppermute x7 -> x8, starting transfers between devices: 6.81 us -> 9.66 us  [to_chip(): return lax.ppermute(value, 'tensor', pairs)]
    all_to_all x1, waiting for transfers between devices: 0.01 us -> 1.85 us  [body(): exchanged = lax.all_to_all(packed, 'dp', 0, 0, tiled=True)]
  transfers between devices with their start and end apart: 16 -> 18, of which waited for: 8 -> 7; matrix products, arithmetic and copies ran while one was open for 0% -> 0% of each run, Pallas kernels for 33% -> 34%
where the time goes in v12:
time: 96 us; the launch traced here: 95.4 us
  Pallas kernels  33.5 us (35%)
  starting transfers between devices  27.4 us (29%)
  waiting for transfers between devices  26.2 us (27%)
  local copies, waits for them, and re-layouts  7.48 us (8%)
    ppermute x8, waiting for transfers between devices, to_chip(): return lax.ppermute(value, 'tensor', pairs)  16.1 us
    ppermute x8, starting transfers between devices, to_chip(): return lax.ppermute(value, 'tensor', pairs)  9.66 us
    unnamed x16, local copies, waits for them, and re-layouts  7.48 us
    all_to_all x1, starting transfers between devices, body(): exchanged = lax.all_to_all(packed, 'dp', 0, 0, tiled=True)  6.88 us
    pallas_call x2, Pallas kernels, prepared(): pl.pallas_call(kernel, grid=(some // rows,), out_shape=out_shape, in_spec...  6.52 us
    pallas_call x2, Pallas kernels, body(): pl.pallas_call(functools.partial(outside_kernel, static, chips, step, tur...  6.13 us
    pallas_call x1, Pallas kernels, body(): pl.pallas_call(functools.partial(own_kernel, static), out_shape=(jax.Shap...  5.88 us
    ppermute x4, starting transfers between devices, swap_half(): outside[strip].append((piece, lax.ppermute(piece, 'dp', pairs)))  5.61 us
  transfers between devices with their start and end apart: 18, of which 7 were waited for; matrix products, arithmetic and copies ran while one was open for 0% of the time, Pallas kernels for 34%

profile of v12, /device:TPU:0, one launch (start us, length us, event | category | flops | bytes accessed | tf_op | source)
XLA Modules:
  0.0 95.4 jit_solution(1474808014804778213)
XLA Ops:
  0.6 0.5 collective-permute-start
  1.2 0.0 copy-start.5
  1.2 3.2 %shard_map.130 = (bf16[8,192,128]{2,1,0:T(8,128)(2,1)}, f32[3,128,384]{2,1,0:T(8,128)}, f32[3,8,512]{2,1,0:T(8,128)}, bf16[2,1280,128]{2,1,0:T(8,128)(2,1)}, bf16[2,1280,128]{2,1,0:T(8,128)(2,1)}) custom-call(f32[128,1280]{1,0:T(8,128)} %bitcast.20, f32[64,512]{1,0:T(8,128)} %bitcast.24, bf16[5120,512]{1,0:T(8,128)(2,1)} %sibling_block.1, ...), custom_call_target="tpu_custom_call" | custom-call | tf_op jit(solution)/shard_map/pallas_call | solution.py:425
  4.4 6.9 %all-to-all-start = ((bf16[8,192,128]{2,1,0:T(8,128)(2,1)}), bf16[8,192,128]{2,1,0:T(8,128)(2,1)}, u32[]{:S(2)}, u32[]{:S(2)}) async-start(bf16[8,192,128]{2,1,0:T(8,128)(2,1)} %get-tuple-element.35), calls=%async_computation | async-start | bytes 786432 | tf_op jit(solution)/shard_map/all_to_all | solution.py:437
  11.3 1.5 %collective-permute-start.5 = (bf16[2,1280,128]{2,1,0:T(8,128)(2,1)}, bf16[2,1280,128]{2,1,0:T(8,128)(2,1)}, u32[]{:S(2)}, u32[]{:S(2)}) collective-permute-start(bf16[2,1280,128]{2,1,0:T(8,128)(2,1)} %get-tuple-element.48), channel_id=1, source_target_pairs={{0,2},{1,3},{2,0},{3,1},{4,6},{5,7},{6,4},{7,5},{8,10},{9,11},{10,... | collective-permute-start | bytes 1966088 | tf_op jit(solution)/shard_map/ppermute | solution.py:395
  12.8 0.0 copy-done.5
  12.8 0.0 collective-permute-start.1
  12.8 1.2 %collective-permute-done.1.refs_3_.sibling_gain = f32[1,1280]{1,0:T(1,128)S(1)} collective-permute-done((f32[1,1280]{1,0:T(1,128)S(1)}, f32[1,1280]{1,0:T(1,128)S(1)}, u32[]{:S(2)}, u32[]{:S(2)}) %collective-permute-start.1) | collective-permute-done | bytes 5152 | tf_op jit(solution)/shard_map/ppermute | solution.py:387
  13.9 0.0 collective-permute-done.refs_1_.sibling_ref
  13.9 0.0 copy-start.2
  13.9 1.7 %copy-done.2 = bf16[1280,1280]{1,0:T(8,128)(2,1)} copy-done((bf16[1280,1280]{1,0:T(8,128)(2,1)}, bf16[1280,1280]{1,0:T(8,128)(2,1)S(1)}, u32[]{:S(2)}) %copy-start.2) | copy-done | bytes 3276824
  15.6 1.9 %copy-done = bf16[1280,1280]{1,0:T(8,128)(2,1)S(1)} copy-done((bf16[1280,1280]{1,0:T(8,128)(2,1)S(1)}, bf16[1280,1280]{1,0:T(8,128)(2,1)}, u32[]{:S(2)}) %copy-start) | copy-done | bytes 3276824
  17.6 1.9 %copy-done.3 = bf16[1280,1280]{1,0:T(8,128)(2,1)S(1)} copy-done((bf16[1280,1280]{1,0:T(8,128)(2,1)S(1)}, bf16[1280,1280]{1,0:T(8,128)(2,1)}, u32[]{:S(2)}) %copy-start.3) | copy-done | bytes 3276824
  19.5 2.4 %shard_map.131 = (bf16[640,2560]{1,0:T(8,128)(2,1)S(1)}, f32[5,128]{1,0:T(8,128)S(1)}) custom-call(bf16[1280,1280]{1,0:T(8,128)(2,1)S(1)} %copy-done, bf16[1280,1280]{1,0:T(8,128)(2,1)S(1)} %copy-done.3, f32[1,1280]{1,0:T(1,128)S(1)} %broadcast_in_dim.3.refs_2_.own_gain, f32[1,1280]{1,0:T(1,128)S(1)} %collective-permute-done.1.refs_3_.sibling_gain), custom_call_target="tpu_custom_call" | custom-call | tf_op jit(solution)/shard_map/pallas_call | solution.py:471
  21.8 1.9 %all-to-all-done.grad_in = bf16[8,192,128]{2,1,0:T(8,128)(2,1)} async-done(((bf16[8,192,128]{2,1,0:T(8,128)(2,1)}), bf16[8,192,128]{2,1,0:T(8,128)(2,1)}, u32[]{:S(2)}, u32[]{:S(2)}) %all-to-all-start) | async-done | bytes 393248 | tf_op jit(solution)/shard_map/all_to_all | solution.py:437
  23.7 2.5 %shard_map.132 = (f32[3,128,160]{2,1,0:T(8,128)}, f32[3,8,512]{2,1,0:T(8,128)}, bf16[8,192,128]{2,1,0:T(8,128)(2,1)}) custom-call(bf16[8,192,128]{2,1,0:T(8,128)(2,1)} %all-to-all-done.grad_in, f32[3,128,384]{2,1,0:T(8,128)} %get-tuple-element.38.down_in, f32[3,8,512]{2,1,0:T(8,128)} %get-tuple-element.39.up_in), custom_call_target="tpu_custom_call" | custom-call | tf_op jit(solution)/shard_map/pallas_call | solution.py:483
  26.2 4.2 %all-to-all-start.1 = ((bf16[8,192,128]{2,1,0:T(8,128)(2,1)}), bf16[8,192,128]{2,1,0:T(8,128)(2,1)}, u32[]{:S(2)}, u32[]{:S(2)}) async-start(bf16[8,192,128]{2,1,0:T(8,128)(2,1)} %get-tuple-element.42), calls=%async_computation.1 | async-start | bytes 786432 | tf_op jit(solution)/shard_map/all_to_all | solution.py:500
  30.4 0.0 collective-permute-done.5.in_ref
  30.4 1.5 %collective-permute-start.8 = (bf16[2,1280,128]{2,1,0:T(8,128)(2,1)}, bf16[2,1280,128]{2,1,0:T(8,128)(2,1)}, u32[]{:S(2)}, u32[]{:S(2)}) collective-permute-start(bf16[2,1280,128]{2,1,0:T(8,128)(2,1)} %get-tuple-element.55), channel_id=1, source_target_pairs={{0,2},{1,3},{2,0},{3,1},{4,6},{5,7},{6,4},{7,5},{8,10},{9,11},{10,... | collective-permute-start | bytes 1966088 | tf_op jit(solution)/shard_map/ppermute | solution.py:395
  31.9 1.9 %shard_map.134 = (bf16[1280,128]{1,0:T(8,128)(2,1)}, bf16[1280,128]{1,0:T(8,128)(2,1)}) custom-call(bf16[2,1280,128]{2,1,0:T(8,128)(2,1)} %collective-permute-done.5.in_ref), custom_call_target="tpu_custom_call" | custom-call | tf_op jit(solution)/shard_map/pallas_call | solution.py:510
  33.8 1.8 %collective-permute-start.6 = (bf16[1280,128]{1,0:T(8,128)(2,1)}, bf16[1280,128]{1,0:T(8,128)(2,1)}, u32[]{:S(2)}, u32[]{:S(2)}) collective-permute-start(bf16[1280,128]{1,0:T(8,128)(2,1)} %get-tuple-element.50.refs_2_), channel_id=1, source_target_pairs={{0,4},{4,0},{8,12},{12,8},{16,20},{20,16},{24,28},{28,24},{1,5},{5... | collective-permute-start | bytes 983048 | tf_op jit(solution)/shard_map/ppermute | solution.py:519
  35.6 1.5 %collective-permute-start.7 = (bf16[1280,128]{1,0:T(8,128)(2,1)}, bf16[1280,128]{1,0:T(8,128)(2,1)}, u32[]{:S(2)}, u32[]{:S(2)}) collective-permute-start(bf16[1280,128]{1,0:T(8,128)(2,1)} %get-tuple-element.51.refs_4_), channel_id=1, source_target_pairs={{0,8},{4,12},{8,0},{12,4},{16,24},{20,28},{24,16},{28,20},{1,9},{5... | collective-permute-start | bytes 983048 | tf_op jit(solution)/shard_map/ppermute | solution.py:519
  37.1 5.4 %all-to-all-done.1.factor_ref.own_f = bf16[8,192,128]{2,1,0:T(8,128)(2,1)} async-done(((bf16[8,192,128]{2,1,0:T(8,128)(2,1)}), bf16[8,192,128]{2,1,0:T(8,128)(2,1)}, u32[]{:S(2)}, u32[]{:S(2)}) %all-to-all-start.1) | async-done | bytes 393248 | tf_op jit(solution)/shard_map/all_to_all | solution.py:500
  42.5 1.1 %shard_map.133 = (bf16[9,32,128]{2,1,0:T(8,128)(2,1)S(1)}, bf16[4,192,128]{2,1,0:T(8,128)(2,1)S(1)}, bf16[4,192,128]{2,1,0:T(8,128)(2,1)S(1)}) custom-call(bf16[8,192,128]{2,1,0:T(8,128)(2,1)} %all-to-all-done.1.factor_ref.own_f, f32[5,128]{1,0:T(8,128)S(1)} %get-tuple-element.43.sums_ref), custom_call_target="tpu_custom_call" | custom-call | tf_op jit(solution)/shard_map/pallas_call | solution.py:525
  43.6 0.1 collective-permute-start.2
  43.7 0.5 collective-permute-start.3
  44.2 0.8 collective-permute-done.6.refs_3_
  45.0 1.2 %collective-permute-start.4 = (bf16[9,32,128]{2,1,0:T(8,128)(2,1)S(1)}, bf16[9,32,128]{2,1,0:T(8,128)(2,1)S(1)}, u32[]{:S(2)}, u32[]{:S(2)}) collective-permute-start(bf16[9,32,128]{2,1,0:T(8,128)(2,1)S(1)} %get-tuple-element.47), channel_id=1, source_target_pairs={{0,2},{1,3},{2,0},{3,1},{4,6},{5,7},{6,4},{7,5},{8,10},{9,11},{10,... | collective-permute-start | bytes 221192 | tf_op jit(solution)/shard_map/ppermute | solution.py:395
  46.1 0.9 collective-permute-done.7.refs_5_
  47.1 2.3 %collective-permute-done.4.b_ref.refs_0_ = bf16[9,32,128]{2,1,0:T(8,128)(2,1)S(1)} collective-permute-done((bf16[9,32,128]{2,1,0:T(8,128)(2,1)S(1)}, bf16[9,32,128]{2,1,0:T(8,128)(2,1)S(1)}, u32[]{:S(2)}, u32[]{:S(2)}) %collective-permute-start.4) | collective-permute-done | bytes 73760 | tf_op jit(solution)/shard_map/ppermute | solution.py:395
  49.3 0.0 collective-permute-done.2.refs_0_
  49.3 0.0 collective-permute-done.3.refs_1_
  49.3 3.3 %shard_map.135 = (bf16[2560,256]{1,0:T(8,128)(2,1)S(1)}, bf16[640,256]{1,0:T(8,128)(2,1)S(1)}) custom-call(bf16[8,192,128]{2,1,0:T(8,128)(2,1)} %all-to-all-done.1.factor_ref.own_f, bf16[9,32,128]{2,1,0:T(8,128)(2,1)S(1)} %collective-permute-done.4.b_ref.refs_0_, bf16[640,2560]{1,0:T(8,128)(2,1)S(1)} %get-tuple-element.46.x.refs_2_, ...), custom_call_target="tpu_custom_call" | custom-call | tf_op jit(solution)/shard_map/pallas_call | solution.py:561
  52.7 1.2 %collective-permute-start.11 = (bf16[640,256]{1,0:T(8,128)(2,1)S(1)}, bf16[640,256]{1,0:T(8,128)(2,1)S(1)}, u32[]{:S(2)}, u32[]{:S(2)}) collective-permute-start(bf16[640,256]{1,0:T(8,128)(2,1)S(1)} %get-tuple-element.56), channel_id=1, source_target_pairs={{0,2},{1,3},{2,0},{3,1},{4,6},{5,7},{6,4},{7,5},{8,10},{9,11},{10,... | collective-permute-start | bytes 983048 | tf_op jit(solution)/shard_map/ppermute | solution.py:395
  53.9 0.0 collective-permute-done.8.in_ref
  53.9 1.1 %shard_map.137 = (bf16[1280,128]{1,0:T(8,128)(2,1)S(1)}, bf16[1280,128]{1,0:T(8,128)(2,1)S(1)}) custom-call(bf16[2,1280,128]{2,1,0:T(8,128)(2,1)} %collective-permute-done.8.in_ref), custom_call_target="tpu_custom_call" | custom-call | tf_op jit(solution)/shard_map/pallas_call | solution.py:510
  55.0 0.9 collective-permute-start.9
  55.9 1.5 %collective-permute-start.10 = (bf16[1280,128]{1,0:T(8,128)(2,1)S(1)}, bf16[1280,128]{1,0:T(8,128)(2,1)S(1)}, u32[]{:S(2)}, u32[]{:S(2)}) collective-permute-start(bf16[1280,128]{1,0:T(8,128)(2,1)S(1)} %get-tuple-element.59.refs_4_), channel_id=1, source_target_pairs={{0,8},{4,12},{8,0},{12,4},{16,24},{20,28},{24,16},{28,20},{1,9},{5... | collective-permute-start | bytes 983048 | tf_op jit(solution)/shard_map/ppermute | solution.py:519
  57.3 0.0 copy-done.1
  57.4 1.9 %copy-done.4 = bf16[1280,1280]{1,0:T(8,128)(2,1)S(1)} copy-done((bf16[1280,1280]{1,0:T(8,128)(2,1)S(1)}, bf16[1280,1280]{1,0:T(8,128)(2,1)}, u32[]{:S(2)}) %copy-start.4) | copy-done | bytes 3276824
  59.3 4.2 %shard_map.136 = (bf16[640,2560]{1,0:T(8,128)(2,1)S(1)}, f32[5,128]{1,0:T(8,128)S(1)}, bf16[640,256]{1,0:T(8,128)(2,1)S(1)}) custom-call(bf16[1280,1280]{1,0:T(8,128)(2,1)S(1)} %copy-done.1, bf16[1280,1280]{1,0:T(8,128)(2,1)S(1)} %copy-done.4, f32[1,1280]{1,0:T(1,128)S(1)} %broadcast_in_dim.3.refs_2_.own_gain, ...), custom_call_target="tpu_custom_call" | custom-call | tf_op jit(solution)/shard_map/pallas_call | solution.py:471
  63.5 0.0 slice-start.1
  63.5 1.3 %collective-permute-start.12 = (bf16[640,256]{1,0:T(8,128)(2,1)S(1)}, bf16[640,256]{1,0:T(8,128)(2,1)S(1)}, u32[]{:S(2)}, u32[]{:S(2)}) collective-permute-start(bf16[640,256]{1,0:T(8,128)(2,1)S(1)} %get-tuple-element.61), channel_id=1, source_target_pairs={{0,2},{1,3},{2,0},{3,1},{4,6},{5,7},{6,4},{7,5},{8,10},{9,11},{10,... | collective-permute-start | bytes 983048 | tf_op jit(solution)/shard_map/ppermute | solution.py:395
  64.7 0.0 collective-permute-done.11.refs_6_.refs_0_
  64.7 0.0 collective-permute-done.9.refs_3_
  64.7 0.0 collective-permute-done.10.refs_5_
  64.7 2.8 %shard_map.138 = (bf16[2560,256]{1,0:T(8,128)(2,1)S(1)}, bf16[640,256]{1,0:T(8,128)(2,1)S(1)}) custom-call(bf16[8,192,128]{2,1,0:T(8,128)(2,1)} %all-to-all-done.1.factor_ref.own_f, bf16[9,32,128]{2,1,0:T(8,128)(2,1)S(1)} %collective-permute-done.4.b_ref.refs_0_, bf16[640,2560]{1,0:T(8,128)(2,1)S(1)} %get-tuple-element.46.x.refs_2_, ...), custom_call_target="tpu_custom_call" | custom-call | tf_op jit(solution)/shard_map/pallas_call | solution.py:561
  67.5 0.9 collective-permute-start.15
  68.5 1.2 %shard_map.139.refs_4_ = bf16[640,256]{1,0:T(8,128)(2,1)S(1)} custom-call(bf16[640,2560]{1,0:T(8,128)(2,1)S(1)} %get-tuple-element.53.x.refs_3_, bf16[2560,256]{1,0:T(8,128)(2,1)S(1)} %get-tuple-element.60.weights), custom_call_target="tpu_custom_call" | custom-call | tf_op jit(solution)/shard_map/pallas_call | solution.py:572
  69.7 1.2 %collective-permute-start.14 = (bf16[640,256]{1,0:T(8,128)(2,1)S(1)}, bf16[640,256]{1,0:T(8,128)(2,1)S(1)}, u32[]{:S(2)}, u32[]{:S(2)}) collective-permute-start(bf16[640,256]{1,0:T(8,128)(2,1)S(1)} %shard_map.139.refs_4_), channel_id=1, source_target_pairs={{0,2},{1,3},{2,0},{3,1},{4,6},{5,7},{6,4},{7,5},{8,10},{9,11},{10,... | collective-permute-start | bytes 983048 | tf_op jit(solution)/shard_map/ppermute | solution.py:395
  70.9 0.9 collective-permute-start.13
  71.7 0.2 shard_map.142.inv
  71.9 13.8 %collective-permute-done.13.refs_0_ = f32[5,128]{1,0:T(8,128)S(1)} collective-permute-done((f32[5,128]{1,0:T(8,128)S(1)}, f32[5,128]{1,0:T(8,128)S(1)}, u32[]{:S(2)}, u32[]{:S(2)}) %collective-permute-start.13) | collective-permute-done | bytes 2592 | tf_op jit(solution)/shard_map/ppermute | solution.py:395
  85.7 0.2 shard_map.141.inv
  85.9 0.0 collective-permute-done.12.refs_5_.refs_0_
  85.9 0.0 slice-done
  85.9 0.0 slice-done.1
  85.9 5.9 %shard_map.140 = (f32[1280,256]{1,0:T(8,128)S(1)}, f32[1280,256]{1,0:T(8,128)S(1)}) custom-call(bf16[5120,512]{1,0:T(8,128)(2,1)S(1)} %bitcast.19, bf16[5120,512]{1,0:T(8,128)(2,1)S(1)} %bitcast.19, bf16[8,192,128]{2,1,0:T(8,128)(2,1)} %all-to-all-done.1.factor_ref.own_f, bf16[4,192,128]{2,1,0:T(8,128)(2,1)S(1)} %collective-permute-done.2.refs_0_, ...), custom_call_target="tpu_custom_call" | custom-call | flops 3355443200 | bytes 6553600 | tf_op jit(solution)/shard_map/pallas_call | solution.py:589
  91.8 0.9 shard_map.143.refs_1_
  92.7 0.9 shard_map.144.refs_1_
  93.6 0.0 collective-permute-done.15.refs_0_
  93.6 0.9 shard_map.145.refs_1_
  94.5 0.0 collective-permute-done.14.refs_0_
  94.5 0.9 shard_map.146
  (7 shorter events, 0.0 us)
Async XLA Ops:
  0.6 13.3 %collective-permute-start = (bf16[1280,1280]{1,0:T(8,128)(2,1)}, bf16[1280,1280]{1,0:T(8,128)(2,1)S(1)}, u32[]{:S(2)}, u32[]{:S(2)}) collective-permute-start(bf16[1280,1280]{1,0:T(8,128)(2,1)} %own_ref.1), channel_id=1, source_target_pairs={{0,1},{1,0},{2,3},{3,2},{4,5},{5,4},{6,7},{7,6},{8,9},{9,8},{10,11... | collective-permute-start | bytes 9830408 | tf_op jit(solution)/shard_map/ppermute | solution.py:387
  1.2 11.6 %copy-start.5 = (f32[1280]{0:T(1024)S(1)}, f32[1280]{0:T(1024)}, u32[]{:S(2)}) copy-start(f32[1280]{0:T(1024)} %param.12) | copy-start | bytes 15364
  4.4 19.3 %all-to-all-start = ((bf16[8,192,128]{2,1,0:T(8,128)(2,1)}), bf16[8,192,128]{2,1,0:T(8,128)(2,1)}, u32[]{:S(2)}, u32[]{:S(2)}) async-start(bf16[8,192,128]{2,1,0:T(8,128)(2,1)} %get-tuple-element.35), calls=%async_computation | async-start | bytes 786432 | tf_op jit(solution)/shard_map/all_to_all | solution.py:437
  11.3 19.1 %collective-permute-start.5 = (bf16[2,1280,128]{2,1,0:T(8,128)(2,1)}, bf16[2,1280,128]{2,1,0:T(8,128)(2,1)}, u32[]{:S(2)}, u32[]{:S(2)}) collective-permute-start(bf16[2,1280,128]{2,1,0:T(8,128)(2,1)} %get-tuple-element.48), channel_id=1, source_target_pairs={{0,2},{1,3},{2,0},{3,1},{4,6},{5,7},{6,4},{7,5},{8,10},{9,11},{10,... | collective-permute-start | bytes 1966088 | tf_op jit(solution)/shard_map/ppermute | solution.py:395
  12.8 1.2 %collective-permute-start.1 = (f32[1,1280]{1,0:T(1,128)S(1)}, f32[1,1280]{1,0:T(1,128)S(1)}, u32[]{:S(2)}, u32[]{:S(2)}) collective-permute-start(f32[1,1280]{1,0:T(1,128)S(1)} %broadcast_in_dim.3.refs_2_.own_gain), channel_id=1, source_target_pairs={{0,1},{1,0},{2,3},{3,2},{4,5},{5,4},{6,7},{7,6},{8,9},{9,8},{10,11... | collective-permute-start | bytes 15368 | tf_op jit(solution)/shard_map/ppermute | solution.py:387
  13.9 1.7 %copy-start.2 = (bf16[1280,1280]{1,0:T(8,128)(2,1)}, bf16[1280,1280]{1,0:T(8,128)(2,1)S(1)}, u32[]{:S(2)}) copy-start(bf16[1280,1280]{1,0:T(8,128)(2,1)S(1)} %collective-permute-done.refs_1_.sibling_ref) | copy-start | bytes 9830404
  15.6 1.9 %copy-start = (bf16[1280,1280]{1,0:T(8,128)(2,1)S(1)}, bf16[1280,1280]{1,0:T(8,128)(2,1)}, u32[]{:S(2)}) copy-start(bf16[1280,1280]{1,0:T(8,128)(2,1)} %own_ref.1) | copy-start | bytes 9830404
  17.6 1.9 %copy-start.3 = (bf16[1280,1280]{1,0:T(8,128)(2,1)S(1)}, bf16[1280,1280]{1,0:T(8,128)(2,1)}, u32[]{:S(2)}) copy-start(bf16[1280,1280]{1,0:T(8,128)(2,1)} %copy-done.2) | copy-start | bytes 9830404
  26.2 16.3 %all-to-all-start.1 = ((bf16[8,192,128]{2,1,0:T(8,128)(2,1)}), bf16[8,192,128]{2,1,0:T(8,128)(2,1)}, u32[]{:S(2)}, u32[]{:S(2)}) async-start(bf16[8,192,128]{2,1,0:T(8,128)(2,1)} %get-tuple-element.42), calls=%async_computation.1 | async-start | bytes 786432 | tf_op jit(solution)/shard_map/all_to_all | solution.py:500
  30.4 23.5 %collective-permute-start.8 = (bf16[2,1280,128]{2,1,0:T(8,128)(2,1)}, bf16[2,1280,128]{2,1,0:T(8,128)(2,1)}, u32[]{:S(2)}, u32[]{:S(2)}) collective-permute-start(bf16[2,1280,128]{2,1,0:T(8,128)(2,1)} %get-tuple-element.55), channel_id=1, source_target_pairs={{0,2},{1,3},{2,0},{3,1},{4,6},{5,7},{6,4},{7,5},{8,10},{9,11},{10,... | collective-permute-start | bytes 1966088 | tf_op jit(solution)/shard_map/ppermute | solution.py:395
  33.8 11.1 %collective-permute-start.6 = (bf16[1280,128]{1,0:T(8,128)(2,1)}, bf16[1280,128]{1,0:T(8,128)(2,1)}, u32[]{:S(2)}, u32[]{:S(2)}) collective-permute-start(bf16[1280,128]{1,0:T(8,128)(2,1)} %get-tuple-element.50.refs_2_), channel_id=1, source_target_pairs={{0,4},{4,0},{8,12},{12,8},{16,20},{20,16},{24,28},{28,24},{1,5},{5... | collective-permute-start | bytes 983048 | tf_op jit(solution)/shard_map/ppermute | solution.py:519
  35.6 11.4 %collective-permute-start.7 = (bf16[1280,128]{1,0:T(8,128)(2,1)}, bf16[1280,128]{1,0:T(8,128)(2,1)}, u32[]{:S(2)}, u32[]{:S(2)}) collective-permute-start(bf16[1280,128]{1,0:T(8,128)(2,1)} %get-tuple-element.51.refs_4_), channel_id=1, source_target_pairs={{0,8},{4,12},{8,0},{12,4},{16,24},{20,28},{24,16},{28,20},{1,9},{5... | collective-permute-start | bytes 983048 | tf_op jit(solution)/shard_map/ppermute | solution.py:519
  43.6 5.7 %collective-permute-start.2 = (bf16[4,192,128]{2,1,0:T(8,128)(2,1)S(1)}, bf16[4,192,128]{2,1,0:T(8,128)(2,1)S(1)}, u32[]{:S(2)}, u32[]{:S(2)}) collective-permute-start(bf16[4,192,128]{2,1,0:T(8,128)(2,1)S(1)} %get-tuple-element.44), channel_id=1, source_target_pairs={{0,1},{1,0},{2,3},{3,2},{4,5},{5,4},{6,7},{7,6},{8,9},{9,8},{10,11... | collective-permute-start | bytes 589832 | tf_op jit(solution)/shard_map/ppermute | solution.py:387
  43.7 5.6 %collective-permute-start.3 = (bf16[4,192,128]{2,1,0:T(8,128)(2,1)S(1)}, bf16[4,192,128]{2,1,0:T(8,128)(2,1)S(1)}, u32[]{:S(2)}, u32[]{:S(2)}) collective-permute-start(bf16[4,192,128]{2,1,0:T(8,128)(2,1)S(1)} %get-tuple-element.45), channel_id=1, source_target_pairs={{0,1},{1,0},{2,3},{3,2},{4,5},{5,4},{6,7},{7,6},{8,9},{9,8},{10,11... | collective-permute-start | bytes 589832 | tf_op jit(solution)/shard_map/ppermute | solution.py:387
  45.0 4.4 %collective-permute-start.4 = (bf16[9,32,128]{2,1,0:T(8,128)(2,1)S(1)}, bf16[9,32,128]{2,1,0:T(8,128)(2,1)S(1)}, u32[]{:S(2)}, u32[]{:S(2)}) collective-permute-start(bf16[9,32,128]{2,1,0:T(8,128)(2,1)S(1)} %get-tuple-element.47), channel_id=1, source_target_pairs={{0,2},{1,3},{2,0},{3,1},{4,6},{5,7},{6,4},{7,5},{8,10},{9,11},{10,... | collective-permute-start | bytes 221192 | tf_op jit(solution)/shard_map/ppermute | solution.py:395
  49.3 8.0 %copy-start.1 = (bf16[1280,1280]{1,0:T(8,128)(2,1)S(1)}, bf16[1280,1280]{1,0:T(8,128)(2,1)}, u32[]{:S(2)}) copy-start(bf16[1280,1280]{1,0:T(8,128)(2,1)} %own_ref.1) | copy-start | bytes 9830404
  52.7 12.1 %collective-permute-start.11 = (bf16[640,256]{1,0:T(8,128)(2,1)S(1)}, bf16[640,256]{1,0:T(8,128)(2,1)S(1)}, u32[]{:S(2)}, u32[]{:S(2)}) collective-permute-start(bf16[640,256]{1,0:T(8,128)(2,1)S(1)} %get-tuple-element.56), channel_id=1, source_target_pairs={{0,2},{1,3},{2,0},{3,1},{4,6},{5,7},{6,4},{7,5},{8,10},{9,11},{10,... | collective-permute-start | bytes 983048 | tf_op jit(solution)/shard_map/ppermute | solution.py:395
  55.0 9.7 %collective-permute-start.9 = (bf16[1280,128]{1,0:T(8,128)(2,1)S(1)}, bf16[1280,128]{1,0:T(8,128)(2,1)S(1)}, u32[]{:S(2)}, u32[]{:S(2)}) collective-permute-start(bf16[1280,128]{1,0:T(8,128)(2,1)S(1)} %get-tuple-element.58.refs_2_), channel_id=1, source_target_pairs={{0,4},{4,0},{8,12},{12,8},{16,20},{20,16},{24,28},{28,24},{1,5},{5... | collective-permute-start | bytes 983048 | tf_op jit(solution)/shard_map/ppermute | solution.py:519
  55.9 8.8 %collective-permute-start.10 = (bf16[1280,128]{1,0:T(8,128)(2,1)S(1)}, bf16[1280,128]{1,0:T(8,128)(2,1)S(1)}, u32[]{:S(2)}, u32[]{:S(2)}) collective-permute-start(bf16[1280,128]{1,0:T(8,128)(2,1)S(1)} %get-tuple-element.59.refs_4_), channel_id=1, source_target_pairs={{0,8},{4,12},{8,0},{12,4},{16,24},{20,28},{24,16},{28,20},{1,9},{5... | collective-permute-start | bytes 983048 | tf_op jit(solution)/shard_map/ppermute | solution.py:519
  57.4 1.9 %copy-start.4 = (bf16[1280,1280]{1,0:T(8,128)(2,1)S(1)}, bf16[1280,1280]{1,0:T(8,128)(2,1)}, u32[]{:S(2)}) copy-start(bf16[1280,1280]{1,0:T(8,128)(2,1)} %copy-done.2) | copy-start | bytes 9830404
  59.3 26.6 %slice-start = ((s8[5242880]{0:T(1024)(128)(4,1)}), s8[4194304]{0:T(1024)(128)(4,1)S(1)}, s32[]{:S(2)}) async-start(s8[5242880]{0:T(1024)(128)(4,1)} %bitcast.18), calls=%async_computation.2 | async-start | bytes 8388608
  63.5 22.5 %slice-start.1 = ((s8[5242880]{0:T(1024)(128)(4,1)}), s8[1048576]{0:T(1024)(128)(4,1)S(1)}, s32[]{:S(2)}) async-start(s8[5242880]{0:T(1024)(128)(4,1)} %bitcast.18), calls=%async_computation.3 | async-start | bytes 2097152
  63.5 22.4 %collective-permute-start.12 = (bf16[640,256]{1,0:T(8,128)(2,1)S(1)}, bf16[640,256]{1,0:T(8,128)(2,1)S(1)}, u32[]{:S(2)}, u32[]{:S(2)}) collective-permute-start(bf16[640,256]{1,0:T(8,128)(2,1)S(1)} %get-tuple-element.61), channel_id=1, source_target_pairs={{0,2},{1,3},{2,0},{3,1},{4,6},{5,7},{6,4},{7,5},{8,10},{9,11},{10,... | collective-permute-start | bytes 983048 | tf_op jit(solution)/shard_map/ppermute | solution.py:395
  67.5 26.1 %collective-permute-start.15 = (bf16[640,256]{1,0:T(8,128)(2,1)S(1)}, bf16[640,256]{1,0:T(8,128)(2,1)S(1)}, u32[]{:S(2)}, u32[]{:S(2)}) collective-permute-start(bf16[640,256]{1,0:T(8,128)(2,1)S(1)} %get-tuple-element.65), channel_id=1, source_target_pairs={{0,2},{1,3},{2,0},{3,1},{4,6},{5,7},{6,4},{7,5},{8,10},{9,11},{10,... | collective-permute-start | bytes 983048 | tf_op jit(solution)/shard_map/ppermute | solution.py:395
  69.7 24.9 %collective-permute-start.14 = (bf16[640,256]{1,0:T(8,128)(2,1)S(1)}, bf16[640,256]{1,0:T(8,128)(2,1)S(1)}, u32[]{:S(2)}, u32[]{:S(2)}) collective-permute-start(bf16[640,256]{1,0:T(8,128)(2,1)S(1)} %shard_map.139.refs_4_), channel_id=1, source_target_pairs={{0,2},{1,3},{2,0},{3,1},{4,6},{5,7},{6,4},{7,5},{8,10},{9,11},{10,... | collective-permute-start | bytes 983048 | tf_op jit(solution)/shard_map/ppermute | solution.py:395
  70.9 14.8 %collective-permute-start.13 = (f32[5,128]{1,0:T(8,128)S(1)}, f32[5,128]{1,0:T(8,128)S(1)}, u32[]{:S(2)}, u32[]{:S(2)}) collective-permute-start(f32[5,128]{1,0:T(8,128)S(1)} %get-tuple-element.64.sums_ref), channel_id=1, source_target_pairs={{0,2},{1,3},{2,0},{3,1},{4,6},{5,7},{6,4},{7,5},{8,10},{9,11},{10,... | collective-permute-start | bytes 7688 | tf_op jit(solution)/shard_map/ppermute | solution.py:395

commit v13 on v12

--- a/solution.py
+++ b/solution.py
@@ -107,15 +107,17 @@
         out[...] = in_ref[k]
 
 
-def prepare(own_ref, sibling_ref, own_gain, sibling_gain, x_ref, sums_ref, squares):
+def prepare_kernel(own_ref, sibling_ref, own_gain, sibling_gain, *refs):
+    before, (x_ref, sums_ref, squares) = refs[:-3], refs[-3:]
     block, features = own_ref.shape
     step = pl.program_id(0)
+    first = 0 if x_ref.shape[0] == block else step * block
     tile = 16 if block % 16 == 0 else block
 
     @pl.loop(0, block // tile, unroll=2)
     def _(i):
         at = pl.ds(pl.multiple_of(i * tile, tile), tile)
-        to = pl.ds(pl.multiple_of(step * block + i * tile, tile), tile)
+        to = pl.ds(pl.multiple_of(first + i * tile, tile), tile)
         own = own_ref[at, :].astype(jnp.float32)
         x_ref[to, :features] = (own * own_gain[...]).astype(x_ref.dtype)
         total = own * own
@@ -123,25 +125,18 @@
         x_ref[to, features:] = (sibling * sibling_gain[...]).astype(x_ref.dtype)
         total += sibling * sibling
         total = jnp.sum(total, axis=1, keepdims=True)
+        to = pl.ds(pl.multiple_of(step * block + i * tile, tile), tile)
         squares[to, :] = jnp.broadcast_to(total, (tile, LANES))
 
     @pl.when(step == pl.num_programs(0) - 1)
     def _():
-        for i in range(sums_ref.shape[0]):
-            sums_ref[i : i + 1] = squares[i * LANES : (i + 1) * LANES, :].T[:1]
-
-    return pl.ds(pl.multiple_of(step * block, block), block)
-
-
-def prepare_kernel(*refs):
-    prepare(*refs)
-
-
-def prepare_multiply_kernel(own_ref, sibling_ref, own_gain, sibling_gain, weights, *refs):
-    x_ref, sums_ref, product, squares = refs
-    rows = prepare(own_ref, sibling_ref, own_gain, sibling_gain, x_ref, sums_ref, squares)
-    value = jnp.dot(x_ref[rows, :], weights[...], preferred_element_type=jnp.float32)
-    product[rows, :] = value.astype(product.dtype)
+        done = 0
+        for ref in before:
+            sums_ref[: ref.shape[0]] = ref[...]
+            done = ref.shape[0]
+        for i in range(squares.shape[0] // LANES):
+            row = squares[i * LANES : (i + 1) * LANES, :].T[:1]
+            sums_ref[done + i : done + i + 1] = row
 
 
 def message_kernel(factor_ref, sums_ref, out_ref, *refs):
@@ -181,9 +176,6 @@
     total = sums_ref[...]
     count = total.shape[0]
     for ref in messages:
-        if shares == 0:
-            total += ref[...]
-            continue
         rows = [ref[i].astype(jnp.float32) for i in range(shares, ref.shape[0])]
         rows = jnp.concatenate(rows, axis=0)
         total += rows[:count] + rows[count : 2 * count] + rows[2 * count : 3 * count]
@@ -279,16 +271,17 @@
     )
 
 
-def outside_kernel(static, chips, step, turn, own_f, b_ref, x, *refs):
-    sibling_f, blocks = refs[:FACTOR_PIECES], refs[FACTOR_PIECES:]
-    weights, product = refs[-2:]
+def outside_kernel(static, chips, step, turn, b_ref, x, *refs):
+    own_f, sibling_f = refs[:FACTOR_PIECES], refs[FACTOR_PIECES : 2 * FACTOR_PIECES]
+    blocks, (weights, product) = refs[2 * FACTOR_PIECES :], refs[-2:]
     strips = static[3]
     features = blocks[0].shape[0]
-    down_rows = own_f.shape[1] - b_ref.shape[1]
+    down_rows = own_f[0].shape[1] - b_ref.shape[1]
+    shares = FACTOR_PIECES * own_f[0].shape[0]
     place, replica = lax.axis_index("tensor"), lax.axis_index("dp")
     owner = (place // CORES - step + chips) % chips * CORES + place % CORES
-    b = up_factor(static, b_ref[: own_f.shape[0]], owner)
-    own_a, sibling_a = factor_a([own_f], down_rows), factor_a(sibling_f, down_rows)
+    b = up_factor(static, b_ref[:shares], owner)
+    own_a, sibling_a = factor_a(own_f, down_rows), factor_a(sibling_f, down_rows)
     for k, strip in enumerate(strips):
         mine, other = blocks[2 * k : 2 * k + 2]
         even = replica // turn[strip] % 2 == 0
@@ -307,15 +300,17 @@
     multiply(x, weights, store)
 
 
-def own_kernel(static, own_block, sibling_block, own_f, *refs):
-    sibling_f, refs = refs[:FACTOR_PIECES], refs[FACTOR_PIECES:]
+def own_kernel(static, own_block, sibling_block, *refs):
+    own_f, sibling_f = refs[:FACTOR_PIECES], refs[FACTOR_PIECES : 2 * FACTOR_PIECES]
+    refs = refs[2 * FACTOR_PIECES :]
     xs, weights = refs[: static[5]], refs[-1]
     outs = refs[len(refs) - 1 - static[6] : -1]
     features = own_block.shape[0]
     wide = outs[0].shape[1]
-    down_rows = own_f.shape[1] - len(static[3]) * static[2]
-    b = up_factor(static[:5], own_f[:, down_rows:], lax.axis_index("tensor"))
-    for at, factors, block in ((0, [own_f], own_block), (features, sibling_f, sibling_block)):
+    down_rows = own_f[0].shape[1] - len(static[3]) * static[2]
+    b = jnp.concatenate([piece[:, down_rows:] for piece in own_f], axis=0)
+    b = up_factor(static[:5], b, lax.axis_index("tensor"))
+    for at, factors, block in ((0, own_f, own_block), (features, sibling_f, sibling_block)):
         weights[at : at + features] = merge(static[0], block[...], factor_a(factors, down_rows), b)
     for h, x in enumerate(xs):
 
@@ -328,10 +323,11 @@
 
 
 def finish_kernel(sources, first, own, inv, *refs):
-    total = own[pl.ds(first, refs[-1].shape[0]), :]
+    rows = pl.ds(first, refs[-1].shape[0])
+    total = own[rows, :]
     for value in refs[:sources]:
         total = total + value[...].astype(jnp.float32)
-    refs[-1][...] = (total * inv[:, :1]).astype(refs[-1].dtype)
+    refs[-1][...] = (total * inv[rows, :1]).astype(refs[-1].dtype)
 
 
 def finish(own, inv_rms, received, at, shape, before):
@@ -460,26 +456,26 @@
     rows = LANES if some % LANES == 0 else some
     operands = [prompt_hidden_input, to_sibling(prompt_hidden_input), gain, to_sibling(gain)]
 
-    def prepared(half, kernel, more, limit):
+    def prepared(half, before, in_place, limit):
         token_block = pl.BlockSpec((rows, features), lambda i: (half * (some // rows) + i, 0))
         gain_block = pl.BlockSpec((1, features), lambda i: (0, 0))
-        out_shape = (
-            jax.ShapeDtypeStruct((some, CORES * features), bf16),
-            jax.ShapeDtypeStruct((some // LANES, LANES), f32),
-        )
-        out_shape += (jax.ShapeDtypeStruct((some, wide), bf16),) * len(more)
+        x_block = pl.BlockSpec((rows, CORES * features), lambda i: (i, 0))
         return pl.pallas_call(
-            kernel,
+            prepare_kernel,
             grid=(some // rows,),
-            out_shape=out_shape,
-            in_specs=[token_block, token_block, gain_block, gain_block] + in_vmem(len(more)),
-            out_specs=tuple(in_vmem(len(out_shape))),
+            out_shape=(
+                jax.ShapeDtypeStruct((some, CORES * features), bf16),
+                jax.ShapeDtypeStruct(((half + 1) * some // LANES, LANES), f32),
+            ),
+            in_specs=[token_block, token_block, gain_block, gain_block] + in_vmem(len(before)),
+            out_specs=(in_vmem(1)[0] if in_place else x_block, in_vmem(1)[0]),
             scratch_shapes=[pltpu.VMEM((some, LANES), f32)],
             compiler_params=pltpu.CompilerParams(vmem_limit_bytes=limit),
-        )(*operands, *more)
-
-    x0, squares = prepared(0, prepare_kernel, [], PREPARE_VMEM_BYTES)
+        )(*operands, *before)
+
+    x0, squares = prepared(0, [], True, PREPARE_VMEM_BYTES)
     exchanged, squares = lax.optimization_barrier((exchanged, squares))
+    x1, squares = prepared(1, [squares], False, LARGE_VMEM_BYTES)
     a_next, b_next, sent = pl.pallas_call(
         adam_kernel,
         out_shape=(
@@ -519,8 +515,9 @@
                 outside[strip].append((piece, lax.ppermute(piece, "dp", pairs)))
 
     swap_half(0, sent)
+    own_f, squares = lax.optimization_barrier((own_f, squares))
     up_packed = packed_rows - down_rows
-    more = pl.cdiv(3 * (tokens // TOKEN_HALVES // LANES), up_packed)
+    more = pl.cdiv(3 * (tokens // LANES), up_packed)
     piece = jax.ShapeDtypeStruct((n_dp // FACTOR_PIECES, packed_rows, LANES), bf16)
     message, *pieces = pl.pallas_call(
         message_kernel,
@@ -534,22 +531,18 @@
     messages = [to_chip(message, step) for step in steps]
     sibling_f = [to_sibling(piece) for piece in pieces]
 
-    def inverse(shares, *sums):
-        return pl.pallas_call(
-            functools.partial(inverse_kernel, width, shares),
-            out_shape=jax.ShapeDtypeStruct((some, LANES), f32),
-            in_specs=in_vmem(chips),
-            out_specs=in_vmem(1)[0],
-            compiler_params=params(),
-        )(*sums)
-
-    inv_rms = [inverse(n_dp, squares, *messages)]
+    inv_rms = pl.pallas_call(
+        functools.partial(inverse_kernel, width, n_dp),
+        out_shape=jax.ShapeDtypeStruct((tokens, LANES), f32),
+        in_specs=in_vmem(chips),
+        out_specs=in_vmem(1)[0],
+        compiler_params=params(),
+    )(squares, *messages)
 
     scale = 0.5 / math.sqrt(width * rank)
 
     received = {}
     after = []
-    x1 = None
     weights_shape = jax.ShapeDtypeStruct((CORES * features, wide), bf16)
     product_shape = jax.ShapeDtypeStruct((some, wide), bf16)
     for half, group in enumerate(groups):
@@ -561,28 +554,23 @@
             weights, product = pl.pallas_call(
                 functools.partial(outside_kernel, static, chips, step, turn),
                 out_shape=(weights_shape, product_shape),
-                in_specs=in_vmem(3 + FACTOR_PIECES + len(blocks)) + anywhere(len(after)),
+                in_specs=in_vmem(2 + 2 * FACTOR_PIECES + len(blocks)) + anywhere(len(after)),
                 out_specs=tuple(in_vmem(2)),
                 compiler_params=params(),
-            )(own_f, messages[step - 1], x0, *sibling_f, *blocks, *after)
+            )(messages[step - 1], x0, *pieces, *sibling_f, *blocks, *after)
             received.setdefault((0, half), []).append(to_chip(product, chips - step))
-            if x1 is None:
-                x1, sums, second = prepared(1, prepare_multiply_kernel, [weights], VMEM_BYTES)
-            else:
-                second = pl.pallas_call(
-                    more_kernel,
-                    out_shape=product_shape,
-                    in_specs=in_vmem(2),
-                    out_specs=in_vmem(1)[0],
-                    compiler_params=params(),
-                )(x1, weights)
+            second = pl.pallas_call(
+                more_kernel,
+                out_shape=product_shape,
+                in_specs=in_vmem(2),
+                out_specs=in_vmem(1)[0],
+                compiler_params=params(),
+            )(x1, weights)
             products = [product, second]
             after = [second]
             received.setdefault((1, half), []).append(to_chip(second, chips - step))
         if half == 0:
             after = [received[0, 0][0]]
-            sent_sums, _ = lax.optimization_barrier((sums, products))
-            inv_rms.append(inverse(0, sums, *[to_chip(sent_sums, step) for step in steps]))
 
     after.append(received[1, 0][0])
     static = (scale, parts, up_rows, range(strips), columns, TOKEN_HALVES, halves)
@@ -594,7 +582,7 @@
             pl.BlockSpec((features, columns), lambda i: (lax.axis_index("tensor"), 0)),
             pl.BlockSpec((features, columns), lambda i: (lax.axis_index("tensor") ^ 1, 0)),
         ]
-        + in_vmem(1 + FACTOR_PIECES + TOKEN_HALVES)
+        + in_vmem(2 * FACTOR_PIECES + TOKEN_HALVES)
         + anywhere(len(after)),
         out_specs=tuple(in_vmem(halves)),
         scratch_shapes=[pltpu.VMEM((CORES * features, columns), bf16)],
@@ -604,12 +592,12 @@
             bytes_accessed=4 * tokens * features,
             transcendentals=0,
         ),
-    )(frozen_key_value, frozen_key_value, own_f, *sibling_f, x0, x1, *after)
+    )(frozen_key_value, frozen_key_value, *pieces, *sibling_f, x0, x1, *after)
 
     keys_values = None
-    for at, pieces in received.items():
+    for at, values in received.items():
         keys_values = finish(
-            totals[at[1]], inv_rms[at[0]], pieces, at, (tokens, columns), keys_values
+            totals[at[1]], inv_rms, values, at, (tokens, columns), keys_values
         )
     return (a_next, b_next, keys_values)
 

time: 96 us -> 85.4 us (0.89)
  waiting for transfers between devices: 26.2 us -> 13.9 us
    all_to_all x1, waiting for transfers between devices: 5.38 us -> 0.04 us  [body(): own_f = lax.all_to_all(sent, 'dp', 0, 0, tiled=True)]
    ppermute x8 -> x7, waiting for transfers between devices: 16.1 us -> 10.8 us  [to_chip(): return lax.ppermute(value, 'tensor', pairs)]
    pallas_call x4 -> x3, Pallas kernels: 6.86 us -> 8.69 us  [the longest x2 8.45 us: prepared(): pl.pallas_call(prepare_kernel, grid=(some // rows,), out_shape=(jax.Shape...]
    all_to_all x1, waiting for transfers between devices: 1.85 us -> 0.07 us  [body(): exchanged = lax.all_to_all(packed, 'dp', 0, 0, tiled=True)]
    all_to_all x1, starting transfers between devices: 4.19 us -> 5.94 us  [body(): own_f = lax.all_to_all(sent, 'dp', 0, 0, tiled=True)]
    pallas_call x1 -> x2, Pallas kernels: 1.18 us -> 2.36 us  [body(): pl.pallas_call(more_kernel, out_shape=product_shape, in_specs=in_vmem(2),...]
    ppermute x8 -> x7, starting transfers between devices: 9.66 us -> 8.52 us  [to_chip(): return lax.ppermute(value, 'tensor', pairs)]
    pallas_call x2, Pallas kernels: 6.13 us -> 5 us  [body(): pl.pallas_call(functools.partial(outside_kernel, static, chips, step, tur...]
  transfers between devices with their start and end apart: 18 -> 17, of which waited for: 7 -> 11; matrix products, arithmetic and copies ran while one was open for 0% -> 0% of each run, Pallas kernels for 34% -> 39%
where the time goes in v13:
time: 85.4 us; the launch traced here: 84.8 us
  Pallas kernels  34.3 us (40%)
  starting transfers between devices  27.8 us (33%)
  waiting for transfers between devices  13.9 us (16%)
  local copies, waits for them, and re-layouts  8.03 us (9%)
    ppermute x7, waiting for transfers between devices, to_chip(): return lax.ppermute(value, 'tensor', pairs)  10.8 us
    ppermute x7, starting transfers between devices, to_chip(): return lax.ppermute(value, 'tensor', pairs)  8.52 us
    pallas_call x2, Pallas kernels, prepared(): pl.pallas_call(prepare_kernel, grid=(some // rows,), out_shape=(jax.Shape...  8.45 us
    unnamed x24, local copies, waits for them, and re-layouts  8.03 us
    all_to_all x1, starting transfers between devices, body(): exchanged = lax.all_to_all(packed, 'dp', 0, 0, tiled=True)  6.88 us
    all_to_all x1, starting transfers between devices, body(): own_f = lax.all_to_all(sent, 'dp', 0, 0, tiled=True)  5.94 us
    ppermute x4, starting transfers between devices, swap_half(): outside[strip].append((piece, lax.ppermute(piece, 'dp', pairs)))  5.33 us
    pallas_call x2, Pallas kernels, body(): pl.pallas_call(functools.partial(outside_kernel, static, chips, step, tur...  5 us
  transfers between devices with their start and end apart: 17, of which 11 were waited for; matrix products, arithmetic and copies ran while one was open for 0% of the time, Pallas kernels for 39%

profile of v13, /device:TPU:0, one launch (start us, length us, event | category | flops | bytes accessed | tf_op | source)
XLA Modules:
  0.0 84.8 jit_solution(13845967455992095546)
XLA Ops:
  0.6 0.5 collective-permute-start
  1.2 3.2 %shard_map.130 = (bf16[8,192,128]{2,1,0:T(8,128)(2,1)}, f32[3,128,384]{2,1,0:T(8,128)}, f32[3,8,512]{2,1,0:T(8,128)}, bf16[2,1280,128]{2,1,0:T(8,128)(2,1)}, bf16[2,1280,128]{2,1,0:T(8,128)(2,1)}) custom-call(f32[128,1280]{1,0:T(8,128)} %bitcast.20, f32[64,512]{1,0:T(8,128)} %bitcast.24, bf16[5120,512]{1,0:T(8,128)(2,1)} %sibling_block.1, ...), custom_call_target="tpu_custom_call" | custom-call | tf_op jit(solution)/shard_map/pallas_call | solution.py:421
  4.4 6.9 %all-to-all-start = ((bf16[8,192,128]{2,1,0:T(8,128)(2,1)}), bf16[8,192,128]{2,1,0:T(8,128)(2,1)}, u32[]{:S(2)}, u32[]{:S(2)}) async-start(bf16[8,192,128]{2,1,0:T(8,128)(2,1)} %get-tuple-element.35), calls=%async_computation | async-start | bytes 786432 | tf_op jit(solution)/shard_map/all_to_all | solution.py:433
  11.3 1.5 %collective-permute-start.5 = (bf16[2,1280,128]{2,1,0:T(8,128)(2,1)}, bf16[2,1280,128]{2,1,0:T(8,128)(2,1)}, u32[]{:S(2)}, u32[]{:S(2)}) collective-permute-start(bf16[2,1280,128]{2,1,0:T(8,128)(2,1)} %get-tuple-element.53), channel_id=1, source_target_pairs={{0,2},{1,3},{2,0},{3,1},{4,6},{5,7},{6,4},{7,5},{8,10},{9,11},{10,... | collective-permute-start | bytes 1966088 | tf_op jit(solution)/shard_map/ppermute | solution.py:391
  12.8 0.0 copy-done.9
  12.8 0.0 collective-permute-start.1
  12.8 1.2 %collective-permute-done.1.sibling_gain = f32[1,1280]{1,0:T(1,128)S(1)} collective-permute-done((f32[1,1280]{1,0:T(1,128)S(1)}, f32[1,1280]{1,0:T(1,128)S(1)}, u32[]{:S(2)}, u32[]{:S(2)}) %collective-permute-start.1) | collective-permute-done | bytes 5152 | tf_op jit(solution)/shard_map/ppermute | solution.py:383
  13.9 0.0 collective-permute-done.sibling_ref
  13.9 1.7 %copy-done.2 = bf16[1280,1280]{1,0:T(8,128)(2,1)} copy-done((bf16[1280,1280]{1,0:T(8,128)(2,1)}, bf16[1280,1280]{1,0:T(8,128)(2,1)S(1)}, u32[]{:S(2)}) %copy-start.2) | copy-done | bytes 3276824
  15.6 1.9 %copy-done.1 = bf16[1280,1280]{1,0:T(8,128)(2,1)S(1)} copy-done((bf16[1280,1280]{1,0:T(8,128)(2,1)S(1)}, bf16[1280,1280]{1,0:T(8,128)(2,1)}, u32[]{:S(2)}) %copy-start.1) | copy-done | bytes 3276824
  17.5 1.9 %copy-done.3 = bf16[1280,1280]{1,0:T(8,128)(2,1)S(1)} copy-done((bf16[1280,1280]{1,0:T(8,128)(2,1)S(1)}, bf16[1280,1280]{1,0:T(8,128)(2,1)}, u32[]{:S(2)}) %copy-start.3) | copy-done | bytes 3276824
  19.5 2.4 %shard_map.131 = (bf16[640,2560]{1,0:T(8,128)(2,1)S(1)}, f32[5,128]{1,0:T(8,128)S(1)}) custom-call(bf16[1280,1280]{1,0:T(8,128)(2,1)S(1)} %copy-done.1, bf16[1280,1280]{1,0:T(8,128)(2,1)S(1)} %copy-done.3, f32[1,1280]{1,0:T(1,128)S(1)} %broadcast_in_dim.3.own_gain, f32[1,1280]{1,0:T(1,128)S(1)} %collective-permute-done.1.sibling_gain), custom_call_target="tpu_custom_call" | custom-call | tf_op jit(solution)/shard_map/pallas_call | solution.py:463
  21.8 0.6 copy-done.4
  22.4 0.6 copy-done.7
  23.0 0.6 copy-done.8
  23.6 0.1 all-to-all-done.grad_in
  23.7 2.5 %shard_map.132 = (f32[3,128,160]{2,1,0:T(8,128)}, f32[3,8,512]{2,1,0:T(8,128)}, bf16[8,192,128]{2,1,0:T(8,128)(2,1)}) custom-call(bf16[8,192,128]{2,1,0:T(8,128)(2,1)} %all-to-all-done.grad_in, f32[3,128,384]{2,1,0:T(8,128)} %get-tuple-element.38.down_in, f32[3,8,512]{2,1,0:T(8,128)} %get-tuple-element.39.up_in), custom_call_target="tpu_custom_call" | custom-call | tf_op jit(solution)/shard_map/pallas_call | solution.py:479
  26.2 5.9 %all-to-all-start.1 = ((bf16[8,192,128]{2,1,0:T(8,128)(2,1)}), bf16[8,192,128]{2,1,0:T(8,128)(2,1)}, u32[]{:S(2)}, u32[]{:S(2)}) async-start(bf16[8,192,128]{2,1,0:T(8,128)(2,1)} %get-tuple-element.42), calls=%async_computation.1 | async-start | bytes 786432 | tf_op jit(solution)/shard_map/all_to_all | solution.py:496
  32.1 0.0 collective-permute-done.5.in_ref
  32.2 0.6 collective-permute-start.6
  32.8 2.0 %shard_map.135 = (bf16[1280,128]{1,0:T(8,128)(2,1)}, bf16[1280,128]{1,0:T(8,128)(2,1)}) custom-call(bf16[2,1280,128]{2,1,0:T(8,128)(2,1)} %collective-permute-done.5.in_ref), custom_call_target="tpu_custom_call" | custom-call | tf_op jit(solution)/shard_map/pallas_call | solution.py:506
  34.7 2.0 %collective-permute-start.7 = (bf16[1280,128]{1,0:T(8,128)(2,1)}, bf16[1280,128]{1,0:T(8,128)(2,1)}, u32[]{:S(2)}, u32[]{:S(2)}) collective-permute-start(bf16[1280,128]{1,0:T(8,128)(2,1)} %get-tuple-element.56.refs_4_), channel_id=1, source_target_pairs={{0,4},{4,0},{8,12},{12,8},{16,20},{20,16},{24,28},{28,24},{1,5},{5... | collective-permute-start | bytes 983048 | tf_op jit(solution)/shard_map/ppermute | solution.py:515
  36.7 1.5 %collective-permute-start.8 = (bf16[1280,128]{1,0:T(8,128)(2,1)}, bf16[1280,128]{1,0:T(8,128)(2,1)}, u32[]{:S(2)}, u32[]{:S(2)}) collective-permute-start(bf16[1280,128]{1,0:T(8,128)(2,1)} %get-tuple-element.57.refs_6_), channel_id=1, source_target_pairs={{0,8},{4,12},{8,0},{12,4},{16,24},{20,28},{24,16},{28,20},{1,9},{5... | collective-permute-start | bytes 983048 | tf_op jit(solution)/shard_map/ppermute | solution.py:515
  38.1 6.1 %shard_map.133 = (bf16[640,2560]{1,0:T(8,128)(2,1)}, f32[10,128]{1,0:T(8,128)}) custom-call(bf16[1280,1280]{1,0:T(8,128)(2,1)} %own_ref.3, bf16[1280,1280]{1,0:T(8,128)(2,1)} %copy-done.2, f32[1,1280]{1,0:T(1,128)} %copy-done.4, f32[1,1280]{1,0:T(1,128)} %copy-done.7, f32[5,128]{1,0:T(8,128)} %copy-done.8), custom_call_target="tpu_custom_call" | custom-call | tf_op jit(solution)/shard_map/pallas_call | solution.py:463
  44.2 0.0 all-to-all-done.1.factor_ref
  44.3 0.7 copy-done.5
  45.0 1.1 %shard_map.134 = (bf16[9,32,128]{2,1,0:T(8,128)(2,1)S(1)}, bf16[4,192,128]{2,1,0:T(8,128)(2,1)S(1)}, bf16[4,192,128]{2,1,0:T(8,128)(2,1)S(1)}) custom-call(bf16[8,192,128]{2,1,0:T(8,128)(2,1)} %all-to-all-done.1.factor_ref, f32[10,128]{1,0:T(8,128)S(1)} %copy-done.5), custom_call_target="tpu_custom_call" | custom-call | tf_op jit(solution)/shard_map/pallas_call | solution.py:522
  46.1 0.1 collective-permute-start.2
  46.1 0.5 collective-permute-start.3
  46.6 0.1 collective-permute-done.7.refs_5_
  46.7 1.4 %collective-permute-start.4 = (bf16[9,32,128]{2,1,0:T(8,128)(2,1)S(1)}, bf16[9,32,128]{2,1,0:T(8,128)(2,1)S(1)}, u32[]{:S(2)}, u32[]{:S(2)}) collective-permute-start(bf16[9,32,128]{2,1,0:T(8,128)(2,1)S(1)} %get-tuple-element.51), channel_id=1, source_target_pairs={{0,2},{1,3},{2,0},{3,1},{4,6},{5,7},{6,4},{7,5},{8,10},{9,11},{10,... | collective-permute-start | bytes 221192 | tf_op jit(solution)/shard_map/ppermute | solution.py:391
  48.1 0.6 collective-permute-done.8.refs_7_
  48.7 2.4 %collective-permute-done.4.b_ref.refs_0_ = bf16[9,32,128]{2,1,0:T(8,128)(2,1)S(1)} collective-permute-done((bf16[9,32,128]{2,1,0:T(8,128)(2,1)S(1)}, bf16[9,32,128]{2,1,0:T(8,128)(2,1)S(1)}, u32[]{:S(2)}, u32[]{:S(2)}) %collective-permute-start.4) | collective-permute-done | bytes 73760 | tf_op jit(solution)/shard_map/ppermute | solution.py:391
  51.1 0.0 collective-permute-done.2.refs_2_
  51.1 0.0 collective-permute-done.3.refs_3_
  51.1 3.2 %shard_map.136 = (bf16[2560,256]{1,0:T(8,128)(2,1)S(1)}, bf16[640,256]{1,0:T(8,128)(2,1)S(1)}) custom-call(bf16[9,32,128]{2,1,0:T(8,128)(2,1)S(1)} %collective-permute-done.4.b_ref.refs_0_, bf16[640,2560]{1,0:T(8,128)(2,1)S(1)} %get-tuple-element.49.x.refs_4_, bf16[4,192,128]{2,1,0:T(8,128)(2,1)S(1)} %get-tuple-element.47.refs_0_, ...), custom_call_target="tpu_custom_call" | custom-call | tf_op jit(solution)/shard_map/pallas_call | solution.py:554
  54.3 1.4 %collective-permute-start.11 = (bf16[640,256]{1,0:T(8,128)(2,1)S(1)}, bf16[640,256]{1,0:T(8,128)(2,1)S(1)}, u32[]{:S(2)}, u32[]{:S(2)}) collective-permute-start(bf16[640,256]{1,0:T(8,128)(2,1)S(1)} %get-tuple-element.58), channel_id=1, source_target_pairs={{0,2},{1,3},{2,0},{3,1},{4,6},{5,7},{6,4},{7,5},{8,10},{9,11},{10,... | collective-permute-start | bytes 983048 | tf_op jit(solution)/shard_map/ppermute | solution.py:391
  55.7 0.0 collective-permute-done.6.in_ref
  55.7 1.1 %shard_map.137 = (bf16[1280,128]{1,0:T(8,128)(2,1)S(1)}, bf16[1280,128]{1,0:T(8,128)(2,1)S(1)}) custom-call(bf16[2,1280,128]{2,1,0:T(8,128)(2,1)} %collective-permute-done.6.in_ref), custom_call_target="tpu_custom_call" | custom-call | tf_op jit(solution)/shard_map/pallas_call | solution.py:506
  56.9 0.6 collective-permute-start.9
  57.5 1.3 %collective-permute-start.10 = (bf16[1280,128]{1,0:T(8,128)(2,1)S(1)}, bf16[1280,128]{1,0:T(8,128)(2,1)S(1)}, u32[]{:S(2)}, u32[]{:S(2)}) collective-permute-start(bf16[1280,128]{1,0:T(8,128)(2,1)S(1)} %get-tuple-element.61.refs_6_), channel_id=1, source_target_pairs={{0,8},{4,12},{8,0},{12,4},{16,24},{20,28},{24,16},{28,20},{1,9},{5... | collective-permute-start | bytes 983048 | tf_op jit(solution)/shard_map/ppermute | solution.py:515
  58.8 0.0 copy-done
  58.8 1.2 %shard_map.140 = bf16[640,256]{1,0:T(8,128)(2,1)S(1)} custom-call(bf16[640,2560]{1,0:T(8,128)(2,1)S(1)} %copy-done, bf16[2560,256]{1,0:T(8,128)(2,1)S(1)} %get-tuple-element.63.weights), custom_call_target="tpu_custom_call" | custom-call | tf_op jit(solution)/shard_map/pallas_call | solution.py:562
  60.0 0.0 slice-start.1
  60.0 1.5 %collective-permute-start.12 = (bf16[640,256]{1,0:T(8,128)(2,1)S(1)}, bf16[640,256]{1,0:T(8,128)(2,1)S(1)}, u32[]{:S(2)}, u32[]{:S(2)}) collective-permute-start(bf16[640,256]{1,0:T(8,128)(2,1)S(1)} %shard_map.140), channel_id=1, source_target_pairs={{0,2},{1,3},{2,0},{3,1},{4,6},{5,7},{6,4},{7,5},{8,10},{9,11},{10,... | collective-permute-start | bytes 983048 | tf_op jit(solution)/shard_map/ppermute | solution.py:391
  61.5 3.0 %collective-permute-done.11.refs_8_.refs_0_ = bf16[640,256]{1,0:T(8,128)(2,1)S(1)} collective-permute-done((bf16[640,256]{1,0:T(8,128)(2,1)S(1)}, bf16[640,256]{1,0:T(8,128)(2,1)S(1)}, u32[]{:S(2)}, u32[]{:S(2)}) %collective-permute-start.11) | collective-permute-done | bytes 327712 | tf_op jit(solution)/shard_map/ppermute | solution.py:391
  64.4 0.8 collective-permute-done.9.refs_5_
  65.2 0.3 collective-permute-done.10.refs_7_
  65.5 1.8 %shard_map.138 = (bf16[2560,256]{1,0:T(8,128)(2,1)S(1)}, bf16[640,256]{1,0:T(8,128)(2,1)S(1)}) custom-call(bf16[9,32,128]{2,1,0:T(8,128)(2,1)S(1)} %collective-permute-done.4.b_ref.refs_0_, bf16[640,2560]{1,0:T(8,128)(2,1)S(1)} %get-tuple-element.49.x.refs_4_, bf16[4,192,128]{2,1,0:T(8,128)(2,1)S(1)} %get-tuple-element.47.refs_0_, ...), custom_call_target="tpu_custom_call" | custom-call | tf_op jit(solution)/shard_map/pallas_call | solution.py:554
  67.3 1.5 %collective-permute-start.14 = (bf16[640,256]{1,0:T(8,128)(2,1)S(1)}, bf16[640,256]{1,0:T(8,128)(2,1)S(1)}, u32[]{:S(2)}, u32[]{:S(2)}) collective-permute-start(bf16[640,256]{1,0:T(8,128)(2,1)S(1)} %get-tuple-element.65), channel_id=1, source_target_pairs={{0,2},{1,3},{2,0},{3,1},{4,6},{5,7},{6,4},{7,5},{8,10},{9,11},{10,... | collective-permute-start | bytes 983048 | tf_op jit(solution)/shard_map/ppermute | solution.py:391
  68.8 1.2 %shard_map.139.refs_6_ = bf16[640,256]{1,0:T(8,128)(2,1)S(1)} custom-call(bf16[640,2560]{1,0:T(8,128)(2,1)S(1)} %copy-done, bf16[2560,256]{1,0:T(8,128)(2,1)S(1)} %get-tuple-element.62.weights), custom_call_target="tpu_custom_call" | custom-call | tf_op jit(solution)/shard_map/pallas_call | solution.py:562
  70.0 0.6 collective-permute-start.13
  70.6 0.0 copy-done.6
  70.6 0.2 shard_map.142.inv
  70.9 0.6 collective-permute-done.12.refs_7_.refs_0_
  71.5 0.0 slice-done
  71.5 0.0 slice-done.1
  71.5 4.9 %shard_map.141 = (f32[1280,256]{1,0:T(8,128)S(1)}, f32[1280,256]{1,0:T(8,128)S(1)}) custom-call(bf16[5120,512]{1,0:T(8,128)(2,1)S(1)} %bitcast.19, bf16[5120,512]{1,0:T(8,128)(2,1)S(1)} %bitcast.19, bf16[4,192,128]{2,1,0:T(8,128)(2,1)S(1)} %get-tuple-element.47.refs_0_, bf16[4,192,128]{2,1,0:T(8,128)(2,1)S(1)} %get-tuple-element.48.refs_1_, ...), custom_call_target="tpu_custom_call" | custom-call | flops 3355443200 | bytes 6553600 | tf_op jit(solution)/shard_map/pallas_call | solution.py:577
  76.3 0.9 %shard_map.143.refs_1_ = bf16[1280,512]{1,0:T(8,128)(2,1)} custom-call(f32[1280,256]{1,0:T(8,128)S(1)} %get-tuple-element.66.own, f32[1280,128]{1,0:T(8,128)S(1)} %shard_map.142.inv, bf16[640,256]{1,0:T(8,128)(2,1)S(1)} %collective-permute-done.11.refs_8_.refs_0_), custom_call_target="tpu_custom_call" | custom-call | tf_op jit(solution)/shard_map/pallas_call | solution.py:342
  77.2 0.9 %shard_map.144.refs_1_ = bf16[1280,512]{1,0:T(8,128)(2,1)} custom-call(f32[1280,256]{1,0:T(8,128)S(1)} %get-tuple-element.66.own, f32[1280,128]{1,0:T(8,128)S(1)} %shard_map.142.inv, bf16[640,256]{1,0:T(8,128)(2,1)S(1)} %collective-permute-done.12.refs_7_.refs_0_, bf16[1280,512]{1,0:T(8,128)(2,1)} %shard_map.143.refs_1_), custom_call_target="tpu_custom_call", output_to_operand_aliasing={{}: (3, {})} | custom-call | tf_op jit(solution)/shard_map/pallas_call | solution.py:342
  78.1 0.4 collective-permute-done.14.refs_0_
  78.5 0.9 %shard_map.145.refs_1_ = bf16[1280,512]{1,0:T(8,128)(2,1)} custom-call(f32[1280,256]{1,0:T(8,128)S(1)} %get-tuple-element.64.own, f32[1280,128]{1,0:T(8,128)S(1)} %shard_map.142.inv, bf16[640,256]{1,0:T(8,128)(2,1)S(1)} %collective-permute-done.14.refs_0_, bf16[1280,512]{1,0:T(8,128)(2,1)} %shard_map.144.refs_1_), custom_call_target="tpu_custom_call", output_to_operand_aliasing={{}: (3, {})} | custom-call | tf_op jit(solution)/shard_map/pallas_call | solution.py:342
  79.4 4.5 %collective-permute-done.13.refs_0_ = bf16[640,256]{1,0:T(8,128)(2,1)S(1)} collective-permute-done((bf16[640,256]{1,0:T(8,128)(2,1)S(1)}, bf16[640,256]{1,0:T(8,128)(2,1)S(1)}, u32[]{:S(2)}, u32[]{:S(2)}) %collective-permute-start.13) | collective-permute-done | bytes 327712 | tf_op jit(solution)/shard_map/ppermute | solution.py:391
  83.9 0.9 %shard_map.146 = bf16[1280,512]{1,0:T(8,128)(2,1)} custom-call(f32[1280,256]{1,0:T(8,128)S(1)} %get-tuple-element.64.own, f32[1280,128]{1,0:T(8,128)S(1)} %shard_map.142.inv, bf16[640,256]{1,0:T(8,128)(2,1)S(1)} %collective-permute-done.13.refs_0_, bf16[1280,512]{1,0:T(8,128)(2,1)} %shard_map.145.refs_1_), custom_call_target="tpu_custom_call", output_to_operand_aliasing={{}: (3, {})} | custom-call | tf_op jit(solution)/shard_map/pallas_call | solution.py:342
  (13 shorter events, 0.0 us)
Async XLA Ops:
  0.6 13.3 %collective-permute-start = (bf16[1280,1280]{1,0:T(8,128)(2,1)}, bf16[1280,1280]{1,0:T(8,128)(2,1)S(1)}, u32[]{:S(2)}, u32[]{:S(2)}) collective-permute-start(bf16[1280,1280]{1,0:T(8,128)(2,1)} %own_ref.3), channel_id=1, source_target_pairs={{0,1},{1,0},{2,3},{3,2},{4,5},{5,4},{6,7},{7,6},{8,9},{9,8},{10,11... | collective-permute-start | bytes 9830408 | tf_op jit(solution)/shard_map/ppermute | solution.py:383
  1.2 11.6 %copy-start.9 = (f32[1280]{0:T(1024)S(1)}, f32[1280]{0:T(1024)}, u32[]{:S(2)}) copy-start(f32[1280]{0:T(1024)} %param.12) | copy-start | bytes 15364
  4.4 19.3 %all-to-all-start = ((bf16[8,192,128]{2,1,0:T(8,128)(2,1)}), bf16[8,192,128]{2,1,0:T(8,128)(2,1)}, u32[]{:S(2)}, u32[]{:S(2)}) async-start(bf16[8,192,128]{2,1,0:T(8,128)(2,1)} %get-tuple-element.35), calls=%async_computation | async-start | bytes 786432 | tf_op jit(solution)/shard_map/all_to_all | solution.py:433
  11.3 20.9 %collective-permute-start.5 = (bf16[2,1280,128]{2,1,0:T(8,128)(2,1)}, bf16[2,1280,128]{2,1,0:T(8,128)(2,1)}, u32[]{:S(2)}, u32[]{:S(2)}) collective-permute-start(bf16[2,1280,128]{2,1,0:T(8,128)(2,1)} %get-tuple-element.53), channel_id=1, source_target_pairs={{0,2},{1,3},{2,0},{3,1},{4,6},{5,7},{6,4},{7,5},{8,10},{9,11},{10,... | collective-permute-start | bytes 1966088 | tf_op jit(solution)/shard_map/ppermute | solution.py:391
  12.8 1.2 %collective-permute-start.1 = (f32[1,1280]{1,0:T(1,128)S(1)}, f32[1,1280]{1,0:T(1,128)S(1)}, u32[]{:S(2)}, u32[]{:S(2)}) collective-permute-start(f32[1,1280]{1,0:T(1,128)S(1)} %broadcast_in_dim.3.own_gain), channel_id=1, source_target_pairs={{0,1},{1,0},{2,3},{3,2},{4,5},{5,4},{6,7},{7,6},{8,9},{9,8},{10,11... | collective-permute-start | bytes 15368 | tf_op jit(solution)/shard_map/ppermute | solution.py:383
  13.9 1.7 %copy-start.2 = (bf16[1280,1280]{1,0:T(8,128)(2,1)}, bf16[1280,1280]{1,0:T(8,128)(2,1)S(1)}, u32[]{:S(2)}) copy-start(bf16[1280,1280]{1,0:T(8,128)(2,1)S(1)} %collective-permute-done.sibling_ref) | copy-start | bytes 9830404
  15.6 1.9 %copy-start.1 = (bf16[1280,1280]{1,0:T(8,128)(2,1)S(1)}, bf16[1280,1280]{1,0:T(8,128)(2,1)}, u32[]{:S(2)}) copy-start(bf16[1280,1280]{1,0:T(8,128)(2,1)} %own_ref.3) | copy-start | bytes 9830404
  17.5 1.9 %copy-start.3 = (bf16[1280,1280]{1,0:T(8,128)(2,1)S(1)}, bf16[1280,1280]{1,0:T(8,128)(2,1)}, u32[]{:S(2)}) copy-start(bf16[1280,1280]{1,0:T(8,128)(2,1)} %copy-done.2) | copy-start | bytes 9830404
  21.8 0.6 copy-start.4
  22.4 0.6 copy-start.7
  23.0 0.6 copy-start.8
  26.2 18.1 %all-to-all-start.1 = ((bf16[8,192,128]{2,1,0:T(8,128)(2,1)}), bf16[8,192,128]{2,1,0:T(8,128)(2,1)}, u32[]{:S(2)}, u32[]{:S(2)}) async-start(bf16[8,192,128]{2,1,0:T(8,128)(2,1)} %get-tuple-element.42), calls=%async_computation.1 | async-start | bytes 786432 | tf_op jit(solution)/shard_map/all_to_all | solution.py:496
  32.2 23.6 %collective-permute-start.6 = (bf16[2,1280,128]{2,1,0:T(8,128)(2,1)}, bf16[2,1280,128]{2,1,0:T(8,128)(2,1)}, u32[]{:S(2)}, u32[]{:S(2)}) collective-permute-start(bf16[2,1280,128]{2,1,0:T(8,128)(2,1)} %get-tuple-element.54), channel_id=1, source_target_pairs={{0,2},{1,3},{2,0},{3,1},{4,6},{5,7},{6,4},{7,5},{8,10},{9,11},{10,... | collective-permute-start | bytes 1966088 | tf_op jit(solution)/shard_map/ppermute | solution.py:391
  34.7 12.0 %collective-permute-start.7 = (bf16[1280,128]{1,0:T(8,128)(2,1)}, bf16[1280,128]{1,0:T(8,128)(2,1)}, u32[]{:S(2)}, u32[]{:S(2)}) collective-permute-start(bf16[1280,128]{1,0:T(8,128)(2,1)} %get-tuple-element.56.refs_4_), channel_id=1, source_target_pairs={{0,4},{4,0},{8,12},{12,8},{16,20},{20,16},{24,28},{28,24},{1,5},{5... | collective-permute-start | bytes 983048 | tf_op jit(solution)/shard_map/ppermute | solution.py:515
  36.7 12.0 %collective-permute-start.8 = (bf16[1280,128]{1,0:T(8,128)(2,1)}, bf16[1280,128]{1,0:T(8,128)(2,1)}, u32[]{:S(2)}, u32[]{:S(2)}) collective-permute-start(bf16[1280,128]{1,0:T(8,128)(2,1)} %get-tuple-element.57.refs_6_), channel_id=1, source_target_pairs={{0,8},{4,12},{8,0},{12,4},{16,24},{20,28},{24,16},{28,20},{1,9},{5... | collective-permute-start | bytes 983048 | tf_op jit(solution)/shard_map/ppermute | solution.py:515
  44.3 0.7 copy-start.5
  46.1 5.0 %collective-permute-start.2 = (bf16[4,192,128]{2,1,0:T(8,128)(2,1)S(1)}, bf16[4,192,128]{2,1,0:T(8,128)(2,1)S(1)}, u32[]{:S(2)}, u32[]{:S(2)}) collective-permute-start(bf16[4,192,128]{2,1,0:T(8,128)(2,1)S(1)} %get-tuple-element.47.refs_0_), channel_id=1, source_target_pairs={{0,1},{1,0},{2,3},{3,2},{4,5},{5,4},{6,7},{7,6},{8,9},{9,8},{10,11... | collective-permute-start | bytes 589832 | tf_op jit(solution)/shard_map/ppermute | solution.py:383
  46.1 4.9 %collective-permute-start.3 = (bf16[4,192,128]{2,1,0:T(8,128)(2,1)S(1)}, bf16[4,192,128]{2,1,0:T(8,128)(2,1)S(1)}, u32[]{:S(2)}, u32[]{:S(2)}) collective-permute-start(bf16[4,192,128]{2,1,0:T(8,128)(2,1)S(1)} %get-tuple-element.48.refs_1_), channel_id=1, source_target_pairs={{0,1},{1,0},{2,3},{3,2},{4,5},{5,4},{6,7},{7,6},{8,9},{9,8},{10,11... | collective-permute-start | bytes 589832 | tf_op jit(solution)/shard_map/ppermute | solution.py:383
  46.7 4.4 %collective-permute-start.4 = (bf16[9,32,128]{2,1,0:T(8,128)(2,1)S(1)}, bf16[9,32,128]{2,1,0:T(8,128)(2,1)S(1)}, u32[]{:S(2)}, u32[]{:S(2)}) collective-permute-start(bf16[9,32,128]{2,1,0:T(8,128)(2,1)S(1)} %get-tuple-element.51), channel_id=1, source_target_pairs={{0,2},{1,3},{2,0},{3,1},{4,6},{5,7},{6,4},{7,5},{8,10},{9,11},{10,... | collective-permute-start | bytes 221192 | tf_op jit(solution)/shard_map/ppermute | solution.py:391
  51.1 7.7 %copy-start = (bf16[640,2560]{1,0:T(8,128)(2,1)S(1)}, bf16[640,2560]{1,0:T(8,128)(2,1)}, u32[]{:S(2)}) copy-start(bf16[640,2560]{1,0:T(8,128)(2,1)} %get-tuple-element.50.x.refs_5_) | copy-start | bytes 9830404
  54.3 10.2 %collective-permute-start.11 = (bf16[640,256]{1,0:T(8,128)(2,1)S(1)}, bf16[640,256]{1,0:T(8,128)(2,1)S(1)}, u32[]{:S(2)}, u32[]{:S(2)}) collective-permute-start(bf16[640,256]{1,0:T(8,128)(2,1)S(1)} %get-tuple-element.58), channel_id=1, source_target_pairs={{0,2},{1,3},{2,0},{3,1},{4,6},{5,7},{6,4},{7,5},{8,10},{9,11},{10,... | collective-permute-start | bytes 983048 | tf_op jit(solution)/shard_map/ppermute | solution.py:391
  56.9 8.3 %collective-permute-start.9 = (bf16[1280,128]{1,0:T(8,128)(2,1)S(1)}, bf16[1280,128]{1,0:T(8,128)(2,1)S(1)}, u32[]{:S(2)}, u32[]{:S(2)}) collective-permute-start(bf16[1280,128]{1,0:T(8,128)(2,1)S(1)} %get-tuple-element.60.refs_4_), channel_id=1, source_target_pairs={{0,4},{4,0},{8,12},{12,8},{16,20},{20,16},{24,28},{28,24},{1,5},{5... | collective-permute-start | bytes 983048 | tf_op jit(solution)/shard_map/ppermute | solution.py:515
  57.5 8.0 %collective-permute-start.10 = (bf16[1280,128]{1,0:T(8,128)(2,1)S(1)}, bf16[1280,128]{1,0:T(8,128)(2,1)S(1)}, u32[]{:S(2)}, u32[]{:S(2)}) collective-permute-start(bf16[1280,128]{1,0:T(8,128)(2,1)S(1)} %get-tuple-element.61.refs_6_), channel_id=1, source_target_pairs={{0,8},{4,12},{8,0},{12,4},{16,24},{20,28},{24,16},{28,20},{1,9},{5... | collective-permute-start | bytes 983048 | tf_op jit(solution)/shard_map/ppermute | solution.py:515
  58.8 12.7 %slice-start = ((s8[5242880]{0:T(1024)(128)(4,1)}), s8[4194304]{0:T(1024)(128)(4,1)S(1)}, s32[]{:S(2)}) async-start(s8[5242880]{0:T(1024)(128)(4,1)} %bitcast.18), calls=%async_computation.2 | async-start | bytes 8388608
  60.0 11.5 %slice-start.1 = ((s8[5242880]{0:T(1024)(128)(4,1)}), s8[1048576]{0:T(1024)(128)(4,1)S(1)}, s32[]{:S(2)}) async-start(s8[5242880]{0:T(1024)(128)(4,1)} %bitcast.18), calls=%async_computation.3 | async-start | bytes 2097152
  60.0 11.5 %collective-permute-start.12 = (bf16[640,256]{1,0:T(8,128)(2,1)S(1)}, bf16[640,256]{1,0:T(8,128)(2,1)S(1)}, u32[]{:S(2)}, u32[]{:S(2)}) collective-permute-start(bf16[640,256]{1,0:T(8,128)(2,1)S(1)} %shard_map.140), channel_id=1, source_target_pairs={{0,2},{1,3},{2,0},{3,1},{4,6},{5,7},{6,4},{7,5},{8,10},{9,11},{10,... | collective-permute-start | bytes 983048 | tf_op jit(solution)/shard_map/ppermute | solution.py:391
  67.3 11.2 %collective-permute-start.14 = (bf16[640,256]{1,0:T(8,128)(2,1)S(1)}, bf16[640,256]{1,0:T(8,128)(2,1)S(1)}, u32[]{:S(2)}, u32[]{:S(2)}) collective-permute-start(bf16[640,256]{1,0:T(8,128)(2,1)S(1)} %get-tuple-element.65), channel_id=1, source_target_pairs={{0,2},{1,3},{2,0},{3,1},{4,6},{5,7},{6,4},{7,5},{8,10},{9,11},{10,... | collective-permute-start | bytes 983048 | tf_op jit(solution)/shard_map/ppermute | solution.py:391
  68.8 1.8 %copy-start.6 = (f32[10,128]{1,0:T(8,128)S(1)}, f32[10,128]{1,0:T(8,128)}, u32[]{:S(2)}) copy-start(f32[10,128]{1,0:T(8,128)} %get-tuple-element.46.sums_ref) | copy-start | bytes 15364
  70.0 13.9 %collective-permute-start.13 = (bf16[640,256]{1,0:T(8,128)(2,1)S(1)}, bf16[640,256]{1,0:T(8,128)(2,1)S(1)}, u32[]{:S(2)}, u32[]{:S(2)}) collective-permute-start(bf16[640,256]{1,0:T(8,128)(2,1)S(1)} %shard_map.139.refs_6_), channel_id=1, source_target_pairs={{0,2},{1,3},{2,0},{3,1},{4,6},{5,7},{6,4},{7,5},{8,10},{9,11},{10,... | collective-permute-start | bytes 983048 | tf_op jit(solution)/shard_map/ppermute | solution.py:391

commit v14 on v13

--- a/solution.py
+++ b/solution.py
@@ -42,7 +42,7 @@
     return pltpu.CompilerParams(vmem_limit_bytes=VMEM_BYTES, **more)
 
 
-def pack(down, up, out_ref):
+def pack(down, up, out_ref, ready):
     shares = out_ref.shape[0]
     down = down.T
     down_rows, up_rows = down.shape[0] // shares, up.shape[0] // shares
@@ -51,29 +51,31 @@
         for k in range(up.shape[1] // LANES):
             pieces.append(up[i * up_rows : (i + 1) * up_rows, k * LANES : (k + 1) * LANES])
         out_ref[i] = jnp.concatenate(pieces, axis=0).astype(jnp.bfloat16)
+        ready(i)
 
 
 def first_lane(share, window, size):
     return jnp.minimum(share // LANES * LANES, size - window)
 
 
-def begin_kernel(chips, turn, aligned, *refs):
-    down_ref, up_ref, weights_ref = refs[:3]
-    state, refs = refs[3 : 3 + 6 * aligned], refs[3 + 6 * aligned :]
-    packed, refs = refs[0], refs[1:]
-    windows, refs = refs[: 2 * aligned], refs[2 * aligned :]
-    outs, (down, up, sem) = refs[:-3], refs[-3:]
-    features = outs[0].shape[1]
+def begin_kernel(chips, turn, down_ref, up_ref, weights_ref, packed, *refs):
+    outs, (down, up, blocks, strips, sem, sem_out) = refs[:-6], refs[-6:]
+    features = strips.shape[1]
     place, replica = lax.axis_index("tensor"), lax.axis_index("dp")
     chip, core = place // CORES, place % CORES
-    copies = []
+    copies, back = [], []
 
     def add(source, target):
         copies.append(pltpu.make_async_copy(source, target, sem.at[len(copies)]))
         copies[-1].start()
 
+    def add_back(source, target):
+        back.append(pltpu.make_async_copy(source, target, sem_out.at[len(back)]))
+        back[-1].start()
+
     add(down_ref, down)
     add(up_ref, up)
+    targets = []
     for i, out in enumerate(outs):
         step, first = 1 + i % (chips - 1), i // (chips - 1) * out.shape[0]
         for k in range(out.shape[0]):
@@ -84,21 +86,16 @@
                     pl.ds(pl.multiple_of(row, features), features),
                     pl.ds((first + k) * LANES, LANES),
                 ],
-                out.at[k],
+                strips.at[len(targets)],
             )
-    if aligned:
-        down_win, up_win = windows
-        window, up_rows = down_win.shape[2], up_win.shape[1]
-        share = replica * (features // packed.shape[0])
-        lane = pl.multiple_of(first_lane(share, window, features), LANES)
-        row = pl.multiple_of(replica * up_rows, up_rows)
-        for i in range(3):
-            add(state[i].at[:, pl.ds(lane, window)], down_win.at[i])
-            add(state[3 + i].at[pl.ds(row, up_rows)], up_win.at[i])
+            targets.append(out.at[k])
     copies[0].wait()
     copies[1].wait()
-    pack(down[...], up[...], packed)
-    for copy in copies[2:]:
+    pack(down[...], up[...], blocks, lambda i: add_back(blocks.at[i], packed.at[i]))
+    for i, target in enumerate(targets):
+        copies[2 + i].wait()
+        add_back(strips.at[i], target)
+    for copy in back:
         copy.wait()
 
 
@@ -108,10 +105,15 @@
 
 
 def prepare_kernel(own_ref, sibling_ref, own_gain, sibling_gain, *refs):
-    before, (x_ref, sums_ref, squares) = refs[:-3], refs[-3:]
     block, features = own_ref.shape
     step = pl.program_id(0)
-    first = 0 if x_ref.shape[0] == block else step * block
+    sums_ref, squares = refs[-2:]
+    sibling_x = refs[-3]
+    if sibling_x.shape[1] == features:
+        before, own_x, lane = refs[:-4], refs[-4], 0
+    else:
+        before, own_x, lane = refs[:-3], sibling_x, features
+    first = 0 if refs[-3].shape[0] == block else step * block
     tile = 16 if block % 16 == 0 else block
 
     @pl.loop(0, block // tile, unroll=2)
@@ -119,10 +121,11 @@
         at = pl.ds(pl.multiple_of(i * tile, tile), tile)
         to = pl.ds(pl.multiple_of(first + i * tile, tile), tile)
         own = own_ref[at, :].astype(jnp.float32)
-        x_ref[to, :features] = (own * own_gain[...]).astype(x_ref.dtype)
+        own_x[to, :features] = (own * own_gain[...]).astype(own_x.dtype)
         total = own * own
         sibling = sibling_ref[at, :].astype(jnp.float32)
-        x_ref[to, features:] = (sibling * sibling_gain[...]).astype(x_ref.dtype)
+        scaled = (sibling * sibling_gain[...]).astype(sibling_x.dtype)
+        sibling_x[to, lane : lane + features] = scaled
         total += sibling * sibling
         total = jnp.sum(total, axis=1, keepdims=True)
         to = pl.ds(pl.multiple_of(step * block + i * tile, tile), tile)
@@ -140,8 +143,10 @@
 
 
 def message_kernel(factor_ref, sums_ref, out_ref, *refs):
-    pieces, sem = refs[:-1], refs[-1]
+    pieces, (sums, sem) = refs[:-2], refs[-2:]
     shares, up_rows = factor_ref.shape[0], out_ref.shape[1]
+    sums_copy = pltpu.make_async_copy(sums_ref, sums, sem.at[1 + len(pieces)])
+    sums_copy.start()
     copies = [
         pltpu.make_async_copy(
             factor_ref.at[:, pl.ds(factor_ref.shape[1] - up_rows, up_rows)],
@@ -156,7 +161,8 @@
         )
     for copy in copies:
         copy.start()
-    left = sums_ref[...]
+    sums_copy.wait()
+    left = sums[...]
     terms = []
     for _ in range(3):
         terms.append(left.astype(jnp.bfloat16).astype(jnp.float32))
@@ -204,26 +210,35 @@
     return jnp.concatenate(pieces, axis=0).astype(jnp.bfloat16)
 
 
-def adam_kernel(grad_in, down_in, up_in, a_ref, b_ref, factor_ref, grad_ref, down_win, up_win, sem):
-    copies = [
-        pltpu.make_async_copy(source, target, sem.at[i])
-        for i, (source, target) in enumerate(
-            ((grad_in, grad_ref), (down_in, down_win), (up_in, up_win))
-        )
-    ]
+def adam_kernel(grad_in, *refs):
+    state, refs = refs[:6], refs[6:]
+    a_ref, b_ref, factor_ref, grad_ref, down_win, up_win, sem = refs
+    replicas = grad_ref.shape[0]
+    down_rows, window = a_ref.shape[2], down_win.shape[2]
+    up_rows = up_win.shape[1]
+    replica = lax.axis_index("dp")
+    share = replica * down_rows
+    size = down_rows * replicas
+    copies = [pltpu.make_async_copy(grad_in, grad_ref, sem.at[6])]
+    for i in range(3):
+        down, up = state[i], state[3 + i]
+        if window != down_rows:
+            lane = pl.multiple_of(first_lane(share, window, size), LANES)
+            down = down.at[:, pl.ds(lane, window)]
+            up = up.at[pl.ds(pl.multiple_of(replica * up_rows, up_rows), up_rows)]
+        copies.append(pltpu.make_async_copy(down, down_win.at[i], sem.at[i]))
+        copies.append(pltpu.make_async_copy(up, up_win.at[i], sem.at[3 + i]))
     for copy in copies:
         copy.start()
-    for copy in copies:
+    copies[0].wait()
+    total = jnp.sum(grad_ref[...].astype(jnp.float32), axis=0) / replicas
+    for copy in copies[1:]:
         copy.wait()
-    replicas = grad_ref.shape[0]
-    down_rows, window = a_ref.shape[2], down_win.shape[2]
-    total = jnp.sum(grad_ref[...].astype(jnp.float32), axis=0) / replicas
 
     def down():
         if window == down_rows:
             return [down_win[i] for i in range(3)]
-        share = lax.axis_index("dp") * down_rows
-        shift = window - (share - first_lane(share, window, down_rows * replicas))
+        shift = window - (share - first_lane(share, window, size))
         return [pltpu.roll(down_win[i], shift, 1)[:, :down_rows] for i in range(3)]
 
     rounded = update(total, down, lambda: [up_win[i] for i in range(3)], a_ref, b_ref)
@@ -234,7 +249,11 @@
 def factor_a(refs, down_rows):
     pieces = []
     for ref in refs:
-        pieces += [ref[i].astype(jnp.float32)[:down_rows] for i in range(ref.shape[0])]
+        for i in range(ref.shape[0]):
+            if down_rows % 16 == 0:
+                pieces.append(ref[i, :down_rows, :])
+            else:
+                pieces.append(ref[i].astype(jnp.float32)[:down_rows])
     return jnp.concatenate(pieces, axis=0).astype(jnp.bfloat16)
 
 
@@ -253,14 +272,21 @@
     return (block.astype(jnp.float32) + scale * change).astype(jnp.bfloat16)
 
 
-def multiply(x, weights, store):
-    rows = x.shape[0]
+def multiply(xs, weights, store):
+    rows = xs[0].shape[0]
     tile = rows // 2 if rows % 32 == 0 else rows
 
     @pl.loop(0, rows // tile)
     def _(i):
         at = pl.ds(pl.multiple_of(i * tile, tile), tile)
-        store(i * tile, tile, jnp.dot(x[at, :], weights[...], preferred_element_type=jnp.float32))
+        value, first = None, 0
+        for x in xs:
+            size = x.shape[1]
+            part = jnp.dot(
+                x[at, :], weights[first : first + size, :], preferred_element_type=jnp.float32
+            )
+            value, first = part if value is None else value + part, first + size
+        store(i * tile, tile, value)
 
 
 def up_factor(static, packed, owner):
@@ -293,18 +319,20 @@
     more_kernel(x, weights, product)
 
 
-def more_kernel(x, weights, product):
+def more_kernel(*refs):
+    xs, (weights, product) = refs[:-2], refs[-2:]
+
     def store(first, size, value):
         product[pl.ds(first, size), :] = value.astype(product.dtype)
 
-    multiply(x, weights, store)
+    multiply(xs, weights, store)
 
 
 def own_kernel(static, own_block, sibling_block, *refs):
     own_f, sibling_f = refs[:FACTOR_PIECES], refs[FACTOR_PIECES : 2 * FACTOR_PIECES]
     refs = refs[2 * FACTOR_PIECES :]
-    xs, weights = refs[: static[5]], refs[-1]
-    outs = refs[len(refs) - 1 - static[6] : -1]
+    xs, weights = [refs[:1], refs[1:3]], refs[-1]
+    outs = refs[len(refs) - 1 - static[5] : -1]
     features = own_block.shape[0]
     wide = outs[0].shape[1]
     down_rows = own_f[0].shape[1] - len(static[3]) * static[2]
@@ -315,7 +343,7 @@
     for h, x in enumerate(xs):
 
         def store(first, size, value):
-            to = pl.ds(pl.multiple_of(h * x.shape[0] + first, 16), size)
+            to = pl.ds(pl.multiple_of(h * x[0].shape[0] + first, 16), size)
             for k, out in enumerate(outs):
                 out[to, :] = value[:, k * wide : (k + 1) * wide]
 
@@ -401,46 +429,37 @@
     aligned = features % LANES == 0 and window <= features
     aligned = aligned and up_rows % 8 == 0 and down_rows % 16 == 0
     window = window if aligned else down_rows
-    windows = (
-        jax.ShapeDtypeStruct((3, factors, window), f32),
-        jax.ShapeDtypeStruct((3, up_rows, columns), f32),
-    )
-
     turns = [1, 2] if n_dp % 4 == 0 else [1, 1]
     turn = [turns[strip % 2] for strip in range(strips)]
     halves = min(COLUMN_HALVES, strips)
     wide = columns // halves
     groups = [range(k * strips // halves, (k + 1) * strips // halves) for k in range(halves)]
-    out_shape = (shares,) + windows * aligned
-    out_shape += tuple(
+    out_shape = (shares,) + tuple(
         jax.ShapeDtypeStruct((len(group), features, LANES), bf16)
         for group in groups
         for _ in steps
     )
-    state = (down_state + up_state) * aligned
-    packed, *rest = pl.pallas_call(
-        functools.partial(begin_kernel, chips, turn, aligned),
+    packed, *taken = pl.pallas_call(
+        functools.partial(begin_kernel, chips, turn),
         out_shape=out_shape,
-        in_specs=anywhere(3 + len(state)),
-        out_specs=tuple(in_vmem(len(out_shape))),
+        in_specs=anywhere(3),
+        out_specs=tuple(anywhere(len(out_shape))),
         scratch_shapes=[
             pltpu.VMEM((factors, features), f32),
             pltpu.VMEM((rank, columns), f32),
-            pltpu.SemaphoreType.DMA((2 + len(steps) * strips + len(state),)),
+            pltpu.VMEM(shares.shape, bf16),
+            pltpu.VMEM((len(steps) * strips, features, LANES), bf16),
+            pltpu.SemaphoreType.DMA((2 + len(steps) * strips,)),
+            pltpu.SemaphoreType.DMA((n_dp + len(steps) * strips,)),
         ],
         compiler_params=pltpu.CompilerParams(vmem_limit_bytes=LARGE_VMEM_BYTES),
-    )(down_sent, up_gradient[0], frozen_key_value, *state)
+    )(down_sent, up_gradient[0], frozen_key_value)
     exchanged = lax.all_to_all(packed, "dp", 0, 0, tiled=True)
-    if aligned:
-        down_win, up_win, *taken = rest
-    else:
-        taken = rest
-        down_win = jnp.stack(
-            [lax.dynamic_slice_in_dim(v, replica * down_rows, down_rows, 1) for v in down_state]
-        )
-        up_win = jnp.stack(
-            [lax.dynamic_slice_in_dim(v, replica * up_rows, up_rows, 0) for v in up_state]
-        )
+    if not aligned:
+        down_state = [
+            lax.dynamic_slice_in_dim(v, replica * down_rows, down_rows, 1) for v in down_state
+        ]
+        up_state = [lax.dynamic_slice_in_dim(v, replica * up_rows, up_rows, 0) for v in up_state]
     mine = []
 
     def send_half(half, after):
@@ -459,19 +478,23 @@
     def prepared(half, before, in_place, limit):
         token_block = pl.BlockSpec((rows, features), lambda i: (half * (some // rows) + i, 0))
         gain_block = pl.BlockSpec((1, features), lambda i: (0, 0))
-        x_block = pl.BlockSpec((rows, CORES * features), lambda i: (i, 0))
-        return pl.pallas_call(
+        if in_place:
+            x_shape = (jax.ShapeDtypeStruct((some, CORES * features), bf16),)
+            x_specs = tuple(in_vmem(1))
+        else:
+            x_shape = (jax.ShapeDtypeStruct((some, features), bf16),) * 2
+            x_specs = (pl.BlockSpec((rows, features), lambda i: (i, 0)),) * 2
+        *x, squares = pl.pallas_call(
             prepare_kernel,
             grid=(some // rows,),
-            out_shape=(
-                jax.ShapeDtypeStruct((some, CORES * features), bf16),
-                jax.ShapeDtypeStruct(((half + 1) * some // LANES, LANES), f32),
-            ),
+            out_shape=x_shape
+            + (jax.ShapeDtypeStruct(((half + 1) * some // LANES, LANES), f32),),
             in_specs=[token_block, token_block, gain_block, gain_block] + in_vmem(len(before)),
-            out_specs=(in_vmem(1)[0] if in_place else x_block, in_vmem(1)[0]),
+            out_specs=x_specs + tuple(in_vmem(1)),
             scratch_shapes=[pltpu.VMEM((some, LANES), f32)],
             compiler_params=pltpu.CompilerParams(vmem_limit_bytes=limit),
         )(*operands, *before)
+        return x, squares
 
     x0, squares = prepared(0, [], True, PREPARE_VMEM_BYTES)
     exchanged, squares = lax.optimization_barrier((exchanged, squares))
@@ -483,16 +506,16 @@
             jax.ShapeDtypeStruct((3, up_rows, columns), f32),
             shares,
         ),
-        in_specs=anywhere(3),
+        in_specs=anywhere(7),
         out_specs=tuple(in_vmem(3)),
         scratch_shapes=[
             pltpu.VMEM((n_dp, packed_rows, LANES), bf16),
             pltpu.VMEM((3, factors, window), f32),
             pltpu.VMEM((3, up_rows, columns), f32),
-            pltpu.SemaphoreType.DMA((3,)),
+            pltpu.SemaphoreType.DMA((7,)),
         ],
         compiler_params=pltpu.CompilerParams(vmem_limit_bytes=LARGE_VMEM_BYTES),
-    )(exchanged, down_win, up_win)
+    )(exchanged, *down_state, *up_state)
     own_f = lax.all_to_all(sent, "dp", 0, 0, tiled=True)
     for half in range(1, halves):
         send_half(half, (mine[-1], sent))
@@ -523,9 +546,12 @@
         message_kernel,
         out_shape=(jax.ShapeDtypeStruct((n_dp + more, up_packed, LANES), bf16),)
         + (piece,) * FACTOR_PIECES,
-        in_specs=anywhere(1) + in_vmem(1),
+        in_specs=anywhere(2),
         out_specs=tuple(in_vmem(1 + FACTOR_PIECES)),
-        scratch_shapes=[pltpu.SemaphoreType.DMA((1 + FACTOR_PIECES,))],
+        scratch_shapes=[
+            pltpu.VMEM(squares.shape, f32),
+            pltpu.SemaphoreType.DMA((2 + FACTOR_PIECES,)),
+        ],
         compiler_params=params(),
     )(own_f, squares)
     messages = [to_chip(message, step) for step in steps]
@@ -557,15 +583,15 @@
                 in_specs=in_vmem(2 + 2 * FACTOR_PIECES + len(blocks)) + anywhere(len(after)),
                 out_specs=tuple(in_vmem(2)),
                 compiler_params=params(),
-            )(messages[step - 1], x0, *pieces, *sibling_f, *blocks, *after)
+            )(messages[step - 1], *x0, *pieces, *sibling_f, *blocks, *after)
             received.setdefault((0, half), []).append(to_chip(product, chips - step))
             second = pl.pallas_call(
                 more_kernel,
                 out_shape=product_shape,
-                in_specs=in_vmem(2),
+                in_specs=in_vmem(3),
                 out_specs=in_vmem(1)[0],
                 compiler_params=params(),
-            )(x1, weights)
+            )(*x1, weights)
             products = [product, second]
             after = [second]
             received.setdefault((1, half), []).append(to_chip(second, chips - step))
@@ -573,7 +599,7 @@
             after = [received[0, 0][0]]
 
     after.append(received[1, 0][0])
-    static = (scale, parts, up_rows, range(strips), columns, TOKEN_HALVES, halves)
+    static = (scale, parts, up_rows, range(strips), columns, halves)
     totals = pl.pallas_call(
         functools.partial(own_kernel, static),
         out_shape=(jax.ShapeDtypeStruct((tokens, wide), f32),) * halves,
@@ -582,7 +608,7 @@
             pl.BlockSpec((features, columns), lambda i: (lax.axis_index("tensor"), 0)),
             pl.BlockSpec((features, columns), lambda i: (lax.axis_index("tensor") ^ 1, 0)),
         ]
-        + in_vmem(2 * FACTOR_PIECES + TOKEN_HALVES)
+        + in_vmem(2 * FACTOR_PIECES + 3)
         + anywhere(len(after)),
         out_specs=tuple(in_vmem(halves)),
         scratch_shapes=[pltpu.VMEM((CORES * features, columns), bf16)],
@@ -592,7 +618,7 @@
             bytes_accessed=4 * tokens * features,
             transcendentals=0,
         ),
-    )(frozen_key_value, frozen_key_value, *pieces, *sibling_f, x0, x1, *after)
+    )(frozen_key_value, frozen_key_value, *pieces, *sibling_f, *x0, *x1, *after)
 
     keys_values = None
     for at, values in received.items():

time: 85.4 us -> 84.8 us (level)
    unnamed x24 -> x26, local copies, waits for them, and re-layouts: 8.03 us -> 8.03 us
where the time goes in v14:
time: 84.8 us; the launch traced here: 84.1 us
  Pallas kernels  33.7 us (40%)
  starting transfers between devices  27.7 us (33%)
  waiting for transfers between devices  13.9 us (16%)
  local copies, waits for them, and re-layouts  8.03 us (9%)
    ppermute x7, waiting for transfers between devices, to_chip(): return lax.ppermute(value, 'tensor', pairs)  10.9 us
    ppermute x7, starting transfers between devices, to_chip(): return lax.ppermute(value, 'tensor', pairs)  8.57 us
    pallas_call x2, Pallas kernels, prepared(): pl.pallas_call(prepare_kernel, grid=(some // rows,), out_shape=x_shape +...  8.47 us
    unnamed x26, local copies, waits for them, and re-layouts  8.03 us
    all_to_all x1, starting transfers between devices, body(): exchanged = lax.all_to_all(packed, 'dp', 0, 0, tiled=True)  6.86 us
    all_to_all x1, starting transfers between devices, body(): own_f = lax.all_to_all(sent, 'dp', 0, 0, tiled=True)  5.92 us
    ppermute x4, starting transfers between devices, swap_half(): outside[strip].append((piece, lax.ppermute(piece, 'dp', pairs)))  5.29 us
    pallas_call x2, Pallas kernels, body(): pl.pallas_call(functools.partial(outside_kernel, static, chips, step, tur...  4.99 us
  transfers between devices with their start and end apart: 17, of which 11 were waited for; matrix products, arithmetic and copies ran while one was open for 0% of the time, Pallas kernels for 39%

profile of v14, /device:TPU:0, one launch (start us, length us, event | category | flops | bytes accessed | tf_op | source)
XLA Modules:
  0.0 84.1 jit_solution(4738886605369678754)
XLA Ops:
  0.6 0.5 collective-permute-start
  1.2 2.5 %shard_map.130 = (bf16[8,192,128]{2,1,0:T(8,128)(2,1)}, bf16[2,1280,128]{2,1,0:T(8,128)(2,1)}, bf16[2,1280,128]{2,1,0:T(8,128)(2,1)}) custom-call(f32[128,1280]{1,0:T(8,128)} %bitcast.20, f32[64,512]{1,0:T(8,128)} %bitcast.24, bf16[5120,512]{1,0:T(8,128)(2,1)} %sibling_block.1), custom_call_target="tpu_custom_call" | custom-call | tf_op jit(solution)/shard_map/pallas_call | solution.py:442
  3.7 6.9 %all-to-all-start = ((bf16[8,192,128]{2,1,0:T(8,128)(2,1)}), bf16[8,192,128]{2,1,0:T(8,128)(2,1)}, u32[]{:S(2)}, u32[]{:S(2)}) async-start(bf16[8,192,128]{2,1,0:T(8,128)(2,1)} %get-tuple-element.34), calls=%async_computation | async-start | bytes 786432 | tf_op jit(solution)/shard_map/all_to_all | solution.py:457
  10.6 1.5 %collective-permute-start.5 = (bf16[2,1280,128]{2,1,0:T(8,128)(2,1)}, bf16[2,1280,128]{2,1,0:T(8,128)(2,1)}, u32[]{:S(2)}, u32[]{:S(2)}) collective-permute-start(bf16[2,1280,128]{2,1,0:T(8,128)(2,1)} %get-tuple-element.51), channel_id=1, source_target_pairs={{0,2},{1,3},{2,0},{3,1},{4,6},{5,7},{6,4},{7,5},{8,10},{9,11},{10,... | collective-permute-start | bytes 1966088 | tf_op jit(solution)/shard_map/ppermute | solution.py:419
  12.1 0.0 copy-done.10
  12.1 0.0 collective-permute-start.1
  12.1 1.2 %collective-permute-done.1.sibling_gain = f32[1,1280]{1,0:T(1,128)S(1)} collective-permute-done((f32[1,1280]{1,0:T(1,128)S(1)}, f32[1,1280]{1,0:T(1,128)S(1)}, u32[]{:S(2)}, u32[]{:S(2)}) %collective-permute-start.1) | collective-permute-done | bytes 5152 | tf_op jit(solution)/shard_map/ppermute | solution.py:411
  13.2 0.0 collective-permute-done.sibling_ref
  13.2 1.7 %copy-done.3 = bf16[1280,1280]{1,0:T(8,128)(2,1)} copy-done((bf16[1280,1280]{1,0:T(8,128)(2,1)}, bf16[1280,1280]{1,0:T(8,128)(2,1)S(1)}, u32[]{:S(2)}) %copy-start.3) | copy-done | bytes 3276824
  14.9 1.9 %copy-done.2 = bf16[1280,1280]{1,0:T(8,128)(2,1)S(1)} copy-done((bf16[1280,1280]{1,0:T(8,128)(2,1)S(1)}, bf16[1280,1280]{1,0:T(8,128)(2,1)}, u32[]{:S(2)}) %copy-start.2) | copy-done | bytes 3276824
  16.8 1.9 %copy-done.4 = bf16[1280,1280]{1,0:T(8,128)(2,1)S(1)} copy-done((bf16[1280,1280]{1,0:T(8,128)(2,1)S(1)}, bf16[1280,1280]{1,0:T(8,128)(2,1)}, u32[]{:S(2)}) %copy-start.4) | copy-done | bytes 3276824
  18.7 2.4 %shard_map.131 = (bf16[640,2560]{1,0:T(8,128)(2,1)S(1)}, f32[5,128]{1,0:T(8,128)S(1)}) custom-call(bf16[1280,1280]{1,0:T(8,128)(2,1)S(1)} %copy-done.2, bf16[1280,1280]{1,0:T(8,128)(2,1)S(1)} %copy-done.4, f32[1,1280]{1,0:T(1,128)S(1)} %broadcast_in_dim.3.own_gain, f32[1,1280]{1,0:T(1,128)S(1)} %collective-permute-done.1.sibling_gain), custom_call_target="tpu_custom_call" | custom-call | tf_op jit(solution)/shard_map/pallas_call | solution.py:487
  21.1 0.6 copy-done.5
  21.7 0.6 copy-done.8
  22.3 0.6 copy-done.9
  22.9 0.1 all-to-all-done.grad_in
  23.0 2.5 %shard_map.132 = (f32[3,128,160]{2,1,0:T(8,128)}, f32[3,8,512]{2,1,0:T(8,128)}, bf16[8,192,128]{2,1,0:T(8,128)(2,1)}) custom-call(bf16[8,192,128]{2,1,0:T(8,128)(2,1)} %all-to-all-done.grad_in, f32[128,1280]{1,0:T(8,128)} %bitcast.21, f32[128,1280]{1,0:T(8,128)} %bitcast.22, f32[128,1280]{1,0:T(8,128)} %bitcast.23, f32[64,512]{1,0:T(8,128)} %refs_3_.1, ...), custom_call_target="tpu_custom_call" | custom-call | tf_op jit(solution)/shard_map/pallas_call | solution.py:502
  25.6 5.9 %all-to-all-start.1 = ((bf16[8,192,128]{2,1,0:T(8,128)(2,1)}), bf16[8,192,128]{2,1,0:T(8,128)(2,1)}, u32[]{:S(2)}, u32[]{:S(2)}) async-start(bf16[8,192,128]{2,1,0:T(8,128)(2,1)} %get-tuple-element.39), calls=%async_computation.1 | async-start | bytes 786432 | tf_op jit(solution)/shard_map/all_to_all | solution.py:519
  31.5 0.0 collective-permute-done.5.in_ref
  31.5 0.6 collective-permute-start.6
  32.1 1.9 %shard_map.135 = (bf16[1280,128]{1,0:T(8,128)(2,1)}, bf16[1280,128]{1,0:T(8,128)(2,1)}) custom-call(bf16[2,1280,128]{2,1,0:T(8,128)(2,1)} %collective-permute-done.5.in_ref), custom_call_target="tpu_custom_call" | custom-call | tf_op jit(solution)/shard_map/pallas_call | solution.py:529
  34.0 2.0 %collective-permute-start.7 = (bf16[1280,128]{1,0:T(8,128)(2,1)}, bf16[1280,128]{1,0:T(8,128)(2,1)}, u32[]{:S(2)}, u32[]{:S(2)}) collective-permute-start(bf16[1280,128]{1,0:T(8,128)(2,1)} %get-tuple-element.54.refs_4_), channel_id=1, source_target_pairs={{0,4},{4,0},{8,12},{12,8},{16,20},{20,16},{24,28},{28,24},{1,5},{5... | collective-permute-start | bytes 983048 | tf_op jit(solution)/shard_map/ppermute | solution.py:538
  36.0 1.5 %collective-permute-start.8 = (bf16[1280,128]{1,0:T(8,128)(2,1)}, bf16[1280,128]{1,0:T(8,128)(2,1)}, u32[]{:S(2)}, u32[]{:S(2)}) collective-permute-start(bf16[1280,128]{1,0:T(8,128)(2,1)} %get-tuple-element.55.refs_6_), channel_id=1, source_target_pairs={{0,8},{4,12},{8,0},{12,4},{16,24},{20,28},{24,16},{28,20},{1,9},{5... | collective-permute-start | bytes 983048 | tf_op jit(solution)/shard_map/ppermute | solution.py:538
  37.5 6.1 %shard_map.133 = (bf16[640,1280]{1,0:T(8,128)(2,1)}, bf16[640,1280]{1,0:T(8,128)(2,1)}, f32[10,128]{1,0:T(8,128)}) custom-call(bf16[1280,1280]{1,0:T(8,128)(2,1)} %own_ref.3, bf16[1280,1280]{1,0:T(8,128)(2,1)} %copy-done.3, f32[1,1280]{1,0:T(1,128)} %copy-done.5, f32[1,1280]{1,0:T(1,128)} %copy-done.8, f32[5,128]{1,0:T(8,128)} %copy-done.9), custom_call_target="tpu_custom_call" | custom-call | tf_op jit(solution)/shard_map/pallas_call | solution.py:487
  43.6 0.0 all-to-all-done.1.factor_ref
  43.6 0.7 copy-done.6
  44.3 1.1 %shard_map.134 = (bf16[9,32,128]{2,1,0:T(8,128)(2,1)S(1)}, bf16[4,192,128]{2,1,0:T(8,128)(2,1)S(1)}, bf16[4,192,128]{2,1,0:T(8,128)(2,1)S(1)}) custom-call(bf16[8,192,128]{2,1,0:T(8,128)(2,1)} %all-to-all-done.1.factor_ref, f32[10,128]{1,0:T(8,128)S(1)} %copy-done.6), custom_call_target="tpu_custom_call" | custom-call | tf_op jit(solution)/shard_map/pallas_call | solution.py:545
  45.4 0.1 collective-permute-start.2
  45.5 0.5 collective-permute-start.3
  46.0 0.1 collective-permute-done.7.refs_5_
  46.1 1.4 %collective-permute-start.4 = (bf16[9,32,128]{2,1,0:T(8,128)(2,1)S(1)}, bf16[9,32,128]{2,1,0:T(8,128)(2,1)S(1)}, u32[]{:S(2)}, u32[]{:S(2)}) collective-permute-start(bf16[9,32,128]{2,1,0:T(8,128)(2,1)S(1)} %get-tuple-element.49), channel_id=1, source_target_pairs={{0,2},{1,3},{2,0},{3,1},{4,6},{5,7},{6,4},{7,5},{8,10},{9,11},{10,... | collective-permute-start | bytes 221192 | tf_op jit(solution)/shard_map/ppermute | solution.py:419
  47.4 0.6 collective-permute-done.8.refs_7_
  48.0 2.4 %collective-permute-done.4.b_ref.refs_0_ = bf16[9,32,128]{2,1,0:T(8,128)(2,1)S(1)} collective-permute-done((bf16[9,32,128]{2,1,0:T(8,128)(2,1)S(1)}, bf16[9,32,128]{2,1,0:T(8,128)(2,1)S(1)}, u32[]{:S(2)}, u32[]{:S(2)}) %collective-permute-start.4) | collective-permute-done | bytes 73760 | tf_op jit(solution)/shard_map/ppermute | solution.py:419
  50.4 0.0 collective-permute-done.2.refs_2_
  50.4 0.0 collective-permute-done.3.refs_3_
  50.4 0.0 copy-start.1
  50.4 3.2 %shard_map.136 = (bf16[2560,256]{1,0:T(8,128)(2,1)S(1)}, bf16[640,256]{1,0:T(8,128)(2,1)S(1)}) custom-call(bf16[9,32,128]{2,1,0:T(8,128)(2,1)S(1)} %collective-permute-done.4.b_ref.refs_0_, bf16[640,2560]{1,0:T(8,128)(2,1)S(1)} %get-tuple-element.46.x.refs_4_, bf16[4,192,128]{2,1,0:T(8,128)(2,1)S(1)} %get-tuple-element.44.refs_0_, ...), custom_call_target="tpu_custom_call" | custom-call | tf_op jit(solution)/shard_map/pallas_call | solution.py:580
  53.6 1.5 %collective-permute-start.11 = (bf16[640,256]{1,0:T(8,128)(2,1)S(1)}, bf16[640,256]{1,0:T(8,128)(2,1)S(1)}, u32[]{:S(2)}, u32[]{:S(2)}) collective-permute-start(bf16[640,256]{1,0:T(8,128)(2,1)S(1)} %get-tuple-element.56), channel_id=1, source_target_pairs={{0,2},{1,3},{2,0},{3,1},{4,6},{5,7},{6,4},{7,5},{8,10},{9,11},{10,... | collective-permute-start | bytes 983048 | tf_op jit(solution)/shard_map/ppermute | solution.py:419
  55.1 0.0 collective-permute-done.6.in_ref
  55.1 1.1 %shard_map.137 = (bf16[1280,128]{1,0:T(8,128)(2,1)S(1)}, bf16[1280,128]{1,0:T(8,128)(2,1)S(1)}) custom-call(bf16[2,1280,128]{2,1,0:T(8,128)(2,1)} %collective-permute-done.6.in_ref), custom_call_target="tpu_custom_call" | custom-call | tf_op jit(solution)/shard_map/pallas_call | solution.py:529
  56.2 0.6 collective-permute-start.9
  56.8 1.2 %collective-permute-start.10 = (bf16[1280,128]{1,0:T(8,128)(2,1)S(1)}, bf16[1280,128]{1,0:T(8,128)(2,1)S(1)}, u32[]{:S(2)}, u32[]{:S(2)}) collective-permute-start(bf16[1280,128]{1,0:T(8,128)(2,1)S(1)} %get-tuple-element.59.refs_6_), channel_id=1, source_target_pairs={{0,8},{4,12},{8,0},{12,4},{16,24},{20,28},{24,16},{28,20},{1,9},{5... | collective-permute-start | bytes 983048 | tf_op jit(solution)/shard_map/ppermute | solution.py:538
  58.1 0.0 copy-done
  58.1 1.2 %shard_map.140 = bf16[640,256]{1,0:T(8,128)(2,1)S(1)} custom-call(bf16[640,1280]{1,0:T(8,128)(2,1)S(1)} %copy-done, bf16[640,1280]{1,0:T(8,128)(2,1)S(1)} %copy-done.1, bf16[2560,256]{1,0:T(8,128)(2,1)S(1)} %get-tuple-element.61.refs_2_), custom_call_target="tpu_custom_call" | custom-call | tf_op jit(solution)/shard_map/pallas_call | solution.py:588
  59.3 0.0 slice-start.1
  59.3 1.5 %collective-permute-start.12 = (bf16[640,256]{1,0:T(8,128)(2,1)S(1)}, bf16[640,256]{1,0:T(8,128)(2,1)S(1)}, u32[]{:S(2)}, u32[]{:S(2)}) collective-permute-start(bf16[640,256]{1,0:T(8,128)(2,1)S(1)} %shard_map.140), channel_id=1, source_target_pairs={{0,2},{1,3},{2,0},{3,1},{4,6},{5,7},{6,4},{7,5},{8,10},{9,11},{10,... | collective-permute-start | bytes 983048 | tf_op jit(solution)/shard_map/ppermute | solution.py:419
  60.8 3.0 %collective-permute-done.11.refs_8_.refs_0_ = bf16[640,256]{1,0:T(8,128)(2,1)S(1)} collective-permute-done((bf16[640,256]{1,0:T(8,128)(2,1)S(1)}, bf16[640,256]{1,0:T(8,128)(2,1)S(1)}, u32[]{:S(2)}, u32[]{:S(2)}) %collective-permute-start.11) | collective-permute-done | bytes 327712 | tf_op jit(solution)/shard_map/ppermute | solution.py:419
  63.8 0.7 collective-permute-done.9.refs_5_
  64.5 0.3 collective-permute-done.10.refs_7_
  64.8 1.8 %shard_map.138 = (bf16[2560,256]{1,0:T(8,128)(2,1)S(1)}, bf16[640,256]{1,0:T(8,128)(2,1)S(1)}) custom-call(bf16[9,32,128]{2,1,0:T(8,128)(2,1)S(1)} %collective-permute-done.4.b_ref.refs_0_, bf16[640,2560]{1,0:T(8,128)(2,1)S(1)} %get-tuple-element.46.x.refs_4_, bf16[4,192,128]{2,1,0:T(8,128)(2,1)S(1)} %get-tuple-element.44.refs_0_, ...), custom_call_target="tpu_custom_call" | custom-call | tf_op jit(solution)/shard_map/pallas_call | solution.py:580
  66.6 1.5 %collective-permute-start.14 = (bf16[640,256]{1,0:T(8,128)(2,1)S(1)}, bf16[640,256]{1,0:T(8,128)(2,1)S(1)}, u32[]{:S(2)}, u32[]{:S(2)}) collective-permute-start(bf16[640,256]{1,0:T(8,128)(2,1)S(1)} %get-tuple-element.63), channel_id=1, source_target_pairs={{0,2},{1,3},{2,0},{3,1},{4,6},{5,7},{6,4},{7,5},{8,10},{9,11},{10,... | collective-permute-start | bytes 983048 | tf_op jit(solution)/shard_map/ppermute | solution.py:419
  68.2 1.2 %shard_map.139.refs_7_ = bf16[640,256]{1,0:T(8,128)(2,1)S(1)} custom-call(bf16[640,1280]{1,0:T(8,128)(2,1)S(1)} %copy-done, bf16[640,1280]{1,0:T(8,128)(2,1)S(1)} %copy-done.1, bf16[2560,256]{1,0:T(8,128)(2,1)S(1)} %get-tuple-element.60.refs_2_), custom_call_target="tpu_custom_call" | custom-call | tf_op jit(solution)/shard_map/pallas_call | solution.py:588
  69.4 0.6 collective-permute-start.13
  70.0 0.0 copy-done.7
  70.0 0.2 shard_map.142.inv
  70.2 0.6 collective-permute-done.12.refs_8_.refs_0_
  70.8 0.0 slice-done
  70.8 4.9 %shard_map.141 = (f32[1280,256]{1,0:T(8,128)S(1)}, f32[1280,256]{1,0:T(8,128)S(1)}) custom-call(bf16[5120,512]{1,0:T(8,128)(2,1)S(1)} %bitcast.19, bf16[5120,512]{1,0:T(8,128)(2,1)S(1)} %bitcast.19, bf16[4,192,128]{2,1,0:T(8,128)(2,1)S(1)} %get-tuple-element.44.refs_0_, bf16[4,192,128]{2,1,0:T(8,128)(2,1)S(1)} %get-tuple-element.45.refs_1_, ...), custom_call_target="tpu_custom_call" | custom-call | flops 3355443200 | bytes 6553600 | tf_op jit(solution)/shard_map/pallas_call | solution.py:603
  75.7 0.9 %shard_map.143.refs_1_ = bf16[1280,512]{1,0:T(8,128)(2,1)} custom-call(f32[1280,256]{1,0:T(8,128)S(1)} %get-tuple-element.64.own, f32[1280,128]{1,0:T(8,128)S(1)} %shard_map.142.inv, bf16[640,256]{1,0:T(8,128)(2,1)S(1)} %collective-permute-done.11.refs_8_.refs_0_), custom_call_target="tpu_custom_call" | custom-call | tf_op jit(solution)/shard_map/pallas_call | solution.py:370
  76.6 0.9 %shard_map.144.refs_1_ = bf16[1280,512]{1,0:T(8,128)(2,1)} custom-call(f32[1280,256]{1,0:T(8,128)S(1)} %get-tuple-element.64.own, f32[1280,128]{1,0:T(8,128)S(1)} %shard_map.142.inv, bf16[640,256]{1,0:T(8,128)(2,1)S(1)} %collective-permute-done.12.refs_8_.refs_0_, bf16[1280,512]{1,0:T(8,128)(2,1)} %shard_map.143.refs_1_), custom_call_target="tpu_custom_call", output_to_operand_aliasing={{}: (3, {})} | custom-call | tf_op jit(solution)/shard_map/pallas_call | solution.py:370
  77.5 0.4 collective-permute-done.14.refs_0_
  77.9 0.9 %shard_map.145.refs_1_ = bf16[1280,512]{1,0:T(8,128)(2,1)} custom-call(f32[1280,256]{1,0:T(8,128)S(1)} %get-tuple-element.62.own, f32[1280,128]{1,0:T(8,128)S(1)} %shard_map.142.inv, bf16[640,256]{1,0:T(8,128)(2,1)S(1)} %collective-permute-done.14.refs_0_, bf16[1280,512]{1,0:T(8,128)(2,1)} %shard_map.144.refs_1_), custom_call_target="tpu_custom_call", output_to_operand_aliasing={{}: (3, {})} | custom-call | tf_op jit(solution)/shard_map/pallas_call | solution.py:370
  78.7 4.5 %collective-permute-done.13.refs_0_ = bf16[640,256]{1,0:T(8,128)(2,1)S(1)} collective-permute-done((bf16[640,256]{1,0:T(8,128)(2,1)S(1)}, bf16[640,256]{1,0:T(8,128)(2,1)S(1)}, u32[]{:S(2)}, u32[]{:S(2)}) %collective-permute-start.13) | collective-permute-done | bytes 327712 | tf_op jit(solution)/shard_map/ppermute | solution.py:419
  83.2 0.9 %shard_map.146 = bf16[1280,512]{1,0:T(8,128)(2,1)} custom-call(f32[1280,256]{1,0:T(8,128)S(1)} %get-tuple-element.62.own, f32[1280,128]{1,0:T(8,128)S(1)} %shard_map.142.inv, bf16[640,256]{1,0:T(8,128)(2,1)S(1)} %collective-permute-done.13.refs_0_, bf16[1280,512]{1,0:T(8,128)(2,1)} %shard_map.145.refs_1_), custom_call_target="tpu_custom_call", output_to_operand_aliasing={{}: (3, {})} | custom-call | tf_op jit(solution)/shard_map/pallas_call | solution.py:370
  (15 shorter events, 0.0 us)
Async XLA Ops:
  0.6 12.6 %collective-permute-start = (bf16[1280,1280]{1,0:T(8,128)(2,1)}, bf16[1280,1280]{1,0:T(8,128)(2,1)S(1)}, u32[]{:S(2)}, u32[]{:S(2)}) collective-permute-start(bf16[1280,1280]{1,0:T(8,128)(2,1)} %own_ref.3), channel_id=1, source_target_pairs={{0,1},{1,0},{2,3},{3,2},{4,5},{5,4},{6,7},{7,6},{8,9},{9,8},{10,11... | collective-permute-start | bytes 9830408 | tf_op jit(solution)/shard_map/ppermute | solution.py:411
  1.1 10.9 %copy-start.10 = (f32[1280]{0:T(1024)S(1)}, f32[1280]{0:T(1024)}, u32[]{:S(2)}) copy-start(f32[1280]{0:T(1024)} %param.12) | copy-start | bytes 15364
  3.7 19.3 %all-to-all-start = ((bf16[8,192,128]{2,1,0:T(8,128)(2,1)}), bf16[8,192,128]{2,1,0:T(8,128)(2,1)}, u32[]{:S(2)}, u32[]{:S(2)}) async-start(bf16[8,192,128]{2,1,0:T(8,128)(2,1)} %get-tuple-element.34), calls=%async_computation | async-start | bytes 786432 | tf_op jit(solution)/shard_map/all_to_all | solution.py:457
  10.6 20.9 %collective-permute-start.5 = (bf16[2,1280,128]{2,1,0:T(8,128)(2,1)}, bf16[2,1280,128]{2,1,0:T(8,128)(2,1)}, u32[]{:S(2)}, u32[]{:S(2)}) collective-permute-start(bf16[2,1280,128]{2,1,0:T(8,128)(2,1)} %get-tuple-element.51), channel_id=1, source_target_pairs={{0,2},{1,3},{2,0},{3,1},{4,6},{5,7},{6,4},{7,5},{8,10},{9,11},{10,... | collective-permute-start | bytes 1966088 | tf_op jit(solution)/shard_map/ppermute | solution.py:419
  12.1 1.2 %collective-permute-start.1 = (f32[1,1280]{1,0:T(1,128)S(1)}, f32[1,1280]{1,0:T(1,128)S(1)}, u32[]{:S(2)}, u32[]{:S(2)}) collective-permute-start(f32[1,1280]{1,0:T(1,128)S(1)} %broadcast_in_dim.3.own_gain), channel_id=1, source_target_pairs={{0,1},{1,0},{2,3},{3,2},{4,5},{5,4},{6,7},{7,6},{8,9},{9,8},{10,11... | collective-permute-start | bytes 15368 | tf_op jit(solution)/shard_map/ppermute | solution.py:411
  13.2 1.7 %copy-start.3 = (bf16[1280,1280]{1,0:T(8,128)(2,1)}, bf16[1280,1280]{1,0:T(8,128)(2,1)S(1)}, u32[]{:S(2)}) copy-start(bf16[1280,1280]{1,0:T(8,128)(2,1)S(1)} %collective-permute-done.sibling_ref) | copy-start | bytes 9830404
  14.9 1.9 %copy-start.2 = (bf16[1280,1280]{1,0:T(8,128)(2,1)S(1)}, bf16[1280,1280]{1,0:T(8,128)(2,1)}, u32[]{:S(2)}) copy-start(bf16[1280,1280]{1,0:T(8,128)(2,1)} %own_ref.3) | copy-start | bytes 9830404
  16.8 1.9 %copy-start.4 = (bf16[1280,1280]{1,0:T(8,128)(2,1)S(1)}, bf16[1280,1280]{1,0:T(8,128)(2,1)}, u32[]{:S(2)}) copy-start(bf16[1280,1280]{1,0:T(8,128)(2,1)} %copy-done.3) | copy-start | bytes 9830404
  21.1 0.6 copy-start.5
  21.7 0.6 copy-start.8
  22.3 0.6 copy-start.9
  25.6 18.0 %all-to-all-start.1 = ((bf16[8,192,128]{2,1,0:T(8,128)(2,1)}), bf16[8,192,128]{2,1,0:T(8,128)(2,1)}, u32[]{:S(2)}, u32[]{:S(2)}) async-start(bf16[8,192,128]{2,1,0:T(8,128)(2,1)} %get-tuple-element.39), calls=%async_computation.1 | async-start | bytes 786432 | tf_op jit(solution)/shard_map/all_to_all | solution.py:519
  31.5 23.6 %collective-permute-start.6 = (bf16[2,1280,128]{2,1,0:T(8,128)(2,1)}, bf16[2,1280,128]{2,1,0:T(8,128)(2,1)}, u32[]{:S(2)}, u32[]{:S(2)}) collective-permute-start(bf16[2,1280,128]{2,1,0:T(8,128)(2,1)} %get-tuple-element.52), channel_id=1, source_target_pairs={{0,2},{1,3},{2,0},{3,1},{4,6},{5,7},{6,4},{7,5},{8,10},{9,11},{10,... | collective-permute-start | bytes 1966088 | tf_op jit(solution)/shard_map/ppermute | solution.py:419
  34.0 12.0 %collective-permute-start.7 = (bf16[1280,128]{1,0:T(8,128)(2,1)}, bf16[1280,128]{1,0:T(8,128)(2,1)}, u32[]{:S(2)}, u32[]{:S(2)}) collective-permute-start(bf16[1280,128]{1,0:T(8,128)(2,1)} %get-tuple-element.54.refs_4_), channel_id=1, source_target_pairs={{0,4},{4,0},{8,12},{12,8},{16,20},{20,16},{24,28},{28,24},{1,5},{5... | collective-permute-start | bytes 983048 | tf_op jit(solution)/shard_map/ppermute | solution.py:538
  36.0 12.0 %collective-permute-start.8 = (bf16[1280,128]{1,0:T(8,128)(2,1)}, bf16[1280,128]{1,0:T(8,128)(2,1)}, u32[]{:S(2)}, u32[]{:S(2)}) collective-permute-start(bf16[1280,128]{1,0:T(8,128)(2,1)} %get-tuple-element.55.refs_6_), channel_id=1, source_target_pairs={{0,8},{4,12},{8,0},{12,4},{16,24},{20,28},{24,16},{28,20},{1,9},{5... | collective-permute-start | bytes 983048 | tf_op jit(solution)/shard_map/ppermute | solution.py:538
  43.6 0.7 copy-start.6
  45.4 5.0 %collective-permute-start.2 = (bf16[4,192,128]{2,1,0:T(8,128)(2,1)S(1)}, bf16[4,192,128]{2,1,0:T(8,128)(2,1)S(1)}, u32[]{:S(2)}, u32[]{:S(2)}) collective-permute-start(bf16[4,192,128]{2,1,0:T(8,128)(2,1)S(1)} %get-tuple-element.44.refs_0_), channel_id=1, source_target_pairs={{0,1},{1,0},{2,3},{3,2},{4,5},{5,4},{6,7},{7,6},{8,9},{9,8},{10,11... | collective-permute-start | bytes 589832 | tf_op jit(solution)/shard_map/ppermute | solution.py:411
  45.5 4.9 %collective-permute-start.3 = (bf16[4,192,128]{2,1,0:T(8,128)(2,1)S(1)}, bf16[4,192,128]{2,1,0:T(8,128)(2,1)S(1)}, u32[]{:S(2)}, u32[]{:S(2)}) collective-permute-start(bf16[4,192,128]{2,1,0:T(8,128)(2,1)S(1)} %get-tuple-element.45.refs_1_), channel_id=1, source_target_pairs={{0,1},{1,0},{2,3},{3,2},{4,5},{5,4},{6,7},{7,6},{8,9},{9,8},{10,11... | collective-permute-start | bytes 589832 | tf_op jit(solution)/shard_map/ppermute | solution.py:411
  46.1 4.4 %collective-permute-start.4 = (bf16[9,32,128]{2,1,0:T(8,128)(2,1)S(1)}, bf16[9,32,128]{2,1,0:T(8,128)(2,1)S(1)}, u32[]{:S(2)}, u32[]{:S(2)}) collective-permute-start(bf16[9,32,128]{2,1,0:T(8,128)(2,1)S(1)} %get-tuple-element.49), channel_id=1, source_target_pairs={{0,2},{1,3},{2,0},{3,1},{4,6},{5,7},{6,4},{7,5},{8,10},{9,11},{10,... | collective-permute-start | bytes 221192 | tf_op jit(solution)/shard_map/ppermute | solution.py:419
  50.4 7.7 %copy-start = (bf16[640,1280]{1,0:T(8,128)(2,1)S(1)}, bf16[640,1280]{1,0:T(8,128)(2,1)}, u32[]{:S(2)}) copy-start(bf16[640,1280]{1,0:T(8,128)(2,1)} %get-tuple-element.47.refs_0_.refs_5_) | copy-start | bytes 4915204
  50.4 7.7 %copy-start.1 = (bf16[640,1280]{1,0:T(8,128)(2,1)S(1)}, bf16[640,1280]{1,0:T(8,128)(2,1)}, u32[]{:S(2)}) copy-start(bf16[640,1280]{1,0:T(8,128)(2,1)} %get-tuple-element.48.refs_1_.refs_6_) | copy-start | bytes 4915204
  53.6 10.2 %collective-permute-start.11 = (bf16[640,256]{1,0:T(8,128)(2,1)S(1)}, bf16[640,256]{1,0:T(8,128)(2,1)S(1)}, u32[]{:S(2)}, u32[]{:S(2)}) collective-permute-start(bf16[640,256]{1,0:T(8,128)(2,1)S(1)} %get-tuple-element.56), channel_id=1, source_target_pairs={{0,2},{1,3},{2,0},{3,1},{4,6},{5,7},{6,4},{7,5},{8,10},{9,11},{10,... | collective-permute-start | bytes 983048 | tf_op jit(solution)/shard_map/ppermute | solution.py:419
  56.2 8.3 %collective-permute-start.9 = (bf16[1280,128]{1,0:T(8,128)(2,1)S(1)}, bf16[1280,128]{1,0:T(8,128)(2,1)S(1)}, u32[]{:S(2)}, u32[]{:S(2)}) collective-permute-start(bf16[1280,128]{1,0:T(8,128)(2,1)S(1)} %get-tuple-element.58.refs_4_), channel_id=1, source_target_pairs={{0,4},{4,0},{8,12},{12,8},{16,20},{20,16},{24,28},{28,24},{1,5},{5... | collective-permute-start | bytes 983048 | tf_op jit(solution)/shard_map/ppermute | solution.py:538
  56.8 8.0 %collective-permute-start.10 = (bf16[1280,128]{1,0:T(8,128)(2,1)S(1)}, bf16[1280,128]{1,0:T(8,128)(2,1)S(1)}, u32[]{:S(2)}, u32[]{:S(2)}) collective-permute-start(bf16[1280,128]{1,0:T(8,128)(2,1)S(1)} %get-tuple-element.59.refs_6_), channel_id=1, source_target_pairs={{0,8},{4,12},{8,0},{12,4},{16,24},{20,28},{24,16},{28,20},{1,9},{5... | collective-permute-start | bytes 983048 | tf_op jit(solution)/shard_map/ppermute | solution.py:538
  58.1 12.7 %slice-start = ((s8[5242880]{0:T(1024)(128)(4,1)}), s8[4194304]{0:T(1024)(128)(4,1)S(1)}, s32[]{:S(2)}) async-start(s8[5242880]{0:T(1024)(128)(4,1)} %bitcast.18), calls=%async_computation.2 | async-start | bytes 8388608
  59.3 11.6 %slice-start.1 = ((s8[5242880]{0:T(1024)(128)(4,1)}), s8[1048576]{0:T(1024)(128)(4,1)S(1)}, s32[]{:S(2)}) async-start(s8[5242880]{0:T(1024)(128)(4,1)} %bitcast.18), calls=%async_computation.3 | async-start | bytes 2097152
  59.3 11.5 %collective-permute-start.12 = (bf16[640,256]{1,0:T(8,128)(2,1)S(1)}, bf16[640,256]{1,0:T(8,128)(2,1)S(1)}, u32[]{:S(2)}, u32[]{:S(2)}) collective-permute-start(bf16[640,256]{1,0:T(8,128)(2,1)S(1)} %shard_map.140), channel_id=1, source_target_pairs={{0,2},{1,3},{2,0},{3,1},{4,6},{5,7},{6,4},{7,5},{8,10},{9,11},{10,... | collective-permute-start | bytes 983048 | tf_op jit(solution)/shard_map/ppermute | solution.py:419
  66.6 11.2 %collective-permute-start.14 = (bf16[640,256]{1,0:T(8,128)(2,1)S(1)}, bf16[640,256]{1,0:T(8,128)(2,1)S(1)}, u32[]{:S(2)}, u32[]{:S(2)}) collective-permute-start(bf16[640,256]{1,0:T(8,128)(2,1)S(1)} %get-tuple-element.63), channel_id=1, source_target_pairs={{0,2},{1,3},{2,0},{3,1},{4,6},{5,7},{6,4},{7,5},{8,10},{9,11},{10,... | collective-permute-start | bytes 983048 | tf_op jit(solution)/shard_map/ppermute | solution.py:419
  68.2 1.8 %copy-start.7 = (f32[10,128]{1,0:T(8,128)S(1)}, f32[10,128]{1,0:T(8,128)}, u32[]{:S(2)}) copy-start(f32[10,128]{1,0:T(8,128)} %get-tuple-element.43.sums_ref) | copy-start | bytes 15364
  69.4 13.9 %collective-permute-start.13 = (bf16[640,256]{1,0:T(8,128)(2,1)S(1)}, bf16[640,256]{1,0:T(8,128)(2,1)S(1)}, u32[]{:S(2)}, u32[]{:S(2)}) collective-permute-start(bf16[640,256]{1,0:T(8,128)(2,1)S(1)} %shard_map.139.refs_7_), channel_id=1, source_target_pairs={{0,2},{1,3},{2,0},{3,1},{4,6},{5,7},{6,4},{7,5},{8,10},{9,11},{10,... | collective-permute-start | bytes 983048 | tf_op jit(solution)/shard_map/ppermute | solution.py:419

commit v15 on v14

--- a/solution.py
+++ b/solution.py
@@ -17,7 +17,7 @@
 FACTOR_PIECES = 2
 VMEM_BYTES = 16 * 2**20
 LARGE_VMEM_BYTES = 58 * 2**20
-PREPARE_VMEM_BYTES = 40 * 2**20
+PREPARE_VMEM_BYTES = 49 * 2**20
 
 
 def adaptive_moment_update(param, first, second, grad_mean):
@@ -104,42 +104,65 @@
         out[...] = in_ref[k]
 
 
-def prepare_kernel(own_ref, sibling_ref, own_gain, sibling_gain, *refs):
-    block, features = own_ref.shape
-    step = pl.program_id(0)
-    sums_ref, squares = refs[-2:]
-    sibling_x = refs[-3]
-    if sibling_x.shape[1] == features:
-        before, own_x, lane = refs[:-4], refs[-4], 0
-    else:
-        before, own_x, lane = refs[:-3], sibling_x, features
-    first = 0 if refs[-3].shape[0] == block else step * block
+def prepare_kernel(first, own_in, sibling_in, own_gain, sibling_gain, *refs):
+    own, sibling, squares, sem = refs[-4:]
+    rows, features = own.shape
+    together = refs[-6].shape[1] > features
+    outs, sums_ref = refs[-6 if together else -7 : -5], refs[-5]
+    before = refs[: -6 if together else -7]
+    block = LANES if rows % LANES == 0 else rows
     tile = 16 if block % 16 == 0 else block
-
-    @pl.loop(0, block // tile, unroll=2)
-    def _(i):
-        at = pl.ds(pl.multiple_of(i * tile, tile), tile)
-        to = pl.ds(pl.multiple_of(first + i * tile, tile), tile)
-        own = own_ref[at, :].astype(jnp.float32)
-        own_x[to, :features] = (own * own_gain[...]).astype(own_x.dtype)
-        total = own * own
-        sibling = sibling_ref[at, :].astype(jnp.float32)
-        scaled = (sibling * sibling_gain[...]).astype(sibling_x.dtype)
-        sibling_x[to, lane : lane + features] = scaled
-        total += sibling * sibling
-        total = jnp.sum(total, axis=1, keepdims=True)
-        to = pl.ds(pl.multiple_of(step * block + i * tile, tile), tile)
-        squares[to, :] = jnp.broadcast_to(total, (tile, LANES))
-
-    @pl.when(step == pl.num_programs(0) - 1)
-    def _():
-        done = 0
-        for ref in before:
-            sums_ref[: ref.shape[0]] = ref[...]
-            done = ref.shape[0]
-        for i in range(squares.shape[0] // LANES):
-            row = squares[i * LANES : (i + 1) * LANES, :].T[:1]
-            sums_ref[done + i : done + i + 1] = row
+    count = rows // block
+    raw = ((own_in, own), (sibling_in, sibling))
+    loads = [
+        [
+            pltpu.make_async_copy(
+                source.at[pl.ds(first + k * block, block)],
+                target.at[pl.ds(k * block, block)],
+                sem.at[2 * k + side],
+            )
+            for side, (source, target) in enumerate(raw)
+        ]
+        for k in range(count)
+    ]
+    for pair in loads:
+        for copy in pair:
+            copy.start()
+    stores = []
+    for k in range(count):
+        for copy in loads[k]:
+            copy.wait()
+
+        @pl.loop(0, block // tile, unroll=2)
+        def _(i):
+            at = pl.ds(pl.multiple_of(k * block + i * tile, tile), tile)
+            total = None
+            for side, (ref, gain) in enumerate(((own, own_gain), (sibling, sibling_gain))):
+                value = ref[at, :].astype(jnp.float32)
+                scaled = (value * gain[...]).astype(ref.dtype)
+                if together:
+                    outs[0][at, side * features : (side + 1) * features] = scaled
+                else:
+                    ref[at, :] = scaled
+                total = value * value if total is None else total + value * value
+            total = jnp.sum(total, axis=1, keepdims=True)
+            squares[at, :] = jnp.broadcast_to(total, (tile, LANES))
+
+        if not together:
+            part = pl.ds(k * block, block)
+            for side, (source, out) in enumerate(((own, outs[0]), (sibling, outs[1]))):
+                place = sem.at[2 * (count + k) + side]
+                stores.append(pltpu.make_async_copy(source.at[part], out.at[part], place))
+                stores[-1].start()
+    done = 0
+    for ref in before:
+        sums_ref[: ref.shape[0]] = ref[...]
+        done = ref.shape[0]
+    for i in range(rows // LANES):
+        row = squares[i * LANES : (i + 1) * LANES, :].T[:1]
+        sums_ref[done + i : done + i + 1] = row
+    for copy in stores:
+        copy.wait()
 
 
 def message_kernel(factor_ref, sums_ref, out_ref, *refs):
@@ -299,23 +322,34 @@
 
 def outside_kernel(static, chips, step, turn, b_ref, x, *refs):
     own_f, sibling_f = refs[:FACTOR_PIECES], refs[FACTOR_PIECES : 2 * FACTOR_PIECES]
-    blocks, (weights, product) = refs[2 * FACTOR_PIECES :], refs[-2:]
+    weights, product, blocks, sem = refs[-4:]
     strips = static[3]
-    features = blocks[0].shape[0]
+    copies = [
+        pltpu.make_async_copy(refs[2 * FACTOR_PIECES + k], blocks.at[k], sem.at[k])
+        for k in range(2 * len(strips))
+    ]
+    for copy in copies:
+        copy.start()
+    features = blocks.shape[1]
     down_rows = own_f[0].shape[1] - b_ref.shape[1]
     shares = FACTOR_PIECES * own_f[0].shape[0]
     place, replica = lax.axis_index("tensor"), lax.axis_index("dp")
     owner = (place // CORES - step + chips) % chips * CORES + place % CORES
     b = up_factor(static, b_ref[:shares], owner)
-    own_a, sibling_a = factor_a(own_f, down_rows), factor_a(sibling_f, down_rows)
+    changes = [
+        jnp.dot(factor_a(f, down_rows), b, preferred_element_type=jnp.float32)
+        for f in (own_f, sibling_f)
+    ]
+    for copy in copies:
+        copy.wait()
     for k, strip in enumerate(strips):
-        mine, other = blocks[2 * k : 2 * k + 2]
+        mine, other = blocks.at[2 * k], blocks.at[2 * k + 1]
         even = replica // turn[strip] % 2 == 0
         lanes = slice(k * LANES, (k + 1) * LANES)
-        block = jnp.where(even, mine[...], other[...])
-        weights[:features, lanes] = merge(static[0], block, own_a, b[:, lanes])
-        block = jnp.where(even, other[...], mine[...])
-        weights[features:, lanes] = merge(static[0], block, sibling_a, b[:, lanes])
+        for side, (near, far) in enumerate(((mine, other), (other, mine))):
+            block = jnp.where(even, near[...], far[...]).astype(jnp.float32)
+            block = (block + static[0] * changes[side][:, lanes]).astype(jnp.bfloat16)
+            weights[side * features : (side + 1) * features, lanes] = block
     more_kernel(x, weights, product)
 
 
@@ -472,26 +506,27 @@
 
     gain = input_norm_gain[None, :]
     some = tokens // TOKEN_HALVES
-    rows = LANES if some % LANES == 0 else some
     operands = [prompt_hidden_input, to_sibling(prompt_hidden_input), gain, to_sibling(gain)]
 
     def prepared(half, before, in_place, limit):
-        token_block = pl.BlockSpec((rows, features), lambda i: (half * (some // rows) + i, 0))
-        gain_block = pl.BlockSpec((1, features), lambda i: (0, 0))
         if in_place:
             x_shape = (jax.ShapeDtypeStruct((some, CORES * features), bf16),)
             x_specs = tuple(in_vmem(1))
         else:
             x_shape = (jax.ShapeDtypeStruct((some, features), bf16),) * 2
-            x_specs = (pl.BlockSpec((rows, features), lambda i: (i, 0)),) * 2
+            x_specs = tuple(anywhere(2))
         *x, squares = pl.pallas_call(
-            prepare_kernel,
-            grid=(some // rows,),
+            functools.partial(prepare_kernel, half * some),
             out_shape=x_shape
             + (jax.ShapeDtypeStruct(((half + 1) * some // LANES, LANES), f32),),
-            in_specs=[token_block, token_block, gain_block, gain_block] + in_vmem(len(before)),
+            in_specs=anywhere(2) + in_vmem(2 + len(before)),
             out_specs=x_specs + tuple(in_vmem(1)),
-            scratch_shapes=[pltpu.VMEM((some, LANES), f32)],
+            scratch_shapes=[
+                pltpu.VMEM((some, features), bf16),
+                pltpu.VMEM((some, features), bf16),
+                pltpu.VMEM((some, LANES), f32),
+                pltpu.SemaphoreType.DMA((4 * pl.cdiv(some, LANES),)),
+            ],
             compiler_params=pltpu.CompilerParams(vmem_limit_bytes=limit),
         )(*operands, *before)
         return x, squares
@@ -580,8 +615,12 @@
             weights, product = pl.pallas_call(
                 functools.partial(outside_kernel, static, chips, step, turn),
                 out_shape=(weights_shape, product_shape),
-                in_specs=in_vmem(2 + 2 * FACTOR_PIECES + len(blocks)) + anywhere(len(after)),
+                in_specs=in_vmem(2 + 2 * FACTOR_PIECES) + anywhere(len(blocks) + len(after)),
                 out_specs=tuple(in_vmem(2)),
+                scratch_shapes=[
+                    pltpu.VMEM((len(blocks), features, LANES), bf16),
+                    pltpu.SemaphoreType.DMA((len(blocks),)),
+                ],
                 compiler_params=params(),
             )(messages[step - 1], *x0, *pieces, *sibling_f, *blocks, *after)
             received.setdefault((0, half), []).append(to_chip(product, chips - step))

time: 84.8 us -> 84.1 us (level)
  local copies, waits for them, and re-layouts: 8.03 us -> 1.31 us
  waiting for transfers between devices: 13.9 us -> 20.1 us
  starting transfers between devices: 27.7 us -> 24.9 us
  Pallas kernels: 33.7 us -> 36.3 us
    unnamed x26 -> x20, local copies, waits for them, and re-layouts: 8.03 us -> 1.31 us
    all_to_all x1, waiting for transfers between devices: 0.09 us -> 5.42 us  [body(): exchanged = lax.all_to_all(packed, 'dp', 0, 0, tiled=True)]
    all_to_all x1, starting transfers between devices: 5.92 us -> 4.11 us  [body(): own_f = lax.all_to_all(sent, 'dp', 0, 0, tiled=True)]
    ppermute x7, waiting for transfers between devices: 10.9 us -> 12.7 us  [to_chip(): return lax.ppermute(value, 'tensor', pairs)]
    ppermute x7, starting transfers between devices: 8.57 us -> 7.18 us  [to_chip(): return lax.ppermute(value, 'tensor', pairs)]
    pallas_call x2, Pallas kernels: 4.99 us -> 6.35 us  [body(): pl.pallas_call(functools.partial(outside_kernel, static, chips, step, tur...]
    pallas_call x2, Pallas kernels: 8.47 us -> 9.71 us  [prepared(): pl.pallas_call(functools.partial(prepare_kernel, half * some), out_shape=...]
  transfers between devices with their start and end apart: 17 -> 17, of which waited for: 11 -> 8; matrix products, arithmetic and copies ran while one was open for 0% -> 0% of each run, Pallas kernels for 39% -> 42%
where the time goes in v15:
time: 84.1 us; the launch traced here: 83.5 us
  Pallas kernels  36.3 us (43%)
  starting transfers between devices  24.9 us (30%)
  waiting for transfers between devices  20.1 us (24%)
  local copies, waits for them, and re-layouts  1.31 us (2%)
  between operations  0.87 us (1%)
    ppermute x7, waiting for transfers between devices, to_chip(): return lax.ppermute(value, 'tensor', pairs)  12.7 us
    pallas_call x2, Pallas kernels, prepared(): pl.pallas_call(functools.partial(prepare_kernel, half * some), out_shape=...  9.71 us
    ppermute x7, starting transfers between devices, to_chip(): return lax.ppermute(value, 'tensor', pairs)  7.18 us
    all_to_all x1, starting transfers between devices, body(): exchanged = lax.all_to_all(packed, 'dp', 0, 0, tiled=True)  6.86 us
    pallas_call x2, Pallas kernels, body(): pl.pallas_call(functools.partial(outside_kernel, static, chips, step, tur...  6.35 us
    ppermute x4, starting transfers between devices, swap_half(): outside[strip].append((piece, lax.ppermute(piece, 'dp', pairs)))  5.61 us
    all_to_all x1, waiting for transfers between devices, body(): exchanged = lax.all_to_all(packed, 'dp', 0, 0, tiled=True)  5.42 us
    pallas_call x1, Pallas kernels, body(): pl.pallas_call(functools.partial(own_kernel, static), out_shape=(jax.Shap...  4.87 us
  transfers between devices with their start and end apart: 17, of which 8 were waited for; matrix products, arithmetic and copies ran while one was open for 0% of the time, Pallas kernels for 42%

profile of v15, /device:TPU:0, one launch (start us, length us, event | category | flops | bytes accessed | tf_op | source)
XLA Modules:
  0.0 83.5 jit_solution(12366202595011182252)
XLA Ops:
  0.6 0.5 collective-permute-start
  1.2 2.5 %shard_map.130 = (bf16[8,192,128]{2,1,0:T(8,128)(2,1)}, bf16[2,1280,128]{2,1,0:T(8,128)(2,1)}, bf16[2,1280,128]{2,1,0:T(8,128)(2,1)}) custom-call(f32[128,1280]{1,0:T(8,128)} %bitcast.20, f32[64,512]{1,0:T(8,128)} %bitcast.24, bf16[5120,512]{1,0:T(8,128)(2,1)} %sibling_block.1), custom_call_target="tpu_custom_call" | custom-call | tf_op jit(solution)/shard_map/pallas_call | solution.py:476
  3.7 6.9 %all-to-all-start = ((bf16[8,192,128]{2,1,0:T(8,128)(2,1)}), bf16[8,192,128]{2,1,0:T(8,128)(2,1)}, u32[]{:S(2)}, u32[]{:S(2)}) async-start(bf16[8,192,128]{2,1,0:T(8,128)(2,1)} %get-tuple-element.34), calls=%async_computation | async-start | bytes 786432 | tf_op jit(solution)/shard_map/all_to_all | solution.py:491
  10.6 1.5 %collective-permute-start.5 = (bf16[2,1280,128]{2,1,0:T(8,128)(2,1)}, bf16[2,1280,128]{2,1,0:T(8,128)(2,1)}, u32[]{:S(2)}, u32[]{:S(2)}) collective-permute-start(bf16[2,1280,128]{2,1,0:T(8,128)(2,1)} %get-tuple-element.51), channel_id=1, source_target_pairs={{0,2},{1,3},{2,0},{3,1},{4,6},{5,7},{6,4},{7,5},{8,10},{9,11},{10,... | collective-permute-start | bytes 1966088 | tf_op jit(solution)/shard_map/ppermute | solution.py:453
  12.0 0.0 copy-done.7
  12.1 0.1 collective-permute-start.1
  12.1 1.2 %collective-permute-done.1.sibling_gain = f32[1,1280]{1,0:T(1,128)S(1)} collective-permute-done((f32[1,1280]{1,0:T(1,128)S(1)}, f32[1,1280]{1,0:T(1,128)S(1)}, u32[]{:S(2)}, u32[]{:S(2)}) %collective-permute-start.1) | collective-permute-done | bytes 5152 | tf_op jit(solution)/shard_map/ppermute | solution.py:445
  13.3 0.0 collective-permute-done.sibling_in
  13.3 3.7 %shard_map.131 = (bf16[640,2560]{1,0:T(8,128)(2,1)S(1)}, f32[5,128]{1,0:T(8,128)S(1)}) custom-call(bf16[1280,1280]{1,0:T(8,128)(2,1)} %own_in.3, bf16[1280,1280]{1,0:T(8,128)(2,1)} %collective-permute-done.sibling_in, f32[1,1280]{1,0:T(1,128)S(1)} %broadcast_in_dim.3.own_gain, f32[1,1280]{1,0:T(1,128)S(1)} %collective-permute-done.1.sibling_gain), custom_call_target="tpu_custom_call" | custom-call | tf_op jit(solution)/shard_map/pallas_call | solution.py:518
  17.0 0.0 copy-done.2
  17.0 0.0 copy-done.5
  17.0 0.0 copy-start.6
  17.0 0.6 copy-done.6
  17.6 5.4 %all-to-all-done.grad_in = bf16[8,192,128]{2,1,0:T(8,128)(2,1)} async-done(((bf16[8,192,128]{2,1,0:T(8,128)(2,1)}), bf16[8,192,128]{2,1,0:T(8,128)(2,1)}, u32[]{:S(2)}, u32[]{:S(2)}) %all-to-all-start) | async-done | bytes 393248 | tf_op jit(solution)/shard_map/all_to_all | solution.py:491
  23.0 2.6 %shard_map.132 = (f32[3,128,160]{2,1,0:T(8,128)}, f32[3,8,512]{2,1,0:T(8,128)}, bf16[8,192,128]{2,1,0:T(8,128)(2,1)}) custom-call(bf16[8,192,128]{2,1,0:T(8,128)(2,1)} %all-to-all-done.grad_in, f32[128,1280]{1,0:T(8,128)} %bitcast.21, f32[128,1280]{1,0:T(8,128)} %bitcast.22, f32[128,1280]{1,0:T(8,128)} %bitcast.23, f32[64,512]{1,0:T(8,128)} %refs_3_.1, ...), custom_call_target="tpu_custom_call" | custom-call | tf_op jit(solution)/shard_map/pallas_call | solution.py:537
  25.6 4.1 %all-to-all-start.1 = ((bf16[8,192,128]{2,1,0:T(8,128)(2,1)}), bf16[8,192,128]{2,1,0:T(8,128)(2,1)}, u32[]{:S(2)}, u32[]{:S(2)}) async-start(bf16[8,192,128]{2,1,0:T(8,128)(2,1)} %get-tuple-element.39), calls=%async_computation.1 | async-start | bytes 786432 | tf_op jit(solution)/shard_map/all_to_all | solution.py:554
  29.7 0.0 collective-permute-done.5.in_ref
  29.7 1.6 %collective-permute-start.6 = (bf16[2,1280,128]{2,1,0:T(8,128)(2,1)}, bf16[2,1280,128]{2,1,0:T(8,128)(2,1)}, u32[]{:S(2)}, u32[]{:S(2)}) collective-permute-start(bf16[2,1280,128]{2,1,0:T(8,128)(2,1)} %get-tuple-element.52), channel_id=1, source_target_pairs={{0,2},{1,3},{2,0},{3,1},{4,6},{5,7},{6,4},{7,5},{8,10},{9,11},{10,... | collective-permute-start | bytes 1966088 | tf_op jit(solution)/shard_map/ppermute | solution.py:453
  31.2 2.0 %shard_map.135 = (bf16[1280,128]{1,0:T(8,128)(2,1)}, bf16[1280,128]{1,0:T(8,128)(2,1)}) custom-call(bf16[2,1280,128]{2,1,0:T(8,128)(2,1)} %collective-permute-done.5.in_ref), custom_call_target="tpu_custom_call" | custom-call | tf_op jit(solution)/shard_map/pallas_call | solution.py:564
  33.2 1.8 %collective-permute-start.7 = (bf16[1280,128]{1,0:T(8,128)(2,1)}, bf16[1280,128]{1,0:T(8,128)(2,1)}, u32[]{:S(2)}, u32[]{:S(2)}) collective-permute-start(bf16[1280,128]{1,0:T(8,128)(2,1)} %get-tuple-element.54.refs_4_), channel_id=1, source_target_pairs={{0,4},{4,0},{8,12},{12,8},{16,20},{20,16},{24,28},{28,24},{1,5},{5... | collective-permute-start | bytes 983048 | tf_op jit(solution)/shard_map/ppermute | solution.py:573
  35.0 1.5 %collective-permute-start.8 = (bf16[1280,128]{1,0:T(8,128)(2,1)}, bf16[1280,128]{1,0:T(8,128)(2,1)}, u32[]{:S(2)}, u32[]{:S(2)}) collective-permute-start(bf16[1280,128]{1,0:T(8,128)(2,1)} %get-tuple-element.55.refs_6_), channel_id=1, source_target_pairs={{0,8},{4,12},{8,0},{12,4},{16,24},{20,28},{24,16},{28,20},{1,9},{5... | collective-permute-start | bytes 983048 | tf_op jit(solution)/shard_map/ppermute | solution.py:573
  36.5 6.1 %shard_map.133 = (bf16[640,1280]{1,0:T(8,128)(2,1)}, bf16[640,1280]{1,0:T(8,128)(2,1)}, f32[10,128]{1,0:T(8,128)}) custom-call(bf16[1280,1280]{1,0:T(8,128)(2,1)} %own_in.3, bf16[1280,1280]{1,0:T(8,128)(2,1)} %collective-permute-done.sibling_in, f32[1,1280]{1,0:T(1,128)} %copy-done.2, f32[1,1280]{1,0:T(1,128)} %copy-done.5, f32[5,128]{1,0:T(8,128)} %copy-done.6), custom_call_target="tpu_custom_call" | custom-call | tf_op jit(solution)/shard_map/pallas_call | solution.py:518
  42.6 0.0 all-to-all-done.1.factor_ref
  42.6 0.0 copy-start.3
  42.6 0.7 copy-done.3
  43.3 1.1 %shard_map.134 = (bf16[9,32,128]{2,1,0:T(8,128)(2,1)S(1)}, bf16[4,192,128]{2,1,0:T(8,128)(2,1)S(1)}, bf16[4,192,128]{2,1,0:T(8,128)(2,1)S(1)}) custom-call(bf16[8,192,128]{2,1,0:T(8,128)(2,1)} %all-to-all-done.1.factor_ref, f32[10,128]{1,0:T(8,128)S(1)} %copy-done.3), custom_call_target="tpu_custom_call" | custom-call | tf_op jit(solution)/shard_map/pallas_call | solution.py:580
  44.4 0.1 collective-permute-start.2
  44.5 0.5 collective-permute-start.3
  45.0 0.0 collective-permute-done.7.refs_5_
  45.0 0.5 collective-permute-start.4
  45.5 0.2 collective-permute-done.8.refs_7_
  45.7 3.6 %collective-permute-done.4.b_ref.refs_0_ = bf16[9,32,128]{2,1,0:T(8,128)(2,1)S(1)} collective-permute-done((bf16[9,32,128]{2,1,0:T(8,128)(2,1)S(1)}, bf16[9,32,128]{2,1,0:T(8,128)(2,1)S(1)}, u32[]{:S(2)}, u32[]{:S(2)}) %collective-permute-start.4) | collective-permute-done | bytes 73760 | tf_op jit(solution)/shard_map/ppermute | solution.py:453
  49.3 0.0 collective-permute-done.2.refs_2_
  49.3 0.0 collective-permute-done.3.refs_3_
  49.3 0.0 copy-start.1
  49.3 3.6 %shard_map.136 = (bf16[2560,256]{1,0:T(8,128)(2,1)S(1)}, bf16[640,256]{1,0:T(8,128)(2,1)S(1)}) custom-call(bf16[9,32,128]{2,1,0:T(8,128)(2,1)S(1)} %collective-permute-done.4.b_ref.refs_0_, bf16[640,2560]{1,0:T(8,128)(2,1)S(1)} %get-tuple-element.46.x.refs_4_, bf16[4,192,128]{2,1,0:T(8,128)(2,1)S(1)} %get-tuple-element.44.refs_0_, ...), custom_call_target="tpu_custom_call" | custom-call | tf_op jit(solution)/shard_map/pallas_call | solution.py:615
  53.0 0.6 collective-permute-start.11
  53.6 0.0 collective-permute-done.6.in_ref
  53.6 1.1 %shard_map.137 = (bf16[1280,128]{1,0:T(8,128)(2,1)S(1)}, bf16[1280,128]{1,0:T(8,128)(2,1)S(1)}) custom-call(bf16[2,1280,128]{2,1,0:T(8,128)(2,1)} %collective-permute-done.6.in_ref), custom_call_target="tpu_custom_call" | custom-call | tf_op jit(solution)/shard_map/pallas_call | solution.py:564
  54.7 0.8 %collective-permute-start.9 = (bf16[1280,128]{1,0:T(8,128)(2,1)S(1)}, bf16[1280,128]{1,0:T(8,128)(2,1)S(1)}, u32[]{:S(2)}, u32[]{:S(2)}) collective-permute-start(bf16[1280,128]{1,0:T(8,128)(2,1)S(1)} %get-tuple-element.58.refs_4_), channel_id=1, source_target_pairs={{0,4},{4,0},{8,12},{12,8},{16,20},{20,16},{24,28},{28,24},{1,5},{5... | collective-permute-start | bytes 983048 | tf_op jit(solution)/shard_map/ppermute | solution.py:573
  55.6 1.5 %collective-permute-start.10 = (bf16[1280,128]{1,0:T(8,128)(2,1)S(1)}, bf16[1280,128]{1,0:T(8,128)(2,1)S(1)}, u32[]{:S(2)}, u32[]{:S(2)}) collective-permute-start(bf16[1280,128]{1,0:T(8,128)(2,1)S(1)} %get-tuple-element.59.refs_6_), channel_id=1, source_target_pairs={{0,8},{4,12},{8,0},{12,4},{16,24},{20,28},{24,16},{28,20},{1,9},{5... | collective-permute-start | bytes 983048 | tf_op jit(solution)/shard_map/ppermute | solution.py:573
  57.0 0.0 copy-done
  57.0 0.0 copy-done.1
  57.0 1.2 %shard_map.140 = bf16[640,256]{1,0:T(8,128)(2,1)S(1)} custom-call(bf16[640,1280]{1,0:T(8,128)(2,1)S(1)} %copy-done, bf16[640,1280]{1,0:T(8,128)(2,1)S(1)} %copy-done.1, bf16[2560,256]{1,0:T(8,128)(2,1)S(1)} %get-tuple-element.61.refs_2_), custom_call_target="tpu_custom_call" | custom-call | tf_op jit(solution)/shard_map/pallas_call | solution.py:627
  58.2 0.0 slice-start.1
  58.2 0.8 collective-permute-start.12
  59.1 4.4 %collective-permute-done.11.refs_8_.refs_0_ = bf16[640,256]{1,0:T(8,128)(2,1)S(1)} collective-permute-done((bf16[640,256]{1,0:T(8,128)(2,1)S(1)}, bf16[640,256]{1,0:T(8,128)(2,1)S(1)}, u32[]{:S(2)}, u32[]{:S(2)}) %collective-permute-start.11) | collective-permute-done | bytes 327712 | tf_op jit(solution)/shard_map/ppermute | solution.py:453
  63.5 0.0 collective-permute-done.9.refs_5_
  63.5 0.6 collective-permute-done.10.refs_7_
  64.1 2.7 %shard_map.138 = (bf16[2560,256]{1,0:T(8,128)(2,1)S(1)}, bf16[640,256]{1,0:T(8,128)(2,1)S(1)}) custom-call(bf16[9,32,128]{2,1,0:T(8,128)(2,1)S(1)} %collective-permute-done.4.b_ref.refs_0_, bf16[640,2560]{1,0:T(8,128)(2,1)S(1)} %get-tuple-element.46.x.refs_4_, bf16[4,192,128]{2,1,0:T(8,128)(2,1)S(1)} %get-tuple-element.44.refs_0_, ...), custom_call_target="tpu_custom_call" | custom-call | tf_op jit(solution)/shard_map/pallas_call | solution.py:615
  66.9 0.8 collective-permute-start.14
  67.6 1.2 %shard_map.139.refs_7_ = bf16[640,256]{1,0:T(8,128)(2,1)S(1)} custom-call(bf16[640,1280]{1,0:T(8,128)(2,1)S(1)} %copy-done, bf16[640,1280]{1,0:T(8,128)(2,1)S(1)} %copy-done.1, bf16[2560,256]{1,0:T(8,128)(2,1)S(1)} %get-tuple-element.60.refs_2_), custom_call_target="tpu_custom_call" | custom-call | tf_op jit(solution)/shard_map/pallas_call | solution.py:627
  68.8 1.4 %collective-permute-start.13 = (bf16[640,256]{1,0:T(8,128)(2,1)S(1)}, bf16[640,256]{1,0:T(8,128)(2,1)S(1)}, u32[]{:S(2)}, u32[]{:S(2)}) collective-permute-start(bf16[640,256]{1,0:T(8,128)(2,1)S(1)} %shard_map.139.refs_7_), channel_id=1, source_target_pairs={{0,2},{1,3},{2,0},{3,1},{4,6},{5,7},{6,4},{7,5},{8,10},{9,11},{10,... | collective-permute-start | bytes 983048 | tf_op jit(solution)/shard_map/ppermute | solution.py:453
  70.2 0.0 copy-done.4
  70.2 0.2 shard_map.142.inv
  70.4 0.0 collective-permute-done.12.refs_8_.refs_0_
  70.5 0.0 slice-done
  70.5 4.9 %shard_map.141 = (f32[1280,256]{1,0:T(8,128)S(1)}, f32[1280,256]{1,0:T(8,128)S(1)}) custom-call(bf16[5120,512]{1,0:T(8,128)(2,1)S(1)} %bitcast.19, bf16[5120,512]{1,0:T(8,128)(2,1)S(1)} %bitcast.19, bf16[4,192,128]{2,1,0:T(8,128)(2,1)S(1)} %get-tuple-element.44.refs_0_, bf16[4,192,128]{2,1,0:T(8,128)(2,1)S(1)} %get-tuple-element.45.refs_1_, ...), custom_call_target="tpu_custom_call" | custom-call | flops 3355443200 | bytes 6553600 | tf_op jit(solution)/shard_map/pallas_call | solution.py:642
  75.4 0.9 %shard_map.143.refs_1_ = bf16[1280,512]{1,0:T(8,128)(2,1)} custom-call(f32[1280,256]{1,0:T(8,128)S(1)} %get-tuple-element.64.own, f32[1280,128]{1,0:T(8,128)S(1)} %shard_map.142.inv, bf16[640,256]{1,0:T(8,128)(2,1)S(1)} %collective-permute-done.11.refs_8_.refs_0_), custom_call_target="tpu_custom_call" | custom-call | tf_op jit(solution)/shard_map/pallas_call | solution.py:404
  76.2 0.9 %shard_map.144.refs_1_ = bf16[1280,512]{1,0:T(8,128)(2,1)} custom-call(f32[1280,256]{1,0:T(8,128)S(1)} %get-tuple-element.64.own, f32[1280,128]{1,0:T(8,128)S(1)} %shard_map.142.inv, bf16[640,256]{1,0:T(8,128)(2,1)S(1)} %collective-permute-done.12.refs_8_.refs_0_, bf16[1280,512]{1,0:T(8,128)(2,1)} %shard_map.143.refs_1_), custom_call_target="tpu_custom_call", output_to_operand_aliasing={{}: (3, {})} | custom-call | tf_op jit(solution)/shard_map/pallas_call | solution.py:404
  77.1 0.4 collective-permute-done.14.refs_0_
  77.6 0.9 %shard_map.145.refs_1_ = bf16[1280,512]{1,0:T(8,128)(2,1)} custom-call(f32[1280,256]{1,0:T(8,128)S(1)} %get-tuple-element.62.own, f32[1280,128]{1,0:T(8,128)S(1)} %shard_map.142.inv, bf16[640,256]{1,0:T(8,128)(2,1)S(1)} %collective-permute-done.14.refs_0_, bf16[1280,512]{1,0:T(8,128)(2,1)} %shard_map.144.refs_1_), custom_call_target="tpu_custom_call", output_to_operand_aliasing={{}: (3, {})} | custom-call | tf_op jit(solution)/shard_map/pallas_call | solution.py:404
  78.4 4.2 %collective-permute-done.13.refs_0_ = bf16[640,256]{1,0:T(8,128)(2,1)S(1)} collective-permute-done((bf16[640,256]{1,0:T(8,128)(2,1)S(1)}, bf16[640,256]{1,0:T(8,128)(2,1)S(1)}, u32[]{:S(2)}, u32[]{:S(2)}) %collective-permute-start.13) | collective-permute-done | bytes 327712 | tf_op jit(solution)/shard_map/ppermute | solution.py:453
  82.7 0.9 %shard_map.146 = bf16[1280,512]{1,0:T(8,128)(2,1)} custom-call(f32[1280,256]{1,0:T(8,128)S(1)} %get-tuple-element.62.own, f32[1280,128]{1,0:T(8,128)S(1)} %shard_map.142.inv, bf16[640,256]{1,0:T(8,128)(2,1)S(1)} %collective-permute-done.13.refs_0_, bf16[1280,512]{1,0:T(8,128)(2,1)} %shard_map.145.refs_1_), custom_call_target="tpu_custom_call", output_to_operand_aliasing={{}: (3, {})} | custom-call | tf_op jit(solution)/shard_map/pallas_call | solution.py:404
  (9 shorter events, 0.0 us)
Async XLA Ops:
  0.6 12.7 %collective-permute-start = (bf16[1280,1280]{1,0:T(8,128)(2,1)}, bf16[1280,1280]{1,0:T(8,128)(2,1)}, u32[]{:S(2)}, u32[]{:S(2)}) collective-permute-start(bf16[1280,1280]{1,0:T(8,128)(2,1)} %own_in.3), channel_id=1, source_target_pairs={{0,1},{1,0},{2,3},{3,2},{4,5},{5,4},{6,7},{7,6},{8,9},{9,8},{10,11... | collective-permute-start | bytes 9830408 | tf_op jit(solution)/shard_map/ppermute | solution.py:445
  1.1 10.9 %copy-start.7 = (f32[1280]{0:T(1024)S(1)}, f32[1280]{0:T(1024)}, u32[]{:S(2)}) copy-start(f32[1280]{0:T(1024)} %param.12) | copy-start | bytes 15364
  3.7 19.3 %all-to-all-start = ((bf16[8,192,128]{2,1,0:T(8,128)(2,1)}), bf16[8,192,128]{2,1,0:T(8,128)(2,1)}, u32[]{:S(2)}, u32[]{:S(2)}) async-start(bf16[8,192,128]{2,1,0:T(8,128)(2,1)} %get-tuple-element.34), calls=%async_computation | async-start | bytes 786432 | tf_op jit(solution)/shard_map/all_to_all | solution.py:491
  10.6 19.1 %collective-permute-start.5 = (bf16[2,1280,128]{2,1,0:T(8,128)(2,1)}, bf16[2,1280,128]{2,1,0:T(8,128)(2,1)}, u32[]{:S(2)}, u32[]{:S(2)}) collective-permute-start(bf16[2,1280,128]{2,1,0:T(8,128)(2,1)} %get-tuple-element.51), channel_id=1, source_target_pairs={{0,2},{1,3},{2,0},{3,1},{4,6},{5,7},{6,4},{7,5},{8,10},{9,11},{10,... | collective-permute-start | bytes 1966088 | tf_op jit(solution)/shard_map/ppermute | solution.py:453
  12.1 4.9 %copy-start.2 = (f32[1,1280]{1,0:T(1,128)}, f32[1,1280]{1,0:T(1,128)S(1)}, u32[]{:S(2)}) copy-start(f32[1,1280]{1,0:T(1,128)S(1)} %broadcast_in_dim.3.own_gain) | copy-start | bytes 15364
  12.1 1.2 %collective-permute-start.1 = (f32[1,1280]{1,0:T(1,128)S(1)}, f32[1,1280]{1,0:T(1,128)S(1)}, u32[]{:S(2)}, u32[]{:S(2)}) collective-permute-start(f32[1,1280]{1,0:T(1,128)S(1)} %broadcast_in_dim.3.own_gain), channel_id=1, source_target_pairs={{0,1},{1,0},{2,3},{3,2},{4,5},{5,4},{6,7},{7,6},{8,9},{9,8},{10,11... | collective-permute-start | bytes 15368 | tf_op jit(solution)/shard_map/ppermute | solution.py:445
  13.3 3.7 %copy-start.5 = (f32[1,1280]{1,0:T(1,128)}, f32[1,1280]{1,0:T(1,128)S(1)}, u32[]{:S(2)}) copy-start(f32[1,1280]{1,0:T(1,128)S(1)} %collective-permute-done.1.sibling_gain) | copy-start | bytes 15364
  17.0 0.6 copy-start.6
  25.6 17.0 %all-to-all-start.1 = ((bf16[8,192,128]{2,1,0:T(8,128)(2,1)}), bf16[8,192,128]{2,1,0:T(8,128)(2,1)}, u32[]{:S(2)}, u32[]{:S(2)}) async-start(bf16[8,192,128]{2,1,0:T(8,128)(2,1)} %get-tuple-element.39), calls=%async_computation.1 | async-start | bytes 786432 | tf_op jit(solution)/shard_map/all_to_all | solution.py:554
  29.7 23.9 %collective-permute-start.6 = (bf16[2,1280,128]{2,1,0:T(8,128)(2,1)}, bf16[2,1280,128]{2,1,0:T(8,128)(2,1)}, u32[]{:S(2)}, u32[]{:S(2)}) collective-permute-start(bf16[2,1280,128]{2,1,0:T(8,128)(2,1)} %get-tuple-element.52), channel_id=1, source_target_pairs={{0,2},{1,3},{2,0},{3,1},{4,6},{5,7},{6,4},{7,5},{8,10},{9,11},{10,... | collective-permute-start | bytes 1966088 | tf_op jit(solution)/shard_map/ppermute | solution.py:453
  33.2 11.8 %collective-permute-start.7 = (bf16[1280,128]{1,0:T(8,128)(2,1)}, bf16[1280,128]{1,0:T(8,128)(2,1)}, u32[]{:S(2)}, u32[]{:S(2)}) collective-permute-start(bf16[1280,128]{1,0:T(8,128)(2,1)} %get-tuple-element.54.refs_4_), channel_id=1, source_target_pairs={{0,4},{4,0},{8,12},{12,8},{16,20},{20,16},{24,28},{28,24},{1,5},{5... | collective-permute-start | bytes 983048 | tf_op jit(solution)/shard_map/ppermute | solution.py:573
  35.0 10.7 %collective-permute-start.8 = (bf16[1280,128]{1,0:T(8,128)(2,1)}, bf16[1280,128]{1,0:T(8,128)(2,1)}, u32[]{:S(2)}, u32[]{:S(2)}) collective-permute-start(bf16[1280,128]{1,0:T(8,128)(2,1)} %get-tuple-element.55.refs_6_), channel_id=1, source_target_pairs={{0,8},{4,12},{8,0},{12,4},{16,24},{20,28},{24,16},{28,20},{1,9},{5... | collective-permute-start | bytes 983048 | tf_op jit(solution)/shard_map/ppermute | solution.py:573
  42.6 0.7 copy-start.3
  44.4 4.9 %collective-permute-start.2 = (bf16[4,192,128]{2,1,0:T(8,128)(2,1)S(1)}, bf16[4,192,128]{2,1,0:T(8,128)(2,1)S(1)}, u32[]{:S(2)}, u32[]{:S(2)}) collective-permute-start(bf16[4,192,128]{2,1,0:T(8,128)(2,1)S(1)} %get-tuple-element.44.refs_0_), channel_id=1, source_target_pairs={{0,1},{1,0},{2,3},{3,2},{4,5},{5,4},{6,7},{7,6},{8,9},{9,8},{10,11... | collective-permute-start | bytes 589832 | tf_op jit(solution)/shard_map/ppermute | solution.py:445
  44.5 4.9 %collective-permute-start.3 = (bf16[4,192,128]{2,1,0:T(8,128)(2,1)S(1)}, bf16[4,192,128]{2,1,0:T(8,128)(2,1)S(1)}, u32[]{:S(2)}, u32[]{:S(2)}) collective-permute-start(bf16[4,192,128]{2,1,0:T(8,128)(2,1)S(1)} %get-tuple-element.45.refs_1_), channel_id=1, source_target_pairs={{0,1},{1,0},{2,3},{3,2},{4,5},{5,4},{6,7},{7,6},{8,9},{9,8},{10,11... | collective-permute-start | bytes 589832 | tf_op jit(solution)/shard_map/ppermute | solution.py:445
  45.0 4.4 %collective-permute-start.4 = (bf16[9,32,128]{2,1,0:T(8,128)(2,1)S(1)}, bf16[9,32,128]{2,1,0:T(8,128)(2,1)S(1)}, u32[]{:S(2)}, u32[]{:S(2)}) collective-permute-start(bf16[9,32,128]{2,1,0:T(8,128)(2,1)S(1)} %get-tuple-element.49), channel_id=1, source_target_pairs={{0,2},{1,3},{2,0},{3,1},{4,6},{5,7},{6,4},{7,5},{8,10},{9,11},{10,... | collective-permute-start | bytes 221192 | tf_op jit(solution)/shard_map/ppermute | solution.py:453
  49.3 7.7 %copy-start = (bf16[640,1280]{1,0:T(8,128)(2,1)S(1)}, bf16[640,1280]{1,0:T(8,128)(2,1)}, u32[]{:S(2)}) copy-start(bf16[640,1280]{1,0:T(8,128)(2,1)} %get-tuple-element.47.refs_0_.refs_5_) | copy-start | bytes 4915204
  49.3 7.7 %copy-start.1 = (bf16[640,1280]{1,0:T(8,128)(2,1)S(1)}, bf16[640,1280]{1,0:T(8,128)(2,1)}, u32[]{:S(2)}) copy-start(bf16[640,1280]{1,0:T(8,128)(2,1)} %get-tuple-element.48.refs_1_.refs_6_) | copy-start | bytes 4915204
  53.0 10.5 %collective-permute-start.11 = (bf16[640,256]{1,0:T(8,128)(2,1)S(1)}, bf16[640,256]{1,0:T(8,128)(2,1)S(1)}, u32[]{:S(2)}, u32[]{:S(2)}) collective-permute-start(bf16[640,256]{1,0:T(8,128)(2,1)S(1)} %get-tuple-element.56), channel_id=1, source_target_pairs={{0,2},{1,3},{2,0},{3,1},{4,6},{5,7},{6,4},{7,5},{8,10},{9,11},{10,... | collective-permute-start | bytes 983048 | tf_op jit(solution)/shard_map/ppermute | solution.py:453
  54.7 8.8 %collective-permute-start.9 = (bf16[1280,128]{1,0:T(8,128)(2,1)S(1)}, bf16[1280,128]{1,0:T(8,128)(2,1)S(1)}, u32[]{:S(2)}, u32[]{:S(2)}) collective-permute-start(bf16[1280,128]{1,0:T(8,128)(2,1)S(1)} %get-tuple-element.58.refs_4_), channel_id=1, source_target_pairs={{0,4},{4,0},{8,12},{12,8},{16,20},{20,16},{24,28},{28,24},{1,5},{5... | collective-permute-start | bytes 983048 | tf_op jit(solution)/shard_map/ppermute | solution.py:573
  55.6 8.6 %collective-permute-start.10 = (bf16[1280,128]{1,0:T(8,128)(2,1)S(1)}, bf16[1280,128]{1,0:T(8,128)(2,1)S(1)}, u32[]{:S(2)}, u32[]{:S(2)}) collective-permute-start(bf16[1280,128]{1,0:T(8,128)(2,1)S(1)} %get-tuple-element.59.refs_6_), channel_id=1, source_target_pairs={{0,8},{4,12},{8,0},{12,4},{16,24},{20,28},{24,16},{28,20},{1,9},{5... | collective-permute-start | bytes 983048 | tf_op jit(solution)/shard_map/ppermute | solution.py:573
  57.0 13.4 %slice-start = ((s8[5242880]{0:T(1024)(128)(4,1)}), s8[4194304]{0:T(1024)(128)(4,1)S(1)}, s32[]{:S(2)}) async-start(s8[5242880]{0:T(1024)(128)(4,1)} %bitcast.18), calls=%async_computation.2 | async-start | bytes 8388608
  58.2 12.2 %slice-start.1 = ((s8[5242880]{0:T(1024)(128)(4,1)}), s8[1048576]{0:T(1024)(128)(4,1)S(1)}, s32[]{:S(2)}) async-start(s8[5242880]{0:T(1024)(128)(4,1)} %bitcast.18), calls=%async_computation.3 | async-start | bytes 2097152
  58.2 12.2 %collective-permute-start.12 = (bf16[640,256]{1,0:T(8,128)(2,1)S(1)}, bf16[640,256]{1,0:T(8,128)(2,1)S(1)}, u32[]{:S(2)}, u32[]{:S(2)}) collective-permute-start(bf16[640,256]{1,0:T(8,128)(2,1)S(1)} %shard_map.140), channel_id=1, source_target_pairs={{0,2},{1,3},{2,0},{3,1},{4,6},{5,7},{6,4},{7,5},{8,10},{9,11},{10,... | collective-permute-start | bytes 983048 | tf_op jit(solution)/shard_map/ppermute | solution.py:453
  66.9 10.7 %collective-permute-start.14 = (bf16[640,256]{1,0:T(8,128)(2,1)S(1)}, bf16[640,256]{1,0:T(8,128)(2,1)S(1)}, u32[]{:S(2)}, u32[]{:S(2)}) collective-permute-start(bf16[640,256]{1,0:T(8,128)(2,1)S(1)} %get-tuple-element.63), channel_id=1, source_target_pairs={{0,2},{1,3},{2,0},{3,1},{4,6},{5,7},{6,4},{7,5},{8,10},{9,11},{10,... | collective-permute-start | bytes 983048 | tf_op jit(solution)/shard_map/ppermute | solution.py:453
  67.6 2.6 %copy-start.4 = (f32[10,128]{1,0:T(8,128)S(1)}, f32[10,128]{1,0:T(8,128)}, u32[]{:S(2)}) copy-start(f32[10,128]{1,0:T(8,128)} %get-tuple-element.43.sums_ref) | copy-start | bytes 15364
  68.8 13.9 %collective-permute-start.13 = (bf16[640,256]{1,0:T(8,128)(2,1)S(1)}, bf16[640,256]{1,0:T(8,128)(2,1)S(1)}, u32[]{:S(2)}, u32[]{:S(2)}) collective-permute-start(bf16[640,256]{1,0:T(8,128)(2,1)S(1)} %shard_map.139.refs_7_), channel_id=1, source_target_pairs={{0,2},{1,3},{2,0},{3,1},{4,6},{5,7},{6,4},{7,5},{8,10},{9,11},{10,... | collective-permute-start | bytes 983048 | tf_op jit(solution)/shard_map/ppermute | solution.py:453

commit v16 on v15

--- a/solution.py
+++ b/solution.py
@@ -322,34 +322,23 @@
 
 def outside_kernel(static, chips, step, turn, b_ref, x, *refs):
     own_f, sibling_f = refs[:FACTOR_PIECES], refs[FACTOR_PIECES : 2 * FACTOR_PIECES]
-    weights, product, blocks, sem = refs[-4:]
+    blocks, (weights, product) = refs[2 * FACTOR_PIECES :], refs[-2:]
     strips = static[3]
-    copies = [
-        pltpu.make_async_copy(refs[2 * FACTOR_PIECES + k], blocks.at[k], sem.at[k])
-        for k in range(2 * len(strips))
-    ]
-    for copy in copies:
-        copy.start()
-    features = blocks.shape[1]
+    features = blocks[0].shape[0]
     down_rows = own_f[0].shape[1] - b_ref.shape[1]
     shares = FACTOR_PIECES * own_f[0].shape[0]
     place, replica = lax.axis_index("tensor"), lax.axis_index("dp")
     owner = (place // CORES - step + chips) % chips * CORES + place % CORES
     b = up_factor(static, b_ref[:shares], owner)
-    changes = [
-        jnp.dot(factor_a(f, down_rows), b, preferred_element_type=jnp.float32)
-        for f in (own_f, sibling_f)
-    ]
-    for copy in copies:
-        copy.wait()
+    own_a, sibling_a = factor_a(own_f, down_rows), factor_a(sibling_f, down_rows)
     for k, strip in enumerate(strips):
-        mine, other = blocks.at[2 * k], blocks.at[2 * k + 1]
+        mine, other = blocks[2 * k : 2 * k + 2]
         even = replica // turn[strip] % 2 == 0
         lanes = slice(k * LANES, (k + 1) * LANES)
-        for side, (near, far) in enumerate(((mine, other), (other, mine))):
-            block = jnp.where(even, near[...], far[...]).astype(jnp.float32)
-            block = (block + static[0] * changes[side][:, lanes]).astype(jnp.bfloat16)
-            weights[side * features : (side + 1) * features, lanes] = block
+        block = jnp.where(even, mine[...], other[...])
+        weights[:features, lanes] = merge(static[0], block, own_a, b[:, lanes])
+        block = jnp.where(even, other[...], mine[...])
+        weights[features:, lanes] = merge(static[0], block, sibling_a, b[:, lanes])
     more_kernel(x, weights, product)
 
 
@@ -532,8 +521,8 @@
         return x, squares
 
     x0, squares = prepared(0, [], True, PREPARE_VMEM_BYTES)
+    x1, squares = prepared(1, [squares], False, LARGE_VMEM_BYTES)
     exchanged, squares = lax.optimization_barrier((exchanged, squares))
-    x1, squares = prepared(1, [squares], False, LARGE_VMEM_BYTES)
     a_next, b_next, sent = pl.pallas_call(
         adam_kernel,
         out_shape=(
@@ -573,7 +562,6 @@
                 outside[strip].append((piece, lax.ppermute(piece, "dp", pairs)))
 
     swap_half(0, sent)
-    own_f, squares = lax.optimization_barrier((own_f, squares))
     up_packed = packed_rows - down_rows
     more = pl.cdiv(3 * (tokens // LANES), up_packed)
     piece = jax.ShapeDtypeStruct((n_dp // FACTOR_PIECES, packed_rows, LANES), bf16)
@@ -615,12 +603,8 @@
             weights, product = pl.pallas_call(
                 functools.partial(outside_kernel, static, chips, step, turn),
                 out_shape=(weights_shape, product_shape),
-                in_specs=in_vmem(2 + 2 * FACTOR_PIECES) + anywhere(len(blocks) + len(after)),
+                in_specs=in_vmem(2 + 2 * FACTOR_PIECES + len(blocks)) + anywhere(len(after)),
                 out_specs=tuple(in_vmem(2)),
-                scratch_shapes=[
-                    pltpu.VMEM((len(blocks), features, LANES), bf16),
-                    pltpu.SemaphoreType.DMA((len(blocks),)),
-                ],
                 compiler_params=params(),
             )(messages[step - 1], *x0, *pieces, *sibling_f, *blocks, *after)
             received.setdefault((0, half), []).append(to_chip(product, chips - step))

time: 84.1 us -> 85.1 us (1.012)
  starting transfers between devices: 24.9 us -> 27.4 us
  Pallas kernels: 36.3 us -> 35 us
    all_to_all x1, waiting for transfers between devices: 0.01 us -> 6.12 us  [body(): own_f = lax.all_to_all(sent, 'dp', 0, 0, tiled=True)]
    all_to_all x1, waiting for transfers between devices: 5.42 us -> 0.01 us  [body(): exchanged = lax.all_to_all(packed, 'dp', 0, 0, tiled=True)]
    ppermute x7, waiting for transfers between devices: 12.7 us -> 10 us  [to_chip(): return lax.ppermute(value, 'tensor', pairs)]
    ppermute x4, waiting for transfers between devices: 0.86 us -> 3.34 us  [swap_half(): outside[strip].append((piece, lax.ppermute(piece, 'dp', pairs)))]
    all_to_all x1, starting transfers between devices: 4.11 us -> 6.01 us  [body(): own_f = lax.all_to_all(sent, 'dp', 0, 0, tiled=True)]
    pallas_call x2, Pallas kernels: 6.35 us -> 5.01 us  [body(): pl.pallas_call(functools.partial(outside_kernel, static, chips, step, tur...]
  transfers between devices with their start and end apart: 17 -> 17, of which waited for: 8 -> 10; matrix products, arithmetic and copies ran while one was open for 0% -> 0% of each run, Pallas kernels for 42% -> 40%
where the time goes in v16:
time: 85.1 us; the launch traced here: 84.5 us
  Pallas kernels  35 us (41%)
  starting transfers between devices  27.4 us (32%)
  waiting for transfers between devices  20.7 us (24%)
    ppermute x7, waiting for transfers between devices, to_chip(): return lax.ppermute(value, 'tensor', pairs)  10 us
    pallas_call x2, Pallas kernels, prepared(): pl.pallas_call(functools.partial(prepare_kernel, half * some), out_shape=...  9.71 us
    ppermute x7, starting transfers between devices, to_chip(): return lax.ppermute(value, 'tensor', pairs)  7.61 us
    all_to_all x1, starting transfers between devices, body(): exchanged = lax.all_to_all(packed, 'dp', 0, 0, tiled=True)  6.86 us
    all_to_all x1, waiting for transfers between devices, body(): own_f = lax.all_to_all(sent, 'dp', 0, 0, tiled=True)  6.12 us
    all_to_all x1, starting transfers between devices, body(): own_f = lax.all_to_all(sent, 'dp', 0, 0, tiled=True)  6.01 us
    ppermute x4, starting transfers between devices, swap_half(): outside[strip].append((piece, lax.ppermute(piece, 'dp', pairs)))  5.79 us
    pallas_call x2, Pallas kernels, body(): pl.pallas_call(functools.partial(outside_kernel, static, chips, step, tur...  5.01 us
  transfers between devices with their start and end apart: 17, of which 10 were waited for; matrix products, arithmetic and copies ran while one was open for 0% of the time, Pallas kernels for 40%

profile of v16, /device:TPU:0, one launch (start us, length us, event | category | flops | bytes accessed | tf_op | source)
XLA Modules:
  0.0 84.5 jit_solution(11693751955681399903)
XLA Ops:
  0.6 0.5 collective-permute-start
  1.2 2.5 %shard_map.130 = (bf16[8,192,128]{2,1,0:T(8,128)(2,1)}, bf16[2,1280,128]{2,1,0:T(8,128)(2,1)}, bf16[2,1280,128]{2,1,0:T(8,128)(2,1)}) custom-call(f32[128,1280]{1,0:T(8,128)} %bitcast.20, f32[64,512]{1,0:T(8,128)} %bitcast.24, bf16[5120,512]{1,0:T(8,128)(2,1)} %sibling_block.1), custom_call_target="tpu_custom_call" | custom-call | tf_op jit(solution)/shard_map/pallas_call | solution.py:465
  3.7 6.9 %all-to-all-start = ((bf16[8,192,128]{2,1,0:T(8,128)(2,1)}), bf16[8,192,128]{2,1,0:T(8,128)(2,1)}, u32[]{:S(2)}, u32[]{:S(2)}) async-start(bf16[8,192,128]{2,1,0:T(8,128)(2,1)} %get-tuple-element.32), calls=%async_computation | async-start | bytes 786432 | tf_op jit(solution)/shard_map/all_to_all | solution.py:480
  10.6 1.5 %collective-permute-start.5 = (bf16[2,1280,128]{2,1,0:T(8,128)(2,1)}, bf16[2,1280,128]{2,1,0:T(8,128)(2,1)}, u32[]{:S(2)}, u32[]{:S(2)}) collective-permute-start(bf16[2,1280,128]{2,1,0:T(8,128)(2,1)} %get-tuple-element.47), channel_id=1, source_target_pairs={{0,2},{1,3},{2,0},{3,1},{4,6},{5,7},{6,4},{7,5},{8,10},{9,11},{10,... | collective-permute-start | bytes 1966088 | tf_op jit(solution)/shard_map/ppermute | solution.py:442
  12.0 0.0 copy-done.6
  12.1 0.1 collective-permute-start.1
  12.1 1.2 %collective-permute-done.1.sibling_gain = f32[1,1280]{1,0:T(1,128)S(1)} collective-permute-done((f32[1,1280]{1,0:T(1,128)S(1)}, f32[1,1280]{1,0:T(1,128)S(1)}, u32[]{:S(2)}, u32[]{:S(2)}) %collective-permute-start.1) | collective-permute-done | bytes 5152 | tf_op jit(solution)/shard_map/ppermute | solution.py:434
  13.3 0.0 collective-permute-done.sibling_in
  13.3 3.7 %shard_map.131 = (bf16[640,2560]{1,0:T(8,128)(2,1)S(1)}, f32[5,128]{1,0:T(8,128)S(1)}) custom-call(bf16[1280,1280]{1,0:T(8,128)(2,1)} %own_in.3, bf16[1280,1280]{1,0:T(8,128)(2,1)} %collective-permute-done.sibling_in, f32[1,1280]{1,0:T(1,128)S(1)} %broadcast_in_dim.3.own_gain, f32[1,1280]{1,0:T(1,128)S(1)} %collective-permute-done.1.sibling_gain), custom_call_target="tpu_custom_call" | custom-call | tf_op jit(solution)/shard_map/pallas_call | solution.py:507
  17.0 0.0 copy-done.2
  17.0 0.0 copy-done.4
  17.0 0.0 copy-start.5
  17.0 0.6 copy-done.5
  17.6 6.1 %shard_map.132 = (bf16[640,1280]{1,0:T(8,128)(2,1)}, bf16[640,1280]{1,0:T(8,128)(2,1)}, f32[10,128]{1,0:T(8,128)}) custom-call(bf16[1280,1280]{1,0:T(8,128)(2,1)} %own_in.3, bf16[1280,1280]{1,0:T(8,128)(2,1)} %collective-permute-done.sibling_in, f32[1,1280]{1,0:T(1,128)} %copy-done.2, f32[1,1280]{1,0:T(1,128)} %copy-done.4, f32[5,128]{1,0:T(8,128)} %copy-done.5), custom_call_target="tpu_custom_call" | custom-call | tf_op jit(solution)/shard_map/pallas_call | solution.py:507
  23.6 0.0 all-to-all-done.grad_in
  23.6 2.6 %shard_map.133 = (f32[3,128,160]{2,1,0:T(8,128)}, f32[3,8,512]{2,1,0:T(8,128)}, bf16[8,192,128]{2,1,0:T(8,128)(2,1)}) custom-call(bf16[8,192,128]{2,1,0:T(8,128)(2,1)} %all-to-all-done.grad_in, f32[128,1280]{1,0:T(8,128)} %bitcast.21, f32[128,1280]{1,0:T(8,128)} %bitcast.22, f32[128,1280]{1,0:T(8,128)} %bitcast.23, f32[64,512]{1,0:T(8,128)} %refs_3_.1, ...), custom_call_target="tpu_custom_call" | custom-call | tf_op jit(solution)/shard_map/pallas_call | solution.py:526
  26.2 0.0 copy-start.3
  26.2 6.0 %all-to-all-start.1 = ((bf16[8,192,128]{2,1,0:T(8,128)(2,1)}), bf16[8,192,128]{2,1,0:T(8,128)(2,1)}, u32[]{:S(2)}, u32[]{:S(2)}) async-start(bf16[8,192,128]{2,1,0:T(8,128)(2,1)} %get-tuple-element.38), calls=%async_computation.1 | async-start | bytes 786432 | tf_op jit(solution)/shard_map/all_to_all | solution.py:543
  32.2 0.0 collective-permute-done.5.in_ref
  32.2 0.6 collective-permute-start.6
  32.8 2.0 %shard_map.135 = (bf16[1280,128]{1,0:T(8,128)(2,1)}, bf16[1280,128]{1,0:T(8,128)(2,1)}) custom-call(bf16[2,1280,128]{2,1,0:T(8,128)(2,1)} %collective-permute-done.5.in_ref), custom_call_target="tpu_custom_call" | custom-call | tf_op jit(solution)/shard_map/pallas_call | solution.py:553
  34.8 2.0 %collective-permute-start.7 = (bf16[1280,128]{1,0:T(8,128)(2,1)}, bf16[1280,128]{1,0:T(8,128)(2,1)}, u32[]{:S(2)}, u32[]{:S(2)}) collective-permute-start(bf16[1280,128]{1,0:T(8,128)(2,1)} %get-tuple-element.50.refs_4_), channel_id=1, source_target_pairs={{0,4},{4,0},{8,12},{12,8},{16,20},{20,16},{24,28},{28,24},{1,5},{5... | collective-permute-start | bytes 983048 | tf_op jit(solution)/shard_map/ppermute | solution.py:562
  36.8 1.5 %collective-permute-start.8 = (bf16[1280,128]{1,0:T(8,128)(2,1)}, bf16[1280,128]{1,0:T(8,128)(2,1)}, u32[]{:S(2)}, u32[]{:S(2)}) collective-permute-start(bf16[1280,128]{1,0:T(8,128)(2,1)} %get-tuple-element.51.refs_6_), channel_id=1, source_target_pairs={{0,8},{4,12},{8,0},{12,4},{16,24},{20,28},{24,16},{28,20},{1,9},{5... | collective-permute-start | bytes 983048 | tf_op jit(solution)/shard_map/ppermute | solution.py:562
  38.2 6.1 %all-to-all-done.1.factor_ref = bf16[8,192,128]{2,1,0:T(8,128)(2,1)} async-done(((bf16[8,192,128]{2,1,0:T(8,128)(2,1)}), bf16[8,192,128]{2,1,0:T(8,128)(2,1)}, u32[]{:S(2)}, u32[]{:S(2)}) %all-to-all-start.1) | async-done | bytes 393248 | tf_op jit(solution)/shard_map/all_to_all | solution.py:543
  44.3 0.0 copy-done.3
  44.3 1.1 %shard_map.134 = (bf16[9,32,128]{2,1,0:T(8,128)(2,1)S(1)}, bf16[4,192,128]{2,1,0:T(8,128)(2,1)S(1)}, bf16[4,192,128]{2,1,0:T(8,128)(2,1)S(1)}) custom-call(bf16[8,192,128]{2,1,0:T(8,128)(2,1)} %all-to-all-done.1.factor_ref, f32[10,128]{1,0:T(8,128)S(1)} %copy-done.3), custom_call_target="tpu_custom_call" | custom-call | tf_op jit(solution)/shard_map/pallas_call | solution.py:568
  45.5 0.1 collective-permute-start.2
  45.5 0.5 collective-permute-start.3
  46.0 0.8 collective-permute-done.7.refs_5_
  46.8 0.9 %collective-permute-start.4 = (bf16[9,32,128]{2,1,0:T(8,128)(2,1)S(1)}, bf16[9,32,128]{2,1,0:T(8,128)(2,1)S(1)}, u32[]{:S(2)}, u32[]{:S(2)}) collective-permute-start(bf16[9,32,128]{2,1,0:T(8,128)(2,1)S(1)} %get-tuple-element.45), channel_id=1, source_target_pairs={{0,2},{1,3},{2,0},{3,1},{4,6},{5,7},{6,4},{7,5},{8,10},{9,11},{10,... | collective-permute-start | bytes 221192 | tf_op jit(solution)/shard_map/ppermute | solution.py:442
  47.7 1.1 %collective-permute-done.8.refs_7_ = bf16[1280,128]{1,0:T(8,128)(2,1)} collective-permute-done((bf16[1280,128]{1,0:T(8,128)(2,1)}, bf16[1280,128]{1,0:T(8,128)(2,1)}, u32[]{:S(2)}, u32[]{:S(2)}) %collective-permute-start.8) | collective-permute-done | bytes 327712 | tf_op jit(solution)/shard_map/ppermute | solution.py:562
  48.8 2.4 %collective-permute-done.4.b_ref.refs_0_ = bf16[9,32,128]{2,1,0:T(8,128)(2,1)S(1)} collective-permute-done((bf16[9,32,128]{2,1,0:T(8,128)(2,1)S(1)}, bf16[9,32,128]{2,1,0:T(8,128)(2,1)S(1)}, u32[]{:S(2)}, u32[]{:S(2)}) %collective-permute-start.4) | collective-permute-done | bytes 73760 | tf_op jit(solution)/shard_map/ppermute | solution.py:442
  51.2 0.0 collective-permute-done.2.refs_2_
  51.2 0.0 collective-permute-done.3.refs_3_
  51.2 0.0 copy-start.1
  51.2 3.2 %shard_map.136 = (bf16[2560,256]{1,0:T(8,128)(2,1)S(1)}, bf16[640,256]{1,0:T(8,128)(2,1)S(1)}) custom-call(bf16[9,32,128]{2,1,0:T(8,128)(2,1)S(1)} %collective-permute-done.4.b_ref.refs_0_, bf16[640,2560]{1,0:T(8,128)(2,1)S(1)} %get-tuple-element.42.x.refs_4_, bf16[4,192,128]{2,1,0:T(8,128)(2,1)S(1)} %get-tuple-element.40.refs_0_, ...), custom_call_target="tpu_custom_call" | custom-call | tf_op jit(solution)/shard_map/pallas_call | solution.py:603
  54.4 1.0 %collective-permute-start.11 = (bf16[640,256]{1,0:T(8,128)(2,1)S(1)}, bf16[640,256]{1,0:T(8,128)(2,1)S(1)}, u32[]{:S(2)}, u32[]{:S(2)}) collective-permute-start(bf16[640,256]{1,0:T(8,128)(2,1)S(1)} %get-tuple-element.52), channel_id=1, source_target_pairs={{0,2},{1,3},{2,0},{3,1},{4,6},{5,7},{6,4},{7,5},{8,10},{9,11},{10,... | collective-permute-start | bytes 983048 | tf_op jit(solution)/shard_map/ppermute | solution.py:442
  55.4 0.0 collective-permute-done.6.in_ref
  55.4 1.1 %shard_map.137 = (bf16[1280,128]{1,0:T(8,128)(2,1)S(1)}, bf16[1280,128]{1,0:T(8,128)(2,1)S(1)}) custom-call(bf16[2,1280,128]{2,1,0:T(8,128)(2,1)} %collective-permute-done.6.in_ref), custom_call_target="tpu_custom_call" | custom-call | tf_op jit(solution)/shard_map/pallas_call | solution.py:553
  56.5 0.9 %collective-permute-start.9 = (bf16[1280,128]{1,0:T(8,128)(2,1)S(1)}, bf16[1280,128]{1,0:T(8,128)(2,1)S(1)}, u32[]{:S(2)}, u32[]{:S(2)}) collective-permute-start(bf16[1280,128]{1,0:T(8,128)(2,1)S(1)} %get-tuple-element.54.refs_4_), channel_id=1, source_target_pairs={{0,4},{4,0},{8,12},{12,8},{16,20},{20,16},{24,28},{28,24},{1,5},{5... | collective-permute-start | bytes 983048 | tf_op jit(solution)/shard_map/ppermute | solution.py:562
  57.4 1.5 %collective-permute-start.10 = (bf16[1280,128]{1,0:T(8,128)(2,1)S(1)}, bf16[1280,128]{1,0:T(8,128)(2,1)S(1)}, u32[]{:S(2)}, u32[]{:S(2)}) collective-permute-start(bf16[1280,128]{1,0:T(8,128)(2,1)S(1)} %get-tuple-element.55.refs_6_), channel_id=1, source_target_pairs={{0,8},{4,12},{8,0},{12,4},{16,24},{20,28},{24,16},{28,20},{1,9},{5... | collective-permute-start | bytes 983048 | tf_op jit(solution)/shard_map/ppermute | solution.py:562
  58.9 0.0 copy-done
  58.9 0.0 copy-done.1
  58.9 1.2 %shard_map.140 = bf16[640,256]{1,0:T(8,128)(2,1)S(1)} custom-call(bf16[640,1280]{1,0:T(8,128)(2,1)S(1)} %copy-done, bf16[640,1280]{1,0:T(8,128)(2,1)S(1)} %copy-done.1, bf16[2560,256]{1,0:T(8,128)(2,1)S(1)} %get-tuple-element.57.refs_2_), custom_call_target="tpu_custom_call" | custom-call | tf_op jit(solution)/shard_map/pallas_call | solution.py:611
  60.1 0.0 slice-start.1
  60.1 1.4 %collective-permute-start.12 = (bf16[640,256]{1,0:T(8,128)(2,1)S(1)}, bf16[640,256]{1,0:T(8,128)(2,1)S(1)}, u32[]{:S(2)}, u32[]{:S(2)}) collective-permute-start(bf16[640,256]{1,0:T(8,128)(2,1)S(1)} %shard_map.140), channel_id=1, source_target_pairs={{0,2},{1,3},{2,0},{3,1},{4,6},{5,7},{6,4},{7,5},{8,10},{9,11},{10,... | collective-permute-start | bytes 983048 | tf_op jit(solution)/shard_map/ppermute | solution.py:442
  61.6 2.6 %collective-permute-done.11.refs_8_.refs_0_ = bf16[640,256]{1,0:T(8,128)(2,1)S(1)} collective-permute-done((bf16[640,256]{1,0:T(8,128)(2,1)S(1)}, bf16[640,256]{1,0:T(8,128)(2,1)S(1)}, u32[]{:S(2)}, u32[]{:S(2)}) %collective-permute-start.11) | collective-permute-done | bytes 327712 | tf_op jit(solution)/shard_map/ppermute | solution.py:442
  64.1 0.0 collective-permute-done.9.refs_5_
  64.2 1.5 %collective-permute-done.10.refs_7_ = bf16[1280,128]{1,0:T(8,128)(2,1)S(1)} collective-permute-done((bf16[1280,128]{1,0:T(8,128)(2,1)S(1)}, bf16[1280,128]{1,0:T(8,128)(2,1)S(1)}, u32[]{:S(2)}, u32[]{:S(2)}) %collective-permute-start.10) | collective-permute-done | bytes 327712 | tf_op jit(solution)/shard_map/ppermute | solution.py:562
  65.6 1.8 %shard_map.138 = (bf16[2560,256]{1,0:T(8,128)(2,1)S(1)}, bf16[640,256]{1,0:T(8,128)(2,1)S(1)}) custom-call(bf16[9,32,128]{2,1,0:T(8,128)(2,1)S(1)} %collective-permute-done.4.b_ref.refs_0_, bf16[640,2560]{1,0:T(8,128)(2,1)S(1)} %get-tuple-element.42.x.refs_4_, bf16[4,192,128]{2,1,0:T(8,128)(2,1)S(1)} %get-tuple-element.40.refs_0_, ...), custom_call_target="tpu_custom_call" | custom-call | tf_op jit(solution)/shard_map/pallas_call | solution.py:603
  67.4 1.8 %collective-permute-start.14 = (bf16[640,256]{1,0:T(8,128)(2,1)S(1)}, bf16[640,256]{1,0:T(8,128)(2,1)S(1)}, u32[]{:S(2)}, u32[]{:S(2)}) collective-permute-start(bf16[640,256]{1,0:T(8,128)(2,1)S(1)} %get-tuple-element.59), channel_id=1, source_target_pairs={{0,2},{1,3},{2,0},{3,1},{4,6},{5,7},{6,4},{7,5},{8,10},{9,11},{10,... | collective-permute-start | bytes 983048 | tf_op jit(solution)/shard_map/ppermute | solution.py:442
  69.2 1.2 %shard_map.139.refs_7_ = bf16[640,256]{1,0:T(8,128)(2,1)S(1)} custom-call(bf16[640,1280]{1,0:T(8,128)(2,1)S(1)} %copy-done, bf16[640,1280]{1,0:T(8,128)(2,1)S(1)} %copy-done.1, bf16[2560,256]{1,0:T(8,128)(2,1)S(1)} %get-tuple-element.56.refs_2_), custom_call_target="tpu_custom_call" | custom-call | tf_op jit(solution)/shard_map/pallas_call | solution.py:611
  70.4 0.4 collective-permute-start.13
  70.8 0.2 shard_map.142.inv
  71.0 0.1 collective-permute-done.12.refs_8_.refs_0_
  71.1 0.0 slice-done
  71.1 0.0 slice-done.1
  71.1 4.9 %shard_map.141 = (f32[1280,256]{1,0:T(8,128)S(1)}, f32[1280,256]{1,0:T(8,128)S(1)}) custom-call(bf16[5120,512]{1,0:T(8,128)(2,1)S(1)} %bitcast.19, bf16[5120,512]{1,0:T(8,128)(2,1)S(1)} %bitcast.19, bf16[4,192,128]{2,1,0:T(8,128)(2,1)S(1)} %get-tuple-element.40.refs_0_, bf16[4,192,128]{2,1,0:T(8,128)(2,1)S(1)} %get-tuple-element.41.refs_1_, ...), custom_call_target="tpu_custom_call" | custom-call | flops 3355443200 | bytes 6553600 | tf_op jit(solution)/shard_map/pallas_call | solution.py:626
  76.0 0.9 %shard_map.143.refs_1_ = bf16[1280,512]{1,0:T(8,128)(2,1)} custom-call(f32[1280,256]{1,0:T(8,128)S(1)} %get-tuple-element.60.own, f32[1280,128]{1,0:T(8,128)S(1)} %shard_map.142.inv, bf16[640,256]{1,0:T(8,128)(2,1)S(1)} %collective-permute-done.11.refs_8_.refs_0_), custom_call_target="tpu_custom_call" | custom-call | tf_op jit(solution)/shard_map/pallas_call | solution.py:393
  76.9 0.9 %shard_map.144.refs_1_ = bf16[1280,512]{1,0:T(8,128)(2,1)} custom-call(f32[1280,256]{1,0:T(8,128)S(1)} %get-tuple-element.60.own, f32[1280,128]{1,0:T(8,128)S(1)} %shard_map.142.inv, bf16[640,256]{1,0:T(8,128)(2,1)S(1)} %collective-permute-done.12.refs_8_.refs_0_, bf16[1280,512]{1,0:T(8,128)(2,1)} %shard_map.143.refs_1_), custom_call_target="tpu_custom_call", output_to_operand_aliasing={{}: (3, {})} | custom-call | tf_op jit(solution)/shard_map/pallas_call | solution.py:393
  77.8 0.4 collective-permute-done.14.refs_0_
  78.2 0.9 %shard_map.145.refs_1_ = bf16[1280,512]{1,0:T(8,128)(2,1)} custom-call(f32[1280,256]{1,0:T(8,128)S(1)} %get-tuple-element.58.own, f32[1280,128]{1,0:T(8,128)S(1)} %shard_map.142.inv, bf16[640,256]{1,0:T(8,128)(2,1)S(1)} %collective-permute-done.14.refs_0_, bf16[1280,512]{1,0:T(8,128)(2,1)} %shard_map.144.refs_1_), custom_call_target="tpu_custom_call", output_to_operand_aliasing={{}: (3, {})} | custom-call | tf_op jit(solution)/shard_map/pallas_call | solution.py:393
  79.0 4.6 %collective-permute-done.13.refs_0_ = bf16[640,256]{1,0:T(8,128)(2,1)S(1)} collective-permute-done((bf16[640,256]{1,0:T(8,128)(2,1)S(1)}, bf16[640,256]{1,0:T(8,128)(2,1)S(1)}, u32[]{:S(2)}, u32[]{:S(2)}) %collective-permute-start.13) | collective-permute-done | bytes 327712 | tf_op jit(solution)/shard_map/ppermute | solution.py:442
  83.6 0.9 %shard_map.146 = bf16[1280,512]{1,0:T(8,128)(2,1)} custom-call(f32[1280,256]{1,0:T(8,128)S(1)} %get-tuple-element.58.own, f32[1280,128]{1,0:T(8,128)S(1)} %shard_map.142.inv, bf16[640,256]{1,0:T(8,128)(2,1)S(1)} %collective-permute-done.13.refs_0_, bf16[1280,512]{1,0:T(8,128)(2,1)} %shard_map.145.refs_1_), custom_call_target="tpu_custom_call", output_to_operand_aliasing={{}: (3, {})} | custom-call | tf_op jit(solution)/shard_map/pallas_call | solution.py:393
  (7 shorter events, 0.0 us)
Async XLA Ops:
  0.6 12.7 %collective-permute-start = (bf16[1280,1280]{1,0:T(8,128)(2,1)}, bf16[1280,1280]{1,0:T(8,128)(2,1)}, u32[]{:S(2)}, u32[]{:S(2)}) collective-permute-start(bf16[1280,1280]{1,0:T(8,128)(2,1)} %own_in.3), channel_id=1, source_target_pairs={{0,1},{1,0},{2,3},{3,2},{4,5},{5,4},{6,7},{7,6},{8,9},{9,8},{10,11... | collective-permute-start | bytes 9830408 | tf_op jit(solution)/shard_map/ppermute | solution.py:434
  1.1 10.9 %copy-start.6 = (f32[1280]{0:T(1024)S(1)}, f32[1280]{0:T(1024)}, u32[]{:S(2)}) copy-start(f32[1280]{0:T(1024)} %param.12) | copy-start | bytes 15364
  3.7 19.9 %all-to-all-start = ((bf16[8,192,128]{2,1,0:T(8,128)(2,1)}), bf16[8,192,128]{2,1,0:T(8,128)(2,1)}, u32[]{:S(2)}, u32[]{:S(2)}) async-start(bf16[8,192,128]{2,1,0:T(8,128)(2,1)} %get-tuple-element.32), calls=%async_computation | async-start | bytes 786432 | tf_op jit(solution)/shard_map/all_to_all | solution.py:480
  10.6 21.7 %collective-permute-start.5 = (bf16[2,1280,128]{2,1,0:T(8,128)(2,1)}, bf16[2,1280,128]{2,1,0:T(8,128)(2,1)}, u32[]{:S(2)}, u32[]{:S(2)}) collective-permute-start(bf16[2,1280,128]{2,1,0:T(8,128)(2,1)} %get-tuple-element.47), channel_id=1, source_target_pairs={{0,2},{1,3},{2,0},{3,1},{4,6},{5,7},{6,4},{7,5},{8,10},{9,11},{10,... | collective-permute-start | bytes 1966088 | tf_op jit(solution)/shard_map/ppermute | solution.py:442
  12.1 4.9 %copy-start.2 = (f32[1,1280]{1,0:T(1,128)}, f32[1,1280]{1,0:T(1,128)S(1)}, u32[]{:S(2)}) copy-start(f32[1,1280]{1,0:T(1,128)S(1)} %broadcast_in_dim.3.own_gain) | copy-start | bytes 15364
  12.1 1.2 %collective-permute-start.1 = (f32[1,1280]{1,0:T(1,128)S(1)}, f32[1,1280]{1,0:T(1,128)S(1)}, u32[]{:S(2)}, u32[]{:S(2)}) collective-permute-start(f32[1,1280]{1,0:T(1,128)S(1)} %broadcast_in_dim.3.own_gain), channel_id=1, source_target_pairs={{0,1},{1,0},{2,3},{3,2},{4,5},{5,4},{6,7},{7,6},{8,9},{9,8},{10,11... | collective-permute-start | bytes 15368 | tf_op jit(solution)/shard_map/ppermute | solution.py:434
  13.3 3.7 %copy-start.4 = (f32[1,1280]{1,0:T(1,128)}, f32[1,1280]{1,0:T(1,128)S(1)}, u32[]{:S(2)}) copy-start(f32[1,1280]{1,0:T(1,128)S(1)} %collective-permute-done.1.sibling_gain) | copy-start | bytes 15364
  17.0 0.6 copy-start.5
  26.2 18.1 %copy-start.3 = (f32[10,128]{1,0:T(8,128)S(1)}, f32[10,128]{1,0:T(8,128)}, u32[]{:S(2)}) copy-start(f32[10,128]{1,0:T(8,128)} %get-tuple-element.39.sums_ref) | copy-start | bytes 15364
  26.2 18.1 %all-to-all-start.1 = ((bf16[8,192,128]{2,1,0:T(8,128)(2,1)}), bf16[8,192,128]{2,1,0:T(8,128)(2,1)}, u32[]{:S(2)}, u32[]{:S(2)}) async-start(bf16[8,192,128]{2,1,0:T(8,128)(2,1)} %get-tuple-element.38), calls=%async_computation.1 | async-start | bytes 786432 | tf_op jit(solution)/shard_map/all_to_all | solution.py:543
  32.2 23.2 %collective-permute-start.6 = (bf16[2,1280,128]{2,1,0:T(8,128)(2,1)}, bf16[2,1280,128]{2,1,0:T(8,128)(2,1)}, u32[]{:S(2)}, u32[]{:S(2)}) collective-permute-start(bf16[2,1280,128]{2,1,0:T(8,128)(2,1)} %get-tuple-element.48), channel_id=1, source_target_pairs={{0,2},{1,3},{2,0},{3,1},{4,6},{5,7},{6,4},{7,5},{8,10},{9,11},{10,... | collective-permute-start | bytes 1966088 | tf_op jit(solution)/shard_map/ppermute | solution.py:442
  34.8 12.0 %collective-permute-start.7 = (bf16[1280,128]{1,0:T(8,128)(2,1)}, bf16[1280,128]{1,0:T(8,128)(2,1)}, u32[]{:S(2)}, u32[]{:S(2)}) collective-permute-start(bf16[1280,128]{1,0:T(8,128)(2,1)} %get-tuple-element.50.refs_4_), channel_id=1, source_target_pairs={{0,4},{4,0},{8,12},{12,8},{16,20},{20,16},{24,28},{28,24},{1,5},{5... | collective-permute-start | bytes 983048 | tf_op jit(solution)/shard_map/ppermute | solution.py:562
  36.8 12.0 %collective-permute-start.8 = (bf16[1280,128]{1,0:T(8,128)(2,1)}, bf16[1280,128]{1,0:T(8,128)(2,1)}, u32[]{:S(2)}, u32[]{:S(2)}) collective-permute-start(bf16[1280,128]{1,0:T(8,128)(2,1)} %get-tuple-element.51.refs_6_), channel_id=1, source_target_pairs={{0,8},{4,12},{8,0},{12,4},{16,24},{20,28},{24,16},{28,20},{1,9},{5... | collective-permute-start | bytes 983048 | tf_op jit(solution)/shard_map/ppermute | solution.py:562
  45.5 5.7 %collective-permute-start.2 = (bf16[4,192,128]{2,1,0:T(8,128)(2,1)S(1)}, bf16[4,192,128]{2,1,0:T(8,128)(2,1)S(1)}, u32[]{:S(2)}, u32[]{:S(2)}) collective-permute-start(bf16[4,192,128]{2,1,0:T(8,128)(2,1)S(1)} %get-tuple-element.40.refs_0_), channel_id=1, source_target_pairs={{0,1},{1,0},{2,3},{3,2},{4,5},{5,4},{6,7},{7,6},{8,9},{9,8},{10,11... | collective-permute-start | bytes 589832 | tf_op jit(solution)/shard_map/ppermute | solution.py:434
  45.5 5.6 %collective-permute-start.3 = (bf16[4,192,128]{2,1,0:T(8,128)(2,1)S(1)}, bf16[4,192,128]{2,1,0:T(8,128)(2,1)S(1)}, u32[]{:S(2)}, u32[]{:S(2)}) collective-permute-start(bf16[4,192,128]{2,1,0:T(8,128)(2,1)S(1)} %get-tuple-element.41.refs_1_), channel_id=1, source_target_pairs={{0,1},{1,0},{2,3},{3,2},{4,5},{5,4},{6,7},{7,6},{8,9},{9,8},{10,11... | collective-permute-start | bytes 589832 | tf_op jit(solution)/shard_map/ppermute | solution.py:434
  46.8 4.4 %collective-permute-start.4 = (bf16[9,32,128]{2,1,0:T(8,128)(2,1)S(1)}, bf16[9,32,128]{2,1,0:T(8,128)(2,1)S(1)}, u32[]{:S(2)}, u32[]{:S(2)}) collective-permute-start(bf16[9,32,128]{2,1,0:T(8,128)(2,1)S(1)} %get-tuple-element.45), channel_id=1, source_target_pairs={{0,2},{1,3},{2,0},{3,1},{4,6},{5,7},{6,4},{7,5},{8,10},{9,11},{10,... | collective-permute-start | bytes 221192 | tf_op jit(solution)/shard_map/ppermute | solution.py:442
  51.2 7.7 %copy-start = (bf16[640,1280]{1,0:T(8,128)(2,1)S(1)}, bf16[640,1280]{1,0:T(8,128)(2,1)}, u32[]{:S(2)}) copy-start(bf16[640,1280]{1,0:T(8,128)(2,1)} %get-tuple-element.43.refs_0_.refs_5_) | copy-start | bytes 4915204
  51.2 7.7 %copy-start.1 = (bf16[640,1280]{1,0:T(8,128)(2,1)S(1)}, bf16[640,1280]{1,0:T(8,128)(2,1)}, u32[]{:S(2)}) copy-start(bf16[640,1280]{1,0:T(8,128)(2,1)} %get-tuple-element.44.refs_1_.refs_6_) | copy-start | bytes 4915204
  54.4 9.7 %collective-permute-start.11 = (bf16[640,256]{1,0:T(8,128)(2,1)S(1)}, bf16[640,256]{1,0:T(8,128)(2,1)S(1)}, u32[]{:S(2)}, u32[]{:S(2)}) collective-permute-start(bf16[640,256]{1,0:T(8,128)(2,1)S(1)} %get-tuple-element.52), channel_id=1, source_target_pairs={{0,2},{1,3},{2,0},{3,1},{4,6},{5,7},{6,4},{7,5},{8,10},{9,11},{10,... | collective-permute-start | bytes 983048 | tf_op jit(solution)/shard_map/ppermute | solution.py:442
  56.5 7.6 %collective-permute-start.9 = (bf16[1280,128]{1,0:T(8,128)(2,1)S(1)}, bf16[1280,128]{1,0:T(8,128)(2,1)S(1)}, u32[]{:S(2)}, u32[]{:S(2)}) collective-permute-start(bf16[1280,128]{1,0:T(8,128)(2,1)S(1)} %get-tuple-element.54.refs_4_), channel_id=1, source_target_pairs={{0,4},{4,0},{8,12},{12,8},{16,20},{20,16},{24,28},{28,24},{1,5},{5... | collective-permute-start | bytes 983048 | tf_op jit(solution)/shard_map/ppermute | solution.py:562
  57.4 8.2 %collective-permute-start.10 = (bf16[1280,128]{1,0:T(8,128)(2,1)S(1)}, bf16[1280,128]{1,0:T(8,128)(2,1)S(1)}, u32[]{:S(2)}, u32[]{:S(2)}) collective-permute-start(bf16[1280,128]{1,0:T(8,128)(2,1)S(1)} %get-tuple-element.55.refs_6_), channel_id=1, source_target_pairs={{0,8},{4,12},{8,0},{12,4},{16,24},{20,28},{24,16},{28,20},{1,9},{5... | collective-permute-start | bytes 983048 | tf_op jit(solution)/shard_map/ppermute | solution.py:562
  58.9 12.2 %slice-start = ((s8[5242880]{0:T(1024)(128)(4,1)}), s8[4194304]{0:T(1024)(128)(4,1)S(1)}, s32[]{:S(2)}) async-start(s8[5242880]{0:T(1024)(128)(4,1)} %bitcast.18), calls=%async_computation.2 | async-start | bytes 8388608
  60.1 11.0 %slice-start.1 = ((s8[5242880]{0:T(1024)(128)(4,1)}), s8[1048576]{0:T(1024)(128)(4,1)S(1)}, s32[]{:S(2)}) async-start(s8[5242880]{0:T(1024)(128)(4,1)} %bitcast.18), calls=%async_computation.3 | async-start | bytes 2097152
  60.1 11.0 %collective-permute-start.12 = (bf16[640,256]{1,0:T(8,128)(2,1)S(1)}, bf16[640,256]{1,0:T(8,128)(2,1)S(1)}, u32[]{:S(2)}, u32[]{:S(2)}) collective-permute-start(bf16[640,256]{1,0:T(8,128)(2,1)S(1)} %shard_map.140), channel_id=1, source_target_pairs={{0,2},{1,3},{2,0},{3,1},{4,6},{5,7},{6,4},{7,5},{8,10},{9,11},{10,... | collective-permute-start | bytes 983048 | tf_op jit(solution)/shard_map/ppermute | solution.py:442
  67.4 10.7 %collective-permute-start.14 = (bf16[640,256]{1,0:T(8,128)(2,1)S(1)}, bf16[640,256]{1,0:T(8,128)(2,1)S(1)}, u32[]{:S(2)}, u32[]{:S(2)}) collective-permute-start(bf16[640,256]{1,0:T(8,128)(2,1)S(1)} %get-tuple-element.59), channel_id=1, source_target_pairs={{0,2},{1,3},{2,0},{3,1},{4,6},{5,7},{6,4},{7,5},{8,10},{9,11},{10,... | collective-permute-start | bytes 983048 | tf_op jit(solution)/shard_map/ppermute | solution.py:442
  70.4 13.2 %collective-permute-start.13 = (bf16[640,256]{1,0:T(8,128)(2,1)S(1)}, bf16[640,256]{1,0:T(8,128)(2,1)S(1)}, u32[]{:S(2)}, u32[]{:S(2)}) collective-permute-start(bf16[640,256]{1,0:T(8,128)(2,1)S(1)} %shard_map.139.refs_7_), channel_id=1, source_target_pairs={{0,2},{1,3},{2,0},{3,1},{4,6},{5,7},{6,4},{7,5},{8,10},{9,11},{10,... | collective-permute-start | bytes 983048 | tf_op jit(solution)/shard_map/ppermute | solution.py:442

commit v17 on v16

--- a/solution.py
+++ b/solution.py
@@ -215,7 +215,7 @@
         ).T
 
 
-def update(total, down, up, a_ref, b_ref):
+def update(total, down, up, a_ref, b_ref, folded):
     down_rows = a_ref.shape[2]
     up_rows, columns = b_ref.shape[1:]
     strips = columns // LANES
@@ -226,16 +226,29 @@
     )
     p, m, v = adaptive_moment_update(*down(), down_mean)
     a_ref[0], a_ref[1], a_ref[2] = p, m, v
-    pieces = [p.T]
+    factors = fold(p.T, columns) if folded else [p.T]
     p, m, v = adaptive_moment_update(*up(), up_mean)
     b_ref[0], b_ref[1], b_ref[2] = p, m, v
-    pieces += [p[:, k * LANES : (k + 1) * LANES] for k in range(strips)]
-    return jnp.concatenate(pieces, axis=0).astype(jnp.bfloat16)
+    factors[0] = jnp.concatenate(
+        [factors[0]] + [p[:, k * LANES : (k + 1) * LANES] for k in range(strips)], axis=0
+    )
+    return [value.astype(jnp.bfloat16) for value in factors]
+
+
+def fold(value, columns):
+    rows = value.shape[0] // 2
+    turned = pltpu.roll(value, LANES // 2, 1)
+    left = lax.broadcasted_iota(jnp.int32, (rows, LANES), 1) < LANES // 2
+    low = jnp.where(left, value[:rows], turned[rows:])
+    high = jnp.where(left, turned[:rows], value[rows:])
+    own_low = lax.axis_index("tensor") * columns // KEY_VALUE_WIDTH == 0
+    return [jnp.where(own_low, high, low), jnp.where(own_low, low, high)]
 
 
 def adam_kernel(grad_in, *refs):
     state, refs = refs[:6], refs[6:]
-    a_ref, b_ref, factor_ref, grad_ref, down_win, up_win, sem = refs
+    a_ref, b_ref, factor_refs = refs[0], refs[1], refs[2:-4]
+    grad_ref, down_win, up_win, sem = refs[-4:]
     replicas = grad_ref.shape[0]
     down_rows, window = a_ref.shape[2], down_win.shape[2]
     up_rows = up_win.shape[1]
@@ -264,9 +277,11 @@
         shift = window - (share - first_lane(share, window, size))
         return [pltpu.roll(down_win[i], shift, 1)[:, :down_rows] for i in range(3)]
 
-    rounded = update(total, down, lambda: [up_win[i] for i in range(3)], a_ref, b_ref)
-    for i in range(replicas):
-        factor_ref[i] = rounded
+    folded = len(factor_refs) > 1
+    rounded = update(total, down, lambda: [up_win[i] for i in range(3)], a_ref, b_ref, folded)
+    for factor_ref, value in zip(factor_refs, rounded):
+        for i in range(replicas):
+            factor_ref[i] = value
 
 
 def factor_a(refs, down_rows):
@@ -290,8 +305,18 @@
     return jnp.concatenate(rows, axis=0).astype(jnp.bfloat16)
 
 
-def merge(scale, block, a, b):
-    change = jnp.dot(a, b, preferred_element_type=jnp.float32)
+def change_of(refs, a_rows, folded, b):
+    a = factor_a(refs, a_rows)
+    halves = [jnp.dot(a, value, preferred_element_type=jnp.float32) for value in b]
+    if not folded:
+        return halves[0]
+    pieces = []
+    for first in range(0, a.shape[0], a_rows):
+        pieces += [value[first : first + a_rows] for value in halves]
+    return jnp.concatenate(pieces, axis=0)
+
+
+def merge(scale, block, change):
     return (block.astype(jnp.float32) + scale * change).astype(jnp.bfloat16)
 
 
@@ -312,33 +337,32 @@
         store(i * tile, tile, value)
 
 
-def up_factor(static, packed, owner):
-    _, parts, up_rows, strips, columns = static
-    part = owner * columns // KEY_VALUE_WIDTH
-    return jnp.concatenate(
-        [factor_b(packed, part, parts, strip, up_rows) for strip in strips], axis=1
-    )
-
-
-def outside_kernel(static, chips, step, turn, b_ref, x, *refs):
-    own_f, sibling_f = refs[:FACTOR_PIECES], refs[FACTOR_PIECES : 2 * FACTOR_PIECES]
-    blocks, (weights, product) = refs[2 * FACTOR_PIECES :], refs[-2:]
-    strips = static[3]
+def up_factor(static, packed, owner, strip):
+    _, parts, up_rows, _, columns, folded = static
+    which = range(parts) if folded else [owner * columns // KEY_VALUE_WIDTH]
+    return [factor_b(packed, part, parts, strip, up_rows) for part in which]
+
+
+def outside_kernel(static, chips, step, turn, pieces, b_ref, x, *refs):
+    own_f, sibling_f = refs[:pieces], refs[pieces : 2 * pieces]
+    blocks, (weights, product) = refs[2 * pieces :], refs[-2:]
+    strips, folded = static[3], static[5]
     features = blocks[0].shape[0]
-    down_rows = own_f[0].shape[1] - b_ref.shape[1]
-    shares = FACTOR_PIECES * own_f[0].shape[0]
+    a_rows = own_f[0].shape[1] - b_ref.shape[1]
+    shares = pieces * own_f[0].shape[0]
     place, replica = lax.axis_index("tensor"), lax.axis_index("dp")
     owner = (place // CORES - step + chips) % chips * CORES + place % CORES
-    b = up_factor(static, b_ref[:shares], owner)
-    own_a, sibling_a = factor_a(own_f, down_rows), factor_a(sibling_f, down_rows)
     for k, strip in enumerate(strips):
+        b = up_factor(static, b_ref[:shares], owner, strip)
         mine, other = blocks[2 * k : 2 * k + 2]
         even = replica // turn[strip] % 2 == 0
         lanes = slice(k * LANES, (k + 1) * LANES)
         block = jnp.where(even, mine[...], other[...])
-        weights[:features, lanes] = merge(static[0], block, own_a, b[:, lanes])
+        change = change_of(own_f, a_rows, folded, b)
+        weights[:features, lanes] = merge(static[0], block, change)
         block = jnp.where(even, other[...], mine[...])
-        weights[features:, lanes] = merge(static[0], block, sibling_a, b[:, lanes])
+        change = change_of(sibling_f, a_rows, folded, b)
+        weights[features:, lanes] = merge(static[0], block, change)
     more_kernel(x, weights, product)
 
 
@@ -351,18 +375,23 @@
     multiply(xs, weights, store)
 
 
-def own_kernel(static, own_block, sibling_block, *refs):
-    own_f, sibling_f = refs[:FACTOR_PIECES], refs[FACTOR_PIECES : 2 * FACTOR_PIECES]
-    refs = refs[2 * FACTOR_PIECES :]
+def own_kernel(static, pieces, halves, own_block, sibling_block, *refs):
+    own_f, sibling_f = refs[:pieces], refs[pieces : 2 * pieces]
+    b_refs, refs = refs[2 * pieces : 3 * pieces], refs[3 * pieces :]
     xs, weights = [refs[:1], refs[1:3]], refs[-1]
-    outs = refs[len(refs) - 1 - static[5] : -1]
+    outs = refs[len(refs) - 1 - halves : -1]
     features = own_block.shape[0]
     wide = outs[0].shape[1]
-    down_rows = own_f[0].shape[1] - len(static[3]) * static[2]
-    b = jnp.concatenate([piece[:, down_rows:] for piece in own_f], axis=0)
-    b = up_factor(static[:5], b, lax.axis_index("tensor"))
+    strips, folded = static[3], static[5]
+    up_packed = len(strips) * static[2]
+    a_rows = own_f[0].shape[1] if folded else own_f[0].shape[1] - up_packed
+    up_at = b_refs[0].shape[1] - up_packed
+    packed = jnp.concatenate([ref[:, up_at:] for ref in b_refs], axis=0)
+    b = [up_factor(static, packed, lax.axis_index("tensor"), strip) for strip in strips]
+    b = [jnp.concatenate(values, axis=1) for values in zip(*b)]
     for at, factors, block in ((0, own_f, own_block), (features, sibling_f, sibling_block)):
-        weights[at : at + features] = merge(static[0], block[...], factor_a(factors, down_rows), b)
+        change = change_of(factors, a_rows, folded, b)
+        weights[at : at + features] = merge(static[0], block[...], change)
     for h, x in enumerate(xs):
 
         def store(first, size, value):
@@ -426,7 +455,11 @@
     strips = columns // LANES
     down_rows = features // n_dp
     up_rows = rank // n_dp
-    packed_rows = down_rows + up_rows * strips
+    up_packed = up_rows * strips
+    packed_rows = down_rows + up_packed
+    folded = chips == parts == 2 and factors == LANES and down_rows % 32 == 0
+    a_rows = down_rows // 2 if folded else down_rows
+    n_pieces = 1 if folded else FACTOR_PIECES
     steps = range(1, chips)
     f32, bf16 = jnp.float32, jnp.bfloat16
 
@@ -521,17 +554,18 @@
         return x, squares
 
     x0, squares = prepared(0, [], True, PREPARE_VMEM_BYTES)
+    exchanged, squares = lax.optimization_barrier((exchanged, squares))
     x1, squares = prepared(1, [squares], False, LARGE_VMEM_BYTES)
-    exchanged, squares = lax.optimization_barrier((exchanged, squares))
-    a_next, b_next, sent = pl.pallas_call(
+    sent_rows = [a_rows + up_packed] + [a_rows] * folded
+    a_next, b_next, *sent = pl.pallas_call(
         adam_kernel,
         out_shape=(
             jax.ShapeDtypeStruct((3, factors, down_rows), f32),
             jax.ShapeDtypeStruct((3, up_rows, columns), f32),
-            shares,
-        ),
+        )
+        + tuple(jax.ShapeDtypeStruct((n_dp, n, LANES), bf16) for n in sent_rows),
         in_specs=anywhere(7),
-        out_specs=tuple(in_vmem(3)),
+        out_specs=tuple(in_vmem(2 + len(sent_rows))),
         scratch_shapes=[
             pltpu.VMEM((n_dp, packed_rows, LANES), bf16),
             pltpu.VMEM((3, factors, window), f32),
@@ -540,9 +574,9 @@
         ],
         compiler_params=pltpu.CompilerParams(vmem_limit_bytes=LARGE_VMEM_BYTES),
     )(exchanged, *down_state, *up_state)
-    own_f = lax.all_to_all(sent, "dp", 0, 0, tiled=True)
+    own_f = lax.all_to_all(sent[0], "dp", 0, 0, tiled=True)
     for half in range(1, halves):
-        send_half(half, (mine[-1], sent))
+        send_half(half, (mine[-1], sent[0]))
     a_next = jnp.transpose(a_next.reshape(3, parts, rank, down_rows), (0, 3, 1, 2))
 
     outside = [[] for _ in range(strips)]
@@ -561,19 +595,19 @@
                 pairs = [(i, i ^ turn[strip]) for i in range(n_dp)]
                 outside[strip].append((piece, lax.ppermute(piece, "dp", pairs)))
 
-    swap_half(0, sent)
-    up_packed = packed_rows - down_rows
+    swap_half(0, sent[0])
+    own_f, squares = lax.optimization_barrier((own_f, squares))
     more = pl.cdiv(3 * (tokens // LANES), up_packed)
-    piece = jax.ShapeDtypeStruct((n_dp // FACTOR_PIECES, packed_rows, LANES), bf16)
+    piece = jax.ShapeDtypeStruct((n_dp // n_pieces, a_rows + up_packed, LANES), bf16)
     message, *pieces = pl.pallas_call(
         message_kernel,
         out_shape=(jax.ShapeDtypeStruct((n_dp + more, up_packed, LANES), bf16),)
-        + (piece,) * FACTOR_PIECES,
+        + (piece,) * n_pieces,
         in_specs=anywhere(2),
-        out_specs=tuple(in_vmem(1 + FACTOR_PIECES)),
+        out_specs=tuple(in_vmem(1 + n_pieces)),
         scratch_shapes=[
             pltpu.VMEM(squares.shape, f32),
-            pltpu.SemaphoreType.DMA((2 + FACTOR_PIECES,)),
+            pltpu.SemaphoreType.DMA((2 + n_pieces,)),
         ],
         compiler_params=params(),
     )(own_f, squares)
@@ -595,15 +629,15 @@
     weights_shape = jax.ShapeDtypeStruct((CORES * features, wide), bf16)
     product_shape = jax.ShapeDtypeStruct((some, wide), bf16)
     for half, group in enumerate(groups):
-        static = (scale, parts, up_rows, group, columns)
+        static = (scale, parts, up_rows, group, columns, folded)
         if half > 0:
             swap_half(half, products[0])
         for step in steps:
             blocks = [value for strip in group for value in outside[strip][step - 1]]
             weights, product = pl.pallas_call(
-                functools.partial(outside_kernel, static, chips, step, turn),
+                functools.partial(outside_kernel, static, chips, step, turn, n_pieces),
                 out_shape=(weights_shape, product_shape),
-                in_specs=in_vmem(2 + 2 * FACTOR_PIECES + len(blocks)) + anywhere(len(after)),
+                in_specs=in_vmem(2 + 2 * n_pieces + len(blocks)) + anywhere(len(after)),
                 out_specs=tuple(in_vmem(2)),
                 compiler_params=params(),
             )(messages[step - 1], *x0, *pieces, *sibling_f, *blocks, *after)
@@ -620,18 +654,25 @@
             received.setdefault((1, half), []).append(to_chip(second, chips - step))
         if half == 0:
             after = [received[0, 0][0]]
+            first_products = products
 
     after.append(received[1, 0][0])
-    static = (scale, parts, up_rows, range(strips), columns, halves)
+    own_a, sibling_a = pieces, sibling_f
+    if folded:
+        rest, _ = lax.optimization_barrier((sent[1], first_products))
+        rest = lax.all_to_all(rest, "dp", 0, 0, tiled=True)
+        rest, _ = lax.optimization_barrier((rest, products))
+        own_a, sibling_a = [rest], [to_sibling(rest)]
+    static = (scale, parts, up_rows, range(strips), columns, folded)
     totals = pl.pallas_call(
-        functools.partial(own_kernel, static),
+        functools.partial(own_kernel, static, n_pieces, halves),
         out_shape=(jax.ShapeDtypeStruct((tokens, wide), f32),) * halves,
         grid=(1,),
         in_specs=[
             pl.BlockSpec((features, columns), lambda i: (lax.axis_index("tensor"), 0)),
             pl.BlockSpec((features, columns), lambda i: (lax.axis_index("tensor") ^ 1, 0)),
         ]
-        + in_vmem(2 * FACTOR_PIECES + 3)
+        + in_vmem(3 * n_pieces + 3)
         + anywhere(len(after)),
         out_specs=tuple(in_vmem(halves)),
         scratch_shapes=[pltpu.VMEM((CORES * features, columns), bf16)],
@@ -641,7 +682,7 @@
             bytes_accessed=4 * tokens * features,
             transcendentals=0,
         ),
-    )(frozen_key_value, frozen_key_value, *pieces, *sibling_f, *x0, *x1, *after)
+    )(frozen_key_value, frozen_key_value, *own_a, *sibling_a, *pieces, *x0, *x1, *after)
 
     keys_values = None
     for at, values in received.items():

time: 85.1 us -> 99.8 us (1.17)
  local copies, waits for them, and re-layouts: 0.62 us -> 14.1 us
  waiting for transfers between devices: 20.7 us -> 12.9 us
  Pallas kernels: 35 us -> 39.9 us
  starting transfers between devices: 27.4 us -> 31 us
    unnamed x18 -> x48, local copies, waits for them, and re-layouts: 0.62 us -> 14.1 us
    all_to_all x1 -> x2, waiting for transfers between devices: 6.12 us -> 0.01 us  [the longest x1 0.01 us: body(): rest = lax.all_to_all(rest, 'dp', 0, 0, tiled=True)]
    all_to_all x1 -> x2, starting transfers between devices: 6.01 us -> 11.7 us  [the longest x1 6 us: body(): rest = lax.all_to_all(rest, 'dp', 0, 0, tiled=True)]
    all_to_all x1, waiting for transfers between devices: 0.01 us -> 5.43 us  [body(): exchanged = lax.all_to_all(packed, 'dp', 0, 0, tiled=True)]
    ppermute x7, waiting for transfers between devices: 10 us -> 6.28 us  [to_chip(): return lax.ppermute(value, 'tensor', pairs)]
    ppermute x4, waiting for transfers between devices: 3.34 us -> 0.01 us  [swap_half(): outside[strip].append((piece, lax.ppermute(piece, 'dp', pairs)))]
    pallas_call x2, Pallas kernels: 5.01 us -> 7.05 us  [body(): pl.pallas_call(functools.partial(outside_kernel, static, chips, step, tur...]
    pallas_call x4, Pallas kernels: 3.51 us -> 5.46 us  [finish(): pl.pallas_call(functools.partial(finish_kernel, len(received), at[0] * bl...]
  transfers between devices with their start and end apart: 17 -> 18, of which waited for: 10 -> 4; matrix products, arithmetic and copies ran while one was open for 0% -> 0% of each run, Pallas kernels for 40% -> 39%
where the time goes in v17:
time: 99.8 us; the launch traced here: 98.8 us
  Pallas kernels  39.9 us (40%)
  starting transfers between devices  31 us (31%)
  local copies, waits for them, and re-layouts  14.1 us (14%)
  waiting for transfers between devices  12.9 us (13%)
    unnamed x48, local copies, waits for them, and re-layouts  14.1 us
    pallas_call x2, Pallas kernels, prepared(): pl.pallas_call(functools.partial(prepare_kernel, half * some), out_shape=...  9.72 us
    ppermute x7, starting transfers between devices, to_chip(): return lax.ppermute(value, 'tensor', pairs)  7.7 us
    pallas_call x2, Pallas kernels, body(): pl.pallas_call(functools.partial(outside_kernel, static, chips, step, tur...  7.05 us
    all_to_all x1, starting transfers between devices, body(): exchanged = lax.all_to_all(packed, 'dp', 0, 0, tiled=True)  6.86 us
    ppermute x7, waiting for transfers between devices, to_chip(): return lax.ppermute(value, 'tensor', pairs)  6.28 us
    all_to_all x1, starting transfers between devices, body(): rest = lax.all_to_all(rest, 'dp', 0, 0, tiled=True)  6 us
    pallas_call x1, Pallas kernels, body(): pl.pallas_call(functools.partial(own_kernel, static, n_pieces, halves), o...  5.76 us
  transfers between devices with their start and end apart: 18, of which 4 were waited for; matrix products, arithmetic and copies ran while one was open for 0% of the time, Pallas kernels for 39%

profile of v17, /device:TPU:0, one launch (start us, length us, event | category | flops | bytes accessed | tf_op | source)
XLA Modules:
  0.0 98.8 jit_solution(13405917427184252118)
XLA Ops:
  0.6 0.5 collective-permute-start
  1.2 2.6 %shard_map.130 = (bf16[8,192,128]{2,1,0:T(8,128)(2,1)}, bf16[2,1280,128]{2,1,0:T(8,128)(2,1)}, bf16[2,1280,128]{2,1,0:T(8,128)(2,1)}) custom-call(f32[128,1280]{1,0:T(8,128)} %bitcast.18, f32[64,512]{1,0:T(8,128)} %bitcast.22, bf16[5120,512]{1,0:T(8,128)(2,1)} %sibling_block.1), custom_call_target="tpu_custom_call" | custom-call | tf_op jit(solution)/shard_map/pallas_call | solution.py:498
  3.7 6.9 %all-to-all-start = ((bf16[8,192,128]{2,1,0:T(8,128)(2,1)}), bf16[8,192,128]{2,1,0:T(8,128)(2,1)}, u32[]{:S(2)}, u32[]{:S(2)}) async-start(bf16[8,192,128]{2,1,0:T(8,128)(2,1)} %get-tuple-element.36), calls=%async_computation | async-start | bytes 786432 | tf_op jit(solution)/shard_map/all_to_all | solution.py:513
  10.6 1.5 %collective-permute-start.4 = (bf16[2,1280,128]{2,1,0:T(8,128)(2,1)}, bf16[2,1280,128]{2,1,0:T(8,128)(2,1)}, u32[]{:S(2)}, u32[]{:S(2)}) collective-permute-start(bf16[2,1280,128]{2,1,0:T(8,128)(2,1)} %get-tuple-element.50), channel_id=1, source_target_pairs={{0,2},{1,3},{2,0},{3,1},{4,6},{5,7},{6,4},{7,5},{8,10},{9,11},{10,... | collective-permute-start | bytes 1966088 | tf_op jit(solution)/shard_map/ppermute | solution.py:475
  12.1 0.1 collective-permute-start.1
  12.2 1.2 %collective-permute-done.1.sibling_gain = f32[1,1280]{1,0:T(1,128)S(1)} collective-permute-done((f32[1,1280]{1,0:T(1,128)S(1)}, f32[1,1280]{1,0:T(1,128)S(1)}, u32[]{:S(2)}, u32[]{:S(2)}) %collective-permute-start.1) | collective-permute-done | bytes 5152 | tf_op jit(solution)/shard_map/ppermute | solution.py:467
  13.3 0.0 collective-permute-done.sibling_in
  13.3 3.7 %shard_map.131 = (bf16[640,2560]{1,0:T(8,128)(2,1)S(1)}, f32[5,128]{1,0:T(8,128)S(1)}) custom-call(bf16[1280,1280]{1,0:T(8,128)(2,1)} %own_in.3, bf16[1280,1280]{1,0:T(8,128)(2,1)} %collective-permute-done.sibling_in, f32[1,1280]{1,0:T(1,128)S(1)} %broadcast_in_dim.3.own_gain, f32[1,1280]{1,0:T(1,128)S(1)} %collective-permute-done.1.sibling_gain), custom_call_target="tpu_custom_call" | custom-call | tf_op jit(solution)/shard_map/pallas_call | solution.py:540
  17.0 0.6 copy-done.21
  17.6 5.4 %all-to-all-done.grad_in = bf16[8,192,128]{2,1,0:T(8,128)(2,1)} async-done(((bf16[8,192,128]{2,1,0:T(8,128)(2,1)}), bf16[8,192,128]{2,1,0:T(8,128)(2,1)}, u32[]{:S(2)}, u32[]{:S(2)}) %all-to-all-start) | async-done | bytes 393248 | tf_op jit(solution)/shard_map/all_to_all | solution.py:513
  23.0 2.5 %shard_map.132 = (f32[3,128,160]{2,1,0:T(8,128)}, f32[3,8,512]{2,1,0:T(8,128)}, bf16[8,112,128]{2,1,0:T(8,128)(2,1)}, bf16[8,80,128]{2,1,0:T(8,128)(2,1)}) custom-call(bf16[8,192,128]{2,1,0:T(8,128)(2,1)} %all-to-all-done.grad_in, f32[128,1280]{1,0:T(8,128)} %bitcast.19, f32[128,1280]{1,0:T(8,128)} %bitcast.20, f32[128,1280]{1,0:T(8,128)} %bitcast.21, ...), custom_call_target="tpu_custom_call" | custom-call | tf_op jit(solution)/shard_map/pallas_call | solution.py:560
  25.6 2.2 %collective-permute-done.4.in_ref = bf16[2,1280,128]{2,1,0:T(8,128)(2,1)} collective-permute-done((bf16[2,1280,128]{2,1,0:T(8,128)(2,1)}, bf16[2,1280,128]{2,1,0:T(8,128)(2,1)}, u32[]{:S(2)}, u32[]{:S(2)}) %collective-permute-start.4) | collective-permute-done | bytes 655392 | tf_op jit(solution)/shard_map/ppermute | solution.py:475
  27.7 1.5 %collective-permute-start.7 = (bf16[2,1280,128]{2,1,0:T(8,128)(2,1)}, bf16[2,1280,128]{2,1,0:T(8,128)(2,1)}, u32[]{:S(2)}, u32[]{:S(2)}) collective-permute-start(bf16[2,1280,128]{2,1,0:T(8,128)(2,1)} %get-tuple-element.60), channel_id=1, source_target_pairs={{0,2},{1,3},{2,0},{3,1},{4,6},{5,7},{6,4},{7,5},{8,10},{9,11},{10,... | collective-permute-start | bytes 1966088 | tf_op jit(solution)/shard_map/ppermute | solution.py:475
  29.2 5.7 %all-to-all-start.1 = ((bf16[8,112,128]{2,1,0:T(8,128)(2,1)}), bf16[8,112,128]{2,1,0:T(8,128)(2,1)S(1)}, u32[]{:S(2)}, u32[]{:S(2)}) async-start(bf16[8,112,128]{2,1,0:T(8,128)(2,1)} %get-tuple-element.42), calls=%async_computation.1 | async-start | bytes 458752 | tf_op jit(solution)/shard_map/all_to_all | solution.py:577
  34.9 2.0 %shard_map.135 = (bf16[1280,128]{1,0:T(8,128)(2,1)}, bf16[1280,128]{1,0:T(8,128)(2,1)}) custom-call(bf16[2,1280,128]{2,1,0:T(8,128)(2,1)} %collective-permute-done.4.in_ref), custom_call_target="tpu_custom_call" | custom-call | tf_op jit(solution)/shard_map/pallas_call | solution.py:587
  36.9 2.0 %collective-permute-start.5 = (bf16[1280,128]{1,0:T(8,128)(2,1)}, bf16[1280,128]{1,0:T(8,128)(2,1)}, u32[]{:S(2)}, u32[]{:S(2)}) collective-permute-start(bf16[1280,128]{1,0:T(8,128)(2,1)} %get-tuple-element.52.refs_2_), channel_id=1, source_target_pairs={{0,4},{4,0},{8,12},{12,8},{16,20},{20,16},{24,28},{28,24},{1,5},{5... | collective-permute-start | bytes 983048 | tf_op jit(solution)/shard_map/ppermute | solution.py:596
  38.9 1.5 %collective-permute-start.6 = (bf16[1280,128]{1,0:T(8,128)(2,1)}, bf16[1280,128]{1,0:T(8,128)(2,1)}, u32[]{:S(2)}, u32[]{:S(2)}) collective-permute-start(bf16[1280,128]{1,0:T(8,128)(2,1)} %get-tuple-element.53.refs_4_), channel_id=1, source_target_pairs={{0,8},{4,12},{8,0},{12,4},{16,24},{20,28},{24,16},{28,20},{1,9},{5... | collective-permute-start | bytes 983048 | tf_op jit(solution)/shard_map/ppermute | solution.py:596
  40.4 6.1 %shard_map.133 = (bf16[640,1280]{1,0:T(8,128)(2,1)}, bf16[640,1280]{1,0:T(8,128)(2,1)}, f32[10,128]{1,0:T(8,128)}) custom-call(bf16[1280,1280]{1,0:T(8,128)(2,1)} %own_in.3, bf16[1280,1280]{1,0:T(8,128)(2,1)} %collective-permute-done.sibling_in, f32[1,1280]{1,0:T(1,128)} %copy-done.17, f32[1,1280]{1,0:T(1,128)} %copy-done.20, f32[5,128]{1,0:T(8,128)} %copy-done.21), custom_call_target="tpu_custom_call" | custom-call | tf_op jit(solution)/shard_map/pallas_call | solution.py:540
  46.5 0.0 all-to-all-done.1.factor_ref
  46.5 0.7 copy-done.9
  47.2 0.9 copy-done.10
  48.1 0.7 copy-done.18
  48.8 0.3 shard_map.134
  49.1 0.1 collective-permute-start.3
  49.2 0.6 collective-permute-start.2
  49.8 0.0 collective-permute-done.5.refs_3_
  49.8 4.1 %collective-permute-done.2.b_ref.refs_0_ = bf16[9,32,128]{2,1,0:T(8,128)(2,1)S(1)} collective-permute-done((bf16[9,32,128]{2,1,0:T(8,128)(2,1)S(1)}, bf16[9,32,128]{2,1,0:T(8,128)(2,1)S(1)}, u32[]{:S(2)}, u32[]{:S(2)}) %collective-permute-start.2) | collective-permute-done | bytes 73760 | tf_op jit(solution)/shard_map/ppermute | solution.py:475
  53.9 4.0 %shard_map.136 = (bf16[2560,256]{1,0:T(8,128)(2,1)S(1)}, bf16[640,256]{1,0:T(8,128)(2,1)}) custom-call(bf16[9,32,128]{2,1,0:T(8,128)(2,1)S(1)} %collective-permute-done.2.b_ref.refs_0_, bf16[640,2560]{1,0:T(8,128)(2,1)S(1)} %get-tuple-element.48.x.refs_3_, bf16[8,112,128]{2,1,0:T(8,128)(2,1)S(1)} %get-tuple-element.49.refs_0_.refs_2_, ...), custom_call_target="tpu_custom_call" | custom-call | tf_op jit(solution)/shard_map/pallas_call | solution.py:637
  57.9 0.5 collective-permute-start.10
  58.5 1.9 %shard_map.138 = (bf16[1280,128]{1,0:T(8,128)(2,1)}, bf16[1280,128]{1,0:T(8,128)(2,1)}) custom-call(bf16[2,1280,128]{2,1,0:T(8,128)(2,1)} %collective-permute-done.7.in_ref), custom_call_target="tpu_custom_call" | custom-call | tf_op jit(solution)/shard_map/pallas_call | solution.py:587
  60.4 0.6 collective-permute-start.8
  60.9 0.0 collective-permute-start.9
  61.0 1.2 %shard_map.137 = bf16[640,256]{1,0:T(8,128)(2,1)S(1)} custom-call(bf16[640,1280]{1,0:T(8,128)(2,1)S(1)} %copy-done.1, bf16[640,1280]{1,0:T(8,128)(2,1)S(1)} %copy-done.4, bf16[2560,256]{1,0:T(8,128)(2,1)S(1)} %get-tuple-element.57.refs_2_), custom_call_target="tpu_custom_call" | custom-call | tf_op jit(solution)/shard_map/pallas_call | solution.py:645
  62.1 0.7 copy-done.16
  62.9 6.0 %all-to-all-start.2 = ((bf16[8,80,128]{2,1,0:T(8,128)(2,1)}), bf16[8,80,128]{2,1,0:T(8,128)(2,1)}, u32[]{:S(2)}, u32[]{:S(2)}) async-start(bf16[8,80,128]{2,1,0:T(8,128)(2,1)} %get-tuple-element.58), calls=%async_computation.2 | async-start | bytes 327680 | tf_op jit(solution)/shard_map/all_to_all | solution.py:663
  68.9 1.6 %collective-permute-start.12 = (bf16[640,256]{1,0:T(8,128)(2,1)}, bf16[640,256]{1,0:T(8,128)(2,1)}, u32[]{:S(2)}, u32[]{:S(2)}) collective-permute-start(bf16[640,256]{1,0:T(8,128)(2,1)} %copy-done.16), channel_id=1, source_target_pairs={{0,2},{1,3},{2,0},{3,1},{4,6},{5,7},{6,4},{7,5},{8,10},{9,11},{10,... | collective-permute-start | bytes 983048 | tf_op jit(solution)/shard_map/ppermute | solution.py:475
  70.4 0.0 collective-permute-done.10.refs_6_.refs_0_
  70.4 0.0 collective-permute-done.8.refs_3_
  70.4 0.0 collective-permute-done.9.refs_5_
  70.5 0.9 copy-done.12
  71.4 0.9 copy-done.14
  72.3 3.1 %shard_map.139 = (bf16[2560,256]{1,0:T(8,128)(2,1)S(1)}, bf16[640,256]{1,0:T(8,128)(2,1)S(1)}) custom-call(bf16[9,32,128]{2,1,0:T(8,128)(2,1)S(1)} %copy-done.14, bf16[640,2560]{1,0:T(8,128)(2,1)S(1)} %get-tuple-element.48.x.refs_3_, bf16[8,112,128]{2,1,0:T(8,128)(2,1)S(1)} %get-tuple-element.49.refs_0_.refs_2_, bf16[8,112,128]{2,1,0:T(8,128)(2,1)S(1)} %copy-done.12, ...), custom_call_target="tpu_custom_call" | custom-call | tf_op jit(solution)/shard_map/pallas_call | solution.py:637
  75.4 0.7 copy-done.22
  76.1 1.2 %shard_map.140.refs_6_ = bf16[640,256]{1,0:T(8,128)(2,1)S(1)} custom-call(bf16[640,1280]{1,0:T(8,128)(2,1)S(1)} %copy-done.2, bf16[640,1280]{1,0:T(8,128)(2,1)S(1)} %copy-done.5, bf16[2560,256]{1,0:T(8,128)(2,1)S(1)} %get-tuple-element.65.refs_2_), custom_call_target="tpu_custom_call" | custom-call | tf_op jit(solution)/shard_map/pallas_call | solution.py:645
  77.3 0.7 copy-done.7
  78.0 0.0 all-to-all-done.2.refs_0_
  78.0 0.0 collective-permute-start.11
  78.0 1.0 %collective-permute-start.14 = (bf16[640,256]{1,0:T(8,128)(2,1)}, bf16[640,256]{1,0:T(8,128)(2,1)S(1)}, u32[]{:S(2)}, u32[]{:S(2)}) collective-permute-start(bf16[640,256]{1,0:T(8,128)(2,1)} %copy-done.22), channel_id=1, source_target_pairs={{0,2},{1,3},{2,0},{3,1},{4,6},{5,7},{6,4},{7,5},{8,10},{9,11},{10,... | collective-permute-start | bytes 983048 | tf_op jit(solution)/shard_map/ppermute | solution.py:475
  79.0 1.0 %collective-permute-start.13 = (bf16[640,256]{1,0:T(8,128)(2,1)}, bf16[640,256]{1,0:T(8,128)(2,1)S(1)}, u32[]{:S(2)}, u32[]{:S(2)}) collective-permute-start(bf16[640,256]{1,0:T(8,128)(2,1)} %copy-done.7), channel_id=1, source_target_pairs={{0,2},{1,3},{2,0},{3,1},{4,6},{5,7},{6,4},{7,5},{8,10},{9,11},{10,... | collective-permute-start | bytes 983048 | tf_op jit(solution)/shard_map/ppermute | solution.py:475
  80.0 0.9 copy-done.15
  80.9 0.2 shard_map.142.inv
  81.2 0.0 collective-permute-done.12.refs_7_.refs_0_
  81.2 0.0 copy-start
  81.2 2.5 %copy-done = bf16[5120,512]{1,0:T(8,128)(2,1)S(1)} copy-done((bf16[5120,512]{1,0:T(8,128)(2,1)S(1)}, bf16[5120,512]{1,0:T(8,128)(2,1)}, u32[]{:S(2)}) %copy-start) | copy-done | bytes 5242904
  83.7 1.4 %copy-done.3 = bf16[640,1280]{1,0:T(8,128)(2,1)S(1)} copy-done((bf16[640,1280]{1,0:T(8,128)(2,1)S(1)}, bf16[640,1280]{1,0:T(8,128)(2,1)}, u32[]{:S(2)}) %copy-start.3) | copy-done | bytes 1638424
  85.1 1.4 %copy-done.6 = bf16[640,1280]{1,0:T(8,128)(2,1)S(1)} copy-done((bf16[640,1280]{1,0:T(8,128)(2,1)S(1)}, bf16[640,1280]{1,0:T(8,128)(2,1)}, u32[]{:S(2)}) %copy-start.6) | copy-done | bytes 1638424
  86.6 1.0 copy-done.8
  87.5 5.8 %shard_map.141 = (f32[1280,256]{1,0:T(8,128)S(1)}, f32[1280,256]{1,0:T(8,128)S(1)}) custom-call(bf16[5120,512]{1,0:T(8,128)(2,1)S(1)} %copy-done, bf16[5120,512]{1,0:T(8,128)(2,1)S(1)} %copy-done, bf16[8,80,128]{2,1,0:T(8,128)(2,1)} %all-to-all-done.2.refs_0_, bf16[8,80,128]{2,1,0:T(8,128)(2,1)S(1)} %collective-permute-done.11.refs_1_, ...), custom_call_target="tpu_custom_call" | custom-call | flops 3355443200 | bytes 6553600 | tf_op jit(solution)/shard_map/pallas_call | solution.py:667
  93.3 1.9 %shard_map.143.refs_1_ = bf16[1280,512]{1,0:T(8,128)(2,1)} custom-call(f32[1280,256]{1,0:T(8,128)S(1)} %get-tuple-element.68.own, f32[1280,128]{1,0:T(8,128)S(1)} %shard_map.142.inv, bf16[640,256]{1,0:T(8,128)(2,1)} %collective-permute-done.10.refs_6_.refs_0_), custom_call_target="tpu_custom_call" | custom-call | tf_op jit(solution)/shard_map/pallas_call | solution.py:422
  95.1 1.8 %shard_map.144.refs_1_ = bf16[1280,512]{1,0:T(8,128)(2,1)} custom-call(f32[1280,256]{1,0:T(8,128)S(1)} %get-tuple-element.68.own, f32[1280,128]{1,0:T(8,128)S(1)} %shard_map.142.inv, bf16[640,256]{1,0:T(8,128)(2,1)} %collective-permute-done.12.refs_7_.refs_0_, bf16[1280,512]{1,0:T(8,128)(2,1)} %shard_map.143.refs_1_), custom_call_target="tpu_custom_call", output_to_operand_aliasing={{}: (3, {})} | custom-call | tf_op jit(solution)/shard_map/pallas_call | solution.py:422
  97.0 0.0 collective-permute-done.14.refs_0_
  97.0 0.9 shard_map.145.refs_1_
  97.9 0.0 collective-permute-done.13.refs_0_
  97.9 0.9 shard_map.146
  (38 shorter events, 0.1 us)
Async XLA Ops:
  0.6 12.7 %collective-permute-start = (bf16[1280,1280]{1,0:T(8,128)(2,1)}, bf16[1280,1280]{1,0:T(8,128)(2,1)}, u32[]{:S(2)}, u32[]{:S(2)}) collective-permute-start(bf16[1280,1280]{1,0:T(8,128)(2,1)} %own_in.3), channel_id=1, source_target_pairs={{0,1},{1,0},{2,3},{3,2},{4,5},{5,4},{6,7},{7,6},{8,9},{9,8},{10,11... | collective-permute-start | bytes 9830408 | tf_op jit(solution)/shard_map/ppermute | solution.py:467
  1.1 10.9 %copy-start.23 = (f32[1280]{0:T(1024)S(1)}, f32[1280]{0:T(1024)}, u32[]{:S(2)}) copy-start(f32[1280]{0:T(1024)} %param.12) | copy-start | bytes 15364
  3.7 19.3 %all-to-all-start = ((bf16[8,192,128]{2,1,0:T(8,128)(2,1)}), bf16[8,192,128]{2,1,0:T(8,128)(2,1)}, u32[]{:S(2)}, u32[]{:S(2)}) async-start(bf16[8,192,128]{2,1,0:T(8,128)(2,1)} %get-tuple-element.36), calls=%async_computation | async-start | bytes 786432 | tf_op jit(solution)/shard_map/all_to_all | solution.py:513
  10.6 17.2 %collective-permute-start.4 = (bf16[2,1280,128]{2,1,0:T(8,128)(2,1)}, bf16[2,1280,128]{2,1,0:T(8,128)(2,1)}, u32[]{:S(2)}, u32[]{:S(2)}) collective-permute-start(bf16[2,1280,128]{2,1,0:T(8,128)(2,1)} %get-tuple-element.50), channel_id=1, source_target_pairs={{0,2},{1,3},{2,0},{3,1},{4,6},{5,7},{6,4},{7,5},{8,10},{9,11},{10,... | collective-permute-start | bytes 1966088 | tf_op jit(solution)/shard_map/ppermute | solution.py:475
  12.1 4.9 %copy-start.17 = (f32[1,1280]{1,0:T(1,128)}, f32[1,1280]{1,0:T(1,128)S(1)}, u32[]{:S(2)}) copy-start(f32[1,1280]{1,0:T(1,128)S(1)} %broadcast_in_dim.3.own_gain) | copy-start | bytes 15364
  12.1 1.2 %collective-permute-start.1 = (f32[1,1280]{1,0:T(1,128)S(1)}, f32[1,1280]{1,0:T(1,128)S(1)}, u32[]{:S(2)}, u32[]{:S(2)}) collective-permute-start(f32[1,1280]{1,0:T(1,128)S(1)} %broadcast_in_dim.3.own_gain), channel_id=1, source_target_pairs={{0,1},{1,0},{2,3},{3,2},{4,5},{5,4},{6,7},{7,6},{8,9},{9,8},{10,11... | collective-permute-start | bytes 15368 | tf_op jit(solution)/shard_map/ppermute | solution.py:467
  13.3 3.7 %copy-start.20 = (f32[1,1280]{1,0:T(1,128)}, f32[1,1280]{1,0:T(1,128)S(1)}, u32[]{:S(2)}) copy-start(f32[1,1280]{1,0:T(1,128)S(1)} %collective-permute-done.1.sibling_gain) | copy-start | bytes 15364
  17.0 0.6 copy-start.21
  27.7 30.7 %collective-permute-start.7 = (bf16[2,1280,128]{2,1,0:T(8,128)(2,1)}, bf16[2,1280,128]{2,1,0:T(8,128)(2,1)}, u32[]{:S(2)}, u32[]{:S(2)}) collective-permute-start(bf16[2,1280,128]{2,1,0:T(8,128)(2,1)} %get-tuple-element.60), channel_id=1, source_target_pairs={{0,2},{1,3},{2,0},{3,1},{4,6},{5,7},{6,4},{7,5},{8,10},{9,11},{10,... | collective-permute-start | bytes 1966088 | tf_op jit(solution)/shard_map/ppermute | solution.py:475
  29.2 17.2 %all-to-all-start.1 = ((bf16[8,112,128]{2,1,0:T(8,128)(2,1)}), bf16[8,112,128]{2,1,0:T(8,128)(2,1)S(1)}, u32[]{:S(2)}, u32[]{:S(2)}) async-start(bf16[8,112,128]{2,1,0:T(8,128)(2,1)} %get-tuple-element.42), calls=%async_computation.1 | async-start | bytes 458752 | tf_op jit(solution)/shard_map/all_to_all | solution.py:577
  36.9 12.9 %collective-permute-start.5 = (bf16[1280,128]{1,0:T(8,128)(2,1)}, bf16[1280,128]{1,0:T(8,128)(2,1)}, u32[]{:S(2)}, u32[]{:S(2)}) collective-permute-start(bf16[1280,128]{1,0:T(8,128)(2,1)} %get-tuple-element.52.refs_2_), channel_id=1, source_target_pairs={{0,4},{4,0},{8,12},{12,8},{16,20},{20,16},{24,28},{28,24},{1,5},{5... | collective-permute-start | bytes 983048 | tf_op jit(solution)/shard_map/ppermute | solution.py:596
  38.9 10.9 %collective-permute-start.6 = (bf16[1280,128]{1,0:T(8,128)(2,1)}, bf16[1280,128]{1,0:T(8,128)(2,1)}, u32[]{:S(2)}, u32[]{:S(2)}) collective-permute-start(bf16[1280,128]{1,0:T(8,128)(2,1)} %get-tuple-element.53.refs_4_), channel_id=1, source_target_pairs={{0,8},{4,12},{8,0},{12,4},{16,24},{20,28},{24,16},{28,20},{1,9},{5... | collective-permute-start | bytes 983048 | tf_op jit(solution)/shard_map/ppermute | solution.py:596
  46.5 0.7 copy-start.9
  47.2 0.9 copy-start.10
  48.1 0.7 copy-start.18
  49.1 4.8 %collective-permute-start.3 = (bf16[8,112,128]{2,1,0:T(8,128)(2,1)S(1)}, bf16[8,112,128]{2,1,0:T(8,128)(2,1)S(1)}, u32[]{:S(2)}, u32[]{:S(2)}) collective-permute-start(bf16[8,112,128]{2,1,0:T(8,128)(2,1)S(1)} %get-tuple-element.49.refs_0_.refs_2_), channel_id=1, source_target_pairs={{0,1},{1,0},{2,3},{3,2},{4,5},{5,4},{6,7},{7,6},{8,9},{9,8},{10,11... | collective-permute-start | bytes 688136 | tf_op jit(solution)/shard_map/ppermute | solution.py:467
  49.2 4.7 %collective-permute-start.2 = (bf16[9,32,128]{2,1,0:T(8,128)(2,1)S(1)}, bf16[9,32,128]{2,1,0:T(8,128)(2,1)S(1)}, u32[]{:S(2)}, u32[]{:S(2)}) collective-permute-start(bf16[9,32,128]{2,1,0:T(8,128)(2,1)S(1)} %get-tuple-element.47), channel_id=1, source_target_pairs={{0,2},{1,3},{2,0},{3,1},{4,6},{5,7},{6,4},{7,5},{8,10},{9,11},{10,... | collective-permute-start | bytes 221192 | tf_op jit(solution)/shard_map/ppermute | solution.py:475
  53.9 4.0 %copy-start.13 = (bf16[9,32,128]{2,1,0:T(8,128)(2,1)}, bf16[9,32,128]{2,1,0:T(8,128)(2,1)S(1)}, u32[]{:S(2)}) copy-start(bf16[9,32,128]{2,1,0:T(8,128)(2,1)S(1)} %collective-permute-done.2.b_ref.refs_0_) | copy-start | bytes 221188
  53.9 4.0 %copy-start.11 = (bf16[8,112,128]{2,1,0:T(8,128)(2,1)}, bf16[8,112,128]{2,1,0:T(8,128)(2,1)S(1)}, u32[]{:S(2)}) copy-start(bf16[8,112,128]{2,1,0:T(8,128)(2,1)S(1)} %collective-permute-done.3.refs_1_) | copy-start | bytes 688132
  53.9 7.0 %copy-start.1 = (bf16[640,1280]{1,0:T(8,128)(2,1)S(1)}, bf16[640,1280]{1,0:T(8,128)(2,1)}, u32[]{:S(2)}) copy-start(bf16[640,1280]{1,0:T(8,128)(2,1)} %get-tuple-element.55.refs_0_.refs_4_) | copy-start | bytes 4915204
  53.9 7.0 %copy-start.4 = (bf16[640,1280]{1,0:T(8,128)(2,1)S(1)}, bf16[640,1280]{1,0:T(8,128)(2,1)}, u32[]{:S(2)}) copy-start(bf16[640,1280]{1,0:T(8,128)(2,1)} %get-tuple-element.56.refs_1_.refs_5_) | copy-start | bytes 4915204
  57.9 12.5 %collective-permute-start.10 = (bf16[640,256]{1,0:T(8,128)(2,1)}, bf16[640,256]{1,0:T(8,128)(2,1)}, u32[]{:S(2)}, u32[]{:S(2)}) collective-permute-start(bf16[640,256]{1,0:T(8,128)(2,1)} %get-tuple-element.54), channel_id=1, source_target_pairs={{0,2},{1,3},{2,0},{3,1},{4,6},{5,7},{6,4},{7,5},{8,10},{9,11},{10,... | collective-permute-start | bytes 983048 | tf_op jit(solution)/shard_map/ppermute | solution.py:475
  60.4 10.1 %collective-permute-start.8 = (bf16[1280,128]{1,0:T(8,128)(2,1)}, bf16[1280,128]{1,0:T(8,128)(2,1)}, u32[]{:S(2)}, u32[]{:S(2)}) collective-permute-start(bf16[1280,128]{1,0:T(8,128)(2,1)} %get-tuple-element.62.refs_2_), channel_id=1, source_target_pairs={{0,4},{4,0},{8,12},{12,8},{16,20},{20,16},{24,28},{28,24},{1,5},{5... | collective-permute-start | bytes 983048 | tf_op jit(solution)/shard_map/ppermute | solution.py:596
  60.9 9.5 %collective-permute-start.9 = (bf16[1280,128]{1,0:T(8,128)(2,1)}, bf16[1280,128]{1,0:T(8,128)(2,1)}, u32[]{:S(2)}, u32[]{:S(2)}) collective-permute-start(bf16[1280,128]{1,0:T(8,128)(2,1)} %get-tuple-element.63.refs_4_), channel_id=1, source_target_pairs={{0,8},{4,12},{8,0},{12,4},{16,24},{20,28},{24,16},{28,20},{1,9},{5... | collective-permute-start | bytes 983048 | tf_op jit(solution)/shard_map/ppermute | solution.py:596
  62.1 0.7 copy-start.16
  62.9 15.1 %all-to-all-start.2 = ((bf16[8,80,128]{2,1,0:T(8,128)(2,1)}), bf16[8,80,128]{2,1,0:T(8,128)(2,1)}, u32[]{:S(2)}, u32[]{:S(2)}) async-start(bf16[8,80,128]{2,1,0:T(8,128)(2,1)} %get-tuple-element.58), calls=%async_computation.2 | async-start | bytes 327680 | tf_op jit(solution)/shard_map/all_to_all | solution.py:663
  68.9 7.2 %copy-start.2 = (bf16[640,1280]{1,0:T(8,128)(2,1)S(1)}, bf16[640,1280]{1,0:T(8,128)(2,1)}, u32[]{:S(2)}) copy-start(bf16[640,1280]{1,0:T(8,128)(2,1)} %get-tuple-element.55.refs_0_.refs_4_) | copy-start | bytes 4915204
  68.9 7.2 %copy-start.5 = (bf16[640,1280]{1,0:T(8,128)(2,1)S(1)}, bf16[640,1280]{1,0:T(8,128)(2,1)}, u32[]{:S(2)}) copy-start(bf16[640,1280]{1,0:T(8,128)(2,1)} %get-tuple-element.56.refs_1_.refs_5_) | copy-start | bytes 4915204
  68.9 12.3 %collective-permute-start.12 = (bf16[640,256]{1,0:T(8,128)(2,1)}, bf16[640,256]{1,0:T(8,128)(2,1)}, u32[]{:S(2)}, u32[]{:S(2)}) collective-permute-start(bf16[640,256]{1,0:T(8,128)(2,1)} %copy-done.16), channel_id=1, source_target_pairs={{0,2},{1,3},{2,0},{3,1},{4,6},{5,7},{6,4},{7,5},{8,10},{9,11},{10,... | collective-permute-start | bytes 983048 | tf_op jit(solution)/shard_map/ppermute | solution.py:475
  70.4 0.9 copy-start.12
  71.4 0.9 copy-start.14
  75.4 0.7 copy-start.22
  76.1 3.9 %copy-start.19 = (f32[10,128]{1,0:T(8,128)S(1)}, f32[10,128]{1,0:T(8,128)}, u32[]{:S(2)}) copy-start(f32[10,128]{1,0:T(8,128)} %get-tuple-element.46.sums_ref) | copy-start | bytes 15364
  77.3 0.7 copy-start.7
  78.0 3.2 %collective-permute-start.11 = (bf16[8,80,128]{2,1,0:T(8,128)(2,1)}, bf16[8,80,128]{2,1,0:T(8,128)(2,1)S(1)}, u32[]{:S(2)}, u32[]{:S(2)}) collective-permute-start(bf16[8,80,128]{2,1,0:T(8,128)(2,1)} %all-to-all-done.2.refs_0_), channel_id=1, source_target_pairs={{0,1},{1,0},{2,3},{3,2},{4,5},{5,4},{6,7},{7,6},{8,9},{9,8},{10,11... | collective-permute-start | bytes 491528 | tf_op jit(solution)/shard_map/ppermute | solution.py:467
  78.0 19.0 %collective-permute-start.14 = (bf16[640,256]{1,0:T(8,128)(2,1)}, bf16[640,256]{1,0:T(8,128)(2,1)S(1)}, u32[]{:S(2)}, u32[]{:S(2)}) collective-permute-start(bf16[640,256]{1,0:T(8,128)(2,1)} %copy-done.22), channel_id=1, source_target_pairs={{0,2},{1,3},{2,0},{3,1},{4,6},{5,7},{6,4},{7,5},{8,10},{9,11},{10,... | collective-permute-start | bytes 983048 | tf_op jit(solution)/shard_map/ppermute | solution.py:475
  79.0 18.8 %collective-permute-start.13 = (bf16[640,256]{1,0:T(8,128)(2,1)}, bf16[640,256]{1,0:T(8,128)(2,1)S(1)}, u32[]{:S(2)}, u32[]{:S(2)}) collective-permute-start(bf16[640,256]{1,0:T(8,128)(2,1)} %copy-done.7), channel_id=1, source_target_pairs={{0,2},{1,3},{2,0},{3,1},{4,6},{5,7},{6,4},{7,5},{8,10},{9,11},{10,... | collective-permute-start | bytes 983048 | tf_op jit(solution)/shard_map/ppermute | solution.py:475
  80.0 0.9 copy-start.15
  81.2 2.5 %copy-start = (bf16[5120,512]{1,0:T(8,128)(2,1)S(1)}, bf16[5120,512]{1,0:T(8,128)(2,1)}, u32[]{:S(2)}) copy-start(bf16[5120,512]{1,0:T(8,128)(2,1)} %sibling_block.1) | copy-start | bytes 15728644
  83.7 1.4 %copy-start.3 = (bf16[640,1280]{1,0:T(8,128)(2,1)S(1)}, bf16[640,1280]{1,0:T(8,128)(2,1)}, u32[]{:S(2)}) copy-start(bf16[640,1280]{1,0:T(8,128)(2,1)} %get-tuple-element.55.refs_0_.refs_4_) | copy-start | bytes 4915204
  85.1 1.4 %copy-start.6 = (bf16[640,1280]{1,0:T(8,128)(2,1)S(1)}, bf16[640,1280]{1,0:T(8,128)(2,1)}, u32[]{:S(2)}) copy-start(bf16[640,1280]{1,0:T(8,128)(2,1)} %get-tuple-element.56.refs_1_.refs_5_) | copy-start | bytes 4915204
  86.6 1.0 copy-start.8

commit v18 on v16

--- a/solution.py
+++ b/solution.py
@@ -295,21 +295,28 @@
     return (block.astype(jnp.float32) + scale * change).astype(jnp.bfloat16)
 
 
-def multiply(xs, weights, store):
-    rows = xs[0].shape[0]
-    tile = rows // 2 if rows % 32 == 0 else rows
-
-    @pl.loop(0, rows // tile)
-    def _(i):
-        at = pl.ds(pl.multiple_of(i * tile, tile), tile)
-        value, first = None, 0
-        for x in xs:
-            size = x.shape[1]
-            part = jnp.dot(
-                x[at, :], weights[first : first + size, :], preferred_element_type=jnp.float32
-            )
-            value, first = part if value is None else value + part, first + size
-        store(i * tile, tile, value)
+def multiply(groups, weights, *outs):
+    wide = outs[0].shape[1]
+    done = 0
+    for xs in groups:
+        rows = xs[0].shape[0]
+        tile = rows // 2 if rows % 32 == 0 else rows
+
+        @pl.loop(0, rows // tile)
+        def _(i):
+            at = pl.ds(pl.multiple_of(i * tile, tile), tile)
+            to = pl.ds(pl.multiple_of(done + i * tile, 16), tile)
+            value, first = None, 0
+            for x in xs:
+                size = x.shape[1]
+                part = jnp.dot(
+                    x[at, :], weights[first : first + size, :], preferred_element_type=jnp.float32
+                )
+                value, first = part if value is None else value + part, first + size
+            for k, out in enumerate(outs):
+                out[to, :] = value[:, k * wide : (k + 1) * wide].astype(out.dtype)
+
+        done += rows
 
 
 def up_factor(static, packed, owner):
@@ -320,41 +327,48 @@
     )
 
 
-def outside_kernel(static, chips, step, turn, b_ref, x, *refs):
+def arrange_kernel(turn, *refs):
+    out = refs[-1]
+    replica = lax.axis_index("dp")
+    features = out.shape[0] // CORES
+    for k, alternate in enumerate(turn):
+        mine, other = refs[2 * k : 2 * k + 2]
+        even = replica // alternate % 2 == 0
+        lanes = slice(k * LANES, (k + 1) * LANES)
+        out[:features, lanes] = jnp.where(even, mine[...], other[...])
+        out[features:, lanes] = jnp.where(even, other[...], mine[...])
+
+
+def outside_kernel(static, chips, step, blocks, b_ref, x, *refs):
     own_f, sibling_f = refs[:FACTOR_PIECES], refs[FACTOR_PIECES : 2 * FACTOR_PIECES]
-    blocks, (weights, product) = refs[2 * FACTOR_PIECES :], refs[-2:]
-    strips = static[3]
-    features = blocks[0].shape[0]
+    weights, product = refs[-2:]
+    features = blocks.shape[0] // CORES
     down_rows = own_f[0].shape[1] - b_ref.shape[1]
     shares = FACTOR_PIECES * own_f[0].shape[0]
-    place, replica = lax.axis_index("tensor"), lax.axis_index("dp")
+    place = lax.axis_index("tensor")
     owner = (place // CORES - step + chips) % chips * CORES + place % CORES
     b = up_factor(static, b_ref[:shares], owner)
-    own_a, sibling_a = factor_a(own_f, down_rows), factor_a(sibling_f, down_rows)
-    for k, strip in enumerate(strips):
-        mine, other = blocks[2 * k : 2 * k + 2]
-        even = replica // turn[strip] % 2 == 0
-        lanes = slice(k * LANES, (k + 1) * LANES)
-        block = jnp.where(even, mine[...], other[...])
-        weights[:features, lanes] = merge(static[0], block, own_a, b[:, lanes])
-        block = jnp.where(even, other[...], mine[...])
-        weights[features:, lanes] = merge(static[0], block, sibling_a, b[:, lanes])
-    more_kernel(x, weights, product)
-
-
-def more_kernel(*refs):
+    tile = 256 if features % 256 == 0 else features
+    for side, factors in enumerate((own_f, sibling_f)):
+        a = factor_a(factors, down_rows)
+        for first in range(0, features, tile):
+            rows = slice(side * features + first, side * features + first + tile)
+            weights[rows, :] = merge(static[0], blocks[rows, :], a[first : first + tile], b)
+    multiply([[x]], weights, product)
+
+
+def more_kernel(groups, *refs):
     xs, (weights, product) = refs[:-2], refs[-2:]
-
-    def store(first, size, value):
-        product[pl.ds(first, size), :] = value.astype(product.dtype)
-
-    multiply(xs, weights, store)
+    size = len(xs) // groups
+    multiply([xs[k * size : (k + 1) * size] for k in range(groups)], weights, product)
 
 
 def own_kernel(static, own_block, sibling_block, *refs):
     own_f, sibling_f = refs[:FACTOR_PIECES], refs[FACTOR_PIECES : 2 * FACTOR_PIECES]
     refs = refs[2 * FACTOR_PIECES :]
-    xs, weights = [refs[:1], refs[1:3]], refs[-1]
+    groups, weights = [refs[:1]], refs[-1]
+    for k in range(static[6]):
+        groups.append(refs[1 + 2 * k : 3 + 2 * k])
     outs = refs[len(refs) - 1 - static[5] : -1]
     features = own_block.shape[0]
     wide = outs[0].shape[1]
@@ -363,14 +377,7 @@
     b = up_factor(static[:5], b, lax.axis_index("tensor"))
     for at, factors, block in ((0, own_f, own_block), (features, sibling_f, sibling_block)):
         weights[at : at + features] = merge(static[0], block[...], factor_a(factors, down_rows), b)
-    for h, x in enumerate(xs):
-
-        def store(first, size, value):
-            to = pl.ds(pl.multiple_of(h * x[0].shape[0] + first, 16), size)
-            for k, out in enumerate(outs):
-                out[to, :] = value[:, k * wide : (k + 1) * wide]
-
-        multiply(x, weights, store)
+    multiply(groups, weights, *outs)
 
 
 def finish_kernel(sources, first, own, inv, *refs):
@@ -497,32 +504,37 @@
     some = tokens // TOKEN_HALVES
     operands = [prompt_hidden_input, to_sibling(prompt_hidden_input), gain, to_sibling(gain)]
 
-    def prepared(half, before, in_place, limit):
+    def prepared(first, size, before, in_place, limit):
         if in_place:
-            x_shape = (jax.ShapeDtypeStruct((some, CORES * features), bf16),)
+            x_shape = (jax.ShapeDtypeStruct((size, CORES * features), bf16),)
             x_specs = tuple(in_vmem(1))
         else:
-            x_shape = (jax.ShapeDtypeStruct((some, features), bf16),) * 2
+            x_shape = (jax.ShapeDtypeStruct((size, features), bf16),) * 2
             x_specs = tuple(anywhere(2))
         *x, squares = pl.pallas_call(
-            functools.partial(prepare_kernel, half * some),
+            functools.partial(prepare_kernel, first),
             out_shape=x_shape
-            + (jax.ShapeDtypeStruct(((half + 1) * some // LANES, LANES), f32),),
+            + (jax.ShapeDtypeStruct(((first + size) // LANES, LANES), f32),),
             in_specs=anywhere(2) + in_vmem(2 + len(before)),
             out_specs=x_specs + tuple(in_vmem(1)),
             scratch_shapes=[
-                pltpu.VMEM((some, features), bf16),
-                pltpu.VMEM((some, features), bf16),
-                pltpu.VMEM((some, LANES), f32),
-                pltpu.SemaphoreType.DMA((4 * pl.cdiv(some, LANES),)),
+                pltpu.VMEM((size, features), bf16),
+                pltpu.VMEM((size, features), bf16),
+                pltpu.VMEM((size, LANES), f32),
+                pltpu.SemaphoreType.DMA((4 * pl.cdiv(size, LANES),)),
             ],
             compiler_params=pltpu.CompilerParams(vmem_limit_bytes=limit),
         )(*operands, *before)
         return x, squares
 
-    x0, squares = prepared(0, [], True, PREPARE_VMEM_BYTES)
-    x1, squares = prepared(1, [squares], False, LARGE_VMEM_BYTES)
+    cut = some // 2 // LANES * LANES
+    x0, squares = prepared(0, some, [], True, PREPARE_VMEM_BYTES)
+    x1 = []
+    if cut > 0:
+        x1, squares = prepared(some, cut, [squares], False, LARGE_VMEM_BYTES)
     exchanged, squares = lax.optimization_barrier((exchanged, squares))
+    last, squares = prepared(some + cut, some - cut, [squares], False, LARGE_VMEM_BYTES)
+    x1 = x1 + last
     a_next, b_next, sent = pl.pallas_call(
         adam_kernel,
         out_shape=(
@@ -562,6 +574,7 @@
                 outside[strip].append((piece, lax.ppermute(piece, "dp", pairs)))
 
     swap_half(0, sent)
+    own_f, squares = lax.optimization_barrier((own_f, squares))
     up_packed = packed_rows - down_rows
     more = pl.cdiv(3 * (tokens // LANES), up_packed)
     piece = jax.ShapeDtypeStruct((n_dp // FACTOR_PIECES, packed_rows, LANES), bf16)
@@ -600,18 +613,25 @@
             swap_half(half, products[0])
         for step in steps:
             blocks = [value for strip in group for value in outside[strip][step - 1]]
+            arranged = pl.pallas_call(
+                functools.partial(arrange_kernel, [turn[strip] for strip in group]),
+                out_shape=weights_shape,
+                in_specs=in_vmem(len(blocks)) + anywhere(len(after)),
+                out_specs=in_vmem(1)[0],
+                compiler_params=params(),
+            )(*blocks, *after)
             weights, product = pl.pallas_call(
-                functools.partial(outside_kernel, static, chips, step, turn),
+                functools.partial(outside_kernel, static, chips, step),
                 out_shape=(weights_shape, product_shape),
-                in_specs=in_vmem(2 + 2 * FACTOR_PIECES + len(blocks)) + anywhere(len(after)),
+                in_specs=in_vmem(3 + 2 * FACTOR_PIECES),
                 out_specs=tuple(in_vmem(2)),
                 compiler_params=params(),
-            )(messages[step - 1], *x0, *pieces, *sibling_f, *blocks, *after)
+            )(arranged, messages[step - 1], *x0, *pieces, *sibling_f)
             received.setdefault((0, half), []).append(to_chip(product, chips - step))
             second = pl.pallas_call(
-                more_kernel,
+                functools.partial(more_kernel, len(x1) // 2),
                 out_shape=product_shape,
-                in_specs=in_vmem(3),
+                in_specs=in_vmem(1 + len(x1)),
                 out_specs=in_vmem(1)[0],
                 compiler_params=params(),
             )(*x1, weights)
@@ -622,7 +642,7 @@
             after = [received[0, 0][0]]
 
     after.append(received[1, 0][0])
-    static = (scale, parts, up_rows, range(strips), columns, halves)
+    static = (scale, parts, up_rows, range(strips), columns, halves, len(x1) // 2)
     totals = pl.pallas_call(
         functools.partial(own_kernel, static),
         out_shape=(jax.ShapeDtypeStruct((tokens, wide), f32),) * halves,
@@ -631,7 +651,7 @@
             pl.BlockSpec((features, columns), lambda i: (lax.axis_index("tensor"), 0)),
             pl.BlockSpec((features, columns), lambda i: (lax.axis_index("tensor") ^ 1, 0)),
         ]
-        + in_vmem(2 * FACTOR_PIECES + 3)
+        + in_vmem(2 * FACTOR_PIECES + 1 + len(x1))
         + anywhere(len(after)),
         out_specs=tuple(in_vmem(halves)),
         scratch_shapes=[pltpu.VMEM((CORES * features, columns), bf16)],

time: 85.1 us -> 82.3 us (0.967)
  waiting for transfers between devices: 20.7 us -> 13.4 us
  Pallas kernels: 35 us -> 39.6 us
  starting transfers between devices: 27.4 us -> 26.4 us
    all_to_all x1, waiting for transfers between devices: 6.12 us -> 1.2 us  [body(): own_f = lax.all_to_all(sent, 'dp', 0, 0, tiled=True)]
    pallas_call x6 -> x9, Pallas kernels: 17.1 us -> 21.3 us  [the longest x3 12.8 us: prepared(): pl.pallas_call(functools.partial(prepare_kernel, first), out_shape=x_shap...]
    ppermute x7, waiting for transfers between devices: 10 us -> 7.5 us  [to_chip(): return lax.ppermute(value, 'tensor', pairs)]
    all_to_all x1, waiting for transfers between devices: 0.01 us -> 1.09 us  [body(): exchanged = lax.all_to_all(packed, 'dp', 0, 0, tiled=True)]
    all_to_all x1, starting transfers between devices: 6.01 us -> 4.94 us  [body(): own_f = lax.all_to_all(sent, 'dp', 0, 0, tiled=True)]
    ppermute x4, waiting for transfers between devices: 3.34 us -> 2.47 us  [swap_half(): outside[strip].append((piece, lax.ppermute(piece, 'dp', pairs)))]
  transfers between devices with their start and end apart: 17 -> 17, of which waited for: 10 -> 10; matrix products, arithmetic and copies ran while one was open for 0% -> 0% of each run, Pallas kernels for 40% -> 47%
where the time goes in v18:
time: 82.3 us; the launch traced here: 81.6 us
  Pallas kernels  39.6 us (48%)
  starting transfers between devices  26.4 us (32%)
  waiting for transfers between devices  13.4 us (16%)
  local copies, waits for them, and re-layouts  1.33 us (2%)
  between operations  0.88 us (1%)
    pallas_call x3, Pallas kernels, prepared(): pl.pallas_call(functools.partial(prepare_kernel, first), out_shape=x_shap...  12.8 us
    ppermute x7, starting transfers between devices, to_chip(): return lax.ppermute(value, 'tensor', pairs)  7.73 us
    ppermute x7, waiting for transfers between devices, to_chip(): return lax.ppermute(value, 'tensor', pairs)  7.5 us
    all_to_all x1, starting transfers between devices, body(): exchanged = lax.all_to_all(packed, 'dp', 0, 0, tiled=True)  6.86 us
    ppermute x4, starting transfers between devices, swap_half(): outside[strip].append((piece, lax.ppermute(piece, 'dp', pairs)))  5.69 us
    pallas_call x1, Pallas kernels, body(): pl.pallas_call(functools.partial(own_kernel, static), out_shape=(jax.Shap...  5.23 us
    all_to_all x1, starting transfers between devices, body(): own_f = lax.all_to_all(sent, 'dp', 0, 0, tiled=True)  4.94 us
    pallas_call x4, Pallas kernels, finish(): pl.pallas_call(functools.partial(finish_kernel, len(received), at[0] * bl...  3.52 us
  transfers between devices with their start and end apart: 17, of which 10 were waited for; matrix products, arithmetic and copies ran while one was open for 0% of the time, Pallas kernels for 47%

profile of v18, /device:TPU:0, one launch (start us, length us, event | category | flops | bytes accessed | tf_op | source)
XLA Modules:
  0.0 81.6 jit_solution(15021676851278361717)
XLA Ops:
  0.6 0.5 collective-permute-start
  1.2 2.5 %shard_map.130 = (bf16[8,192,128]{2,1,0:T(8,128)(2,1)}, bf16[2,1280,128]{2,1,0:T(8,128)(2,1)}, bf16[2,1280,128]{2,1,0:T(8,128)(2,1)}) custom-call(f32[128,1280]{1,0:T(8,128)} %bitcast.20, f32[64,512]{1,0:T(8,128)} %bitcast.24, bf16[5120,512]{1,0:T(8,128)(2,1)} %sibling_block.1), custom_call_target="tpu_custom_call" | custom-call | tf_op jit(solution)/shard_map/pallas_call | solution.py:472
  3.7 6.9 %all-to-all-start = ((bf16[8,192,128]{2,1,0:T(8,128)(2,1)}), bf16[8,192,128]{2,1,0:T(8,128)(2,1)}, u32[]{:S(2)}, u32[]{:S(2)}) async-start(bf16[8,192,128]{2,1,0:T(8,128)(2,1)} %get-tuple-element.37), calls=%async_computation | async-start | bytes 786432 | tf_op jit(solution)/shard_map/all_to_all | solution.py:487
  10.6 1.5 %collective-permute-start.4 = (bf16[2,1280,128]{2,1,0:T(8,128)(2,1)}, bf16[2,1280,128]{2,1,0:T(8,128)(2,1)}, u32[]{:S(2)}, u32[]{:S(2)}) collective-permute-start(bf16[2,1280,128]{2,1,0:T(8,128)(2,1)} %get-tuple-element.56), channel_id=1, source_target_pairs={{0,2},{1,3},{2,0},{3,1},{4,6},{5,7},{6,4},{7,5},{8,10},{9,11},{10,... | collective-permute-start | bytes 1966088 | tf_op jit(solution)/shard_map/ppermute | solution.py:449
  12.1 0.0 copy-done.9
  12.1 0.1 collective-permute-start.1
  12.1 1.2 %collective-permute-done.1.sibling_gain = f32[1,1280]{1,0:T(1,128)S(1)} collective-permute-done((f32[1,1280]{1,0:T(1,128)S(1)}, f32[1,1280]{1,0:T(1,128)S(1)}, u32[]{:S(2)}, u32[]{:S(2)}) %collective-permute-start.1) | collective-permute-done | bytes 5152 | tf_op jit(solution)/shard_map/ppermute | solution.py:441
  13.3 0.0 collective-permute-done.sibling_in
  13.3 3.7 %shard_map.131 = (bf16[640,2560]{1,0:T(8,128)(2,1)S(1)}, f32[5,128]{1,0:T(8,128)S(1)}) custom-call(bf16[1280,1280]{1,0:T(8,128)(2,1)} %own_in.5, bf16[1280,1280]{1,0:T(8,128)(2,1)} %collective-permute-done.sibling_in, f32[1,1280]{1,0:T(1,128)S(1)} %broadcast_in_dim.3.own_gain, f32[1,1280]{1,0:T(1,128)S(1)} %collective-permute-done.1.sibling_gain), custom_call_target="tpu_custom_call" | custom-call | tf_op jit(solution)/shard_map/pallas_call | solution.py:514
  17.0 0.0 copy-done.4
  17.0 0.0 copy-done.5
  17.0 0.0 copy-start.8
  17.0 0.6 copy-done.8
  17.6 4.3 %shard_map.132 = (bf16[256,1280]{1,0:T(8,128)(2,1)}, bf16[256,1280]{1,0:T(8,128)(2,1)}, f32[7,128]{1,0:T(8,128)}) custom-call(bf16[1280,1280]{1,0:T(8,128)(2,1)} %own_in.5, bf16[1280,1280]{1,0:T(8,128)(2,1)} %collective-permute-done.sibling_in, f32[1,1280]{1,0:T(1,128)} %copy-done.4, f32[1,1280]{1,0:T(1,128)} %copy-done.5, f32[5,128]{1,0:T(8,128)} %copy-done.8), custom_call_target="tpu_custom_call" | custom-call | tf_op jit(solution)/shard_map/pallas_call | solution.py:514
  21.9 1.1 %all-to-all-done.grad_in = bf16[8,192,128]{2,1,0:T(8,128)(2,1)} async-done(((bf16[8,192,128]{2,1,0:T(8,128)(2,1)}), bf16[8,192,128]{2,1,0:T(8,128)(2,1)}, u32[]{:S(2)}, u32[]{:S(2)}) %all-to-all-start) | async-done | bytes 393248 | tf_op jit(solution)/shard_map/all_to_all | solution.py:487
  23.0 2.5 %shard_map.133 = (f32[3,128,160]{2,1,0:T(8,128)}, f32[3,8,512]{2,1,0:T(8,128)}, bf16[8,192,128]{2,1,0:T(8,128)(2,1)}) custom-call(bf16[8,192,128]{2,1,0:T(8,128)(2,1)} %all-to-all-done.grad_in, f32[128,1280]{1,0:T(8,128)} %bitcast.21, f32[128,1280]{1,0:T(8,128)} %bitcast.22, f32[128,1280]{1,0:T(8,128)} %bitcast.23, f32[64,512]{1,0:T(8,128)} %refs_3_.1, ...), custom_call_target="tpu_custom_call" | custom-call | tf_op jit(solution)/shard_map/pallas_call | solution.py:538
  25.5 4.9 %all-to-all-start.1 = ((bf16[8,192,128]{2,1,0:T(8,128)(2,1)}), bf16[8,192,128]{2,1,0:T(8,128)(2,1)}, u32[]{:S(2)}, u32[]{:S(2)}) async-start(bf16[8,192,128]{2,1,0:T(8,128)(2,1)} %get-tuple-element.43), calls=%async_computation.1 | async-start | bytes 786432 | tf_op jit(solution)/shard_map/all_to_all | solution.py:555
  30.5 0.0 collective-permute-done.4.in_ref
  30.5 0.7 collective-permute-start.5
  31.2 2.0 %shard_map.136 = (bf16[1280,128]{1,0:T(8,128)(2,1)}, bf16[1280,128]{1,0:T(8,128)(2,1)}) custom-call(bf16[2,1280,128]{2,1,0:T(8,128)(2,1)} %collective-permute-done.4.in_ref), custom_call_target="tpu_custom_call" | custom-call | tf_op jit(solution)/shard_map/pallas_call | solution.py:565
  33.2 1.8 %collective-permute-start.6 = (bf16[1280,128]{1,0:T(8,128)(2,1)}, bf16[1280,128]{1,0:T(8,128)(2,1)}, u32[]{:S(2)}, u32[]{:S(2)}) collective-permute-start(bf16[1280,128]{1,0:T(8,128)(2,1)} %get-tuple-element.59.refs_0_), channel_id=1, source_target_pairs={{0,4},{4,0},{8,12},{12,8},{16,20},{20,16},{24,28},{28,24},{1,5},{5... | collective-permute-start | bytes 983048 | tf_op jit(solution)/shard_map/ppermute | solution.py:574
  35.1 1.5 %collective-permute-start.7 = (bf16[1280,128]{1,0:T(8,128)(2,1)}, bf16[1280,128]{1,0:T(8,128)(2,1)}, u32[]{:S(2)}, u32[]{:S(2)}) collective-permute-start(bf16[1280,128]{1,0:T(8,128)(2,1)} %get-tuple-element.60.refs_2_), channel_id=1, source_target_pairs={{0,8},{4,12},{8,0},{12,4},{16,24},{20,28},{24,16},{28,20},{1,9},{5... | collective-permute-start | bytes 983048 | tf_op jit(solution)/shard_map/ppermute | solution.py:574
  36.5 4.9 %shard_map.134 = (bf16[384,1280]{1,0:T(8,128)(2,1)}, bf16[384,1280]{1,0:T(8,128)(2,1)}, f32[10,128]{1,0:T(8,128)}) custom-call(bf16[1280,1280]{1,0:T(8,128)(2,1)} %own_in.5, bf16[1280,1280]{1,0:T(8,128)(2,1)} %collective-permute-done.sibling_in, f32[1,1280]{1,0:T(1,128)} %copy-done.4, f32[1,1280]{1,0:T(1,128)} %copy-done.5, f32[7,128]{1,0:T(8,128)} %get-tuple-element.44.refs_0_), custom_call_target="tpu_custom_call" | custom-call | tf_op jit(solution)/shard_map/pallas_call | solution.py:514
  41.4 1.2 %all-to-all-done.1.factor_ref = bf16[8,192,128]{2,1,0:T(8,128)(2,1)} async-done(((bf16[8,192,128]{2,1,0:T(8,128)(2,1)}), bf16[8,192,128]{2,1,0:T(8,128)(2,1)}, u32[]{:S(2)}, u32[]{:S(2)}) %all-to-all-start.1) | async-done | bytes 393248 | tf_op jit(solution)/shard_map/all_to_all | solution.py:555
  42.6 0.7 copy-done.6
  43.3 1.1 %shard_map.135 = (bf16[9,32,128]{2,1,0:T(8,128)(2,1)S(1)}, bf16[4,192,128]{2,1,0:T(8,128)(2,1)S(1)}, bf16[4,192,128]{2,1,0:T(8,128)(2,1)S(1)}) custom-call(bf16[8,192,128]{2,1,0:T(8,128)(2,1)} %all-to-all-done.1.factor_ref, f32[10,128]{1,0:T(8,128)S(1)} %copy-done.6), custom_call_target="tpu_custom_call" | custom-call | tf_op jit(solution)/shard_map/pallas_call | solution.py:581
  44.4 0.1 collective-permute-start.2
  44.5 0.5 collective-permute-start.3
  45.0 0.1 collective-permute-done.6.refs_1_
  45.1 0.9 %collective-permute-start.8 = (bf16[9,32,128]{2,1,0:T(8,128)(2,1)S(1)}, bf16[9,32,128]{2,1,0:T(8,128)(2,1)S(1)}, u32[]{:S(2)}, u32[]{:S(2)}) collective-permute-start(bf16[9,32,128]{2,1,0:T(8,128)(2,1)S(1)} %get-tuple-element.61), channel_id=1, source_target_pairs={{0,2},{1,3},{2,0},{3,1},{4,6},{5,7},{6,4},{7,5},{8,10},{9,11},{10,... | collective-permute-start | bytes 221192 | tf_op jit(solution)/shard_map/ppermute | solution.py:449
  46.0 1.1 %collective-permute-done.7.refs_3_ = bf16[1280,128]{1,0:T(8,128)(2,1)} collective-permute-done((bf16[1280,128]{1,0:T(8,128)(2,1)}, bf16[1280,128]{1,0:T(8,128)(2,1)}, u32[]{:S(2)}, u32[]{:S(2)}) %collective-permute-start.7) | collective-permute-done | bytes 327712 | tf_op jit(solution)/shard_map/ppermute | solution.py:574
  47.1 1.6 %shard_map.137.blocks = bf16[2560,256]{1,0:T(8,128)(2,1)S(1)} custom-call(bf16[1280,128]{1,0:T(8,128)(2,1)} %get-tuple-element.59.refs_0_, bf16[1280,128]{1,0:T(8,128)(2,1)} %collective-permute-done.6.refs_1_, bf16[1280,128]{1,0:T(8,128)(2,1)} %get-tuple-element.60.refs_2_, bf16[1280,128]{1,0:T(8,128)(2,1)} %collective-permute-done.7.refs_3_), custom_call_target="tpu_custom_call" | custom-call | tf_op jit(solution)/shard_map/pallas_call | solution.py:616
  48.7 0.7 collective-permute-done.8.b_ref.refs_0_
  49.4 0.0 collective-permute-done.2.refs_2_
  49.4 0.0 collective-permute-done.3.refs_3_
  49.4 0.0 copy-start.1
  49.4 0.0 copy-start.2
  49.5 1.7 %shard_map.138 = (bf16[2560,256]{1,0:T(8,128)(2,1)S(1)}, bf16[640,256]{1,0:T(8,128)(2,1)S(1)}) custom-call(bf16[2560,256]{1,0:T(8,128)(2,1)S(1)} %shard_map.137.blocks, bf16[9,32,128]{2,1,0:T(8,128)(2,1)S(1)} %collective-permute-done.8.b_ref.refs_0_, bf16[640,2560]{1,0:T(8,128)(2,1)S(1)} %get-tuple-element.50.x.refs_4_, ...), custom_call_target="tpu_custom_call" | custom-call | tf_op jit(solution)/shard_map/pallas_call | solution.py:623
  51.2 1.0 %collective-permute-start.11 = (bf16[640,256]{1,0:T(8,128)(2,1)S(1)}, bf16[640,256]{1,0:T(8,128)(2,1)S(1)}, u32[]{:S(2)}, u32[]{:S(2)}) collective-permute-start(bf16[640,256]{1,0:T(8,128)(2,1)S(1)} %get-tuple-element.62), channel_id=1, source_target_pairs={{0,2},{1,3},{2,0},{3,1},{4,6},{5,7},{6,4},{7,5},{8,10},{9,11},{10,... | collective-permute-start | bytes 983048 | tf_op jit(solution)/shard_map/ppermute | solution.py:449
  52.1 0.0 collective-permute-done.5.in_ref
  52.2 1.1 %shard_map.139 = (bf16[1280,128]{1,0:T(8,128)(2,1)S(1)}, bf16[1280,128]{1,0:T(8,128)(2,1)S(1)}) custom-call(bf16[2,1280,128]{2,1,0:T(8,128)(2,1)} %collective-permute-done.5.in_ref), custom_call_target="tpu_custom_call" | custom-call | tf_op jit(solution)/shard_map/pallas_call | solution.py:565
  53.3 1.1 %collective-permute-start.9 = (bf16[1280,128]{1,0:T(8,128)(2,1)S(1)}, bf16[1280,128]{1,0:T(8,128)(2,1)S(1)}, u32[]{:S(2)}, u32[]{:S(2)}) collective-permute-start(bf16[1280,128]{1,0:T(8,128)(2,1)S(1)} %get-tuple-element.64.refs_0_), channel_id=1, source_target_pairs={{0,4},{4,0},{8,12},{12,8},{16,20},{20,16},{24,28},{28,24},{1,5},{5... | collective-permute-start | bytes 983048 | tf_op jit(solution)/shard_map/ppermute | solution.py:574
  54.3 1.3 %collective-permute-start.10 = (bf16[1280,128]{1,0:T(8,128)(2,1)S(1)}, bf16[1280,128]{1,0:T(8,128)(2,1)S(1)}, u32[]{:S(2)}, u32[]{:S(2)}) collective-permute-start(bf16[1280,128]{1,0:T(8,128)(2,1)S(1)} %get-tuple-element.65.refs_2_), channel_id=1, source_target_pairs={{0,8},{4,12},{8,0},{12,4},{16,24},{20,28},{24,16},{28,20},{1,9},{5... | collective-permute-start | bytes 983048 | tf_op jit(solution)/shard_map/ppermute | solution.py:574
  55.7 0.0 copy-done.3
  55.7 1.6 %shard_map.143 = bf16[640,256]{1,0:T(8,128)(2,1)S(1)} custom-call(bf16[256,1280]{1,0:T(8,128)(2,1)S(1)} %copy-done.2, bf16[256,1280]{1,0:T(8,128)(2,1)S(1)} %copy-done.3, bf16[384,1280]{1,0:T(8,128)(2,1)S(1)} %copy-done, bf16[384,1280]{1,0:T(8,128)(2,1)S(1)} %copy-done.1, bf16[2560,256]{1,0:T(8,128)(2,1)S(1)} %get-tuple-element.67.refs_4_), custom_call_target="tpu_custom_call" | custom-call | tf_op jit(solution)/shard_map/pallas_call | solution.py:631
  57.3 1.4 %collective-permute-start.12 = (bf16[640,256]{1,0:T(8,128)(2,1)S(1)}, bf16[640,256]{1,0:T(8,128)(2,1)S(1)}, u32[]{:S(2)}, u32[]{:S(2)}) collective-permute-start(bf16[640,256]{1,0:T(8,128)(2,1)S(1)} %shard_map.143), channel_id=1, source_target_pairs={{0,2},{1,3},{2,0},{3,1},{4,6},{5,7},{6,4},{7,5},{8,10},{9,11},{10,... | collective-permute-start | bytes 983048 | tf_op jit(solution)/shard_map/ppermute | solution.py:449
  58.7 2.3 %collective-permute-done.11.refs_4_.refs_0_ = bf16[640,256]{1,0:T(8,128)(2,1)S(1)} collective-permute-done((bf16[640,256]{1,0:T(8,128)(2,1)S(1)}, bf16[640,256]{1,0:T(8,128)(2,1)S(1)}, u32[]{:S(2)}, u32[]{:S(2)}) %collective-permute-start.11) | collective-permute-done | bytes 327712 | tf_op jit(solution)/shard_map/ppermute | solution.py:449
  61.0 0.1 collective-permute-done.9.refs_1_
  61.1 1.2 %collective-permute-done.10.refs_3_ = bf16[1280,128]{1,0:T(8,128)(2,1)S(1)} collective-permute-done((bf16[1280,128]{1,0:T(8,128)(2,1)S(1)}, bf16[1280,128]{1,0:T(8,128)(2,1)S(1)}, u32[]{:S(2)}, u32[]{:S(2)}) %collective-permute-start.10) | collective-permute-done | bytes 327712 | tf_op jit(solution)/shard_map/ppermute | solution.py:574
  62.3 0.3 shard_map.140.blocks
  62.7 0.0 slice-start.1
  62.7 1.7 %shard_map.141 = (bf16[2560,256]{1,0:T(8,128)(2,1)S(1)}, bf16[640,256]{1,0:T(8,128)(2,1)S(1)}) custom-call(bf16[2560,256]{1,0:T(8,128)(2,1)S(1)} %shard_map.140.blocks, bf16[9,32,128]{2,1,0:T(8,128)(2,1)S(1)} %collective-permute-done.8.b_ref.refs_0_, bf16[640,2560]{1,0:T(8,128)(2,1)S(1)} %get-tuple-element.50.x.refs_4_, ...), custom_call_target="tpu_custom_call" | custom-call | tf_op jit(solution)/shard_map/pallas_call | solution.py:623
  64.4 1.6 %collective-permute-start.14 = (bf16[640,256]{1,0:T(8,128)(2,1)S(1)}, bf16[640,256]{1,0:T(8,128)(2,1)S(1)}, u32[]{:S(2)}, u32[]{:S(2)}) collective-permute-start(bf16[640,256]{1,0:T(8,128)(2,1)S(1)} %get-tuple-element.69), channel_id=1, source_target_pairs={{0,2},{1,3},{2,0},{3,1},{4,6},{5,7},{6,4},{7,5},{8,10},{9,11},{10,... | collective-permute-start | bytes 983048 | tf_op jit(solution)/shard_map/ppermute | solution.py:449
  66.0 1.6 %shard_map.142.refs_9_ = bf16[640,256]{1,0:T(8,128)(2,1)S(1)} custom-call(bf16[256,1280]{1,0:T(8,128)(2,1)S(1)} %copy-done.2, bf16[256,1280]{1,0:T(8,128)(2,1)S(1)} %copy-done.3, bf16[384,1280]{1,0:T(8,128)(2,1)S(1)} %copy-done, bf16[384,1280]{1,0:T(8,128)(2,1)S(1)} %copy-done.1, bf16[2560,256]{1,0:T(8,128)(2,1)S(1)} %get-tuple-element.66.refs_4_), custom_call_target="tpu_custom_call" | custom-call | tf_op jit(solution)/shard_map/pallas_call | solution.py:631
  67.5 0.6 collective-permute-start.13
  68.1 0.2 shard_map.145.inv
  68.4 0.0 collective-permute-done.12.refs_10_.refs_0_
  68.4 5.2 %shard_map.144 = (f32[1280,256]{1,0:T(8,128)S(1)}, f32[1280,256]{1,0:T(8,128)S(1)}) custom-call(bf16[5120,512]{1,0:T(8,128)(2,1)S(1)} %bitcast.19, bf16[5120,512]{1,0:T(8,128)(2,1)S(1)} %bitcast.19, bf16[4,192,128]{2,1,0:T(8,128)(2,1)S(1)} %get-tuple-element.48.refs_0_, bf16[4,192,128]{2,1,0:T(8,128)(2,1)S(1)} %get-tuple-element.49.refs_1_, ...), custom_call_target="tpu_custom_call" | custom-call | flops 3355443200 | bytes 6553600 | tf_op jit(solution)/shard_map/pallas_call | solution.py:646
  73.7 0.9 %shard_map.146.refs_1_ = bf16[1280,512]{1,0:T(8,128)(2,1)} custom-call(f32[1280,256]{1,0:T(8,128)S(1)} %get-tuple-element.70.own, f32[1280,128]{1,0:T(8,128)S(1)} %shard_map.145.inv, bf16[640,256]{1,0:T(8,128)(2,1)S(1)} %collective-permute-done.11.refs_4_.refs_0_), custom_call_target="tpu_custom_call" | custom-call | tf_op jit(solution)/shard_map/pallas_call | solution.py:400
  74.6 0.9 %shard_map.147.refs_1_ = bf16[1280,512]{1,0:T(8,128)(2,1)} custom-call(f32[1280,256]{1,0:T(8,128)S(1)} %get-tuple-element.70.own, f32[1280,128]{1,0:T(8,128)S(1)} %shard_map.145.inv, bf16[640,256]{1,0:T(8,128)(2,1)S(1)} %collective-permute-done.12.refs_10_.refs_0_, bf16[1280,512]{1,0:T(8,128)(2,1)} %shard_map.146.refs_1_), custom_call_target="tpu_custom_call", output_to_operand_aliasing={{}: (3, {})} | custom-call | tf_op jit(solution)/shard_map/pallas_call | solution.py:400
  75.4 0.0 collective-permute-done.14.refs_0_
  75.4 0.9 %shard_map.148.refs_1_ = bf16[1280,512]{1,0:T(8,128)(2,1)} custom-call(f32[1280,256]{1,0:T(8,128)S(1)} %get-tuple-element.68.own, f32[1280,128]{1,0:T(8,128)S(1)} %shard_map.145.inv, bf16[640,256]{1,0:T(8,128)(2,1)S(1)} %collective-permute-done.14.refs_0_, bf16[1280,512]{1,0:T(8,128)(2,1)} %shard_map.147.refs_1_), custom_call_target="tpu_custom_call", output_to_operand_aliasing={{}: (3, {})} | custom-call | tf_op jit(solution)/shard_map/pallas_call | solution.py:400
  76.3 4.4 %collective-permute-done.13.refs_0_ = bf16[640,256]{1,0:T(8,128)(2,1)S(1)} collective-permute-done((bf16[640,256]{1,0:T(8,128)(2,1)S(1)}, bf16[640,256]{1,0:T(8,128)(2,1)S(1)}, u32[]{:S(2)}, u32[]{:S(2)}) %collective-permute-start.13) | collective-permute-done | bytes 327712 | tf_op jit(solution)/shard_map/ppermute | solution.py:449
  80.8 0.9 %shard_map.149 = bf16[1280,512]{1,0:T(8,128)(2,1)} custom-call(f32[1280,256]{1,0:T(8,128)S(1)} %get-tuple-element.68.own, f32[1280,128]{1,0:T(8,128)S(1)} %shard_map.145.inv, bf16[640,256]{1,0:T(8,128)(2,1)S(1)} %collective-permute-done.13.refs_0_, bf16[1280,512]{1,0:T(8,128)(2,1)} %shard_map.148.refs_1_), custom_call_target="tpu_custom_call", output_to_operand_aliasing={{}: (3, {})} | custom-call | tf_op jit(solution)/shard_map/pallas_call | solution.py:400
  (16 shorter events, 0.0 us)
Async XLA Ops:
  0.6 12.7 %collective-permute-start = (bf16[1280,1280]{1,0:T(8,128)(2,1)}, bf16[1280,1280]{1,0:T(8,128)(2,1)}, u32[]{:S(2)}, u32[]{:S(2)}) collective-permute-start(bf16[1280,1280]{1,0:T(8,128)(2,1)} %own_in.5), channel_id=1, source_target_pairs={{0,1},{1,0},{2,3},{3,2},{4,5},{5,4},{6,7},{7,6},{8,9},{9,8},{10,11... | collective-permute-start | bytes 9830408 | tf_op jit(solution)/shard_map/ppermute | solution.py:441
  1.1 10.9 %copy-start.9 = (f32[1280]{0:T(1024)S(1)}, f32[1280]{0:T(1024)}, u32[]{:S(2)}) copy-start(f32[1280]{0:T(1024)} %param.12) | copy-start | bytes 15364
  3.7 19.3 %all-to-all-start = ((bf16[8,192,128]{2,1,0:T(8,128)(2,1)}), bf16[8,192,128]{2,1,0:T(8,128)(2,1)}, u32[]{:S(2)}, u32[]{:S(2)}) async-start(bf16[8,192,128]{2,1,0:T(8,128)(2,1)} %get-tuple-element.37), calls=%async_computation | async-start | bytes 786432 | tf_op jit(solution)/shard_map/all_to_all | solution.py:487
  10.6 19.9 %collective-permute-start.4 = (bf16[2,1280,128]{2,1,0:T(8,128)(2,1)}, bf16[2,1280,128]{2,1,0:T(8,128)(2,1)}, u32[]{:S(2)}, u32[]{:S(2)}) collective-permute-start(bf16[2,1280,128]{2,1,0:T(8,128)(2,1)} %get-tuple-element.56), channel_id=1, source_target_pairs={{0,2},{1,3},{2,0},{3,1},{4,6},{5,7},{6,4},{7,5},{8,10},{9,11},{10,... | collective-permute-start | bytes 1966088 | tf_op jit(solution)/shard_map/ppermute | solution.py:449
  12.1 4.9 %copy-start.4 = (f32[1,1280]{1,0:T(1,128)}, f32[1,1280]{1,0:T(1,128)S(1)}, u32[]{:S(2)}) copy-start(f32[1,1280]{1,0:T(1,128)S(1)} %broadcast_in_dim.3.own_gain) | copy-start | bytes 15364
  12.1 1.2 %collective-permute-start.1 = (f32[1,1280]{1,0:T(1,128)S(1)}, f32[1,1280]{1,0:T(1,128)S(1)}, u32[]{:S(2)}, u32[]{:S(2)}) collective-permute-start(f32[1,1280]{1,0:T(1,128)S(1)} %broadcast_in_dim.3.own_gain), channel_id=1, source_target_pairs={{0,1},{1,0},{2,3},{3,2},{4,5},{5,4},{6,7},{7,6},{8,9},{9,8},{10,11... | collective-permute-start | bytes 15368 | tf_op jit(solution)/shard_map/ppermute | solution.py:441
  13.3 3.7 %copy-start.5 = (f32[1,1280]{1,0:T(1,128)}, f32[1,1280]{1,0:T(1,128)S(1)}, u32[]{:S(2)}) copy-start(f32[1,1280]{1,0:T(1,128)S(1)} %collective-permute-done.1.sibling_gain) | copy-start | bytes 15364
  17.0 0.6 copy-start.8
  25.5 17.1 %all-to-all-start.1 = ((bf16[8,192,128]{2,1,0:T(8,128)(2,1)}), bf16[8,192,128]{2,1,0:T(8,128)(2,1)}, u32[]{:S(2)}, u32[]{:S(2)}) async-start(bf16[8,192,128]{2,1,0:T(8,128)(2,1)} %get-tuple-element.43), calls=%async_computation.1 | async-start | bytes 786432 | tf_op jit(solution)/shard_map/all_to_all | solution.py:555
  30.5 21.7 %collective-permute-start.5 = (bf16[2,1280,128]{2,1,0:T(8,128)(2,1)}, bf16[2,1280,128]{2,1,0:T(8,128)(2,1)}, u32[]{:S(2)}, u32[]{:S(2)}) collective-permute-start(bf16[2,1280,128]{2,1,0:T(8,128)(2,1)} %get-tuple-element.57), channel_id=1, source_target_pairs={{0,2},{1,3},{2,0},{3,1},{4,6},{5,7},{6,4},{7,5},{8,10},{9,11},{10,... | collective-permute-start | bytes 1966088 | tf_op jit(solution)/shard_map/ppermute | solution.py:449
  33.2 11.8 %collective-permute-start.6 = (bf16[1280,128]{1,0:T(8,128)(2,1)}, bf16[1280,128]{1,0:T(8,128)(2,1)}, u32[]{:S(2)}, u32[]{:S(2)}) collective-permute-start(bf16[1280,128]{1,0:T(8,128)(2,1)} %get-tuple-element.59.refs_0_), channel_id=1, source_target_pairs={{0,4},{4,0},{8,12},{12,8},{16,20},{20,16},{24,28},{28,24},{1,5},{5... | collective-permute-start | bytes 983048 | tf_op jit(solution)/shard_map/ppermute | solution.py:574
  35.1 12.0 %collective-permute-start.7 = (bf16[1280,128]{1,0:T(8,128)(2,1)}, bf16[1280,128]{1,0:T(8,128)(2,1)}, u32[]{:S(2)}, u32[]{:S(2)}) collective-permute-start(bf16[1280,128]{1,0:T(8,128)(2,1)} %get-tuple-element.60.refs_2_), channel_id=1, source_target_pairs={{0,8},{4,12},{8,0},{12,4},{16,24},{20,28},{24,16},{28,20},{1,9},{5... | collective-permute-start | bytes 983048 | tf_op jit(solution)/shard_map/ppermute | solution.py:574
  42.6 0.7 copy-start.6
  44.4 5.0 %collective-permute-start.2 = (bf16[4,192,128]{2,1,0:T(8,128)(2,1)S(1)}, bf16[4,192,128]{2,1,0:T(8,128)(2,1)S(1)}, u32[]{:S(2)}, u32[]{:S(2)}) collective-permute-start(bf16[4,192,128]{2,1,0:T(8,128)(2,1)S(1)} %get-tuple-element.48.refs_0_), channel_id=1, source_target_pairs={{0,1},{1,0},{2,3},{3,2},{4,5},{5,4},{6,7},{7,6},{8,9},{9,8},{10,11... | collective-permute-start | bytes 589832 | tf_op jit(solution)/shard_map/ppermute | solution.py:441
  44.5 4.9 %collective-permute-start.3 = (bf16[4,192,128]{2,1,0:T(8,128)(2,1)S(1)}, bf16[4,192,128]{2,1,0:T(8,128)(2,1)S(1)}, u32[]{:S(2)}, u32[]{:S(2)}) collective-permute-start(bf16[4,192,128]{2,1,0:T(8,128)(2,1)S(1)} %get-tuple-element.49.refs_1_), channel_id=1, source_target_pairs={{0,1},{1,0},{2,3},{3,2},{4,5},{5,4},{6,7},{7,6},{8,9},{9,8},{10,11... | collective-permute-start | bytes 589832 | tf_op jit(solution)/shard_map/ppermute | solution.py:441
  45.1 4.4 %collective-permute-start.8 = (bf16[9,32,128]{2,1,0:T(8,128)(2,1)S(1)}, bf16[9,32,128]{2,1,0:T(8,128)(2,1)S(1)}, u32[]{:S(2)}, u32[]{:S(2)}) collective-permute-start(bf16[9,32,128]{2,1,0:T(8,128)(2,1)S(1)} %get-tuple-element.61), channel_id=1, source_target_pairs={{0,2},{1,3},{2,0},{3,1},{4,6},{5,7},{6,4},{7,5},{8,10},{9,11},{10,... | collective-permute-start | bytes 221192 | tf_op jit(solution)/shard_map/ppermute | solution.py:449
  49.4 6.3 %copy-start = (bf16[384,1280]{1,0:T(8,128)(2,1)S(1)}, bf16[384,1280]{1,0:T(8,128)(2,1)}, u32[]{:S(2)}) copy-start(bf16[384,1280]{1,0:T(8,128)(2,1)} %get-tuple-element.53.refs_2_.refs_7_) | copy-start | bytes 2949124
  49.4 6.3 %copy-start.1 = (bf16[384,1280]{1,0:T(8,128)(2,1)S(1)}, bf16[384,1280]{1,0:T(8,128)(2,1)}, u32[]{:S(2)}) copy-start(bf16[384,1280]{1,0:T(8,128)(2,1)} %get-tuple-element.54.refs_3_.refs_8_) | copy-start | bytes 2949124
  49.4 6.3 %copy-start.2 = (bf16[256,1280]{1,0:T(8,128)(2,1)S(1)}, bf16[256,1280]{1,0:T(8,128)(2,1)}, u32[]{:S(2)}) copy-start(bf16[256,1280]{1,0:T(8,128)(2,1)} %get-tuple-element.51.refs_0_.refs_5_) | copy-start | bytes 1966084
  49.4 6.2 %copy-start.3 = (bf16[256,1280]{1,0:T(8,128)(2,1)S(1)}, bf16[256,1280]{1,0:T(8,128)(2,1)}, u32[]{:S(2)}) copy-start(bf16[256,1280]{1,0:T(8,128)(2,1)} %get-tuple-element.52.refs_1_.refs_6_) | copy-start | bytes 1966084
  51.2 9.9 %collective-permute-start.11 = (bf16[640,256]{1,0:T(8,128)(2,1)S(1)}, bf16[640,256]{1,0:T(8,128)(2,1)S(1)}, u32[]{:S(2)}, u32[]{:S(2)}) collective-permute-start(bf16[640,256]{1,0:T(8,128)(2,1)S(1)} %get-tuple-element.62), channel_id=1, source_target_pairs={{0,2},{1,3},{2,0},{3,1},{4,6},{5,7},{6,4},{7,5},{8,10},{9,11},{10,... | collective-permute-start | bytes 983048 | tf_op jit(solution)/shard_map/ppermute | solution.py:449
  53.3 7.9 %collective-permute-start.9 = (bf16[1280,128]{1,0:T(8,128)(2,1)S(1)}, bf16[1280,128]{1,0:T(8,128)(2,1)S(1)}, u32[]{:S(2)}, u32[]{:S(2)}) collective-permute-start(bf16[1280,128]{1,0:T(8,128)(2,1)S(1)} %get-tuple-element.64.refs_0_), channel_id=1, source_target_pairs={{0,4},{4,0},{8,12},{12,8},{16,20},{20,16},{24,28},{28,24},{1,5},{5... | collective-permute-start | bytes 983048 | tf_op jit(solution)/shard_map/ppermute | solution.py:574
  54.3 8.0 %collective-permute-start.10 = (bf16[1280,128]{1,0:T(8,128)(2,1)S(1)}, bf16[1280,128]{1,0:T(8,128)(2,1)S(1)}, u32[]{:S(2)}, u32[]{:S(2)}) collective-permute-start(bf16[1280,128]{1,0:T(8,128)(2,1)S(1)} %get-tuple-element.65.refs_2_), channel_id=1, source_target_pairs={{0,8},{4,12},{8,0},{12,4},{16,24},{20,28},{24,16},{28,20},{1,9},{5... | collective-permute-start | bytes 983048 | tf_op jit(solution)/shard_map/ppermute | solution.py:574
  57.3 11.1 %collective-permute-start.12 = (bf16[640,256]{1,0:T(8,128)(2,1)S(1)}, bf16[640,256]{1,0:T(8,128)(2,1)S(1)}, u32[]{:S(2)}, u32[]{:S(2)}) collective-permute-start(bf16[640,256]{1,0:T(8,128)(2,1)S(1)} %shard_map.143), channel_id=1, source_target_pairs={{0,2},{1,3},{2,0},{3,1},{4,6},{5,7},{6,4},{7,5},{8,10},{9,11},{10,... | collective-permute-start | bytes 983048 | tf_op jit(solution)/shard_map/ppermute | solution.py:449
  62.3 6.1 %slice-start = ((s8[5242880]{0:T(1024)(128)(4,1)}), s8[4194304]{0:T(1024)(128)(4,1)S(1)}, s32[]{:S(2)}) async-start(s8[5242880]{0:T(1024)(128)(4,1)} %bitcast.18), calls=%async_computation.2 | async-start | bytes 8388608
  62.7 5.7 %slice-start.1 = ((s8[5242880]{0:T(1024)(128)(4,1)}), s8[1048576]{0:T(1024)(128)(4,1)S(1)}, s32[]{:S(2)}) async-start(s8[5242880]{0:T(1024)(128)(4,1)} %bitcast.18), calls=%async_computation.3 | async-start | bytes 2097152
  64.4 11.0 %collective-permute-start.14 = (bf16[640,256]{1,0:T(8,128)(2,1)S(1)}, bf16[640,256]{1,0:T(8,128)(2,1)S(1)}, u32[]{:S(2)}, u32[]{:S(2)}) collective-permute-start(bf16[640,256]{1,0:T(8,128)(2,1)S(1)} %get-tuple-element.69), channel_id=1, source_target_pairs={{0,2},{1,3},{2,0},{3,1},{4,6},{5,7},{6,4},{7,5},{8,10},{9,11},{10,... | collective-permute-start | bytes 983048 | tf_op jit(solution)/shard_map/ppermute | solution.py:449
  66.0 2.2 %copy-start.7 = (f32[10,128]{1,0:T(8,128)S(1)}, f32[10,128]{1,0:T(8,128)}, u32[]{:S(2)}) copy-start(f32[10,128]{1,0:T(8,128)} %get-tuple-element.47.sums_ref) | copy-start | bytes 15364
  67.5 13.2 %collective-permute-start.13 = (bf16[640,256]{1,0:T(8,128)(2,1)S(1)}, bf16[640,256]{1,0:T(8,128)(2,1)S(1)}, u32[]{:S(2)}, u32[]{:S(2)}) collective-permute-start(bf16[640,256]{1,0:T(8,128)(2,1)S(1)} %shard_map.142.refs_9_), channel_id=1, source_target_pairs={{0,2},{1,3},{2,0},{3,1},{4,6},{5,7},{6,4},{7,5},{8,10},{9,11},{10,... | collective-permute-start | bytes 983048 | tf_op jit(solution)/shard_map/ppermute | solution.py:449

commit v19 on v18

--- a/solution.py
+++ b/solution.py
@@ -18,6 +18,7 @@
 VMEM_BYTES = 16 * 2**20
 LARGE_VMEM_BYTES = 58 * 2**20
 PREPARE_VMEM_BYTES = 49 * 2**20
+FINAL_VMEM_BYTES = 55 * 2**20
 
 
 def adaptive_moment_update(param, first, second, grad_mean):
@@ -215,30 +216,25 @@
         ).T
 
 
-def update(total, down, up, a_ref, b_ref):
-    down_rows = a_ref.shape[2]
-    up_rows, columns = b_ref.shape[1:]
-    strips = columns // LANES
+def update(total, down, up, down_rows, columns):
+    up_rows = up[0].shape[0]
     down_mean = total[:down_rows].T
     up_mean = jnp.concatenate(
-        [total[down_rows + k * up_rows : down_rows + (k + 1) * up_rows] for k in range(strips)],
+        [
+            total[down_rows + k * up_rows : down_rows + (k + 1) * up_rows]
+            for k in range(columns // LANES)
+        ],
         axis=1,
     )
-    p, m, v = adaptive_moment_update(*down(), down_mean)
-    a_ref[0], a_ref[1], a_ref[2] = p, m, v
-    pieces = [p.T]
-    p, m, v = adaptive_moment_update(*up(), up_mean)
-    b_ref[0], b_ref[1], b_ref[2] = p, m, v
-    pieces += [p[:, k * LANES : (k + 1) * LANES] for k in range(strips)]
-    return jnp.concatenate(pieces, axis=0).astype(jnp.bfloat16)
-
-
-def adam_kernel(grad_in, *refs):
+    return adaptive_moment_update(*down, down_mean), adaptive_moment_update(*up, up_mean)
+
+
+def adam_kernel(down_rows, final, grad_in, *refs):
     state, refs = refs[:6], refs[6:]
-    a_ref, b_ref, factor_ref, grad_ref, down_win, up_win, sem = refs
+    grad_ref, down_win, up_win, sem = refs[-4:]
+    outs = refs[-6:-4]
     replicas = grad_ref.shape[0]
-    down_rows, window = a_ref.shape[2], down_win.shape[2]
-    up_rows = up_win.shape[1]
+    window, up_rows, columns = down_win.shape[2], up_win.shape[1], up_win.shape[2]
     replica = lax.axis_index("dp")
     share = replica * down_rows
     size = down_rows * replicas
@@ -257,16 +253,24 @@
     total = jnp.sum(grad_ref[...].astype(jnp.float32), axis=0) / replicas
     for copy in copies[1:]:
         copy.wait()
-
-    def down():
-        if window == down_rows:
-            return [down_win[i] for i in range(3)]
+    down = [down_win[i] for i in range(3)]
+    if window != down_rows:
         shift = window - (share - first_lane(share, window, size))
-        return [pltpu.roll(down_win[i], shift, 1)[:, :down_rows] for i in range(3)]
-
-    rounded = update(total, down, lambda: [up_win[i] for i in range(3)], a_ref, b_ref)
-    for i in range(replicas):
-        factor_ref[i] = rounded
+        down = [pltpu.roll(value, shift, 1)[:, :down_rows] for value in down]
+    down, up = update(total, down, [up_win[i] for i in range(3)], down_rows, columns)
+    if final:
+        for i in range(3):
+            outs[0][i], outs[1][i] = down[i], up[i]
+        return
+    target, rounded = outs
+    pieces = [down[0].T]
+    pieces += [up[0][:, k * LANES : (k + 1) * LANES] for k in range(columns // LANES)]
+    rounded[...] = jnp.concatenate(pieces, axis=0).astype(jnp.bfloat16)
+    copies = [pltpu.make_async_copy(rounded, target.at[i], sem.at[i]) for i in range(replicas)]
+    for copy in copies:
+        copy.start()
+    for copy in copies:
+        copy.wait()
 
 
 def factor_a(refs, down_rows):
@@ -535,27 +539,36 @@
     exchanged, squares = lax.optimization_barrier((exchanged, squares))
     last, squares = prepared(some + cut, some - cut, [squares], False, LARGE_VMEM_BYTES)
     x1 = x1 + last
-    a_next, b_next, sent = pl.pallas_call(
-        adam_kernel,
-        out_shape=(
-            jax.ShapeDtypeStruct((3, factors, down_rows), f32),
-            jax.ShapeDtypeStruct((3, up_rows, columns), f32),
-            shares,
-        ),
-        in_specs=anywhere(7),
-        out_specs=tuple(in_vmem(3)),
-        scratch_shapes=[
+    def updated(final, after):
+        scratch_shapes = [
             pltpu.VMEM((n_dp, packed_rows, LANES), bf16),
             pltpu.VMEM((3, factors, window), f32),
             pltpu.VMEM((3, up_rows, columns), f32),
-            pltpu.SemaphoreType.DMA((7,)),
-        ],
-        compiler_params=pltpu.CompilerParams(vmem_limit_bytes=LARGE_VMEM_BYTES),
-    )(exchanged, *down_state, *up_state)
+            pltpu.SemaphoreType.DMA((max(7, n_dp),)),
+        ]
+        if final:
+            out_shape = (
+                jax.ShapeDtypeStruct((3, factors, down_rows), f32),
+                jax.ShapeDtypeStruct((3, up_rows, columns), f32),
+            )
+        else:
+            out_shape = (shares,)
+            scratch_shapes.insert(0, pltpu.VMEM((packed_rows, LANES), bf16))
+        return pl.pallas_call(
+            functools.partial(adam_kernel, down_rows, final),
+            out_shape=out_shape,
+            in_specs=anywhere(7 + len(after)),
+            out_specs=tuple(in_vmem(2) if final else anywhere(1)),
+            scratch_shapes=scratch_shapes,
+            compiler_params=pltpu.CompilerParams(
+                vmem_limit_bytes=FINAL_VMEM_BYTES if final else LARGE_VMEM_BYTES
+            ),
+        )(exchanged, *down_state, *up_state, *after)
+
+    (sent,) = updated(False, [])
     own_f = lax.all_to_all(sent, "dp", 0, 0, tiled=True)
     for half in range(1, halves):
         send_half(half, (mine[-1], sent))
-    a_next = jnp.transpose(a_next.reshape(3, parts, rank, down_rows), (0, 3, 1, 2))
 
     outside = [[] for _ in range(strips)]
 
@@ -574,7 +587,6 @@
                 outside[strip].append((piece, lax.ppermute(piece, "dp", pairs)))
 
     swap_half(0, sent)
-    own_f, squares = lax.optimization_barrier((own_f, squares))
     up_packed = packed_rows - down_rows
     more = pl.cdiv(3 * (tokens // LANES), up_packed)
     piece = jax.ShapeDtypeStruct((n_dp // FACTOR_PIECES, packed_rows, LANES), bf16)
@@ -663,6 +675,8 @@
         ),
     )(frozen_key_value, frozen_key_value, *pieces, *sibling_f, *x0, *x1, *after)
 
+    a_next, b_next = updated(True, totals[:1])
+    a_next = jnp.transpose(a_next.reshape(3, parts, rank, down_rows), (0, 3, 1, 2))
     keys_values = None
     for at, values in received.items():
         keys_values = finish(

time: 82.3 us -> 82.3 us (level)
  waiting for transfers between devices: 13.4 us -> 9.88 us
  Pallas kernels: 39.6 us -> 42.1 us
  local copies, waits for them, and re-layouts: 1.33 us -> 2.39 us
    ppermute x7, waiting for transfers between devices: 7.5 us -> 3.97 us  [to_chip(): return lax.ppermute(value, 'tensor', pairs)]
    pallas_call x1 -> x2, Pallas kernels: 2.52 us -> 4.96 us  [updated(): pl.pallas_call(functools.partial(adam_kernel, down_rows, final), out_shap...]
    unnamed x24 -> x28, local copies, waits for them, and re-layouts: 1.33 us -> 2.38 us
  transfers between devices with their start and end apart: 17 -> 17, of which waited for: 10 -> 10; matrix products, arithmetic and copies ran while one was open for 0% -> 0% of each run, Pallas kernels for 47% -> 50%
where the time goes in v19:
time: 82.3 us; the launch traced here: 81.6 us
  Pallas kernels  42.1 us (51%)
  starting transfers between devices  26.4 us (32%)
  waiting for transfers between devices  9.88 us (12%)
  local copies, waits for them, and re-layouts  2.39 us (3%)
  between operations  0.91 us (1%)
    pallas_call x3, Pallas kernels, prepared(): pl.pallas_call(functools.partial(prepare_kernel, first), out_shape=x_shap...  12.8 us
    ppermute x7, starting transfers between devices, to_chip(): return lax.ppermute(value, 'tensor', pairs)  7.71 us
    all_to_all x1, starting transfers between devices, body(): exchanged = lax.all_to_all(packed, 'dp', 0, 0, tiled=True)  6.86 us
    ppermute x4, starting transfers between devices, swap_half(): outside[strip].append((piece, lax.ppermute(piece, 'dp', pairs)))  5.7 us
    pallas_call x1, Pallas kernels, body(): pl.pallas_call(functools.partial(own_kernel, static), out_shape=(jax.Shap...  5.24 us
    pallas_call x2, Pallas kernels, updated(): pl.pallas_call(functools.partial(adam_kernel, down_rows, final), out_shap...  4.96 us
    all_to_all x1, starting transfers between devices, body(): own_f = lax.all_to_all(sent, 'dp', 0, 0, tiled=True)  4.95 us
    ppermute x7, waiting for transfers between devices, to_chip(): return lax.ppermute(value, 'tensor', pairs)  3.97 us
  transfers between devices with their start and end apart: 17, of which 10 were waited for; matrix products, arithmetic and copies ran while one was open for 0% of the time, Pallas kernels for 50%

profile of v19, /device:TPU:0, one launch (start us, length us, event | category | flops | bytes accessed | tf_op | source)
XLA Modules:
  0.0 81.6 jit_solution(15143767639642736852)
XLA Ops:
  0.6 0.5 collective-permute-start
  1.2 2.6 %shard_map.130 = (bf16[8,192,128]{2,1,0:T(8,128)(2,1)}, bf16[2,1280,128]{2,1,0:T(8,128)(2,1)}, bf16[2,1280,128]{2,1,0:T(8,128)(2,1)}) custom-call(f32[128,1280]{1,0:T(8,128)} %bitcast.26, f32[64,512]{1,0:T(8,128)} %bitcast.27, bf16[5120,512]{1,0:T(8,128)(2,1)} %sibling_block.1), custom_call_target="tpu_custom_call" | custom-call | tf_op jit(solution)/shard_map/pallas_call | solution.py:476
  3.7 6.9 %all-to-all-start = ((bf16[8,192,128]{2,1,0:T(8,128)(2,1)}), bf16[8,192,128]{2,1,0:T(8,128)(2,1)}, u32[]{:S(2)}, u32[]{:S(2)}) async-start(bf16[8,192,128]{2,1,0:T(8,128)(2,1)} %get-tuple-element.34), calls=%async_computation | async-start | bytes 786432 | tf_op jit(solution)/shard_map/all_to_all | solution.py:491
  10.6 1.5 %collective-permute-start.4 = (bf16[2,1280,128]{2,1,0:T(8,128)(2,1)}, bf16[2,1280,128]{2,1,0:T(8,128)(2,1)}, u32[]{:S(2)}, u32[]{:S(2)}) collective-permute-start(bf16[2,1280,128]{2,1,0:T(8,128)(2,1)} %get-tuple-element.48), channel_id=1, source_target_pairs={{0,2},{1,3},{2,0},{3,1},{4,6},{5,7},{6,4},{7,5},{8,10},{9,11},{10,... | collective-permute-start | bytes 1966088 | tf_op jit(solution)/shard_map/ppermute | solution.py:453
  12.1 0.1 collective-permute-start.1
  12.2 1.2 %collective-permute-done.1.sibling_gain = f32[1,1280]{1,0:T(1,128)S(1)} collective-permute-done((f32[1,1280]{1,0:T(1,128)S(1)}, f32[1,1280]{1,0:T(1,128)S(1)}, u32[]{:S(2)}, u32[]{:S(2)}) %collective-permute-start.1) | collective-permute-done | bytes 5152 | tf_op jit(solution)/shard_map/ppermute | solution.py:445
  13.3 0.0 collective-permute-done.sibling_in
  13.3 3.7 %shard_map.131 = (bf16[640,2560]{1,0:T(8,128)(2,1)S(1)}, f32[5,128]{1,0:T(8,128)S(1)}) custom-call(bf16[1280,1280]{1,0:T(8,128)(2,1)} %own_in.5, bf16[1280,1280]{1,0:T(8,128)(2,1)} %collective-permute-done.sibling_in, f32[1,1280]{1,0:T(1,128)S(1)} %broadcast_in_dim.3.own_gain, f32[1,1280]{1,0:T(1,128)S(1)} %collective-permute-done.1.sibling_gain), custom_call_target="tpu_custom_call" | custom-call | tf_op jit(solution)/shard_map/pallas_call | solution.py:518
  17.0 0.0 copy-start.10
  17.0 0.6 copy-done.10
  17.6 4.3 %shard_map.132 = (bf16[256,1280]{1,0:T(8,128)(2,1)}, bf16[256,1280]{1,0:T(8,128)(2,1)}, f32[7,128]{1,0:T(8,128)}) custom-call(bf16[1280,1280]{1,0:T(8,128)(2,1)} %own_in.5, bf16[1280,1280]{1,0:T(8,128)(2,1)} %collective-permute-done.sibling_in, f32[1,1280]{1,0:T(1,128)} %copy-done.6, f32[1,1280]{1,0:T(1,128)} %copy-done.7, f32[5,128]{1,0:T(8,128)} %copy-done.10), custom_call_target="tpu_custom_call" | custom-call | tf_op jit(solution)/shard_map/pallas_call | solution.py:518
  21.9 1.1 %all-to-all-done.grad_in = bf16[8,192,128]{2,1,0:T(8,128)(2,1)} async-done(((bf16[8,192,128]{2,1,0:T(8,128)(2,1)}), bf16[8,192,128]{2,1,0:T(8,128)(2,1)}, u32[]{:S(2)}, u32[]{:S(2)}) %all-to-all-start) | async-done | bytes 393248 | tf_op jit(solution)/shard_map/all_to_all | solution.py:491
  23.0 2.5 %shard_map.133 = bf16[8,192,128]{2,1,0:T(8,128)(2,1)} custom-call(bf16[8,192,128]{2,1,0:T(8,128)(2,1)} %all-to-all-done.grad_in, f32[128,1280]{1,0:T(8,128)} %bitcast.20, f32[128,1280]{1,0:T(8,128)} %bitcast.22, f32[128,1280]{1,0:T(8,128)} %bitcast.24, f32[64,512]{1,0:T(8,128)} %refs_3_.3, f32[64,512]{1,0:T(8,128)} %refs_4_.3, f32[64,512]{1,0:T(8,128)} %refs_5_.3), custom_call_target="tpu_custom_call" | custom-call | tf_op jit(solution)/shard_map/pallas_call | solution.py:557
  25.5 4.9 %all-to-all-start.1 = ((bf16[8,192,128]{2,1,0:T(8,128)(2,1)}), bf16[8,192,128]{2,1,0:T(8,128)(2,1)}, u32[]{:S(2)}, u32[]{:S(2)}) async-start(bf16[8,192,128]{2,1,0:T(8,128)(2,1)} %shard_map.133), calls=%async_computation.1 | async-start | bytes 786432 | tf_op jit(solution)/shard_map/all_to_all | solution.py:569
  30.4 0.0 collective-permute-done.4.in_ref
  30.4 0.7 collective-permute-start.5
  31.2 2.0 %shard_map.136 = (bf16[1280,128]{1,0:T(8,128)(2,1)}, bf16[1280,128]{1,0:T(8,128)(2,1)}) custom-call(bf16[2,1280,128]{2,1,0:T(8,128)(2,1)} %collective-permute-done.4.in_ref), custom_call_target="tpu_custom_call" | custom-call | tf_op jit(solution)/shard_map/pallas_call | solution.py:578
  33.2 1.8 %collective-permute-start.6 = (bf16[1280,128]{1,0:T(8,128)(2,1)}, bf16[1280,128]{1,0:T(8,128)(2,1)}, u32[]{:S(2)}, u32[]{:S(2)}) collective-permute-start(bf16[1280,128]{1,0:T(8,128)(2,1)} %get-tuple-element.51.refs_0_), channel_id=1, source_target_pairs={{0,4},{4,0},{8,12},{12,8},{16,20},{20,16},{24,28},{28,24},{1,5},{5... | collective-permute-start | bytes 983048 | tf_op jit(solution)/shard_map/ppermute | solution.py:587
  35.0 1.5 %collective-permute-start.7 = (bf16[1280,128]{1,0:T(8,128)(2,1)}, bf16[1280,128]{1,0:T(8,128)(2,1)}, u32[]{:S(2)}, u32[]{:S(2)}) collective-permute-start(bf16[1280,128]{1,0:T(8,128)(2,1)} %get-tuple-element.52.refs_2_), channel_id=1, source_target_pairs={{0,8},{4,12},{8,0},{12,4},{16,24},{20,28},{24,16},{28,20},{1,9},{5... | collective-permute-start | bytes 983048 | tf_op jit(solution)/shard_map/ppermute | solution.py:587
  36.5 4.9 %shard_map.134 = (bf16[384,1280]{1,0:T(8,128)(2,1)}, bf16[384,1280]{1,0:T(8,128)(2,1)}, f32[10,128]{1,0:T(8,128)}) custom-call(bf16[1280,1280]{1,0:T(8,128)(2,1)} %own_in.5, bf16[1280,1280]{1,0:T(8,128)(2,1)} %collective-permute-done.sibling_in, f32[1,1280]{1,0:T(1,128)} %copy-done.6, f32[1,1280]{1,0:T(1,128)} %copy-done.7, f32[7,128]{1,0:T(8,128)} %get-tuple-element.38.refs_0_), custom_call_target="tpu_custom_call" | custom-call | tf_op jit(solution)/shard_map/pallas_call | solution.py:518
  41.4 1.2 %all-to-all-done.1.factor_ref = bf16[8,192,128]{2,1,0:T(8,128)(2,1)} async-done(((bf16[8,192,128]{2,1,0:T(8,128)(2,1)}), bf16[8,192,128]{2,1,0:T(8,128)(2,1)}, u32[]{:S(2)}, u32[]{:S(2)}) %all-to-all-start.1) | async-done | bytes 393248 | tf_op jit(solution)/shard_map/all_to_all | solution.py:569
  42.6 0.7 copy-done.8
  43.3 1.1 %shard_map.135 = (bf16[9,32,128]{2,1,0:T(8,128)(2,1)S(1)}, bf16[4,192,128]{2,1,0:T(8,128)(2,1)S(1)}, bf16[4,192,128]{2,1,0:T(8,128)(2,1)S(1)}) custom-call(bf16[8,192,128]{2,1,0:T(8,128)(2,1)} %all-to-all-done.1.factor_ref, f32[10,128]{1,0:T(8,128)S(1)} %copy-done.8), custom_call_target="tpu_custom_call" | custom-call | tf_op jit(solution)/shard_map/pallas_call | solution.py:593
  44.4 0.1 collective-permute-start.2
  44.4 0.5 collective-permute-start.3
  44.9 0.1 collective-permute-done.6.refs_1_
  45.0 0.9 %collective-permute-start.8 = (bf16[9,32,128]{2,1,0:T(8,128)(2,1)S(1)}, bf16[9,32,128]{2,1,0:T(8,128)(2,1)S(1)}, u32[]{:S(2)}, u32[]{:S(2)}) collective-permute-start(bf16[9,32,128]{2,1,0:T(8,128)(2,1)S(1)} %get-tuple-element.53), channel_id=1, source_target_pairs={{0,2},{1,3},{2,0},{3,1},{4,6},{5,7},{6,4},{7,5},{8,10},{9,11},{10,... | collective-permute-start | bytes 221192 | tf_op jit(solution)/shard_map/ppermute | solution.py:453
  45.9 1.1 %collective-permute-done.7.refs_3_ = bf16[1280,128]{1,0:T(8,128)(2,1)} collective-permute-done((bf16[1280,128]{1,0:T(8,128)(2,1)}, bf16[1280,128]{1,0:T(8,128)(2,1)}, u32[]{:S(2)}, u32[]{:S(2)}) %collective-permute-start.7) | collective-permute-done | bytes 327712 | tf_op jit(solution)/shard_map/ppermute | solution.py:587
  47.0 1.6 %shard_map.137.blocks = bf16[2560,256]{1,0:T(8,128)(2,1)S(1)} custom-call(bf16[1280,128]{1,0:T(8,128)(2,1)} %get-tuple-element.51.refs_0_, bf16[1280,128]{1,0:T(8,128)(2,1)} %collective-permute-done.6.refs_1_, bf16[1280,128]{1,0:T(8,128)(2,1)} %get-tuple-element.52.refs_2_, bf16[1280,128]{1,0:T(8,128)(2,1)} %collective-permute-done.7.refs_3_), custom_call_target="tpu_custom_call" | custom-call | tf_op jit(solution)/shard_map/pallas_call | solution.py:628
  48.6 0.7 collective-permute-done.8.b_ref.refs_0_
  49.4 0.0 collective-permute-done.2.refs_2_
  49.4 0.0 collective-permute-done.3.refs_3_
  49.4 0.0 copy-start.3
  49.4 0.0 copy-start.4
  49.4 0.0 copy-start.5
  49.4 1.7 %shard_map.138 = (bf16[2560,256]{1,0:T(8,128)(2,1)S(1)}, bf16[640,256]{1,0:T(8,128)(2,1)S(1)}) custom-call(bf16[2560,256]{1,0:T(8,128)(2,1)S(1)} %shard_map.137.blocks, bf16[9,32,128]{2,1,0:T(8,128)(2,1)S(1)} %collective-permute-done.8.b_ref.refs_0_, bf16[640,2560]{1,0:T(8,128)(2,1)S(1)} %get-tuple-element.42.x.refs_4_, ...), custom_call_target="tpu_custom_call" | custom-call | tf_op jit(solution)/shard_map/pallas_call | solution.py:635
  51.1 1.0 %collective-permute-start.11 = (bf16[640,256]{1,0:T(8,128)(2,1)S(1)}, bf16[640,256]{1,0:T(8,128)(2,1)S(1)}, u32[]{:S(2)}, u32[]{:S(2)}) collective-permute-start(bf16[640,256]{1,0:T(8,128)(2,1)S(1)} %get-tuple-element.54), channel_id=1, source_target_pairs={{0,2},{1,3},{2,0},{3,1},{4,6},{5,7},{6,4},{7,5},{8,10},{9,11},{10,... | collective-permute-start | bytes 983048 | tf_op jit(solution)/shard_map/ppermute | solution.py:453
  52.1 0.0 collective-permute-done.5.in_ref
  52.1 1.1 %shard_map.139 = (bf16[1280,128]{1,0:T(8,128)(2,1)S(1)}, bf16[1280,128]{1,0:T(8,128)(2,1)S(1)}) custom-call(bf16[2,1280,128]{2,1,0:T(8,128)(2,1)} %collective-permute-done.5.in_ref), custom_call_target="tpu_custom_call" | custom-call | tf_op jit(solution)/shard_map/pallas_call | solution.py:578
  53.2 1.1 %collective-permute-start.9 = (bf16[1280,128]{1,0:T(8,128)(2,1)S(1)}, bf16[1280,128]{1,0:T(8,128)(2,1)S(1)}, u32[]{:S(2)}, u32[]{:S(2)}) collective-permute-start(bf16[1280,128]{1,0:T(8,128)(2,1)S(1)} %get-tuple-element.56.refs_0_), channel_id=1, source_target_pairs={{0,4},{4,0},{8,12},{12,8},{16,20},{20,16},{24,28},{28,24},{1,5},{5... | collective-permute-start | bytes 983048 | tf_op jit(solution)/shard_map/ppermute | solution.py:587
  54.3 1.3 %collective-permute-start.10 = (bf16[1280,128]{1,0:T(8,128)(2,1)S(1)}, bf16[1280,128]{1,0:T(8,128)(2,1)S(1)}, u32[]{:S(2)}, u32[]{:S(2)}) collective-permute-start(bf16[1280,128]{1,0:T(8,128)(2,1)S(1)} %get-tuple-element.57.refs_2_), channel_id=1, source_target_pairs={{0,8},{4,12},{8,0},{12,4},{16,24},{20,28},{24,16},{28,20},{1,9},{5... | collective-permute-start | bytes 983048 | tf_op jit(solution)/shard_map/ppermute | solution.py:587
  55.7 1.5 %shard_map.143 = bf16[640,256]{1,0:T(8,128)(2,1)S(1)} custom-call(bf16[256,1280]{1,0:T(8,128)(2,1)S(1)} %copy-done.4, bf16[256,1280]{1,0:T(8,128)(2,1)S(1)} %copy-done.5, bf16[384,1280]{1,0:T(8,128)(2,1)S(1)} %copy-done.2, bf16[384,1280]{1,0:T(8,128)(2,1)S(1)} %copy-done.3, bf16[2560,256]{1,0:T(8,128)(2,1)S(1)} %get-tuple-element.59.refs_4_), custom_call_target="tpu_custom_call" | custom-call | tf_op jit(solution)/shard_map/pallas_call | solution.py:643
  57.2 1.4 %collective-permute-start.12 = (bf16[640,256]{1,0:T(8,128)(2,1)S(1)}, bf16[640,256]{1,0:T(8,128)(2,1)S(1)}, u32[]{:S(2)}, u32[]{:S(2)}) collective-permute-start(bf16[640,256]{1,0:T(8,128)(2,1)S(1)} %shard_map.143), channel_id=1, source_target_pairs={{0,2},{1,3},{2,0},{3,1},{4,6},{5,7},{6,4},{7,5},{8,10},{9,11},{10,... | collective-permute-start | bytes 983048 | tf_op jit(solution)/shard_map/ppermute | solution.py:453
  58.6 2.4 %collective-permute-done.11.refs_4_.refs_0_ = bf16[640,256]{1,0:T(8,128)(2,1)S(1)} collective-permute-done((bf16[640,256]{1,0:T(8,128)(2,1)S(1)}, bf16[640,256]{1,0:T(8,128)(2,1)S(1)}, u32[]{:S(2)}, u32[]{:S(2)}) %collective-permute-start.11) | collective-permute-done | bytes 327712 | tf_op jit(solution)/shard_map/ppermute | solution.py:453
  61.0 0.1 collective-permute-done.9.refs_1_
  61.1 1.2 %collective-permute-done.10.refs_3_ = bf16[1280,128]{1,0:T(8,128)(2,1)S(1)} collective-permute-done((bf16[1280,128]{1,0:T(8,128)(2,1)S(1)}, bf16[1280,128]{1,0:T(8,128)(2,1)S(1)}, u32[]{:S(2)}, u32[]{:S(2)}) %collective-permute-start.10) | collective-permute-done | bytes 327712 | tf_op jit(solution)/shard_map/ppermute | solution.py:587
  62.3 0.3 shard_map.140.blocks
  62.6 0.0 slice-start.1
  62.7 1.7 %shard_map.141 = (bf16[2560,256]{1,0:T(8,128)(2,1)S(1)}, bf16[640,256]{1,0:T(8,128)(2,1)S(1)}) custom-call(bf16[2560,256]{1,0:T(8,128)(2,1)S(1)} %shard_map.140.blocks, bf16[9,32,128]{2,1,0:T(8,128)(2,1)S(1)} %collective-permute-done.8.b_ref.refs_0_, bf16[640,2560]{1,0:T(8,128)(2,1)S(1)} %get-tuple-element.42.x.refs_4_, ...), custom_call_target="tpu_custom_call" | custom-call | tf_op jit(solution)/shard_map/pallas_call | solution.py:635
  64.4 1.6 %collective-permute-start.14 = (bf16[640,256]{1,0:T(8,128)(2,1)S(1)}, bf16[640,256]{1,0:T(8,128)(2,1)S(1)}, u32[]{:S(2)}, u32[]{:S(2)}) collective-permute-start(bf16[640,256]{1,0:T(8,128)(2,1)S(1)} %get-tuple-element.64), channel_id=1, source_target_pairs={{0,2},{1,3},{2,0},{3,1},{4,6},{5,7},{6,4},{7,5},{8,10},{9,11},{10,... | collective-permute-start | bytes 983048 | tf_op jit(solution)/shard_map/ppermute | solution.py:453
  65.9 1.5 %shard_map.142.refs_9_ = bf16[640,256]{1,0:T(8,128)(2,1)S(1)} custom-call(bf16[256,1280]{1,0:T(8,128)(2,1)S(1)} %copy-done.4, bf16[256,1280]{1,0:T(8,128)(2,1)S(1)} %copy-done.5, bf16[384,1280]{1,0:T(8,128)(2,1)S(1)} %copy-done.2, bf16[384,1280]{1,0:T(8,128)(2,1)S(1)} %copy-done.3, bf16[2560,256]{1,0:T(8,128)(2,1)S(1)} %get-tuple-element.58.refs_4_), custom_call_target="tpu_custom_call" | custom-call | tf_op jit(solution)/shard_map/pallas_call | solution.py:643
  67.5 0.6 collective-permute-start.13
  68.1 0.2 shard_map.146.inv
  68.3 0.0 collective-permute-done.12.refs_10_.refs_0_
  68.4 5.2 %shard_map.144 = (f32[1280,256]{1,0:T(8,128)S(1)}, f32[1280,256]{1,0:T(8,128)S(1)}) custom-call(bf16[5120,512]{1,0:T(8,128)(2,1)S(1)} %bitcast.19, bf16[5120,512]{1,0:T(8,128)(2,1)S(1)} %bitcast.19, bf16[4,192,128]{2,1,0:T(8,128)(2,1)S(1)} %get-tuple-element.40.refs_0_, bf16[4,192,128]{2,1,0:T(8,128)(2,1)S(1)} %get-tuple-element.41.refs_1_, ...), custom_call_target="tpu_custom_call" | custom-call | flops 3355443200 | bytes 6553600 | tf_op jit(solution)/shard_map/pallas_call | solution.py:658
  73.6 0.0 copy-start
  73.6 1.0 %copy-done = f32[1280,256]{1,0:T(8,128)} copy-done((f32[1280,256]{1,0:T(8,128)}, f32[1280,256]{1,0:T(8,128)S(1)}, u32[]{:S(2)}) %copy-start) | copy-done | bytes 1310744
  74.7 2.5 %shard_map.145 = (f32[3,128,160]{2,1,0:T(8,128)}, f32[3,8,512]{2,1,0:T(8,128)}) custom-call(bf16[8,192,128]{2,1,0:T(8,128)(2,1)} %all-to-all-done.grad_in, f32[128,1280]{1,0:T(8,128)} %bitcast.21, f32[128,1280]{1,0:T(8,128)} %bitcast.23, f32[128,1280]{1,0:T(8,128)} %bitcast.25, f32[64,512]{1,0:T(8,128)} %refs_3_.3, f32[64,512]{1,0:T(8,128)} %refs_4_.3, ...), custom_call_target="tpu_custom_call" | custom-call | tf_op jit(solution)/shard_map/pallas_call | solution.py:557
  77.2 0.9 %shard_map.147.refs_1_ = bf16[1280,512]{1,0:T(8,128)(2,1)} custom-call(f32[1280,256]{1,0:T(8,128)S(1)} %copy-done.1, f32[1280,128]{1,0:T(8,128)S(1)} %shard_map.146.inv, bf16[640,256]{1,0:T(8,128)(2,1)S(1)} %collective-permute-done.11.refs_4_.refs_0_), custom_call_target="tpu_custom_call" | custom-call | tf_op jit(solution)/shard_map/pallas_call | solution.py:404
  78.1 0.9 %shard_map.148.refs_1_ = bf16[1280,512]{1,0:T(8,128)(2,1)} custom-call(f32[1280,256]{1,0:T(8,128)S(1)} %copy-done.1, f32[1280,128]{1,0:T(8,128)S(1)} %shard_map.146.inv, bf16[640,256]{1,0:T(8,128)(2,1)S(1)} %collective-permute-done.12.refs_10_.refs_0_, bf16[1280,512]{1,0:T(8,128)(2,1)} %shard_map.147.refs_1_), custom_call_target="tpu_custom_call", output_to_operand_aliasing={{}: (3, {})} | custom-call | tf_op jit(solution)/shard_map/pallas_call | solution.py:404
  79.0 0.0 collective-permute-done.14.refs_0_
  79.0 0.9 %shard_map.149.refs_1_ = bf16[1280,512]{1,0:T(8,128)(2,1)} custom-call(f32[1280,256]{1,0:T(8,128)S(1)} %get-tuple-element.63.own, f32[1280,128]{1,0:T(8,128)S(1)} %shard_map.146.inv, bf16[640,256]{1,0:T(8,128)(2,1)S(1)} %collective-permute-done.14.refs_0_, bf16[1280,512]{1,0:T(8,128)(2,1)} %shard_map.148.refs_1_), custom_call_target="tpu_custom_call", output_to_operand_aliasing={{}: (3, {})} | custom-call | tf_op jit(solution)/shard_map/pallas_call | solution.py:404
  79.8 0.9 %collective-permute-done.13.refs_0_ = bf16[640,256]{1,0:T(8,128)(2,1)S(1)} collective-permute-done((bf16[640,256]{1,0:T(8,128)(2,1)S(1)}, bf16[640,256]{1,0:T(8,128)(2,1)S(1)}, u32[]{:S(2)}, u32[]{:S(2)}) %collective-permute-start.13) | collective-permute-done | bytes 327712 | tf_op jit(solution)/shard_map/ppermute | solution.py:453
  80.7 0.9 %shard_map.150 = bf16[1280,512]{1,0:T(8,128)(2,1)} custom-call(f32[1280,256]{1,0:T(8,128)S(1)} %get-tuple-element.63.own, f32[1280,128]{1,0:T(8,128)S(1)} %shard_map.146.inv, bf16[640,256]{1,0:T(8,128)(2,1)S(1)} %collective-permute-done.13.refs_0_, bf16[1280,512]{1,0:T(8,128)(2,1)} %shard_map.149.refs_1_), custom_call_target="tpu_custom_call", output_to_operand_aliasing={{}: (3, {})} | custom-call | tf_op jit(solution)/shard_map/pallas_call | solution.py:404
  (21 shorter events, 0.0 us)
Async XLA Ops:
  0.6 12.7 %collective-permute-start = (bf16[1280,1280]{1,0:T(8,128)(2,1)}, bf16[1280,1280]{1,0:T(8,128)(2,1)}, u32[]{:S(2)}, u32[]{:S(2)}) collective-permute-start(bf16[1280,1280]{1,0:T(8,128)(2,1)} %own_in.5), channel_id=1, source_target_pairs={{0,1},{1,0},{2,3},{3,2},{4,5},{5,4},{6,7},{7,6},{8,9},{9,8},{10,11... | collective-permute-start | bytes 9830408 | tf_op jit(solution)/shard_map/ppermute | solution.py:445
  1.1 10.9 %copy-start.11 = (f32[1280]{0:T(1024)S(1)}, f32[1280]{0:T(1024)}, u32[]{:S(2)}) copy-start(f32[1280]{0:T(1024)} %param.12) | copy-start | bytes 15364
  3.7 19.3 %all-to-all-start = ((bf16[8,192,128]{2,1,0:T(8,128)(2,1)}), bf16[8,192,128]{2,1,0:T(8,128)(2,1)}, u32[]{:S(2)}, u32[]{:S(2)}) async-start(bf16[8,192,128]{2,1,0:T(8,128)(2,1)} %get-tuple-element.34), calls=%async_computation | async-start | bytes 786432 | tf_op jit(solution)/shard_map/all_to_all | solution.py:491
  10.6 19.9 %collective-permute-start.4 = (bf16[2,1280,128]{2,1,0:T(8,128)(2,1)}, bf16[2,1280,128]{2,1,0:T(8,128)(2,1)}, u32[]{:S(2)}, u32[]{:S(2)}) collective-permute-start(bf16[2,1280,128]{2,1,0:T(8,128)(2,1)} %get-tuple-element.48), channel_id=1, source_target_pairs={{0,2},{1,3},{2,0},{3,1},{4,6},{5,7},{6,4},{7,5},{8,10},{9,11},{10,... | collective-permute-start | bytes 1966088 | tf_op jit(solution)/shard_map/ppermute | solution.py:453
  12.1 4.9 %copy-start.6 = (f32[1,1280]{1,0:T(1,128)}, f32[1,1280]{1,0:T(1,128)S(1)}, u32[]{:S(2)}) copy-start(f32[1,1280]{1,0:T(1,128)S(1)} %broadcast_in_dim.3.own_gain) | copy-start | bytes 15364
  12.1 1.2 %collective-permute-start.1 = (f32[1,1280]{1,0:T(1,128)S(1)}, f32[1,1280]{1,0:T(1,128)S(1)}, u32[]{:S(2)}, u32[]{:S(2)}) collective-permute-start(f32[1,1280]{1,0:T(1,128)S(1)} %broadcast_in_dim.3.own_gain), channel_id=1, source_target_pairs={{0,1},{1,0},{2,3},{3,2},{4,5},{5,4},{6,7},{7,6},{8,9},{9,8},{10,11... | collective-permute-start | bytes 15368 | tf_op jit(solution)/shard_map/ppermute | solution.py:445
  13.3 3.7 %copy-start.7 = (f32[1,1280]{1,0:T(1,128)}, f32[1,1280]{1,0:T(1,128)S(1)}, u32[]{:S(2)}) copy-start(f32[1,1280]{1,0:T(1,128)S(1)} %collective-permute-done.1.sibling_gain) | copy-start | bytes 15364
  17.0 0.6 copy-start.10
  25.5 17.1 %all-to-all-start.1 = ((bf16[8,192,128]{2,1,0:T(8,128)(2,1)}), bf16[8,192,128]{2,1,0:T(8,128)(2,1)}, u32[]{:S(2)}, u32[]{:S(2)}) async-start(bf16[8,192,128]{2,1,0:T(8,128)(2,1)} %shard_map.133), calls=%async_computation.1 | async-start | bytes 786432 | tf_op jit(solution)/shard_map/all_to_all | solution.py:569
  30.4 21.7 %collective-permute-start.5 = (bf16[2,1280,128]{2,1,0:T(8,128)(2,1)}, bf16[2,1280,128]{2,1,0:T(8,128)(2,1)}, u32[]{:S(2)}, u32[]{:S(2)}) collective-permute-start(bf16[2,1280,128]{2,1,0:T(8,128)(2,1)} %get-tuple-element.49), channel_id=1, source_target_pairs={{0,2},{1,3},{2,0},{3,1},{4,6},{5,7},{6,4},{7,5},{8,10},{9,11},{10,... | collective-permute-start | bytes 1966088 | tf_op jit(solution)/shard_map/ppermute | solution.py:453
  33.2 11.8 %collective-permute-start.6 = (bf16[1280,128]{1,0:T(8,128)(2,1)}, bf16[1280,128]{1,0:T(8,128)(2,1)}, u32[]{:S(2)}, u32[]{:S(2)}) collective-permute-start(bf16[1280,128]{1,0:T(8,128)(2,1)} %get-tuple-element.51.refs_0_), channel_id=1, source_target_pairs={{0,4},{4,0},{8,12},{12,8},{16,20},{20,16},{24,28},{28,24},{1,5},{5... | collective-permute-start | bytes 983048 | tf_op jit(solution)/shard_map/ppermute | solution.py:587
  35.0 12.0 %collective-permute-start.7 = (bf16[1280,128]{1,0:T(8,128)(2,1)}, bf16[1280,128]{1,0:T(8,128)(2,1)}, u32[]{:S(2)}, u32[]{:S(2)}) collective-permute-start(bf16[1280,128]{1,0:T(8,128)(2,1)} %get-tuple-element.52.refs_2_), channel_id=1, source_target_pairs={{0,8},{4,12},{8,0},{12,4},{16,24},{20,28},{24,16},{28,20},{1,9},{5... | collective-permute-start | bytes 983048 | tf_op jit(solution)/shard_map/ppermute | solution.py:587
  42.6 0.7 copy-start.8
  44.4 5.0 %collective-permute-start.2 = (bf16[4,192,128]{2,1,0:T(8,128)(2,1)S(1)}, bf16[4,192,128]{2,1,0:T(8,128)(2,1)S(1)}, u32[]{:S(2)}, u32[]{:S(2)}) collective-permute-start(bf16[4,192,128]{2,1,0:T(8,128)(2,1)S(1)} %get-tuple-element.40.refs_0_), channel_id=1, source_target_pairs={{0,1},{1,0},{2,3},{3,2},{4,5},{5,4},{6,7},{7,6},{8,9},{9,8},{10,11... | collective-permute-start | bytes 589832 | tf_op jit(solution)/shard_map/ppermute | solution.py:445
  44.4 4.9 %collective-permute-start.3 = (bf16[4,192,128]{2,1,0:T(8,128)(2,1)S(1)}, bf16[4,192,128]{2,1,0:T(8,128)(2,1)S(1)}, u32[]{:S(2)}, u32[]{:S(2)}) collective-permute-start(bf16[4,192,128]{2,1,0:T(8,128)(2,1)S(1)} %get-tuple-element.41.refs_1_), channel_id=1, source_target_pairs={{0,1},{1,0},{2,3},{3,2},{4,5},{5,4},{6,7},{7,6},{8,9},{9,8},{10,11... | collective-permute-start | bytes 589832 | tf_op jit(solution)/shard_map/ppermute | solution.py:445
  45.0 4.4 %collective-permute-start.8 = (bf16[9,32,128]{2,1,0:T(8,128)(2,1)S(1)}, bf16[9,32,128]{2,1,0:T(8,128)(2,1)S(1)}, u32[]{:S(2)}, u32[]{:S(2)}) collective-permute-start(bf16[9,32,128]{2,1,0:T(8,128)(2,1)S(1)} %get-tuple-element.53), channel_id=1, source_target_pairs={{0,2},{1,3},{2,0},{3,1},{4,6},{5,7},{6,4},{7,5},{8,10},{9,11},{10,... | collective-permute-start | bytes 221192 | tf_op jit(solution)/shard_map/ppermute | solution.py:453
  49.4 6.3 %copy-start.2 = (bf16[384,1280]{1,0:T(8,128)(2,1)S(1)}, bf16[384,1280]{1,0:T(8,128)(2,1)}, u32[]{:S(2)}) copy-start(bf16[384,1280]{1,0:T(8,128)(2,1)} %get-tuple-element.45.refs_2_.refs_7_) | copy-start | bytes 2949124
  49.4 6.3 %copy-start.3 = (bf16[384,1280]{1,0:T(8,128)(2,1)S(1)}, bf16[384,1280]{1,0:T(8,128)(2,1)}, u32[]{:S(2)}) copy-start(bf16[384,1280]{1,0:T(8,128)(2,1)} %get-tuple-element.46.refs_3_.refs_8_) | copy-start | bytes 2949124
  49.4 6.3 %copy-start.4 = (bf16[256,1280]{1,0:T(8,128)(2,1)S(1)}, bf16[256,1280]{1,0:T(8,128)(2,1)}, u32[]{:S(2)}) copy-start(bf16[256,1280]{1,0:T(8,128)(2,1)} %get-tuple-element.43.refs_0_.refs_5_) | copy-start | bytes 1966084
  49.4 6.3 %copy-start.5 = (bf16[256,1280]{1,0:T(8,128)(2,1)S(1)}, bf16[256,1280]{1,0:T(8,128)(2,1)}, u32[]{:S(2)}) copy-start(bf16[256,1280]{1,0:T(8,128)(2,1)} %get-tuple-element.44.refs_1_.refs_6_) | copy-start | bytes 1966084
  51.1 9.9 %collective-permute-start.11 = (bf16[640,256]{1,0:T(8,128)(2,1)S(1)}, bf16[640,256]{1,0:T(8,128)(2,1)S(1)}, u32[]{:S(2)}, u32[]{:S(2)}) collective-permute-start(bf16[640,256]{1,0:T(8,128)(2,1)S(1)} %get-tuple-element.54), channel_id=1, source_target_pairs={{0,2},{1,3},{2,0},{3,1},{4,6},{5,7},{6,4},{7,5},{8,10},{9,11},{10,... | collective-permute-start | bytes 983048 | tf_op jit(solution)/shard_map/ppermute | solution.py:453
  53.2 7.9 %collective-permute-start.9 = (bf16[1280,128]{1,0:T(8,128)(2,1)S(1)}, bf16[1280,128]{1,0:T(8,128)(2,1)S(1)}, u32[]{:S(2)}, u32[]{:S(2)}) collective-permute-start(bf16[1280,128]{1,0:T(8,128)(2,1)S(1)} %get-tuple-element.56.refs_0_), channel_id=1, source_target_pairs={{0,4},{4,0},{8,12},{12,8},{16,20},{20,16},{24,28},{28,24},{1,5},{5... | collective-permute-start | bytes 983048 | tf_op jit(solution)/shard_map/ppermute | solution.py:587
  54.3 8.0 %collective-permute-start.10 = (bf16[1280,128]{1,0:T(8,128)(2,1)S(1)}, bf16[1280,128]{1,0:T(8,128)(2,1)S(1)}, u32[]{:S(2)}, u32[]{:S(2)}) collective-permute-start(bf16[1280,128]{1,0:T(8,128)(2,1)S(1)} %get-tuple-element.57.refs_2_), channel_id=1, source_target_pairs={{0,8},{4,12},{8,0},{12,4},{16,24},{20,28},{24,16},{28,20},{1,9},{5... | collective-permute-start | bytes 983048 | tf_op jit(solution)/shard_map/ppermute | solution.py:587
  57.2 11.1 %collective-permute-start.12 = (bf16[640,256]{1,0:T(8,128)(2,1)S(1)}, bf16[640,256]{1,0:T(8,128)(2,1)S(1)}, u32[]{:S(2)}, u32[]{:S(2)}) collective-permute-start(bf16[640,256]{1,0:T(8,128)(2,1)S(1)} %shard_map.143), channel_id=1, source_target_pairs={{0,2},{1,3},{2,0},{3,1},{4,6},{5,7},{6,4},{7,5},{8,10},{9,11},{10,... | collective-permute-start | bytes 983048 | tf_op jit(solution)/shard_map/ppermute | solution.py:453
  62.3 6.0 %slice-start = ((s8[5242880]{0:T(1024)(128)(4,1)}), s8[4194304]{0:T(1024)(128)(4,1)S(1)}, s32[]{:S(2)}) async-start(s8[5242880]{0:T(1024)(128)(4,1)} %bitcast.18), calls=%async_computation.2 | async-start | bytes 8388608
  62.6 5.7 %slice-start.1 = ((s8[5242880]{0:T(1024)(128)(4,1)}), s8[1048576]{0:T(1024)(128)(4,1)S(1)}, s32[]{:S(2)}) async-start(s8[5242880]{0:T(1024)(128)(4,1)} %bitcast.18), calls=%async_computation.3 | async-start | bytes 2097152
  64.4 14.6 %collective-permute-start.14 = (bf16[640,256]{1,0:T(8,128)(2,1)S(1)}, bf16[640,256]{1,0:T(8,128)(2,1)S(1)}, u32[]{:S(2)}, u32[]{:S(2)}) collective-permute-start(bf16[640,256]{1,0:T(8,128)(2,1)S(1)} %get-tuple-element.64), channel_id=1, source_target_pairs={{0,2},{1,3},{2,0},{3,1},{4,6},{5,7},{6,4},{7,5},{8,10},{9,11},{10,... | collective-permute-start | bytes 983048 | tf_op jit(solution)/shard_map/ppermute | solution.py:453
  65.9 2.1 %copy-start.9 = (f32[10,128]{1,0:T(8,128)S(1)}, f32[10,128]{1,0:T(8,128)}, u32[]{:S(2)}) copy-start(f32[10,128]{1,0:T(8,128)} %get-tuple-element.39.sums_ref) | copy-start | bytes 15364
  67.5 13.2 %collective-permute-start.13 = (bf16[640,256]{1,0:T(8,128)(2,1)S(1)}, bf16[640,256]{1,0:T(8,128)(2,1)S(1)}, u32[]{:S(2)}, u32[]{:S(2)}) collective-permute-start(bf16[640,256]{1,0:T(8,128)(2,1)S(1)} %shard_map.142.refs_9_), channel_id=1, source_target_pairs={{0,2},{1,3},{2,0},{3,1},{4,6},{5,7},{6,4},{7,5},{8,10},{9,11},{10,... | collective-permute-start | bytes 983048 | tf_op jit(solution)/shard_map/ppermute | solution.py:453
  73.6 1.1 %copy-start = (f32[1280,256]{1,0:T(8,128)}, f32[1280,256]{1,0:T(8,128)S(1)}, u32[]{:S(2)}) copy-start(f32[1280,256]{1,0:T(8,128)S(1)} %get-tuple-element.60.refs_6_.own) | copy-start | bytes 3932164
  74.7 2.5 %copy-start.1 = (f32[1280,256]{1,0:T(8,128)S(1)}, f32[1280,256]{1,0:T(8,128)}, u32[]{:S(2)}) copy-start(f32[1280,256]{1,0:T(8,128)} %copy-done) | copy-start | bytes 3932164

commit v20 on v18

--- a/solution.py
+++ b/solution.py
@@ -91,10 +91,15 @@
             targets.append(out.at[k])
     copies[0].wait()
     copies[1].wait()
-    pack(down[...], up[...], blocks, lambda i: add_back(blocks.at[i], packed.at[i]))
-    for i, target in enumerate(targets):
-        copies[2 + i].wait()
-        add_back(strips.at[i], target)
+
+    def ready(i):
+        add_back(blocks.at[i], packed.at[i])
+        if i == min(1, blocks.shape[0] - 1):
+            for k, target in enumerate(targets):
+                copies[2 + k].wait()
+                add_back(strips.at[k], target)
+
+    pack(down[...], up[...], blocks, ready)
     for copy in back:
         copy.wait()
 
@@ -574,7 +579,6 @@
                 outside[strip].append((piece, lax.ppermute(piece, "dp", pairs)))
 
     swap_half(0, sent)
-    own_f, squares = lax.optimization_barrier((own_f, squares))
     up_packed = packed_rows - down_rows
     more = pl.cdiv(3 * (tokens // LANES), up_packed)
     piece = jax.ShapeDtypeStruct((n_dp // FACTOR_PIECES, packed_rows, LANES), bf16)

time: 82.3 us -> 82.3 us (level)
  no operation moved by 1% of the time
where the time goes in v20:
time: 82.3 us; the launch traced here: 81.7 us
  Pallas kernels  39.6 us (48%)
  starting transfers between devices  26.4 us (32%)
  waiting for transfers between devices  13.4 us (16%)
  local copies, waits for them, and re-layouts  1.33 us (2%)
  between operations  0.88 us (1%)
    pallas_call x3, Pallas kernels, prepared(): pl.pallas_call(functools.partial(prepare_kernel, first), out_shape=x_shap...  12.8 us
    ppermute x7, starting transfers between devices, to_chip(): return lax.ppermute(value, 'tensor', pairs)  7.73 us
    ppermute x7, waiting for transfers between devices, to_chip(): return lax.ppermute(value, 'tensor', pairs)  7.5 us
    all_to_all x1, starting transfers between devices, body(): exchanged = lax.all_to_all(packed, 'dp', 0, 0, tiled=True)  6.86 us
    ppermute x4, starting transfers between devices, swap_half(): outside[strip].append((piece, lax.ppermute(piece, 'dp', pairs)))  5.69 us
    pallas_call x1, Pallas kernels, body(): pl.pallas_call(functools.partial(own_kernel, static), out_shape=(jax.Shap...  5.23 us
    all_to_all x1, starting transfers between devices, body(): own_f = lax.all_to_all(sent, 'dp', 0, 0, tiled=True)  4.94 us
    pallas_call x4, Pallas kernels, finish(): pl.pallas_call(functools.partial(finish_kernel, len(received), at[0] * bl...  3.52 us
  transfers between devices with their start and end apart: 17, of which 10 were waited for; matrix products, arithmetic and copies ran while one was open for 0% of the time, Pallas kernels for 47%

profile of v20, /device:TPU:0, one launch (start us, length us, event | category | flops | bytes accessed | tf_op | source)
XLA Modules:
  0.0 81.7 jit_solution(515427028508948485)
XLA Ops:
  0.6 0.5 collective-permute-start
  1.2 2.6 %shard_map.130 = (bf16[8,192,128]{2,1,0:T(8,128)(2,1)}, bf16[2,1280,128]{2,1,0:T(8,128)(2,1)}, bf16[2,1280,128]{2,1,0:T(8,128)(2,1)}) custom-call(f32[128,1280]{1,0:T(8,128)} %bitcast.20, f32[64,512]{1,0:T(8,128)} %bitcast.24, bf16[5120,512]{1,0:T(8,128)(2,1)} %sibling_block.1), custom_call_target="tpu_custom_call" | custom-call | tf_op jit(solution)/shard_map/pallas_call | solution.py:477
  3.7 6.9 %all-to-all-start = ((bf16[8,192,128]{2,1,0:T(8,128)(2,1)}), bf16[8,192,128]{2,1,0:T(8,128)(2,1)}, u32[]{:S(2)}, u32[]{:S(2)}) async-start(bf16[8,192,128]{2,1,0:T(8,128)(2,1)} %get-tuple-element.35), calls=%async_computation | async-start | bytes 786432 | tf_op jit(solution)/shard_map/all_to_all | solution.py:492
  10.6 1.5 %collective-permute-start.4 = (bf16[2,1280,128]{2,1,0:T(8,128)(2,1)}, bf16[2,1280,128]{2,1,0:T(8,128)(2,1)}, u32[]{:S(2)}, u32[]{:S(2)}) collective-permute-start(bf16[2,1280,128]{2,1,0:T(8,128)(2,1)} %get-tuple-element.52), channel_id=1, source_target_pairs={{0,2},{1,3},{2,0},{3,1},{4,6},{5,7},{6,4},{7,5},{8,10},{9,11},{10,... | collective-permute-start | bytes 1966088 | tf_op jit(solution)/shard_map/ppermute | solution.py:454
  12.1 0.0 copy-done.9
  12.1 0.1 collective-permute-start.1
  12.2 1.2 %collective-permute-done.1.sibling_gain = f32[1,1280]{1,0:T(1,128)S(1)} collective-permute-done((f32[1,1280]{1,0:T(1,128)S(1)}, f32[1,1280]{1,0:T(1,128)S(1)}, u32[]{:S(2)}, u32[]{:S(2)}) %collective-permute-start.1) | collective-permute-done | bytes 5152 | tf_op jit(solution)/shard_map/ppermute | solution.py:446
  13.3 0.0 collective-permute-done.sibling_in
  13.3 3.7 %shard_map.131 = (bf16[640,2560]{1,0:T(8,128)(2,1)S(1)}, f32[5,128]{1,0:T(8,128)S(1)}) custom-call(bf16[1280,1280]{1,0:T(8,128)(2,1)} %own_in.5, bf16[1280,1280]{1,0:T(8,128)(2,1)} %collective-permute-done.sibling_in, f32[1,1280]{1,0:T(1,128)S(1)} %broadcast_in_dim.3.own_gain, f32[1,1280]{1,0:T(1,128)S(1)} %collective-permute-done.1.sibling_gain), custom_call_target="tpu_custom_call" | custom-call | tf_op jit(solution)/shard_map/pallas_call | solution.py:519
  17.0 0.0 copy-start.8
  17.0 0.6 copy-done.8
  17.6 4.3 %shard_map.132 = (bf16[256,1280]{1,0:T(8,128)(2,1)}, bf16[256,1280]{1,0:T(8,128)(2,1)}, f32[7,128]{1,0:T(8,128)}) custom-call(bf16[1280,1280]{1,0:T(8,128)(2,1)} %own_in.5, bf16[1280,1280]{1,0:T(8,128)(2,1)} %collective-permute-done.sibling_in, f32[1,1280]{1,0:T(1,128)} %copy-done.4, f32[1,1280]{1,0:T(1,128)} %copy-done.5, f32[5,128]{1,0:T(8,128)} %copy-done.8), custom_call_target="tpu_custom_call" | custom-call | tf_op jit(solution)/shard_map/pallas_call | solution.py:519
  21.9 1.1 %all-to-all-done.grad_in = bf16[8,192,128]{2,1,0:T(8,128)(2,1)} async-done(((bf16[8,192,128]{2,1,0:T(8,128)(2,1)}), bf16[8,192,128]{2,1,0:T(8,128)(2,1)}, u32[]{:S(2)}, u32[]{:S(2)}) %all-to-all-start) | async-done | bytes 393248 | tf_op jit(solution)/shard_map/all_to_all | solution.py:492
  23.0 2.5 %shard_map.133 = (f32[3,128,160]{2,1,0:T(8,128)}, f32[3,8,512]{2,1,0:T(8,128)}, bf16[8,192,128]{2,1,0:T(8,128)(2,1)}) custom-call(bf16[8,192,128]{2,1,0:T(8,128)(2,1)} %all-to-all-done.grad_in, f32[128,1280]{1,0:T(8,128)} %bitcast.21, f32[128,1280]{1,0:T(8,128)} %bitcast.22, f32[128,1280]{1,0:T(8,128)} %bitcast.23, f32[64,512]{1,0:T(8,128)} %refs_3_.1, ...), custom_call_target="tpu_custom_call" | custom-call | tf_op jit(solution)/shard_map/pallas_call | solution.py:543
  25.6 4.9 %all-to-all-start.1 = ((bf16[8,192,128]{2,1,0:T(8,128)(2,1)}), bf16[8,192,128]{2,1,0:T(8,128)(2,1)}, u32[]{:S(2)}, u32[]{:S(2)}) async-start(bf16[8,192,128]{2,1,0:T(8,128)(2,1)} %get-tuple-element.41), calls=%async_computation.1 | async-start | bytes 786432 | tf_op jit(solution)/shard_map/all_to_all | solution.py:560
  30.5 0.0 collective-permute-done.4.in_ref
  30.5 0.7 collective-permute-start.5
  31.2 2.0 %shard_map.136 = (bf16[1280,128]{1,0:T(8,128)(2,1)}, bf16[1280,128]{1,0:T(8,128)(2,1)}) custom-call(bf16[2,1280,128]{2,1,0:T(8,128)(2,1)} %collective-permute-done.4.in_ref), custom_call_target="tpu_custom_call" | custom-call | tf_op jit(solution)/shard_map/pallas_call | solution.py:570
  33.3 1.8 %collective-permute-start.6 = (bf16[1280,128]{1,0:T(8,128)(2,1)}, bf16[1280,128]{1,0:T(8,128)(2,1)}, u32[]{:S(2)}, u32[]{:S(2)}) collective-permute-start(bf16[1280,128]{1,0:T(8,128)(2,1)} %get-tuple-element.55.refs_0_), channel_id=1, source_target_pairs={{0,4},{4,0},{8,12},{12,8},{16,20},{20,16},{24,28},{28,24},{1,5},{5... | collective-permute-start | bytes 983048 | tf_op jit(solution)/shard_map/ppermute | solution.py:579
  35.1 1.5 %collective-permute-start.7 = (bf16[1280,128]{1,0:T(8,128)(2,1)}, bf16[1280,128]{1,0:T(8,128)(2,1)}, u32[]{:S(2)}, u32[]{:S(2)}) collective-permute-start(bf16[1280,128]{1,0:T(8,128)(2,1)} %get-tuple-element.56.refs_2_), channel_id=1, source_target_pairs={{0,8},{4,12},{8,0},{12,4},{16,24},{20,28},{24,16},{28,20},{1,9},{5... | collective-permute-start | bytes 983048 | tf_op jit(solution)/shard_map/ppermute | solution.py:579
  36.6 4.9 %shard_map.134 = (bf16[384,1280]{1,0:T(8,128)(2,1)}, bf16[384,1280]{1,0:T(8,128)(2,1)}, f32[10,128]{1,0:T(8,128)}) custom-call(bf16[1280,1280]{1,0:T(8,128)(2,1)} %own_in.5, bf16[1280,1280]{1,0:T(8,128)(2,1)} %collective-permute-done.sibling_in, f32[1,1280]{1,0:T(1,128)} %copy-done.4, f32[1,1280]{1,0:T(1,128)} %copy-done.5, f32[7,128]{1,0:T(8,128)} %get-tuple-element.42.refs_0_), custom_call_target="tpu_custom_call" | custom-call | tf_op jit(solution)/shard_map/pallas_call | solution.py:519
  41.4 1.2 %all-to-all-done.1.factor_ref = bf16[8,192,128]{2,1,0:T(8,128)(2,1)} async-done(((bf16[8,192,128]{2,1,0:T(8,128)(2,1)}), bf16[8,192,128]{2,1,0:T(8,128)(2,1)}, u32[]{:S(2)}, u32[]{:S(2)}) %all-to-all-start.1) | async-done | bytes 393248 | tf_op jit(solution)/shard_map/all_to_all | solution.py:560
  42.6 0.7 copy-done.6
  43.3 1.1 %shard_map.135 = (bf16[9,32,128]{2,1,0:T(8,128)(2,1)S(1)}, bf16[4,192,128]{2,1,0:T(8,128)(2,1)S(1)}, bf16[4,192,128]{2,1,0:T(8,128)(2,1)S(1)}) custom-call(bf16[8,192,128]{2,1,0:T(8,128)(2,1)} %all-to-all-done.1.factor_ref, f32[10,128]{1,0:T(8,128)S(1)} %copy-done.6), custom_call_target="tpu_custom_call" | custom-call | tf_op jit(solution)/shard_map/pallas_call | solution.py:585
  44.4 0.1 collective-permute-start.2
  44.5 0.5 collective-permute-start.3
  45.0 0.1 collective-permute-done.6.refs_1_
  45.1 0.9 %collective-permute-start.8 = (bf16[9,32,128]{2,1,0:T(8,128)(2,1)S(1)}, bf16[9,32,128]{2,1,0:T(8,128)(2,1)S(1)}, u32[]{:S(2)}, u32[]{:S(2)}) collective-permute-start(bf16[9,32,128]{2,1,0:T(8,128)(2,1)S(1)} %get-tuple-element.57), channel_id=1, source_target_pairs={{0,2},{1,3},{2,0},{3,1},{4,6},{5,7},{6,4},{7,5},{8,10},{9,11},{10,... | collective-permute-start | bytes 221192 | tf_op jit(solution)/shard_map/ppermute | solution.py:454
  46.0 1.1 %collective-permute-done.7.refs_3_ = bf16[1280,128]{1,0:T(8,128)(2,1)} collective-permute-done((bf16[1280,128]{1,0:T(8,128)(2,1)}, bf16[1280,128]{1,0:T(8,128)(2,1)}, u32[]{:S(2)}, u32[]{:S(2)}) %collective-permute-start.7) | collective-permute-done | bytes 327712 | tf_op jit(solution)/shard_map/ppermute | solution.py:579
  47.1 1.6 %shard_map.137.blocks = bf16[2560,256]{1,0:T(8,128)(2,1)S(1)} custom-call(bf16[1280,128]{1,0:T(8,128)(2,1)} %get-tuple-element.55.refs_0_, bf16[1280,128]{1,0:T(8,128)(2,1)} %collective-permute-done.6.refs_1_, bf16[1280,128]{1,0:T(8,128)(2,1)} %get-tuple-element.56.refs_2_, bf16[1280,128]{1,0:T(8,128)(2,1)} %collective-permute-done.7.refs_3_), custom_call_target="tpu_custom_call" | custom-call | tf_op jit(solution)/shard_map/pallas_call | solution.py:620
  48.7 0.7 collective-permute-done.8.b_ref.refs_0_
  49.4 0.0 collective-permute-done.2.refs_2_
  49.4 0.0 collective-permute-done.3.refs_3_
  49.5 0.0 copy-start.1
  49.5 0.0 copy-start.2
  49.5 0.0 copy-start.3
  49.5 1.7 %shard_map.138 = (bf16[2560,256]{1,0:T(8,128)(2,1)S(1)}, bf16[640,256]{1,0:T(8,128)(2,1)S(1)}) custom-call(bf16[2560,256]{1,0:T(8,128)(2,1)S(1)} %shard_map.137.blocks, bf16[9,32,128]{2,1,0:T(8,128)(2,1)S(1)} %collective-permute-done.8.b_ref.refs_0_, bf16[640,2560]{1,0:T(8,128)(2,1)S(1)} %get-tuple-element.46.x.refs_4_, ...), custom_call_target="tpu_custom_call" | custom-call | tf_op jit(solution)/shard_map/pallas_call | solution.py:627
  51.2 1.0 %collective-permute-start.11 = (bf16[640,256]{1,0:T(8,128)(2,1)S(1)}, bf16[640,256]{1,0:T(8,128)(2,1)S(1)}, u32[]{:S(2)}, u32[]{:S(2)}) collective-permute-start(bf16[640,256]{1,0:T(8,128)(2,1)S(1)} %get-tuple-element.58), channel_id=1, source_target_pairs={{0,2},{1,3},{2,0},{3,1},{4,6},{5,7},{6,4},{7,5},{8,10},{9,11},{10,... | collective-permute-start | bytes 983048 | tf_op jit(solution)/shard_map/ppermute | solution.py:454
  52.2 0.0 collective-permute-done.5.in_ref
  52.2 1.1 %shard_map.139 = (bf16[1280,128]{1,0:T(8,128)(2,1)S(1)}, bf16[1280,128]{1,0:T(8,128)(2,1)S(1)}) custom-call(bf16[2,1280,128]{2,1,0:T(8,128)(2,1)} %collective-permute-done.5.in_ref), custom_call_target="tpu_custom_call" | custom-call | tf_op jit(solution)/shard_map/pallas_call | solution.py:570
  53.3 1.1 %collective-permute-start.9 = (bf16[1280,128]{1,0:T(8,128)(2,1)S(1)}, bf16[1280,128]{1,0:T(8,128)(2,1)S(1)}, u32[]{:S(2)}, u32[]{:S(2)}) collective-permute-start(bf16[1280,128]{1,0:T(8,128)(2,1)S(1)} %get-tuple-element.60.refs_0_), channel_id=1, source_target_pairs={{0,4},{4,0},{8,12},{12,8},{16,20},{20,16},{24,28},{28,24},{1,5},{5... | collective-permute-start | bytes 983048 | tf_op jit(solution)/shard_map/ppermute | solution.py:579
  54.4 1.3 %collective-permute-start.10 = (bf16[1280,128]{1,0:T(8,128)(2,1)S(1)}, bf16[1280,128]{1,0:T(8,128)(2,1)S(1)}, u32[]{:S(2)}, u32[]{:S(2)}) collective-permute-start(bf16[1280,128]{1,0:T(8,128)(2,1)S(1)} %get-tuple-element.61.refs_2_), channel_id=1, source_target_pairs={{0,8},{4,12},{8,0},{12,4},{16,24},{20,28},{24,16},{28,20},{1,9},{5... | collective-permute-start | bytes 983048 | tf_op jit(solution)/shard_map/ppermute | solution.py:579
  55.7 0.0 copy-done
  55.7 1.6 %shard_map.143 = bf16[640,256]{1,0:T(8,128)(2,1)S(1)} custom-call(bf16[256,1280]{1,0:T(8,128)(2,1)S(1)} %copy-done.2, bf16[256,1280]{1,0:T(8,128)(2,1)S(1)} %copy-done.3, bf16[384,1280]{1,0:T(8,128)(2,1)S(1)} %copy-done, bf16[384,1280]{1,0:T(8,128)(2,1)S(1)} %copy-done.1, bf16[2560,256]{1,0:T(8,128)(2,1)S(1)} %get-tuple-element.63.refs_4_), custom_call_target="tpu_custom_call" | custom-call | tf_op jit(solution)/shard_map/pallas_call | solution.py:635
  57.3 1.4 %collective-permute-start.12 = (bf16[640,256]{1,0:T(8,128)(2,1)S(1)}, bf16[640,256]{1,0:T(8,128)(2,1)S(1)}, u32[]{:S(2)}, u32[]{:S(2)}) collective-permute-start(bf16[640,256]{1,0:T(8,128)(2,1)S(1)} %shard_map.143), channel_id=1, source_target_pairs={{0,2},{1,3},{2,0},{3,1},{4,6},{5,7},{6,4},{7,5},{8,10},{9,11},{10,... | collective-permute-start | bytes 983048 | tf_op jit(solution)/shard_map/ppermute | solution.py:454
  58.7 2.3 %collective-permute-done.11.refs_4_.refs_0_ = bf16[640,256]{1,0:T(8,128)(2,1)S(1)} collective-permute-done((bf16[640,256]{1,0:T(8,128)(2,1)S(1)}, bf16[640,256]{1,0:T(8,128)(2,1)S(1)}, u32[]{:S(2)}, u32[]{:S(2)}) %collective-permute-start.11) | collective-permute-done | bytes 327712 | tf_op jit(solution)/shard_map/ppermute | solution.py:454
  61.0 0.1 collective-permute-done.9.refs_1_
  61.2 1.2 %collective-permute-done.10.refs_3_ = bf16[1280,128]{1,0:T(8,128)(2,1)S(1)} collective-permute-done((bf16[1280,128]{1,0:T(8,128)(2,1)S(1)}, bf16[1280,128]{1,0:T(8,128)(2,1)S(1)}, u32[]{:S(2)}, u32[]{:S(2)}) %collective-permute-start.10) | collective-permute-done | bytes 327712 | tf_op jit(solution)/shard_map/ppermute | solution.py:579
  62.4 0.3 shard_map.140.blocks
  62.7 0.0 slice-start.1
  62.7 1.7 %shard_map.141 = (bf16[2560,256]{1,0:T(8,128)(2,1)S(1)}, bf16[640,256]{1,0:T(8,128)(2,1)S(1)}) custom-call(bf16[2560,256]{1,0:T(8,128)(2,1)S(1)} %shard_map.140.blocks, bf16[9,32,128]{2,1,0:T(8,128)(2,1)S(1)} %collective-permute-done.8.b_ref.refs_0_, bf16[640,2560]{1,0:T(8,128)(2,1)S(1)} %get-tuple-element.46.x.refs_4_, ...), custom_call_target="tpu_custom_call" | custom-call | tf_op jit(solution)/shard_map/pallas_call | solution.py:627
  64.4 1.6 %collective-permute-start.14 = (bf16[640,256]{1,0:T(8,128)(2,1)S(1)}, bf16[640,256]{1,0:T(8,128)(2,1)S(1)}, u32[]{:S(2)}, u32[]{:S(2)}) collective-permute-start(bf16[640,256]{1,0:T(8,128)(2,1)S(1)} %get-tuple-element.65), channel_id=1, source_target_pairs={{0,2},{1,3},{2,0},{3,1},{4,6},{5,7},{6,4},{7,5},{8,10},{9,11},{10,... | collective-permute-start | bytes 983048 | tf_op jit(solution)/shard_map/ppermute | solution.py:454
  66.0 1.6 %shard_map.142.refs_9_ = bf16[640,256]{1,0:T(8,128)(2,1)S(1)} custom-call(bf16[256,1280]{1,0:T(8,128)(2,1)S(1)} %copy-done.2, bf16[256,1280]{1,0:T(8,128)(2,1)S(1)} %copy-done.3, bf16[384,1280]{1,0:T(8,128)(2,1)S(1)} %copy-done, bf16[384,1280]{1,0:T(8,128)(2,1)S(1)} %copy-done.1, bf16[2560,256]{1,0:T(8,128)(2,1)S(1)} %get-tuple-element.62.refs_4_), custom_call_target="tpu_custom_call" | custom-call | tf_op jit(solution)/shard_map/pallas_call | solution.py:635
  67.6 0.6 collective-permute-start.13
  68.2 0.0 copy-done.7
  68.2 0.2 shard_map.145.inv
  68.4 0.0 collective-permute-done.12.refs_10_.refs_0_
  68.4 5.2 %shard_map.144 = (f32[1280,256]{1,0:T(8,128)S(1)}, f32[1280,256]{1,0:T(8,128)S(1)}) custom-call(bf16[5120,512]{1,0:T(8,128)(2,1)S(1)} %bitcast.19, bf16[5120,512]{1,0:T(8,128)(2,1)S(1)} %bitcast.19, bf16[4,192,128]{2,1,0:T(8,128)(2,1)S(1)} %get-tuple-element.44.refs_0_, bf16[4,192,128]{2,1,0:T(8,128)(2,1)S(1)} %get-tuple-element.45.refs_1_, ...), custom_call_target="tpu_custom_call" | custom-call | flops 3355443200 | bytes 6553600 | tf_op jit(solution)/shard_map/pallas_call | solution.py:650
  73.7 0.9 %shard_map.146.refs_1_ = bf16[1280,512]{1,0:T(8,128)(2,1)} custom-call(f32[1280,256]{1,0:T(8,128)S(1)} %get-tuple-element.66.own, f32[1280,128]{1,0:T(8,128)S(1)} %shard_map.145.inv, bf16[640,256]{1,0:T(8,128)(2,1)S(1)} %collective-permute-done.11.refs_4_.refs_0_), custom_call_target="tpu_custom_call" | custom-call | tf_op jit(solution)/shard_map/pallas_call | solution.py:405
  74.6 0.9 %shard_map.147.refs_1_ = bf16[1280,512]{1,0:T(8,128)(2,1)} custom-call(f32[1280,256]{1,0:T(8,128)S(1)} %get-tuple-element.66.own, f32[1280,128]{1,0:T(8,128)S(1)} %shard_map.145.inv, bf16[640,256]{1,0:T(8,128)(2,1)S(1)} %collective-permute-done.12.refs_10_.refs_0_, bf16[1280,512]{1,0:T(8,128)(2,1)} %shard_map.146.refs_1_), custom_call_target="tpu_custom_call", output_to_operand_aliasing={{}: (3, {})} | custom-call | tf_op jit(solution)/shard_map/pallas_call | solution.py:405
  75.4 0.0 collective-permute-done.14.refs_0_
  75.5 0.9 %shard_map.148.refs_1_ = bf16[1280,512]{1,0:T(8,128)(2,1)} custom-call(f32[1280,256]{1,0:T(8,128)S(1)} %get-tuple-element.64.own, f32[1280,128]{1,0:T(8,128)S(1)} %shard_map.145.inv, bf16[640,256]{1,0:T(8,128)(2,1)S(1)} %collective-permute-done.14.refs_0_, bf16[1280,512]{1,0:T(8,128)(2,1)} %shard_map.147.refs_1_), custom_call_target="tpu_custom_call", output_to_operand_aliasing={{}: (3, {})} | custom-call | tf_op jit(solution)/shard_map/pallas_call | solution.py:405
  76.3 4.4 %collective-permute-done.13.refs_0_ = bf16[640,256]{1,0:T(8,128)(2,1)S(1)} collective-permute-done((bf16[640,256]{1,0:T(8,128)(2,1)S(1)}, bf16[640,256]{1,0:T(8,128)(2,1)S(1)}, u32[]{:S(2)}, u32[]{:S(2)}) %collective-permute-start.13) | collective-permute-done | bytes 327712 | tf_op jit(solution)/shard_map/ppermute | solution.py:454
  80.8 0.9 %shard_map.149 = bf16[1280,512]{1,0:T(8,128)(2,1)} custom-call(f32[1280,256]{1,0:T(8,128)S(1)} %get-tuple-element.64.own, f32[1280,128]{1,0:T(8,128)S(1)} %shard_map.145.inv, bf16[640,256]{1,0:T(8,128)(2,1)S(1)} %collective-permute-done.13.refs_0_, bf16[1280,512]{1,0:T(8,128)(2,1)} %shard_map.148.refs_1_), custom_call_target="tpu_custom_call", output_to_operand_aliasing={{}: (3, {})} | custom-call | tf_op jit(solution)/shard_map/pallas_call | solution.py:405
  (16 shorter events, 0.0 us)
Async XLA Ops:
  0.6 12.7 %collective-permute-start = (bf16[1280,1280]{1,0:T(8,128)(2,1)}, bf16[1280,1280]{1,0:T(8,128)(2,1)}, u32[]{:S(2)}, u32[]{:S(2)}) collective-permute-start(bf16[1280,1280]{1,0:T(8,128)(2,1)} %own_in.5), channel_id=1, source_target_pairs={{0,1},{1,0},{2,3},{3,2},{4,5},{5,4},{6,7},{7,6},{8,9},{9,8},{10,11... | collective-permute-start | bytes 9830408 | tf_op jit(solution)/shard_map/ppermute | solution.py:446
  1.1 10.9 %copy-start.9 = (f32[1280]{0:T(1024)S(1)}, f32[1280]{0:T(1024)}, u32[]{:S(2)}) copy-start(f32[1280]{0:T(1024)} %param.12) | copy-start | bytes 15364
  3.7 19.3 %all-to-all-start = ((bf16[8,192,128]{2,1,0:T(8,128)(2,1)}), bf16[8,192,128]{2,1,0:T(8,128)(2,1)}, u32[]{:S(2)}, u32[]{:S(2)}) async-start(bf16[8,192,128]{2,1,0:T(8,128)(2,1)} %get-tuple-element.35), calls=%async_computation | async-start | bytes 786432 | tf_op jit(solution)/shard_map/all_to_all | solution.py:492
  10.6 19.9 %collective-permute-start.4 = (bf16[2,1280,128]{2,1,0:T(8,128)(2,1)}, bf16[2,1280,128]{2,1,0:T(8,128)(2,1)}, u32[]{:S(2)}, u32[]{:S(2)}) collective-permute-start(bf16[2,1280,128]{2,1,0:T(8,128)(2,1)} %get-tuple-element.52), channel_id=1, source_target_pairs={{0,2},{1,3},{2,0},{3,1},{4,6},{5,7},{6,4},{7,5},{8,10},{9,11},{10,... | collective-permute-start | bytes 1966088 | tf_op jit(solution)/shard_map/ppermute | solution.py:454
  12.1 4.9 %copy-start.4 = (f32[1,1280]{1,0:T(1,128)}, f32[1,1280]{1,0:T(1,128)S(1)}, u32[]{:S(2)}) copy-start(f32[1,1280]{1,0:T(1,128)S(1)} %broadcast_in_dim.3.own_gain) | copy-start | bytes 15364
  12.1 1.2 %collective-permute-start.1 = (f32[1,1280]{1,0:T(1,128)S(1)}, f32[1,1280]{1,0:T(1,128)S(1)}, u32[]{:S(2)}, u32[]{:S(2)}) collective-permute-start(f32[1,1280]{1,0:T(1,128)S(1)} %broadcast_in_dim.3.own_gain), channel_id=1, source_target_pairs={{0,1},{1,0},{2,3},{3,2},{4,5},{5,4},{6,7},{7,6},{8,9},{9,8},{10,11... | collective-permute-start | bytes 15368 | tf_op jit(solution)/shard_map/ppermute | solution.py:446
  13.3 3.7 %copy-start.5 = (f32[1,1280]{1,0:T(1,128)}, f32[1,1280]{1,0:T(1,128)S(1)}, u32[]{:S(2)}) copy-start(f32[1,1280]{1,0:T(1,128)S(1)} %collective-permute-done.1.sibling_gain) | copy-start | bytes 15364
  17.0 0.6 copy-start.8
  25.6 17.1 %all-to-all-start.1 = ((bf16[8,192,128]{2,1,0:T(8,128)(2,1)}), bf16[8,192,128]{2,1,0:T(8,128)(2,1)}, u32[]{:S(2)}, u32[]{:S(2)}) async-start(bf16[8,192,128]{2,1,0:T(8,128)(2,1)} %get-tuple-element.41), calls=%async_computation.1 | async-start | bytes 786432 | tf_op jit(solution)/shard_map/all_to_all | solution.py:560
  30.5 21.7 %collective-permute-start.5 = (bf16[2,1280,128]{2,1,0:T(8,128)(2,1)}, bf16[2,1280,128]{2,1,0:T(8,128)(2,1)}, u32[]{:S(2)}, u32[]{:S(2)}) collective-permute-start(bf16[2,1280,128]{2,1,0:T(8,128)(2,1)} %get-tuple-element.53), channel_id=1, source_target_pairs={{0,2},{1,3},{2,0},{3,1},{4,6},{5,7},{6,4},{7,5},{8,10},{9,11},{10,... | collective-permute-start | bytes 1966088 | tf_op jit(solution)/shard_map/ppermute | solution.py:454
  33.3 11.8 %collective-permute-start.6 = (bf16[1280,128]{1,0:T(8,128)(2,1)}, bf16[1280,128]{1,0:T(8,128)(2,1)}, u32[]{:S(2)}, u32[]{:S(2)}) collective-permute-start(bf16[1280,128]{1,0:T(8,128)(2,1)} %get-tuple-element.55.refs_0_), channel_id=1, source_target_pairs={{0,4},{4,0},{8,12},{12,8},{16,20},{20,16},{24,28},{28,24},{1,5},{5... | collective-permute-start | bytes 983048 | tf_op jit(solution)/shard_map/ppermute | solution.py:579
  35.1 12.0 %collective-permute-start.7 = (bf16[1280,128]{1,0:T(8,128)(2,1)}, bf16[1280,128]{1,0:T(8,128)(2,1)}, u32[]{:S(2)}, u32[]{:S(2)}) collective-permute-start(bf16[1280,128]{1,0:T(8,128)(2,1)} %get-tuple-element.56.refs_2_), channel_id=1, source_target_pairs={{0,8},{4,12},{8,0},{12,4},{16,24},{20,28},{24,16},{28,20},{1,9},{5... | collective-permute-start | bytes 983048 | tf_op jit(solution)/shard_map/ppermute | solution.py:579
  42.6 0.7 copy-start.6
  44.4 5.0 %collective-permute-start.2 = (bf16[4,192,128]{2,1,0:T(8,128)(2,1)S(1)}, bf16[4,192,128]{2,1,0:T(8,128)(2,1)S(1)}, u32[]{:S(2)}, u32[]{:S(2)}) collective-permute-start(bf16[4,192,128]{2,1,0:T(8,128)(2,1)S(1)} %get-tuple-element.44.refs_0_), channel_id=1, source_target_pairs={{0,1},{1,0},{2,3},{3,2},{4,5},{5,4},{6,7},{7,6},{8,9},{9,8},{10,11... | collective-permute-start | bytes 589832 | tf_op jit(solution)/shard_map/ppermute | solution.py:446
  44.5 4.9 %collective-permute-start.3 = (bf16[4,192,128]{2,1,0:T(8,128)(2,1)S(1)}, bf16[4,192,128]{2,1,0:T(8,128)(2,1)S(1)}, u32[]{:S(2)}, u32[]{:S(2)}) collective-permute-start(bf16[4,192,128]{2,1,0:T(8,128)(2,1)S(1)} %get-tuple-element.45.refs_1_), channel_id=1, source_target_pairs={{0,1},{1,0},{2,3},{3,2},{4,5},{5,4},{6,7},{7,6},{8,9},{9,8},{10,11... | collective-permute-start | bytes 589832 | tf_op jit(solution)/shard_map/ppermute | solution.py:446
  45.1 4.4 %collective-permute-start.8 = (bf16[9,32,128]{2,1,0:T(8,128)(2,1)S(1)}, bf16[9,32,128]{2,1,0:T(8,128)(2,1)S(1)}, u32[]{:S(2)}, u32[]{:S(2)}) collective-permute-start(bf16[9,32,128]{2,1,0:T(8,128)(2,1)S(1)} %get-tuple-element.57), channel_id=1, source_target_pairs={{0,2},{1,3},{2,0},{3,1},{4,6},{5,7},{6,4},{7,5},{8,10},{9,11},{10,... | collective-permute-start | bytes 221192 | tf_op jit(solution)/shard_map/ppermute | solution.py:454
  49.4 6.3 %copy-start = (bf16[384,1280]{1,0:T(8,128)(2,1)S(1)}, bf16[384,1280]{1,0:T(8,128)(2,1)}, u32[]{:S(2)}) copy-start(bf16[384,1280]{1,0:T(8,128)(2,1)} %get-tuple-element.49.refs_2_.refs_7_) | copy-start | bytes 2949124
  49.5 6.3 %copy-start.1 = (bf16[384,1280]{1,0:T(8,128)(2,1)S(1)}, bf16[384,1280]{1,0:T(8,128)(2,1)}, u32[]{:S(2)}) copy-start(bf16[384,1280]{1,0:T(8,128)(2,1)} %get-tuple-element.50.refs_3_.refs_8_) | copy-start | bytes 2949124
  49.5 6.3 %copy-start.2 = (bf16[256,1280]{1,0:T(8,128)(2,1)S(1)}, bf16[256,1280]{1,0:T(8,128)(2,1)}, u32[]{:S(2)}) copy-start(bf16[256,1280]{1,0:T(8,128)(2,1)} %get-tuple-element.47.refs_0_.refs_5_) | copy-start | bytes 1966084
  49.5 6.2 %copy-start.3 = (bf16[256,1280]{1,0:T(8,128)(2,1)S(1)}, bf16[256,1280]{1,0:T(8,128)(2,1)}, u32[]{:S(2)}) copy-start(bf16[256,1280]{1,0:T(8,128)(2,1)} %get-tuple-element.48.refs_1_.refs_6_) | copy-start | bytes 1966084
  51.2 9.9 %collective-permute-start.11 = (bf16[640,256]{1,0:T(8,128)(2,1)S(1)}, bf16[640,256]{1,0:T(8,128)(2,1)S(1)}, u32[]{:S(2)}, u32[]{:S(2)}) collective-permute-start(bf16[640,256]{1,0:T(8,128)(2,1)S(1)} %get-tuple-element.58), channel_id=1, source_target_pairs={{0,2},{1,3},{2,0},{3,1},{4,6},{5,7},{6,4},{7,5},{8,10},{9,11},{10,... | collective-permute-start | bytes 983048 | tf_op jit(solution)/shard_map/ppermute | solution.py:454
  53.3 7.8 %collective-permute-start.9 = (bf16[1280,128]{1,0:T(8,128)(2,1)S(1)}, bf16[1280,128]{1,0:T(8,128)(2,1)S(1)}, u32[]{:S(2)}, u32[]{:S(2)}) collective-permute-start(bf16[1280,128]{1,0:T(8,128)(2,1)S(1)} %get-tuple-element.60.refs_0_), channel_id=1, source_target_pairs={{0,4},{4,0},{8,12},{12,8},{16,20},{20,16},{24,28},{28,24},{1,5},{5... | collective-permute-start | bytes 983048 | tf_op jit(solution)/shard_map/ppermute | solution.py:579
  54.4 8.0 %collective-permute-start.10 = (bf16[1280,128]{1,0:T(8,128)(2,1)S(1)}, bf16[1280,128]{1,0:T(8,128)(2,1)S(1)}, u32[]{:S(2)}, u32[]{:S(2)}) collective-permute-start(bf16[1280,128]{1,0:T(8,128)(2,1)S(1)} %get-tuple-element.61.refs_2_), channel_id=1, source_target_pairs={{0,8},{4,12},{8,0},{12,4},{16,24},{20,28},{24,16},{28,20},{1,9},{5... | collective-permute-start | bytes 983048 | tf_op jit(solution)/shard_map/ppermute | solution.py:579
  57.3 11.1 %collective-permute-start.12 = (bf16[640,256]{1,0:T(8,128)(2,1)S(1)}, bf16[640,256]{1,0:T(8,128)(2,1)S(1)}, u32[]{:S(2)}, u32[]{:S(2)}) collective-permute-start(bf16[640,256]{1,0:T(8,128)(2,1)S(1)} %shard_map.143), channel_id=1, source_target_pairs={{0,2},{1,3},{2,0},{3,1},{4,6},{5,7},{6,4},{7,5},{8,10},{9,11},{10,... | collective-permute-start | bytes 983048 | tf_op jit(solution)/shard_map/ppermute | solution.py:454
  62.4 6.1 %slice-start = ((s8[5242880]{0:T(1024)(128)(4,1)}), s8[4194304]{0:T(1024)(128)(4,1)S(1)}, s32[]{:S(2)}) async-start(s8[5242880]{0:T(1024)(128)(4,1)} %bitcast.18), calls=%async_computation.2 | async-start | bytes 8388608
  62.7 5.7 %slice-start.1 = ((s8[5242880]{0:T(1024)(128)(4,1)}), s8[1048576]{0:T(1024)(128)(4,1)S(1)}, s32[]{:S(2)}) async-start(s8[5242880]{0:T(1024)(128)(4,1)} %bitcast.18), calls=%async_computation.3 | async-start | bytes 2097152
  64.4 11.0 %collective-permute-start.14 = (bf16[640,256]{1,0:T(8,128)(2,1)S(1)}, bf16[640,256]{1,0:T(8,128)(2,1)S(1)}, u32[]{:S(2)}, u32[]{:S(2)}) collective-permute-start(bf16[640,256]{1,0:T(8,128)(2,1)S(1)} %get-tuple-element.65), channel_id=1, source_target_pairs={{0,2},{1,3},{2,0},{3,1},{4,6},{5,7},{6,4},{7,5},{8,10},{9,11},{10,... | collective-permute-start | bytes 983048 | tf_op jit(solution)/shard_map/ppermute | solution.py:454
  66.0 2.2 %copy-start.7 = (f32[10,128]{1,0:T(8,128)S(1)}, f32[10,128]{1,0:T(8,128)}, u32[]{:S(2)}) copy-start(f32[10,128]{1,0:T(8,128)} %get-tuple-element.43.sums_ref) | copy-start | bytes 15364
  67.6 13.2 %collective-permute-start.13 = (bf16[640,256]{1,0:T(8,128)(2,1)S(1)}, bf16[640,256]{1,0:T(8,128)(2,1)S(1)}, u32[]{:S(2)}, u32[]{:S(2)}) collective-permute-start(bf16[640,256]{1,0:T(8,128)(2,1)S(1)} %shard_map.142.refs_9_), channel_id=1, source_target_pairs={{0,2},{1,3},{2,0},{3,1},{4,6},{5,7},{6,4},{7,5},{8,10},{9,11},{10,... | collective-permute-start | bytes 983048 | tf_op jit(solution)/shard_map/ppermute | solution.py:454

commit v21 on v20

--- a/solution.py
+++ b/solution.py
@@ -109,15 +109,19 @@
         out[...] = in_ref[k]
 
 
-def prepare_kernel(first, own_in, sibling_in, own_gain, sibling_gain, *refs):
+def prepare_kernel(first, summed, own_in, sibling_in, own_gain, sibling_gain, *refs):
     own, sibling, squares, sem = refs[-4:]
-    rows, features = own.shape
-    together = refs[-6].shape[1] > features
-    outs, sums_ref = refs[-6 if together else -7 : -5], refs[-5]
-    before = refs[: -6 if together else -7]
+    copied, features = own.shape
+    refs = refs[:-4]
+    before, sums_ref = [], None
+    if summed:
+        refs, sums_ref = refs[:-1], refs[-1]
+    together = refs[-1].shape[1] > features
+    outs = refs[-1:] if together else refs[-2:]
+    before = refs[: -len(outs)]
+    rows = outs[0].shape[0]
     block = LANES if rows % LANES == 0 else rows
     tile = 16 if block % 16 == 0 else block
-    count = rows // block
     raw = ((own_in, own), (sibling_in, sibling))
     loads = [
         [
@@ -128,15 +132,16 @@
             )
             for side, (source, target) in enumerate(raw)
         ]
-        for k in range(count)
+        for k in range(copied // block)
     ]
     for pair in loads:
         for copy in pair:
             copy.start()
     stores = []
-    for k in range(count):
-        for copy in loads[k]:
+    for k, pair in enumerate(loads):
+        for copy in pair:
             copy.wait()
+        scale, add = k * block < rows, k * block < summed
 
         @pl.loop(0, block // tile, unroll=2)
         def _(i):
@@ -144,28 +149,32 @@
             total = None
             for side, (ref, gain) in enumerate(((own, own_gain), (sibling, sibling_gain))):
                 value = ref[at, :].astype(jnp.float32)
-                scaled = (value * gain[...]).astype(ref.dtype)
-                if together:
-                    outs[0][at, side * features : (side + 1) * features] = scaled
-                else:
-                    ref[at, :] = scaled
-                total = value * value if total is None else total + value * value
-            total = jnp.sum(total, axis=1, keepdims=True)
-            squares[at, :] = jnp.broadcast_to(total, (tile, LANES))
-
-        if not together:
+                if scale:
+                    scaled = (value * gain[...]).astype(ref.dtype)
+                    if together:
+                        outs[0][at, side * features : (side + 1) * features] = scaled
+                    else:
+                        ref[at, :] = scaled
+                if add:
+                    total = value * value if total is None else total + value * value
+            if add:
+                total = jnp.sum(total, axis=1, keepdims=True)
+                squares[at, :] = jnp.broadcast_to(total, (tile, LANES))
+
+        if scale and not together:
             part = pl.ds(k * block, block)
             for side, (source, out) in enumerate(((own, outs[0]), (sibling, outs[1]))):
-                place = sem.at[2 * (count + k) + side]
+                place = sem.at[2 * (len(loads) + k) + side]
                 stores.append(pltpu.make_async_copy(source.at[part], out.at[part], place))
                 stores[-1].start()
-    done = 0
-    for ref in before:
-        sums_ref[: ref.shape[0]] = ref[...]
-        done = ref.shape[0]
-    for i in range(rows // LANES):
-        row = squares[i * LANES : (i + 1) * LANES, :].T[:1]
-        sums_ref[done + i : done + i + 1] = row
+    if summed:
+        done = 0
+        for ref in before:
+            sums_ref[: ref.shape[0]] = ref[...]
+            done = ref.shape[0]
+        for i in range(summed // LANES):
+            row = squares[i * LANES : (i + 1) * LANES, :].T[:1]
+            sums_ref[done + i : done + i + 1] = row
     for copy in stores:
         copy.wait()
 
@@ -509,37 +518,37 @@
     some = tokens // TOKEN_HALVES
     operands = [prompt_hidden_input, to_sibling(prompt_hidden_input), gain, to_sibling(gain)]
 
-    def prepared(first, size, before, in_place, limit):
+    def prepared(first, size, summed, before, in_place, limit):
         if in_place:
             x_shape = (jax.ShapeDtypeStruct((size, CORES * features), bf16),)
             x_specs = tuple(in_vmem(1))
         else:
             x_shape = (jax.ShapeDtypeStruct((size, features), bf16),) * 2
             x_specs = tuple(anywhere(2))
-        *x, squares = pl.pallas_call(
-            functools.partial(prepare_kernel, first),
-            out_shape=x_shape
-            + (jax.ShapeDtypeStruct(((first + size) // LANES, LANES), f32),),
+        copied = max(size, summed)
+        if summed:
+            x_shape += (jax.ShapeDtypeStruct(((first + summed) // LANES, LANES), f32),)
+            x_specs += tuple(in_vmem(1))
+        outs = pl.pallas_call(
+            functools.partial(prepare_kernel, first, summed),
+            out_shape=x_shape,
             in_specs=anywhere(2) + in_vmem(2 + len(before)),
-            out_specs=x_specs + tuple(in_vmem(1)),
+            out_specs=x_specs,
             scratch_shapes=[
-                pltpu.VMEM((size, features), bf16),
-                pltpu.VMEM((size, features), bf16),
-                pltpu.VMEM((size, LANES), f32),
-                pltpu.SemaphoreType.DMA((4 * pl.cdiv(size, LANES),)),
+                pltpu.VMEM((copied, features), bf16),
+                pltpu.VMEM((copied, features), bf16),
+                pltpu.VMEM((copied, LANES), f32),
+                pltpu.SemaphoreType.DMA((4 * pl.cdiv(copied, LANES),)),
             ],
             compiler_params=pltpu.CompilerParams(vmem_limit_bytes=limit),
         )(*operands, *before)
-        return x, squares
+        return (list(outs[:-1]), outs[-1]) if summed else (list(outs), None)
 
     cut = some // 2 // LANES * LANES
-    x0, squares = prepared(0, some, [], True, PREPARE_VMEM_BYTES)
-    x1 = []
-    if cut > 0:
-        x1, squares = prepared(some, cut, [squares], False, LARGE_VMEM_BYTES)
+    x0, squares = prepared(0, some, some, [], True, PREPARE_VMEM_BYTES)
+    x1, squares = prepared(some, cut, some, [squares], False, LARGE_VMEM_BYTES)
     exchanged, squares = lax.optimization_barrier((exchanged, squares))
-    last, squares = prepared(some + cut, some - cut, [squares], False, LARGE_VMEM_BYTES)
-    x1 = x1 + last
+    last, _ = prepared(some + cut, some - cut, 0, [], False, LARGE_VMEM_BYTES)
     a_next, b_next, sent = pl.pallas_call(
         adam_kernel,
         out_shape=(
@@ -579,6 +588,8 @@
                 outside[strip].append((piece, lax.ppermute(piece, "dp", pairs)))
 
     swap_half(0, sent)
+    own_f, last = lax.optimization_barrier((own_f, last))
+    x1 = x1 + last
     up_packed = packed_rows - down_rows
     more = pl.cdiv(3 * (tokens // LANES), up_packed)
     piece = jax.ShapeDtypeStruct((n_dp // FACTOR_PIECES, packed_rows, LANES), bf16)

time: 82.3 us -> 83 us (level)
  waiting for transfers between devices: 13.4 us -> 14.9 us
    all_to_all x1, waiting for transfers between devices: 1.2 us -> 2.81 us  [body(): own_f = lax.all_to_all(sent, 'dp', 0, 0, tiled=True)]
  transfers between devices with their start and end apart: 17 -> 17, of which waited for: 10 -> 9; matrix products, arithmetic and copies ran while one was open for 0% -> 0% of each run, Pallas kernels for 47% -> 46%
where the time goes in v21:
time: 83 us; the launch traced here: 82.4 us
  Pallas kernels  38.9 us (47%)
  starting transfers between devices  27.2 us (33%)
  waiting for transfers between devices  14.9 us (18%)
  between operations  0.88 us (1%)
    pallas_call x3, Pallas kernels, prepared(): pl.pallas_call(functools.partial(prepare_kernel, first, summed), out_shap...  12.1 us
    ppermute x7, starting transfers between devices, to_chip(): return lax.ppermute(value, 'tensor', pairs)  7.59 us
    ppermute x7, waiting for transfers between devices, to_chip(): return lax.ppermute(value, 'tensor', pairs)  7.39 us
    all_to_all x1, starting transfers between devices, body(): exchanged = lax.all_to_all(packed, 'dp', 0, 0, tiled=True)  6.86 us
    ppermute x4, starting transfers between devices, swap_half(): outside[strip].append((piece, lax.ppermute(piece, 'dp', pairs)))  5.8 us
    all_to_all x1, starting transfers between devices, body(): own_f = lax.all_to_all(sent, 'dp', 0, 0, tiled=True)  5.76 us
    pallas_call x1, Pallas kernels, body(): pl.pallas_call(functools.partial(own_kernel, static), out_shape=(jax.Shap...  5.23 us
    pallas_call x4, Pallas kernels, finish(): pl.pallas_call(functools.partial(finish_kernel, len(received), at[0] * bl...  3.51 us
  transfers between devices with their start and end apart: 17, of which 9 were waited for; matrix products, arithmetic and copies ran while one was open for 0% of the time, Pallas kernels for 46%

profile of v21, /device:TPU:0, one launch (start us, length us, event | category | flops | bytes accessed | tf_op | source)
XLA Modules:
  0.0 82.4 jit_solution(8626427618356015080)
XLA Ops:
  0.6 0.5 collective-permute-start
  1.2 2.6 %shard_map.130 = (bf16[8,192,128]{2,1,0:T(8,128)(2,1)}, bf16[2,1280,128]{2,1,0:T(8,128)(2,1)}, bf16[2,1280,128]{2,1,0:T(8,128)(2,1)}) custom-call(f32[128,1280]{1,0:T(8,128)} %bitcast.20, f32[64,512]{1,0:T(8,128)} %bitcast.24, bf16[5120,512]{1,0:T(8,128)(2,1)} %sibling_block.1), custom_call_target="tpu_custom_call" | custom-call | tf_op jit(solution)/shard_map/pallas_call | solution.py:486
  3.7 6.9 %all-to-all-start = ((bf16[8,192,128]{2,1,0:T(8,128)(2,1)}), bf16[8,192,128]{2,1,0:T(8,128)(2,1)}, u32[]{:S(2)}, u32[]{:S(2)}) async-start(bf16[8,192,128]{2,1,0:T(8,128)(2,1)} %get-tuple-element.37), calls=%async_computation | async-start | bytes 786432 | tf_op jit(solution)/shard_map/all_to_all | solution.py:501
  10.6 1.5 %collective-permute-start.4 = (bf16[2,1280,128]{2,1,0:T(8,128)(2,1)}, bf16[2,1280,128]{2,1,0:T(8,128)(2,1)}, u32[]{:S(2)}, u32[]{:S(2)}) collective-permute-start(bf16[2,1280,128]{2,1,0:T(8,128)(2,1)} %get-tuple-element.56), channel_id=1, source_target_pairs={{0,2},{1,3},{2,0},{3,1},{4,6},{5,7},{6,4},{7,5},{8,10},{9,11},{10,... | collective-permute-start | bytes 1966088 | tf_op jit(solution)/shard_map/ppermute | solution.py:463
  12.1 0.0 copy-done.8
  12.1 0.1 collective-permute-start.1
  12.2 1.2 %collective-permute-done.1.sibling_gain = f32[1,1280]{1,0:T(1,128)S(1)} collective-permute-done((f32[1,1280]{1,0:T(1,128)S(1)}, f32[1,1280]{1,0:T(1,128)S(1)}, u32[]{:S(2)}, u32[]{:S(2)}) %collective-permute-start.1) | collective-permute-done | bytes 5152 | tf_op jit(solution)/shard_map/ppermute | solution.py:455
  13.3 0.0 collective-permute-done.sibling_in
  13.3 3.7 %shard_map.131 = (bf16[640,2560]{1,0:T(8,128)(2,1)S(1)}, f32[5,128]{1,0:T(8,128)S(1)}) custom-call(bf16[1280,1280]{1,0:T(8,128)(2,1)} %own_in.5, bf16[1280,1280]{1,0:T(8,128)(2,1)} %collective-permute-done.sibling_in, f32[1,1280]{1,0:T(1,128)S(1)} %broadcast_in_dim.3.own_gain, f32[1,1280]{1,0:T(1,128)S(1)} %collective-permute-done.1.sibling_gain), custom_call_target="tpu_custom_call" | custom-call | tf_op jit(solution)/shard_map/pallas_call | solution.py:532
  17.0 0.0 copy-done.4
  17.0 0.0 copy-done.5
  17.0 0.0 copy-start.7
  17.0 0.6 copy-done.7
  17.6 5.1 %shard_map.132 = (bf16[256,1280]{1,0:T(8,128)(2,1)}, bf16[256,1280]{1,0:T(8,128)(2,1)}, f32[10,128]{1,0:T(8,128)}) custom-call(bf16[1280,1280]{1,0:T(8,128)(2,1)} %own_in.5, bf16[1280,1280]{1,0:T(8,128)(2,1)} %collective-permute-done.sibling_in, f32[1,1280]{1,0:T(1,128)} %copy-done.4, f32[1,1280]{1,0:T(1,128)} %copy-done.5, f32[5,128]{1,0:T(8,128)} %copy-done.7), custom_call_target="tpu_custom_call" | custom-call | tf_op jit(solution)/shard_map/pallas_call | solution.py:532
  22.8 0.3 all-to-all-done.grad_in
  23.0 2.6 %shard_map.133 = (f32[3,128,160]{2,1,0:T(8,128)}, f32[3,8,512]{2,1,0:T(8,128)}, bf16[8,192,128]{2,1,0:T(8,128)(2,1)}) custom-call(bf16[8,192,128]{2,1,0:T(8,128)(2,1)} %all-to-all-done.grad_in, f32[128,1280]{1,0:T(8,128)} %bitcast.21, f32[128,1280]{1,0:T(8,128)} %bitcast.22, f32[128,1280]{1,0:T(8,128)} %bitcast.23, f32[64,512]{1,0:T(8,128)} %refs_3_.1, ...), custom_call_target="tpu_custom_call" | custom-call | tf_op jit(solution)/shard_map/pallas_call | solution.py:552
  25.6 5.8 %all-to-all-start.1 = ((bf16[8,192,128]{2,1,0:T(8,128)(2,1)}), bf16[8,192,128]{2,1,0:T(8,128)(2,1)}, u32[]{:S(2)}, u32[]{:S(2)}) async-start(bf16[8,192,128]{2,1,0:T(8,128)(2,1)} %get-tuple-element.43), calls=%async_computation.1 | async-start | bytes 786432 | tf_op jit(solution)/shard_map/all_to_all | solution.py:569
  31.4 0.0 collective-permute-done.4.in_ref
  31.4 0.6 collective-permute-start.5
  32.0 2.0 %shard_map.136 = (bf16[1280,128]{1,0:T(8,128)(2,1)}, bf16[1280,128]{1,0:T(8,128)(2,1)}) custom-call(bf16[2,1280,128]{2,1,0:T(8,128)(2,1)} %collective-permute-done.4.in_ref), custom_call_target="tpu_custom_call" | custom-call | tf_op jit(solution)/shard_map/pallas_call | solution.py:579
  34.0 2.0 %collective-permute-start.6 = (bf16[1280,128]{1,0:T(8,128)(2,1)}, bf16[1280,128]{1,0:T(8,128)(2,1)}, u32[]{:S(2)}, u32[]{:S(2)}) collective-permute-start(bf16[1280,128]{1,0:T(8,128)(2,1)} %get-tuple-element.59.refs_0_), channel_id=1, source_target_pairs={{0,4},{4,0},{8,12},{12,8},{16,20},{20,16},{24,28},{28,24},{1,5},{5... | collective-permute-start | bytes 983048 | tf_op jit(solution)/shard_map/ppermute | solution.py:588
  35.9 1.5 %collective-permute-start.7 = (bf16[1280,128]{1,0:T(8,128)(2,1)}, bf16[1280,128]{1,0:T(8,128)(2,1)}, u32[]{:S(2)}, u32[]{:S(2)}) collective-permute-start(bf16[1280,128]{1,0:T(8,128)(2,1)} %get-tuple-element.60.refs_2_), channel_id=1, source_target_pairs={{0,8},{4,12},{8,0},{12,4},{16,24},{20,28},{24,16},{28,20},{1,9},{5... | collective-permute-start | bytes 983048 | tf_op jit(solution)/shard_map/ppermute | solution.py:588
  37.4 3.3 %shard_map.134 = (bf16[384,1280]{1,0:T(8,128)(2,1)}, bf16[384,1280]{1,0:T(8,128)(2,1)}) custom-call(bf16[1280,1280]{1,0:T(8,128)(2,1)} %own_in.5, bf16[1280,1280]{1,0:T(8,128)(2,1)} %collective-permute-done.sibling_in, f32[1,1280]{1,0:T(1,128)} %copy-done.4, f32[1,1280]{1,0:T(1,128)} %copy-done.5), custom_call_target="tpu_custom_call" | custom-call | tf_op jit(solution)/shard_map/pallas_call | solution.py:532
  40.7 2.8 %all-to-all-done.1.factor_ref = bf16[8,192,128]{2,1,0:T(8,128)(2,1)} async-done(((bf16[8,192,128]{2,1,0:T(8,128)(2,1)}), bf16[8,192,128]{2,1,0:T(8,128)(2,1)}, u32[]{:S(2)}, u32[]{:S(2)}) %all-to-all-start.1) | async-done | bytes 393248 | tf_op jit(solution)/shard_map/all_to_all | solution.py:569
  43.5 0.0 copy-done.6
  43.5 1.1 %shard_map.135 = (bf16[9,32,128]{2,1,0:T(8,128)(2,1)S(1)}, bf16[4,192,128]{2,1,0:T(8,128)(2,1)S(1)}, bf16[4,192,128]{2,1,0:T(8,128)(2,1)S(1)}) custom-call(bf16[8,192,128]{2,1,0:T(8,128)(2,1)} %all-to-all-done.1.factor_ref, f32[10,128]{1,0:T(8,128)S(1)} %copy-done.6), custom_call_target="tpu_custom_call" | custom-call | tf_op jit(solution)/shard_map/pallas_call | solution.py:596
  44.6 0.1 collective-permute-start.2
  44.7 0.5 collective-permute-start.3
  45.2 0.8 collective-permute-done.6.refs_1_
  45.9 0.9 %collective-permute-start.8 = (bf16[9,32,128]{2,1,0:T(8,128)(2,1)S(1)}, bf16[9,32,128]{2,1,0:T(8,128)(2,1)S(1)}, u32[]{:S(2)}, u32[]{:S(2)}) collective-permute-start(bf16[9,32,128]{2,1,0:T(8,128)(2,1)S(1)} %get-tuple-element.61), channel_id=1, source_target_pairs={{0,2},{1,3},{2,0},{3,1},{4,6},{5,7},{6,4},{7,5},{8,10},{9,11},{10,... | collective-permute-start | bytes 221192 | tf_op jit(solution)/shard_map/ppermute | solution.py:463
  46.9 1.1 %collective-permute-done.7.refs_3_ = bf16[1280,128]{1,0:T(8,128)(2,1)} collective-permute-done((bf16[1280,128]{1,0:T(8,128)(2,1)}, bf16[1280,128]{1,0:T(8,128)(2,1)}, u32[]{:S(2)}, u32[]{:S(2)}) %collective-permute-start.7) | collective-permute-done | bytes 327712 | tf_op jit(solution)/shard_map/ppermute | solution.py:588
  47.9 1.6 %shard_map.137.blocks = bf16[2560,256]{1,0:T(8,128)(2,1)S(1)} custom-call(bf16[1280,128]{1,0:T(8,128)(2,1)} %get-tuple-element.59.refs_0_, bf16[1280,128]{1,0:T(8,128)(2,1)} %collective-permute-done.6.refs_1_, bf16[1280,128]{1,0:T(8,128)(2,1)} %get-tuple-element.60.refs_2_, bf16[1280,128]{1,0:T(8,128)(2,1)} %collective-permute-done.7.refs_3_), custom_call_target="tpu_custom_call" | custom-call | tf_op jit(solution)/shard_map/pallas_call | solution.py:631
  49.6 0.7 collective-permute-done.8.b_ref.refs_0_
  50.3 0.0 collective-permute-done.2.refs_2_
  50.3 0.0 collective-permute-done.3.refs_3_
  50.3 0.0 copy-start.1
  50.3 0.0 copy-start.2
  50.3 1.7 %shard_map.138 = (bf16[2560,256]{1,0:T(8,128)(2,1)S(1)}, bf16[640,256]{1,0:T(8,128)(2,1)S(1)}) custom-call(bf16[2560,256]{1,0:T(8,128)(2,1)S(1)} %shard_map.137.blocks, bf16[9,32,128]{2,1,0:T(8,128)(2,1)S(1)} %collective-permute-done.8.b_ref.refs_0_, bf16[640,2560]{1,0:T(8,128)(2,1)S(1)} %get-tuple-element.50.x.refs_4_, ...), custom_call_target="tpu_custom_call" | custom-call | tf_op jit(solution)/shard_map/pallas_call | solution.py:638
  52.0 1.0 %collective-permute-start.11 = (bf16[640,256]{1,0:T(8,128)(2,1)S(1)}, bf16[640,256]{1,0:T(8,128)(2,1)S(1)}, u32[]{:S(2)}, u32[]{:S(2)}) collective-permute-start(bf16[640,256]{1,0:T(8,128)(2,1)S(1)} %get-tuple-element.62), channel_id=1, source_target_pairs={{0,2},{1,3},{2,0},{3,1},{4,6},{5,7},{6,4},{7,5},{8,10},{9,11},{10,... | collective-permute-start | bytes 983048 | tf_op jit(solution)/shard_map/ppermute | solution.py:463
  53.0 0.0 collective-permute-done.5.in_ref
  53.0 1.1 %shard_map.139 = (bf16[1280,128]{1,0:T(8,128)(2,1)S(1)}, bf16[1280,128]{1,0:T(8,128)(2,1)S(1)}) custom-call(bf16[2,1280,128]{2,1,0:T(8,128)(2,1)} %collective-permute-done.5.in_ref), custom_call_target="tpu_custom_call" | custom-call | tf_op jit(solution)/shard_map/pallas_call | solution.py:579
  54.2 0.9 %collective-permute-start.9 = (bf16[1280,128]{1,0:T(8,128)(2,1)S(1)}, bf16[1280,128]{1,0:T(8,128)(2,1)S(1)}, u32[]{:S(2)}, u32[]{:S(2)}) collective-permute-start(bf16[1280,128]{1,0:T(8,128)(2,1)S(1)} %get-tuple-element.64.refs_0_), channel_id=1, source_target_pairs={{0,4},{4,0},{8,12},{12,8},{16,20},{20,16},{24,28},{28,24},{1,5},{5... | collective-permute-start | bytes 983048 | tf_op jit(solution)/shard_map/ppermute | solution.py:588
  55.1 1.5 %collective-permute-start.10 = (bf16[1280,128]{1,0:T(8,128)(2,1)S(1)}, bf16[1280,128]{1,0:T(8,128)(2,1)S(1)}, u32[]{:S(2)}, u32[]{:S(2)}) collective-permute-start(bf16[1280,128]{1,0:T(8,128)(2,1)S(1)} %get-tuple-element.65.refs_2_), channel_id=1, source_target_pairs={{0,8},{4,12},{8,0},{12,4},{16,24},{20,28},{24,16},{28,20},{1,9},{5... | collective-permute-start | bytes 983048 | tf_op jit(solution)/shard_map/ppermute | solution.py:588
  56.6 0.0 copy-done.1
  56.6 1.6 %shard_map.143 = bf16[640,256]{1,0:T(8,128)(2,1)S(1)} custom-call(bf16[256,1280]{1,0:T(8,128)(2,1)S(1)} %copy-done.2, bf16[256,1280]{1,0:T(8,128)(2,1)S(1)} %copy-done.3, bf16[384,1280]{1,0:T(8,128)(2,1)S(1)} %copy-done, bf16[384,1280]{1,0:T(8,128)(2,1)S(1)} %copy-done.1, bf16[2560,256]{1,0:T(8,128)(2,1)S(1)} %get-tuple-element.67.refs_4_), custom_call_target="tpu_custom_call" | custom-call | tf_op jit(solution)/shard_map/pallas_call | solution.py:646
  58.1 1.4 %collective-permute-start.12 = (bf16[640,256]{1,0:T(8,128)(2,1)S(1)}, bf16[640,256]{1,0:T(8,128)(2,1)S(1)}, u32[]{:S(2)}, u32[]{:S(2)}) collective-permute-start(bf16[640,256]{1,0:T(8,128)(2,1)S(1)} %shard_map.143), channel_id=1, source_target_pairs={{0,2},{1,3},{2,0},{3,1},{4,6},{5,7},{6,4},{7,5},{8,10},{9,11},{10,... | collective-permute-start | bytes 983048 | tf_op jit(solution)/shard_map/ppermute | solution.py:463
  59.6 2.3 %collective-permute-done.11.refs_4_.refs_0_ = bf16[640,256]{1,0:T(8,128)(2,1)S(1)} collective-permute-done((bf16[640,256]{1,0:T(8,128)(2,1)S(1)}, bf16[640,256]{1,0:T(8,128)(2,1)S(1)}, u32[]{:S(2)}, u32[]{:S(2)}) %collective-permute-start.11) | collective-permute-done | bytes 327712 | tf_op jit(solution)/shard_map/ppermute | solution.py:463
  61.9 0.0 collective-permute-done.9.refs_1_
  61.9 1.4 %collective-permute-done.10.refs_3_ = bf16[1280,128]{1,0:T(8,128)(2,1)S(1)} collective-permute-done((bf16[1280,128]{1,0:T(8,128)(2,1)S(1)}, bf16[1280,128]{1,0:T(8,128)(2,1)S(1)}, u32[]{:S(2)}, u32[]{:S(2)}) %collective-permute-start.10) | collective-permute-done | bytes 327712 | tf_op jit(solution)/shard_map/ppermute | solution.py:588
  63.3 0.3 shard_map.140.blocks
  63.6 0.0 slice-start.1
  63.6 1.7 %shard_map.141 = (bf16[2560,256]{1,0:T(8,128)(2,1)S(1)}, bf16[640,256]{1,0:T(8,128)(2,1)S(1)}) custom-call(bf16[2560,256]{1,0:T(8,128)(2,1)S(1)} %shard_map.140.blocks, bf16[9,32,128]{2,1,0:T(8,128)(2,1)S(1)} %collective-permute-done.8.b_ref.refs_0_, bf16[640,2560]{1,0:T(8,128)(2,1)S(1)} %get-tuple-element.50.x.refs_4_, ...), custom_call_target="tpu_custom_call" | custom-call | tf_op jit(solution)/shard_map/pallas_call | solution.py:638
  65.3 1.8 %collective-permute-start.14 = (bf16[640,256]{1,0:T(8,128)(2,1)S(1)}, bf16[640,256]{1,0:T(8,128)(2,1)S(1)}, u32[]{:S(2)}, u32[]{:S(2)}) collective-permute-start(bf16[640,256]{1,0:T(8,128)(2,1)S(1)} %get-tuple-element.69), channel_id=1, source_target_pairs={{0,2},{1,3},{2,0},{3,1},{4,6},{5,7},{6,4},{7,5},{8,10},{9,11},{10,... | collective-permute-start | bytes 983048 | tf_op jit(solution)/shard_map/ppermute | solution.py:463
  67.1 1.5 %shard_map.142.refs_9_ = bf16[640,256]{1,0:T(8,128)(2,1)S(1)} custom-call(bf16[256,1280]{1,0:T(8,128)(2,1)S(1)} %copy-done.2, bf16[256,1280]{1,0:T(8,128)(2,1)S(1)} %copy-done.3, bf16[384,1280]{1,0:T(8,128)(2,1)S(1)} %copy-done, bf16[384,1280]{1,0:T(8,128)(2,1)S(1)} %copy-done.1, bf16[2560,256]{1,0:T(8,128)(2,1)S(1)} %get-tuple-element.66.refs_4_), custom_call_target="tpu_custom_call" | custom-call | tf_op jit(solution)/shard_map/pallas_call | solution.py:646
  68.7 0.4 collective-permute-start.13
  69.0 0.2 shard_map.145.inv
  69.3 0.0 collective-permute-done.12.refs_10_.refs_0_
  69.3 5.2 %shard_map.144 = (f32[1280,256]{1,0:T(8,128)S(1)}, f32[1280,256]{1,0:T(8,128)S(1)}) custom-call(bf16[5120,512]{1,0:T(8,128)(2,1)S(1)} %bitcast.19, bf16[5120,512]{1,0:T(8,128)(2,1)S(1)} %bitcast.19, bf16[4,192,128]{2,1,0:T(8,128)(2,1)S(1)} %get-tuple-element.48.refs_0_, bf16[4,192,128]{2,1,0:T(8,128)(2,1)S(1)} %get-tuple-element.49.refs_1_, ...), custom_call_target="tpu_custom_call" | custom-call | flops 3355443200 | bytes 6553600 | tf_op jit(solution)/shard_map/pallas_call | solution.py:661
  74.6 0.9 %shard_map.146.refs_1_ = bf16[1280,512]{1,0:T(8,128)(2,1)} custom-call(f32[1280,256]{1,0:T(8,128)S(1)} %get-tuple-element.70.own, f32[1280,128]{1,0:T(8,128)S(1)} %shard_map.145.inv, bf16[640,256]{1,0:T(8,128)(2,1)S(1)} %collective-permute-done.11.refs_4_.refs_0_), custom_call_target="tpu_custom_call" | custom-call | tf_op jit(solution)/shard_map/pallas_call | solution.py:414
  75.4 0.9 %shard_map.147.refs_1_ = bf16[1280,512]{1,0:T(8,128)(2,1)} custom-call(f32[1280,256]{1,0:T(8,128)S(1)} %get-tuple-element.70.own, f32[1280,128]{1,0:T(8,128)S(1)} %shard_map.145.inv, bf16[640,256]{1,0:T(8,128)(2,1)S(1)} %collective-permute-done.12.refs_10_.refs_0_, bf16[1280,512]{1,0:T(8,128)(2,1)} %shard_map.146.refs_1_), custom_call_target="tpu_custom_call", output_to_operand_aliasing={{}: (3, {})} | custom-call | tf_op jit(solution)/shard_map/pallas_call | solution.py:414
  76.3 0.0 collective-permute-done.14.refs_0_
  76.3 0.9 %shard_map.148.refs_1_ = bf16[1280,512]{1,0:T(8,128)(2,1)} custom-call(f32[1280,256]{1,0:T(8,128)S(1)} %get-tuple-element.68.own, f32[1280,128]{1,0:T(8,128)S(1)} %shard_map.145.inv, bf16[640,256]{1,0:T(8,128)(2,1)S(1)} %collective-permute-done.14.refs_0_, bf16[1280,512]{1,0:T(8,128)(2,1)} %shard_map.147.refs_1_), custom_call_target="tpu_custom_call", output_to_operand_aliasing={{}: (3, {})} | custom-call | tf_op jit(solution)/shard_map/pallas_call | solution.py:414
  77.2 4.3 %collective-permute-done.13.refs_0_ = bf16[640,256]{1,0:T(8,128)(2,1)S(1)} collective-permute-done((bf16[640,256]{1,0:T(8,128)(2,1)S(1)}, bf16[640,256]{1,0:T(8,128)(2,1)S(1)}, u32[]{:S(2)}, u32[]{:S(2)}) %collective-permute-start.13) | collective-permute-done | bytes 327712 | tf_op jit(solution)/shard_map/ppermute | solution.py:463
  81.5 0.9 %shard_map.149 = bf16[1280,512]{1,0:T(8,128)(2,1)} custom-call(f32[1280,256]{1,0:T(8,128)S(1)} %get-tuple-element.68.own, f32[1280,128]{1,0:T(8,128)S(1)} %shard_map.145.inv, bf16[640,256]{1,0:T(8,128)(2,1)S(1)} %collective-permute-done.13.refs_0_, bf16[1280,512]{1,0:T(8,128)(2,1)} %shard_map.148.refs_1_), custom_call_target="tpu_custom_call", output_to_operand_aliasing={{}: (3, {})} | custom-call | tf_op jit(solution)/shard_map/pallas_call | solution.py:414
  (14 shorter events, 0.0 us)
Async XLA Ops:
  0.6 12.7 %collective-permute-start = (bf16[1280,1280]{1,0:T(8,128)(2,1)}, bf16[1280,1280]{1,0:T(8,128)(2,1)}, u32[]{:S(2)}, u32[]{:S(2)}) collective-permute-start(bf16[1280,1280]{1,0:T(8,128)(2,1)} %own_in.5), channel_id=1, source_target_pairs={{0,1},{1,0},{2,3},{3,2},{4,5},{5,4},{6,7},{7,6},{8,9},{9,8},{10,11... | collective-permute-start | bytes 9830408 | tf_op jit(solution)/shard_map/ppermute | solution.py:455
  1.1 10.9 %copy-start.8 = (f32[1280]{0:T(1024)S(1)}, f32[1280]{0:T(1024)}, u32[]{:S(2)}) copy-start(f32[1280]{0:T(1024)} %param.12) | copy-start | bytes 15364
  3.7 19.3 %all-to-all-start = ((bf16[8,192,128]{2,1,0:T(8,128)(2,1)}), bf16[8,192,128]{2,1,0:T(8,128)(2,1)}, u32[]{:S(2)}, u32[]{:S(2)}) async-start(bf16[8,192,128]{2,1,0:T(8,128)(2,1)} %get-tuple-element.37), calls=%async_computation | async-start | bytes 786432 | tf_op jit(solution)/shard_map/all_to_all | solution.py:501
  10.6 20.8 %collective-permute-start.4 = (bf16[2,1280,128]{2,1,0:T(8,128)(2,1)}, bf16[2,1280,128]{2,1,0:T(8,128)(2,1)}, u32[]{:S(2)}, u32[]{:S(2)}) collective-permute-start(bf16[2,1280,128]{2,1,0:T(8,128)(2,1)} %get-tuple-element.56), channel_id=1, source_target_pairs={{0,2},{1,3},{2,0},{3,1},{4,6},{5,7},{6,4},{7,5},{8,10},{9,11},{10,... | collective-permute-start | bytes 1966088 | tf_op jit(solution)/shard_map/ppermute | solution.py:463
  12.1 4.9 %copy-start.4 = (f32[1,1280]{1,0:T(1,128)}, f32[1,1280]{1,0:T(1,128)S(1)}, u32[]{:S(2)}) copy-start(f32[1,1280]{1,0:T(1,128)S(1)} %broadcast_in_dim.3.own_gain) | copy-start | bytes 15364
  12.1 1.2 %collective-permute-start.1 = (f32[1,1280]{1,0:T(1,128)S(1)}, f32[1,1280]{1,0:T(1,128)S(1)}, u32[]{:S(2)}, u32[]{:S(2)}) collective-permute-start(f32[1,1280]{1,0:T(1,128)S(1)} %broadcast_in_dim.3.own_gain), channel_id=1, source_target_pairs={{0,1},{1,0},{2,3},{3,2},{4,5},{5,4},{6,7},{7,6},{8,9},{9,8},{10,11... | collective-permute-start | bytes 15368 | tf_op jit(solution)/shard_map/ppermute | solution.py:455
  13.3 3.7 %copy-start.5 = (f32[1,1280]{1,0:T(1,128)}, f32[1,1280]{1,0:T(1,128)S(1)}, u32[]{:S(2)}) copy-start(f32[1,1280]{1,0:T(1,128)S(1)} %collective-permute-done.1.sibling_gain) | copy-start | bytes 15364
  17.0 0.6 copy-start.7
  25.6 17.9 %all-to-all-start.1 = ((bf16[8,192,128]{2,1,0:T(8,128)(2,1)}), bf16[8,192,128]{2,1,0:T(8,128)(2,1)}, u32[]{:S(2)}, u32[]{:S(2)}) async-start(bf16[8,192,128]{2,1,0:T(8,128)(2,1)} %get-tuple-element.43), calls=%async_computation.1 | async-start | bytes 786432 | tf_op jit(solution)/shard_map/all_to_all | solution.py:569
  31.4 21.7 %collective-permute-start.5 = (bf16[2,1280,128]{2,1,0:T(8,128)(2,1)}, bf16[2,1280,128]{2,1,0:T(8,128)(2,1)}, u32[]{:S(2)}, u32[]{:S(2)}) collective-permute-start(bf16[2,1280,128]{2,1,0:T(8,128)(2,1)} %get-tuple-element.57), channel_id=1, source_target_pairs={{0,2},{1,3},{2,0},{3,1},{4,6},{5,7},{6,4},{7,5},{8,10},{9,11},{10,... | collective-permute-start | bytes 1966088 | tf_op jit(solution)/shard_map/ppermute | solution.py:463
  34.0 12.0 %collective-permute-start.6 = (bf16[1280,128]{1,0:T(8,128)(2,1)}, bf16[1280,128]{1,0:T(8,128)(2,1)}, u32[]{:S(2)}, u32[]{:S(2)}) collective-permute-start(bf16[1280,128]{1,0:T(8,128)(2,1)} %get-tuple-element.59.refs_0_), channel_id=1, source_target_pairs={{0,4},{4,0},{8,12},{12,8},{16,20},{20,16},{24,28},{28,24},{1,5},{5... | collective-permute-start | bytes 983048 | tf_op jit(solution)/shard_map/ppermute | solution.py:588
  35.9 7.6 %copy-start.6 = (f32[10,128]{1,0:T(8,128)S(1)}, f32[10,128]{1,0:T(8,128)}, u32[]{:S(2)}) copy-start(f32[10,128]{1,0:T(8,128)} %get-tuple-element.47.sums_ref) | copy-start | bytes 15364
  35.9 12.0 %collective-permute-start.7 = (bf16[1280,128]{1,0:T(8,128)(2,1)}, bf16[1280,128]{1,0:T(8,128)(2,1)}, u32[]{:S(2)}, u32[]{:S(2)}) collective-permute-start(bf16[1280,128]{1,0:T(8,128)(2,1)} %get-tuple-element.60.refs_2_), channel_id=1, source_target_pairs={{0,8},{4,12},{8,0},{12,4},{16,24},{20,28},{24,16},{28,20},{1,9},{5... | collective-permute-start | bytes 983048 | tf_op jit(solution)/shard_map/ppermute | solution.py:588
  44.6 5.7 %collective-permute-start.2 = (bf16[4,192,128]{2,1,0:T(8,128)(2,1)S(1)}, bf16[4,192,128]{2,1,0:T(8,128)(2,1)S(1)}, u32[]{:S(2)}, u32[]{:S(2)}) collective-permute-start(bf16[4,192,128]{2,1,0:T(8,128)(2,1)S(1)} %get-tuple-element.48.refs_0_), channel_id=1, source_target_pairs={{0,1},{1,0},{2,3},{3,2},{4,5},{5,4},{6,7},{7,6},{8,9},{9,8},{10,11... | collective-permute-start | bytes 589832 | tf_op jit(solution)/shard_map/ppermute | solution.py:455
  44.7 5.6 %collective-permute-start.3 = (bf16[4,192,128]{2,1,0:T(8,128)(2,1)S(1)}, bf16[4,192,128]{2,1,0:T(8,128)(2,1)S(1)}, u32[]{:S(2)}, u32[]{:S(2)}) collective-permute-start(bf16[4,192,128]{2,1,0:T(8,128)(2,1)S(1)} %get-tuple-element.49.refs_1_), channel_id=1, source_target_pairs={{0,1},{1,0},{2,3},{3,2},{4,5},{5,4},{6,7},{7,6},{8,9},{9,8},{10,11... | collective-permute-start | bytes 589832 | tf_op jit(solution)/shard_map/ppermute | solution.py:455
  45.9 4.4 %collective-permute-start.8 = (bf16[9,32,128]{2,1,0:T(8,128)(2,1)S(1)}, bf16[9,32,128]{2,1,0:T(8,128)(2,1)S(1)}, u32[]{:S(2)}, u32[]{:S(2)}) collective-permute-start(bf16[9,32,128]{2,1,0:T(8,128)(2,1)S(1)} %get-tuple-element.61), channel_id=1, source_target_pairs={{0,2},{1,3},{2,0},{3,1},{4,6},{5,7},{6,4},{7,5},{8,10},{9,11},{10,... | collective-permute-start | bytes 221192 | tf_op jit(solution)/shard_map/ppermute | solution.py:463
  50.3 6.3 %copy-start = (bf16[384,1280]{1,0:T(8,128)(2,1)S(1)}, bf16[384,1280]{1,0:T(8,128)(2,1)}, u32[]{:S(2)}) copy-start(bf16[384,1280]{1,0:T(8,128)(2,1)} %get-tuple-element.53.refs_2_.refs_7_) | copy-start | bytes 2949124
  50.3 6.3 %copy-start.1 = (bf16[384,1280]{1,0:T(8,128)(2,1)S(1)}, bf16[384,1280]{1,0:T(8,128)(2,1)}, u32[]{:S(2)}) copy-start(bf16[384,1280]{1,0:T(8,128)(2,1)} %get-tuple-element.54.refs_3_.refs_8_) | copy-start | bytes 2949124
  50.3 6.2 %copy-start.2 = (bf16[256,1280]{1,0:T(8,128)(2,1)S(1)}, bf16[256,1280]{1,0:T(8,128)(2,1)}, u32[]{:S(2)}) copy-start(bf16[256,1280]{1,0:T(8,128)(2,1)} %get-tuple-element.51.refs_0_.refs_5_) | copy-start | bytes 1966084
  50.3 6.2 %copy-start.3 = (bf16[256,1280]{1,0:T(8,128)(2,1)S(1)}, bf16[256,1280]{1,0:T(8,128)(2,1)}, u32[]{:S(2)}) copy-start(bf16[256,1280]{1,0:T(8,128)(2,1)} %get-tuple-element.52.refs_1_.refs_6_) | copy-start | bytes 1966084
  52.0 9.8 %collective-permute-start.11 = (bf16[640,256]{1,0:T(8,128)(2,1)S(1)}, bf16[640,256]{1,0:T(8,128)(2,1)S(1)}, u32[]{:S(2)}, u32[]{:S(2)}) collective-permute-start(bf16[640,256]{1,0:T(8,128)(2,1)S(1)} %get-tuple-element.62), channel_id=1, source_target_pairs={{0,2},{1,3},{2,0},{3,1},{4,6},{5,7},{6,4},{7,5},{8,10},{9,11},{10,... | collective-permute-start | bytes 983048 | tf_op jit(solution)/shard_map/ppermute | solution.py:463
  54.2 7.7 %collective-permute-start.9 = (bf16[1280,128]{1,0:T(8,128)(2,1)S(1)}, bf16[1280,128]{1,0:T(8,128)(2,1)S(1)}, u32[]{:S(2)}, u32[]{:S(2)}) collective-permute-start(bf16[1280,128]{1,0:T(8,128)(2,1)S(1)} %get-tuple-element.64.refs_0_), channel_id=1, source_target_pairs={{0,4},{4,0},{8,12},{12,8},{16,20},{20,16},{24,28},{28,24},{1,5},{5... | collective-permute-start | bytes 983048 | tf_op jit(solution)/shard_map/ppermute | solution.py:588
  55.1 8.2 %collective-permute-start.10 = (bf16[1280,128]{1,0:T(8,128)(2,1)S(1)}, bf16[1280,128]{1,0:T(8,128)(2,1)S(1)}, u32[]{:S(2)}, u32[]{:S(2)}) collective-permute-start(bf16[1280,128]{1,0:T(8,128)(2,1)S(1)} %get-tuple-element.65.refs_2_), channel_id=1, source_target_pairs={{0,8},{4,12},{8,0},{12,4},{16,24},{20,28},{24,16},{28,20},{1,9},{5... | collective-permute-start | bytes 983048 | tf_op jit(solution)/shard_map/ppermute | solution.py:588
  58.1 11.2 %collective-permute-start.12 = (bf16[640,256]{1,0:T(8,128)(2,1)S(1)}, bf16[640,256]{1,0:T(8,128)(2,1)S(1)}, u32[]{:S(2)}, u32[]{:S(2)}) collective-permute-start(bf16[640,256]{1,0:T(8,128)(2,1)S(1)} %shard_map.143), channel_id=1, source_target_pairs={{0,2},{1,3},{2,0},{3,1},{4,6},{5,7},{6,4},{7,5},{8,10},{9,11},{10,... | collective-permute-start | bytes 983048 | tf_op jit(solution)/shard_map/ppermute | solution.py:463
  63.2 6.0 %slice-start = ((s8[5242880]{0:T(1024)(128)(4,1)}), s8[4194304]{0:T(1024)(128)(4,1)S(1)}, s32[]{:S(2)}) async-start(s8[5242880]{0:T(1024)(128)(4,1)} %bitcast.18), calls=%async_computation.2 | async-start | bytes 8388608
  63.6 5.7 %slice-start.1 = ((s8[5242880]{0:T(1024)(128)(4,1)}), s8[1048576]{0:T(1024)(128)(4,1)S(1)}, s32[]{:S(2)}) async-start(s8[5242880]{0:T(1024)(128)(4,1)} %bitcast.18), calls=%async_computation.3 | async-start | bytes 2097152
  65.3 11.0 %collective-permute-start.14 = (bf16[640,256]{1,0:T(8,128)(2,1)S(1)}, bf16[640,256]{1,0:T(8,128)(2,1)S(1)}, u32[]{:S(2)}, u32[]{:S(2)}) collective-permute-start(bf16[640,256]{1,0:T(8,128)(2,1)S(1)} %get-tuple-element.69), channel_id=1, source_target_pairs={{0,2},{1,3},{2,0},{3,1},{4,6},{5,7},{6,4},{7,5},{8,10},{9,11},{10,... | collective-permute-start | bytes 983048 | tf_op jit(solution)/shard_map/ppermute | solution.py:463
  68.7 12.9 %collective-permute-start.13 = (bf16[640,256]{1,0:T(8,128)(2,1)S(1)}, bf16[640,256]{1,0:T(8,128)(2,1)S(1)}, u32[]{:S(2)}, u32[]{:S(2)}) collective-permute-start(bf16[640,256]{1,0:T(8,128)(2,1)S(1)} %shard_map.142.refs_9_), channel_id=1, source_target_pairs={{0,2},{1,3},{2,0},{3,1},{4,6},{5,7},{6,4},{7,5},{8,10},{9,11},{10,... | collective-permute-start | bytes 983048 | tf_op jit(solution)/shard_map/ppermute | solution.py:463

commit v22 on v21

--- a/solution.py
+++ b/solution.py
@@ -545,9 +545,9 @@
         return (list(outs[:-1]), outs[-1]) if summed else (list(outs), None)
 
     cut = some // 2 // LANES * LANES
-    x0, squares = prepared(0, some, some, [], True, PREPARE_VMEM_BYTES)
-    x1, squares = prepared(some, cut, some, [squares], False, LARGE_VMEM_BYTES)
-    exchanged, squares = lax.optimization_barrier((exchanged, squares))
+    x0, squares = prepared(0, some, tokens, [], True, PREPARE_VMEM_BYTES)
+    x1, _ = prepared(some, cut, 0, [squares], False, LARGE_VMEM_BYTES)
+    exchanged, squares, x1 = lax.optimization_barrier((exchanged, squares, x1))
     last, _ = prepared(some + cut, some - cut, 0, [], False, LARGE_VMEM_BYTES)
     a_next, b_next, sent = pl.pallas_call(
         adam_kernel,

time: 83 us -> 83.5 us (level)
  transfers between devices with their start and end apart: 17 -> 17, of which waited for: 9 -> 8; matrix products, arithmetic and copies ran while one was open for 0% -> 0% of each run, Pallas kernels for 46% -> 46%
where the time goes in v22:
time: 83.5 us; the launch traced here: 82.8 us
  Pallas kernels  39.3 us (47%)
  starting transfers between devices  27.4 us (33%)
  waiting for transfers between devices  14.6 us (17%)
  between operations  0.89 us (1%)
    pallas_call x3, Pallas kernels, prepared(): pl.pallas_call(functools.partial(prepare_kernel, first, summed), out_shap...  12.5 us
    ppermute x7, starting transfers between devices, to_chip(): return lax.ppermute(value, 'tensor', pairs)  7.59 us
    ppermute x7, waiting for transfers between devices, to_chip(): return lax.ppermute(value, 'tensor', pairs)  7.39 us
    all_to_all x1, starting transfers between devices, body(): exchanged = lax.all_to_all(packed, 'dp', 0, 0, tiled=True)  6.86 us
    all_to_all x1, starting transfers between devices, body(): own_f = lax.all_to_all(sent, 'dp', 0, 0, tiled=True)  6.01 us
    ppermute x4, starting transfers between devices, swap_half(): outside[strip].append((piece, lax.ppermute(piece, 'dp', pairs)))  5.8 us
    pallas_call x1, Pallas kernels, body(): pl.pallas_call(functools.partial(own_kernel, static), out_shape=(jax.Shap...  5.23 us
    pallas_call x4, Pallas kernels, finish(): pl.pallas_call(functools.partial(finish_kernel, len(received), at[0] * bl...  3.51 us
  transfers between devices with their start and end apart: 17, of which 8 were waited for; matrix products, arithmetic and copies ran while one was open for 0% of the time, Pallas kernels for 46%

profile of v22, /device:TPU:0, one launch (start us, length us, event | category | flops | bytes accessed | tf_op | source)
XLA Modules:
  0.0 82.8 jit_solution(8337919222152124704)
XLA Ops:
  0.6 0.5 collective-permute-start
  1.2 2.6 %shard_map.130 = (bf16[8,192,128]{2,1,0:T(8,128)(2,1)}, bf16[2,1280,128]{2,1,0:T(8,128)(2,1)}, bf16[2,1280,128]{2,1,0:T(8,128)(2,1)}) custom-call(f32[128,1280]{1,0:T(8,128)} %bitcast.20, f32[64,512]{1,0:T(8,128)} %bitcast.24, bf16[5120,512]{1,0:T(8,128)(2,1)} %sibling_block.1), custom_call_target="tpu_custom_call" | custom-call | tf_op jit(solution)/shard_map/pallas_call | solution.py:486
  3.7 6.9 %all-to-all-start = ((bf16[8,192,128]{2,1,0:T(8,128)(2,1)}), bf16[8,192,128]{2,1,0:T(8,128)(2,1)}, u32[]{:S(2)}, u32[]{:S(2)}) async-start(bf16[8,192,128]{2,1,0:T(8,128)(2,1)} %get-tuple-element.38), calls=%async_computation | async-start | bytes 786432 | tf_op jit(solution)/shard_map/all_to_all | solution.py:501
  10.6 1.5 %collective-permute-start.4 = (bf16[2,1280,128]{2,1,0:T(8,128)(2,1)}, bf16[2,1280,128]{2,1,0:T(8,128)(2,1)}, u32[]{:S(2)}, u32[]{:S(2)}) collective-permute-start(bf16[2,1280,128]{2,1,0:T(8,128)(2,1)} %get-tuple-element.58), channel_id=1, source_target_pairs={{0,2},{1,3},{2,0},{3,1},{4,6},{5,7},{6,4},{7,5},{8,10},{9,11},{10,... | collective-permute-start | bytes 1966088 | tf_op jit(solution)/shard_map/ppermute | solution.py:463
  12.1 0.0 copy-done.8
  12.1 0.1 collective-permute-start.1
  12.2 1.2 %collective-permute-done.1.sibling_gain = f32[1,1280]{1,0:T(1,128)S(1)} collective-permute-done((f32[1,1280]{1,0:T(1,128)S(1)}, f32[1,1280]{1,0:T(1,128)S(1)}, u32[]{:S(2)}, u32[]{:S(2)}) %collective-permute-start.1) | collective-permute-done | bytes 5152 | tf_op jit(solution)/shard_map/ppermute | solution.py:455
  13.3 0.0 collective-permute-done.sibling_in
  13.3 6.2 %shard_map.131 = (bf16[640,2560]{1,0:T(8,128)(2,1)S(1)}, f32[10,128]{1,0:T(8,128)S(1)}) custom-call(bf16[1280,1280]{1,0:T(8,128)(2,1)} %own_in.5, bf16[1280,1280]{1,0:T(8,128)(2,1)} %collective-permute-done.sibling_in, f32[1,1280]{1,0:T(1,128)S(1)} %broadcast_in_dim.3.own_gain, f32[1,1280]{1,0:T(1,128)S(1)} %collective-permute-done.1.sibling_gain), custom_call_target="tpu_custom_call" | custom-call | tf_op jit(solution)/shard_map/pallas_call | solution.py:532
  19.5 0.0 copy-done.4
  19.5 0.0 copy-done.7
  19.5 0.0 copy-start.5
  19.5 0.6 copy-done.5
  20.1 3.1 %shard_map.132 = (bf16[256,1280]{1,0:T(8,128)(2,1)}, bf16[256,1280]{1,0:T(8,128)(2,1)}) custom-call(bf16[1280,1280]{1,0:T(8,128)(2,1)} %own_in.5, bf16[1280,1280]{1,0:T(8,128)(2,1)} %collective-permute-done.sibling_in, f32[1,1280]{1,0:T(1,128)} %copy-done.4, f32[1,1280]{1,0:T(1,128)} %copy-done.7, f32[10,128]{1,0:T(8,128)} %copy-done.5), custom_call_target="tpu_custom_call" | custom-call | tf_op jit(solution)/shard_map/pallas_call | solution.py:532
  23.2 0.0 all-to-all-done.grad_in
  23.2 2.6 %shard_map.133 = (f32[3,128,160]{2,1,0:T(8,128)}, f32[3,8,512]{2,1,0:T(8,128)}, bf16[8,192,128]{2,1,0:T(8,128)(2,1)}) custom-call(bf16[8,192,128]{2,1,0:T(8,128)(2,1)} %all-to-all-done.grad_in, f32[128,1280]{1,0:T(8,128)} %bitcast.21, f32[128,1280]{1,0:T(8,128)} %bitcast.22, f32[128,1280]{1,0:T(8,128)} %bitcast.23, f32[64,512]{1,0:T(8,128)} %refs_3_.1, ...), custom_call_target="tpu_custom_call" | custom-call | tf_op jit(solution)/shard_map/pallas_call | solution.py:552
  25.8 6.0 %all-to-all-start.1 = ((bf16[8,192,128]{2,1,0:T(8,128)(2,1)}), bf16[8,192,128]{2,1,0:T(8,128)(2,1)}, u32[]{:S(2)}, u32[]{:S(2)}) async-start(bf16[8,192,128]{2,1,0:T(8,128)(2,1)} %get-tuple-element.45), calls=%async_computation.1 | async-start | bytes 786432 | tf_op jit(solution)/shard_map/all_to_all | solution.py:569
  31.8 0.0 collective-permute-done.4.in_ref
  31.8 0.6 collective-permute-start.5
  32.4 2.0 %shard_map.136 = (bf16[1280,128]{1,0:T(8,128)(2,1)}, bf16[1280,128]{1,0:T(8,128)(2,1)}) custom-call(bf16[2,1280,128]{2,1,0:T(8,128)(2,1)} %collective-permute-done.4.in_ref), custom_call_target="tpu_custom_call" | custom-call | tf_op jit(solution)/shard_map/pallas_call | solution.py:579
  34.4 2.0 %collective-permute-start.6 = (bf16[1280,128]{1,0:T(8,128)(2,1)}, bf16[1280,128]{1,0:T(8,128)(2,1)}, u32[]{:S(2)}, u32[]{:S(2)}) collective-permute-start(bf16[1280,128]{1,0:T(8,128)(2,1)} %get-tuple-element.61.refs_0_), channel_id=1, source_target_pairs={{0,4},{4,0},{8,12},{12,8},{16,20},{20,16},{24,28},{28,24},{1,5},{5... | collective-permute-start | bytes 983048 | tf_op jit(solution)/shard_map/ppermute | solution.py:588
  36.4 1.5 %collective-permute-start.7 = (bf16[1280,128]{1,0:T(8,128)(2,1)}, bf16[1280,128]{1,0:T(8,128)(2,1)}, u32[]{:S(2)}, u32[]{:S(2)}) collective-permute-start(bf16[1280,128]{1,0:T(8,128)(2,1)} %get-tuple-element.62.refs_2_), channel_id=1, source_target_pairs={{0,8},{4,12},{8,0},{12,4},{16,24},{20,28},{24,16},{28,20},{1,9},{5... | collective-permute-start | bytes 983048 | tf_op jit(solution)/shard_map/ppermute | solution.py:588
  37.8 3.3 %shard_map.134 = (bf16[384,1280]{1,0:T(8,128)(2,1)}, bf16[384,1280]{1,0:T(8,128)(2,1)}) custom-call(bf16[1280,1280]{1,0:T(8,128)(2,1)} %own_in.5, bf16[1280,1280]{1,0:T(8,128)(2,1)} %collective-permute-done.sibling_in, f32[1,1280]{1,0:T(1,128)} %copy-done.4, f32[1,1280]{1,0:T(1,128)} %copy-done.7), custom_call_target="tpu_custom_call" | custom-call | tf_op jit(solution)/shard_map/pallas_call | solution.py:532
  41.1 2.8 %all-to-all-done.1.factor_ref = bf16[8,192,128]{2,1,0:T(8,128)(2,1)} async-done(((bf16[8,192,128]{2,1,0:T(8,128)(2,1)}), bf16[8,192,128]{2,1,0:T(8,128)(2,1)}, u32[]{:S(2)}, u32[]{:S(2)}) %all-to-all-start.1) | async-done | bytes 393248 | tf_op jit(solution)/shard_map/all_to_all | solution.py:569
  43.9 0.0 copy-done.6
  43.9 1.1 %shard_map.135 = (bf16[9,32,128]{2,1,0:T(8,128)(2,1)S(1)}, bf16[4,192,128]{2,1,0:T(8,128)(2,1)S(1)}, bf16[4,192,128]{2,1,0:T(8,128)(2,1)S(1)}) custom-call(bf16[8,192,128]{2,1,0:T(8,128)(2,1)} %all-to-all-done.1.factor_ref, f32[10,128]{1,0:T(8,128)S(1)} %copy-done.6), custom_call_target="tpu_custom_call" | custom-call | tf_op jit(solution)/shard_map/pallas_call | solution.py:596
  45.0 0.1 collective-permute-start.2
  45.1 0.5 collective-permute-start.3
  45.6 0.8 collective-permute-done.6.refs_1_
  46.4 0.9 %collective-permute-start.8 = (bf16[9,32,128]{2,1,0:T(8,128)(2,1)S(1)}, bf16[9,32,128]{2,1,0:T(8,128)(2,1)S(1)}, u32[]{:S(2)}, u32[]{:S(2)}) collective-permute-start(bf16[9,32,128]{2,1,0:T(8,128)(2,1)S(1)} %get-tuple-element.63), channel_id=1, source_target_pairs={{0,2},{1,3},{2,0},{3,1},{4,6},{5,7},{6,4},{7,5},{8,10},{9,11},{10,... | collective-permute-start | bytes 221192 | tf_op jit(solution)/shard_map/ppermute | solution.py:463
  47.3 1.1 %collective-permute-done.7.refs_3_ = bf16[1280,128]{1,0:T(8,128)(2,1)} collective-permute-done((bf16[1280,128]{1,0:T(8,128)(2,1)}, bf16[1280,128]{1,0:T(8,128)(2,1)}, u32[]{:S(2)}, u32[]{:S(2)}) %collective-permute-start.7) | collective-permute-done | bytes 327712 | tf_op jit(solution)/shard_map/ppermute | solution.py:588
  48.4 1.6 %shard_map.137.blocks = bf16[2560,256]{1,0:T(8,128)(2,1)S(1)} custom-call(bf16[1280,128]{1,0:T(8,128)(2,1)} %get-tuple-element.61.refs_0_, bf16[1280,128]{1,0:T(8,128)(2,1)} %collective-permute-done.6.refs_1_, bf16[1280,128]{1,0:T(8,128)(2,1)} %get-tuple-element.62.refs_2_, bf16[1280,128]{1,0:T(8,128)(2,1)} %collective-permute-done.7.refs_3_), custom_call_target="tpu_custom_call" | custom-call | tf_op jit(solution)/shard_map/pallas_call | solution.py:631
  50.0 0.7 collective-permute-done.8.b_ref.refs_0_
  50.7 0.0 collective-permute-done.2.refs_2_
  50.7 0.0 collective-permute-done.3.refs_3_
  50.7 0.0 copy-start.1
  50.8 0.0 copy-start.2
  50.8 1.7 %shard_map.138 = (bf16[2560,256]{1,0:T(8,128)(2,1)S(1)}, bf16[640,256]{1,0:T(8,128)(2,1)S(1)}) custom-call(bf16[2560,256]{1,0:T(8,128)(2,1)S(1)} %shard_map.137.blocks, bf16[9,32,128]{2,1,0:T(8,128)(2,1)S(1)} %collective-permute-done.8.b_ref.refs_0_, bf16[640,2560]{1,0:T(8,128)(2,1)S(1)} %get-tuple-element.52.x.refs_4_, ...), custom_call_target="tpu_custom_call" | custom-call | tf_op jit(solution)/shard_map/pallas_call | solution.py:638
  52.5 1.0 %collective-permute-start.11 = (bf16[640,256]{1,0:T(8,128)(2,1)S(1)}, bf16[640,256]{1,0:T(8,128)(2,1)S(1)}, u32[]{:S(2)}, u32[]{:S(2)}) collective-permute-start(bf16[640,256]{1,0:T(8,128)(2,1)S(1)} %get-tuple-element.64), channel_id=1, source_target_pairs={{0,2},{1,3},{2,0},{3,1},{4,6},{5,7},{6,4},{7,5},{8,10},{9,11},{10,... | collective-permute-start | bytes 983048 | tf_op jit(solution)/shard_map/ppermute | solution.py:463
  53.5 0.0 collective-permute-done.5.in_ref
  53.5 1.1 %shard_map.139 = (bf16[1280,128]{1,0:T(8,128)(2,1)S(1)}, bf16[1280,128]{1,0:T(8,128)(2,1)S(1)}) custom-call(bf16[2,1280,128]{2,1,0:T(8,128)(2,1)} %collective-permute-done.5.in_ref), custom_call_target="tpu_custom_call" | custom-call | tf_op jit(solution)/shard_map/pallas_call | solution.py:579
  54.6 0.9 %collective-permute-start.9 = (bf16[1280,128]{1,0:T(8,128)(2,1)S(1)}, bf16[1280,128]{1,0:T(8,128)(2,1)S(1)}, u32[]{:S(2)}, u32[]{:S(2)}) collective-permute-start(bf16[1280,128]{1,0:T(8,128)(2,1)S(1)} %get-tuple-element.66.refs_0_), channel_id=1, source_target_pairs={{0,4},{4,0},{8,12},{12,8},{16,20},{20,16},{24,28},{28,24},{1,5},{5... | collective-permute-start | bytes 983048 | tf_op jit(solution)/shard_map/ppermute | solution.py:588
  55.5 1.5 %collective-permute-start.10 = (bf16[1280,128]{1,0:T(8,128)(2,1)S(1)}, bf16[1280,128]{1,0:T(8,128)(2,1)S(1)}, u32[]{:S(2)}, u32[]{:S(2)}) collective-permute-start(bf16[1280,128]{1,0:T(8,128)(2,1)S(1)} %get-tuple-element.67.refs_2_), channel_id=1, source_target_pairs={{0,8},{4,12},{8,0},{12,4},{16,24},{20,28},{24,16},{28,20},{1,9},{5... | collective-permute-start | bytes 983048 | tf_op jit(solution)/shard_map/ppermute | solution.py:588
  57.0 0.0 copy-done.1
  57.0 1.6 %shard_map.143 = bf16[640,256]{1,0:T(8,128)(2,1)S(1)} custom-call(bf16[256,1280]{1,0:T(8,128)(2,1)S(1)} %copy-done.2, bf16[256,1280]{1,0:T(8,128)(2,1)S(1)} %copy-done.3, bf16[384,1280]{1,0:T(8,128)(2,1)S(1)} %copy-done, bf16[384,1280]{1,0:T(8,128)(2,1)S(1)} %copy-done.1, bf16[2560,256]{1,0:T(8,128)(2,1)S(1)} %get-tuple-element.69.refs_4_), custom_call_target="tpu_custom_call" | custom-call | tf_op jit(solution)/shard_map/pallas_call | solution.py:646
  58.6 1.4 %collective-permute-start.12 = (bf16[640,256]{1,0:T(8,128)(2,1)S(1)}, bf16[640,256]{1,0:T(8,128)(2,1)S(1)}, u32[]{:S(2)}, u32[]{:S(2)}) collective-permute-start(bf16[640,256]{1,0:T(8,128)(2,1)S(1)} %shard_map.143), channel_id=1, source_target_pairs={{0,2},{1,3},{2,0},{3,1},{4,6},{5,7},{6,4},{7,5},{8,10},{9,11},{10,... | collective-permute-start | bytes 983048 | tf_op jit(solution)/shard_map/ppermute | solution.py:463
  60.0 2.3 %collective-permute-done.11.refs_4_.refs_0_ = bf16[640,256]{1,0:T(8,128)(2,1)S(1)} collective-permute-done((bf16[640,256]{1,0:T(8,128)(2,1)S(1)}, bf16[640,256]{1,0:T(8,128)(2,1)S(1)}, u32[]{:S(2)}, u32[]{:S(2)}) %collective-permute-start.11) | collective-permute-done | bytes 327712 | tf_op jit(solution)/shard_map/ppermute | solution.py:463
  62.3 0.0 collective-permute-done.9.refs_1_
  62.3 1.4 %collective-permute-done.10.refs_3_ = bf16[1280,128]{1,0:T(8,128)(2,1)S(1)} collective-permute-done((bf16[1280,128]{1,0:T(8,128)(2,1)S(1)}, bf16[1280,128]{1,0:T(8,128)(2,1)S(1)}, u32[]{:S(2)}, u32[]{:S(2)}) %collective-permute-start.10) | collective-permute-done | bytes 327712 | tf_op jit(solution)/shard_map/ppermute | solution.py:588
  63.7 0.3 shard_map.140.blocks
  64.0 0.0 slice-start.1
  64.1 1.7 %shard_map.141 = (bf16[2560,256]{1,0:T(8,128)(2,1)S(1)}, bf16[640,256]{1,0:T(8,128)(2,1)S(1)}) custom-call(bf16[2560,256]{1,0:T(8,128)(2,1)S(1)} %shard_map.140.blocks, bf16[9,32,128]{2,1,0:T(8,128)(2,1)S(1)} %collective-permute-done.8.b_ref.refs_0_, bf16[640,2560]{1,0:T(8,128)(2,1)S(1)} %get-tuple-element.52.x.refs_4_, ...), custom_call_target="tpu_custom_call" | custom-call | tf_op jit(solution)/shard_map/pallas_call | solution.py:638
  65.8 1.8 %collective-permute-start.14 = (bf16[640,256]{1,0:T(8,128)(2,1)S(1)}, bf16[640,256]{1,0:T(8,128)(2,1)S(1)}, u32[]{:S(2)}, u32[]{:S(2)}) collective-permute-start(bf16[640,256]{1,0:T(8,128)(2,1)S(1)} %get-tuple-element.71), channel_id=1, source_target_pairs={{0,2},{1,3},{2,0},{3,1},{4,6},{5,7},{6,4},{7,5},{8,10},{9,11},{10,... | collective-permute-start | bytes 983048 | tf_op jit(solution)/shard_map/ppermute | solution.py:463
  67.6 1.5 %shard_map.142.refs_9_ = bf16[640,256]{1,0:T(8,128)(2,1)S(1)} custom-call(bf16[256,1280]{1,0:T(8,128)(2,1)S(1)} %copy-done.2, bf16[256,1280]{1,0:T(8,128)(2,1)S(1)} %copy-done.3, bf16[384,1280]{1,0:T(8,128)(2,1)S(1)} %copy-done, bf16[384,1280]{1,0:T(8,128)(2,1)S(1)} %copy-done.1, bf16[2560,256]{1,0:T(8,128)(2,1)S(1)} %get-tuple-element.68.refs_4_), custom_call_target="tpu_custom_call" | custom-call | tf_op jit(solution)/shard_map/pallas_call | solution.py:646
  69.1 0.4 collective-permute-start.13
  69.5 0.2 shard_map.145.inv
  69.7 0.0 collective-permute-done.12.refs_10_.refs_0_
  69.8 5.2 %shard_map.144 = (f32[1280,256]{1,0:T(8,128)S(1)}, f32[1280,256]{1,0:T(8,128)S(1)}) custom-call(bf16[5120,512]{1,0:T(8,128)(2,1)S(1)} %bitcast.19, bf16[5120,512]{1,0:T(8,128)(2,1)S(1)} %bitcast.19, bf16[4,192,128]{2,1,0:T(8,128)(2,1)S(1)} %get-tuple-element.50.refs_0_, bf16[4,192,128]{2,1,0:T(8,128)(2,1)S(1)} %get-tuple-element.51.refs_1_, ...), custom_call_target="tpu_custom_call" | custom-call | flops 3355443200 | bytes 6553600 | tf_op jit(solution)/shard_map/pallas_call | solution.py:661
  75.0 0.9 %shard_map.146.refs_1_ = bf16[1280,512]{1,0:T(8,128)(2,1)} custom-call(f32[1280,256]{1,0:T(8,128)S(1)} %get-tuple-element.72.own, f32[1280,128]{1,0:T(8,128)S(1)} %shard_map.145.inv, bf16[640,256]{1,0:T(8,128)(2,1)S(1)} %collective-permute-done.11.refs_4_.refs_0_), custom_call_target="tpu_custom_call" | custom-call | tf_op jit(solution)/shard_map/pallas_call | solution.py:414
  75.9 0.9 %shard_map.147.refs_1_ = bf16[1280,512]{1,0:T(8,128)(2,1)} custom-call(f32[1280,256]{1,0:T(8,128)S(1)} %get-tuple-element.72.own, f32[1280,128]{1,0:T(8,128)S(1)} %shard_map.145.inv, bf16[640,256]{1,0:T(8,128)(2,1)S(1)} %collective-permute-done.12.refs_10_.refs_0_, bf16[1280,512]{1,0:T(8,128)(2,1)} %shard_map.146.refs_1_), custom_call_target="tpu_custom_call", output_to_operand_aliasing={{}: (3, {})} | custom-call | tf_op jit(solution)/shard_map/pallas_call | solution.py:414
  76.7 0.0 collective-permute-done.14.refs_0_
  76.8 0.9 %shard_map.148.refs_1_ = bf16[1280,512]{1,0:T(8,128)(2,1)} custom-call(f32[1280,256]{1,0:T(8,128)S(1)} %get-tuple-element.70.own, f32[1280,128]{1,0:T(8,128)S(1)} %shard_map.145.inv, bf16[640,256]{1,0:T(8,128)(2,1)S(1)} %collective-permute-done.14.refs_0_, bf16[1280,512]{1,0:T(8,128)(2,1)} %shard_map.147.refs_1_), custom_call_target="tpu_custom_call", output_to_operand_aliasing={{}: (3, {})} | custom-call | tf_op jit(solution)/shard_map/pallas_call | solution.py:414
  77.6 4.3 %collective-permute-done.13.refs_0_ = bf16[640,256]{1,0:T(8,128)(2,1)S(1)} collective-permute-done((bf16[640,256]{1,0:T(8,128)(2,1)S(1)}, bf16[640,256]{1,0:T(8,128)(2,1)S(1)}, u32[]{:S(2)}, u32[]{:S(2)}) %collective-permute-start.13) | collective-permute-done | bytes 327712 | tf_op jit(solution)/shard_map/ppermute | solution.py:463
  82.0 0.9 %shard_map.149 = bf16[1280,512]{1,0:T(8,128)(2,1)} custom-call(f32[1280,256]{1,0:T(8,128)S(1)} %get-tuple-element.70.own, f32[1280,128]{1,0:T(8,128)S(1)} %shard_map.145.inv, bf16[640,256]{1,0:T(8,128)(2,1)S(1)} %collective-permute-done.13.refs_0_, bf16[1280,512]{1,0:T(8,128)(2,1)} %shard_map.148.refs_1_), custom_call_target="tpu_custom_call", output_to_operand_aliasing={{}: (3, {})} | custom-call | tf_op jit(solution)/shard_map/pallas_call | solution.py:414
  (14 shorter events, 0.0 us)
Async XLA Ops:
  0.6 12.7 %collective-permute-start = (bf16[1280,1280]{1,0:T(8,128)(2,1)}, bf16[1280,1280]{1,0:T(8,128)(2,1)}, u32[]{:S(2)}, u32[]{:S(2)}) collective-permute-start(bf16[1280,1280]{1,0:T(8,128)(2,1)} %own_in.5), channel_id=1, source_target_pairs={{0,1},{1,0},{2,3},{3,2},{4,5},{5,4},{6,7},{7,6},{8,9},{9,8},{10,11... | collective-permute-start | bytes 9830408 | tf_op jit(solution)/shard_map/ppermute | solution.py:455
  1.1 10.9 %copy-start.8 = (f32[1280]{0:T(1024)S(1)}, f32[1280]{0:T(1024)}, u32[]{:S(2)}) copy-start(f32[1280]{0:T(1024)} %param.12) | copy-start | bytes 15364
  3.7 19.5 %all-to-all-start = ((bf16[8,192,128]{2,1,0:T(8,128)(2,1)}), bf16[8,192,128]{2,1,0:T(8,128)(2,1)}, u32[]{:S(2)}, u32[]{:S(2)}) async-start(bf16[8,192,128]{2,1,0:T(8,128)(2,1)} %get-tuple-element.38), calls=%async_computation | async-start | bytes 786432 | tf_op jit(solution)/shard_map/all_to_all | solution.py:501
  10.6 21.2 %collective-permute-start.4 = (bf16[2,1280,128]{2,1,0:T(8,128)(2,1)}, bf16[2,1280,128]{2,1,0:T(8,128)(2,1)}, u32[]{:S(2)}, u32[]{:S(2)}) collective-permute-start(bf16[2,1280,128]{2,1,0:T(8,128)(2,1)} %get-tuple-element.58), channel_id=1, source_target_pairs={{0,2},{1,3},{2,0},{3,1},{4,6},{5,7},{6,4},{7,5},{8,10},{9,11},{10,... | collective-permute-start | bytes 1966088 | tf_op jit(solution)/shard_map/ppermute | solution.py:463
  12.1 7.4 %copy-start.4 = (f32[1,1280]{1,0:T(1,128)}, f32[1,1280]{1,0:T(1,128)S(1)}, u32[]{:S(2)}) copy-start(f32[1,1280]{1,0:T(1,128)S(1)} %broadcast_in_dim.3.own_gain) | copy-start | bytes 15364
  12.1 1.2 %collective-permute-start.1 = (f32[1,1280]{1,0:T(1,128)S(1)}, f32[1,1280]{1,0:T(1,128)S(1)}, u32[]{:S(2)}, u32[]{:S(2)}) collective-permute-start(f32[1,1280]{1,0:T(1,128)S(1)} %broadcast_in_dim.3.own_gain), channel_id=1, source_target_pairs={{0,1},{1,0},{2,3},{3,2},{4,5},{5,4},{6,7},{7,6},{8,9},{9,8},{10,11... | collective-permute-start | bytes 15368 | tf_op jit(solution)/shard_map/ppermute | solution.py:455
  13.3 6.2 %copy-start.7 = (f32[1,1280]{1,0:T(1,128)}, f32[1,1280]{1,0:T(1,128)S(1)}, u32[]{:S(2)}) copy-start(f32[1,1280]{1,0:T(1,128)S(1)} %collective-permute-done.1.sibling_gain) | copy-start | bytes 15364
  19.5 0.6 copy-start.5
  25.8 18.1 %all-to-all-start.1 = ((bf16[8,192,128]{2,1,0:T(8,128)(2,1)}), bf16[8,192,128]{2,1,0:T(8,128)(2,1)}, u32[]{:S(2)}, u32[]{:S(2)}) async-start(bf16[8,192,128]{2,1,0:T(8,128)(2,1)} %get-tuple-element.45), calls=%async_computation.1 | async-start | bytes 786432 | tf_op jit(solution)/shard_map/all_to_all | solution.py:569
  31.8 21.7 %collective-permute-start.5 = (bf16[2,1280,128]{2,1,0:T(8,128)(2,1)}, bf16[2,1280,128]{2,1,0:T(8,128)(2,1)}, u32[]{:S(2)}, u32[]{:S(2)}) collective-permute-start(bf16[2,1280,128]{2,1,0:T(8,128)(2,1)} %get-tuple-element.59), channel_id=1, source_target_pairs={{0,2},{1,3},{2,0},{3,1},{4,6},{5,7},{6,4},{7,5},{8,10},{9,11},{10,... | collective-permute-start | bytes 1966088 | tf_op jit(solution)/shard_map/ppermute | solution.py:463
  34.4 12.0 %collective-permute-start.6 = (bf16[1280,128]{1,0:T(8,128)(2,1)}, bf16[1280,128]{1,0:T(8,128)(2,1)}, u32[]{:S(2)}, u32[]{:S(2)}) collective-permute-start(bf16[1280,128]{1,0:T(8,128)(2,1)} %get-tuple-element.61.refs_0_), channel_id=1, source_target_pairs={{0,4},{4,0},{8,12},{12,8},{16,20},{20,16},{24,28},{28,24},{1,5},{5... | collective-permute-start | bytes 983048 | tf_op jit(solution)/shard_map/ppermute | solution.py:588
  36.4 7.6 %copy-start.6 = (f32[10,128]{1,0:T(8,128)S(1)}, f32[10,128]{1,0:T(8,128)}, u32[]{:S(2)}) copy-start(f32[10,128]{1,0:T(8,128)} %copy-done.5) | copy-start | bytes 15364
  36.4 12.0 %collective-permute-start.7 = (bf16[1280,128]{1,0:T(8,128)(2,1)}, bf16[1280,128]{1,0:T(8,128)(2,1)}, u32[]{:S(2)}, u32[]{:S(2)}) collective-permute-start(bf16[1280,128]{1,0:T(8,128)(2,1)} %get-tuple-element.62.refs_2_), channel_id=1, source_target_pairs={{0,8},{4,12},{8,0},{12,4},{16,24},{20,28},{24,16},{28,20},{1,9},{5... | collective-permute-start | bytes 983048 | tf_op jit(solution)/shard_map/ppermute | solution.py:588
  45.0 5.7 %collective-permute-start.2 = (bf16[4,192,128]{2,1,0:T(8,128)(2,1)S(1)}, bf16[4,192,128]{2,1,0:T(8,128)(2,1)S(1)}, u32[]{:S(2)}, u32[]{:S(2)}) collective-permute-start(bf16[4,192,128]{2,1,0:T(8,128)(2,1)S(1)} %get-tuple-element.50.refs_0_), channel_id=1, source_target_pairs={{0,1},{1,0},{2,3},{3,2},{4,5},{5,4},{6,7},{7,6},{8,9},{9,8},{10,11... | collective-permute-start | bytes 589832 | tf_op jit(solution)/shard_map/ppermute | solution.py:455
  45.1 5.6 %collective-permute-start.3 = (bf16[4,192,128]{2,1,0:T(8,128)(2,1)S(1)}, bf16[4,192,128]{2,1,0:T(8,128)(2,1)S(1)}, u32[]{:S(2)}, u32[]{:S(2)}) collective-permute-start(bf16[4,192,128]{2,1,0:T(8,128)(2,1)S(1)} %get-tuple-element.51.refs_1_), channel_id=1, source_target_pairs={{0,1},{1,0},{2,3},{3,2},{4,5},{5,4},{6,7},{7,6},{8,9},{9,8},{10,11... | collective-permute-start | bytes 589832 | tf_op jit(solution)/shard_map/ppermute | solution.py:455
  46.4 4.4 %collective-permute-start.8 = (bf16[9,32,128]{2,1,0:T(8,128)(2,1)S(1)}, bf16[9,32,128]{2,1,0:T(8,128)(2,1)S(1)}, u32[]{:S(2)}, u32[]{:S(2)}) collective-permute-start(bf16[9,32,128]{2,1,0:T(8,128)(2,1)S(1)} %get-tuple-element.63), channel_id=1, source_target_pairs={{0,2},{1,3},{2,0},{3,1},{4,6},{5,7},{6,4},{7,5},{8,10},{9,11},{10,... | collective-permute-start | bytes 221192 | tf_op jit(solution)/shard_map/ppermute | solution.py:463
  50.7 6.3 %copy-start = (bf16[384,1280]{1,0:T(8,128)(2,1)S(1)}, bf16[384,1280]{1,0:T(8,128)(2,1)}, u32[]{:S(2)}) copy-start(bf16[384,1280]{1,0:T(8,128)(2,1)} %get-tuple-element.55.refs_2_.refs_7_) | copy-start | bytes 2949124
  50.7 6.3 %copy-start.1 = (bf16[384,1280]{1,0:T(8,128)(2,1)S(1)}, bf16[384,1280]{1,0:T(8,128)(2,1)}, u32[]{:S(2)}) copy-start(bf16[384,1280]{1,0:T(8,128)(2,1)} %get-tuple-element.56.refs_3_.refs_8_) | copy-start | bytes 2949124
  50.8 6.2 %copy-start.2 = (bf16[256,1280]{1,0:T(8,128)(2,1)S(1)}, bf16[256,1280]{1,0:T(8,128)(2,1)}, u32[]{:S(2)}) copy-start(bf16[256,1280]{1,0:T(8,128)(2,1)} %get-tuple-element.53.refs_0_.refs_5_) | copy-start | bytes 1966084
  50.8 6.2 %copy-start.3 = (bf16[256,1280]{1,0:T(8,128)(2,1)S(1)}, bf16[256,1280]{1,0:T(8,128)(2,1)}, u32[]{:S(2)}) copy-start(bf16[256,1280]{1,0:T(8,128)(2,1)} %get-tuple-element.54.refs_1_.refs_6_) | copy-start | bytes 1966084
  52.5 9.8 %collective-permute-start.11 = (bf16[640,256]{1,0:T(8,128)(2,1)S(1)}, bf16[640,256]{1,0:T(8,128)(2,1)S(1)}, u32[]{:S(2)}, u32[]{:S(2)}) collective-permute-start(bf16[640,256]{1,0:T(8,128)(2,1)S(1)} %get-tuple-element.64), channel_id=1, source_target_pairs={{0,2},{1,3},{2,0},{3,1},{4,6},{5,7},{6,4},{7,5},{8,10},{9,11},{10,... | collective-permute-start | bytes 983048 | tf_op jit(solution)/shard_map/ppermute | solution.py:463
  54.6 7.7 %collective-permute-start.9 = (bf16[1280,128]{1,0:T(8,128)(2,1)S(1)}, bf16[1280,128]{1,0:T(8,128)(2,1)S(1)}, u32[]{:S(2)}, u32[]{:S(2)}) collective-permute-start(bf16[1280,128]{1,0:T(8,128)(2,1)S(1)} %get-tuple-element.66.refs_0_), channel_id=1, source_target_pairs={{0,4},{4,0},{8,12},{12,8},{16,20},{20,16},{24,28},{28,24},{1,5},{5... | collective-permute-start | bytes 983048 | tf_op jit(solution)/shard_map/ppermute | solution.py:588
  55.5 8.2 %collective-permute-start.10 = (bf16[1280,128]{1,0:T(8,128)(2,1)S(1)}, bf16[1280,128]{1,0:T(8,128)(2,1)S(1)}, u32[]{:S(2)}, u32[]{:S(2)}) collective-permute-start(bf16[1280,128]{1,0:T(8,128)(2,1)S(1)} %get-tuple-element.67.refs_2_), channel_id=1, source_target_pairs={{0,8},{4,12},{8,0},{12,4},{16,24},{20,28},{24,16},{28,20},{1,9},{5... | collective-permute-start | bytes 983048 | tf_op jit(solution)/shard_map/ppermute | solution.py:588
  58.6 11.2 %collective-permute-start.12 = (bf16[640,256]{1,0:T(8,128)(2,1)S(1)}, bf16[640,256]{1,0:T(8,128)(2,1)S(1)}, u32[]{:S(2)}, u32[]{:S(2)}) collective-permute-start(bf16[640,256]{1,0:T(8,128)(2,1)S(1)} %shard_map.143), channel_id=1, source_target_pairs={{0,2},{1,3},{2,0},{3,1},{4,6},{5,7},{6,4},{7,5},{8,10},{9,11},{10,... | collective-permute-start | bytes 983048 | tf_op jit(solution)/shard_map/ppermute | solution.py:463
  63.7 6.0 %slice-start = ((s8[5242880]{0:T(1024)(128)(4,1)}), s8[4194304]{0:T(1024)(128)(4,1)S(1)}, s32[]{:S(2)}) async-start(s8[5242880]{0:T(1024)(128)(4,1)} %bitcast.18), calls=%async_computation.2 | async-start | bytes 8388608
  64.0 5.7 %slice-start.1 = ((s8[5242880]{0:T(1024)(128)(4,1)}), s8[1048576]{0:T(1024)(128)(4,1)S(1)}, s32[]{:S(2)}) async-start(s8[5242880]{0:T(1024)(128)(4,1)} %bitcast.18), calls=%async_computation.3 | async-start | bytes 2097152
  65.8 11.0 %collective-permute-start.14 = (bf16[640,256]{1,0:T(8,128)(2,1)S(1)}, bf16[640,256]{1,0:T(8,128)(2,1)S(1)}, u32[]{:S(2)}, u32[]{:S(2)}) collective-permute-start(bf16[640,256]{1,0:T(8,128)(2,1)S(1)} %get-tuple-element.71), channel_id=1, source_target_pairs={{0,2},{1,3},{2,0},{3,1},{4,6},{5,7},{6,4},{7,5},{8,10},{9,11},{10,... | collective-permute-start | bytes 983048 | tf_op jit(solution)/shard_map/ppermute | solution.py:463
  69.1 12.9 %collective-permute-start.13 = (bf16[640,256]{1,0:T(8,128)(2,1)S(1)}, bf16[640,256]{1,0:T(8,128)(2,1)S(1)}, u32[]{:S(2)}, u32[]{:S(2)}) collective-permute-start(bf16[640,256]{1,0:T(8,128)(2,1)S(1)} %shard_map.142.refs_9_), channel_id=1, source_target_pairs={{0,2},{1,3},{2,0},{3,1},{4,6},{5,7},{6,4},{7,5},{8,10},{9,11},{10,... | collective-permute-start | bytes 983048 | tf_op jit(solution)/shard_map/ppermute | solution.py:463

commit v23 on v22

--- a/solution.py
+++ b/solution.py
@@ -544,11 +544,9 @@
         )(*operands, *before)
         return (list(outs[:-1]), outs[-1]) if summed else (list(outs), None)
 
-    cut = some // 2 // LANES * LANES
     x0, squares = prepared(0, some, tokens, [], True, PREPARE_VMEM_BYTES)
-    x1, _ = prepared(some, cut, 0, [squares], False, LARGE_VMEM_BYTES)
-    exchanged, squares, x1 = lax.optimization_barrier((exchanged, squares, x1))
-    last, _ = prepared(some + cut, some - cut, 0, [], False, LARGE_VMEM_BYTES)
+    exchanged, squares = lax.optimization_barrier((exchanged, squares))
+    x1, _ = prepared(some, some, 0, [squares], False, LARGE_VMEM_BYTES)
     a_next, b_next, sent = pl.pallas_call(
         adam_kernel,
         out_shape=(
@@ -588,8 +586,7 @@
                 outside[strip].append((piece, lax.ppermute(piece, "dp", pairs)))
 
     swap_half(0, sent)
-    own_f, last = lax.optimization_barrier((own_f, last))
-    x1 = x1 + last
+    own_f, x1 = lax.optimization_barrier((own_f, x1))
     up_packed = packed_rows - down_rows
     more = pl.cdiv(3 * (tokens // LANES), up_packed)
     piece = jax.ShapeDtypeStruct((n_dp // FACTOR_PIECES, packed_rows, LANES), bf16)

time: 83.5 us -> 80.5 us (0.964)
  Pallas kernels: 39.3 us -> 35.6 us
  waiting for transfers between devices: 14.6 us -> 16.1 us
    all_to_all x1, waiting for transfers between devices: 0.01 us -> 2.92 us  [body(): exchanged = lax.all_to_all(packed, 'dp', 0, 0, tiled=True)]
    pallas_call x3 -> x2, Pallas kernels: 12.5 us -> 9.96 us  [prepared(): pl.pallas_call(functools.partial(prepare_kernel, first, summed), out_shap...]
    all_to_all x1, starting transfers between devices: 6.01 us -> 4.11 us  [body(): own_f = lax.all_to_all(sent, 'dp', 0, 0, tiled=True)]
    all_to_all x1, waiting for transfers between devices: 2.81 us -> 1.29 us  [body(): own_f = lax.all_to_all(sent, 'dp', 0, 0, tiled=True)]
    ppermute x7, starting transfers between devices: 7.59 us -> 9.06 us  [to_chip(): return lax.ppermute(value, 'tensor', pairs)]
    ppermute x4, waiting for transfers between devices: 3.23 us -> 4.22 us  [swap_half(): outside[strip].append((piece, lax.ppermute(piece, 'dp', pairs)))]
    ppermute x7, waiting for transfers between devices: 7.39 us -> 6.48 us  [to_chip(): return lax.ppermute(value, 'tensor', pairs)]
  transfers between devices with their start and end apart: 17 -> 17, of which waited for: 8 -> 11; matrix products, arithmetic and copies ran while one was open for 0% -> 0% of each run, Pallas kernels for 46% -> 43%
where the time goes in v23:
time: 80.5 us; the launch traced here: 80 us
  Pallas kernels  35.6 us (44%)
  starting transfers between devices  26.8 us (33%)
  waiting for transfers between devices  16.1 us (20%)
  between operations  0.87 us (1%)
    pallas_call x2, Pallas kernels, prepared(): pl.pallas_call(functools.partial(prepare_kernel, first, summed), out_shap...  9.96 us
    ppermute x7, starting transfers between devices, to_chip(): return lax.ppermute(value, 'tensor', pairs)  9.06 us
    all_to_all x1, starting transfers between devices, body(): exchanged = lax.all_to_all(packed, 'dp', 0, 0, tiled=True)  6.86 us
    ppermute x7, waiting for transfers between devices, to_chip(): return lax.ppermute(value, 'tensor', pairs)  6.48 us
    ppermute x4, starting transfers between devices, swap_half(): outside[strip].append((piece, lax.ppermute(piece, 'dp', pairs)))  5.61 us
    pallas_call x1, Pallas kernels, body(): pl.pallas_call(functools.partial(own_kernel, static), out_shape=(jax.Shap...  4.88 us
    ppermute x4, waiting for transfers between devices, swap_half(): outside[strip].append((piece, lax.ppermute(piece, 'dp', pairs)))  4.22 us
    all_to_all x1, starting transfers between devices, body(): own_f = lax.all_to_all(sent, 'dp', 0, 0, tiled=True)  4.11 us
  transfers between devices with their start and end apart: 17, of which 11 were waited for; matrix products, arithmetic and copies ran while one was open for 0% of the time, Pallas kernels for 43%

profile of v23, /device:TPU:0, one launch (start us, length us, event | category | flops | bytes accessed | tf_op | source)
XLA Modules:
  0.0 80.0 jit_solution(12637180025889025711)
XLA Ops:
  0.6 0.5 collective-permute-start
  1.2 2.6 %shard_map.130 = (bf16[8,192,128]{2,1,0:T(8,128)(2,1)}, bf16[2,1280,128]{2,1,0:T(8,128)(2,1)}, bf16[2,1280,128]{2,1,0:T(8,128)(2,1)}) custom-call(f32[128,1280]{1,0:T(8,128)} %bitcast.20, f32[64,512]{1,0:T(8,128)} %bitcast.24, bf16[5120,512]{1,0:T(8,128)(2,1)} %sibling_block.1), custom_call_target="tpu_custom_call" | custom-call | tf_op jit(solution)/shard_map/pallas_call | solution.py:486
  3.7 6.9 %all-to-all-start = ((bf16[8,192,128]{2,1,0:T(8,128)(2,1)}), bf16[8,192,128]{2,1,0:T(8,128)(2,1)}, u32[]{:S(2)}, u32[]{:S(2)}) async-start(bf16[8,192,128]{2,1,0:T(8,128)(2,1)} %get-tuple-element.34), calls=%async_computation | async-start | bytes 786432 | tf_op jit(solution)/shard_map/all_to_all | solution.py:501
  10.6 1.5 %collective-permute-start.4 = (bf16[2,1280,128]{2,1,0:T(8,128)(2,1)}, bf16[2,1280,128]{2,1,0:T(8,128)(2,1)}, u32[]{:S(2)}, u32[]{:S(2)}) collective-permute-start(bf16[2,1280,128]{2,1,0:T(8,128)(2,1)} %get-tuple-element.50), channel_id=1, source_target_pairs={{0,2},{1,3},{2,0},{3,1},{4,6},{5,7},{6,4},{7,5},{8,10},{9,11},{10,... | collective-permute-start | bytes 1966088 | tf_op jit(solution)/shard_map/ppermute | solution.py:463
  12.1 0.0 copy-done.6
  12.1 0.1 collective-permute-start.1
  12.2 1.2 %collective-permute-done.1.sibling_gain = f32[1,1280]{1,0:T(1,128)S(1)} collective-permute-done((f32[1,1280]{1,0:T(1,128)S(1)}, f32[1,1280]{1,0:T(1,128)S(1)}, u32[]{:S(2)}, u32[]{:S(2)}) %collective-permute-start.1) | collective-permute-done | bytes 5152 | tf_op jit(solution)/shard_map/ppermute | solution.py:455
  13.3 0.0 collective-permute-done.sibling_in
  13.3 6.2 %shard_map.131 = (bf16[640,2560]{1,0:T(8,128)(2,1)S(1)}, f32[10,128]{1,0:T(8,128)S(1)}) custom-call(bf16[1280,1280]{1,0:T(8,128)(2,1)} %own_in.3, bf16[1280,1280]{1,0:T(8,128)(2,1)} %collective-permute-done.sibling_in, f32[1,1280]{1,0:T(1,128)S(1)} %broadcast_in_dim.3.own_gain, f32[1,1280]{1,0:T(1,128)S(1)} %collective-permute-done.1.sibling_gain), custom_call_target="tpu_custom_call" | custom-call | tf_op jit(solution)/shard_map/pallas_call | solution.py:532
  19.5 0.0 copy-done.4
  19.5 0.0 copy-done.5
  19.5 0.0 copy-start.2
  19.5 0.6 copy-done.2
  20.1 2.9 %all-to-all-done.grad_in = bf16[8,192,128]{2,1,0:T(8,128)(2,1)} async-done(((bf16[8,192,128]{2,1,0:T(8,128)(2,1)}), bf16[8,192,128]{2,1,0:T(8,128)(2,1)}, u32[]{:S(2)}, u32[]{:S(2)}) %all-to-all-start) | async-done | bytes 393248 | tf_op jit(solution)/shard_map/all_to_all | solution.py:501
  23.0 2.6 %shard_map.132 = (f32[3,128,160]{2,1,0:T(8,128)}, f32[3,8,512]{2,1,0:T(8,128)}, bf16[8,192,128]{2,1,0:T(8,128)(2,1)}) custom-call(bf16[8,192,128]{2,1,0:T(8,128)(2,1)} %all-to-all-done.grad_in, f32[128,1280]{1,0:T(8,128)} %bitcast.21, f32[128,1280]{1,0:T(8,128)} %bitcast.22, f32[128,1280]{1,0:T(8,128)} %bitcast.23, f32[64,512]{1,0:T(8,128)} %refs_3_.1, ...), custom_call_target="tpu_custom_call" | custom-call | tf_op jit(solution)/shard_map/pallas_call | solution.py:550
  25.6 4.1 %all-to-all-start.1 = ((bf16[8,192,128]{2,1,0:T(8,128)(2,1)}), bf16[8,192,128]{2,1,0:T(8,128)(2,1)}, u32[]{:S(2)}, u32[]{:S(2)}) async-start(bf16[8,192,128]{2,1,0:T(8,128)(2,1)} %get-tuple-element.39), calls=%async_computation.1 | async-start | bytes 786432 | tf_op jit(solution)/shard_map/all_to_all | solution.py:567
  29.7 0.0 collective-permute-done.4.in_ref
  29.8 1.6 %collective-permute-start.5 = (bf16[2,1280,128]{2,1,0:T(8,128)(2,1)}, bf16[2,1280,128]{2,1,0:T(8,128)(2,1)}, u32[]{:S(2)}, u32[]{:S(2)}) collective-permute-start(bf16[2,1280,128]{2,1,0:T(8,128)(2,1)} %get-tuple-element.51), channel_id=1, source_target_pairs={{0,2},{1,3},{2,0},{3,1},{4,6},{5,7},{6,4},{7,5},{8,10},{9,11},{10,... | collective-permute-start | bytes 1966088 | tf_op jit(solution)/shard_map/ppermute | solution.py:463
  31.3 2.0 %shard_map.135 = (bf16[1280,128]{1,0:T(8,128)(2,1)}, bf16[1280,128]{1,0:T(8,128)(2,1)}) custom-call(bf16[2,1280,128]{2,1,0:T(8,128)(2,1)} %collective-permute-done.4.in_ref), custom_call_target="tpu_custom_call" | custom-call | tf_op jit(solution)/shard_map/pallas_call | solution.py:577
  33.3 1.8 %collective-permute-start.6 = (bf16[1280,128]{1,0:T(8,128)(2,1)}, bf16[1280,128]{1,0:T(8,128)(2,1)}, u32[]{:S(2)}, u32[]{:S(2)}) collective-permute-start(bf16[1280,128]{1,0:T(8,128)(2,1)} %get-tuple-element.53.refs_0_), channel_id=1, source_target_pairs={{0,4},{4,0},{8,12},{12,8},{16,20},{20,16},{24,28},{28,24},{1,5},{5... | collective-permute-start | bytes 983048 | tf_op jit(solution)/shard_map/ppermute | solution.py:586
  35.1 1.5 %collective-permute-start.7 = (bf16[1280,128]{1,0:T(8,128)(2,1)}, bf16[1280,128]{1,0:T(8,128)(2,1)}, u32[]{:S(2)}, u32[]{:S(2)}) collective-permute-start(bf16[1280,128]{1,0:T(8,128)(2,1)} %get-tuple-element.54.refs_2_), channel_id=1, source_target_pairs={{0,8},{4,12},{8,0},{12,4},{16,24},{20,28},{24,16},{28,20},{1,9},{5... | collective-permute-start | bytes 983048 | tf_op jit(solution)/shard_map/ppermute | solution.py:586
  36.6 3.8 %shard_map.133 = (bf16[640,1280]{1,0:T(8,128)(2,1)}, bf16[640,1280]{1,0:T(8,128)(2,1)}) custom-call(bf16[1280,1280]{1,0:T(8,128)(2,1)} %own_in.3, bf16[1280,1280]{1,0:T(8,128)(2,1)} %collective-permute-done.sibling_in, f32[1,1280]{1,0:T(1,128)} %copy-done.4, f32[1,1280]{1,0:T(1,128)} %copy-done.5, f32[10,128]{1,0:T(8,128)} %copy-done.2), custom_call_target="tpu_custom_call" | custom-call | tf_op jit(solution)/shard_map/pallas_call | solution.py:532
  40.4 1.3 %all-to-all-done.1.factor_ref = bf16[8,192,128]{2,1,0:T(8,128)(2,1)} async-done(((bf16[8,192,128]{2,1,0:T(8,128)(2,1)}), bf16[8,192,128]{2,1,0:T(8,128)(2,1)}, u32[]{:S(2)}, u32[]{:S(2)}) %all-to-all-start.1) | async-done | bytes 393248 | tf_op jit(solution)/shard_map/all_to_all | solution.py:567
  41.7 0.0 copy-done.3
  41.7 1.1 %shard_map.134 = (bf16[9,32,128]{2,1,0:T(8,128)(2,1)S(1)}, bf16[4,192,128]{2,1,0:T(8,128)(2,1)S(1)}, bf16[4,192,128]{2,1,0:T(8,128)(2,1)S(1)}) custom-call(bf16[8,192,128]{2,1,0:T(8,128)(2,1)} %all-to-all-done.1.factor_ref, f32[10,128]{1,0:T(8,128)S(1)} %copy-done.3), custom_call_target="tpu_custom_call" | custom-call | tf_op jit(solution)/shard_map/pallas_call | solution.py:593
  42.8 0.1 collective-permute-start.2
  42.8 0.5 collective-permute-start.3
  43.3 0.7 collective-permute-done.6.refs_1_
  44.1 1.5 %collective-permute-start.8 = (bf16[9,32,128]{2,1,0:T(8,128)(2,1)S(1)}, bf16[9,32,128]{2,1,0:T(8,128)(2,1)S(1)}, u32[]{:S(2)}, u32[]{:S(2)}) collective-permute-start(bf16[9,32,128]{2,1,0:T(8,128)(2,1)S(1)} %get-tuple-element.55), channel_id=1, source_target_pairs={{0,2},{1,3},{2,0},{3,1},{4,6},{5,7},{6,4},{7,5},{8,10},{9,11},{10,... | collective-permute-start | bytes 221192 | tf_op jit(solution)/shard_map/ppermute | solution.py:463
  45.6 0.2 collective-permute-done.7.refs_3_
  45.8 1.6 %shard_map.136.blocks = bf16[2560,256]{1,0:T(8,128)(2,1)S(1)} custom-call(bf16[1280,128]{1,0:T(8,128)(2,1)} %get-tuple-element.53.refs_0_, bf16[1280,128]{1,0:T(8,128)(2,1)} %collective-permute-done.6.refs_1_, bf16[1280,128]{1,0:T(8,128)(2,1)} %get-tuple-element.54.refs_2_, bf16[1280,128]{1,0:T(8,128)(2,1)} %collective-permute-done.7.refs_3_), custom_call_target="tpu_custom_call" | custom-call | tf_op jit(solution)/shard_map/pallas_call | solution.py:628
  47.4 1.0 %collective-permute-done.8.b_ref.refs_0_ = bf16[9,32,128]{2,1,0:T(8,128)(2,1)S(1)} collective-permute-done((bf16[9,32,128]{2,1,0:T(8,128)(2,1)S(1)}, bf16[9,32,128]{2,1,0:T(8,128)(2,1)S(1)}, u32[]{:S(2)}, u32[]{:S(2)}) %collective-permute-start.8) | collective-permute-done | bytes 73760 | tf_op jit(solution)/shard_map/ppermute | solution.py:463
  48.4 0.0 collective-permute-done.2.refs_2_
  48.4 0.0 collective-permute-done.3.refs_3_
  48.4 0.0 copy-start.1
  48.4 1.7 %shard_map.137 = (bf16[2560,256]{1,0:T(8,128)(2,1)S(1)}, bf16[640,256]{1,0:T(8,128)(2,1)S(1)}) custom-call(bf16[2560,256]{1,0:T(8,128)(2,1)S(1)} %shard_map.136.blocks, bf16[9,32,128]{2,1,0:T(8,128)(2,1)S(1)} %collective-permute-done.8.b_ref.refs_0_, bf16[640,2560]{1,0:T(8,128)(2,1)S(1)} %get-tuple-element.46.x.refs_4_, ...), custom_call_target="tpu_custom_call" | custom-call | tf_op jit(solution)/shard_map/pallas_call | solution.py:635
  50.2 1.6 %collective-permute-start.11 = (bf16[640,256]{1,0:T(8,128)(2,1)S(1)}, bf16[640,256]{1,0:T(8,128)(2,1)S(1)}, u32[]{:S(2)}, u32[]{:S(2)}) collective-permute-start(bf16[640,256]{1,0:T(8,128)(2,1)S(1)} %get-tuple-element.56), channel_id=1, source_target_pairs={{0,2},{1,3},{2,0},{3,1},{4,6},{5,7},{6,4},{7,5},{8,10},{9,11},{10,... | collective-permute-start | bytes 983048 | tf_op jit(solution)/shard_map/ppermute | solution.py:463
  51.7 0.0 collective-permute-done.5.in_ref
  51.7 1.1 %shard_map.138 = (bf16[1280,128]{1,0:T(8,128)(2,1)S(1)}, bf16[1280,128]{1,0:T(8,128)(2,1)S(1)}) custom-call(bf16[2,1280,128]{2,1,0:T(8,128)(2,1)} %collective-permute-done.5.in_ref), custom_call_target="tpu_custom_call" | custom-call | tf_op jit(solution)/shard_map/pallas_call | solution.py:577
  52.8 0.8 %collective-permute-start.9 = (bf16[1280,128]{1,0:T(8,128)(2,1)S(1)}, bf16[1280,128]{1,0:T(8,128)(2,1)S(1)}, u32[]{:S(2)}, u32[]{:S(2)}) collective-permute-start(bf16[1280,128]{1,0:T(8,128)(2,1)S(1)} %get-tuple-element.58.refs_0_), channel_id=1, source_target_pairs={{0,4},{4,0},{8,12},{12,8},{16,20},{20,16},{24,28},{28,24},{1,5},{5... | collective-permute-start | bytes 983048 | tf_op jit(solution)/shard_map/ppermute | solution.py:586
  53.7 1.5 %collective-permute-start.10 = (bf16[1280,128]{1,0:T(8,128)(2,1)S(1)}, bf16[1280,128]{1,0:T(8,128)(2,1)S(1)}, u32[]{:S(2)}, u32[]{:S(2)}) collective-permute-start(bf16[1280,128]{1,0:T(8,128)(2,1)S(1)} %get-tuple-element.59.refs_2_), channel_id=1, source_target_pairs={{0,8},{4,12},{8,0},{12,4},{16,24},{20,28},{24,16},{28,20},{1,9},{5... | collective-permute-start | bytes 983048 | tf_op jit(solution)/shard_map/ppermute | solution.py:586
  55.2 0.0 copy-done
  55.2 1.2 %shard_map.142 = bf16[640,256]{1,0:T(8,128)(2,1)S(1)} custom-call(bf16[640,1280]{1,0:T(8,128)(2,1)S(1)} %copy-done, bf16[640,1280]{1,0:T(8,128)(2,1)S(1)} %copy-done.1, bf16[2560,256]{1,0:T(8,128)(2,1)S(1)} %get-tuple-element.61.refs_2_), custom_call_target="tpu_custom_call" | custom-call | tf_op jit(solution)/shard_map/pallas_call | solution.py:643
  56.4 0.8 %collective-permute-start.12 = (bf16[640,256]{1,0:T(8,128)(2,1)S(1)}, bf16[640,256]{1,0:T(8,128)(2,1)S(1)}, u32[]{:S(2)}, u32[]{:S(2)}) collective-permute-start(bf16[640,256]{1,0:T(8,128)(2,1)S(1)} %shard_map.142), channel_id=1, source_target_pairs={{0,2},{1,3},{2,0},{3,1},{4,6},{5,7},{6,4},{7,5},{8,10},{9,11},{10,... | collective-permute-start | bytes 983048 | tf_op jit(solution)/shard_map/ppermute | solution.py:463
  57.2 1.6 %collective-permute-done.11.refs_4_.refs_0_ = bf16[640,256]{1,0:T(8,128)(2,1)S(1)} collective-permute-done((bf16[640,256]{1,0:T(8,128)(2,1)S(1)}, bf16[640,256]{1,0:T(8,128)(2,1)S(1)}, u32[]{:S(2)}, u32[]{:S(2)}) %collective-permute-start.11) | collective-permute-done | bytes 327712 | tf_op jit(solution)/shard_map/ppermute | solution.py:463
  58.8 1.8 %collective-permute-done.9.refs_1_ = bf16[1280,128]{1,0:T(8,128)(2,1)S(1)} collective-permute-done((bf16[1280,128]{1,0:T(8,128)(2,1)S(1)}, bf16[1280,128]{1,0:T(8,128)(2,1)S(1)}, u32[]{:S(2)}, u32[]{:S(2)}) %collective-permute-start.9) | collective-permute-done | bytes 327712 | tf_op jit(solution)/shard_map/ppermute | solution.py:586
  60.6 1.5 %collective-permute-done.10.refs_3_ = bf16[1280,128]{1,0:T(8,128)(2,1)S(1)} collective-permute-done((bf16[1280,128]{1,0:T(8,128)(2,1)S(1)}, bf16[1280,128]{1,0:T(8,128)(2,1)S(1)}, u32[]{:S(2)}, u32[]{:S(2)}) %collective-permute-start.10) | collective-permute-done | bytes 327712 | tf_op jit(solution)/shard_map/ppermute | solution.py:586
  62.1 0.3 shard_map.139.blocks
  62.4 0.0 slice-start.1
  62.4 1.7 %shard_map.140 = (bf16[2560,256]{1,0:T(8,128)(2,1)S(1)}, bf16[640,256]{1,0:T(8,128)(2,1)S(1)}) custom-call(bf16[2560,256]{1,0:T(8,128)(2,1)S(1)} %shard_map.139.blocks, bf16[9,32,128]{2,1,0:T(8,128)(2,1)S(1)} %collective-permute-done.8.b_ref.refs_0_, bf16[640,2560]{1,0:T(8,128)(2,1)S(1)} %get-tuple-element.46.x.refs_4_, ...), custom_call_target="tpu_custom_call" | custom-call | tf_op jit(solution)/shard_map/pallas_call | solution.py:635
  64.1 0.6 collective-permute-start.14
  64.7 1.2 %shard_map.141.refs_7_ = bf16[640,256]{1,0:T(8,128)(2,1)S(1)} custom-call(bf16[640,1280]{1,0:T(8,128)(2,1)S(1)} %copy-done, bf16[640,1280]{1,0:T(8,128)(2,1)S(1)} %copy-done.1, bf16[2560,256]{1,0:T(8,128)(2,1)S(1)} %get-tuple-element.60.refs_2_), custom_call_target="tpu_custom_call" | custom-call | tf_op jit(solution)/shard_map/pallas_call | solution.py:643
  65.9 1.6 %collective-permute-start.13 = (bf16[640,256]{1,0:T(8,128)(2,1)S(1)}, bf16[640,256]{1,0:T(8,128)(2,1)S(1)}, u32[]{:S(2)}, u32[]{:S(2)}) collective-permute-start(bf16[640,256]{1,0:T(8,128)(2,1)S(1)} %shard_map.141.refs_7_), channel_id=1, source_target_pairs={{0,2},{1,3},{2,0},{3,1},{4,6},{5,7},{6,4},{7,5},{8,10},{9,11},{10,... | collective-permute-start | bytes 983048 | tf_op jit(solution)/shard_map/ppermute | solution.py:463
  67.5 0.2 shard_map.144.inv
  67.7 0.0 collective-permute-done.12.refs_8_.refs_0_
  67.7 0.0 slice-done
  67.8 0.0 slice-done.1
  67.8 4.9 %shard_map.143 = (f32[1280,256]{1,0:T(8,128)S(1)}, f32[1280,256]{1,0:T(8,128)S(1)}) custom-call(bf16[5120,512]{1,0:T(8,128)(2,1)S(1)} %bitcast.19, bf16[5120,512]{1,0:T(8,128)(2,1)S(1)} %bitcast.19, bf16[4,192,128]{2,1,0:T(8,128)(2,1)S(1)} %get-tuple-element.44.refs_0_, bf16[4,192,128]{2,1,0:T(8,128)(2,1)S(1)} %get-tuple-element.45.refs_1_, ...), custom_call_target="tpu_custom_call" | custom-call | flops 3355443200 | bytes 6553600 | tf_op jit(solution)/shard_map/pallas_call | solution.py:658
  72.7 0.9 %shard_map.145.refs_1_ = bf16[1280,512]{1,0:T(8,128)(2,1)} custom-call(f32[1280,256]{1,0:T(8,128)S(1)} %get-tuple-element.64.own, f32[1280,128]{1,0:T(8,128)S(1)} %shard_map.144.inv, bf16[640,256]{1,0:T(8,128)(2,1)S(1)} %collective-permute-done.11.refs_4_.refs_0_), custom_call_target="tpu_custom_call" | custom-call | tf_op jit(solution)/shard_map/pallas_call | solution.py:414
  73.5 0.9 %shard_map.146.refs_1_ = bf16[1280,512]{1,0:T(8,128)(2,1)} custom-call(f32[1280,256]{1,0:T(8,128)S(1)} %get-tuple-element.64.own, f32[1280,128]{1,0:T(8,128)S(1)} %shard_map.144.inv, bf16[640,256]{1,0:T(8,128)(2,1)S(1)} %collective-permute-done.12.refs_8_.refs_0_, bf16[1280,512]{1,0:T(8,128)(2,1)} %shard_map.145.refs_1_), custom_call_target="tpu_custom_call", output_to_operand_aliasing={{}: (3, {})} | custom-call | tf_op jit(solution)/shard_map/pallas_call | solution.py:414
  74.4 0.4 collective-permute-done.14.refs_0_
  74.9 0.9 %shard_map.147.refs_1_ = bf16[1280,512]{1,0:T(8,128)(2,1)} custom-call(f32[1280,256]{1,0:T(8,128)S(1)} %get-tuple-element.62.own, f32[1280,128]{1,0:T(8,128)S(1)} %shard_map.144.inv, bf16[640,256]{1,0:T(8,128)(2,1)S(1)} %collective-permute-done.14.refs_0_, bf16[1280,512]{1,0:T(8,128)(2,1)} %shard_map.146.refs_1_), custom_call_target="tpu_custom_call", output_to_operand_aliasing={{}: (3, {})} | custom-call | tf_op jit(solution)/shard_map/pallas_call | solution.py:414
  75.7 3.4 %collective-permute-done.13.refs_0_ = bf16[640,256]{1,0:T(8,128)(2,1)S(1)} collective-permute-done((bf16[640,256]{1,0:T(8,128)(2,1)S(1)}, bf16[640,256]{1,0:T(8,128)(2,1)S(1)}, u32[]{:S(2)}, u32[]{:S(2)}) %collective-permute-start.13) | collective-permute-done | bytes 327712 | tf_op jit(solution)/shard_map/ppermute | solution.py:463
  79.1 0.9 %shard_map.148 = bf16[1280,512]{1,0:T(8,128)(2,1)} custom-call(f32[1280,256]{1,0:T(8,128)S(1)} %get-tuple-element.62.own, f32[1280,128]{1,0:T(8,128)S(1)} %shard_map.144.inv, bf16[640,256]{1,0:T(8,128)(2,1)S(1)} %collective-permute-done.13.refs_0_, bf16[1280,512]{1,0:T(8,128)(2,1)} %shard_map.147.refs_1_), custom_call_target="tpu_custom_call", output_to_operand_aliasing={{}: (3, {})} | custom-call | tf_op jit(solution)/shard_map/pallas_call | solution.py:414
  (9 shorter events, 0.0 us)
Async XLA Ops:
  0.6 12.7 %collective-permute-start = (bf16[1280,1280]{1,0:T(8,128)(2,1)}, bf16[1280,1280]{1,0:T(8,128)(2,1)}, u32[]{:S(2)}, u32[]{:S(2)}) collective-permute-start(bf16[1280,1280]{1,0:T(8,128)(2,1)} %own_in.3), channel_id=1, source_target_pairs={{0,1},{1,0},{2,3},{3,2},{4,5},{5,4},{6,7},{7,6},{8,9},{9,8},{10,11... | collective-permute-start | bytes 9830408 | tf_op jit(solution)/shard_map/ppermute | solution.py:455
  1.1 10.9 %copy-start.6 = (f32[1280]{0:T(1024)S(1)}, f32[1280]{0:T(1024)}, u32[]{:S(2)}) copy-start(f32[1280]{0:T(1024)} %param.12) | copy-start | bytes 15364
  3.7 19.3 %all-to-all-start = ((bf16[8,192,128]{2,1,0:T(8,128)(2,1)}), bf16[8,192,128]{2,1,0:T(8,128)(2,1)}, u32[]{:S(2)}, u32[]{:S(2)}) async-start(bf16[8,192,128]{2,1,0:T(8,128)(2,1)} %get-tuple-element.34), calls=%async_computation | async-start | bytes 786432 | tf_op jit(solution)/shard_map/all_to_all | solution.py:501
  10.6 19.1 %collective-permute-start.4 = (bf16[2,1280,128]{2,1,0:T(8,128)(2,1)}, bf16[2,1280,128]{2,1,0:T(8,128)(2,1)}, u32[]{:S(2)}, u32[]{:S(2)}) collective-permute-start(bf16[2,1280,128]{2,1,0:T(8,128)(2,1)} %get-tuple-element.50), channel_id=1, source_target_pairs={{0,2},{1,3},{2,0},{3,1},{4,6},{5,7},{6,4},{7,5},{8,10},{9,11},{10,... | collective-permute-start | bytes 1966088 | tf_op jit(solution)/shard_map/ppermute | solution.py:463
  12.1 7.4 %copy-start.4 = (f32[1,1280]{1,0:T(1,128)}, f32[1,1280]{1,0:T(1,128)S(1)}, u32[]{:S(2)}) copy-start(f32[1,1280]{1,0:T(1,128)S(1)} %broadcast_in_dim.3.own_gain) | copy-start | bytes 15364
  12.1 1.2 %collective-permute-start.1 = (f32[1,1280]{1,0:T(1,128)S(1)}, f32[1,1280]{1,0:T(1,128)S(1)}, u32[]{:S(2)}, u32[]{:S(2)}) collective-permute-start(f32[1,1280]{1,0:T(1,128)S(1)} %broadcast_in_dim.3.own_gain), channel_id=1, source_target_pairs={{0,1},{1,0},{2,3},{3,2},{4,5},{5,4},{6,7},{7,6},{8,9},{9,8},{10,11... | collective-permute-start | bytes 15368 | tf_op jit(solution)/shard_map/ppermute | solution.py:455
  13.3 6.2 %copy-start.5 = (f32[1,1280]{1,0:T(1,128)}, f32[1,1280]{1,0:T(1,128)S(1)}, u32[]{:S(2)}) copy-start(f32[1,1280]{1,0:T(1,128)S(1)} %collective-permute-done.1.sibling_gain) | copy-start | bytes 15364
  19.5 0.6 copy-start.2
  25.6 16.0 %all-to-all-start.1 = ((bf16[8,192,128]{2,1,0:T(8,128)(2,1)}), bf16[8,192,128]{2,1,0:T(8,128)(2,1)}, u32[]{:S(2)}, u32[]{:S(2)}) async-start(bf16[8,192,128]{2,1,0:T(8,128)(2,1)} %get-tuple-element.39), calls=%async_computation.1 | async-start | bytes 786432 | tf_op jit(solution)/shard_map/all_to_all | solution.py:567
  29.8 22.0 %collective-permute-start.5 = (bf16[2,1280,128]{2,1,0:T(8,128)(2,1)}, bf16[2,1280,128]{2,1,0:T(8,128)(2,1)}, u32[]{:S(2)}, u32[]{:S(2)}) collective-permute-start(bf16[2,1280,128]{2,1,0:T(8,128)(2,1)} %get-tuple-element.51), channel_id=1, source_target_pairs={{0,2},{1,3},{2,0},{3,1},{4,6},{5,7},{6,4},{7,5},{8,10},{9,11},{10,... | collective-permute-start | bytes 1966088 | tf_op jit(solution)/shard_map/ppermute | solution.py:463
  33.3 10.8 %collective-permute-start.6 = (bf16[1280,128]{1,0:T(8,128)(2,1)}, bf16[1280,128]{1,0:T(8,128)(2,1)}, u32[]{:S(2)}, u32[]{:S(2)}) collective-permute-start(bf16[1280,128]{1,0:T(8,128)(2,1)} %get-tuple-element.53.refs_0_), channel_id=1, source_target_pairs={{0,4},{4,0},{8,12},{12,8},{16,20},{20,16},{24,28},{28,24},{1,5},{5... | collective-permute-start | bytes 983048 | tf_op jit(solution)/shard_map/ppermute | solution.py:586
  35.1 6.6 %copy-start.3 = (f32[10,128]{1,0:T(8,128)S(1)}, f32[10,128]{1,0:T(8,128)}, u32[]{:S(2)}) copy-start(f32[10,128]{1,0:T(8,128)} %copy-done.2) | copy-start | bytes 15364
  35.1 10.7 %collective-permute-start.7 = (bf16[1280,128]{1,0:T(8,128)(2,1)}, bf16[1280,128]{1,0:T(8,128)(2,1)}, u32[]{:S(2)}, u32[]{:S(2)}) collective-permute-start(bf16[1280,128]{1,0:T(8,128)(2,1)} %get-tuple-element.54.refs_2_), channel_id=1, source_target_pairs={{0,8},{4,12},{8,0},{12,4},{16,24},{20,28},{24,16},{28,20},{1,9},{5... | collective-permute-start | bytes 983048 | tf_op jit(solution)/shard_map/ppermute | solution.py:586
  42.8 5.7 %collective-permute-start.2 = (bf16[4,192,128]{2,1,0:T(8,128)(2,1)S(1)}, bf16[4,192,128]{2,1,0:T(8,128)(2,1)S(1)}, u32[]{:S(2)}, u32[]{:S(2)}) collective-permute-start(bf16[4,192,128]{2,1,0:T(8,128)(2,1)S(1)} %get-tuple-element.44.refs_0_), channel_id=1, source_target_pairs={{0,1},{1,0},{2,3},{3,2},{4,5},{5,4},{6,7},{7,6},{8,9},{9,8},{10,11... | collective-permute-start | bytes 589832 | tf_op jit(solution)/shard_map/ppermute | solution.py:455
  42.8 5.6 %collective-permute-start.3 = (bf16[4,192,128]{2,1,0:T(8,128)(2,1)S(1)}, bf16[4,192,128]{2,1,0:T(8,128)(2,1)S(1)}, u32[]{:S(2)}, u32[]{:S(2)}) collective-permute-start(bf16[4,192,128]{2,1,0:T(8,128)(2,1)S(1)} %get-tuple-element.45.refs_1_), channel_id=1, source_target_pairs={{0,1},{1,0},{2,3},{3,2},{4,5},{5,4},{6,7},{7,6},{8,9},{9,8},{10,11... | collective-permute-start | bytes 589832 | tf_op jit(solution)/shard_map/ppermute | solution.py:455
  44.1 4.4 %collective-permute-start.8 = (bf16[9,32,128]{2,1,0:T(8,128)(2,1)S(1)}, bf16[9,32,128]{2,1,0:T(8,128)(2,1)S(1)}, u32[]{:S(2)}, u32[]{:S(2)}) collective-permute-start(bf16[9,32,128]{2,1,0:T(8,128)(2,1)S(1)} %get-tuple-element.55), channel_id=1, source_target_pairs={{0,2},{1,3},{2,0},{3,1},{4,6},{5,7},{6,4},{7,5},{8,10},{9,11},{10,... | collective-permute-start | bytes 221192 | tf_op jit(solution)/shard_map/ppermute | solution.py:463
  48.4 6.7 %copy-start = (bf16[640,1280]{1,0:T(8,128)(2,1)S(1)}, bf16[640,1280]{1,0:T(8,128)(2,1)}, u32[]{:S(2)}) copy-start(bf16[640,1280]{1,0:T(8,128)(2,1)} %get-tuple-element.47.refs_0_.refs_5_) | copy-start | bytes 4915204
  48.4 6.7 %copy-start.1 = (bf16[640,1280]{1,0:T(8,128)(2,1)S(1)}, bf16[640,1280]{1,0:T(8,128)(2,1)}, u32[]{:S(2)}) copy-start(bf16[640,1280]{1,0:T(8,128)(2,1)} %get-tuple-element.48.refs_1_.refs_6_) | copy-start | bytes 4915204
  50.2 8.6 %collective-permute-start.11 = (bf16[640,256]{1,0:T(8,128)(2,1)S(1)}, bf16[640,256]{1,0:T(8,128)(2,1)S(1)}, u32[]{:S(2)}, u32[]{:S(2)}) collective-permute-start(bf16[640,256]{1,0:T(8,128)(2,1)S(1)} %get-tuple-element.56), channel_id=1, source_target_pairs={{0,2},{1,3},{2,0},{3,1},{4,6},{5,7},{6,4},{7,5},{8,10},{9,11},{10,... | collective-permute-start | bytes 983048 | tf_op jit(solution)/shard_map/ppermute | solution.py:463
  52.8 7.8 %collective-permute-start.9 = (bf16[1280,128]{1,0:T(8,128)(2,1)S(1)}, bf16[1280,128]{1,0:T(8,128)(2,1)S(1)}, u32[]{:S(2)}, u32[]{:S(2)}) collective-permute-start(bf16[1280,128]{1,0:T(8,128)(2,1)S(1)} %get-tuple-element.58.refs_0_), channel_id=1, source_target_pairs={{0,4},{4,0},{8,12},{12,8},{16,20},{20,16},{24,28},{28,24},{1,5},{5... | collective-permute-start | bytes 983048 | tf_op jit(solution)/shard_map/ppermute | solution.py:586
  53.7 8.4 %collective-permute-start.10 = (bf16[1280,128]{1,0:T(8,128)(2,1)S(1)}, bf16[1280,128]{1,0:T(8,128)(2,1)S(1)}, u32[]{:S(2)}, u32[]{:S(2)}) collective-permute-start(bf16[1280,128]{1,0:T(8,128)(2,1)S(1)} %get-tuple-element.59.refs_2_), channel_id=1, source_target_pairs={{0,8},{4,12},{8,0},{12,4},{16,24},{20,28},{24,16},{28,20},{1,9},{5... | collective-permute-start | bytes 983048 | tf_op jit(solution)/shard_map/ppermute | solution.py:586
  56.4 11.4 %collective-permute-start.12 = (bf16[640,256]{1,0:T(8,128)(2,1)S(1)}, bf16[640,256]{1,0:T(8,128)(2,1)S(1)}, u32[]{:S(2)}, u32[]{:S(2)}) collective-permute-start(bf16[640,256]{1,0:T(8,128)(2,1)S(1)} %shard_map.142), channel_id=1, source_target_pairs={{0,2},{1,3},{2,0},{3,1},{4,6},{5,7},{6,4},{7,5},{8,10},{9,11},{10,... | collective-permute-start | bytes 983048 | tf_op jit(solution)/shard_map/ppermute | solution.py:463
  62.1 5.7 %slice-start = ((s8[5242880]{0:T(1024)(128)(4,1)}), s8[4194304]{0:T(1024)(128)(4,1)S(1)}, s32[]{:S(2)}) async-start(s8[5242880]{0:T(1024)(128)(4,1)} %bitcast.18), calls=%async_computation.2 | async-start | bytes 8388608
  62.4 5.3 %slice-start.1 = ((s8[5242880]{0:T(1024)(128)(4,1)}), s8[1048576]{0:T(1024)(128)(4,1)S(1)}, s32[]{:S(2)}) async-start(s8[5242880]{0:T(1024)(128)(4,1)} %bitcast.18), calls=%async_computation.3 | async-start | bytes 2097152
  64.1 10.7 %collective-permute-start.14 = (bf16[640,256]{1,0:T(8,128)(2,1)S(1)}, bf16[640,256]{1,0:T(8,128)(2,1)S(1)}, u32[]{:S(2)}, u32[]{:S(2)}) collective-permute-start(bf16[640,256]{1,0:T(8,128)(2,1)S(1)} %get-tuple-element.63), channel_id=1, source_target_pairs={{0,2},{1,3},{2,0},{3,1},{4,6},{5,7},{6,4},{7,5},{8,10},{9,11},{10,... | collective-permute-start | bytes 983048 | tf_op jit(solution)/shard_map/ppermute | solution.py:463
  65.9 13.2 %collective-permute-start.13 = (bf16[640,256]{1,0:T(8,128)(2,1)S(1)}, bf16[640,256]{1,0:T(8,128)(2,1)S(1)}, u32[]{:S(2)}, u32[]{:S(2)}) collective-permute-start(bf16[640,256]{1,0:T(8,128)(2,1)S(1)} %shard_map.141.refs_7_), channel_id=1, source_target_pairs={{0,2},{1,3},{2,0},{3,1},{4,6},{5,7},{6,4},{7,5},{8,10},{9,11},{10,... | collective-permute-start | bytes 983048 | tf_op jit(solution)/shard_map/ppermute | solution.py:463

commit v24 on v23

--- a/solution.py
+++ b/solution.py
@@ -104,9 +104,25 @@
         copy.wait()
 
 
-def split_kernel(in_ref, *outs):
-    for k, out in enumerate(outs):
-        out[...] = in_ref[k]
+def split_kernel(in_ref, *refs):
+    outs, (buffer, sem_in, sem_out) = refs[:-3], refs[-3:]
+    rows = buffer.shape[1] // 2
+    pieces = [(k, pl.ds(half * rows, rows)) for k in range(len(outs)) for half in range(2)]
+    loads = [
+        pltpu.make_async_copy(in_ref.at[k, part], buffer.at[k, part], sem_in.at[i])
+        for i, (k, part) in enumerate(pieces)
+    ]
+    stores = [
+        pltpu.make_async_copy(buffer.at[k, part], outs[k].at[part], sem_out.at[i])
+        for i, (k, part) in enumerate(pieces)
+    ]
+    for copy in loads:
+        copy.start()
+    for load, store in zip(loads, stores):
+        load.wait()
+        store.start()
+    for copy in stores:
+        copy.wait()
 
 
 def prepare_kernel(first, summed, own_in, sibling_in, own_gain, sibling_gain, *refs):
@@ -577,8 +593,13 @@
             split = pl.pallas_call(
                 split_kernel,
                 out_shape=(jax.ShapeDtypeStruct((features, LANES), bf16),) * len(groups[half]),
-                in_specs=in_vmem(1),
-                out_specs=tuple(in_vmem(len(groups[half]))),
+                in_specs=anywhere(1),
+                out_specs=tuple(anywhere(len(groups[half]))),
+                scratch_shapes=[
+                    pltpu.VMEM(value.shape, bf16),
+                    pltpu.SemaphoreType.DMA((2 * len(groups[half]),)),
+                    pltpu.SemaphoreType.DMA((2 * len(groups[half]),)),
+                ],
                 compiler_params=params(),
             )(value)
             for piece, strip in zip(split, groups[half]):

time: 80.5 us -> 80.7 us (level)
    ppermute x7, waiting for transfers between devices: 6.48 us -> 4.7 us  [to_chip(): return lax.ppermute(value, 'tensor', pairs)]
    ppermute x4, waiting for transfers between devices: 4.22 us -> 5.57 us  [swap_half(): outside[strip].append((piece, lax.ppermute(piece, 'dp', pairs)))]
  transfers between devices with their start and end apart: 17 -> 17, of which waited for: 11 -> 11; matrix products, arithmetic and copies ran while one was open for 0% -> 0% of each run, Pallas kernels for 43% -> 44%
where the time goes in v24:
time: 80.7 us; the launch traced here: 80.2 us
  Pallas kernels  36.2 us (45%)
  starting transfers between devices  26.9 us (33%)
  waiting for transfers between devices  15.6 us (19%)
  between operations  0.88 us (1%)
    pallas_call x2, Pallas kernels, prepared(): pl.pallas_call(functools.partial(prepare_kernel, first, summed), out_shap...  9.96 us
    ppermute x7, starting transfers between devices, to_chip(): return lax.ppermute(value, 'tensor', pairs)  9.07 us
    all_to_all x1, starting transfers between devices, body(): exchanged = lax.all_to_all(packed, 'dp', 0, 0, tiled=True)  6.86 us
    ppermute x4, starting transfers between devices, swap_half(): outside[strip].append((piece, lax.ppermute(piece, 'dp', pairs)))  5.67 us
    ppermute x4, waiting for transfers between devices, swap_half(): outside[strip].append((piece, lax.ppermute(piece, 'dp', pairs)))  5.57 us
    pallas_call x1, Pallas kernels, body(): pl.pallas_call(functools.partial(own_kernel, static), out_shape=(jax.Shap...  4.88 us
    ppermute x7, waiting for transfers between devices, to_chip(): return lax.ppermute(value, 'tensor', pairs)  4.7 us
    all_to_all x1, starting transfers between devices, body(): own_f = lax.all_to_all(sent, 'dp', 0, 0, tiled=True)  4.11 us
  transfers between devices with their start and end apart: 17, of which 11 were waited for; matrix products, arithmetic and copies ran while one was open for 0% of the time, Pallas kernels for 44%

profile of v24, /device:TPU:0, one launch (start us, length us, event | category | flops | bytes accessed | tf_op | source)
XLA Modules:
  0.0 80.2 jit_solution(11675741276634212250)
XLA Ops:
  0.6 0.5 collective-permute-start
  1.2 2.6 %shard_map.130 = (bf16[8,192,128]{2,1,0:T(8,128)(2,1)}, bf16[2,1280,128]{2,1,0:T(8,128)(2,1)}, bf16[2,1280,128]{2,1,0:T(8,128)(2,1)}) custom-call(f32[128,1280]{1,0:T(8,128)} %bitcast.20, f32[64,512]{1,0:T(8,128)} %bitcast.24, bf16[5120,512]{1,0:T(8,128)(2,1)} %sibling_block.1), custom_call_target="tpu_custom_call" | custom-call | tf_op jit(solution)/shard_map/pallas_call | solution.py:502
  3.7 6.9 %all-to-all-start = ((bf16[8,192,128]{2,1,0:T(8,128)(2,1)}), bf16[8,192,128]{2,1,0:T(8,128)(2,1)}, u32[]{:S(2)}, u32[]{:S(2)}) async-start(bf16[8,192,128]{2,1,0:T(8,128)(2,1)} %get-tuple-element.34), calls=%async_computation | async-start | bytes 786432 | tf_op jit(solution)/shard_map/all_to_all | solution.py:517
  10.6 1.5 %collective-permute-start.4 = (bf16[2,1280,128]{2,1,0:T(8,128)(2,1)}, bf16[2,1280,128]{2,1,0:T(8,128)(2,1)}, u32[]{:S(2)}, u32[]{:S(2)}) collective-permute-start(bf16[2,1280,128]{2,1,0:T(8,128)(2,1)} %get-tuple-element.50), channel_id=1, source_target_pairs={{0,2},{1,3},{2,0},{3,1},{4,6},{5,7},{6,4},{7,5},{8,10},{9,11},{10,... | collective-permute-start | bytes 1966088 | tf_op jit(solution)/shard_map/ppermute | solution.py:479
  12.1 0.0 copy-done.6
  12.1 0.1 collective-permute-start.1
  12.2 1.2 %collective-permute-done.1.sibling_gain = f32[1,1280]{1,0:T(1,128)S(1)} collective-permute-done((f32[1,1280]{1,0:T(1,128)S(1)}, f32[1,1280]{1,0:T(1,128)S(1)}, u32[]{:S(2)}, u32[]{:S(2)}) %collective-permute-start.1) | collective-permute-done | bytes 5152 | tf_op jit(solution)/shard_map/ppermute | solution.py:471
  13.3 0.0 collective-permute-done.sibling_in
  13.3 6.2 %shard_map.131 = (bf16[640,2560]{1,0:T(8,128)(2,1)S(1)}, f32[10,128]{1,0:T(8,128)S(1)}) custom-call(bf16[1280,1280]{1,0:T(8,128)(2,1)} %own_in.3, bf16[1280,1280]{1,0:T(8,128)(2,1)} %collective-permute-done.sibling_in, f32[1,1280]{1,0:T(1,128)S(1)} %broadcast_in_dim.3.own_gain, f32[1,1280]{1,0:T(1,128)S(1)} %collective-permute-done.1.sibling_gain), custom_call_target="tpu_custom_call" | custom-call | tf_op jit(solution)/shard_map/pallas_call | solution.py:548
  19.5 0.0 copy-done.4
  19.5 0.0 copy-done.5
  19.5 0.0 copy-start.2
  19.5 0.6 copy-done.2
  20.1 2.9 %all-to-all-done.grad_in = bf16[8,192,128]{2,1,0:T(8,128)(2,1)} async-done(((bf16[8,192,128]{2,1,0:T(8,128)(2,1)}), bf16[8,192,128]{2,1,0:T(8,128)(2,1)}, u32[]{:S(2)}, u32[]{:S(2)}) %all-to-all-start) | async-done | bytes 393248 | tf_op jit(solution)/shard_map/all_to_all | solution.py:517
  23.0 2.6 %shard_map.132 = (f32[3,128,160]{2,1,0:T(8,128)}, f32[3,8,512]{2,1,0:T(8,128)}, bf16[8,192,128]{2,1,0:T(8,128)(2,1)}) custom-call(bf16[8,192,128]{2,1,0:T(8,128)(2,1)} %all-to-all-done.grad_in, f32[128,1280]{1,0:T(8,128)} %bitcast.21, f32[128,1280]{1,0:T(8,128)} %bitcast.22, f32[128,1280]{1,0:T(8,128)} %bitcast.23, f32[64,512]{1,0:T(8,128)} %refs_3_.1, ...), custom_call_target="tpu_custom_call" | custom-call | tf_op jit(solution)/shard_map/pallas_call | solution.py:566
  25.6 4.1 %all-to-all-start.1 = ((bf16[8,192,128]{2,1,0:T(8,128)(2,1)}), bf16[8,192,128]{2,1,0:T(8,128)(2,1)}, u32[]{:S(2)}, u32[]{:S(2)}) async-start(bf16[8,192,128]{2,1,0:T(8,128)(2,1)} %get-tuple-element.39), calls=%async_computation.1 | async-start | bytes 786432 | tf_op jit(solution)/shard_map/all_to_all | solution.py:583
  29.7 0.0 collective-permute-done.4.in_ref
  29.8 1.6 %collective-permute-start.5 = (bf16[2,1280,128]{2,1,0:T(8,128)(2,1)}, bf16[2,1280,128]{2,1,0:T(8,128)(2,1)}, u32[]{:S(2)}, u32[]{:S(2)}) collective-permute-start(bf16[2,1280,128]{2,1,0:T(8,128)(2,1)} %get-tuple-element.51), channel_id=1, source_target_pairs={{0,2},{1,3},{2,0},{3,1},{4,6},{5,7},{6,4},{7,5},{8,10},{9,11},{10,... | collective-permute-start | bytes 1966088 | tf_op jit(solution)/shard_map/ppermute | solution.py:479
  31.3 1.9 %shard_map.135 = (bf16[1280,128]{1,0:T(8,128)(2,1)}, bf16[1280,128]{1,0:T(8,128)(2,1)}) custom-call(bf16[2,1280,128]{2,1,0:T(8,128)(2,1)} %collective-permute-done.4.in_ref), custom_call_target="tpu_custom_call" | custom-call | tf_op jit(solution)/shard_map/pallas_call | solution.py:593
  33.2 1.9 %collective-permute-start.6 = (bf16[1280,128]{1,0:T(8,128)(2,1)}, bf16[1280,128]{1,0:T(8,128)(2,1)}, u32[]{:S(2)}, u32[]{:S(2)}) collective-permute-start(bf16[1280,128]{1,0:T(8,128)(2,1)} %get-tuple-element.53.refs_0_), channel_id=1, source_target_pairs={{0,4},{4,0},{8,12},{12,8},{16,20},{20,16},{24,28},{28,24},{1,5},{5... | collective-permute-start | bytes 983048 | tf_op jit(solution)/shard_map/ppermute | solution.py:607
  35.1 1.5 %collective-permute-start.7 = (bf16[1280,128]{1,0:T(8,128)(2,1)}, bf16[1280,128]{1,0:T(8,128)(2,1)}, u32[]{:S(2)}, u32[]{:S(2)}) collective-permute-start(bf16[1280,128]{1,0:T(8,128)(2,1)} %get-tuple-element.54.refs_2_), channel_id=1, source_target_pairs={{0,8},{4,12},{8,0},{12,4},{16,24},{20,28},{24,16},{28,20},{1,9},{5... | collective-permute-start | bytes 983048 | tf_op jit(solution)/shard_map/ppermute | solution.py:607
  36.6 3.8 %shard_map.133 = (bf16[640,1280]{1,0:T(8,128)(2,1)}, bf16[640,1280]{1,0:T(8,128)(2,1)}) custom-call(bf16[1280,1280]{1,0:T(8,128)(2,1)} %own_in.3, bf16[1280,1280]{1,0:T(8,128)(2,1)} %collective-permute-done.sibling_in, f32[1,1280]{1,0:T(1,128)} %copy-done.4, f32[1,1280]{1,0:T(1,128)} %copy-done.5, f32[10,128]{1,0:T(8,128)} %copy-done.2), custom_call_target="tpu_custom_call" | custom-call | tf_op jit(solution)/shard_map/pallas_call | solution.py:548
  40.4 1.3 %all-to-all-done.1.factor_ref = bf16[8,192,128]{2,1,0:T(8,128)(2,1)} async-done(((bf16[8,192,128]{2,1,0:T(8,128)(2,1)}), bf16[8,192,128]{2,1,0:T(8,128)(2,1)}, u32[]{:S(2)}, u32[]{:S(2)}) %all-to-all-start.1) | async-done | bytes 393248 | tf_op jit(solution)/shard_map/all_to_all | solution.py:583
  41.7 0.0 copy-done.3
  41.7 1.1 %shard_map.134 = (bf16[9,32,128]{2,1,0:T(8,128)(2,1)S(1)}, bf16[4,192,128]{2,1,0:T(8,128)(2,1)S(1)}, bf16[4,192,128]{2,1,0:T(8,128)(2,1)S(1)}) custom-call(bf16[8,192,128]{2,1,0:T(8,128)(2,1)} %all-to-all-done.1.factor_ref, f32[10,128]{1,0:T(8,128)S(1)} %copy-done.3), custom_call_target="tpu_custom_call" | custom-call | tf_op jit(solution)/shard_map/pallas_call | solution.py:614
  42.8 0.1 collective-permute-start.2
  42.8 0.5 collective-permute-start.3
  43.3 0.7 collective-permute-done.6.refs_1_
  44.1 1.5 %collective-permute-start.8 = (bf16[9,32,128]{2,1,0:T(8,128)(2,1)S(1)}, bf16[9,32,128]{2,1,0:T(8,128)(2,1)S(1)}, u32[]{:S(2)}, u32[]{:S(2)}) collective-permute-start(bf16[9,32,128]{2,1,0:T(8,128)(2,1)S(1)} %get-tuple-element.55), channel_id=1, source_target_pairs={{0,2},{1,3},{2,0},{3,1},{4,6},{5,7},{6,4},{7,5},{8,10},{9,11},{10,... | collective-permute-start | bytes 221192 | tf_op jit(solution)/shard_map/ppermute | solution.py:479
  45.6 0.2 collective-permute-done.7.refs_3_
  45.8 1.6 %shard_map.136.blocks = bf16[2560,256]{1,0:T(8,128)(2,1)S(1)} custom-call(bf16[1280,128]{1,0:T(8,128)(2,1)} %get-tuple-element.53.refs_0_, bf16[1280,128]{1,0:T(8,128)(2,1)} %collective-permute-done.6.refs_1_, bf16[1280,128]{1,0:T(8,128)(2,1)} %get-tuple-element.54.refs_2_, bf16[1280,128]{1,0:T(8,128)(2,1)} %collective-permute-done.7.refs_3_), custom_call_target="tpu_custom_call" | custom-call | tf_op jit(solution)/shard_map/pallas_call | solution.py:649
  47.4 1.0 %collective-permute-done.8.b_ref.refs_0_ = bf16[9,32,128]{2,1,0:T(8,128)(2,1)S(1)} collective-permute-done((bf16[9,32,128]{2,1,0:T(8,128)(2,1)S(1)}, bf16[9,32,128]{2,1,0:T(8,128)(2,1)S(1)}, u32[]{:S(2)}, u32[]{:S(2)}) %collective-permute-start.8) | collective-permute-done | bytes 73760 | tf_op jit(solution)/shard_map/ppermute | solution.py:479
  48.4 0.0 collective-permute-done.2.refs_2_
  48.4 0.0 collective-permute-done.3.refs_3_
  48.4 0.0 copy-start.1
  48.4 1.7 %shard_map.137 = (bf16[2560,256]{1,0:T(8,128)(2,1)S(1)}, bf16[640,256]{1,0:T(8,128)(2,1)S(1)}) custom-call(bf16[2560,256]{1,0:T(8,128)(2,1)S(1)} %shard_map.136.blocks, bf16[9,32,128]{2,1,0:T(8,128)(2,1)S(1)} %collective-permute-done.8.b_ref.refs_0_, bf16[640,2560]{1,0:T(8,128)(2,1)S(1)} %get-tuple-element.46.x.refs_4_, ...), custom_call_target="tpu_custom_call" | custom-call | tf_op jit(solution)/shard_map/pallas_call | solution.py:656
  50.2 1.6 %collective-permute-start.11 = (bf16[640,256]{1,0:T(8,128)(2,1)S(1)}, bf16[640,256]{1,0:T(8,128)(2,1)S(1)}, u32[]{:S(2)}, u32[]{:S(2)}) collective-permute-start(bf16[640,256]{1,0:T(8,128)(2,1)S(1)} %get-tuple-element.56), channel_id=1, source_target_pairs={{0,2},{1,3},{2,0},{3,1},{4,6},{5,7},{6,4},{7,5},{8,10},{9,11},{10,... | collective-permute-start | bytes 983048 | tf_op jit(solution)/shard_map/ppermute | solution.py:479
  51.7 0.0 collective-permute-done.5.in_ref
  51.7 1.8 %shard_map.138 = (bf16[1280,128]{1,0:T(8,128)(2,1)S(1)}, bf16[1280,128]{1,0:T(8,128)(2,1)S(1)}) custom-call(bf16[2,1280,128]{2,1,0:T(8,128)(2,1)} %collective-permute-done.5.in_ref), custom_call_target="tpu_custom_call" | custom-call | tf_op jit(solution)/shard_map/pallas_call | solution.py:593
  53.5 0.8 %collective-permute-start.9 = (bf16[1280,128]{1,0:T(8,128)(2,1)S(1)}, bf16[1280,128]{1,0:T(8,128)(2,1)S(1)}, u32[]{:S(2)}, u32[]{:S(2)}) collective-permute-start(bf16[1280,128]{1,0:T(8,128)(2,1)S(1)} %get-tuple-element.58.refs_0_), channel_id=1, source_target_pairs={{0,4},{4,0},{8,12},{12,8},{16,20},{20,16},{24,28},{28,24},{1,5},{5... | collective-permute-start | bytes 983048 | tf_op jit(solution)/shard_map/ppermute | solution.py:607
  54.4 1.5 %collective-permute-start.10 = (bf16[1280,128]{1,0:T(8,128)(2,1)S(1)}, bf16[1280,128]{1,0:T(8,128)(2,1)S(1)}, u32[]{:S(2)}, u32[]{:S(2)}) collective-permute-start(bf16[1280,128]{1,0:T(8,128)(2,1)S(1)} %get-tuple-element.59.refs_2_), channel_id=1, source_target_pairs={{0,8},{4,12},{8,0},{12,4},{16,24},{20,28},{24,16},{28,20},{1,9},{5... | collective-permute-start | bytes 983048 | tf_op jit(solution)/shard_map/ppermute | solution.py:607
  55.8 0.0 copy-done
  55.8 0.0 copy-done.1
  55.8 1.2 %shard_map.142 = bf16[640,256]{1,0:T(8,128)(2,1)S(1)} custom-call(bf16[640,1280]{1,0:T(8,128)(2,1)S(1)} %copy-done, bf16[640,1280]{1,0:T(8,128)(2,1)S(1)} %copy-done.1, bf16[2560,256]{1,0:T(8,128)(2,1)S(1)} %get-tuple-element.61.refs_2_), custom_call_target="tpu_custom_call" | custom-call | tf_op jit(solution)/shard_map/pallas_call | solution.py:664
  57.0 0.8 %collective-permute-start.12 = (bf16[640,256]{1,0:T(8,128)(2,1)S(1)}, bf16[640,256]{1,0:T(8,128)(2,1)S(1)}, u32[]{:S(2)}, u32[]{:S(2)}) collective-permute-start(bf16[640,256]{1,0:T(8,128)(2,1)S(1)} %shard_map.142), channel_id=1, source_target_pairs={{0,2},{1,3},{2,0},{3,1},{4,6},{5,7},{6,4},{7,5},{8,10},{9,11},{10,... | collective-permute-start | bytes 983048 | tf_op jit(solution)/shard_map/ppermute | solution.py:479
  57.8 0.3 collective-permute-done.11.refs_4_.refs_0_
  58.1 3.2 %collective-permute-done.9.refs_1_ = bf16[1280,128]{1,0:T(8,128)(2,1)S(1)} collective-permute-done((bf16[1280,128]{1,0:T(8,128)(2,1)S(1)}, bf16[1280,128]{1,0:T(8,128)(2,1)S(1)}, u32[]{:S(2)}, u32[]{:S(2)}) %collective-permute-start.9) | collective-permute-done | bytes 327712 | tf_op jit(solution)/shard_map/ppermute | solution.py:607
  61.3 1.5 %collective-permute-done.10.refs_3_ = bf16[1280,128]{1,0:T(8,128)(2,1)S(1)} collective-permute-done((bf16[1280,128]{1,0:T(8,128)(2,1)S(1)}, bf16[1280,128]{1,0:T(8,128)(2,1)S(1)}, u32[]{:S(2)}, u32[]{:S(2)}) %collective-permute-start.10) | collective-permute-done | bytes 327712 | tf_op jit(solution)/shard_map/ppermute | solution.py:607
  62.7 0.3 shard_map.139.blocks
  63.1 0.0 slice-start.1
  63.1 1.7 %shard_map.140 = (bf16[2560,256]{1,0:T(8,128)(2,1)S(1)}, bf16[640,256]{1,0:T(8,128)(2,1)S(1)}) custom-call(bf16[2560,256]{1,0:T(8,128)(2,1)S(1)} %shard_map.139.blocks, bf16[9,32,128]{2,1,0:T(8,128)(2,1)S(1)} %collective-permute-done.8.b_ref.refs_0_, bf16[640,2560]{1,0:T(8,128)(2,1)S(1)} %get-tuple-element.46.x.refs_4_, ...), custom_call_target="tpu_custom_call" | custom-call | tf_op jit(solution)/shard_map/pallas_call | solution.py:656
  64.8 0.6 collective-permute-start.14
  65.4 1.2 %shard_map.141.refs_7_ = bf16[640,256]{1,0:T(8,128)(2,1)S(1)} custom-call(bf16[640,1280]{1,0:T(8,128)(2,1)S(1)} %copy-done, bf16[640,1280]{1,0:T(8,128)(2,1)S(1)} %copy-done.1, bf16[2560,256]{1,0:T(8,128)(2,1)S(1)} %get-tuple-element.60.refs_2_), custom_call_target="tpu_custom_call" | custom-call | tf_op jit(solution)/shard_map/pallas_call | solution.py:664
  66.6 1.6 %collective-permute-start.13 = (bf16[640,256]{1,0:T(8,128)(2,1)S(1)}, bf16[640,256]{1,0:T(8,128)(2,1)S(1)}, u32[]{:S(2)}, u32[]{:S(2)}) collective-permute-start(bf16[640,256]{1,0:T(8,128)(2,1)S(1)} %shard_map.141.refs_7_), channel_id=1, source_target_pairs={{0,2},{1,3},{2,0},{3,1},{4,6},{5,7},{6,4},{7,5},{8,10},{9,11},{10,... | collective-permute-start | bytes 983048 | tf_op jit(solution)/shard_map/ppermute | solution.py:479
  68.2 0.2 shard_map.144.inv
  68.4 0.0 collective-permute-done.12.refs_8_.refs_0_
  68.4 0.0 slice-done
  68.4 4.9 %shard_map.143 = (f32[1280,256]{1,0:T(8,128)S(1)}, f32[1280,256]{1,0:T(8,128)S(1)}) custom-call(bf16[5120,512]{1,0:T(8,128)(2,1)S(1)} %bitcast.19, bf16[5120,512]{1,0:T(8,128)(2,1)S(1)} %bitcast.19, bf16[4,192,128]{2,1,0:T(8,128)(2,1)S(1)} %get-tuple-element.44.refs_0_, bf16[4,192,128]{2,1,0:T(8,128)(2,1)S(1)} %get-tuple-element.45.refs_1_, ...), custom_call_target="tpu_custom_call" | custom-call | flops 3355443200 | bytes 6553600 | tf_op jit(solution)/shard_map/pallas_call | solution.py:679
  73.3 0.9 %shard_map.145.refs_1_ = bf16[1280,512]{1,0:T(8,128)(2,1)} custom-call(f32[1280,256]{1,0:T(8,128)S(1)} %get-tuple-element.64.own, f32[1280,128]{1,0:T(8,128)S(1)} %shard_map.144.inv, bf16[640,256]{1,0:T(8,128)(2,1)S(1)} %collective-permute-done.11.refs_4_.refs_0_), custom_call_target="tpu_custom_call" | custom-call | tf_op jit(solution)/shard_map/pallas_call | solution.py:430
  74.2 0.9 %shard_map.146.refs_1_ = bf16[1280,512]{1,0:T(8,128)(2,1)} custom-call(f32[1280,256]{1,0:T(8,128)S(1)} %get-tuple-element.64.own, f32[1280,128]{1,0:T(8,128)S(1)} %shard_map.144.inv, bf16[640,256]{1,0:T(8,128)(2,1)S(1)} %collective-permute-done.12.refs_8_.refs_0_, bf16[1280,512]{1,0:T(8,128)(2,1)} %shard_map.145.refs_1_), custom_call_target="tpu_custom_call", output_to_operand_aliasing={{}: (3, {})} | custom-call | tf_op jit(solution)/shard_map/pallas_call | solution.py:430
  75.1 0.4 collective-permute-done.14.refs_0_
  75.5 0.9 %shard_map.147.refs_1_ = bf16[1280,512]{1,0:T(8,128)(2,1)} custom-call(f32[1280,256]{1,0:T(8,128)S(1)} %get-tuple-element.62.own, f32[1280,128]{1,0:T(8,128)S(1)} %shard_map.144.inv, bf16[640,256]{1,0:T(8,128)(2,1)S(1)} %collective-permute-done.14.refs_0_, bf16[1280,512]{1,0:T(8,128)(2,1)} %shard_map.146.refs_1_), custom_call_target="tpu_custom_call", output_to_operand_aliasing={{}: (3, {})} | custom-call | tf_op jit(solution)/shard_map/pallas_call | solution.py:430
  76.4 3.0 %collective-permute-done.13.refs_0_ = bf16[640,256]{1,0:T(8,128)(2,1)S(1)} collective-permute-done((bf16[640,256]{1,0:T(8,128)(2,1)S(1)}, bf16[640,256]{1,0:T(8,128)(2,1)S(1)}, u32[]{:S(2)}, u32[]{:S(2)}) %collective-permute-start.13) | collective-permute-done | bytes 327712 | tf_op jit(solution)/shard_map/ppermute | solution.py:479
  79.4 0.9 %shard_map.148 = bf16[1280,512]{1,0:T(8,128)(2,1)} custom-call(f32[1280,256]{1,0:T(8,128)S(1)} %get-tuple-element.62.own, f32[1280,128]{1,0:T(8,128)S(1)} %shard_map.144.inv, bf16[640,256]{1,0:T(8,128)(2,1)S(1)} %collective-permute-done.13.refs_0_, bf16[1280,512]{1,0:T(8,128)(2,1)} %shard_map.147.refs_1_), custom_call_target="tpu_custom_call", output_to_operand_aliasing={{}: (3, {})} | custom-call | tf_op jit(solution)/shard_map/pallas_call | solution.py:430
  (9 shorter events, 0.0 us)
Async XLA Ops:
  0.6 12.7 %collective-permute-start = (bf16[1280,1280]{1,0:T(8,128)(2,1)}, bf16[1280,1280]{1,0:T(8,128)(2,1)}, u32[]{:S(2)}, u32[]{:S(2)}) collective-permute-start(bf16[1280,1280]{1,0:T(8,128)(2,1)} %own_in.3), channel_id=1, source_target_pairs={{0,1},{1,0},{2,3},{3,2},{4,5},{5,4},{6,7},{7,6},{8,9},{9,8},{10,11... | collective-permute-start | bytes 9830408 | tf_op jit(solution)/shard_map/ppermute | solution.py:471
  1.1 10.9 %copy-start.6 = (f32[1280]{0:T(1024)S(1)}, f32[1280]{0:T(1024)}, u32[]{:S(2)}) copy-start(f32[1280]{0:T(1024)} %param.12) | copy-start | bytes 15364
  3.7 19.3 %all-to-all-start = ((bf16[8,192,128]{2,1,0:T(8,128)(2,1)}), bf16[8,192,128]{2,1,0:T(8,128)(2,1)}, u32[]{:S(2)}, u32[]{:S(2)}) async-start(bf16[8,192,128]{2,1,0:T(8,128)(2,1)} %get-tuple-element.34), calls=%async_computation | async-start | bytes 786432 | tf_op jit(solution)/shard_map/all_to_all | solution.py:517
  10.6 19.1 %collective-permute-start.4 = (bf16[2,1280,128]{2,1,0:T(8,128)(2,1)}, bf16[2,1280,128]{2,1,0:T(8,128)(2,1)}, u32[]{:S(2)}, u32[]{:S(2)}) collective-permute-start(bf16[2,1280,128]{2,1,0:T(8,128)(2,1)} %get-tuple-element.50), channel_id=1, source_target_pairs={{0,2},{1,3},{2,0},{3,1},{4,6},{5,7},{6,4},{7,5},{8,10},{9,11},{10,... | collective-permute-start | bytes 1966088 | tf_op jit(solution)/shard_map/ppermute | solution.py:479
  12.1 7.4 %copy-start.4 = (f32[1,1280]{1,0:T(1,128)}, f32[1,1280]{1,0:T(1,128)S(1)}, u32[]{:S(2)}) copy-start(f32[1,1280]{1,0:T(1,128)S(1)} %broadcast_in_dim.3.own_gain) | copy-start | bytes 15364
  12.1 1.2 %collective-permute-start.1 = (f32[1,1280]{1,0:T(1,128)S(1)}, f32[1,1280]{1,0:T(1,128)S(1)}, u32[]{:S(2)}, u32[]{:S(2)}) collective-permute-start(f32[1,1280]{1,0:T(1,128)S(1)} %broadcast_in_dim.3.own_gain), channel_id=1, source_target_pairs={{0,1},{1,0},{2,3},{3,2},{4,5},{5,4},{6,7},{7,6},{8,9},{9,8},{10,11... | collective-permute-start | bytes 15368 | tf_op jit(solution)/shard_map/ppermute | solution.py:471
  13.3 6.2 %copy-start.5 = (f32[1,1280]{1,0:T(1,128)}, f32[1,1280]{1,0:T(1,128)S(1)}, u32[]{:S(2)}) copy-start(f32[1,1280]{1,0:T(1,128)S(1)} %collective-permute-done.1.sibling_gain) | copy-start | bytes 15364
  19.5 0.6 copy-start.2
  25.6 16.0 %all-to-all-start.1 = ((bf16[8,192,128]{2,1,0:T(8,128)(2,1)}), bf16[8,192,128]{2,1,0:T(8,128)(2,1)}, u32[]{:S(2)}, u32[]{:S(2)}) async-start(bf16[8,192,128]{2,1,0:T(8,128)(2,1)} %get-tuple-element.39), calls=%async_computation.1 | async-start | bytes 786432 | tf_op jit(solution)/shard_map/all_to_all | solution.py:583
  29.8 22.0 %collective-permute-start.5 = (bf16[2,1280,128]{2,1,0:T(8,128)(2,1)}, bf16[2,1280,128]{2,1,0:T(8,128)(2,1)}, u32[]{:S(2)}, u32[]{:S(2)}) collective-permute-start(bf16[2,1280,128]{2,1,0:T(8,128)(2,1)} %get-tuple-element.51), channel_id=1, source_target_pairs={{0,2},{1,3},{2,0},{3,1},{4,6},{5,7},{6,4},{7,5},{8,10},{9,11},{10,... | collective-permute-start | bytes 1966088 | tf_op jit(solution)/shard_map/ppermute | solution.py:479
  33.2 10.9 %collective-permute-start.6 = (bf16[1280,128]{1,0:T(8,128)(2,1)}, bf16[1280,128]{1,0:T(8,128)(2,1)}, u32[]{:S(2)}, u32[]{:S(2)}) collective-permute-start(bf16[1280,128]{1,0:T(8,128)(2,1)} %get-tuple-element.53.refs_0_), channel_id=1, source_target_pairs={{0,4},{4,0},{8,12},{12,8},{16,20},{20,16},{24,28},{28,24},{1,5},{5... | collective-permute-start | bytes 983048 | tf_op jit(solution)/shard_map/ppermute | solution.py:607
  35.1 6.6 %copy-start.3 = (f32[10,128]{1,0:T(8,128)S(1)}, f32[10,128]{1,0:T(8,128)}, u32[]{:S(2)}) copy-start(f32[10,128]{1,0:T(8,128)} %copy-done.2) | copy-start | bytes 15364
  35.1 10.7 %collective-permute-start.7 = (bf16[1280,128]{1,0:T(8,128)(2,1)}, bf16[1280,128]{1,0:T(8,128)(2,1)}, u32[]{:S(2)}, u32[]{:S(2)}) collective-permute-start(bf16[1280,128]{1,0:T(8,128)(2,1)} %get-tuple-element.54.refs_2_), channel_id=1, source_target_pairs={{0,8},{4,12},{8,0},{12,4},{16,24},{20,28},{24,16},{28,20},{1,9},{5... | collective-permute-start | bytes 983048 | tf_op jit(solution)/shard_map/ppermute | solution.py:607
  42.8 5.7 %collective-permute-start.2 = (bf16[4,192,128]{2,1,0:T(8,128)(2,1)S(1)}, bf16[4,192,128]{2,1,0:T(8,128)(2,1)S(1)}, u32[]{:S(2)}, u32[]{:S(2)}) collective-permute-start(bf16[4,192,128]{2,1,0:T(8,128)(2,1)S(1)} %get-tuple-element.44.refs_0_), channel_id=1, source_target_pairs={{0,1},{1,0},{2,3},{3,2},{4,5},{5,4},{6,7},{7,6},{8,9},{9,8},{10,11... | collective-permute-start | bytes 589832 | tf_op jit(solution)/shard_map/ppermute | solution.py:471
  42.8 5.6 %collective-permute-start.3 = (bf16[4,192,128]{2,1,0:T(8,128)(2,1)S(1)}, bf16[4,192,128]{2,1,0:T(8,128)(2,1)S(1)}, u32[]{:S(2)}, u32[]{:S(2)}) collective-permute-start(bf16[4,192,128]{2,1,0:T(8,128)(2,1)S(1)} %get-tuple-element.45.refs_1_), channel_id=1, source_target_pairs={{0,1},{1,0},{2,3},{3,2},{4,5},{5,4},{6,7},{7,6},{8,9},{9,8},{10,11... | collective-permute-start | bytes 589832 | tf_op jit(solution)/shard_map/ppermute | solution.py:471
  44.1 4.4 %collective-permute-start.8 = (bf16[9,32,128]{2,1,0:T(8,128)(2,1)S(1)}, bf16[9,32,128]{2,1,0:T(8,128)(2,1)S(1)}, u32[]{:S(2)}, u32[]{:S(2)}) collective-permute-start(bf16[9,32,128]{2,1,0:T(8,128)(2,1)S(1)} %get-tuple-element.55), channel_id=1, source_target_pairs={{0,2},{1,3},{2,0},{3,1},{4,6},{5,7},{6,4},{7,5},{8,10},{9,11},{10,... | collective-permute-start | bytes 221192 | tf_op jit(solution)/shard_map/ppermute | solution.py:479
  48.4 7.4 %copy-start = (bf16[640,1280]{1,0:T(8,128)(2,1)S(1)}, bf16[640,1280]{1,0:T(8,128)(2,1)}, u32[]{:S(2)}) copy-start(bf16[640,1280]{1,0:T(8,128)(2,1)} %get-tuple-element.47.refs_0_.refs_5_) | copy-start | bytes 4915204
  48.4 7.4 %copy-start.1 = (bf16[640,1280]{1,0:T(8,128)(2,1)S(1)}, bf16[640,1280]{1,0:T(8,128)(2,1)}, u32[]{:S(2)}) copy-start(bf16[640,1280]{1,0:T(8,128)(2,1)} %get-tuple-element.48.refs_1_.refs_6_) | copy-start | bytes 4915204
  50.2 8.0 %collective-permute-start.11 = (bf16[640,256]{1,0:T(8,128)(2,1)S(1)}, bf16[640,256]{1,0:T(8,128)(2,1)S(1)}, u32[]{:S(2)}, u32[]{:S(2)}) collective-permute-start(bf16[640,256]{1,0:T(8,128)(2,1)S(1)} %get-tuple-element.56), channel_id=1, source_target_pairs={{0,2},{1,3},{2,0},{3,1},{4,6},{5,7},{6,4},{7,5},{8,10},{9,11},{10,... | collective-permute-start | bytes 983048 | tf_op jit(solution)/shard_map/ppermute | solution.py:479
  53.5 7.8 %collective-permute-start.9 = (bf16[1280,128]{1,0:T(8,128)(2,1)S(1)}, bf16[1280,128]{1,0:T(8,128)(2,1)S(1)}, u32[]{:S(2)}, u32[]{:S(2)}) collective-permute-start(bf16[1280,128]{1,0:T(8,128)(2,1)S(1)} %get-tuple-element.58.refs_0_), channel_id=1, source_target_pairs={{0,4},{4,0},{8,12},{12,8},{16,20},{20,16},{24,28},{28,24},{1,5},{5... | collective-permute-start | bytes 983048 | tf_op jit(solution)/shard_map/ppermute | solution.py:607
  54.4 8.4 %collective-permute-start.10 = (bf16[1280,128]{1,0:T(8,128)(2,1)S(1)}, bf16[1280,128]{1,0:T(8,128)(2,1)S(1)}, u32[]{:S(2)}, u32[]{:S(2)}) collective-permute-start(bf16[1280,128]{1,0:T(8,128)(2,1)S(1)} %get-tuple-element.59.refs_2_), channel_id=1, source_target_pairs={{0,8},{4,12},{8,0},{12,4},{16,24},{20,28},{24,16},{28,20},{1,9},{5... | collective-permute-start | bytes 983048 | tf_op jit(solution)/shard_map/ppermute | solution.py:607
  57.0 11.4 %collective-permute-start.12 = (bf16[640,256]{1,0:T(8,128)(2,1)S(1)}, bf16[640,256]{1,0:T(8,128)(2,1)S(1)}, u32[]{:S(2)}, u32[]{:S(2)}) collective-permute-start(bf16[640,256]{1,0:T(8,128)(2,1)S(1)} %shard_map.142), channel_id=1, source_target_pairs={{0,2},{1,3},{2,0},{3,1},{4,6},{5,7},{6,4},{7,5},{8,10},{9,11},{10,... | collective-permute-start | bytes 983048 | tf_op jit(solution)/shard_map/ppermute | solution.py:479
  62.7 5.7 %slice-start = ((s8[5242880]{0:T(1024)(128)(4,1)}), s8[4194304]{0:T(1024)(128)(4,1)S(1)}, s32[]{:S(2)}) async-start(s8[5242880]{0:T(1024)(128)(4,1)} %bitcast.18), calls=%async_computation.2 | async-start | bytes 8388608
  63.1 5.3 %slice-start.1 = ((s8[5242880]{0:T(1024)(128)(4,1)}), s8[1048576]{0:T(1024)(128)(4,1)S(1)}, s32[]{:S(2)}) async-start(s8[5242880]{0:T(1024)(128)(4,1)} %bitcast.18), calls=%async_computation.3 | async-start | bytes 2097152
  64.8 10.7 %collective-permute-start.14 = (bf16[640,256]{1,0:T(8,128)(2,1)S(1)}, bf16[640,256]{1,0:T(8,128)(2,1)S(1)}, u32[]{:S(2)}, u32[]{:S(2)}) collective-permute-start(bf16[640,256]{1,0:T(8,128)(2,1)S(1)} %get-tuple-element.63), channel_id=1, source_target_pairs={{0,2},{1,3},{2,0},{3,1},{4,6},{5,7},{6,4},{7,5},{8,10},{9,11},{10,... | collective-permute-start | bytes 983048 | tf_op jit(solution)/shard_map/ppermute | solution.py:479
  66.6 12.8 %collective-permute-start.13 = (bf16[640,256]{1,0:T(8,128)(2,1)S(1)}, bf16[640,256]{1,0:T(8,128)(2,1)S(1)}, u32[]{:S(2)}, u32[]{:S(2)}) collective-permute-start(bf16[640,256]{1,0:T(8,128)(2,1)S(1)} %shard_map.141.refs_7_), channel_id=1, source_target_pairs={{0,2},{1,3},{2,0},{3,1},{4,6},{5,7},{6,4},{7,5},{8,10},{9,11},{10,... | collective-permute-start | bytes 983048 | tf_op jit(solution)/shard_map/ppermute | solution.py:479

commit v25 on v24

--- a/solution.py
+++ b/solution.py
@@ -58,49 +58,50 @@
     return jnp.minimum(share // LANES * LANES, size - window)
 
 
-def begin_kernel(chips, turn, down_ref, up_ref, weights_ref, packed, *refs):
-    outs, (down, up, blocks, strips, sem, sem_out) = refs[:-6], refs[-6:]
+def pack_kernel(down_ref, up_ref, packed, down, up, blocks, sem, sem_out):
+    loads = [
+        pltpu.make_async_copy(down_ref, down, sem.at[0]),
+        pltpu.make_async_copy(up_ref, up, sem.at[1]),
+    ]
+    back = []
+    for copy in loads:
+        copy.start()
+    for copy in loads:
+        copy.wait()
+
+    def ready(i):
+        back.append(pltpu.make_async_copy(blocks.at[i], packed.at[i], sem_out.at[i]))
+        back[-1].start()
+
+    pack(down[...], up[...], blocks, ready)
+    for copy in back:
+        copy.wait()
+
+
+def take_kernel(chips, turn, weights_ref, _, *refs):
+    outs, (strips, sem, sem_out) = refs[:-3], refs[-3:]
     features = strips.shape[1]
     place, replica = lax.axis_index("tensor"), lax.axis_index("dp")
     chip, core = place // CORES, place % CORES
-    copies, back = [], []
-
-    def add(source, target):
-        copies.append(pltpu.make_async_copy(source, target, sem.at[len(copies)]))
-        copies[-1].start()
-
-    def add_back(source, target):
-        back.append(pltpu.make_async_copy(source, target, sem_out.at[len(back)]))
-        back[-1].start()
-
-    add(down_ref, down)
-    add(up_ref, up)
-    targets = []
+    loads, stores = [], []
     for i, out in enumerate(outs):
         step, first = 1 + i % (chips - 1), i // (chips - 1) * out.shape[0]
         for k in range(out.shape[0]):
             half = (core + replica // turn[first + k]) % 2
             row = ((chip + step) % chips * CORES + half) * features
-            add(
-                weights_ref.at[
-                    pl.ds(pl.multiple_of(row, features), features),
-                    pl.ds((first + k) * LANES, LANES),
-                ],
-                strips.at[len(targets)],
-            )
-            targets.append(out.at[k])
-    copies[0].wait()
-    copies[1].wait()
-
-    def ready(i):
-        add_back(blocks.at[i], packed.at[i])
-        if i == min(1, blocks.shape[0] - 1):
-            for k, target in enumerate(targets):
-                copies[2 + k].wait()
-                add_back(strips.at[k], target)
-
-    pack(down[...], up[...], blocks, ready)
-    for copy in back:
+            source = weights_ref.at[
+                pl.ds(pl.multiple_of(row, features), features),
+                pl.ds((first + k) * LANES, LANES),
+            ]
+            at = len(loads)
+            loads.append(pltpu.make_async_copy(source, strips.at[at], sem.at[at]))
+            stores.append(pltpu.make_async_copy(strips.at[at], out.at[k], sem_out.at[at]))
+    for copy in loads:
+        copy.start()
+    for load, store in zip(loads, stores):
+        load.wait()
+        store.start()
+    for copy in stores:
         copy.wait()
 
 
@@ -494,26 +495,37 @@
     halves = min(COLUMN_HALVES, strips)
     wide = columns // halves
     groups = [range(k * strips // halves, (k + 1) * strips // halves) for k in range(halves)]
-    out_shape = (shares,) + tuple(
+    packed = pl.pallas_call(
+        pack_kernel,
+        out_shape=shares,
+        in_specs=anywhere(2),
+        out_specs=anywhere(1)[0],
+        scratch_shapes=[
+            pltpu.VMEM((factors, features), f32),
+            pltpu.VMEM((rank, columns), f32),
+            pltpu.VMEM(shares.shape, bf16),
+            pltpu.SemaphoreType.DMA((2,)),
+            pltpu.SemaphoreType.DMA((n_dp,)),
+        ],
+        compiler_params=pltpu.CompilerParams(vmem_limit_bytes=LARGE_VMEM_BYTES),
+    )(down_sent, up_gradient[0])
+    out_shape = tuple(
         jax.ShapeDtypeStruct((len(group), features, LANES), bf16)
         for group in groups
         for _ in steps
     )
-    packed, *taken = pl.pallas_call(
-        functools.partial(begin_kernel, chips, turn),
+    taken = pl.pallas_call(
+        functools.partial(take_kernel, chips, turn),
         out_shape=out_shape,
-        in_specs=anywhere(3),
+        in_specs=anywhere(2),
         out_specs=tuple(anywhere(len(out_shape))),
         scratch_shapes=[
-            pltpu.VMEM((factors, features), f32),
-            pltpu.VMEM((rank, columns), f32),
-            pltpu.VMEM(shares.shape, bf16),
             pltpu.VMEM((len(steps) * strips, features, LANES), bf16),
-            pltpu.SemaphoreType.DMA((2 + len(steps) * strips,)),
-            pltpu.SemaphoreType.DMA((n_dp + len(steps) * strips,)),
+            pltpu.SemaphoreType.DMA((len(steps) * strips,)),
+            pltpu.SemaphoreType.DMA((len(steps) * strips,)),
         ],
         compiler_params=pltpu.CompilerParams(vmem_limit_bytes=LARGE_VMEM_BYTES),
-    )(down_sent, up_gradient[0], frozen_key_value)
+    )(frozen_key_value, packed)
     exchanged = lax.all_to_all(packed, "dp", 0, 0, tiled=True)
     if not aligned:
         down_state = [

time: 80.7 us -> 81.9 us (1.015)
  Pallas kernels: 36.2 us -> 37.8 us
    all_to_all x1, waiting for transfers between devices: 2.92 us -> 0.73 us  [body(): exchanged = lax.all_to_all(packed, 'dp', 0, 0, tiled=True)]
    ppermute x7, waiting for transfers between devices: 4.7 us -> 6.88 us  [to_chip(): return lax.ppermute(value, 'tensor', pairs)]
    pallas_call x1 -> x2, Pallas kernels: 2.58 us -> 4.13 us  [the longest x1 2.11 us: body(): pl.pallas_call(functools.partial(take_kernel, chips, turn), out_shape=out...]
    ppermute x4, waiting for transfers between devices: 5.57 us -> 4.15 us  [swap_half(): outside[strip].append((piece, lax.ppermute(piece, 'dp', pairs)))]
    ppermute x7, starting transfers between devices: 9.07 us -> 7.7 us  [to_chip(): return lax.ppermute(value, 'tensor', pairs)]
    all_to_all x1, starting transfers between devices: 4.11 us -> 5.27 us  [body(): own_f = lax.all_to_all(sent, 'dp', 0, 0, tiled=True)]
    all_to_all x1, waiting for transfers between devices: 1.28 us -> 2.33 us  [body(): own_f = lax.all_to_all(sent, 'dp', 0, 0, tiled=True)]
  transfers between devices with their start and end apart: 17 -> 17, of which waited for: 11 -> 11; matrix products, arithmetic and copies ran while one was open for 0% -> 0% of each run, Pallas kernels for 44% -> 45%
where the time goes in v25:
time: 81.9 us; the launch traced here: 81.3 us
  Pallas kernels  37.8 us (46%)
  starting transfers between devices  26.8 us (33%)
  waiting for transfers between devices  15.3 us (19%)
  between operations  0.88 us (1%)
    pallas_call x2, Pallas kernels, prepared(): pl.pallas_call(functools.partial(prepare_kernel, first, summed), out_shap...  9.96 us
    ppermute x7, starting transfers between devices, to_chip(): return lax.ppermute(value, 'tensor', pairs)  7.7 us
    ppermute x7, waiting for transfers between devices, to_chip(): return lax.ppermute(value, 'tensor', pairs)  6.88 us
    all_to_all x1, starting transfers between devices, body(): exchanged = lax.all_to_all(packed, 'dp', 0, 0, tiled=True)  6.86 us
    ppermute x4, starting transfers between devices, swap_half(): outside[strip].append((piece, lax.ppermute(piece, 'dp', pairs)))  5.83 us
    all_to_all x1, starting transfers between devices, body(): own_f = lax.all_to_all(sent, 'dp', 0, 0, tiled=True)  5.27 us
    pallas_call x1, Pallas kernels, body(): pl.pallas_call(functools.partial(own_kernel, static), out_shape=(jax.Shap...  4.88 us
    ppermute x4, waiting for transfers between devices, swap_half(): outside[strip].append((piece, lax.ppermute(piece, 'dp', pairs)))  4.15 us
  transfers between devices with their start and end apart: 17, of which 11 were waited for; matrix products, arithmetic and copies ran while one was open for 0% of the time, Pallas kernels for 45%

profile of v25, /device:TPU:0, one launch (start us, length us, event | category | flops | bytes accessed | tf_op | source)
XLA Modules:
  0.0 81.3 jit_solution(3226552646160416063)
XLA Ops:
  0.6 0.5 collective-permute-start
  1.1 2.0 %shard_map.130._ = bf16[8,192,128]{2,1,0:T(8,128)(2,1)} custom-call(f32[128,1280]{1,0:T(8,128)} %bitcast.20, f32[64,512]{1,0:T(8,128)} %bitcast.24), custom_call_target="tpu_custom_call" | custom-call | tf_op jit(solution)/shard_map/pallas_call | solution.py:498
  3.2 6.9 %all-to-all-start = ((bf16[8,192,128]{2,1,0:T(8,128)(2,1)}), bf16[8,192,128]{2,1,0:T(8,128)(2,1)}, u32[]{:S(2)}, u32[]{:S(2)}) async-start(bf16[8,192,128]{2,1,0:T(8,128)(2,1)} %shard_map.130._), calls=%async_computation | async-start | bytes 786432 | tf_op jit(solution)/shard_map/all_to_all | solution.py:529
  10.0 2.1 %shard_map.135 = (bf16[2,1280,128]{2,1,0:T(8,128)(2,1)}, bf16[2,1280,128]{2,1,0:T(8,128)(2,1)}) custom-call(bf16[5120,512]{1,0:T(8,128)(2,1)} %sibling_block.1, bf16[8,192,128]{2,1,0:T(8,128)(2,1)} %shard_map.130._), custom_call_target="tpu_custom_call" | custom-call | tf_op jit(solution)/shard_map/pallas_call | solution.py:517
  12.2 1.6 %collective-permute-start.4 = (bf16[2,1280,128]{2,1,0:T(8,128)(2,1)}, bf16[2,1280,128]{2,1,0:T(8,128)(2,1)}, u32[]{:S(2)}, u32[]{:S(2)}) collective-permute-start(bf16[2,1280,128]{2,1,0:T(8,128)(2,1)} %get-tuple-element.48), channel_id=1, source_target_pairs={{0,2},{1,3},{2,0},{3,1},{4,6},{5,7},{6,4},{7,5},{8,10},{9,11},{10,... | collective-permute-start | bytes 1966088 | tf_op jit(solution)/shard_map/ppermute | solution.py:480
  13.7 0.0 copy-done.6
  13.7 0.1 collective-permute-start.1
  13.8 1.2 %collective-permute-done.1.sibling_gain = f32[1,1280]{1,0:T(1,128)S(1)} collective-permute-done((f32[1,1280]{1,0:T(1,128)S(1)}, f32[1,1280]{1,0:T(1,128)S(1)}, u32[]{:S(2)}, u32[]{:S(2)}) %collective-permute-start.1) | collective-permute-done | bytes 5152 | tf_op jit(solution)/shard_map/ppermute | solution.py:472
  15.0 0.0 collective-permute-done.sibling_in
  15.0 6.2 %shard_map.131 = (bf16[640,2560]{1,0:T(8,128)(2,1)S(1)}, f32[10,128]{1,0:T(8,128)S(1)}) custom-call(bf16[1280,1280]{1,0:T(8,128)(2,1)} %own_in.3, bf16[1280,1280]{1,0:T(8,128)(2,1)} %collective-permute-done.sibling_in, f32[1,1280]{1,0:T(1,128)S(1)} %broadcast_in_dim.3.own_gain, f32[1,1280]{1,0:T(1,128)S(1)} %collective-permute-done.1.sibling_gain), custom_call_target="tpu_custom_call" | custom-call | tf_op jit(solution)/shard_map/pallas_call | solution.py:560
  21.1 0.0 copy-done.4
  21.1 0.0 copy-done.5
  21.2 0.0 copy-start.2
  21.2 0.6 copy-done.2
  21.7 0.7 all-to-all-done.grad_in
  22.5 2.6 %shard_map.132 = (f32[3,128,160]{2,1,0:T(8,128)}, f32[3,8,512]{2,1,0:T(8,128)}, bf16[8,192,128]{2,1,0:T(8,128)(2,1)}) custom-call(bf16[8,192,128]{2,1,0:T(8,128)(2,1)} %all-to-all-done.grad_in, f32[128,1280]{1,0:T(8,128)} %bitcast.21, f32[128,1280]{1,0:T(8,128)} %bitcast.22, f32[128,1280]{1,0:T(8,128)} %bitcast.23, f32[64,512]{1,0:T(8,128)} %refs_3_.1, ...), custom_call_target="tpu_custom_call" | custom-call | tf_op jit(solution)/shard_map/pallas_call | solution.py:578
  25.1 5.3 %all-to-all-start.1 = ((bf16[8,192,128]{2,1,0:T(8,128)(2,1)}), bf16[8,192,128]{2,1,0:T(8,128)(2,1)}, u32[]{:S(2)}, u32[]{:S(2)}) async-start(bf16[8,192,128]{2,1,0:T(8,128)(2,1)} %get-tuple-element.37), calls=%async_computation.1 | async-start | bytes 786432 | tf_op jit(solution)/shard_map/all_to_all | solution.py:595
  30.3 0.0 collective-permute-done.4.in_ref
  30.3 0.6 collective-permute-start.5
  30.9 1.9 %shard_map.136 = (bf16[1280,128]{1,0:T(8,128)(2,1)}, bf16[1280,128]{1,0:T(8,128)(2,1)}) custom-call(bf16[2,1280,128]{2,1,0:T(8,128)(2,1)} %collective-permute-done.4.in_ref), custom_call_target="tpu_custom_call" | custom-call | tf_op jit(solution)/shard_map/pallas_call | solution.py:605
  32.8 2.0 %collective-permute-start.6 = (bf16[1280,128]{1,0:T(8,128)(2,1)}, bf16[1280,128]{1,0:T(8,128)(2,1)}, u32[]{:S(2)}, u32[]{:S(2)}) collective-permute-start(bf16[1280,128]{1,0:T(8,128)(2,1)} %get-tuple-element.51.refs_0_), channel_id=1, source_target_pairs={{0,4},{4,0},{8,12},{12,8},{16,20},{20,16},{24,28},{28,24},{1,5},{5... | collective-permute-start | bytes 983048 | tf_op jit(solution)/shard_map/ppermute | solution.py:619
  34.9 1.5 %collective-permute-start.7 = (bf16[1280,128]{1,0:T(8,128)(2,1)}, bf16[1280,128]{1,0:T(8,128)(2,1)}, u32[]{:S(2)}, u32[]{:S(2)}) collective-permute-start(bf16[1280,128]{1,0:T(8,128)(2,1)} %get-tuple-element.52.refs_2_), channel_id=1, source_target_pairs={{0,8},{4,12},{8,0},{12,4},{16,24},{20,28},{24,16},{28,20},{1,9},{5... | collective-permute-start | bytes 983048 | tf_op jit(solution)/shard_map/ppermute | solution.py:619
  36.3 3.8 %shard_map.133 = (bf16[640,1280]{1,0:T(8,128)(2,1)}, bf16[640,1280]{1,0:T(8,128)(2,1)}) custom-call(bf16[1280,1280]{1,0:T(8,128)(2,1)} %own_in.3, bf16[1280,1280]{1,0:T(8,128)(2,1)} %collective-permute-done.sibling_in, f32[1,1280]{1,0:T(1,128)} %copy-done.4, f32[1,1280]{1,0:T(1,128)} %copy-done.5, f32[10,128]{1,0:T(8,128)} %copy-done.2), custom_call_target="tpu_custom_call" | custom-call | tf_op jit(solution)/shard_map/pallas_call | solution.py:560
  40.1 2.3 %all-to-all-done.1.factor_ref = bf16[8,192,128]{2,1,0:T(8,128)(2,1)} async-done(((bf16[8,192,128]{2,1,0:T(8,128)(2,1)}), bf16[8,192,128]{2,1,0:T(8,128)(2,1)}, u32[]{:S(2)}, u32[]{:S(2)}) %all-to-all-start.1) | async-done | bytes 393248 | tf_op jit(solution)/shard_map/all_to_all | solution.py:595
  42.5 0.0 copy-done.3
  42.5 1.1 %shard_map.134 = (bf16[9,32,128]{2,1,0:T(8,128)(2,1)S(1)}, bf16[4,192,128]{2,1,0:T(8,128)(2,1)S(1)}, bf16[4,192,128]{2,1,0:T(8,128)(2,1)S(1)}) custom-call(bf16[8,192,128]{2,1,0:T(8,128)(2,1)} %all-to-all-done.1.factor_ref, f32[10,128]{1,0:T(8,128)S(1)} %copy-done.3), custom_call_target="tpu_custom_call" | custom-call | tf_op jit(solution)/shard_map/pallas_call | solution.py:626
  43.6 0.1 collective-permute-start.2
  43.6 0.5 collective-permute-start.3
  44.1 0.8 collective-permute-done.6.refs_1_
  44.9 0.9 %collective-permute-start.8 = (bf16[9,32,128]{2,1,0:T(8,128)(2,1)S(1)}, bf16[9,32,128]{2,1,0:T(8,128)(2,1)S(1)}, u32[]{:S(2)}, u32[]{:S(2)}) collective-permute-start(bf16[9,32,128]{2,1,0:T(8,128)(2,1)S(1)} %get-tuple-element.53), channel_id=1, source_target_pairs={{0,2},{1,3},{2,0},{3,1},{4,6},{5,7},{6,4},{7,5},{8,10},{9,11},{10,... | collective-permute-start | bytes 221192 | tf_op jit(solution)/shard_map/ppermute | solution.py:480
  45.8 1.1 %collective-permute-done.7.refs_3_ = bf16[1280,128]{1,0:T(8,128)(2,1)} collective-permute-done((bf16[1280,128]{1,0:T(8,128)(2,1)}, bf16[1280,128]{1,0:T(8,128)(2,1)}, u32[]{:S(2)}, u32[]{:S(2)}) %collective-permute-start.7) | collective-permute-done | bytes 327712 | tf_op jit(solution)/shard_map/ppermute | solution.py:619
  46.9 1.6 %shard_map.137.blocks = bf16[2560,256]{1,0:T(8,128)(2,1)S(1)} custom-call(bf16[1280,128]{1,0:T(8,128)(2,1)} %get-tuple-element.51.refs_0_, bf16[1280,128]{1,0:T(8,128)(2,1)} %collective-permute-done.6.refs_1_, bf16[1280,128]{1,0:T(8,128)(2,1)} %get-tuple-element.52.refs_2_, bf16[1280,128]{1,0:T(8,128)(2,1)} %collective-permute-done.7.refs_3_), custom_call_target="tpu_custom_call" | custom-call | tf_op jit(solution)/shard_map/pallas_call | solution.py:661
  48.5 0.8 collective-permute-done.8.b_ref.refs_0_
  49.3 0.0 collective-permute-done.2.refs_2_
  49.3 0.0 collective-permute-done.3.refs_3_
  49.3 0.0 copy-start.1
  49.3 1.7 %shard_map.138 = (bf16[2560,256]{1,0:T(8,128)(2,1)S(1)}, bf16[640,256]{1,0:T(8,128)(2,1)S(1)}) custom-call(bf16[2560,256]{1,0:T(8,128)(2,1)S(1)} %shard_map.137.blocks, bf16[9,32,128]{2,1,0:T(8,128)(2,1)S(1)} %collective-permute-done.8.b_ref.refs_0_, bf16[640,2560]{1,0:T(8,128)(2,1)S(1)} %get-tuple-element.44.x.refs_4_, ...), custom_call_target="tpu_custom_call" | custom-call | tf_op jit(solution)/shard_map/pallas_call | solution.py:668
  51.0 1.0 %collective-permute-start.11 = (bf16[640,256]{1,0:T(8,128)(2,1)S(1)}, bf16[640,256]{1,0:T(8,128)(2,1)S(1)}, u32[]{:S(2)}, u32[]{:S(2)}) collective-permute-start(bf16[640,256]{1,0:T(8,128)(2,1)S(1)} %get-tuple-element.54), channel_id=1, source_target_pairs={{0,2},{1,3},{2,0},{3,1},{4,6},{5,7},{6,4},{7,5},{8,10},{9,11},{10,... | collective-permute-start | bytes 983048 | tf_op jit(solution)/shard_map/ppermute | solution.py:480
  52.0 0.0 collective-permute-done.5.in_ref
  52.0 1.8 %shard_map.139 = (bf16[1280,128]{1,0:T(8,128)(2,1)S(1)}, bf16[1280,128]{1,0:T(8,128)(2,1)S(1)}) custom-call(bf16[2,1280,128]{2,1,0:T(8,128)(2,1)} %collective-permute-done.5.in_ref), custom_call_target="tpu_custom_call" | custom-call | tf_op jit(solution)/shard_map/pallas_call | solution.py:605
  53.8 0.9 %collective-permute-start.9 = (bf16[1280,128]{1,0:T(8,128)(2,1)S(1)}, bf16[1280,128]{1,0:T(8,128)(2,1)S(1)}, u32[]{:S(2)}, u32[]{:S(2)}) collective-permute-start(bf16[1280,128]{1,0:T(8,128)(2,1)S(1)} %get-tuple-element.56.refs_0_), channel_id=1, source_target_pairs={{0,4},{4,0},{8,12},{12,8},{16,20},{20,16},{24,28},{28,24},{1,5},{5... | collective-permute-start | bytes 983048 | tf_op jit(solution)/shard_map/ppermute | solution.py:619
  54.7 1.4 %collective-permute-start.10 = (bf16[1280,128]{1,0:T(8,128)(2,1)S(1)}, bf16[1280,128]{1,0:T(8,128)(2,1)S(1)}, u32[]{:S(2)}, u32[]{:S(2)}) collective-permute-start(bf16[1280,128]{1,0:T(8,128)(2,1)S(1)} %get-tuple-element.57.refs_2_), channel_id=1, source_target_pairs={{0,8},{4,12},{8,0},{12,4},{16,24},{20,28},{24,16},{28,20},{1,9},{5... | collective-permute-start | bytes 983048 | tf_op jit(solution)/shard_map/ppermute | solution.py:619
  56.1 0.0 copy-done
  56.1 0.0 copy-done.1
  56.1 1.2 %shard_map.143 = bf16[640,256]{1,0:T(8,128)(2,1)S(1)} custom-call(bf16[640,1280]{1,0:T(8,128)(2,1)S(1)} %copy-done, bf16[640,1280]{1,0:T(8,128)(2,1)S(1)} %copy-done.1, bf16[2560,256]{1,0:T(8,128)(2,1)S(1)} %get-tuple-element.59.refs_2_), custom_call_target="tpu_custom_call" | custom-call | tf_op jit(solution)/shard_map/pallas_call | solution.py:676
  57.3 1.5 %collective-permute-start.12 = (bf16[640,256]{1,0:T(8,128)(2,1)S(1)}, bf16[640,256]{1,0:T(8,128)(2,1)S(1)}, u32[]{:S(2)}, u32[]{:S(2)}) collective-permute-start(bf16[640,256]{1,0:T(8,128)(2,1)S(1)} %shard_map.143), channel_id=1, source_target_pairs={{0,2},{1,3},{2,0},{3,1},{4,6},{5,7},{6,4},{7,5},{8,10},{9,11},{10,... | collective-permute-start | bytes 983048 | tf_op jit(solution)/shard_map/ppermute | solution.py:480
  58.8 1.8 %collective-permute-done.11.refs_4_.refs_0_ = bf16[640,256]{1,0:T(8,128)(2,1)S(1)} collective-permute-done((bf16[640,256]{1,0:T(8,128)(2,1)S(1)}, bf16[640,256]{1,0:T(8,128)(2,1)S(1)}, u32[]{:S(2)}, u32[]{:S(2)}) %collective-permute-start.11) | collective-permute-done | bytes 327712 | tf_op jit(solution)/shard_map/ppermute | solution.py:480
  60.6 0.9 %collective-permute-done.9.refs_1_ = bf16[1280,128]{1,0:T(8,128)(2,1)S(1)} collective-permute-done((bf16[1280,128]{1,0:T(8,128)(2,1)S(1)}, bf16[1280,128]{1,0:T(8,128)(2,1)S(1)}, u32[]{:S(2)}, u32[]{:S(2)}) %collective-permute-start.9) | collective-permute-done | bytes 327712 | tf_op jit(solution)/shard_map/ppermute | solution.py:619
  61.4 1.5 %collective-permute-done.10.refs_3_ = bf16[1280,128]{1,0:T(8,128)(2,1)S(1)} collective-permute-done((bf16[1280,128]{1,0:T(8,128)(2,1)S(1)}, bf16[1280,128]{1,0:T(8,128)(2,1)S(1)}, u32[]{:S(2)}, u32[]{:S(2)}) %collective-permute-start.10) | collective-permute-done | bytes 327712 | tf_op jit(solution)/shard_map/ppermute | solution.py:619
  62.9 0.3 shard_map.140.blocks
  63.2 0.0 slice-start.1
  63.2 1.7 %shard_map.141 = (bf16[2560,256]{1,0:T(8,128)(2,1)S(1)}, bf16[640,256]{1,0:T(8,128)(2,1)S(1)}) custom-call(bf16[2560,256]{1,0:T(8,128)(2,1)S(1)} %shard_map.140.blocks, bf16[9,32,128]{2,1,0:T(8,128)(2,1)S(1)} %collective-permute-done.8.b_ref.refs_0_, bf16[640,2560]{1,0:T(8,128)(2,1)S(1)} %get-tuple-element.44.x.refs_4_, ...), custom_call_target="tpu_custom_call" | custom-call | tf_op jit(solution)/shard_map/pallas_call | solution.py:668
  65.0 1.8 %collective-permute-start.14 = (bf16[640,256]{1,0:T(8,128)(2,1)S(1)}, bf16[640,256]{1,0:T(8,128)(2,1)S(1)}, u32[]{:S(2)}, u32[]{:S(2)}) collective-permute-start(bf16[640,256]{1,0:T(8,128)(2,1)S(1)} %get-tuple-element.61), channel_id=1, source_target_pairs={{0,2},{1,3},{2,0},{3,1},{4,6},{5,7},{6,4},{7,5},{8,10},{9,11},{10,... | collective-permute-start | bytes 983048 | tf_op jit(solution)/shard_map/ppermute | solution.py:480
  66.7 1.2 %shard_map.142.refs_7_ = bf16[640,256]{1,0:T(8,128)(2,1)S(1)} custom-call(bf16[640,1280]{1,0:T(8,128)(2,1)S(1)} %copy-done, bf16[640,1280]{1,0:T(8,128)(2,1)S(1)} %copy-done.1, bf16[2560,256]{1,0:T(8,128)(2,1)S(1)} %get-tuple-element.58.refs_2_), custom_call_target="tpu_custom_call" | custom-call | tf_op jit(solution)/shard_map/pallas_call | solution.py:676
  67.9 0.4 collective-permute-start.13
  68.3 0.2 shard_map.145.inv
  68.5 0.0 collective-permute-done.12.refs_8_.refs_0_
  68.6 4.9 %shard_map.144 = (f32[1280,256]{1,0:T(8,128)S(1)}, f32[1280,256]{1,0:T(8,128)S(1)}) custom-call(bf16[5120,512]{1,0:T(8,128)(2,1)S(1)} %bitcast.19, bf16[5120,512]{1,0:T(8,128)(2,1)S(1)} %bitcast.19, bf16[4,192,128]{2,1,0:T(8,128)(2,1)S(1)} %get-tuple-element.42.refs_0_, bf16[4,192,128]{2,1,0:T(8,128)(2,1)S(1)} %get-tuple-element.43.refs_1_, ...), custom_call_target="tpu_custom_call" | custom-call | flops 3355443200 | bytes 6553600 | tf_op jit(solution)/shard_map/pallas_call | solution.py:691
  73.5 0.9 %shard_map.146.refs_1_ = bf16[1280,512]{1,0:T(8,128)(2,1)} custom-call(f32[1280,256]{1,0:T(8,128)S(1)} %get-tuple-element.62.own, f32[1280,128]{1,0:T(8,128)S(1)} %shard_map.145.inv, bf16[640,256]{1,0:T(8,128)(2,1)S(1)} %collective-permute-done.11.refs_4_.refs_0_), custom_call_target="tpu_custom_call" | custom-call | tf_op jit(solution)/shard_map/pallas_call | solution.py:431
  74.3 0.9 %shard_map.147.refs_1_ = bf16[1280,512]{1,0:T(8,128)(2,1)} custom-call(f32[1280,256]{1,0:T(8,128)S(1)} %get-tuple-element.62.own, f32[1280,128]{1,0:T(8,128)S(1)} %shard_map.145.inv, bf16[640,256]{1,0:T(8,128)(2,1)S(1)} %collective-permute-done.12.refs_8_.refs_0_, bf16[1280,512]{1,0:T(8,128)(2,1)} %shard_map.146.refs_1_), custom_call_target="tpu_custom_call", output_to_operand_aliasing={{}: (3, {})} | custom-call | tf_op jit(solution)/shard_map/pallas_call | solution.py:431
  75.2 0.4 collective-permute-done.14.refs_0_
  75.7 0.9 %shard_map.148.refs_1_ = bf16[1280,512]{1,0:T(8,128)(2,1)} custom-call(f32[1280,256]{1,0:T(8,128)S(1)} %get-tuple-element.60.own, f32[1280,128]{1,0:T(8,128)S(1)} %shard_map.145.inv, bf16[640,256]{1,0:T(8,128)(2,1)S(1)} %collective-permute-done.14.refs_0_, bf16[1280,512]{1,0:T(8,128)(2,1)} %shard_map.147.refs_1_), custom_call_target="tpu_custom_call", output_to_operand_aliasing={{}: (3, {})} | custom-call | tf_op jit(solution)/shard_map/pallas_call | solution.py:431
  76.5 3.9 %collective-permute-done.13.refs_0_ = bf16[640,256]{1,0:T(8,128)(2,1)S(1)} collective-permute-done((bf16[640,256]{1,0:T(8,128)(2,1)S(1)}, bf16[640,256]{1,0:T(8,128)(2,1)S(1)}, u32[]{:S(2)}, u32[]{:S(2)}) %collective-permute-start.13) | collective-permute-done | bytes 327712 | tf_op jit(solution)/shard_map/ppermute | solution.py:480
  80.5 0.9 %shard_map.149 = bf16[1280,512]{1,0:T(8,128)(2,1)} custom-call(f32[1280,256]{1,0:T(8,128)S(1)} %get-tuple-element.60.own, f32[1280,128]{1,0:T(8,128)S(1)} %shard_map.145.inv, bf16[640,256]{1,0:T(8,128)(2,1)S(1)} %collective-permute-done.13.refs_0_, bf16[1280,512]{1,0:T(8,128)(2,1)} %shard_map.148.refs_1_), custom_call_target="tpu_custom_call", output_to_operand_aliasing={{}: (3, {})} | custom-call | tf_op jit(solution)/shard_map/pallas_call | solution.py:431
  (10 shorter events, 0.0 us)
Async XLA Ops:
  0.6 14.3 %collective-permute-start = (bf16[1280,1280]{1,0:T(8,128)(2,1)}, bf16[1280,1280]{1,0:T(8,128)(2,1)}, u32[]{:S(2)}, u32[]{:S(2)}) collective-permute-start(bf16[1280,1280]{1,0:T(8,128)(2,1)} %own_in.3), channel_id=1, source_target_pairs={{0,1},{1,0},{2,3},{3,2},{4,5},{5,4},{6,7},{7,6},{8,9},{9,8},{10,11... | collective-permute-start | bytes 9830408 | tf_op jit(solution)/shard_map/ppermute | solution.py:472
  3.2 19.3 %all-to-all-start = ((bf16[8,192,128]{2,1,0:T(8,128)(2,1)}), bf16[8,192,128]{2,1,0:T(8,128)(2,1)}, u32[]{:S(2)}, u32[]{:S(2)}) async-start(bf16[8,192,128]{2,1,0:T(8,128)(2,1)} %shard_map.130._), calls=%async_computation | async-start | bytes 786432 | tf_op jit(solution)/shard_map/all_to_all | solution.py:529
  10.0 3.7 %copy-start.6 = (f32[1280]{0:T(1024)S(1)}, f32[1280]{0:T(1024)}, u32[]{:S(2)}) copy-start(f32[1280]{0:T(1024)} %param.12) | copy-start | bytes 15364
  12.2 18.2 %collective-permute-start.4 = (bf16[2,1280,128]{2,1,0:T(8,128)(2,1)}, bf16[2,1280,128]{2,1,0:T(8,128)(2,1)}, u32[]{:S(2)}, u32[]{:S(2)}) collective-permute-start(bf16[2,1280,128]{2,1,0:T(8,128)(2,1)} %get-tuple-element.48), channel_id=1, source_target_pairs={{0,2},{1,3},{2,0},{3,1},{4,6},{5,7},{6,4},{7,5},{8,10},{9,11},{10,... | collective-permute-start | bytes 1966088 | tf_op jit(solution)/shard_map/ppermute | solution.py:480
  13.7 7.4 %copy-start.4 = (f32[1,1280]{1,0:T(1,128)}, f32[1,1280]{1,0:T(1,128)S(1)}, u32[]{:S(2)}) copy-start(f32[1,1280]{1,0:T(1,128)S(1)} %broadcast_in_dim.3.own_gain) | copy-start | bytes 15364
  13.7 1.2 %collective-permute-start.1 = (f32[1,1280]{1,0:T(1,128)S(1)}, f32[1,1280]{1,0:T(1,128)S(1)}, u32[]{:S(2)}, u32[]{:S(2)}) collective-permute-start(f32[1,1280]{1,0:T(1,128)S(1)} %broadcast_in_dim.3.own_gain), channel_id=1, source_target_pairs={{0,1},{1,0},{2,3},{3,2},{4,5},{5,4},{6,7},{7,6},{8,9},{9,8},{10,11... | collective-permute-start | bytes 15368 | tf_op jit(solution)/shard_map/ppermute | solution.py:472
  15.0 6.2 %copy-start.5 = (f32[1,1280]{1,0:T(1,128)}, f32[1,1280]{1,0:T(1,128)S(1)}, u32[]{:S(2)}) copy-start(f32[1,1280]{1,0:T(1,128)S(1)} %collective-permute-done.1.sibling_gain) | copy-start | bytes 15364
  21.2 0.6 copy-start.2
  25.1 17.4 %all-to-all-start.1 = ((bf16[8,192,128]{2,1,0:T(8,128)(2,1)}), bf16[8,192,128]{2,1,0:T(8,128)(2,1)}, u32[]{:S(2)}, u32[]{:S(2)}) async-start(bf16[8,192,128]{2,1,0:T(8,128)(2,1)} %get-tuple-element.37), calls=%async_computation.1 | async-start | bytes 786432 | tf_op jit(solution)/shard_map/all_to_all | solution.py:595
  30.3 21.6 %collective-permute-start.5 = (bf16[2,1280,128]{2,1,0:T(8,128)(2,1)}, bf16[2,1280,128]{2,1,0:T(8,128)(2,1)}, u32[]{:S(2)}, u32[]{:S(2)}) collective-permute-start(bf16[2,1280,128]{2,1,0:T(8,128)(2,1)} %get-tuple-element.49), channel_id=1, source_target_pairs={{0,2},{1,3},{2,0},{3,1},{4,6},{5,7},{6,4},{7,5},{8,10},{9,11},{10,... | collective-permute-start | bytes 1966088 | tf_op jit(solution)/shard_map/ppermute | solution.py:480
  32.8 12.1 %collective-permute-start.6 = (bf16[1280,128]{1,0:T(8,128)(2,1)}, bf16[1280,128]{1,0:T(8,128)(2,1)}, u32[]{:S(2)}, u32[]{:S(2)}) collective-permute-start(bf16[1280,128]{1,0:T(8,128)(2,1)} %get-tuple-element.51.refs_0_), channel_id=1, source_target_pairs={{0,4},{4,0},{8,12},{12,8},{16,20},{20,16},{24,28},{28,24},{1,5},{5... | collective-permute-start | bytes 983048 | tf_op jit(solution)/shard_map/ppermute | solution.py:619
  34.9 7.6 %copy-start.3 = (f32[10,128]{1,0:T(8,128)S(1)}, f32[10,128]{1,0:T(8,128)}, u32[]{:S(2)}) copy-start(f32[10,128]{1,0:T(8,128)} %copy-done.2) | copy-start | bytes 15364
  34.9 12.0 %collective-permute-start.7 = (bf16[1280,128]{1,0:T(8,128)(2,1)}, bf16[1280,128]{1,0:T(8,128)(2,1)}, u32[]{:S(2)}, u32[]{:S(2)}) collective-permute-start(bf16[1280,128]{1,0:T(8,128)(2,1)} %get-tuple-element.52.refs_2_), channel_id=1, source_target_pairs={{0,8},{4,12},{8,0},{12,4},{16,24},{20,28},{24,16},{28,20},{1,9},{5... | collective-permute-start | bytes 983048 | tf_op jit(solution)/shard_map/ppermute | solution.py:619
  43.6 5.7 %collective-permute-start.2 = (bf16[4,192,128]{2,1,0:T(8,128)(2,1)S(1)}, bf16[4,192,128]{2,1,0:T(8,128)(2,1)S(1)}, u32[]{:S(2)}, u32[]{:S(2)}) collective-permute-start(bf16[4,192,128]{2,1,0:T(8,128)(2,1)S(1)} %get-tuple-element.42.refs_0_), channel_id=1, source_target_pairs={{0,1},{1,0},{2,3},{3,2},{4,5},{5,4},{6,7},{7,6},{8,9},{9,8},{10,11... | collective-permute-start | bytes 589832 | tf_op jit(solution)/shard_map/ppermute | solution.py:472
  43.6 5.6 %collective-permute-start.3 = (bf16[4,192,128]{2,1,0:T(8,128)(2,1)S(1)}, bf16[4,192,128]{2,1,0:T(8,128)(2,1)S(1)}, u32[]{:S(2)}, u32[]{:S(2)}) collective-permute-start(bf16[4,192,128]{2,1,0:T(8,128)(2,1)S(1)} %get-tuple-element.43.refs_1_), channel_id=1, source_target_pairs={{0,1},{1,0},{2,3},{3,2},{4,5},{5,4},{6,7},{7,6},{8,9},{9,8},{10,11... | collective-permute-start | bytes 589832 | tf_op jit(solution)/shard_map/ppermute | solution.py:472
  44.9 4.4 %collective-permute-start.8 = (bf16[9,32,128]{2,1,0:T(8,128)(2,1)S(1)}, bf16[9,32,128]{2,1,0:T(8,128)(2,1)S(1)}, u32[]{:S(2)}, u32[]{:S(2)}) collective-permute-start(bf16[9,32,128]{2,1,0:T(8,128)(2,1)S(1)} %get-tuple-element.53), channel_id=1, source_target_pairs={{0,2},{1,3},{2,0},{3,1},{4,6},{5,7},{6,4},{7,5},{8,10},{9,11},{10,... | collective-permute-start | bytes 221192 | tf_op jit(solution)/shard_map/ppermute | solution.py:480
  49.3 6.9 %copy-start = (bf16[640,1280]{1,0:T(8,128)(2,1)S(1)}, bf16[640,1280]{1,0:T(8,128)(2,1)}, u32[]{:S(2)}) copy-start(bf16[640,1280]{1,0:T(8,128)(2,1)} %get-tuple-element.45.refs_0_.refs_5_) | copy-start | bytes 4915204
  49.3 6.9 %copy-start.1 = (bf16[640,1280]{1,0:T(8,128)(2,1)S(1)}, bf16[640,1280]{1,0:T(8,128)(2,1)}, u32[]{:S(2)}) copy-start(bf16[640,1280]{1,0:T(8,128)(2,1)} %get-tuple-element.46.refs_1_.refs_6_) | copy-start | bytes 4915204
  51.0 9.6 %collective-permute-start.11 = (bf16[640,256]{1,0:T(8,128)(2,1)S(1)}, bf16[640,256]{1,0:T(8,128)(2,1)S(1)}, u32[]{:S(2)}, u32[]{:S(2)}) collective-permute-start(bf16[640,256]{1,0:T(8,128)(2,1)S(1)} %get-tuple-element.54), channel_id=1, source_target_pairs={{0,2},{1,3},{2,0},{3,1},{4,6},{5,7},{6,4},{7,5},{8,10},{9,11},{10,... | collective-permute-start | bytes 983048 | tf_op jit(solution)/shard_map/ppermute | solution.py:480
  53.8 7.6 %collective-permute-start.9 = (bf16[1280,128]{1,0:T(8,128)(2,1)S(1)}, bf16[1280,128]{1,0:T(8,128)(2,1)S(1)}, u32[]{:S(2)}, u32[]{:S(2)}) collective-permute-start(bf16[1280,128]{1,0:T(8,128)(2,1)S(1)} %get-tuple-element.56.refs_0_), channel_id=1, source_target_pairs={{0,4},{4,0},{8,12},{12,8},{16,20},{20,16},{24,28},{28,24},{1,5},{5... | collective-permute-start | bytes 983048 | tf_op jit(solution)/shard_map/ppermute | solution.py:619
  54.7 8.2 %collective-permute-start.10 = (bf16[1280,128]{1,0:T(8,128)(2,1)S(1)}, bf16[1280,128]{1,0:T(8,128)(2,1)S(1)}, u32[]{:S(2)}, u32[]{:S(2)}) collective-permute-start(bf16[1280,128]{1,0:T(8,128)(2,1)S(1)} %get-tuple-element.57.refs_2_), channel_id=1, source_target_pairs={{0,8},{4,12},{8,0},{12,4},{16,24},{20,28},{24,16},{28,20},{1,9},{5... | collective-permute-start | bytes 983048 | tf_op jit(solution)/shard_map/ppermute | solution.py:619
  57.3 11.2 %collective-permute-start.12 = (bf16[640,256]{1,0:T(8,128)(2,1)S(1)}, bf16[640,256]{1,0:T(8,128)(2,1)S(1)}, u32[]{:S(2)}, u32[]{:S(2)}) collective-permute-start(bf16[640,256]{1,0:T(8,128)(2,1)S(1)} %shard_map.143), channel_id=1, source_target_pairs={{0,2},{1,3},{2,0},{3,1},{4,6},{5,7},{6,4},{7,5},{8,10},{9,11},{10,... | collective-permute-start | bytes 983048 | tf_op jit(solution)/shard_map/ppermute | solution.py:480
  62.9 5.7 %slice-start = ((s8[5242880]{0:T(1024)(128)(4,1)}), s8[4194304]{0:T(1024)(128)(4,1)S(1)}, s32[]{:S(2)}) async-start(s8[5242880]{0:T(1024)(128)(4,1)} %bitcast.18), calls=%async_computation.2 | async-start | bytes 8388608
  63.2 5.3 %slice-start.1 = ((s8[5242880]{0:T(1024)(128)(4,1)}), s8[1048576]{0:T(1024)(128)(4,1)S(1)}, s32[]{:S(2)}) async-start(s8[5242880]{0:T(1024)(128)(4,1)} %bitcast.18), calls=%async_computation.3 | async-start | bytes 2097152
  65.0 10.7 %collective-permute-start.14 = (bf16[640,256]{1,0:T(8,128)(2,1)S(1)}, bf16[640,256]{1,0:T(8,128)(2,1)S(1)}, u32[]{:S(2)}, u32[]{:S(2)}) collective-permute-start(bf16[640,256]{1,0:T(8,128)(2,1)S(1)} %get-tuple-element.61), channel_id=1, source_target_pairs={{0,2},{1,3},{2,0},{3,1},{4,6},{5,7},{6,4},{7,5},{8,10},{9,11},{10,... | collective-permute-start | bytes 983048 | tf_op jit(solution)/shard_map/ppermute | solution.py:480
  67.9 12.5 %collective-permute-start.13 = (bf16[640,256]{1,0:T(8,128)(2,1)S(1)}, bf16[640,256]{1,0:T(8,128)(2,1)S(1)}, u32[]{:S(2)}, u32[]{:S(2)}) collective-permute-start(bf16[640,256]{1,0:T(8,128)(2,1)S(1)} %shard_map.142.refs_7_), channel_id=1, source_target_pairs={{0,2},{1,3},{2,0},{3,1},{4,6},{5,7},{6,4},{7,5},{8,10},{9,11},{10,... | collective-permute-start | bytes 983048 | tf_op jit(solution)/shard_map/ppermute | solution.py:480

commit v26 on v24

--- a/solution.py
+++ b/solution.py
@@ -489,7 +489,7 @@
     aligned = features % LANES == 0 and window <= features
     aligned = aligned and up_rows % 8 == 0 and down_rows % 16 == 0
     window = window if aligned else down_rows
-    turns = [1, 2] if n_dp % 4 == 0 else [1, 1]
+    turns = [2, 1] if n_dp % 4 == 0 else [1, 1]
     turn = [turns[strip % 2] for strip in range(strips)]
     halves = min(COLUMN_HALVES, strips)
     wide = columns // halves

time: 80.7 us -> 82.5 us (1.022)
  waiting for transfers between devices: 15.6 us -> 18.4 us
  starting transfers between devices: 26.9 us -> 25.9 us
    ppermute x7, waiting for transfers between devices: 4.7 us -> 9.4 us  [to_chip(): return lax.ppermute(value, 'tensor', pairs)]
    ppermute x4, waiting for transfers between devices: 5.57 us -> 3.6 us  [swap_half(): outside[strip].append((piece, lax.ppermute(piece, 'dp', pairs)))]
  transfers between devices with their start and end apart: 17 -> 17, of which waited for: 11 -> 11; matrix products, arithmetic and copies ran while one was open for 0% -> 0% of each run, Pallas kernels for 44% -> 43%
where the time goes in v26:
time: 82.5 us; the launch traced here: 82 us
  Pallas kernels  36.2 us (44%)
  starting transfers between devices  25.9 us (31%)
  waiting for transfers between devices  18.4 us (22%)
  between operations  0.86 us (1%)
    pallas_call x2, Pallas kernels, prepared(): pl.pallas_call(functools.partial(prepare_kernel, first, summed), out_shap...  9.96 us
    ppermute x7, waiting for transfers between devices, to_chip(): return lax.ppermute(value, 'tensor', pairs)  9.4 us
    ppermute x7, starting transfers between devices, to_chip(): return lax.ppermute(value, 'tensor', pairs)  8.86 us
    all_to_all x1, starting transfers between devices, body(): exchanged = lax.all_to_all(packed, 'dp', 0, 0, tiled=True)  6.86 us
    ppermute x4, starting transfers between devices, swap_half(): outside[strip].append((piece, lax.ppermute(piece, 'dp', pairs)))  4.94 us
    pallas_call x1, Pallas kernels, body(): pl.pallas_call(functools.partial(own_kernel, static), out_shape=(jax.Shap...  4.87 us
    all_to_all x1, starting transfers between devices, body(): own_f = lax.all_to_all(sent, 'dp', 0, 0, tiled=True)  4.11 us
    pallas_call x2, Pallas kernels, swap_half(): pl.pallas_call(split_kernel, out_shape=(jax.ShapeDtypeStruct((features, L...  3.69 us
  transfers between devices with their start and end apart: 17, of which 11 were waited for; matrix products, arithmetic and copies ran while one was open for 0% of the time, Pallas kernels for 43%

profile of v26, /device:TPU:0, one launch (start us, length us, event | category | flops | bytes accessed | tf_op | source)
XLA Modules:
  0.0 82.0 jit_solution(15140032576483235616)
XLA Ops:
  0.6 0.5 collective-permute-start
  1.2 2.6 %shard_map.130 = (bf16[8,192,128]{2,1,0:T(8,128)(2,1)}, bf16[2,1280,128]{2,1,0:T(8,128)(2,1)}, bf16[2,1280,128]{2,1,0:T(8,128)(2,1)}) custom-call(f32[128,1280]{1,0:T(8,128)} %bitcast.20, f32[64,512]{1,0:T(8,128)} %bitcast.24, bf16[5120,512]{1,0:T(8,128)(2,1)} %sibling_block.1), custom_call_target="tpu_custom_call" | custom-call | tf_op jit(solution)/shard_map/pallas_call | solution.py:502
  3.7 6.9 %all-to-all-start = ((bf16[8,192,128]{2,1,0:T(8,128)(2,1)}), bf16[8,192,128]{2,1,0:T(8,128)(2,1)}, u32[]{:S(2)}, u32[]{:S(2)}) async-start(bf16[8,192,128]{2,1,0:T(8,128)(2,1)} %get-tuple-element.34), calls=%async_computation | async-start | bytes 786432 | tf_op jit(solution)/shard_map/all_to_all | solution.py:517
  10.6 1.5 %collective-permute-start.4 = (bf16[2,1280,128]{2,1,0:T(8,128)(2,1)}, bf16[2,1280,128]{2,1,0:T(8,128)(2,1)}, u32[]{:S(2)}, u32[]{:S(2)}) collective-permute-start(bf16[2,1280,128]{2,1,0:T(8,128)(2,1)} %get-tuple-element.50), channel_id=1, source_target_pairs={{0,2},{1,3},{2,0},{3,1},{4,6},{5,7},{6,4},{7,5},{8,10},{9,11},{10,... | collective-permute-start | bytes 1966088 | tf_op jit(solution)/shard_map/ppermute | solution.py:479
  12.1 0.0 copy-done.6
  12.1 0.1 collective-permute-start.1
  12.2 1.2 %collective-permute-done.1.sibling_gain = f32[1,1280]{1,0:T(1,128)S(1)} collective-permute-done((f32[1,1280]{1,0:T(1,128)S(1)}, f32[1,1280]{1,0:T(1,128)S(1)}, u32[]{:S(2)}, u32[]{:S(2)}) %collective-permute-start.1) | collective-permute-done | bytes 5152 | tf_op jit(solution)/shard_map/ppermute | solution.py:471
  13.3 0.0 collective-permute-done.sibling_in
  13.3 6.2 %shard_map.131 = (bf16[640,2560]{1,0:T(8,128)(2,1)S(1)}, f32[10,128]{1,0:T(8,128)S(1)}) custom-call(bf16[1280,1280]{1,0:T(8,128)(2,1)} %own_in.3, bf16[1280,1280]{1,0:T(8,128)(2,1)} %collective-permute-done.sibling_in, f32[1,1280]{1,0:T(1,128)S(1)} %broadcast_in_dim.3.own_gain, f32[1,1280]{1,0:T(1,128)S(1)} %collective-permute-done.1.sibling_gain), custom_call_target="tpu_custom_call" | custom-call | tf_op jit(solution)/shard_map/pallas_call | solution.py:548
  19.5 0.0 copy-done.4
  19.5 0.0 copy-done.5
  19.5 0.0 copy-start.2
  19.5 0.6 copy-done.2
  20.1 2.9 %all-to-all-done.grad_in = bf16[8,192,128]{2,1,0:T(8,128)(2,1)} async-done(((bf16[8,192,128]{2,1,0:T(8,128)(2,1)}), bf16[8,192,128]{2,1,0:T(8,128)(2,1)}, u32[]{:S(2)}, u32[]{:S(2)}) %all-to-all-start) | async-done | bytes 393248 | tf_op jit(solution)/shard_map/all_to_all | solution.py:517
  23.0 2.6 %shard_map.132 = (f32[3,128,160]{2,1,0:T(8,128)}, f32[3,8,512]{2,1,0:T(8,128)}, bf16[8,192,128]{2,1,0:T(8,128)(2,1)}) custom-call(bf16[8,192,128]{2,1,0:T(8,128)(2,1)} %all-to-all-done.grad_in, f32[128,1280]{1,0:T(8,128)} %bitcast.21, f32[128,1280]{1,0:T(8,128)} %bitcast.22, f32[128,1280]{1,0:T(8,128)} %bitcast.23, f32[64,512]{1,0:T(8,128)} %refs_3_.1, ...), custom_call_target="tpu_custom_call" | custom-call | tf_op jit(solution)/shard_map/pallas_call | solution.py:566
  25.6 4.1 %all-to-all-start.1 = ((bf16[8,192,128]{2,1,0:T(8,128)(2,1)}), bf16[8,192,128]{2,1,0:T(8,128)(2,1)}, u32[]{:S(2)}, u32[]{:S(2)}) async-start(bf16[8,192,128]{2,1,0:T(8,128)(2,1)} %get-tuple-element.39), calls=%async_computation.1 | async-start | bytes 786432 | tf_op jit(solution)/shard_map/all_to_all | solution.py:583
  29.7 0.0 collective-permute-done.4.in_ref
  29.8 1.6 %collective-permute-start.5 = (bf16[2,1280,128]{2,1,0:T(8,128)(2,1)}, bf16[2,1280,128]{2,1,0:T(8,128)(2,1)}, u32[]{:S(2)}, u32[]{:S(2)}) collective-permute-start(bf16[2,1280,128]{2,1,0:T(8,128)(2,1)} %get-tuple-element.51), channel_id=1, source_target_pairs={{0,2},{1,3},{2,0},{3,1},{4,6},{5,7},{6,4},{7,5},{8,10},{9,11},{10,... | collective-permute-start | bytes 1966088 | tf_op jit(solution)/shard_map/ppermute | solution.py:479
  31.3 1.9 %shard_map.135 = (bf16[1280,128]{1,0:T(8,128)(2,1)}, bf16[1280,128]{1,0:T(8,128)(2,1)}) custom-call(bf16[2,1280,128]{2,1,0:T(8,128)(2,1)} %collective-permute-done.4.in_ref), custom_call_target="tpu_custom_call" | custom-call | tf_op jit(solution)/shard_map/pallas_call | solution.py:593
  33.2 1.9 %collective-permute-start.6 = (bf16[1280,128]{1,0:T(8,128)(2,1)}, bf16[1280,128]{1,0:T(8,128)(2,1)}, u32[]{:S(2)}, u32[]{:S(2)}) collective-permute-start(bf16[1280,128]{1,0:T(8,128)(2,1)} %get-tuple-element.53.refs_0_), channel_id=1, source_target_pairs={{0,8},{4,12},{8,0},{12,4},{16,24},{20,28},{24,16},{28,20},{1,9},{5... | collective-permute-start | bytes 983048 | tf_op jit(solution)/shard_map/ppermute | solution.py:607
  35.1 1.5 %collective-permute-start.7 = (bf16[1280,128]{1,0:T(8,128)(2,1)}, bf16[1280,128]{1,0:T(8,128)(2,1)}, u32[]{:S(2)}, u32[]{:S(2)}) collective-permute-start(bf16[1280,128]{1,0:T(8,128)(2,1)} %get-tuple-element.54.refs_2_), channel_id=1, source_target_pairs={{0,4},{4,0},{8,12},{12,8},{16,20},{20,16},{24,28},{28,24},{1,5},{5... | collective-permute-start | bytes 983048 | tf_op jit(solution)/shard_map/ppermute | solution.py:607
  36.6 3.8 %shard_map.133 = (bf16[640,1280]{1,0:T(8,128)(2,1)}, bf16[640,1280]{1,0:T(8,128)(2,1)}) custom-call(bf16[1280,1280]{1,0:T(8,128)(2,1)} %own_in.3, bf16[1280,1280]{1,0:T(8,128)(2,1)} %collective-permute-done.sibling_in, f32[1,1280]{1,0:T(1,128)} %copy-done.4, f32[1,1280]{1,0:T(1,128)} %copy-done.5, f32[10,128]{1,0:T(8,128)} %copy-done.2), custom_call_target="tpu_custom_call" | custom-call | tf_op jit(solution)/shard_map/pallas_call | solution.py:548
  40.4 1.3 %all-to-all-done.1.factor_ref = bf16[8,192,128]{2,1,0:T(8,128)(2,1)} async-done(((bf16[8,192,128]{2,1,0:T(8,128)(2,1)}), bf16[8,192,128]{2,1,0:T(8,128)(2,1)}, u32[]{:S(2)}, u32[]{:S(2)}) %all-to-all-start.1) | async-done | bytes 393248 | tf_op jit(solution)/shard_map/all_to_all | solution.py:583
  41.7 0.0 copy-done.3
  41.7 1.1 %shard_map.134 = (bf16[9,32,128]{2,1,0:T(8,128)(2,1)S(1)}, bf16[4,192,128]{2,1,0:T(8,128)(2,1)S(1)}, bf16[4,192,128]{2,1,0:T(8,128)(2,1)S(1)}) custom-call(bf16[8,192,128]{2,1,0:T(8,128)(2,1)} %all-to-all-done.1.factor_ref, f32[10,128]{1,0:T(8,128)S(1)} %copy-done.3), custom_call_target="tpu_custom_call" | custom-call | tf_op jit(solution)/shard_map/pallas_call | solution.py:614
  42.8 0.1 collective-permute-start.2
  42.8 0.5 collective-permute-start.3
  43.3 2.4 %collective-permute-done.6.refs_1_ = bf16[1280,128]{1,0:T(8,128)(2,1)} collective-permute-done((bf16[1280,128]{1,0:T(8,128)(2,1)}, bf16[1280,128]{1,0:T(8,128)(2,1)}, u32[]{:S(2)}, u32[]{:S(2)}) %collective-permute-start.6) | collective-permute-done | bytes 327712 | tf_op jit(solution)/shard_map/ppermute | solution.py:607
  45.8 1.5 %collective-permute-start.8 = (bf16[9,32,128]{2,1,0:T(8,128)(2,1)S(1)}, bf16[9,32,128]{2,1,0:T(8,128)(2,1)S(1)}, u32[]{:S(2)}, u32[]{:S(2)}) collective-permute-start(bf16[9,32,128]{2,1,0:T(8,128)(2,1)S(1)} %get-tuple-element.55), channel_id=1, source_target_pairs={{0,2},{1,3},{2,0},{3,1},{4,6},{5,7},{6,4},{7,5},{8,10},{9,11},{10,... | collective-permute-start | bytes 221192 | tf_op jit(solution)/shard_map/ppermute | solution.py:479
  47.3 0.0 collective-permute-done.7.refs_3_
  47.3 1.6 %shard_map.136.blocks = bf16[2560,256]{1,0:T(8,128)(2,1)S(1)} custom-call(bf16[1280,128]{1,0:T(8,128)(2,1)} %get-tuple-element.53.refs_0_, bf16[1280,128]{1,0:T(8,128)(2,1)} %collective-permute-done.6.refs_1_, bf16[1280,128]{1,0:T(8,128)(2,1)} %get-tuple-element.54.refs_2_, bf16[1280,128]{1,0:T(8,128)(2,1)} %collective-permute-done.7.refs_3_), custom_call_target="tpu_custom_call" | custom-call | tf_op jit(solution)/shard_map/pallas_call | solution.py:649
  48.9 1.2 %collective-permute-done.8.b_ref.refs_0_ = bf16[9,32,128]{2,1,0:T(8,128)(2,1)S(1)} collective-permute-done((bf16[9,32,128]{2,1,0:T(8,128)(2,1)S(1)}, bf16[9,32,128]{2,1,0:T(8,128)(2,1)S(1)}, u32[]{:S(2)}, u32[]{:S(2)}) %collective-permute-start.8) | collective-permute-done | bytes 73760 | tf_op jit(solution)/shard_map/ppermute | solution.py:479
  50.1 0.0 collective-permute-done.2.refs_2_
  50.1 0.0 collective-permute-done.3.refs_3_
  50.1 0.0 copy-start.1
  50.2 1.7 %shard_map.137 = (bf16[2560,256]{1,0:T(8,128)(2,1)S(1)}, bf16[640,256]{1,0:T(8,128)(2,1)S(1)}) custom-call(bf16[2560,256]{1,0:T(8,128)(2,1)S(1)} %shard_map.136.blocks, bf16[9,32,128]{2,1,0:T(8,128)(2,1)S(1)} %collective-permute-done.8.b_ref.refs_0_, bf16[640,2560]{1,0:T(8,128)(2,1)S(1)} %get-tuple-element.46.x.refs_4_, ...), custom_call_target="tpu_custom_call" | custom-call | tf_op jit(solution)/shard_map/pallas_call | solution.py:656
  51.9 1.6 %collective-permute-start.11 = (bf16[640,256]{1,0:T(8,128)(2,1)S(1)}, bf16[640,256]{1,0:T(8,128)(2,1)S(1)}, u32[]{:S(2)}, u32[]{:S(2)}) collective-permute-start(bf16[640,256]{1,0:T(8,128)(2,1)S(1)} %get-tuple-element.56), channel_id=1, source_target_pairs={{0,2},{1,3},{2,0},{3,1},{4,6},{5,7},{6,4},{7,5},{8,10},{9,11},{10,... | collective-permute-start | bytes 983048 | tf_op jit(solution)/shard_map/ppermute | solution.py:479
  53.4 0.0 collective-permute-done.5.in_ref
  53.4 1.8 %shard_map.138 = (bf16[1280,128]{1,0:T(8,128)(2,1)S(1)}, bf16[1280,128]{1,0:T(8,128)(2,1)S(1)}) custom-call(bf16[2,1280,128]{2,1,0:T(8,128)(2,1)} %collective-permute-done.5.in_ref), custom_call_target="tpu_custom_call" | custom-call | tf_op jit(solution)/shard_map/pallas_call | solution.py:593
  55.2 0.1 collective-permute-start.9
  55.3 1.5 %collective-permute-start.10 = (bf16[1280,128]{1,0:T(8,128)(2,1)S(1)}, bf16[1280,128]{1,0:T(8,128)(2,1)S(1)}, u32[]{:S(2)}, u32[]{:S(2)}) collective-permute-start(bf16[1280,128]{1,0:T(8,128)(2,1)S(1)} %get-tuple-element.59.refs_2_), channel_id=1, source_target_pairs={{0,4},{4,0},{8,12},{12,8},{16,20},{20,16},{24,28},{28,24},{1,5},{5... | collective-permute-start | bytes 983048 | tf_op jit(solution)/shard_map/ppermute | solution.py:607
  56.8 0.0 copy-done
  56.8 0.0 copy-done.1
  56.8 1.2 %shard_map.142 = bf16[640,256]{1,0:T(8,128)(2,1)S(1)} custom-call(bf16[640,1280]{1,0:T(8,128)(2,1)S(1)} %copy-done, bf16[640,1280]{1,0:T(8,128)(2,1)S(1)} %copy-done.1, bf16[2560,256]{1,0:T(8,128)(2,1)S(1)} %get-tuple-element.61.refs_2_), custom_call_target="tpu_custom_call" | custom-call | tf_op jit(solution)/shard_map/pallas_call | solution.py:664
  58.0 0.6 collective-permute-start.12
  58.6 3.3 %collective-permute-done.11.refs_4_.refs_0_ = bf16[640,256]{1,0:T(8,128)(2,1)S(1)} collective-permute-done((bf16[640,256]{1,0:T(8,128)(2,1)S(1)}, bf16[640,256]{1,0:T(8,128)(2,1)S(1)}, u32[]{:S(2)}, u32[]{:S(2)}) %collective-permute-start.11) | collective-permute-done | bytes 327712 | tf_op jit(solution)/shard_map/ppermute | solution.py:479
  61.9 1.1 %collective-permute-done.9.refs_1_ = bf16[1280,128]{1,0:T(8,128)(2,1)S(1)} collective-permute-done((bf16[1280,128]{1,0:T(8,128)(2,1)S(1)}, bf16[1280,128]{1,0:T(8,128)(2,1)S(1)}, u32[]{:S(2)}, u32[]{:S(2)}) %collective-permute-start.9) | collective-permute-done | bytes 327712 | tf_op jit(solution)/shard_map/ppermute | solution.py:607
  63.0 0.1 collective-permute-done.10.refs_3_
  63.1 0.3 shard_map.139.blocks
  63.4 0.0 slice-start.1
  63.4 1.7 %shard_map.140 = (bf16[2560,256]{1,0:T(8,128)(2,1)S(1)}, bf16[640,256]{1,0:T(8,128)(2,1)S(1)}) custom-call(bf16[2560,256]{1,0:T(8,128)(2,1)S(1)} %shard_map.139.blocks, bf16[9,32,128]{2,1,0:T(8,128)(2,1)S(1)} %collective-permute-done.8.b_ref.refs_0_, bf16[640,2560]{1,0:T(8,128)(2,1)S(1)} %get-tuple-element.46.x.refs_4_, ...), custom_call_target="tpu_custom_call" | custom-call | tf_op jit(solution)/shard_map/pallas_call | solution.py:656
  65.2 1.1 %collective-permute-start.14 = (bf16[640,256]{1,0:T(8,128)(2,1)S(1)}, bf16[640,256]{1,0:T(8,128)(2,1)S(1)}, u32[]{:S(2)}, u32[]{:S(2)}) collective-permute-start(bf16[640,256]{1,0:T(8,128)(2,1)S(1)} %get-tuple-element.63), channel_id=1, source_target_pairs={{0,2},{1,3},{2,0},{3,1},{4,6},{5,7},{6,4},{7,5},{8,10},{9,11},{10,... | collective-permute-start | bytes 983048 | tf_op jit(solution)/shard_map/ppermute | solution.py:479
  66.2 1.2 %shard_map.141.refs_7_ = bf16[640,256]{1,0:T(8,128)(2,1)S(1)} custom-call(bf16[640,1280]{1,0:T(8,128)(2,1)S(1)} %copy-done, bf16[640,1280]{1,0:T(8,128)(2,1)S(1)} %copy-done.1, bf16[2560,256]{1,0:T(8,128)(2,1)S(1)} %get-tuple-element.60.refs_2_), custom_call_target="tpu_custom_call" | custom-call | tf_op jit(solution)/shard_map/pallas_call | solution.py:664
  67.4 1.1 %collective-permute-start.13 = (bf16[640,256]{1,0:T(8,128)(2,1)S(1)}, bf16[640,256]{1,0:T(8,128)(2,1)S(1)}, u32[]{:S(2)}, u32[]{:S(2)}) collective-permute-start(bf16[640,256]{1,0:T(8,128)(2,1)S(1)} %shard_map.141.refs_7_), channel_id=1, source_target_pairs={{0,2},{1,3},{2,0},{3,1},{4,6},{5,7},{6,4},{7,5},{8,10},{9,11},{10,... | collective-permute-start | bytes 983048 | tf_op jit(solution)/shard_map/ppermute | solution.py:479
  68.5 0.2 shard_map.144.inv
  68.7 0.2 collective-permute-done.12.refs_8_.refs_0_
  68.9 0.0 slice-done
  68.9 4.9 %shard_map.143 = (f32[1280,256]{1,0:T(8,128)S(1)}, f32[1280,256]{1,0:T(8,128)S(1)}) custom-call(bf16[5120,512]{1,0:T(8,128)(2,1)S(1)} %bitcast.19, bf16[5120,512]{1,0:T(8,128)(2,1)S(1)} %bitcast.19, bf16[4,192,128]{2,1,0:T(8,128)(2,1)S(1)} %get-tuple-element.44.refs_0_, bf16[4,192,128]{2,1,0:T(8,128)(2,1)S(1)} %get-tuple-element.45.refs_1_, ...), custom_call_target="tpu_custom_call" | custom-call | flops 3355443200 | bytes 6553600 | tf_op jit(solution)/shard_map/pallas_call | solution.py:679
  73.8 0.9 %shard_map.145.refs_1_ = bf16[1280,512]{1,0:T(8,128)(2,1)} custom-call(f32[1280,256]{1,0:T(8,128)S(1)} %get-tuple-element.64.own, f32[1280,128]{1,0:T(8,128)S(1)} %shard_map.144.inv, bf16[640,256]{1,0:T(8,128)(2,1)S(1)} %collective-permute-done.11.refs_4_.refs_0_), custom_call_target="tpu_custom_call" | custom-call | tf_op jit(solution)/shard_map/pallas_call | solution.py:430
  74.7 0.9 %shard_map.146.refs_1_ = bf16[1280,512]{1,0:T(8,128)(2,1)} custom-call(f32[1280,256]{1,0:T(8,128)S(1)} %get-tuple-element.64.own, f32[1280,128]{1,0:T(8,128)S(1)} %shard_map.144.inv, bf16[640,256]{1,0:T(8,128)(2,1)S(1)} %collective-permute-done.12.refs_8_.refs_0_, bf16[1280,512]{1,0:T(8,128)(2,1)} %shard_map.145.refs_1_), custom_call_target="tpu_custom_call", output_to_operand_aliasing={{}: (3, {})} | custom-call | tf_op jit(solution)/shard_map/pallas_call | solution.py:430
  75.6 0.4 collective-permute-done.14.refs_0_
  76.0 0.9 %shard_map.147.refs_1_ = bf16[1280,512]{1,0:T(8,128)(2,1)} custom-call(f32[1280,256]{1,0:T(8,128)S(1)} %get-tuple-element.62.own, f32[1280,128]{1,0:T(8,128)S(1)} %shard_map.144.inv, bf16[640,256]{1,0:T(8,128)(2,1)S(1)} %collective-permute-done.14.refs_0_, bf16[1280,512]{1,0:T(8,128)(2,1)} %shard_map.146.refs_1_), custom_call_target="tpu_custom_call", output_to_operand_aliasing={{}: (3, {})} | custom-call | tf_op jit(solution)/shard_map/pallas_call | solution.py:430
  76.8 4.3 %collective-permute-done.13.refs_0_ = bf16[640,256]{1,0:T(8,128)(2,1)S(1)} collective-permute-done((bf16[640,256]{1,0:T(8,128)(2,1)S(1)}, bf16[640,256]{1,0:T(8,128)(2,1)S(1)}, u32[]{:S(2)}, u32[]{:S(2)}) %collective-permute-start.13) | collective-permute-done | bytes 327712 | tf_op jit(solution)/shard_map/ppermute | solution.py:479
  81.1 0.9 %shard_map.148 = bf16[1280,512]{1,0:T(8,128)(2,1)} custom-call(f32[1280,256]{1,0:T(8,128)S(1)} %get-tuple-element.62.own, f32[1280,128]{1,0:T(8,128)S(1)} %shard_map.144.inv, bf16[640,256]{1,0:T(8,128)(2,1)S(1)} %collective-permute-done.13.refs_0_, bf16[1280,512]{1,0:T(8,128)(2,1)} %shard_map.147.refs_1_), custom_call_target="tpu_custom_call", output_to_operand_aliasing={{}: (3, {})} | custom-call | tf_op jit(solution)/shard_map/pallas_call | solution.py:430
  (9 shorter events, 0.0 us)
Async XLA Ops:
  0.6 12.7 %collective-permute-start = (bf16[1280,1280]{1,0:T(8,128)(2,1)}, bf16[1280,1280]{1,0:T(8,128)(2,1)}, u32[]{:S(2)}, u32[]{:S(2)}) collective-permute-start(bf16[1280,1280]{1,0:T(8,128)(2,1)} %own_in.3), channel_id=1, source_target_pairs={{0,1},{1,0},{2,3},{3,2},{4,5},{5,4},{6,7},{7,6},{8,9},{9,8},{10,11... | collective-permute-start | bytes 9830408 | tf_op jit(solution)/shard_map/ppermute | solution.py:471
  1.1 10.9 %copy-start.6 = (f32[1280]{0:T(1024)S(1)}, f32[1280]{0:T(1024)}, u32[]{:S(2)}) copy-start(f32[1280]{0:T(1024)} %param.12) | copy-start | bytes 15364
  3.7 19.3 %all-to-all-start = ((bf16[8,192,128]{2,1,0:T(8,128)(2,1)}), bf16[8,192,128]{2,1,0:T(8,128)(2,1)}, u32[]{:S(2)}, u32[]{:S(2)}) async-start(bf16[8,192,128]{2,1,0:T(8,128)(2,1)} %get-tuple-element.34), calls=%async_computation | async-start | bytes 786432 | tf_op jit(solution)/shard_map/all_to_all | solution.py:517
  10.6 19.1 %collective-permute-start.4 = (bf16[2,1280,128]{2,1,0:T(8,128)(2,1)}, bf16[2,1280,128]{2,1,0:T(8,128)(2,1)}, u32[]{:S(2)}, u32[]{:S(2)}) collective-permute-start(bf16[2,1280,128]{2,1,0:T(8,128)(2,1)} %get-tuple-element.50), channel_id=1, source_target_pairs={{0,2},{1,3},{2,0},{3,1},{4,6},{5,7},{6,4},{7,5},{8,10},{9,11},{10,... | collective-permute-start | bytes 1966088 | tf_op jit(solution)/shard_map/ppermute | solution.py:479
  12.1 7.4 %copy-start.4 = (f32[1,1280]{1,0:T(1,128)}, f32[1,1280]{1,0:T(1,128)S(1)}, u32[]{:S(2)}) copy-start(f32[1,1280]{1,0:T(1,128)S(1)} %broadcast_in_dim.3.own_gain) | copy-start | bytes 15364
  12.1 1.2 %collective-permute-start.1 = (f32[1,1280]{1,0:T(1,128)S(1)}, f32[1,1280]{1,0:T(1,128)S(1)}, u32[]{:S(2)}, u32[]{:S(2)}) collective-permute-start(f32[1,1280]{1,0:T(1,128)S(1)} %broadcast_in_dim.3.own_gain), channel_id=1, source_target_pairs={{0,1},{1,0},{2,3},{3,2},{4,5},{5,4},{6,7},{7,6},{8,9},{9,8},{10,11... | collective-permute-start | bytes 15368 | tf_op jit(solution)/shard_map/ppermute | solution.py:471
  13.3 6.2 %copy-start.5 = (f32[1,1280]{1,0:T(1,128)}, f32[1,1280]{1,0:T(1,128)S(1)}, u32[]{:S(2)}) copy-start(f32[1,1280]{1,0:T(1,128)S(1)} %collective-permute-done.1.sibling_gain) | copy-start | bytes 15364
  19.5 0.6 copy-start.2
  25.6 16.0 %all-to-all-start.1 = ((bf16[8,192,128]{2,1,0:T(8,128)(2,1)}), bf16[8,192,128]{2,1,0:T(8,128)(2,1)}, u32[]{:S(2)}, u32[]{:S(2)}) async-start(bf16[8,192,128]{2,1,0:T(8,128)(2,1)} %get-tuple-element.39), calls=%async_computation.1 | async-start | bytes 786432 | tf_op jit(solution)/shard_map/all_to_all | solution.py:583
  29.8 23.7 %collective-permute-start.5 = (bf16[2,1280,128]{2,1,0:T(8,128)(2,1)}, bf16[2,1280,128]{2,1,0:T(8,128)(2,1)}, u32[]{:S(2)}, u32[]{:S(2)}) collective-permute-start(bf16[2,1280,128]{2,1,0:T(8,128)(2,1)} %get-tuple-element.51), channel_id=1, source_target_pairs={{0,2},{1,3},{2,0},{3,1},{4,6},{5,7},{6,4},{7,5},{8,10},{9,11},{10,... | collective-permute-start | bytes 1966088 | tf_op jit(solution)/shard_map/ppermute | solution.py:479
  33.2 12.6 %collective-permute-start.6 = (bf16[1280,128]{1,0:T(8,128)(2,1)}, bf16[1280,128]{1,0:T(8,128)(2,1)}, u32[]{:S(2)}, u32[]{:S(2)}) collective-permute-start(bf16[1280,128]{1,0:T(8,128)(2,1)} %get-tuple-element.53.refs_0_), channel_id=1, source_target_pairs={{0,8},{4,12},{8,0},{12,4},{16,24},{20,28},{24,16},{28,20},{1,9},{5... | collective-permute-start | bytes 983048 | tf_op jit(solution)/shard_map/ppermute | solution.py:607
  35.1 6.6 %copy-start.3 = (f32[10,128]{1,0:T(8,128)S(1)}, f32[10,128]{1,0:T(8,128)}, u32[]{:S(2)}) copy-start(f32[10,128]{1,0:T(8,128)} %copy-done.2) | copy-start | bytes 15364
  35.1 12.2 %collective-permute-start.7 = (bf16[1280,128]{1,0:T(8,128)(2,1)}, bf16[1280,128]{1,0:T(8,128)(2,1)}, u32[]{:S(2)}, u32[]{:S(2)}) collective-permute-start(bf16[1280,128]{1,0:T(8,128)(2,1)} %get-tuple-element.54.refs_2_), channel_id=1, source_target_pairs={{0,4},{4,0},{8,12},{12,8},{16,20},{20,16},{24,28},{28,24},{1,5},{5... | collective-permute-start | bytes 983048 | tf_op jit(solution)/shard_map/ppermute | solution.py:607
  42.8 7.4 %collective-permute-start.2 = (bf16[4,192,128]{2,1,0:T(8,128)(2,1)S(1)}, bf16[4,192,128]{2,1,0:T(8,128)(2,1)S(1)}, u32[]{:S(2)}, u32[]{:S(2)}) collective-permute-start(bf16[4,192,128]{2,1,0:T(8,128)(2,1)S(1)} %get-tuple-element.44.refs_0_), channel_id=1, source_target_pairs={{0,1},{1,0},{2,3},{3,2},{4,5},{5,4},{6,7},{7,6},{8,9},{9,8},{10,11... | collective-permute-start | bytes 589832 | tf_op jit(solution)/shard_map/ppermute | solution.py:471
  42.8 7.3 %collective-permute-start.3 = (bf16[4,192,128]{2,1,0:T(8,128)(2,1)S(1)}, bf16[4,192,128]{2,1,0:T(8,128)(2,1)S(1)}, u32[]{:S(2)}, u32[]{:S(2)}) collective-permute-start(bf16[4,192,128]{2,1,0:T(8,128)(2,1)S(1)} %get-tuple-element.45.refs_1_), channel_id=1, source_target_pairs={{0,1},{1,0},{2,3},{3,2},{4,5},{5,4},{6,7},{7,6},{8,9},{9,8},{10,11... | collective-permute-start | bytes 589832 | tf_op jit(solution)/shard_map/ppermute | solution.py:471
  45.8 4.4 %collective-permute-start.8 = (bf16[9,32,128]{2,1,0:T(8,128)(2,1)S(1)}, bf16[9,32,128]{2,1,0:T(8,128)(2,1)S(1)}, u32[]{:S(2)}, u32[]{:S(2)}) collective-permute-start(bf16[9,32,128]{2,1,0:T(8,128)(2,1)S(1)} %get-tuple-element.55), channel_id=1, source_target_pairs={{0,2},{1,3},{2,0},{3,1},{4,6},{5,7},{6,4},{7,5},{8,10},{9,11},{10,... | collective-permute-start | bytes 221192 | tf_op jit(solution)/shard_map/ppermute | solution.py:479
  50.1 6.7 %copy-start = (bf16[640,1280]{1,0:T(8,128)(2,1)S(1)}, bf16[640,1280]{1,0:T(8,128)(2,1)}, u32[]{:S(2)}) copy-start(bf16[640,1280]{1,0:T(8,128)(2,1)} %get-tuple-element.47.refs_0_.refs_5_) | copy-start | bytes 4915204
  50.1 6.7 %copy-start.1 = (bf16[640,1280]{1,0:T(8,128)(2,1)S(1)}, bf16[640,1280]{1,0:T(8,128)(2,1)}, u32[]{:S(2)}) copy-start(bf16[640,1280]{1,0:T(8,128)(2,1)} %get-tuple-element.48.refs_1_.refs_6_) | copy-start | bytes 4915204
  51.9 10.1 %collective-permute-start.11 = (bf16[640,256]{1,0:T(8,128)(2,1)S(1)}, bf16[640,256]{1,0:T(8,128)(2,1)S(1)}, u32[]{:S(2)}, u32[]{:S(2)}) collective-permute-start(bf16[640,256]{1,0:T(8,128)(2,1)S(1)} %get-tuple-element.56), channel_id=1, source_target_pairs={{0,2},{1,3},{2,0},{3,1},{4,6},{5,7},{6,4},{7,5},{8,10},{9,11},{10,... | collective-permute-start | bytes 983048 | tf_op jit(solution)/shard_map/ppermute | solution.py:479
  55.2 7.8 %collective-permute-start.9 = (bf16[1280,128]{1,0:T(8,128)(2,1)S(1)}, bf16[1280,128]{1,0:T(8,128)(2,1)S(1)}, u32[]{:S(2)}, u32[]{:S(2)}) collective-permute-start(bf16[1280,128]{1,0:T(8,128)(2,1)S(1)} %get-tuple-element.58.refs_0_), channel_id=1, source_target_pairs={{0,8},{4,12},{8,0},{12,4},{16,24},{20,28},{24,16},{28,20},{1,9},{5... | collective-permute-start | bytes 983048 | tf_op jit(solution)/shard_map/ppermute | solution.py:607
  55.3 7.8 %collective-permute-start.10 = (bf16[1280,128]{1,0:T(8,128)(2,1)S(1)}, bf16[1280,128]{1,0:T(8,128)(2,1)S(1)}, u32[]{:S(2)}, u32[]{:S(2)}) collective-permute-start(bf16[1280,128]{1,0:T(8,128)(2,1)S(1)} %get-tuple-element.59.refs_2_), channel_id=1, source_target_pairs={{0,4},{4,0},{8,12},{12,8},{16,20},{20,16},{24,28},{28,24},{1,5},{5... | collective-permute-start | bytes 983048 | tf_op jit(solution)/shard_map/ppermute | solution.py:607
  58.0 10.9 %collective-permute-start.12 = (bf16[640,256]{1,0:T(8,128)(2,1)S(1)}, bf16[640,256]{1,0:T(8,128)(2,1)S(1)}, u32[]{:S(2)}, u32[]{:S(2)}) collective-permute-start(bf16[640,256]{1,0:T(8,128)(2,1)S(1)} %shard_map.142), channel_id=1, source_target_pairs={{0,2},{1,3},{2,0},{3,1},{4,6},{5,7},{6,4},{7,5},{8,10},{9,11},{10,... | collective-permute-start | bytes 983048 | tf_op jit(solution)/shard_map/ppermute | solution.py:479
  63.1 5.9 %slice-start = ((s8[5242880]{0:T(1024)(128)(4,1)}), s8[4194304]{0:T(1024)(128)(4,1)S(1)}, s32[]{:S(2)}) async-start(s8[5242880]{0:T(1024)(128)(4,1)} %bitcast.18), calls=%async_computation.2 | async-start | bytes 8388608
  63.4 5.5 %slice-start.1 = ((s8[5242880]{0:T(1024)(128)(4,1)}), s8[1048576]{0:T(1024)(128)(4,1)S(1)}, s32[]{:S(2)}) async-start(s8[5242880]{0:T(1024)(128)(4,1)} %bitcast.18), calls=%async_computation.3 | async-start | bytes 2097152
  65.2 10.8 %collective-permute-start.14 = (bf16[640,256]{1,0:T(8,128)(2,1)S(1)}, bf16[640,256]{1,0:T(8,128)(2,1)S(1)}, u32[]{:S(2)}, u32[]{:S(2)}) collective-permute-start(bf16[640,256]{1,0:T(8,128)(2,1)S(1)} %get-tuple-element.63), channel_id=1, source_target_pairs={{0,2},{1,3},{2,0},{3,1},{4,6},{5,7},{6,4},{7,5},{8,10},{9,11},{10,... | collective-permute-start | bytes 983048 | tf_op jit(solution)/shard_map/ppermute | solution.py:479
  67.4 13.7 %collective-permute-start.13 = (bf16[640,256]{1,0:T(8,128)(2,1)S(1)}, bf16[640,256]{1,0:T(8,128)(2,1)S(1)}, u32[]{:S(2)}, u32[]{:S(2)}) collective-permute-start(bf16[640,256]{1,0:T(8,128)(2,1)S(1)} %shard_map.141.refs_7_), channel_id=1, source_target_pairs={{0,2},{1,3},{2,0},{3,1},{4,6},{5,7},{6,4},{7,5},{8,10},{9,11},{10,... | collective-permute-start | bytes 983048 | tf_op jit(solution)/shard_map/ppermute | solution.py:479
